TPU v7x, 128 devices: a whole 4x4x4 slice. The times are simulated.
128 devices in a mesh: batch: 32 (over z_hi, y, x), dim: 4 (over z_lo, core).
Axes of the slice: x: 4, y: 4, z: 4 (z_hi: 2, z_lo: 2; z = z_hi * 2 + z_lo), core: 2. Of those that a mesh axis runs over, the one named last changes fastest.
Arguments:
- picture_embeds: bfloat16 [11264, 1152], P('batch', 'dim'), may hold values from -0.1875 to 0.1875
- caption_embeds: bfloat16 [11264, 1152], P('batch', 'dim'), may hold values from -0.1875 to 0.1875
- logit_scaler: float32 [1], replicated, may hold values from 10 to 30
- logit_offset_term: float32 [1], replicated, may hold values from -4 to -2
Outputs:
- image_grad: float32 [11264, 1152], P('batch', 'dim')
- text_grad: float32 [11264, 1152], P('batch', 'dim')
- scalar_grads: float32 [2], replicated
All inputs are finite; a program needn't handle non-finite values.
Results may differ from a plain program's by a relative error of at most 0.0003.
The roundings to bfloat16 on the way count: a program that leaves them out, or rounds other values in their place, can miss the bound.
Values may be sent and summed in bfloat16 or wider, within the bound.
No kernel may reach another device: no remote copies, remote signals or barrier semaphores. Data moves between devices by JAX's collectives and lax.ppermute only.
A program may use at most 64 MiB of HBM per device.

v0:
```python
import jax
import jax.numpy as jnp
from jax import lax
from jax.sharding import PartitionSpec as P


def from_behind(array, axis, by):
    devices = lax.axis_size(axis)
    return lax.ppermute(array, axis, [(i, (i + by) % devices) for i in range(devices)])


def pair_dot(left, right):
    return lax.dot_general(
        left, right, (((1,), (1,)), ((), ())), preferred_element_type=jnp.float32
    )


def coefficients(similar, row_ids, column_ids, iteration, scaling_factor, offset):
    logits = scaling_factor * similar + offset
    matched = (row_ids[:, None] == column_ids[None, :]) & (iteration == 0)
    labels = jnp.where(matched, jnp.float32(1.0), jnp.float32(-1.0))
    coeff = -labels * jax.nn.sigmoid(-labels * logits)
    return (coeff, jnp.sum(coeff * similar), jnp.sum(coeff))


def body(picture_embeds, caption_embeds, logit_scaler, logit_offset_term):
    row_count = picture_embeds.shape[0]
    cycle_size = lax.axis_size("batch")
    scaling_factor = logit_scaler[0]
    offset = logit_offset_term[0]
    whole_feature_list = jnp.arange(row_count, dtype=jnp.int32)
    block_rows, features = caption_embeds.shape

    def patch_coefficients(caption_slice, iteration):
        similar = lax.psum(pair_dot(picture_embeds, caption_slice), "dim")
        coeff, temp_part, bias_part = coefficients(
            similar, whole_feature_list, whole_feature_list, iteration, scaling_factor, offset
        )
        return (coeff.astype(jnp.bfloat16), temp_part, bias_part)

    image_zero = jnp.zeros((row_count, features), jnp.float32)
    text_zero = jnp.zeros((block_rows, features), jnp.float32)

    def carried_rotation(iteration, carry):
        caption_slice, text_acc, image_acc, temp_acc, bias_running_total = carry
        coeff_low, temp_part, bias_part = patch_coefficients(caption_slice, iteration)
        image_acc = image_acc + scaling_factor * jnp.dot(
            coeff_low, caption_slice, preferred_element_type=jnp.float32
        )
        text_acc = text_acc + scaling_factor * lax.dot_general(
            coeff_low, picture_embeds, (((0,), (0,)), ((), ())), preferred_element_type=jnp.float32
        )
        caption_slice, text_acc = (
            from_behind(caption_slice.astype(jnp.float32), "batch", 1).astype(caption_slice.dtype),
            from_behind(text_acc, "batch", 1),
        )
        return (
            caption_slice,
            text_acc,
            image_acc,
            temp_acc + temp_part,
            bias_running_total + bias_part,
        )

    start = (caption_embeds, text_zero, image_zero, jnp.float32(0.0), jnp.float32(0.0))
    final = lax.fori_loop(0, cycle_size, carried_rotation, start)
    text_local = final[1]
    image_resident_rows, temp_acc, bias_running_total = (final[2], final[3], final[4])
    local_pair = jnp.stack([temp_acc, bias_running_total])
    scalar_grads = lax.psum(local_pair, "batch")
    return (image_resident_rows, text_local, scalar_grads)


def solution(mesh):
    placed = (P("batch", "dim"), P("batch", "dim"), P(), P())
    return jax.shard_map(
        body,
        mesh=mesh,
        in_specs=placed,
        out_specs=(P("batch", "dim"), P("batch", "dim"), P()),
        check_vma=False,
    )
```

profile of v0, /device:TPU:1, one launch (start us, length us, event | category | flops | bytes accessed | tf_op | source)
XLA Modules:
  0.0 1964.2 jit_solution(1276767660547669917)
XLA Ops:
  8.2 1872.0 %while.22 = (s32[]{:T(128)}, bf16[352,288]{0,1:T(8,128)(2,1)S(1)}, f32[352,288]{0,1:T(8,128)S(1)}, f32[352,288]{0,1:T(8,128)S(1)}, f32[]{:T(128)}, /*index=5*/f3...) while((s32[]{:T(128)}, bf16[352,288]{0,1:T(8,128)(2,1)S(1)}, ...), condition=%wide.region_4.5_spmd.clone, body=%wide.region_0.4_spmd.clone.sunk | while | flops 219445248 | bytes 12300613 | solution.py:66
  11.5 41.6 %all-reduce.2.cloned.1.call-done = f32[352,352]{1,0:T(8,128)} async-done(((f32[352,352]{1,0:T(8,128)}), f32[352,352]{1,0:T(8,128)}) %all-reduce.2.cloned.1.call-update) | async-done | bytes 495632 | tf_op jit(solution)/shard_map/while/body/eval_jaxpr/psum | solution.py:35
  62.6 10.7 collective-permute-done.1
  74.6 36.9 %all-reduce.2.cloned.1.call-done = f32[352,352]{1,0:T(8,128)} async-done(((f32[352,352]{1,0:T(8,128)}), f32[352,352]{1,0:T(8,128)}) %all-reduce.2.cloned.1.call-update) | async-done | bytes 495632 | tf_op jit(solution)/shard_map/while/body/eval_jaxpr/psum | solution.py:35
  121.1 10.7 collective-permute-done.1
  133.1 36.8 %all-reduce.2.cloned.1.call-done = f32[352,352]{1,0:T(8,128)} async-done(((f32[352,352]{1,0:T(8,128)}), f32[352,352]{1,0:T(8,128)}) %all-reduce.2.cloned.1.call-update) | async-done | bytes 495632 | tf_op jit(solution)/shard_map/while/body/eval_jaxpr/psum | solution.py:35
  179.5 10.7 collective-permute-done.1
  191.5 36.5 %all-reduce.2.cloned.1.call-done = f32[352,352]{1,0:T(8,128)} async-done(((f32[352,352]{1,0:T(8,128)}), f32[352,352]{1,0:T(8,128)}) %all-reduce.2.cloned.1.call-update) | async-done | bytes 495632 | tf_op jit(solution)/shard_map/while/body/eval_jaxpr/psum | solution.py:35
  237.5 10.7 collective-permute-done.1
  249.5 36.6 %all-reduce.2.cloned.1.call-done = f32[352,352]{1,0:T(8,128)} async-done(((f32[352,352]{1,0:T(8,128)}), f32[352,352]{1,0:T(8,128)}) %all-reduce.2.cloned.1.call-update) | async-done | bytes 495632 | tf_op jit(solution)/shard_map/while/body/eval_jaxpr/psum | solution.py:35
  295.6 10.7 collective-permute-done.1
  307.6 36.5 %all-reduce.2.cloned.1.call-done = f32[352,352]{1,0:T(8,128)} async-done(((f32[352,352]{1,0:T(8,128)}), f32[352,352]{1,0:T(8,128)}) %all-reduce.2.cloned.1.call-update) | async-done | bytes 495632 | tf_op jit(solution)/shard_map/while/body/eval_jaxpr/psum | solution.py:35
  353.7 10.7 collective-permute-done.1
  365.7 36.9 %all-reduce.2.cloned.1.call-done = f32[352,352]{1,0:T(8,128)} async-done(((f32[352,352]{1,0:T(8,128)}), f32[352,352]{1,0:T(8,128)}) %all-reduce.2.cloned.1.call-update) | async-done | bytes 495632 | tf_op jit(solution)/shard_map/while/body/eval_jaxpr/psum | solution.py:35
  412.2 10.7 collective-permute-done.1
  424.2 36.9 %all-reduce.2.cloned.1.call-done = f32[352,352]{1,0:T(8,128)} async-done(((f32[352,352]{1,0:T(8,128)}), f32[352,352]{1,0:T(8,128)}) %all-reduce.2.cloned.1.call-update) | async-done | bytes 495632 | tf_op jit(solution)/shard_map/while/body/eval_jaxpr/psum | solution.py:35
  470.6 10.7 collective-permute-done.1
  482.6 36.8 %all-reduce.2.cloned.1.call-done = f32[352,352]{1,0:T(8,128)} async-done(((f32[352,352]{1,0:T(8,128)}), f32[352,352]{1,0:T(8,128)}) %all-reduce.2.cloned.1.call-update) | async-done | bytes 495632 | tf_op jit(solution)/shard_map/while/body/eval_jaxpr/psum | solution.py:35
  541.0 36.6 %all-reduce.2.cloned.1.call-done = f32[352,352]{1,0:T(8,128)} async-done(((f32[352,352]{1,0:T(8,128)}), f32[352,352]{1,0:T(8,128)}) %all-reduce.2.cloned.1.call-update) | async-done | bytes 495632 | tf_op jit(solution)/shard_map/while/body/eval_jaxpr/psum | solution.py:35
  599.1 36.8 %all-reduce.2.cloned.1.call-done = f32[352,352]{1,0:T(8,128)} async-done(((f32[352,352]{1,0:T(8,128)}), f32[352,352]{1,0:T(8,128)}) %all-reduce.2.cloned.1.call-update) | async-done | bytes 495632 | tf_op jit(solution)/shard_map/while/body/eval_jaxpr/psum | solution.py:35
  645.5 10.7 collective-permute-done.1
  657.5 36.6 %all-reduce.2.cloned.1.call-done = f32[352,352]{1,0:T(8,128)} async-done(((f32[352,352]{1,0:T(8,128)}), f32[352,352]{1,0:T(8,128)}) %all-reduce.2.cloned.1.call-update) | async-done | bytes 495632 | tf_op jit(solution)/shard_map/while/body/eval_jaxpr/psum | solution.py:35
  703.6 10.7 collective-permute-done.1
  715.6 36.9 %all-reduce.2.cloned.1.call-done = f32[352,352]{1,0:T(8,128)} async-done(((f32[352,352]{1,0:T(8,128)}), f32[352,352]{1,0:T(8,128)}) %all-reduce.2.cloned.1.call-update) | async-done | bytes 495632 | tf_op jit(solution)/shard_map/while/body/eval_jaxpr/psum | solution.py:35
  774.1 36.5 %all-reduce.2.cloned.1.call-done = f32[352,352]{1,0:T(8,128)} async-done(((f32[352,352]{1,0:T(8,128)}), f32[352,352]{1,0:T(8,128)}) %all-reduce.2.cloned.1.call-update) | async-done | bytes 495632 | tf_op jit(solution)/shard_map/while/body/eval_jaxpr/psum | solution.py:35
  832.1 36.6 %all-reduce.2.cloned.1.call-done = f32[352,352]{1,0:T(8,128)} async-done(((f32[352,352]{1,0:T(8,128)}), f32[352,352]{1,0:T(8,128)}) %all-reduce.2.cloned.1.call-update) | async-done | bytes 495632 | tf_op jit(solution)/shard_map/while/body/eval_jaxpr/psum | solution.py:35
  890.3 36.6 %all-reduce.2.cloned.1.call-done = f32[352,352]{1,0:T(8,128)} async-done(((f32[352,352]{1,0:T(8,128)}), f32[352,352]{1,0:T(8,128)}) %all-reduce.2.cloned.1.call-update) | async-done | bytes 495632 | tf_op jit(solution)/shard_map/while/body/eval_jaxpr/psum | solution.py:35
  948.4 36.6 %all-reduce.2.cloned.1.call-done = f32[352,352]{1,0:T(8,128)} async-done(((f32[352,352]{1,0:T(8,128)}), f32[352,352]{1,0:T(8,128)}) %all-reduce.2.cloned.1.call-update) | async-done | bytes 495632 | tf_op jit(solution)/shard_map/while/body/eval_jaxpr/psum | solution.py:35
  1006.6 36.6 %all-reduce.2.cloned.1.call-done = f32[352,352]{1,0:T(8,128)} async-done(((f32[352,352]{1,0:T(8,128)}), f32[352,352]{1,0:T(8,128)}) %all-reduce.2.cloned.1.call-update) | async-done | bytes 495632 | tf_op jit(solution)/shard_map/while/body/eval_jaxpr/psum | solution.py:35
  1052.7 10.7 collective-permute-done.1
  1064.7 36.9 %all-reduce.2.cloned.1.call-done = f32[352,352]{1,0:T(8,128)} async-done(((f32[352,352]{1,0:T(8,128)}), f32[352,352]{1,0:T(8,128)}) %all-reduce.2.cloned.1.call-update) | async-done | bytes 495632 | tf_op jit(solution)/shard_map/while/body/eval_jaxpr/psum | solution.py:35
  1123.2 36.6 %all-reduce.2.cloned.1.call-done = f32[352,352]{1,0:T(8,128)} async-done(((f32[352,352]{1,0:T(8,128)}), f32[352,352]{1,0:T(8,128)}) %all-reduce.2.cloned.1.call-update) | async-done | bytes 495632 | tf_op jit(solution)/shard_map/while/body/eval_jaxpr/psum | solution.py:35
  1181.4 36.9 %all-reduce.2.cloned.1.call-done = f32[352,352]{1,0:T(8,128)} async-done(((f32[352,352]{1,0:T(8,128)}), f32[352,352]{1,0:T(8,128)}) %all-reduce.2.cloned.1.call-update) | async-done | bytes 495632 | tf_op jit(solution)/shard_map/while/body/eval_jaxpr/psum | solution.py:35
  1239.8 36.9 %all-reduce.2.cloned.1.call-done = f32[352,352]{1,0:T(8,128)} async-done(((f32[352,352]{1,0:T(8,128)}), f32[352,352]{1,0:T(8,128)}) %all-reduce.2.cloned.1.call-update) | async-done | bytes 495632 | tf_op jit(solution)/shard_map/while/body/eval_jaxpr/psum | solution.py:35
  1298.2 36.9 %all-reduce.2.cloned.1.call-done = f32[352,352]{1,0:T(8,128)} async-done(((f32[352,352]{1,0:T(8,128)}), f32[352,352]{1,0:T(8,128)}) %all-reduce.2.cloned.1.call-update) | async-done | bytes 495632 | tf_op jit(solution)/shard_map/while/body/eval_jaxpr/psum | solution.py:35
  1356.6 36.6 %all-reduce.2.cloned.1.call-done = f32[352,352]{1,0:T(8,128)} async-done(((f32[352,352]{1,0:T(8,128)}), f32[352,352]{1,0:T(8,128)}) %all-reduce.2.cloned.1.call-update) | async-done | bytes 495632 | tf_op jit(solution)/shard_map/while/body/eval_jaxpr/psum | solution.py:35
  1414.8 36.9 %all-reduce.2.cloned.1.call-done = f32[352,352]{1,0:T(8,128)} async-done(((f32[352,352]{1,0:T(8,128)}), f32[352,352]{1,0:T(8,128)}) %all-reduce.2.cloned.1.call-update) | async-done | bytes 495632 | tf_op jit(solution)/shard_map/while/body/eval_jaxpr/psum | solution.py:35
  1473.2 36.6 %all-reduce.2.cloned.1.call-done = f32[352,352]{1,0:T(8,128)} async-done(((f32[352,352]{1,0:T(8,128)}), f32[352,352]{1,0:T(8,128)}) %all-reduce.2.cloned.1.call-update) | async-done | bytes 495632 | tf_op jit(solution)/shard_map/while/body/eval_jaxpr/psum | solution.py:35
  1531.4 36.6 %all-reduce.2.cloned.1.call-done = f32[352,352]{1,0:T(8,128)} async-done(((f32[352,352]{1,0:T(8,128)}), f32[352,352]{1,0:T(8,128)}) %all-reduce.2.cloned.1.call-update) | async-done | bytes 495632 | tf_op jit(solution)/shard_map/while/body/eval_jaxpr/psum | solution.py:35
  1577.6 10.7 collective-permute-done.1
  1589.6 36.9 %all-reduce.2.cloned.1.call-done = f32[352,352]{1,0:T(8,128)} async-done(((f32[352,352]{1,0:T(8,128)}), f32[352,352]{1,0:T(8,128)}) %all-reduce.2.cloned.1.call-update) | async-done | bytes 495632 | tf_op jit(solution)/shard_map/while/body/eval_jaxpr/psum | solution.py:35
  1648.0 36.9 %all-reduce.2.cloned.1.call-done = f32[352,352]{1,0:T(8,128)} async-done(((f32[352,352]{1,0:T(8,128)}), f32[352,352]{1,0:T(8,128)}) %all-reduce.2.cloned.1.call-update) | async-done | bytes 495632 | tf_op jit(solution)/shard_map/while/body/eval_jaxpr/psum | solution.py:35
  1694.5 10.7 collective-permute-done.1
  1706.5 36.6 %all-reduce.2.cloned.1.call-done = f32[352,352]{1,0:T(8,128)} async-done(((f32[352,352]{1,0:T(8,128)}), f32[352,352]{1,0:T(8,128)}) %all-reduce.2.cloned.1.call-update) | async-done | bytes 495632 | tf_op jit(solution)/shard_map/while/body/eval_jaxpr/psum | solution.py:35
  1764.6 36.9 %all-reduce.2.cloned.1.call-done = f32[352,352]{1,0:T(8,128)} async-done(((f32[352,352]{1,0:T(8,128)}), f32[352,352]{1,0:T(8,128)}) %all-reduce.2.cloned.1.call-update) | async-done | bytes 495632 | tf_op jit(solution)/shard_map/while/body/eval_jaxpr/psum | solution.py:35
  1811.1 10.7 collective-permute-done.1
  1823.1 36.9 %all-reduce.2.cloned.1.call-done = f32[352,352]{1,0:T(8,128)} async-done(((f32[352,352]{1,0:T(8,128)}), f32[352,352]{1,0:T(8,128)}) %all-reduce.2.cloned.1.call-update) | async-done | bytes 495632 | tf_op jit(solution)/shard_map/while/body/eval_jaxpr/psum | solution.py:35
  1880.3 76.6 %psum.18 = f32[2]{0:T(128)} all-reduce(f32[2]{0:T(128)S(1)} %pad_maximum_fusion), channel_id=1, replica_groups=mesh['batch'=32,'dim'=4] {'batch'}, use_global_device_ids=true, to_apply=%region_5.6 | all-reduce | flops 2 | bytes 16 | tf_op jit(solution)/shard_map/psum | solution.py:70
  (412 shorter events, 498.0 us)
Async XLA Ops:
  8.2 44.9 %all-reduce.2.cloned.1.call-start = ((), (), s32[]{:S(2)}) async-start(), calls=%async_computation | async-start | bytes 1081344 | tf_op jit(solution)/shard_map/while/body/eval_jaxpr/psum | solution.py:35
  9.4 53.2 %collective-permute-start = (bf16[352,288]{0,1:T(8,128)(2,1)S(1)}, bf16[352,288]{0,1:T(8,128)(2,1)S(1)}, u32[]{:S(2)}, u32[]{:S(2)}) collective-permute-start(bf16[352,288]{0,1:T(8,128)(2,1)S(1)} %copy.15), channel_id=1, source_target_pairs={{0,4},{4,8},{8,12},{12,16},{16,20},{20,24},{24,28},{28,32},{32,36}... | collective-permute-start | bytes 608264 | tf_op jit(solution)/shard_map/while/body/eval_jaxpr/ppermute | solution.py:9
  73.3 38.2 %all-reduce.2.cloned.1.call-start = ((), (), s32[]{:S(2)}) async-start(), calls=%async_computation | async-start | bytes 1081344 | tf_op jit(solution)/shard_map/while/body/eval_jaxpr/psum | solution.py:35
  74.6 46.5 %collective-permute-start = (bf16[352,288]{0,1:T(8,128)(2,1)S(1)}, bf16[352,288]{0,1:T(8,128)(2,1)S(1)}, u32[]{:S(2)}, u32[]{:S(2)}) collective-permute-start(bf16[352,288]{0,1:T(8,128)(2,1)S(1)} %copy.15), channel_id=1, source_target_pairs={{0,4},{4,8},{8,12},{12,16},{16,20},{20,24},{24,28},{28,32},{32,36}... | collective-permute-start | bytes 608264 | tf_op jit(solution)/shard_map/while/body/eval_jaxpr/ppermute | solution.py:9
  131.8 38.1 %all-reduce.2.cloned.1.call-start = ((), (), s32[]{:S(2)}) async-start(), calls=%async_computation | async-start | bytes 1081344 | tf_op jit(solution)/shard_map/while/body/eval_jaxpr/psum | solution.py:35
  133.0 46.4 %collective-permute-start = (bf16[352,288]{0,1:T(8,128)(2,1)S(1)}, bf16[352,288]{0,1:T(8,128)(2,1)S(1)}, u32[]{:S(2)}, u32[]{:S(2)}) collective-permute-start(bf16[352,288]{0,1:T(8,128)(2,1)S(1)} %copy.15), channel_id=1, source_target_pairs={{0,4},{4,8},{8,12},{12,16},{16,20},{20,24},{24,28},{28,32},{32,36}... | collective-permute-start | bytes 608264 | tf_op jit(solution)/shard_map/while/body/eval_jaxpr/ppermute | solution.py:9
  191.4 46.1 %collective-permute-start = (bf16[352,288]{0,1:T(8,128)(2,1)S(1)}, bf16[352,288]{0,1:T(8,128)(2,1)S(1)}, u32[]{:S(2)}, u32[]{:S(2)}) collective-permute-start(bf16[352,288]{0,1:T(8,128)(2,1)S(1)} %copy.15), channel_id=1, source_target_pairs={{0,4},{4,8},{8,12},{12,16},{16,20},{20,24},{24,28},{28,32},{32,36}... | collective-permute-start | bytes 608264 | tf_op jit(solution)/shard_map/while/body/eval_jaxpr/ppermute | solution.py:9
  249.4 46.2 %collective-permute-start = (bf16[352,288]{0,1:T(8,128)(2,1)S(1)}, bf16[352,288]{0,1:T(8,128)(2,1)S(1)}, u32[]{:S(2)}, u32[]{:S(2)}) collective-permute-start(bf16[352,288]{0,1:T(8,128)(2,1)S(1)} %copy.15), channel_id=1, source_target_pairs={{0,4},{4,8},{8,12},{12,16},{16,20},{20,24},{24,28},{28,32},{32,36}... | collective-permute-start | bytes 608264 | tf_op jit(solution)/shard_map/while/body/eval_jaxpr/ppermute | solution.py:9
  307.6 46.1 %collective-permute-start = (bf16[352,288]{0,1:T(8,128)(2,1)S(1)}, bf16[352,288]{0,1:T(8,128)(2,1)S(1)}, u32[]{:S(2)}, u32[]{:S(2)}) collective-permute-start(bf16[352,288]{0,1:T(8,128)(2,1)S(1)} %copy.15), channel_id=1, source_target_pairs={{0,4},{4,8},{8,12},{12,16},{16,20},{20,24},{24,28},{28,32},{32,36}... | collective-permute-start | bytes 608264 | tf_op jit(solution)/shard_map/while/body/eval_jaxpr/ppermute | solution.py:9
  364.4 38.2 %all-reduce.2.cloned.1.call-start = ((), (), s32[]{:S(2)}) async-start(), calls=%async_computation | async-start | bytes 1081344 | tf_op jit(solution)/shard_map/while/body/eval_jaxpr/psum | solution.py:35
  365.6 46.5 %collective-permute-start = (bf16[352,288]{0,1:T(8,128)(2,1)S(1)}, bf16[352,288]{0,1:T(8,128)(2,1)S(1)}, u32[]{:S(2)}, u32[]{:S(2)}) collective-permute-start(bf16[352,288]{0,1:T(8,128)(2,1)S(1)} %copy.15), channel_id=1, source_target_pairs={{0,4},{4,8},{8,12},{12,16},{16,20},{20,24},{24,28},{28,32},{32,36}... | collective-permute-start | bytes 608264 | tf_op jit(solution)/shard_map/while/body/eval_jaxpr/ppermute | solution.py:9
  422.9 38.2 %all-reduce.2.cloned.1.call-start = ((), (), s32[]{:S(2)}) async-start(), calls=%async_computation | async-start | bytes 1081344 | tf_op jit(solution)/shard_map/while/body/eval_jaxpr/psum | solution.py:35
  424.1 46.5 %collective-permute-start = (bf16[352,288]{0,1:T(8,128)(2,1)S(1)}, bf16[352,288]{0,1:T(8,128)(2,1)S(1)}, u32[]{:S(2)}, u32[]{:S(2)}) collective-permute-start(bf16[352,288]{0,1:T(8,128)(2,1)S(1)} %copy.15), channel_id=1, source_target_pairs={{0,4},{4,8},{8,12},{12,16},{16,20},{20,24},{24,28},{28,32},{32,36}... | collective-permute-start | bytes 608264 | tf_op jit(solution)/shard_map/while/body/eval_jaxpr/ppermute | solution.py:9
  481.3 38.1 %all-reduce.2.cloned.1.call-start = ((), (), s32[]{:S(2)}) async-start(), calls=%async_computation | async-start | bytes 1081344 | tf_op jit(solution)/shard_map/while/body/eval_jaxpr/psum | solution.py:35
  482.5 46.4 %collective-permute-start = (bf16[352,288]{0,1:T(8,128)(2,1)S(1)}, bf16[352,288]{0,1:T(8,128)(2,1)S(1)}, u32[]{:S(2)}, u32[]{:S(2)}) collective-permute-start(bf16[352,288]{0,1:T(8,128)(2,1)S(1)} %copy.15), channel_id=1, source_target_pairs={{0,4},{4,8},{8,12},{12,16},{16,20},{20,24},{24,28},{28,32},{32,36}... | collective-permute-start | bytes 608264 | tf_op jit(solution)/shard_map/while/body/eval_jaxpr/ppermute | solution.py:9
  540.9 46.2 %collective-permute-start = (bf16[352,288]{0,1:T(8,128)(2,1)S(1)}, bf16[352,288]{0,1:T(8,128)(2,1)S(1)}, u32[]{:S(2)}, u32[]{:S(2)}) collective-permute-start(bf16[352,288]{0,1:T(8,128)(2,1)S(1)} %copy.15), channel_id=1, source_target_pairs={{0,4},{4,8},{8,12},{12,16},{16,20},{20,24},{24,28},{28,32},{32,36}... | collective-permute-start | bytes 608264 | tf_op jit(solution)/shard_map/while/body/eval_jaxpr/ppermute | solution.py:9
  599.0 46.4 %collective-permute-start = (bf16[352,288]{0,1:T(8,128)(2,1)S(1)}, bf16[352,288]{0,1:T(8,128)(2,1)S(1)}, u32[]{:S(2)}, u32[]{:S(2)}) collective-permute-start(bf16[352,288]{0,1:T(8,128)(2,1)S(1)} %copy.15), channel_id=1, source_target_pairs={{0,4},{4,8},{8,12},{12,16},{16,20},{20,24},{24,28},{28,32},{32,36}... | collective-permute-start | bytes 608264 | tf_op jit(solution)/shard_map/while/body/eval_jaxpr/ppermute | solution.py:9
  657.4 46.2 %collective-permute-start = (bf16[352,288]{0,1:T(8,128)(2,1)S(1)}, bf16[352,288]{0,1:T(8,128)(2,1)S(1)}, u32[]{:S(2)}, u32[]{:S(2)}) collective-permute-start(bf16[352,288]{0,1:T(8,128)(2,1)S(1)} %copy.15), channel_id=1, source_target_pairs={{0,4},{4,8},{8,12},{12,16},{16,20},{20,24},{24,28},{28,32},{32,36}... | collective-permute-start | bytes 608264 | tf_op jit(solution)/shard_map/while/body/eval_jaxpr/ppermute | solution.py:9
  714.3 38.2 %all-reduce.2.cloned.1.call-start = ((), (), s32[]{:S(2)}) async-start(), calls=%async_computation | async-start | bytes 1081344 | tf_op jit(solution)/shard_map/while/body/eval_jaxpr/psum | solution.py:35
  715.5 46.5 %collective-permute-start = (bf16[352,288]{0,1:T(8,128)(2,1)S(1)}, bf16[352,288]{0,1:T(8,128)(2,1)S(1)}, u32[]{:S(2)}, u32[]{:S(2)}) collective-permute-start(bf16[352,288]{0,1:T(8,128)(2,1)S(1)} %copy.15), channel_id=1, source_target_pairs={{0,4},{4,8},{8,12},{12,16},{16,20},{20,24},{24,28},{28,32},{32,36}... | collective-permute-start | bytes 608264 | tf_op jit(solution)/shard_map/while/body/eval_jaxpr/ppermute | solution.py:9
  774.0 46.1 %collective-permute-start = (bf16[352,288]{0,1:T(8,128)(2,1)S(1)}, bf16[352,288]{0,1:T(8,128)(2,1)S(1)}, u32[]{:S(2)}, u32[]{:S(2)}) collective-permute-start(bf16[352,288]{0,1:T(8,128)(2,1)S(1)} %copy.15), channel_id=1, source_target_pairs={{0,4},{4,8},{8,12},{12,16},{16,20},{20,24},{24,28},{28,32},{32,36}... | collective-permute-start | bytes 608264 | tf_op jit(solution)/shard_map/while/body/eval_jaxpr/ppermute | solution.py:9
  832.1 46.2 %collective-permute-start = (bf16[352,288]{0,1:T(8,128)(2,1)S(1)}, bf16[352,288]{0,1:T(8,128)(2,1)S(1)}, u32[]{:S(2)}, u32[]{:S(2)}) collective-permute-start(bf16[352,288]{0,1:T(8,128)(2,1)S(1)} %copy.15), channel_id=1, source_target_pairs={{0,4},{4,8},{8,12},{12,16},{16,20},{20,24},{24,28},{28,32},{32,36}... | collective-permute-start | bytes 608264 | tf_op jit(solution)/shard_map/while/body/eval_jaxpr/ppermute | solution.py:9
  890.2 46.2 %collective-permute-start = (bf16[352,288]{0,1:T(8,128)(2,1)S(1)}, bf16[352,288]{0,1:T(8,128)(2,1)S(1)}, u32[]{:S(2)}, u32[]{:S(2)}) collective-permute-start(bf16[352,288]{0,1:T(8,128)(2,1)S(1)} %copy.15), channel_id=1, source_target_pairs={{0,4},{4,8},{8,12},{12,16},{16,20},{20,24},{24,28},{28,32},{32,36}... | collective-permute-start | bytes 608264 | tf_op jit(solution)/shard_map/while/body/eval_jaxpr/ppermute | solution.py:9
  948.4 46.2 %collective-permute-start = (bf16[352,288]{0,1:T(8,128)(2,1)S(1)}, bf16[352,288]{0,1:T(8,128)(2,1)S(1)}, u32[]{:S(2)}, u32[]{:S(2)}) collective-permute-start(bf16[352,288]{0,1:T(8,128)(2,1)S(1)} %copy.15), channel_id=1, source_target_pairs={{0,4},{4,8},{8,12},{12,16},{16,20},{20,24},{24,28},{28,32},{32,36}... | collective-permute-start | bytes 608264 | tf_op jit(solution)/shard_map/while/body/eval_jaxpr/ppermute | solution.py:9
  1006.5 46.2 %collective-permute-start = (bf16[352,288]{0,1:T(8,128)(2,1)S(1)}, bf16[352,288]{0,1:T(8,128)(2,1)S(1)}, u32[]{:S(2)}, u32[]{:S(2)}) collective-permute-start(bf16[352,288]{0,1:T(8,128)(2,1)S(1)} %copy.15), channel_id=1, source_target_pairs={{0,4},{4,8},{8,12},{12,16},{16,20},{20,24},{24,28},{28,32},{32,36}... | collective-permute-start | bytes 608264 | tf_op jit(solution)/shard_map/while/body/eval_jaxpr/ppermute | solution.py:9
  1063.4 38.2 %all-reduce.2.cloned.1.call-start = ((), (), s32[]{:S(2)}) async-start(), calls=%async_computation | async-start | bytes 1081344 | tf_op jit(solution)/shard_map/while/body/eval_jaxpr/psum | solution.py:35
  1064.7 46.5 %collective-permute-start = (bf16[352,288]{0,1:T(8,128)(2,1)S(1)}, bf16[352,288]{0,1:T(8,128)(2,1)S(1)}, u32[]{:S(2)}, u32[]{:S(2)}) collective-permute-start(bf16[352,288]{0,1:T(8,128)(2,1)S(1)} %copy.15), channel_id=1, source_target_pairs={{0,4},{4,8},{8,12},{12,16},{16,20},{20,24},{24,28},{28,32},{32,36}... | collective-permute-start | bytes 608264 | tf_op jit(solution)/shard_map/while/body/eval_jaxpr/ppermute | solution.py:9
  1123.1 46.2 %collective-permute-start = (bf16[352,288]{0,1:T(8,128)(2,1)S(1)}, bf16[352,288]{0,1:T(8,128)(2,1)S(1)}, u32[]{:S(2)}, u32[]{:S(2)}) collective-permute-start(bf16[352,288]{0,1:T(8,128)(2,1)S(1)} %copy.15), channel_id=1, source_target_pairs={{0,4},{4,8},{8,12},{12,16},{16,20},{20,24},{24,28},{28,32},{32,36}... | collective-permute-start | bytes 608264 | tf_op jit(solution)/shard_map/while/body/eval_jaxpr/ppermute | solution.py:9
  1180.1 38.2 %all-reduce.2.cloned.1.call-start = ((), (), s32[]{:S(2)}) async-start(), calls=%async_computation | async-start | bytes 1081344 | tf_op jit(solution)/shard_map/while/body/eval_jaxpr/psum | solution.py:35
  1181.3 46.5 %collective-permute-start = (bf16[352,288]{0,1:T(8,128)(2,1)S(1)}, bf16[352,288]{0,1:T(8,128)(2,1)S(1)}, u32[]{:S(2)}, u32[]{:S(2)}) collective-permute-start(bf16[352,288]{0,1:T(8,128)(2,1)S(1)} %copy.15), channel_id=1, source_target_pairs={{0,4},{4,8},{8,12},{12,16},{16,20},{20,24},{24,28},{28,32},{32,36}... | collective-permute-start | bytes 608264 | tf_op jit(solution)/shard_map/while/body/eval_jaxpr/ppermute | solution.py:9
  1238.5 38.1 %all-reduce.2.cloned.1.call-start = ((), (), s32[]{:S(2)}) async-start(), calls=%async_computation | async-start | bytes 1081344 | tf_op jit(solution)/shard_map/while/body/eval_jaxpr/psum | solution.py:35
  1239.7 46.5 %collective-permute-start = (bf16[352,288]{0,1:T(8,128)(2,1)S(1)}, bf16[352,288]{0,1:T(8,128)(2,1)S(1)}, u32[]{:S(2)}, u32[]{:S(2)}) collective-permute-start(bf16[352,288]{0,1:T(8,128)(2,1)S(1)} %copy.15), channel_id=1, source_target_pairs={{0,4},{4,8},{8,12},{12,16},{16,20},{20,24},{24,28},{28,32},{32,36}... | collective-permute-start | bytes 608264 | tf_op jit(solution)/shard_map/while/body/eval_jaxpr/ppermute | solution.py:9
  1296.9 38.2 %all-reduce.2.cloned.1.call-start = ((), (), s32[]{:S(2)}) async-start(), calls=%async_computation | async-start | bytes 1081344 | tf_op jit(solution)/shard_map/while/body/eval_jaxpr/psum | solution.py:35
  1298.1 46.5 %collective-permute-start = (bf16[352,288]{0,1:T(8,128)(2,1)S(1)}, bf16[352,288]{0,1:T(8,128)(2,1)S(1)}, u32[]{:S(2)}, u32[]{:S(2)}) collective-permute-start(bf16[352,288]{0,1:T(8,128)(2,1)S(1)} %copy.15), channel_id=1, source_target_pairs={{0,4},{4,8},{8,12},{12,16},{16,20},{20,24},{24,28},{28,32},{32,36}... | collective-permute-start | bytes 608264 | tf_op jit(solution)/shard_map/while/body/eval_jaxpr/ppermute | solution.py:9
  1356.6 46.2 %collective-permute-start = (bf16[352,288]{0,1:T(8,128)(2,1)S(1)}, bf16[352,288]{0,1:T(8,128)(2,1)S(1)}, u32[]{:S(2)}, u32[]{:S(2)}) collective-permute-start(bf16[352,288]{0,1:T(8,128)(2,1)S(1)} %copy.15), channel_id=1, source_target_pairs={{0,4},{4,8},{8,12},{12,16},{16,20},{20,24},{24,28},{28,32},{32,36}... | collective-permute-start | bytes 608264 | tf_op jit(solution)/shard_map/while/body/eval_jaxpr/ppermute | solution.py:9
  1413.5 38.2 %all-reduce.2.cloned.1.call-start = ((), (), s32[]{:S(2)}) async-start(), calls=%async_computation | async-start | bytes 1081344 | tf_op jit(solution)/shard_map/while/body/eval_jaxpr/psum | solution.py:35
  1414.7 46.5 %collective-permute-start = (bf16[352,288]{0,1:T(8,128)(2,1)S(1)}, bf16[352,288]{0,1:T(8,128)(2,1)S(1)}, u32[]{:S(2)}, u32[]{:S(2)}) collective-permute-start(bf16[352,288]{0,1:T(8,128)(2,1)S(1)} %copy.15), channel_id=1, source_target_pairs={{0,4},{4,8},{8,12},{12,16},{16,20},{20,24},{24,28},{28,32},{32,36}... | collective-permute-start | bytes 608264 | tf_op jit(solution)/shard_map/while/body/eval_jaxpr/ppermute | solution.py:9
  1473.2 46.2 %collective-permute-start = (bf16[352,288]{0,1:T(8,128)(2,1)S(1)}, bf16[352,288]{0,1:T(8,128)(2,1)S(1)}, u32[]{:S(2)}, u32[]{:S(2)}) collective-permute-start(bf16[352,288]{0,1:T(8,128)(2,1)S(1)} %copy.15), channel_id=1, source_target_pairs={{0,4},{4,8},{8,12},{12,16},{16,20},{20,24},{24,28},{28,32},{32,36}... | collective-permute-start | bytes 608264 | tf_op jit(solution)/shard_map/while/body/eval_jaxpr/ppermute | solution.py:9
  1531.3 46.2 %collective-permute-start = (bf16[352,288]{0,1:T(8,128)(2,1)S(1)}, bf16[352,288]{0,1:T(8,128)(2,1)S(1)}, u32[]{:S(2)}, u32[]{:S(2)}) collective-permute-start(bf16[352,288]{0,1:T(8,128)(2,1)S(1)} %copy.15), channel_id=1, source_target_pairs={{0,4},{4,8},{8,12},{12,16},{16,20},{20,24},{24,28},{28,32},{32,36}... | collective-permute-start | bytes 608264 | tf_op jit(solution)/shard_map/while/body/eval_jaxpr/ppermute | solution.py:9
  1588.3 38.2 %all-reduce.2.cloned.1.call-start = ((), (), s32[]{:S(2)}) async-start(), calls=%async_computation | async-start | bytes 1081344 | tf_op jit(solution)/shard_map/while/body/eval_jaxpr/psum | solution.py:35
  1589.5 46.5 %collective-permute-start = (bf16[352,288]{0,1:T(8,128)(2,1)S(1)}, bf16[352,288]{0,1:T(8,128)(2,1)S(1)}, u32[]{:S(2)}, u32[]{:S(2)}) collective-permute-start(bf16[352,288]{0,1:T(8,128)(2,1)S(1)} %copy.15), channel_id=1, source_target_pairs={{0,4},{4,8},{8,12},{12,16},{16,20},{20,24},{24,28},{28,32},{32,36}... | collective-permute-start | bytes 608264 | tf_op jit(solution)/shard_map/while/body/eval_jaxpr/ppermute | solution.py:9
  1646.7 38.2 %all-reduce.2.cloned.1.call-start = ((), (), s32[]{:S(2)}) async-start(), calls=%async_computation | async-start | bytes 1081344 | tf_op jit(solution)/shard_map/while/body/eval_jaxpr/psum | solution.py:35
  1647.9 46.5 %collective-permute-start = (bf16[352,288]{0,1:T(8,128)(2,1)S(1)}, bf16[352,288]{0,1:T(8,128)(2,1)S(1)}, u32[]{:S(2)}, u32[]{:S(2)}) collective-permute-start(bf16[352,288]{0,1:T(8,128)(2,1)S(1)} %copy.15), channel_id=1, source_target_pairs={{0,4},{4,8},{8,12},{12,16},{16,20},{20,24},{24,28},{28,32},{32,36}... | collective-permute-start | bytes 608264 | tf_op jit(solution)/shard_map/while/body/eval_jaxpr/ppermute | solution.py:9
  1706.4 46.2 %collective-permute-start = (bf16[352,288]{0,1:T(8,128)(2,1)S(1)}, bf16[352,288]{0,1:T(8,128)(2,1)S(1)}, u32[]{:S(2)}, u32[]{:S(2)}) collective-permute-start(bf16[352,288]{0,1:T(8,128)(2,1)S(1)} %copy.15), channel_id=1, source_target_pairs={{0,4},{4,8},{8,12},{12,16},{16,20},{20,24},{24,28},{28,32},{32,36}... | collective-permute-start | bytes 608264 | tf_op jit(solution)/shard_map/while/body/eval_jaxpr/ppermute | solution.py:9
  1763.3 38.2 %all-reduce.2.cloned.1.call-start = ((), (), s32[]{:S(2)}) async-start(), calls=%async_computation | async-start | bytes 1081344 | tf_op jit(solution)/shard_map/while/body/eval_jaxpr/psum | solution.py:35
  1764.5 46.5 %collective-permute-start = (bf16[352,288]{0,1:T(8,128)(2,1)S(1)}, bf16[352,288]{0,1:T(8,128)(2,1)S(1)}, u32[]{:S(2)}, u32[]{:S(2)}) collective-permute-start(bf16[352,288]{0,1:T(8,128)(2,1)S(1)} %copy.15), channel_id=1, source_target_pairs={{0,4},{4,8},{8,12},{12,16},{16,20},{20,24},{24,28},{28,32},{32,36}... | collective-permute-start | bytes 608264 | tf_op jit(solution)/shard_map/while/body/eval_jaxpr/ppermute | solution.py:9
  1821.8 38.2 %all-reduce.2.cloned.1.call-start = ((), (), s32[]{:S(2)}) async-start(), calls=%async_computation | async-start | bytes 1081344 | tf_op jit(solution)/shard_map/while/body/eval_jaxpr/psum | solution.py:35
  1823.0 46.5 %collective-permute-start = (bf16[352,288]{0,1:T(8,128)(2,1)S(1)}, bf16[352,288]{0,1:T(8,128)(2,1)S(1)}, u32[]{:S(2)}, u32[]{:S(2)}) collective-permute-start(bf16[352,288]{0,1:T(8,128)(2,1)S(1)} %copy.15), channel_id=1, source_target_pairs={{0,4},{4,8},{8,12},{12,16},{16,20},{20,24},{24,28},{28,32},{32,36}... | collective-permute-start | bytes 608264 | tf_op jit(solution)/shard_map/while/body/eval_jaxpr/ppermute | solution.py:9
  (83 other events, 1373.5 us)
Sparse Core Ops, SparseCore 0:
  11.5 41.5 all-reduce.1
  76.7 34.8 all-reduce.1
  135.1 34.7 all-reduce.1
  193.2 34.7 all-reduce.1
  251.2 34.8 all-reduce.1
  309.4 34.7 all-reduce.1
  367.7 34.8 all-reduce.1
  426.2 34.8 all-reduce.1
  484.7 34.7 all-reduce.1
  542.7 34.8 all-reduce.1
  601.2 34.7 all-reduce.1
  659.2 34.8 all-reduce.1
  717.7 34.8 all-reduce.1
  775.8 34.7 all-reduce.1
  833.9 34.8 all-reduce.1
  892.0 34.8 all-reduce.1
  950.2 34.8 all-reduce.1
  1008.3 34.8 all-reduce.1
  1066.8 34.8 all-reduce.1
  1124.9 34.8 all-reduce.1
  1183.4 34.8 all-reduce.1
  1241.8 34.7 all-reduce.1
  1300.2 34.8 all-reduce.1
  1358.4 34.8 all-reduce.1
  1416.8 34.8 all-reduce.1
  1475.0 34.8 all-reduce.1
  1533.1 34.8 all-reduce.1
  1591.6 34.8 all-reduce.1
  1650.0 34.8 all-reduce.1
  1708.2 34.8 all-reduce.1
  1766.7 34.8 all-reduce.1
  1825.1 34.8 all-reduce.1
where the time goes:
time: 1980 us; the launch traced here: 1960 us
  waiting for transfers between devices  1520 us (77%)
  matrix products  184 us (9%)
  blocking collectives  76.6 us (4%)
  other arithmetic  73.9 us (4%)
  loops' own time  44.7 us (2%)
  starting transfers between devices  44.7 us (2%)
    psum x32, waiting for transfers between devices, patch_coefficients(): similar = lax.psum(pair_dot(picture_embeds, caption_slice), 'dim')  1180 us
    ppermute x64, waiting for transfers between devices, from_behind(): lax.ppermute(array, axis, [(i, (i + by) % devices) for i in range(devices)])  342 us
    dot_general x32, matrix products, carried_rotation(): lax.dot_general(coeff_low, picture_embeds, (((0,), (0,)), ((), ())), pref...  89.9 us
    psum x1, blocking collectives, body(): scalar_grads = lax.psum(local_pair, 'batch')  76.6 us
    reduce_sum x32, other arithmetic, coefficients(): return (coeff, jnp.sum(coeff * similar), jnp.sum(coeff))  73.8 us
    dot_general x32, matrix products, carried_rotation(): jnp.dot(coeff_low, caption_slice, preferred_element_type=jnp.float32)  56.7 us
    another operation x1, loops' own time, body(): final = lax.fori_loop(0, cycle_size, carried_rotation, start)  44.7 us
    ppermute x64, starting transfers between devices, from_behind(): lax.ppermute(array, axis, [(i, (i + by) % devices) for i in range(devices)])  44.6 us
  transfers between devices with their start and end apart: 96, of which 64 were waited for; matrix products, arithmetic and copies ran while one was open for 11% of the time, Pallas kernels for 0%

commit v1 on v0

v1 whole, which is shorter than its diff:
```python
import functools

import jax
import jax.numpy as jnp
from jax import lax
from jax.experimental import pallas as pl
from jax.experimental.pallas import tpu as pltpu
from jax.sharding import PartitionSpec as P

BF = jnp.bfloat16
F32 = jnp.float32
AXES = ("batch", "dim")
CORE = 1


def x_mask(k):
    return k << 2


def y_mask(k):
    return k << 4


def z_mask(k):
    return ((k >> 1) << 6) | ((k & 1) << 1)


def swap(array, mask0, mask1=None):
    mask1 = mask0 if mask1 is None else mask1
    n = lax.axis_size("batch") * lax.axis_size("dim")
    return lax.ppermute(array, AXES, [(i, i ^ (mask1 if i & 1 else mask0)) for i in range(n)])


LOW = 2.0**-3.5


def encode(v, m):
    a = jnp.abs(v) * (127.0 * LOW / m) + LOW
    for _ in range(5):
        a = a * a
    return jnp.where(v < 0, -a, a)


def decode(code, m):
    c = code.astype(F32)
    a = jnp.exp(jnp.log(jnp.abs(c)) * (1.0 / 32.0)) * (1.0 / LOW) - 1.0
    v = a * (m * (1.0 / 127.0))
    return jnp.where(c < 0, -v, v)


def top_of(largest):
    return (largest * 1.01 + 1e-30).astype(BF).astype(F32)


def tile_kernel(
    rows, half, feats,
    core_ref, scale_ref, text_ids, image_ids, own_ref, t1_ref, t2_ref, t3_ref, im0_ref, im1_ref,
    text_own, m1_ref, m2_ref, m3_ref, img0_ref, img1_ref, sums_ref,
    texts, images, t_rel, coeff_low, grads, img_acc, sems,
):
    core = core_ref[0]
    scaling, offset = scale_ref[0], scale_ref[1]
    quarter = 4 * rows
    copies = [
        pltpu.make_async_copy(src, texts.at[j], sems.at[j])
        for j, src in enumerate((own_ref, t1_ref, t2_ref, t3_ref))
    ] + [
        pltpu.make_async_copy(src, images.at[pl.ds(o * quarter, quarter)], sems.at[4 + o])
        for o, src in enumerate((im0_ref, im1_ref))
    ]
    for copy in copies:
        copy.start()
    for copy in copies:
        copy.wait()
    img_acc[...] = jnp.zeros_like(img_acc)
    step = 2 * rows

    def chunk(zp, sums):
        def build(yo, carry):
            def block(zo):
                return texts[jnp.where(core == 0, zo, yo), jnp.where(core == 0, yo, zo)].astype(F32)

            p0, p1 = block(2 * zp), block(2 * zp + 1)
            top = jnp.concatenate([p0[:, :half], p1[:, :half]], axis=1)
            bottom = jnp.concatenate([p0[:, half:], p1[:, half:]], axis=1)
            at = pl.ds(pl.multiple_of(yo * step, 16), step)
            t_rel[at, :] = jnp.concatenate([top, bottom], axis=0).astype(BF)
            return carry

        lax.fori_loop(0, 4, build, 0)
        similar = lax.dot_general(
            t_rel[...], images[...], (((1,), (1,)), ((), ())), preferred_element_type=F32
        )
        logits = scaling * similar + offset
        matched = text_ids[zp] == image_ids[...]
        signed = jnp.where(matched, -logits, logits)
        sig = 1.0 / (1.0 + jnp.exp(-signed))
        coeff = jnp.where(matched, -sig, sig)
        coeff_low[...] = coeff.astype(BF)
        temp = sums[0] + jnp.sum(coeff * similar, axis=0, keepdims=True)
        bias = sums[1] + jnp.sum(coeff, axis=0, keepdims=True)
        text_part = jnp.dot(coeff_low[...], images[...], preferred_element_type=F32)
        for yo in range(4):
            top = text_part[yo * step : yo * step + rows]
            bottom = text_part[yo * step + rows : (yo + 1) * step]
            grads[2 * zp, yo] = jnp.concatenate([top[:, :half], bottom[:, :half]], axis=1)
            grads[2 * zp + 1, yo] = jnp.concatenate([top[:, half:], bottom[:, half:]], axis=1)
        img_acc[...] += lax.dot_general(
            coeff_low[...], t_rel[...], (((0,), (0,)), ((), ())), preferred_element_type=F32
        )
        return (temp, bias)

    zero = jnp.zeros((1, 2 * quarter), F32)
    temp, bias = lax.fori_loop(0, 2, chunk, (zero, zero))
    sums_ref[...] = jnp.concatenate(
        [jnp.broadcast_to(jnp.sum(v, axis=1, keepdims=True), (4, 128)) for v in (temp, bias)], axis=0
    )
    img0_ref[...] = img_acc[0:quarter]
    img1_ref[...] = img_acc[quarter : 2 * quarter]

    def grad_block(j, i):
        return grads[jnp.where(core == 0, j, i), jnp.where(core == 0, i, j)]

    for i in range(4):
        text_own[i] = grad_block(0, i)
    for j, m_ref in ((1, m1_ref), (2, m2_ref), (3, m3_ref)):
        whole = jnp.concatenate([grad_block(j, i) for i in range(4)], axis=0)
        m = top_of(jnp.max(jnp.max(jnp.abs(whole), axis=0, keepdims=True), axis=1, keepdims=True))
        m_ref[0:quarter, :] = encode(whole, m).astype(BF)
        m_ref[quarter : quarter + 16, :] = jnp.broadcast_to(m, (16, feats)).astype(BF)


def first_sum_kernel(rows, feats, own_ref, r1_ref, r2_ref, r3_ref, out_ref, m1_ref, m2_ref, m3_ref):
    quarter = 4 * rows
    received = [(r[0:quarter], r[quarter : quarter + 16].astype(F32)[0:1, :]) for r in (r1_ref, r2_ref, r3_ref)]
    total = jnp.concatenate([own_ref[i] for i in range(4)], axis=0)
    for code, m in received:
        total = total + decode(code, m)
    out_ref[...] = total[0:rows]
    for i, m_ref in ((1, m1_ref), (2, m2_ref), (3, m3_ref)):
        part = total[i * rows : (i + 1) * rows]
        m = top_of(jnp.max(jnp.max(jnp.abs(part), axis=0, keepdims=True), axis=1, keepdims=True))
        m_ref[...] = jnp.concatenate([encode(part, m), jnp.broadcast_to(m, (16, feats))], axis=0).astype(BF)


def last_sum_kernel(rows, scale_ref, own_ref, r1_ref, r2_ref, r3_ref, out_ref):
    total = own_ref[...]
    for r in (r1_ref, r2_ref, r3_ref):
        whole = r[...].astype(F32)
        total = total + decode(whole[0:rows], whole[rows : rows + 1])
    out_ref[...] = total * scale_ref[0]


VMEM = pl.BlockSpec(memory_space=pltpu.VMEM)
SMEM = pl.BlockSpec(memory_space=pltpu.SMEM)
HBM = pl.BlockSpec(memory_space=pl.ANY)
BIG = pltpu.CompilerParams(vmem_limit_bytes=56 * 1024 * 1024)


def body(picture_embeds, caption_embeds, logit_scaler, logit_offset_term):
    height, width = picture_embeds.shape
    rows, half, feats = height // 4, 2 * width, 4 * width
    step, quarter = 2 * rows, 4 * rows
    index = lax.axis_index("batch") * lax.axis_size("dim") + lax.axis_index("dim")
    core, z_lo = index & 1, (index >> 1) & 1
    on0, lo0 = core == 0, z_lo == 0
    scaling = logit_scaler[0]

    def by_core(first, second):
        return jnp.where(on0, first, second), jnp.where(on0, second, first)

    keep, send = by_core(caption_embeds[:step], caption_embeds[step:])
    got = swap(send, CORE)
    chip = jnp.concatenate(by_core(keep, got), axis=1)
    packed = jnp.concatenate([chip[:rows], chip[rows:]], axis=1)
    dim = index & 3
    parts = [lax.dynamic_slice(picture_embeds, (rows * (dim ^ q), 0), (rows, width)) for q in range(4)]
    parts = [parts[0]] + [swap(parts[q], q) for q in range(1, 4)]
    image = jnp.concatenate(by_core(parts[0], parts[1]) + by_core(parts[2], parts[3]), axis=1)

    first = [packed] + [swap(packed, y_mask(i), z_mask(i)) for i in range(1, 4)]
    images_own = jnp.concatenate([image] + [swap(image, x_mask(k)) for k in range(1, 4)], axis=0)
    stack = jnp.stack(first)
    images_other = swap(images_own, CORE)
    second = [stack] + [swap(stack, z_mask(j), y_mask(j)) for j in range(1, 4)]

    batch = index >> 2
    zh_bit, x_of = lax.axis_size("batch") // 2, batch & 3
    r = jnp.arange(step, dtype=jnp.int32)
    text_ids = jnp.concatenate(
        [(batch ^ (zp * zh_bit) ^ (yo << 2)) * height + step * core + r for zp in range(2) for yo in range(4)]
    ).reshape(2, 4 * step, 1)
    r = jnp.arange(rows, dtype=jnp.int32)
    image_ids = jnp.concatenate(
        [(batch ^ k) * height + rows * (2 * z_lo + (core ^ o)) + r for o in range(2) for k in range(4)]
    ).reshape(1, 2 * quarter)

    message = jax.ShapeDtypeStruct((quarter + 16, feats), BF)
    text_own, m1, m2, m3, img_own, img_other, sums = pl.pallas_call(
        functools.partial(tile_kernel, rows, half, feats),
        out_shape=(
            jax.ShapeDtypeStruct((4, rows, feats), F32), message, message, message,
            jax.ShapeDtypeStruct((quarter, feats), F32), jax.ShapeDtypeStruct((quarter, feats), F32),
            jax.ShapeDtypeStruct((8, 128), F32),
        ),
        in_specs=[SMEM, SMEM, VMEM, VMEM] + [HBM] * 6,
        out_specs=(VMEM,) * 7,
        scratch_shapes=[
            pltpu.VMEM((4, 4, rows, feats), BF),
            pltpu.VMEM((2 * quarter, feats), BF),
            pltpu.VMEM((4 * step, feats), BF),
            pltpu.VMEM((4 * step, 2 * quarter), BF),
            pltpu.VMEM((4, 4, rows, feats), F32),
            pltpu.VMEM((2 * quarter, feats), F32),
            pltpu.SemaphoreType.DMA((6,)),
        ],
        compiler_params=BIG,
        name="tile",
    )(core.reshape(1), jnp.stack([scaling, logit_offset_term[0]]), text_ids, image_ids, *second, images_own, images_other)

    got = [swap(m, z_mask(j), y_mask(j)) for j, m in ((1, m1), (2, m2), (3, m3))]
    img = img_own + swap(img_other, CORE)
    img = img.reshape(4, rows, feats)
    img_got = [swap(img[k], x_mask(k)) for k in range(1, 4)]

    message = jax.ShapeDtypeStruct((rows + 16, feats), BF)
    text, n1, n2, n3 = pl.pallas_call(
        functools.partial(first_sum_kernel, rows, feats),
        out_shape=(jax.ShapeDtypeStruct((rows, feats), F32), message, message, message),
        in_specs=[VMEM] * 4,
        out_specs=(VMEM,) * 4,
        compiler_params=BIG,
        name="first_sum",
    )(text_own, *got)
    got = [swap(m, y_mask(i), z_mask(i)) for i, m in ((1, n1), (2, n2), (3, n3))]

    img = scaling * (img[0] + img_got[0] + img_got[1] + img_got[2])
    quarters = by_core(img[:, :width], img[:, width:half]) + by_core(img[:, half : half + width], img[:, half + width :])
    back = [quarters[0]] + [swap(quarters[q], q) for q in range(1, 4)]
    back = list(by_core(back[0], back[1]) + by_core(back[2], back[3]))
    back = [jnp.where(lo0, back[e], back[e ^ 2]) for e in range(4)]
    image_grad = jnp.concatenate(back, axis=0)

    for mask in (CORE, x_mask(1), x_mask(2), y_mask(1), y_mask(2), z_mask(1), z_mask(2)):
        sums = sums + swap(sums, mask)
    scalar_grads = jnp.stack([sums[0, 0], sums[4, 0]])

    text = pl.pallas_call(
        functools.partial(last_sum_kernel, rows),
        out_shape=jax.ShapeDtypeStruct((rows, feats), F32),
        in_specs=[SMEM] + [VMEM] * 4,
        out_specs=VMEM,
        compiler_params=BIG,
        name="last_sum",
    )(logit_scaler, text, *got)
    chip = jnp.concatenate([text[:, :half], text[:, half:]], axis=0)
    mine, other = by_core(chip[:, :width], chip[:, width:])
    text_grad = jnp.concatenate(by_core(mine, swap(other, CORE)), axis=0)
    return (image_grad, text_grad, scalar_grads)


def solution(mesh):
    placed = (P("batch", "dim"), P("batch", "dim"), P(), P())
    return jax.shard_map(
        body,
        mesh=mesh,
        in_specs=placed,
        out_specs=(P("batch", "dim"), P("batch", "dim"), P()),
        check_vma=False,
    )
```

time: 1980 us -> 170 us (0.09)
  waiting for transfers between devices: 1520 us -> 71.5 us
  matrix products: 184 us -> 0 us
  blocking collectives: 76.6 us -> 0 us
  other arithmetic: 73.9 us -> 4.7 us
  loops' own time: 44.7 us -> 0 us
  Pallas kernels: 0 us -> 30.6 us
    psum x32 -> x0, waiting for transfers between devices: 1180 us -> none  [patch_coefficients(): similar = lax.psum(pair_dot(picture_embeds, caption_slice), 'dim')]
    ppermute x64 -> x35, waiting for transfers between devices: 342 us -> 71.5 us  [swap(): lax.ppermute(array, AXES, [(i, i ^ (mask1 if i & 1 else mask0)) for i in...]
    dot_general x96 -> x0, matrix products: 184 us -> none  [the longest x32 89.9 us: carried_rotation(): lax.dot_general(coeff_low, picture_embeds, (((0,), (0,)), ((), ())), pref...]
    psum x1 -> x0, blocking collectives: 76.6 us -> none  [body(): scalar_grads = lax.psum(local_pair, 'batch')]
    reduce_sum x32 -> x0, other arithmetic: 73.8 us -> none  [coefficients(): return (coeff, jnp.sum(coeff * similar), jnp.sum(coeff))]
    another operation x1 -> x0, loops' own time: 44.7 us -> none  [body(): final = lax.fori_loop(0, cycle_size, carried_rotation, start)]
    pallas_call x0 -> x3, Pallas kernels: none -> 30.6 us  [the longest x1 21.1 us: body(): pl.pallas_call(functools.partial(tile_kernel, rows, half, feats), out_sha...]
    ppermute x64 -> x35, starting transfers between devices: 44.6 us -> 49.5 us  [swap(): lax.ppermute(array, AXES, [(i, i ^ (mask1 if i & 1 else mask0)) for i in...]
  transfers between devices with their start and end apart: 96 -> 35, of which waited for: 64 -> 19; matrix products, arithmetic and copies ran while one was open for 11% -> 7% of each run, Pallas kernels for 0% -> 6%
where the time goes in v1:
time: 170 us; the launch traced here: 169 us
  waiting for transfers between devices  71.5 us (42%)
  starting transfers between devices  49.5 us (29%)
  Pallas kernels  30.6 us (18%)
  local copies, waits for them, and re-layouts  10.9 us (6%)
  other arithmetic  4.7 us (3%)
  between operations  2.29 us (1%)
    ppermute x35, waiting for transfers between devices, swap(): lax.ppermute(array, AXES, [(i, i ^ (mask1 if i & 1 else mask0)) for i in...  71.5 us
    ppermute x35, starting transfers between devices, swap(): lax.ppermute(array, AXES, [(i, i ^ (mask1 if i & 1 else mask0)) for i in...  49.5 us
    pallas_call x1, Pallas kernels, body(): pl.pallas_call(functools.partial(tile_kernel, rows, half, feats), out_sha...  21.1 us
    pallas_call x1, Pallas kernels, body(): pl.pallas_call(functools.partial(first_sum_kernel, rows, feats), out_shap...  6.9 us
    unnamed x26, local copies, waits for them, and re-layouts  4.36 us
  transfers between devices with their start and end apart: 35, of which 19 were waited for; matrix products, arithmetic and copies ran while one was open for 7% of the time, Pallas kernels for 6%

profile of v1, /device:TPU:1, one launch (start us, length us, event | category | flops | bytes accessed | tf_op | source)
XLA Modules:
  0.0 169.5 jit_solution(17877332204964600893)
XLA Ops:
  0.7 1.3 constant_dynamic-slice_fusion
  2.0 1.5 collective-permute-start.7
  3.6 1.8 %collective-permute-start.8 = (bf16[88,288]{1,0:T(8,128)(2,1)S(1)}, bf16[88,288]{1,0:T(8,128)(2,1)S(1)}, u32[]{:S(2)}, u32[]{:S(2)}) collective-permute-start(bf16[88,288]{1,0:T(8,128)(2,1)S(1)} %copy.28), channel_id=1, source_target_pairs={{0,2},{1,3},{2,0},{3,1},{4,6},{5,7},{6,4},{7,5},{8,10},{9,11},{10,... | collective-permute-start | bytes 152072 | tf_op jit(solution)/shard_map/ppermute | solution.py:31
  5.7 1.1 fusion.8
  7.9 1.8 %collective-permute-done.9 = bf16[88,288]{1,0:T(8,128)(2,1)S(1)} collective-permute-done((bf16[88,288]{1,0:T(8,128)(2,1)S(1)}, bf16[88,288]{1,0:T(8,128)(2,1)S(1)}, u32[]{:S(2)}, u32[]{:S(2)}) %collective-permute-start.9) | collective-permute-done | bytes 50720 | tf_op jit(solution)/shard_map/ppermute | solution.py:31
  9.9 2.6 %collective-permute-start.12 = (bf16[88,1152]{1,0:T(8,128)(2,1)S(1)}, bf16[88,1152]{1,0:T(8,128)(2,1)S(1)}, u32[]{:S(2)}, u32[]{:S(2)}) collective-permute-start(bf16[88,1152]{1,0:T(8,128)(2,1)S(1)} %concatenate.31), channel_id=1, source_target_pairs={{0,12},{1,13},{2,14},{3,15},{4,8},{5,9},{6,10},{7,11},{8,4},{9,5},... | collective-permute-start | bytes 608264 | tf_op jit(solution)/shard_map/ppermute | solution.py:31
  13.5 3.3 %collective-permute-start.3 = (bf16[88,1152]{1,0:T(8,128)(2,1)S(1)}, bf16[88,1152]{1,0:T(8,128)(2,1)S(1)}, u32[]{:S(2)}, u32[]{:S(2)}) collective-permute-start(bf16[88,1152]{1,0:T(8,128)(2,1)S(1)} %fusion.4), channel_id=1, source_target_pairs={{0,48},{1,67},{2,50},{3,65},{4,52},{5,71},{6,54},{7,69},{8,56},{9,... | collective-permute-start | bytes 608264 | tf_op jit(solution)/shard_map/ppermute | solution.py:31
  17.0 4.4 %collective-permute-done.12 = bf16[88,1152]{1,0:T(8,128)(2,1)S(1)} collective-permute-done((bf16[88,1152]{1,0:T(8,128)(2,1)S(1)}, bf16[88,1152]{1,0:T(8,128)(2,1)S(1)}, u32[]{:S(2)}, u32[]{:S(2)}) %collective-permute-start.12) | collective-permute-done | bytes 202784 | tf_op jit(solution)/shard_map/ppermute | solution.py:31
  21.4 1.4 collective-permute-start.1
  22.8 1.9 %collective-permute-start.13 = (bf16[352,1152]{1,0:T(8,128)(2,1)S(1)}, bf16[352,1152]{1,0:T(8,128)(2,1)S(1)}, u32[]{:S(2)}, u32[]{:S(2)}) collective-permute-start(bf16[352,1152]{1,0:T(8,128)(2,1)S(1)} %pad_maximum_fusion.1.im0_ref), channel_id=1, source_target_pairs={{0,1},{1,0},{2,3},{3,2},{4,5},{5,4},{6,7},{7,6},{8,9},{9,8},{10,11... | collective-permute-start | bytes 2433032 | tf_op jit(solution)/shard_map/ppermute | solution.py:31
  24.7 1.5 collective-permute-done.1
  26.4 2.8 %collective-permute-start.6 = (bf16[4,88,1152]{2,1,0:T(8,128)(2,1)S(1)}, bf16[4,88,1152]{2,1,0:T(8,128)(2,1)S(1)}, u32[]{:S(2)}, u32[]{:S(2)}) collective-permute-start(bf16[4,88,1152]{2,1,0:T(8,128)(2,1)S(1)} %pad_maximum_fusion.own_ref), channel_id=1, source_target_pairs={{0,66},{1,49},{2,64},{3,51},{4,70},{5,53},{6,68},{7,55},{8,74},{9,... | collective-permute-start | bytes 2433032 | tf_op jit(solution)/shard_map/ppermute | solution.py:31
  32.0 1.4 reshape.27.text_ids
  34.0 13.8 %collective-permute-done.6.t3_ref = bf16[4,88,1152]{2,1,0:T(8,128)(2,1)S(1)} collective-permute-done((bf16[4,88,1152]{2,1,0:T(8,128)(2,1)S(1)}, bf16[4,88,1152]{2,1,0:T(8,128)(2,1)S(1)}, u32[]{:S(2)}, u32[]{:S(2)}) %collective-permute-start.6) | collective-permute-done | bytes 811040 | tf_op jit(solution)/shard_map/ppermute | solution.py:31
  47.8 0.8 collective-permute-done.4.t1_ref
  48.7 21.1 %tile.1 = (f32[4,88,1152]{2,1,0:T(8,128)}, bf16[368,1152]{1,0:T(8,128)(2,1)}, bf16[368,1152]{1,0:T(8,128)(2,1)}, bf16[368,1152]{1,0:T(8,128)(2,1)}, f32[352,1152...) custom-call(s32[1]{0:T(128)} %bitcast.1.core_ref, f32[2]{0:T(128)} %pad_maximum_fusion.6.scale_ref, ...), custom_call_target="tpu_custom_call" | custom-call | tf_op jit(solution)/shard_map/tile/pallas_call | solution.py:199
  69.8 3.8 %collective-permute-start.14 = (f32[352,1152]{1,0:T(8,128)}, f32[352,1152]{1,0:T(8,128)S(1)}, u32[]{:S(2)}, u32[]{:S(2)}) collective-permute-start(f32[352,1152]{1,0:T(8,128)} %get-tuple-element.15), channel_id=1, source_target_pairs={{0,1},{1,0},{2,3},{3,2},{4,5},{5,4},{6,7},{7,6},{8,9},{9,8},{10,11... | collective-permute-start | bytes 4866056 | tf_op jit(solution)/shard_map/ppermute | solution.py:31
  73.5 1.3 collective-permute-start.21
  74.8 2.6 %collective-permute-start.22 = (bf16[368,1152]{1,0:T(8,128)(2,1)}, bf16[368,1152]{1,0:T(8,128)(2,1)S(1)}, u32[]{:S(2)}, u32[]{:S(2)}) collective-permute-start(bf16[368,1152]{1,0:T(8,128)(2,1)} %get-tuple-element.18), channel_id=1, source_target_pairs={{0,64},{1,33},{2,66},{3,35},{4,68},{5,37},{6,70},{7,39},{8,72},{9,... | collective-permute-start | bytes 2543624 | tf_op jit(solution)/shard_map/ppermute | solution.py:31
  77.5 0.9 collective-permute-start.28
  78.3 1.0 collective-permute-done.28
  80.1 2.7 %collective-permute-done.29 = f32[8,128]{1,0:T(8,128)S(1)} collective-permute-done((f32[8,128]{1,0:T(8,128)S(1)}, f32[8,128]{1,0:T(8,128)S(1)}, u32[]{:S(2)}, u32[]{:S(2)}) %collective-permute-start.29) | collective-permute-done | bytes 4128 | tf_op jit(solution)/shard_map/ppermute | solution.py:31
  82.8 2.2 %collective-permute-start.30 = (f32[8,128]{1,0:T(8,128)S(1)}, f32[8,128]{1,0:T(8,128)S(1)}, u32[]{:S(2)}, u32[]{:S(2)}) collective-permute-start(f32[8,128]{1,0:T(8,128)S(1)} %add.264), channel_id=1, source_target_pairs={{0,8},{1,9},{2,10},{3,11},{4,12},{5,13},{6,14},{7,15},{8,0},{9,1},... | collective-permute-start | bytes 12296 | tf_op jit(solution)/shard_map/ppermute | solution.py:31
  85.0 1.8 %collective-permute-done.30 = f32[8,128]{1,0:T(8,128)S(1)} collective-permute-done((f32[8,128]{1,0:T(8,128)S(1)}, f32[8,128]{1,0:T(8,128)S(1)}, u32[]{:S(2)}, u32[]{:S(2)}) %collective-permute-start.30) | collective-permute-done | bytes 4128 | tf_op jit(solution)/shard_map/ppermute | solution.py:31
  86.8 1.3 collective-permute-start.31
  88.1 9.1 %collective-permute-done.22.r2_ref = bf16[368,1152]{1,0:T(8,128)(2,1)S(1)} collective-permute-done((bf16[368,1152]{1,0:T(8,128)(2,1)}, bf16[368,1152]{1,0:T(8,128)(2,1)S(1)}, u32[]{:S(2)}, u32[]{:S(2)}) %collective-permute-start.22) | collective-permute-done | bytes 847904 | tf_op jit(solution)/shard_map/ppermute | solution.py:31
  97.2 2.6 %collective-permute-done.23.r3_ref = bf16[368,1152]{1,0:T(8,128)(2,1)S(1)} collective-permute-done((bf16[368,1152]{1,0:T(8,128)(2,1)}, bf16[368,1152]{1,0:T(8,128)(2,1)S(1)}, u32[]{:S(2)}, u32[]{:S(2)}) %collective-permute-start.23) | collective-permute-done | bytes 847904 | tf_op jit(solution)/shard_map/ppermute | solution.py:31
  99.8 0.9 copy-done.5
  100.7 6.9 %first_sum.1 = (f32[88,1152]{1,0:T(8,128)}, bf16[104,1152]{1,0:T(8,128)(2,1)}, bf16[104,1152]{1,0:T(8,128)(2,1)}, bf16[104,1152]{1,0:T(8,128)(2,1)}) custom-call(f32[4,88,1152]{2,1,0:T(8,128)} %get-tuple-element.16.own_ref, bf16[368,1152]{1,0:T(8,128)(2,1)} %copy-done.3, bf16[368,1152]{1,0:T(8,128)(2,1)} %copy-done.4, bf16[368,1152]{1,0:T(8,128)(2,1)} %copy-done.5), custom_call_target="tpu_custom_call" | custom-call | tf_op jit(solution)/shard_map/first_sum/pallas_call | solution.py:227
  108.3 3.0 %collective-permute-start.25 = (bf16[104,1152]{1,0:T(8,128)(2,1)}, bf16[104,1152]{1,0:T(8,128)(2,1)}, u32[]{:S(2)}, u32[]{:S(2)}) collective-permute-start(bf16[104,1152]{1,0:T(8,128)(2,1)} %get-tuple-element.22), channel_id=1, source_target_pairs={{0,32},{1,65},{2,34},{3,67},{4,36},{5,69},{6,38},{7,71},{8,40},{9,... | collective-permute-start | bytes 718856 | tf_op jit(solution)/shard_map/ppermute | solution.py:31
  111.5 4.0 %collective-permute-done.32 = f32[8,128]{1,0:T(8,128)S(1)} collective-permute-done((f32[8,128]{1,0:T(8,128)S(1)}, f32[8,128]{1,0:T(8,128)S(1)}, u32[]{:S(2)}, u32[]{:S(2)}) %collective-permute-start.32) | collective-permute-done | bytes 4128 | tf_op jit(solution)/shard_map/ppermute | solution.py:31
  115.4 2.9 %collective-permute-done.33 = f32[8,128]{1,0:T(8,128)S(1)} collective-permute-done((f32[8,128]{1,0:T(8,128)S(1)}, f32[8,128]{1,0:T(8,128)S(1)}, u32[]{:S(2)}, u32[]{:S(2)}) %collective-permute-start.33) | collective-permute-done | bytes 4128 | tf_op jit(solution)/shard_map/ppermute | solution.py:31
  118.3 2.8 %collective-permute-start.34 = (f32[8,128]{1,0:T(8,128)S(1)}, f32[8,128]{1,0:T(8,128)S(1)}, u32[]{:S(2)}, u32[]{:S(2)}) collective-permute-start(f32[8,128]{1,0:T(8,128)S(1)} %add.268), channel_id=1, source_target_pairs={{0,64},{1,65},{2,66},{3,67},{4,68},{5,69},{6,70},{7,71},{8,72},{9,... | collective-permute-start | bytes 12296 | tf_op jit(solution)/shard_map/ppermute | solution.py:31
  121.1 1.2 collective-permute-done.34
  122.8 1.8 %pad_maximum_fusion.7 = f32[2]{0:T(128)} fusion(f32[1]{0:T(128)} %bitcast.7, f32[1]{0:T(128)} %bitcast.6), kind=kLoop, calls=%fused_computation.54 | loop fusion | flops 2 | bytes 16 | tf_op jit(solution)/shard_map/stack | solution.py:246
  125.4 2.6 %last_sum.1 = f32[88,1152]{1,0:T(8,128)} custom-call(f32[1]{0:T(128)} %copy.30.scale_ref, f32[88,1152]{1,0:T(8,128)} %get-tuple-element.20.own_ref, bf16[104,1152]{1,0:T(8,128)(2,1)} %copy-done.8, bf16[104,1152]{1,0:T(8,128)(2,1)} %collective-permute-done.25.r2_ref, bf16[104,1152]{1,0:T(8,128)(2,1)} %collective-permute-done.26.r3_ref), custom_call_target="tpu_custom_call" | custom-call | tf_op jit(solution)/shard_map/last_sum/pallas_call | solution.py:248
  128.0 1.2 fusion.7
  129.4 7.4 %collective-permute-start.27 = (f32[176,288]{1,0:T(8,128)S(1)}, f32[176,288]{1,0:T(8,128)S(1)}, u32[]{:S(2)}, u32[]{:S(2)}) collective-permute-start(f32[176,288]{1,0:T(8,128)S(1)} %broadcast_select_fusion.2), channel_id=1, source_target_pairs={{0,1},{1,0},{2,3},{3,2},{4,5},{5,4},{6,7},{7,6},{8,9},{9,8},{10,11... | collective-permute-start | bytes 608264 | tf_op jit(solution)/shard_map/ppermute | solution.py:31
  137.1 2.6 %collective-permute-start.17 = (f32[88,1152]{1,0:T(8,128)S(1)}, f32[88,1152]{1,0:T(8,128)S(1)}, u32[]{:S(2)}, u32[]{:S(2)}) collective-permute-start(f32[88,1152]{1,0:T(8,128)S(1)} %get-tuple-element.36), channel_id=1, source_target_pairs={{0,12},{1,13},{2,14},{3,15},{4,8},{5,9},{6,10},{7,11},{8,4},{9,5},... | collective-permute-start | bytes 1216520 | tf_op jit(solution)/shard_map/ppermute | solution.py:31
  139.7 1.1 collective-permute-start.16
  140.9 7.1 %collective-permute-done.15 = f32[88,1152]{1,0:T(8,128)S(1)} collective-permute-done((f32[88,1152]{1,0:T(8,128)S(1)}, f32[88,1152]{1,0:T(8,128)S(1)}, u32[]{:S(2)}, u32[]{:S(2)}) %collective-permute-start.15) | collective-permute-done | bytes 405536 | tf_op jit(solution)/shard_map/ppermute | solution.py:31
  148.1 8.9 %collective-permute-done.17 = f32[88,1152]{1,0:T(8,128)S(1)} collective-permute-done((f32[88,1152]{1,0:T(8,128)S(1)}, f32[88,1152]{1,0:T(8,128)S(1)}, u32[]{:S(2)}, u32[]{:S(2)}) %collective-permute-start.17) | collective-permute-done | bytes 405536 | tf_op jit(solution)/shard_map/ppermute | solution.py:31
  157.0 2.0 %collective-permute-done.16 = f32[88,1152]{1,0:T(8,128)S(1)} collective-permute-done((f32[88,1152]{1,0:T(8,128)S(1)}, f32[88,1152]{1,0:T(8,128)S(1)}, u32[]{:S(2)}, u32[]{:S(2)}) %collective-permute-start.16) | collective-permute-done | bytes 405536 | tf_op jit(solution)/shard_map/ppermute | solution.py:31
  159.8 1.7 %collective-permute-start.19 = (f32[88,288]{1,0:T(8,128)S(1)}, f32[88,288]{1,0:T(8,128)S(1)}, u32[]{:S(2)}, u32[]{:S(2)}) collective-permute-start(f32[88,288]{1,0:T(8,128)S(1)} %get-tuple-element.44), channel_id=1, source_target_pairs={{0,2},{1,3},{2,0},{3,1},{4,6},{5,7},{6,4},{7,5},{8,10},{9,11},{10,... | collective-permute-start | bytes 304136 | tf_op jit(solution)/shard_map/ppermute | solution.py:31
  161.5 1.0 copy.23
  162.5 2.9 %collective-permute-done.20 = f32[88,288]{1,0:T(8,128)S(1)} collective-permute-done((f32[88,288]{1,0:T(8,128)S(1)}, f32[88,288]{1,0:T(8,128)S(1)}, u32[]{:S(2)}, u32[]{:S(2)}) %collective-permute-start.20) | collective-permute-done | bytes 101408 | tf_op jit(solution)/shard_map/ppermute | solution.py:31
  165.4 2.9 %collective-permute-done.19 = f32[88,288]{1,0:T(8,128)S(1)} collective-permute-done((f32[88,288]{1,0:T(8,128)S(1)}, f32[88,288]{1,0:T(8,128)S(1)}, u32[]{:S(2)}, u32[]{:S(2)}) %collective-permute-start.19) | collective-permute-done | bytes 101408 | tf_op jit(solution)/shard_map/ppermute | solution.py:31
  168.5 1.0 copy.22
  (96 shorter events, 9.8 us)
Async XLA Ops:
  2.0 5.6 %collective-permute-start.7 = (bf16[88,288]{1,0:T(8,128)(2,1)S(1)}, bf16[88,288]{1,0:T(8,128)(2,1)S(1)}, u32[]{:S(2)}, u32[]{:S(2)}) collective-permute-start(bf16[88,288]{1,0:T(8,128)(2,1)S(1)} %copy.27), channel_id=1, source_target_pairs={{0,1},{1,0},{2,3},{3,2},{4,5},{5,4},{6,7},{7,6},{8,9},{9,8},{10,11... | collective-permute-start | bytes 152072 | tf_op jit(solution)/shard_map/ppermute | solution.py:31
  3.6 4.3 %collective-permute-start.8 = (bf16[88,288]{1,0:T(8,128)(2,1)S(1)}, bf16[88,288]{1,0:T(8,128)(2,1)S(1)}, u32[]{:S(2)}, u32[]{:S(2)}) collective-permute-start(bf16[88,288]{1,0:T(8,128)(2,1)S(1)} %copy.28), channel_id=1, source_target_pairs={{0,2},{1,3},{2,0},{3,1},{4,6},{5,7},{6,4},{7,5},{8,10},{9,11},{10,... | collective-permute-start | bytes 152072 | tf_op jit(solution)/shard_map/ppermute | solution.py:31
  5.6 4.1 %collective-permute-start.9 = (bf16[88,288]{1,0:T(8,128)(2,1)S(1)}, bf16[88,288]{1,0:T(8,128)(2,1)S(1)}, u32[]{:S(2)}, u32[]{:S(2)}) collective-permute-start(bf16[88,288]{1,0:T(8,128)(2,1)S(1)} %copy.29), channel_id=1, source_target_pairs={{0,3},{1,2},{2,1},{3,0},{4,7},{5,6},{6,5},{7,4},{8,11},{9,10},{10,... | collective-permute-start | bytes 152072 | tf_op jit(solution)/shard_map/ppermute | solution.py:31
  7.1 6.2 %collective-permute-start = (bf16[176,288]{1,0:T(8,128)(2,1)S(1)}, bf16[176,288]{1,0:T(8,128)(2,1)S(1)}, u32[]{:S(2)}, u32[]{:S(2)}) collective-permute-start(bf16[176,288]{1,0:T(8,128)(2,1)S(1)} %broadcast_select_fusion.6), channel_id=1, source_target_pairs={{0,1},{1,0},{2,3},{3,2},{4,5},{5,4},{6,7},{7,6},{8,9},{9,8},{10,11... | collective-permute-start | bytes 304136 | tf_op jit(solution)/shard_map/ppermute | solution.py:31
  9.9 11.5 %collective-permute-start.12 = (bf16[88,1152]{1,0:T(8,128)(2,1)S(1)}, bf16[88,1152]{1,0:T(8,128)(2,1)S(1)}, u32[]{:S(2)}, u32[]{:S(2)}) collective-permute-start(bf16[88,1152]{1,0:T(8,128)(2,1)S(1)} %concatenate.31), channel_id=1, source_target_pairs={{0,12},{1,13},{2,14},{3,15},{4,8},{5,9},{6,10},{7,11},{8,4},{9,5},... | collective-permute-start | bytes 608264 | tf_op jit(solution)/shard_map/ppermute | solution.py:31
  12.4 10.3 %collective-permute-start.11 = (bf16[88,1152]{1,0:T(8,128)(2,1)S(1)}, bf16[88,1152]{1,0:T(8,128)(2,1)S(1)}, u32[]{:S(2)}, u32[]{:S(2)}) collective-permute-start(bf16[88,1152]{1,0:T(8,128)(2,1)S(1)} %concatenate.31), channel_id=1, source_target_pairs={{0,8},{1,9},{2,10},{3,11},{4,12},{5,13},{6,14},{7,15},{8,0},{9,1},... | collective-permute-start | bytes 608264 | tf_op jit(solution)/shard_map/ppermute | solution.py:31
  13.0 9.8 %collective-permute-start.10 = (bf16[88,1152]{1,0:T(8,128)(2,1)S(1)}, bf16[88,1152]{1,0:T(8,128)(2,1)S(1)}, u32[]{:S(2)}, u32[]{:S(2)}) collective-permute-start(bf16[88,1152]{1,0:T(8,128)(2,1)S(1)} %concatenate.31), channel_id=1, source_target_pairs={{0,4},{1,5},{2,6},{3,7},{4,0},{5,1},{6,2},{7,3},{8,12},{9,13},{10,... | collective-permute-start | bytes 608264 | tf_op jit(solution)/shard_map/ppermute | solution.py:31
  13.5 11.2 %collective-permute-start.3 = (bf16[88,1152]{1,0:T(8,128)(2,1)S(1)}, bf16[88,1152]{1,0:T(8,128)(2,1)S(1)}, u32[]{:S(2)}, u32[]{:S(2)}) collective-permute-start(bf16[88,1152]{1,0:T(8,128)(2,1)S(1)} %fusion.4), channel_id=1, source_target_pairs={{0,48},{1,67},{2,50},{3,65},{4,52},{5,71},{6,54},{7,69},{8,56},{9,... | collective-permute-start | bytes 608264 | tf_op jit(solution)/shard_map/ppermute | solution.py:31
  16.8 8.0 %collective-permute-start.2 = (bf16[88,1152]{1,0:T(8,128)(2,1)S(1)}, bf16[88,1152]{1,0:T(8,128)(2,1)S(1)}, u32[]{:S(2)}, u32[]{:S(2)}) collective-permute-start(bf16[88,1152]{1,0:T(8,128)(2,1)S(1)} %fusion.4), channel_id=1, source_target_pairs={{0,32},{1,65},{2,34},{3,67},{4,36},{5,69},{6,38},{7,71},{8,40},{9,... | collective-permute-start | bytes 608264 | tf_op jit(solution)/shard_map/ppermute | solution.py:31
  21.4 4.9 %collective-permute-start.1 = (bf16[88,1152]{1,0:T(8,128)(2,1)S(1)}, bf16[88,1152]{1,0:T(8,128)(2,1)S(1)}, u32[]{:S(2)}, u32[]{:S(2)}) collective-permute-start(bf16[88,1152]{1,0:T(8,128)(2,1)S(1)} %fusion.4), channel_id=1, source_target_pairs={{0,16},{1,3},{2,18},{3,1},{4,20},{5,7},{6,22},{7,5},{8,24},{9,11},... | collective-permute-start | bytes 608264 | tf_op jit(solution)/shard_map/ppermute | solution.py:31
  22.8 25.8 %copy-start = (bf16[352,1152]{1,0:T(8,128)(2,1)}, bf16[352,1152]{1,0:T(8,128)(2,1)S(1)}, u32[]{:S(2)}) copy-start(bf16[352,1152]{1,0:T(8,128)(2,1)S(1)} %pad_maximum_fusion.1.im0_ref) | copy-start | bytes 2433028
  22.8 11.2 %collective-permute-start.13 = (bf16[352,1152]{1,0:T(8,128)(2,1)S(1)}, bf16[352,1152]{1,0:T(8,128)(2,1)S(1)}, u32[]{:S(2)}, u32[]{:S(2)}) collective-permute-start(bf16[352,1152]{1,0:T(8,128)(2,1)S(1)} %pad_maximum_fusion.1.im0_ref), channel_id=1, source_target_pairs={{0,1},{1,0},{2,3},{3,2},{4,5},{5,4},{6,7},{7,6},{8,9},{9,8},{10,11... | collective-permute-start | bytes 2433032 | tf_op jit(solution)/shard_map/ppermute | solution.py:31
  26.4 22.3 %copy-start.1 = (bf16[4,88,1152]{2,1,0:T(8,128)(2,1)}, bf16[4,88,1152]{2,1,0:T(8,128)(2,1)S(1)}, u32[]{:S(2)}) copy-start(bf16[4,88,1152]{2,1,0:T(8,128)(2,1)S(1)} %pad_maximum_fusion.own_ref) | copy-start | bytes 2433028
  26.4 21.4 %collective-permute-start.6 = (bf16[4,88,1152]{2,1,0:T(8,128)(2,1)S(1)}, bf16[4,88,1152]{2,1,0:T(8,128)(2,1)S(1)}, u32[]{:S(2)}, u32[]{:S(2)}) collective-permute-start(bf16[4,88,1152]{2,1,0:T(8,128)(2,1)S(1)} %pad_maximum_fusion.own_ref), channel_id=1, source_target_pairs={{0,66},{1,49},{2,64},{3,51},{4,70},{5,53},{6,68},{7,55},{8,74},{9,... | collective-permute-start | bytes 2433032 | tf_op jit(solution)/shard_map/ppermute | solution.py:31
  29.2 18.6 %collective-permute-start.5 = (bf16[4,88,1152]{2,1,0:T(8,128)(2,1)S(1)}, bf16[4,88,1152]{2,1,0:T(8,128)(2,1)}, u32[]{:S(2)}, u32[]{:S(2)}) collective-permute-start(bf16[4,88,1152]{2,1,0:T(8,128)(2,1)S(1)} %pad_maximum_fusion.own_ref), channel_id=1, source_target_pairs={{0,64},{1,33},{2,66},{3,35},{4,68},{5,37},{6,70},{7,39},{8,72},{9,... | collective-permute-start | bytes 2433032 | tf_op jit(solution)/shard_map/ppermute | solution.py:31
  29.5 19.1 %collective-permute-start.4 = (bf16[4,88,1152]{2,1,0:T(8,128)(2,1)S(1)}, bf16[4,88,1152]{2,1,0:T(8,128)(2,1)}, u32[]{:S(2)}, u32[]{:S(2)}) collective-permute-start(bf16[4,88,1152]{2,1,0:T(8,128)(2,1)S(1)} %pad_maximum_fusion.own_ref), channel_id=1, source_target_pairs={{0,2},{1,17},{2,0},{3,19},{4,6},{5,21},{6,4},{7,23},{8,10},{9,25},... | collective-permute-start | bytes 2433032 | tf_op jit(solution)/shard_map/ppermute | solution.py:31
  34.0 14.6 %copy-start.6 = (bf16[352,1152]{1,0:T(8,128)(2,1)}, bf16[352,1152]{1,0:T(8,128)(2,1)S(1)}, u32[]{:S(2)}) copy-start(bf16[352,1152]{1,0:T(8,128)(2,1)S(1)} %collective-permute-done.13.im1_ref) | copy-start | bytes 2433028
  47.8 0.9 copy-start.7
  69.8 67.0 %collective-permute-start.14 = (f32[352,1152]{1,0:T(8,128)}, f32[352,1152]{1,0:T(8,128)S(1)}, u32[]{:S(2)}, u32[]{:S(2)}) collective-permute-start(f32[352,1152]{1,0:T(8,128)} %get-tuple-element.15), channel_id=1, source_target_pairs={{0,1},{1,0},{2,3},{3,2},{4,5},{5,4},{6,7},{7,6},{8,9},{9,8},{10,11... | collective-permute-start | bytes 4866056 | tf_op jit(solution)/shard_map/ppermute | solution.py:31
  73.5 14.5 %collective-permute-start.21 = (bf16[368,1152]{1,0:T(8,128)(2,1)}, bf16[368,1152]{1,0:T(8,128)(2,1)S(1)}, u32[]{:S(2)}, u32[]{:S(2)}) collective-permute-start(bf16[368,1152]{1,0:T(8,128)(2,1)} %get-tuple-element.17), channel_id=1, source_target_pairs={{0,2},{1,17},{2,0},{3,19},{4,6},{5,21},{6,4},{7,23},{8,10},{9,25},... | collective-permute-start | bytes 2543624 | tf_op jit(solution)/shard_map/ppermute | solution.py:31
  74.8 22.3 %collective-permute-start.22 = (bf16[368,1152]{1,0:T(8,128)(2,1)}, bf16[368,1152]{1,0:T(8,128)(2,1)S(1)}, u32[]{:S(2)}, u32[]{:S(2)}) collective-permute-start(bf16[368,1152]{1,0:T(8,128)(2,1)} %get-tuple-element.18), channel_id=1, source_target_pairs={{0,64},{1,33},{2,66},{3,35},{4,68},{5,37},{6,70},{7,39},{8,72},{9,... | collective-permute-start | bytes 2543624 | tf_op jit(solution)/shard_map/ppermute | solution.py:31
  77.5 22.3 %collective-permute-start.23 = (bf16[368,1152]{1,0:T(8,128)(2,1)}, bf16[368,1152]{1,0:T(8,128)(2,1)S(1)}, u32[]{:S(2)}, u32[]{:S(2)}) collective-permute-start(bf16[368,1152]{1,0:T(8,128)(2,1)} %get-tuple-element.19), channel_id=1, source_target_pairs={{0,66},{1,49},{2,64},{3,51},{4,70},{5,53},{6,68},{7,55},{8,74},{9,... | collective-permute-start | bytes 2543624 | tf_op jit(solution)/shard_map/ppermute | solution.py:31
  77.5 1.9 %collective-permute-start.28 = (f32[8,128]{1,0:T(8,128)}, f32[8,128]{1,0:T(8,128)S(1)}, u32[]{:S(2)}, u32[]{:S(2)}) collective-permute-start(f32[8,128]{1,0:T(8,128)} %get-tuple-element.24), channel_id=1, source_target_pairs={{0,1},{1,0},{2,3},{3,2},{4,5},{5,4},{6,7},{7,6},{8,9},{9,8},{10,11... | collective-permute-start | bytes 12296 | tf_op jit(solution)/shard_map/ppermute | solution.py:31
  80.1 2.8 %collective-permute-start.29 = (f32[8,128]{1,0:T(8,128)S(1)}, f32[8,128]{1,0:T(8,128)S(1)}, u32[]{:S(2)}, u32[]{:S(2)}) collective-permute-start(f32[8,128]{1,0:T(8,128)S(1)} %add.263), channel_id=1, source_target_pairs={{0,4},{1,5},{2,6},{3,7},{4,0},{5,1},{6,2},{7,3},{8,12},{9,13},{10,... | collective-permute-start | bytes 12296 | tf_op jit(solution)/shard_map/ppermute | solution.py:31
  82.8 4.0 %collective-permute-start.30 = (f32[8,128]{1,0:T(8,128)S(1)}, f32[8,128]{1,0:T(8,128)S(1)}, u32[]{:S(2)}, u32[]{:S(2)}) collective-permute-start(f32[8,128]{1,0:T(8,128)S(1)} %add.264), channel_id=1, source_target_pairs={{0,8},{1,9},{2,10},{3,11},{4,12},{5,13},{6,14},{7,15},{8,0},{9,1},... | collective-permute-start | bytes 12296 | tf_op jit(solution)/shard_map/ppermute | solution.py:31
  86.8 24.7 %collective-permute-start.31 = (f32[8,128]{1,0:T(8,128)S(1)}, f32[8,128]{1,0:T(8,128)S(1)}, u32[]{:S(2)}, u32[]{:S(2)}) collective-permute-start(f32[8,128]{1,0:T(8,128)S(1)} %add.265), channel_id=1, source_target_pairs={{0,16},{1,17},{2,18},{3,19},{4,20},{5,21},{6,22},{7,23},{8,24},{9,... | collective-permute-start | bytes 12296 | tf_op jit(solution)/shard_map/ppermute | solution.py:31
  88.1 11.7 %copy-start.3 = (bf16[368,1152]{1,0:T(8,128)(2,1)}, bf16[368,1152]{1,0:T(8,128)(2,1)S(1)}, u32[]{:S(2)}) copy-start(bf16[368,1152]{1,0:T(8,128)(2,1)S(1)} %collective-permute-done.21.r1_ref) | copy-start | bytes 2543620
  97.2 2.6 %copy-start.4 = (bf16[368,1152]{1,0:T(8,128)(2,1)}, bf16[368,1152]{1,0:T(8,128)(2,1)S(1)}, u32[]{:S(2)}) copy-start(bf16[368,1152]{1,0:T(8,128)(2,1)S(1)} %collective-permute-done.22.r2_ref) | copy-start | bytes 2543620
  99.8 0.9 copy-start.5
  107.6 29.2 %copy-start.2 = (f32[352,1152]{1,0:T(8,128)S(1)}, f32[352,1152]{1,0:T(8,128)}, u32[]{:S(2)}) copy-start(f32[352,1152]{1,0:T(8,128)} %get-tuple-element.14) | copy-start | bytes 4866052
  107.6 17.1 %collective-permute-start.24 = (bf16[104,1152]{1,0:T(8,128)(2,1)}, bf16[104,1152]{1,0:T(8,128)(2,1)S(1)}, u32[]{:S(2)}, u32[]{:S(2)}) collective-permute-start(bf16[104,1152]{1,0:T(8,128)(2,1)} %get-tuple-element.21), channel_id=1, source_target_pairs={{0,16},{1,3},{2,18},{3,1},{4,20},{5,7},{6,22},{7,5},{8,24},{9,11},... | collective-permute-start | bytes 718856 | tf_op jit(solution)/shard_map/ppermute | solution.py:31
  108.3 16.4 %collective-permute-start.25 = (bf16[104,1152]{1,0:T(8,128)(2,1)}, bf16[104,1152]{1,0:T(8,128)(2,1)}, u32[]{:S(2)}, u32[]{:S(2)}) collective-permute-start(bf16[104,1152]{1,0:T(8,128)(2,1)} %get-tuple-element.22), channel_id=1, source_target_pairs={{0,32},{1,65},{2,34},{3,67},{4,36},{5,69},{6,38},{7,71},{8,40},{9,... | collective-permute-start | bytes 718856 | tf_op jit(solution)/shard_map/ppermute | solution.py:31
  111.3 13.4 %collective-permute-start.26 = (bf16[104,1152]{1,0:T(8,128)(2,1)}, bf16[104,1152]{1,0:T(8,128)(2,1)}, u32[]{:S(2)}, u32[]{:S(2)}) collective-permute-start(bf16[104,1152]{1,0:T(8,128)(2,1)} %get-tuple-element.23), channel_id=1, source_target_pairs={{0,48},{1,67},{2,50},{3,65},{4,52},{5,71},{6,54},{7,69},{8,56},{9,... | collective-permute-start | bytes 718856 | tf_op jit(solution)/shard_map/ppermute | solution.py:31
  111.5 4.0 %collective-permute-start.32 = (f32[8,128]{1,0:T(8,128)S(1)}, f32[8,128]{1,0:T(8,128)S(1)}, u32[]{:S(2)}, u32[]{:S(2)}) collective-permute-start(f32[8,128]{1,0:T(8,128)S(1)} %add.266), channel_id=1, source_target_pairs={{0,32},{1,33},{2,34},{3,35},{4,36},{5,37},{6,38},{7,39},{8,40},{9,... | collective-permute-start | bytes 12296 | tf_op jit(solution)/shard_map/ppermute | solution.py:31
  115.4 2.9 %collective-permute-start.33 = (f32[8,128]{1,0:T(8,128)S(1)}, f32[8,128]{1,0:T(8,128)S(1)}, u32[]{:S(2)}, u32[]{:S(2)}) collective-permute-start(f32[8,128]{1,0:T(8,128)S(1)} %add.267), channel_id=1, source_target_pairs={{0,2},{1,3},{2,0},{3,1},{4,6},{5,7},{6,4},{7,5},{8,10},{9,11},{10,... | collective-permute-start | bytes 12296 | tf_op jit(solution)/shard_map/ppermute | solution.py:31
  118.3 4.0 %collective-permute-start.34 = (f32[8,128]{1,0:T(8,128)S(1)}, f32[8,128]{1,0:T(8,128)S(1)}, u32[]{:S(2)}, u32[]{:S(2)}) collective-permute-start(f32[8,128]{1,0:T(8,128)S(1)} %add.268), channel_id=1, source_target_pairs={{0,64},{1,65},{2,66},{3,67},{4,68},{5,69},{6,70},{7,71},{8,72},{9,... | collective-permute-start | bytes 12296 | tf_op jit(solution)/shard_map/ppermute | solution.py:31
  124.7 0.7 copy-start.8
  129.4 11.4 %collective-permute-start.27 = (f32[176,288]{1,0:T(8,128)S(1)}, f32[176,288]{1,0:T(8,128)S(1)}, u32[]{:S(2)}, u32[]{:S(2)}) collective-permute-start(f32[176,288]{1,0:T(8,128)S(1)} %broadcast_select_fusion.2), channel_id=1, source_target_pairs={{0,1},{1,0},{2,3},{3,2},{4,5},{5,4},{6,7},{7,6},{8,9},{9,8},{10,11... | collective-permute-start | bytes 608264 | tf_op jit(solution)/shard_map/ppermute | solution.py:31
  137.0 11.1 %collective-permute-start.15 = (f32[88,1152]{1,0:T(8,128)S(1)}, f32[88,1152]{1,0:T(8,128)S(1)}, u32[]{:S(2)}, u32[]{:S(2)}) collective-permute-start(f32[88,1152]{1,0:T(8,128)S(1)} %get-tuple-element.35), channel_id=1, source_target_pairs={{0,4},{1,5},{2,6},{3,7},{4,0},{5,1},{6,2},{7,3},{8,12},{9,13},{10,... | collective-permute-start | bytes 1216520 | tf_op jit(solution)/shard_map/ppermute | solution.py:31
  137.1 19.9 %collective-permute-start.17 = (f32[88,1152]{1,0:T(8,128)S(1)}, f32[88,1152]{1,0:T(8,128)S(1)}, u32[]{:S(2)}, u32[]{:S(2)}) collective-permute-start(f32[88,1152]{1,0:T(8,128)S(1)} %get-tuple-element.36), channel_id=1, source_target_pairs={{0,12},{1,13},{2,14},{3,15},{4,8},{5,9},{6,10},{7,11},{8,4},{9,5},... | collective-permute-start | bytes 1216520 | tf_op jit(solution)/shard_map/ppermute | solution.py:31
  139.7 19.3 %collective-permute-start.16 = (f32[88,1152]{1,0:T(8,128)S(1)}, f32[88,1152]{1,0:T(8,128)S(1)}, u32[]{:S(2)}, u32[]{:S(2)}) collective-permute-start(f32[88,1152]{1,0:T(8,128)S(1)} %get-tuple-element.37), channel_id=1, source_target_pairs={{0,8},{1,9},{2,10},{3,11},{4,12},{5,13},{6,14},{7,15},{8,0},{9,1},... | collective-permute-start | bytes 1216520 | tf_op jit(solution)/shard_map/ppermute | solution.py:31
  159.3 6.1 %collective-permute-start.20 = (f32[88,288]{1,0:T(8,128)S(1)}, f32[88,288]{1,0:T(8,128)S(1)}, u32[]{:S(2)}, u32[]{:S(2)}) collective-permute-start(f32[88,288]{1,0:T(8,128)S(1)} %get-tuple-element.43), channel_id=1, source_target_pairs={{0,3},{1,2},{2,1},{3,0},{4,7},{5,6},{6,5},{7,4},{8,11},{9,10},{10,... | collective-permute-start | bytes 304136 | tf_op jit(solution)/shard_map/ppermute | solution.py:31
  159.8 8.5 %collective-permute-start.19 = (f32[88,288]{1,0:T(8,128)S(1)}, f32[88,288]{1,0:T(8,128)S(1)}, u32[]{:S(2)}, u32[]{:S(2)}) collective-permute-start(f32[88,288]{1,0:T(8,128)S(1)} %get-tuple-element.44), channel_id=1, source_target_pairs={{0,2},{1,3},{2,0},{3,1},{4,6},{5,7},{6,4},{7,5},{8,10},{9,11},{10,... | collective-permute-start | bytes 304136 | tf_op jit(solution)/shard_map/ppermute | solution.py:31
  161.5 6.8 %collective-permute-start.18 = (f32[88,288]{1,0:T(8,128)S(1)}, f32[88,288]{1,0:T(8,128)S(1)}, u32[]{:S(2)}, u32[]{:S(2)}) collective-permute-start(f32[88,288]{1,0:T(8,128)S(1)} %get-tuple-element.45), channel_id=1, source_target_pairs={{0,1},{1,0},{2,3},{3,2},{4,5},{5,4},{6,7},{7,6},{8,9},{9,8},{10,11... | collective-permute-start | bytes 304136 | tf_op jit(solution)/shard_map/ppermute | solution.py:31

commit v2 on v0

v2 whole, which is shorter than its diff:
```python
import functools

import jax
import jax.numpy as jnp
from jax import lax
from jax.experimental import pallas as pl
from jax.experimental.pallas import tpu as pltpu
from jax.sharding import PartitionSpec as P

BF = jnp.bfloat16
F32 = jnp.float32
AXES = ("batch", "dim")
CORE = 1


def x_mask(k):
    return k << 2


def y_mask(k):
    return k << 4


def z_mask(k):
    return ((k >> 1) << 6) | ((k & 1) << 1)


def swap(array, mask0, mask1=None):
    mask1 = mask0 if mask1 is None else mask1
    n = lax.axis_size("batch") * lax.axis_size("dim")
    return lax.ppermute(array, AXES, [(i, i ^ (mask1 if i & 1 else mask0)) for i in range(n)])


LOW = 2.0**-3.5


def encode(v, m):
    a = jnp.abs(v) * (127.0 * LOW / m) + LOW
    for _ in range(5):
        a = a * a
    return jnp.where(v < 0, -a, a)


def decode(code, m):
    c = code.astype(F32)
    a = jnp.exp(jnp.log(jnp.abs(c)) * (1.0 / 32.0)) * (1.0 / LOW) - 1.0
    v = a * (m * (1.0 / 127.0))
    return jnp.where(c < 0, -v, v)


def top_of(largest):
    return (largest * 1.01 + 1e-30).astype(BF).astype(F32)


def tile_kernel(
    first, rows, half, feats,
    info_ref, scale_ref, *refs,
):
    if first:
        ta_ref, tb_ref, im0_ref, im1_ref, own_ref, msg_ref, acc_ref, sums_ref, texts, images, t_rel, coeff_low, grads, sems = refs
    else:
        (ta_ref, tb_ref, im0_ref, im1_ref, before_ref, sums_before, ma_ref, mb_ref, img0_ref, img1_ref, sums_ref,
         texts, images, t_rel, coeff_low, grads, sems) = refs
    core, z_lo = info_ref[0], info_ref[1]
    scaling, offset = scale_ref[0], scale_ref[1]
    quarter, step = 4 * rows, 2 * rows
    copies = [pltpu.make_async_copy(src, texts.at[j], sems.at[j]) for j, src in enumerate((ta_ref, tb_ref))] + [
        pltpu.make_async_copy(src, images.at[pl.ds(o * quarter, quarter)], sems.at[2 + o])
        for o, src in enumerate((im0_ref, im1_ref))
    ]
    for copy in copies:
        copy.start()
    for copy in copies:
        copy.wait()

    def place(b, e):
        return jnp.where(core == 0, e, b >> 1), jnp.where(core == 0, b, 2 * (b & 1) + e)

    for b in range(4):
        p0, p1 = (texts[place(b, e)].astype(F32) for e in range(2))
        top = jnp.concatenate([p0[:, :half], p1[:, :half]], axis=1)
        bottom = jnp.concatenate([p0[:, half:], p1[:, half:]], axis=1)
        t_rel[b * step : (b + 1) * step, :] = jnp.concatenate([top, bottom], axis=0).astype(BF)
    similar = lax.dot_general(t_rel[...], images[...], (((1,), (1,)), ((), ())), preferred_element_type=F32)
    temp, bias = jnp.zeros((1, 2 * quarter), F32), jnp.zeros((1, 2 * quarter), F32)
    for b in range(4):
        part = similar[b * step : (b + 1) * step]
        logits = scaling * part + offset
        if first and b == 0:
            row = lax.broadcasted_iota(jnp.int32, part.shape, 0)
            column = lax.broadcasted_iota(jnp.int32, part.shape, 1)
            matched = (row - rows * z_lo == column) & (column < rows)
            sig = 1.0 / (1.0 + jnp.exp(jnp.where(matched, logits, -logits)))
            coeff = jnp.where(matched, -sig, sig)
        else:
            coeff = 1.0 / (1.0 + jnp.exp(-logits))
        coeff_low[b * step : (b + 1) * step, :] = coeff.astype(BF)
        temp = temp + jnp.sum(coeff * part, axis=0, keepdims=True)
        bias = bias + jnp.sum(coeff, axis=0, keepdims=True)
    sums = jnp.concatenate(
        [jnp.broadcast_to(jnp.sum(v, axis=1, keepdims=True), (4, 128)) for v in (temp, bias)], axis=0
    )
    text_part = jnp.dot(coeff_low[...], images[...], preferred_element_type=F32)
    for b in range(4):
        top = text_part[b * step : b * step + rows]
        bottom = text_part[b * step + rows : (b + 1) * step]
        grads[place(b, 0)] = jnp.concatenate([top[:, :half], bottom[:, :half]], axis=1)
        grads[place(b, 1)] = jnp.concatenate([top[:, half:], bottom[:, half:]], axis=1)
    acc = lax.dot_general(coeff_low[...], t_rel[...], (((0,), (0,)), ((), ())), preferred_element_type=F32)

    def send(e, m_ref):
        whole = jnp.concatenate([grads[e, i] for i in range(4)], axis=0)
        m = top_of(jnp.max(jnp.max(jnp.abs(whole), axis=0, keepdims=True), axis=1, keepdims=True))
        m_ref[0:quarter, :] = encode(whole, m).astype(BF)
        m_ref[quarter : quarter + 16, :] = jnp.broadcast_to(m, (16, feats)).astype(BF)

    if first:
        acc_ref[...] = acc
        sums_ref[...] = sums
        own_ref[...] = jnp.concatenate([grads[0, i] for i in range(4)], axis=0)
        send(1, msg_ref)
    else:
        acc = acc + before_ref[...]
        img0_ref[...] = acc[0:quarter]
        img1_ref[...] = acc[quarter : 2 * quarter]
        sums_ref[...] = sums + sums_before[...]
        send(0, ma_ref)
        send(1, mb_ref)


def split3(v):
    hi = v.astype(BF).astype(F32)
    mid = (v - hi).astype(BF).astype(F32)
    return [hi, mid, v - hi - mid]


def first_sum_kernel(rows, feats, coded, own_ref, sums_ref, *refs):
    received, (out_ref, m1_ref, m2_ref, m3_ref) = refs[:-4], refs[-4:]
    quarter = 4 * rows
    total = own_ref[...]
    for r in received:
        total = total + (decode(r[0:quarter], r[quarter : quarter + 16].astype(F32)[0:1, :]) if coded else r[...])
    out_ref[...] = total[0:rows]
    scalars = [jnp.broadcast_to(v, (1, feats)) for at in (0, 4) for v in split3(sums_ref[at : at + 1, 0:1])]
    for i, m_ref in ((1, m1_ref), (2, m2_ref), (3, m3_ref)):
        part = total[i * rows : (i + 1) * rows]
        m = top_of(jnp.max(jnp.max(jnp.abs(part), axis=0, keepdims=True), axis=1, keepdims=True))
        m = jnp.broadcast_to(m, (10, feats))
        m_ref[...] = jnp.concatenate([encode(part, m[0:1]), *scalars, m], axis=0).astype(BF)


def last_sum_kernel(rows, scale_ref, own_ref, sums_ref, r1_ref, r2_ref, r3_ref, out_ref, sums_out):
    total = own_ref[...]
    wholes = [r[...].astype(F32) for r in (r1_ref, r2_ref, r3_ref)]
    for whole in wholes:
        total = total + decode(whole[0:rows], whole[rows + 8 : rows + 9])
    out_ref[...] = total * scale_ref[0]
    extra = [whole[rows : rows + 8, 0:128] for whole in wholes]

    def three(e, at):
        return e[at : at + 1] + (e[at + 1 : at + 2] + e[at + 2 : at + 3])

    for at, src in ((0, 0), (4, 3)):
        a, b, c = (three(e, src) for e in extra)
        sums_out[at : at + 4, :] = jnp.broadcast_to((sums_ref[at : at + 1, :] + a) + (b + c), (4, 128))


VMEM = pl.BlockSpec(memory_space=pltpu.VMEM)
SMEM = pl.BlockSpec(memory_space=pltpu.SMEM)
HBM = pl.BlockSpec(memory_space=pl.ANY)
BIG = pltpu.CompilerParams(vmem_limit_bytes=56 * 1024 * 1024)


def after(array, *others):
    return lax.optimization_barrier((array, *others))[0]


def body(picture_embeds, caption_embeds, logit_scaler, logit_offset_term):
    height, width = picture_embeds.shape
    rows, half, feats = height // 4, 2 * width, 4 * width
    step, quarter = 2 * rows, 4 * rows
    index = lax.axis_index("batch") * lax.axis_size("dim") + lax.axis_index("dim")
    core, z_lo = index & 1, (index >> 1) & 1
    on0, lo0 = core == 0, z_lo == 0
    scaling = logit_scaler[0]

    def by(first_one, own, other):
        return [jnp.where(first_one, own, other), jnp.where(first_one, other, own)]

    both = [jnp.concatenate([t[:step], i[:step]]) for t, i in ((caption_embeds, picture_embeds),)]
    both.append(jnp.concatenate([caption_embeds[step:], picture_embeds[step:]]))
    keep, send = by(on0, *both)
    chip = jnp.concatenate(by(on0, keep, swap(send, CORE)), axis=1)
    packed = jnp.concatenate([chip[:rows], chip[rows:step]], axis=1)
    keep, send = by(lo0, chip[step : step + rows], chip[step + rows :])
    first = [packed] + [swap(packed, y_mask(i), z_mask(i)) for i in range(1, 4)]
    image = jnp.concatenate([keep, swap(send, z_mask(1))], axis=1)
    stack = jnp.stack(first)
    second1, second3 = swap(stack, z_mask(1), y_mask(1)), swap(stack, z_mask(3), y_mask(3))
    images_own = jnp.concatenate([image] + [swap(image, x_mask(k)) for k in range(1, 4)], axis=0)
    images_other = swap(images_own, CORE)
    second2 = swap(after(stack, second1, second3), z_mask(2), y_mask(2))

    info = jnp.stack([core, z_lo]).astype(jnp.int32)
    scales = jnp.stack([scaling, logit_offset_term[0]])
    message = jax.ShapeDtypeStruct((quarter + 16, feats), BF)
    image_part = jax.ShapeDtypeStruct((quarter, feats), F32)
    acc_shape = jax.ShapeDtypeStruct((2 * quarter, feats), F32)
    sums_shape = jax.ShapeDtypeStruct((8, 128), F32)
    scratch = [
        pltpu.VMEM((2, 4, rows, feats), BF),
        pltpu.VMEM((2 * quarter, feats), BF),
        pltpu.VMEM((4 * step, feats), BF),
        pltpu.VMEM((4 * step, 2 * quarter), BF),
        pltpu.VMEM((2, 4, rows, feats), F32),
        pltpu.SemaphoreType.DMA((4,)),
    ]
    cost = pl.CostEstimate(
        flops=3 * 2 * 4 * step * 2 * quarter * feats, bytes_accessed=12 * 4 * step * feats, transcendentals=8 * step * quarter
    )
    text_own, m1, acc, sums = pl.pallas_call(
        functools.partial(tile_kernel, True, rows, half, feats),
        out_shape=(image_part, message, acc_shape, sums_shape),
        in_specs=[SMEM, SMEM] + [HBM] * 4,
        out_specs=(VMEM,) * 4,
        scratch_shapes=scratch,
        compiler_params=BIG,
        cost_estimate=cost,
        name="tile_first",
    )(info, scales, stack, second1, images_own, images_other)
    m2, m3, img_own, img_other, sums = pl.pallas_call(
        functools.partial(tile_kernel, False, rows, half, feats),
        out_shape=(message, message, image_part, image_part, sums_shape),
        in_specs=[SMEM, SMEM] + [HBM] * 4 + [VMEM] * 2,
        out_specs=(VMEM,) * 5,
        scratch_shapes=scratch,
        compiler_params=BIG,
        cost_estimate=cost,
        name="tile_second",
    )(info, scales, second2, second3, images_own, images_other, acc, sums)

    message = jax.ShapeDtypeStruct((rows + 16, feats), BF)

    def first_sum(name, coded, *args):
        return pl.pallas_call(
            functools.partial(first_sum_kernel, rows, feats, coded),
            out_shape=(jax.ShapeDtypeStruct((rows, feats), F32), message, message, message),
            in_specs=[VMEM] * len(args),
            out_specs=(VMEM,) * 4,
            compiler_params=BIG,
            name=name,
        )(*args)

    def last_sum(name, *args):
        return pl.pallas_call(
            functools.partial(last_sum_kernel, rows),
            out_shape=(jax.ShapeDtypeStruct((rows, feats), F32), sums_shape),
            in_specs=[SMEM] + [VMEM] * 5,
            out_specs=(VMEM, VMEM),
            compiler_params=BIG,
            name=name,
        )(logit_scaler, *args)

    got1 = swap(m1, z_mask(1), y_mask(1))
    img, i1, i2, i3 = first_sum("image_first", False, img_own, sums, after(swap(img_other, CORE), got1))
    got2, got3 = swap(m2, z_mask(2), y_mask(2)), swap(m3, z_mask(3), y_mask(3))
    i1, sums = lax.optimization_barrier((i1, sums))
    img_got = [swap(m, x_mask(k)) for k, m in ((1, i1), (2, i2), (3, i3))]
    for mask in ((x_mask(1),), (x_mask(2),), (z_mask(1), y_mask(1)), (z_mask(2), y_mask(2))):
        sums = sums + swap(sums, *mask)

    text, n1, n2, n3 = first_sum("text_first", True, text_own, sums, got1, got2, got3)
    got = [swap(m, y_mask(i), z_mask(i)) for i, m in ((1, n1), (2, n2), (3, n3))]

    img, _ = last_sum("image_last", img, sums, *img_got)
    image = jnp.concatenate(by(lo0, img[:, :half], swap(img[:, half:], z_mask(1))), axis=0)
    text, sums = last_sum("text_last", after(text, image), sums, *got)
    whole = jnp.concatenate([text[:, :half], text[:, half:], image], axis=0)
    mine, other = by(on0, whole[:, :width], whole[:, width:])
    tail = jnp.pad(sums, ((0, 0), (0, width - sums.shape[1])))
    other = swap(jnp.concatenate([other, tail], axis=0), CORE)
    text_grad = jnp.concatenate(by(on0, mine[:step], other[:step]), axis=0)
    image_grad = jnp.concatenate(by(on0, mine[step:], other[step : 2 * step]), axis=0)
    sums = sums + other[2 * step :, :128]
    scalar_grads = jnp.stack([sums[0, 0], sums[4, 0]])
    return (image_grad, text_grad, scalar_grads)


def solution(mesh):
    placed = (P("batch", "dim"), P("batch", "dim"), P(), P())
    return jax.shard_map(
        body,
        mesh=mesh,
        in_specs=placed,
        out_specs=(P("batch", "dim"), P("batch", "dim"), P()),
        check_vma=False,
    )
```

time: 1980 us -> 142 us (0.07)
  waiting for transfers between devices: 1520 us -> 34.8 us
  matrix products: 184 us -> 0 us
  blocking collectives: 76.6 us -> 0 us
  other arithmetic: 73.9 us -> 5.12 us
  loops' own time: 44.7 us -> 0 us
  Pallas kernels: 0 us -> 40 us
    psum x32 -> x0, waiting for transfers between devices: 1180 us -> none  [patch_coefficients(): similar = lax.psum(pair_dot(picture_embeds, caption_slice), 'dim')]
    ppermute x64 -> x28, waiting for transfers between devices: 342 us -> 34.8 us  [swap(): lax.ppermute(array, AXES, [(i, i ^ (mask1 if i & 1 else mask0)) for i in...]
    dot_general x96 -> x0, matrix products: 184 us -> none  [the longest x32 89.9 us: carried_rotation(): lax.dot_general(coeff_low, picture_embeds, (((0,), (0,)), ((), ())), pref...]
    psum x1 -> x0, blocking collectives: 76.6 us -> none  [body(): scalar_grads = lax.psum(local_pair, 'batch')]
    reduce_sum x32 -> x0, other arithmetic: 73.8 us -> none  [coefficients(): return (coeff, jnp.sum(coeff * similar), jnp.sum(coeff))]
    another operation x1 -> x0, loops' own time: 44.7 us -> none  [body(): final = lax.fori_loop(0, cycle_size, carried_rotation, start)]
    pallas_call x0 -> x6, Pallas kernels: none -> 40 us  [the longest x1 13.5 us: body(): pl.pallas_call(functools.partial(tile_kernel, False, rows, half, feats),...]
    ppermute x64 -> x28, starting transfers between devices: 44.6 us -> 44.7 us  [swap(): lax.ppermute(array, AXES, [(i, i ^ (mask1 if i & 1 else mask0)) for i in...]
  transfers between devices with their start and end apart: 96 -> 28, of which waited for: 64 -> 11; matrix products, arithmetic and copies ran while one was open for 11% -> 3% of each run, Pallas kernels for 0% -> 19%
where the time goes in v2:
time: 142 us; the launch traced here: 141 us
  starting transfers between devices  44.7 us (31%)
  Pallas kernels  40 us (28%)
  waiting for transfers between devices  34.8 us (25%)
  local copies, waits for them, and re-layouts  14.4 us (10%)
  other arithmetic  5.12 us (4%)
  between operations  2.3 us (2%)
    ppermute x28, starting transfers between devices, swap(): lax.ppermute(array, AXES, [(i, i ^ (mask1 if i & 1 else mask0)) for i in...  44.7 us
    ppermute x28, waiting for transfers between devices, swap(): lax.ppermute(array, AXES, [(i, i ^ (mask1 if i & 1 else mask0)) for i in...  34.8 us
    pallas_call x1, Pallas kernels, body(): pl.pallas_call(functools.partial(tile_kernel, False, rows, half, feats),...  13.5 us
    pallas_call x1, Pallas kernels, body(): pl.pallas_call(functools.partial(tile_kernel, True, rows, half, feats), o...  10.8 us
    pallas_call x2, Pallas kernels, first_sum(): pl.pallas_call(functools.partial(first_sum_kernel, rows, feats, coded), o...  10.4 us
    unnamed x49, local copies, waits for them, and re-layouts  8.87 us
    pallas_call x2, Pallas kernels, last_sum(): pl.pallas_call(functools.partial(last_sum_kernel, rows), out_shape=(jax.S...  5.27 us
  transfers between devices with their start and end apart: 28, of which 11 were waited for; matrix products, arithmetic and copies ran while one was open for 3% of the time, Pallas kernels for 19%

profile of v2, /device:TPU:1, one launch (start us, length us, event | category | flops | bytes accessed | tf_op | source)
XLA Modules:
  0.0 141.3 jit_solution(4195394537033672096)
XLA Ops:
  0.6 1.1 fusion.6
  2.0 1.1 fusion.5
  3.5 1.5 %collective-permute-start = (bf16[352,288]{1,0:T(8,128)(2,1)S(1)}, bf16[352,288]{1,0:T(8,128)(2,1)S(1)}, u32[]{:S(2)}, u32[]{:S(2)}) collective-permute-start(bf16[352,288]{1,0:T(8,128)(2,1)S(1)} %broadcast_select_fusion.2), channel_id=1, source_target_pairs={{0,1},{1,0},{2,3},{3,2},{4,5},{5,4},{6,7},{7,6},{8,9},{9,8},{10,11... | collective-permute-start | bytes 608264 | tf_op jit(solution)/shard_map/ppermute | solution.py:31
  5.0 1.2 collective-permute-done
  6.7 3.8 %collective-permute-start.2 = (bf16[88,1152]{1,0:T(8,128)(2,1)S(1)}, bf16[88,1152]{1,0:T(8,128)(2,1)S(1)}, u32[]{:S(2)}, u32[]{:S(2)}) collective-permute-start(bf16[88,1152]{1,0:T(8,128)(2,1)S(1)} %pad_maximum_fusion.7), channel_id=1, source_target_pairs={{0,32},{1,65},{2,34},{3,67},{4,36},{5,69},{6,38},{7,71},{8,40},{9,... | collective-permute-start | bytes 608264 | tf_op jit(solution)/shard_map/ppermute | solution.py:31
  10.4 0.7 collective-permute-start.1
  11.2 0.7 collective-permute-start.5
  12.0 1.8 %collective-permute-done.2 = bf16[88,1152]{1,0:T(8,128)(2,1)S(1)} collective-permute-done((bf16[88,1152]{1,0:T(8,128)(2,1)S(1)}, bf16[88,1152]{1,0:T(8,128)(2,1)S(1)}, u32[]{:S(2)}, u32[]{:S(2)}) %collective-permute-start.2) | collective-permute-done | bytes 202784 | tf_op jit(solution)/shard_map/ppermute | solution.py:31
  13.9 3.9 %collective-permute-done.1 = bf16[88,1152]{1,0:T(8,128)(2,1)S(1)} collective-permute-done((bf16[88,1152]{1,0:T(8,128)(2,1)S(1)}, bf16[88,1152]{1,0:T(8,128)(2,1)S(1)}, u32[]{:S(2)}, u32[]{:S(2)}) %collective-permute-start.1) | collective-permute-done | bytes 202784 | tf_op jit(solution)/shard_map/ppermute | solution.py:31
  17.9 2.8 %collective-permute-start.10 = (bf16[4,88,1152]{2,1,0:T(8,128)(2,1)S(1)}, bf16[4,88,1152]{2,1,0:T(8,128)(2,1)S(1)}, u32[]{:S(2)}, u32[]{:S(2)}) collective-permute-start(bf16[4,88,1152]{2,1,0:T(8,128)(2,1)S(1)} %pad_maximum_fusion.1.refs_0_), channel_id=1, source_target_pairs={{0,66},{1,49},{2,64},{3,51},{4,70},{5,53},{6,68},{7,55},{8,74},{9,... | collective-permute-start | bytes 2433032 | tf_op jit(solution)/shard_map/ppermute | solution.py:31
  20.8 2.6 %collective-permute-start.8 = (bf16[88,1152]{1,0:T(8,128)(2,1)S(1)}, bf16[88,1152]{1,0:T(8,128)(2,1)S(1)}, u32[]{:S(2)}, u32[]{:S(2)}) collective-permute-start(bf16[88,1152]{1,0:T(8,128)(2,1)S(1)} %pad_maximum_fusion.8), channel_id=1, source_target_pairs={{0,12},{1,13},{2,14},{3,15},{4,8},{5,9},{6,10},{7,11},{8,4},{9,5},... | collective-permute-start | bytes 608264 | tf_op jit(solution)/shard_map/ppermute | solution.py:31
  24.1 7.6 %collective-permute-done.8 = bf16[88,1152]{1,0:T(8,128)(2,1)S(1)} collective-permute-done((bf16[88,1152]{1,0:T(8,128)(2,1)S(1)}, bf16[88,1152]{1,0:T(8,128)(2,1)S(1)}, u32[]{:S(2)}, u32[]{:S(2)}) %collective-permute-start.8) | collective-permute-done | bytes 202784 | tf_op jit(solution)/shard_map/ppermute | solution.py:31
  31.8 2.9 %collective-permute-start.9 = (bf16[352,1152]{1,0:T(8,128)(2,1)S(1)}, bf16[352,1152]{1,0:T(8,128)(2,1)S(1)}, u32[]{:S(2)}, u32[]{:S(2)}) collective-permute-start(bf16[352,1152]{1,0:T(8,128)(2,1)S(1)} %pad_maximum_fusion.2.refs_2_), channel_id=1, source_target_pairs={{0,1},{1,0},{2,3},{3,2},{4,5},{5,4},{6,7},{7,6},{8,9},{9,8},{10,11... | collective-permute-start | bytes 2433032 | tf_op jit(solution)/shard_map/ppermute | solution.py:31
  34.7 1.5 %collective-permute-start.11 = (bf16[4,88,1152]{2,1,0:T(8,128)(2,1)S(1)}, bf16[4,88,1152]{2,1,0:T(8,128)(2,1)S(1)}, u32[]{:S(2)}, u32[]{:S(2)}) collective-permute-start(bf16[4,88,1152]{2,1,0:T(8,128)(2,1)S(1)} %pad_maximum_fusion.1.refs_0_), channel_id=1, source_target_pairs={{0,64},{1,33},{2,66},{3,35},{4,68},{5,37},{6,70},{7,39},{8,72},{9,... | collective-permute-start | bytes 2433032 | tf_op jit(solution)/shard_map/ppermute | solution.py:31
  38.8 0.9 copy-done.18
  39.6 10.8 %tile_first.1 = (f32[352,1152]{1,0:T(8,128)}, bf16[368,1152]{1,0:T(8,128)(2,1)}, f32[704,1152]{1,0:T(8,128)}, f32[8,128]{1,0:T(8,128)}) custom-call(s32[2]{0:T(128)} %pad_add_fusion.info_ref, f32[2]{0:T(128)} %pad_maximum_fusion.10.scale_ref, bf16[4,88,1152]{2,1,0:T(8,128)(2,1)} %copy-done.4, bf16[4,88,1152]{2,1,0:T(8,128)(2,1)} %copy-done.17, ...), custom_call_target="tpu_custom_call" | custom-call | flops 3425697792 | bytes 9732096 | tf_op jit(solution)/shard_map/tile_first/pallas_call | solution.py:221
  50.5 0.9 copy-done.19
  51.4 13.5 %tile_second.1 = (bf16[368,1152]{1,0:T(8,128)(2,1)}, bf16[368,1152]{1,0:T(8,128)(2,1)}, f32[352,1152]{1,0:T(8,128)}, f32[352,1152]{1,0:T(8,128)}, f32[8,128]{1,0:T(8,128)}) custom-call(s32[2]{0:T(128)} %pad_add_fusion.info_ref, f32[2]{0:T(128)} %pad_maximum_fusion.10.scale_ref, bf16[4,88,1152]{2,1,0:T(8,128)(2,1)} %copy-done.19, ...), custom_call_target="tpu_custom_call" | custom-call | flops 3425697792 | bytes 9732096 | tf_op jit(solution)/shard_map/tile_second/pallas_call | solution.py:231
  65.3 1.5 %collective-permute-start.13 = (bf16[368,1152]{1,0:T(8,128)(2,1)S(1)}, bf16[368,1152]{1,0:T(8,128)(2,1)S(1)}, u32[]{:S(2)}, u32[]{:S(2)}) collective-permute-start(bf16[368,1152]{1,0:T(8,128)(2,1)S(1)} %copy-done.15), channel_id=1, source_target_pairs={{0,2},{1,17},{2,0},{3,19},{4,6},{5,21},{6,4},{7,23},{8,10},{9,25},... | collective-permute-start | bytes 2543624 | tf_op jit(solution)/shard_map/ppermute | solution.py:31
  66.7 2.1 %collective-permute-start.18 = (bf16[368,1152]{1,0:T(8,128)(2,1)}, bf16[368,1152]{1,0:T(8,128)(2,1)S(1)}, u32[]{:S(2)}, u32[]{:S(2)}) collective-permute-start(bf16[368,1152]{1,0:T(8,128)(2,1)} %get-tuple-element.38), channel_id=1, source_target_pairs={{0,64},{1,33},{2,66},{3,35},{4,68},{5,37},{6,70},{7,39},{8,72},{9,... | collective-permute-start | bytes 2543624 | tf_op jit(solution)/shard_map/ppermute | solution.py:31
  69.2 7.9 %collective-permute-done.13.refs_0_ = bf16[368,1152]{1,0:T(8,128)(2,1)S(1)} collective-permute-done((bf16[368,1152]{1,0:T(8,128)(2,1)S(1)}, bf16[368,1152]{1,0:T(8,128)(2,1)S(1)}, u32[]{:S(2)}, u32[]{:S(2)}) %collective-permute-start.13) | collective-permute-done | bytes 847904 | tf_op jit(solution)/shard_map/ppermute | solution.py:31
  77.1 1.2 copy-done
  78.3 3.5 %image_first.1 = (f32[88,1152]{1,0:T(8,128)}, bf16[104,1152]{1,0:T(8,128)(2,1)}, bf16[104,1152]{1,0:T(8,128)(2,1)}, bf16[104,1152]{1,0:T(8,128)(2,1)}) custom-call(f32[352,1152]{1,0:T(8,128)} %get-tuple-element.31.own_ref, f32[8,128]{1,0:T(8,128)} %get-tuple-element.37.sums_ref, f32[352,1152]{1,0:T(8,128)} %copy-done), custom_call_target="tpu_custom_call" | custom-call | tf_op jit(solution)/shard_map/image_first/pallas_call | solution.py:245
  81.9 1.2 collective-permute-start.23
  83.3 5.1 %collective-permute-done.14 = f32[8,128]{1,0:T(8,128)S(1)} collective-permute-done((f32[8,128]{1,0:T(8,128)S(1)}, f32[8,128]{1,0:T(8,128)S(1)}, u32[]{:S(2)}, u32[]{:S(2)}) %collective-permute-start.14) | collective-permute-done | bytes 4128 | tf_op jit(solution)/shard_map/ppermute | solution.py:31
  88.4 2.7 %collective-permute-start.15 = (f32[8,128]{1,0:T(8,128)S(1)}, f32[8,128]{1,0:T(8,128)S(1)}, u32[]{:S(2)}, u32[]{:S(2)}) collective-permute-start(f32[8,128]{1,0:T(8,128)S(1)} %add.21), channel_id=1, source_target_pairs={{0,8},{1,9},{2,10},{3,11},{4,12},{5,13},{6,14},{7,15},{8,0},{9,1},... | collective-permute-start | bytes 12296 | tf_op jit(solution)/shard_map/ppermute | solution.py:31
  91.2 1.2 collective-permute-done.15
  92.4 1.6 %collective-permute-start.16 = (f32[8,128]{1,0:T(8,128)S(1)}, f32[8,128]{1,0:T(8,128)S(1)}, u32[]{:S(2)}, u32[]{:S(2)}) collective-permute-start(f32[8,128]{1,0:T(8,128)S(1)} %add.22), channel_id=1, source_target_pairs={{0,2},{1,17},{2,0},{3,19},{4,6},{5,21},{6,4},{7,23},{8,10},{9,25},... | collective-permute-start | bytes 12296 | tf_op jit(solution)/shard_map/ppermute | solution.py:31
  94.0 1.2 collective-permute-done.16
  95.1 2.2 %collective-permute-start.17 = (f32[8,128]{1,0:T(8,128)S(1)}, f32[8,128]{1,0:T(8,128)S(1)}, u32[]{:S(2)}, u32[]{:S(2)}) collective-permute-start(f32[8,128]{1,0:T(8,128)S(1)} %add.23), channel_id=1, source_target_pairs={{0,64},{1,33},{2,66},{3,35},{4,68},{5,37},{6,70},{7,39},{8,72},{9,... | collective-permute-start | bytes 12296 | tf_op jit(solution)/shard_map/ppermute | solution.py:31
  97.3 2.8 %collective-permute-start.24 = (bf16[104,1152]{1,0:T(8,128)(2,1)}, bf16[104,1152]{1,0:T(8,128)(2,1)S(1)}, u32[]{:S(2)}, u32[]{:S(2)}) collective-permute-start(bf16[104,1152]{1,0:T(8,128)(2,1)} %get-tuple-element.47), channel_id=1, source_target_pairs={{0,8},{1,9},{2,10},{3,11},{4,12},{5,13},{6,14},{7,15},{8,0},{9,1},... | collective-permute-start | bytes 718856 | tf_op jit(solution)/shard_map/ppermute | solution.py:31
  100.1 1.4 %collective-permute-start.25 = (bf16[104,1152]{1,0:T(8,128)(2,1)}, bf16[104,1152]{1,0:T(8,128)(2,1)S(1)}, u32[]{:S(2)}, u32[]{:S(2)}) collective-permute-start(bf16[104,1152]{1,0:T(8,128)(2,1)} %get-tuple-element.48), channel_id=1, source_target_pairs={{0,12},{1,13},{2,14},{3,15},{4,8},{5,9},{6,10},{7,11},{8,4},{9,5},... | collective-permute-start | bytes 718856 | tf_op jit(solution)/shard_map/ppermute | solution.py:31
  102.2 0.9 copy-done.2
  103.3 6.9 %text_first.1 = (f32[88,1152]{1,0:T(8,128)}, bf16[104,1152]{1,0:T(8,128)(2,1)}, bf16[104,1152]{1,0:T(8,128)(2,1)}, bf16[104,1152]{1,0:T(8,128)(2,1)}) custom-call(f32[352,1152]{1,0:T(8,128)} %get-tuple-element.27.own_ref, f32[8,128]{1,0:T(8,128)} %add.24.sums_ref, bf16[368,1152]{1,0:T(8,128)(2,1)} %copy-done.1, bf16[368,1152]{1,0:T(8,128)(2,1)} %copy-done.2, ...), custom_call_target="tpu_custom_call" | custom-call | tf_op jit(solution)/shard_map/text_first/pallas_call | solution.py:245
  110.8 2.6 %collective-permute-start.21 = (bf16[104,1152]{1,0:T(8,128)(2,1)}, bf16[104,1152]{1,0:T(8,128)(2,1)S(1)}, u32[]{:S(2)}, u32[]{:S(2)}) collective-permute-start(bf16[104,1152]{1,0:T(8,128)(2,1)} %get-tuple-element.42), channel_id=1, source_target_pairs={{0,32},{1,65},{2,34},{3,67},{4,36},{5,69},{6,38},{7,71},{8,40},{9,... | collective-permute-start | bytes 718856 | tf_op jit(solution)/shard_map/ppermute | solution.py:31
  113.4 0.7 collective-permute-start.22
  114.9 2.6 %image_last.1 = (f32[88,1152]{1,0:T(8,128)}, f32[8,128]{1,0:T(8,128)}) custom-call(f32[1]{0:T(128)S(6)} %copy.30.scale_ref, f32[88,1152]{1,0:T(8,128)} %get-tuple-element.45.own_ref, f32[8,128]{1,0:T(8,128)} %add.24.sums_ref, bf16[104,1152]{1,0:T(8,128)(2,1)} %copy-done.7, bf16[104,1152]{1,0:T(8,128)(2,1)} %copy-done.8, bf16[104,1152]{1,0:T(8,128)(2,1)} %copy-done.10), custom_call_target="tpu_custom_call" | custom-call | tf_op jit(solution)/shard_map/image_last/pallas_call | solution.py:255
  117.5 1.1 slice.74
  118.8 1.0 collective-permute-done.21.r2_ref
  119.8 2.5 %collective-permute-done.22.r3_ref = bf16[104,1152]{1,0:T(8,128)(2,1)S(1)} collective-permute-done((bf16[104,1152]{1,0:T(8,128)(2,1)}, bf16[104,1152]{1,0:T(8,128)(2,1)S(1)}, u32[]{:S(2)}, u32[]{:S(2)}) %collective-permute-start.22) | collective-permute-done | bytes 239648 | tf_op jit(solution)/shard_map/ppermute | solution.py:31
  122.3 0.7 copy-done.12
  122.9 2.6 %text_last.1 = (f32[88,1152]{1,0:T(8,128)}, f32[8,128]{1,0:T(8,128)}) custom-call(f32[1]{0:T(128)S(6)} %copy.30.scale_ref, f32[88,1152]{1,0:T(8,128)} %get-tuple-element.40.own_ref, f32[8,128]{1,0:T(8,128)} %add.24.sums_ref, bf16[104,1152]{1,0:T(8,128)(2,1)} %copy-done.9, bf16[104,1152]{1,0:T(8,128)(2,1)} %copy-done.11, bf16[104,1152]{1,0:T(8,128)(2,1)} %copy-done.12), custom_call_target="tpu_custom_call" | custom-call | tf_op jit(solution)/shard_map/text_last/pallas_call | solution.py:255
  125.6 1.2 fusion.4
  127.7 7.0 %collective-permute-start.27 = (f32[360,288]{0,1:T(8,128)S(1)}, f32[360,288]{0,1:T(8,128)S(1)}, u32[]{:S(2)}, u32[]{:S(2)}) collective-permute-start(f32[360,288]{0,1:T(8,128)S(1)} %copy.17), channel_id=1, source_target_pairs={{0,1},{1,0},{2,3},{3,2},{4,5},{5,4},{6,7},{7,6},{8,9},{9,8},{10,11... | collective-permute-start | bytes 1244168 | tf_op jit(solution)/shard_map/ppermute | solution.py:31
  134.8 1.4 %collective-permute-done.27 = f32[360,288]{0,1:T(8,128)S(1)} collective-permute-done((f32[360,288]{0,1:T(8,128)S(1)}, f32[360,288]{0,1:T(8,128)S(1)}, u32[]{:S(2)}, u32[]{:S(2)}) %collective-permute-start.27) | collective-permute-done | bytes 414752 | tf_op jit(solution)/shard_map/ppermute | solution.py:31
  137.5 1.0 copy.21
  138.5 1.0 copy.22
  139.5 1.8 %pad_maximum_fusion.11 = f32[2]{0:T(128)} fusion(f32[1]{0:T(128)} %bitcast.7, f32[1]{0:T(128)} %bitcast.6), kind=kLoop, calls=%fused_computation.37 | loop fusion | flops 2 | bytes 16 | tf_op jit(solution)/shard_map/stack | solution.py:285
  (94 shorter events, 9.1 us)
Async XLA Ops:
  3.5 2.7 %collective-permute-start = (bf16[352,288]{1,0:T(8,128)(2,1)S(1)}, bf16[352,288]{1,0:T(8,128)(2,1)S(1)}, u32[]{:S(2)}, u32[]{:S(2)}) collective-permute-start(bf16[352,288]{1,0:T(8,128)(2,1)S(1)} %broadcast_select_fusion.2), channel_id=1, source_target_pairs={{0,1},{1,0},{2,3},{3,2},{4,5},{5,4},{6,7},{7,6},{8,9},{9,8},{10,11... | collective-permute-start | bytes 608264 | tf_op jit(solution)/shard_map/ppermute | solution.py:31
  6.7 7.2 %collective-permute-start.2 = (bf16[88,1152]{1,0:T(8,128)(2,1)S(1)}, bf16[88,1152]{1,0:T(8,128)(2,1)S(1)}, u32[]{:S(2)}, u32[]{:S(2)}) collective-permute-start(bf16[88,1152]{1,0:T(8,128)(2,1)S(1)} %pad_maximum_fusion.7), channel_id=1, source_target_pairs={{0,32},{1,65},{2,34},{3,67},{4,36},{5,69},{6,38},{7,71},{8,40},{9,... | collective-permute-start | bytes 608264 | tf_op jit(solution)/shard_map/ppermute | solution.py:31
  10.4 7.3 %collective-permute-start.1 = (bf16[88,1152]{1,0:T(8,128)(2,1)S(1)}, bf16[88,1152]{1,0:T(8,128)(2,1)S(1)}, u32[]{:S(2)}, u32[]{:S(2)}) collective-permute-start(bf16[88,1152]{1,0:T(8,128)(2,1)S(1)} %pad_maximum_fusion.7), channel_id=1, source_target_pairs={{0,16},{1,3},{2,18},{3,1},{4,20},{5,7},{6,22},{7,5},{8,24},{9,11},... | collective-permute-start | bytes 608264 | tf_op jit(solution)/shard_map/ppermute | solution.py:31
  11.2 6.5 %collective-permute-start.3 = (bf16[88,1152]{1,0:T(8,128)(2,1)S(1)}, bf16[88,1152]{1,0:T(8,128)(2,1)S(1)}, u32[]{:S(2)}, u32[]{:S(2)}) collective-permute-start(bf16[88,1152]{1,0:T(8,128)(2,1)S(1)} %pad_maximum_fusion.7), channel_id=1, source_target_pairs={{0,48},{1,67},{2,50},{3,65},{4,52},{5,71},{6,54},{7,69},{8,56},{9,... | collective-permute-start | bytes 608264 | tf_op jit(solution)/shard_map/ppermute | solution.py:31
  11.2 9.5 %collective-permute-start.5 = (bf16[88,576]{1,0:T(8,128)(2,1)S(1)}, bf16[88,576]{1,0:T(8,128)(2,1)S(1)}, u32[]{:S(2)}, u32[]{:S(2)}) collective-permute-start(bf16[88,576]{1,0:T(8,128)(2,1)S(1)} %get-tuple-element.71), channel_id=1, source_target_pairs={{0,2},{1,3},{2,0},{3,1},{4,6},{5,7},{6,4},{7,5},{8,10},{9,11},{10,... | collective-permute-start | bytes 304136 | tf_op jit(solution)/shard_map/ppermute | solution.py:31
  17.9 20.9 %copy-start.4 = (bf16[4,88,1152]{2,1,0:T(8,128)(2,1)}, bf16[4,88,1152]{2,1,0:T(8,128)(2,1)S(1)}, u32[]{:S(2)}) copy-start(bf16[4,88,1152]{2,1,0:T(8,128)(2,1)S(1)} %pad_maximum_fusion.1.refs_0_) | copy-start | bytes 2433028
  17.9 16.8 %collective-permute-start.10 = (bf16[4,88,1152]{2,1,0:T(8,128)(2,1)S(1)}, bf16[4,88,1152]{2,1,0:T(8,128)(2,1)S(1)}, u32[]{:S(2)}, u32[]{:S(2)}) collective-permute-start(bf16[4,88,1152]{2,1,0:T(8,128)(2,1)S(1)} %pad_maximum_fusion.1.refs_0_), channel_id=1, source_target_pairs={{0,66},{1,49},{2,64},{3,51},{4,70},{5,53},{6,68},{7,55},{8,74},{9,... | collective-permute-start | bytes 2433032 | tf_op jit(solution)/shard_map/ppermute | solution.py:31
  20.7 14.0 %collective-permute-start.4 = (bf16[4,88,1152]{2,1,0:T(8,128)(2,1)S(1)}, bf16[4,88,1152]{2,1,0:T(8,128)(2,1)S(1)}, u32[]{:S(2)}, u32[]{:S(2)}) collective-permute-start(bf16[4,88,1152]{2,1,0:T(8,128)(2,1)S(1)} %pad_maximum_fusion.1.refs_0_), channel_id=1, source_target_pairs={{0,2},{1,17},{2,0},{3,19},{4,6},{5,21},{6,4},{7,23},{8,10},{9,25},... | collective-permute-start | bytes 2433032 | tf_op jit(solution)/shard_map/ppermute | solution.py:31
  20.8 11.0 %collective-permute-start.8 = (bf16[88,1152]{1,0:T(8,128)(2,1)S(1)}, bf16[88,1152]{1,0:T(8,128)(2,1)S(1)}, u32[]{:S(2)}, u32[]{:S(2)}) collective-permute-start(bf16[88,1152]{1,0:T(8,128)(2,1)S(1)} %pad_maximum_fusion.8), channel_id=1, source_target_pairs={{0,12},{1,13},{2,14},{3,15},{4,8},{5,9},{6,10},{7,11},{8,4},{9,5},... | collective-permute-start | bytes 608264 | tf_op jit(solution)/shard_map/ppermute | solution.py:31
  23.3 8.4 %collective-permute-start.7 = (bf16[88,1152]{1,0:T(8,128)(2,1)S(1)}, bf16[88,1152]{1,0:T(8,128)(2,1)S(1)}, u32[]{:S(2)}, u32[]{:S(2)}) collective-permute-start(bf16[88,1152]{1,0:T(8,128)(2,1)S(1)} %pad_maximum_fusion.8), channel_id=1, source_target_pairs={{0,8},{1,9},{2,10},{3,11},{4,12},{5,13},{6,14},{7,15},{8,0},{9,1},... | collective-permute-start | bytes 608264 | tf_op jit(solution)/shard_map/ppermute | solution.py:31
  23.9 7.9 %collective-permute-start.6 = (bf16[88,1152]{1,0:T(8,128)(2,1)S(1)}, bf16[88,1152]{1,0:T(8,128)(2,1)S(1)}, u32[]{:S(2)}, u32[]{:S(2)}) collective-permute-start(bf16[88,1152]{1,0:T(8,128)(2,1)S(1)} %pad_maximum_fusion.8), channel_id=1, source_target_pairs={{0,4},{1,5},{2,6},{3,7},{4,0},{5,1},{6,2},{7,3},{8,12},{9,13},{10,... | collective-permute-start | bytes 608264 | tf_op jit(solution)/shard_map/ppermute | solution.py:31
  31.8 6.9 %copy-start.5 = (bf16[352,1152]{1,0:T(8,128)(2,1)}, bf16[352,1152]{1,0:T(8,128)(2,1)S(1)}, u32[]{:S(2)}) copy-start(bf16[352,1152]{1,0:T(8,128)(2,1)S(1)} %pad_maximum_fusion.2.refs_2_) | copy-start | bytes 2433028
  31.8 6.9 %collective-permute-start.9 = (bf16[352,1152]{1,0:T(8,128)(2,1)S(1)}, bf16[352,1152]{1,0:T(8,128)(2,1)S(1)}, u32[]{:S(2)}, u32[]{:S(2)}) collective-permute-start(bf16[352,1152]{1,0:T(8,128)(2,1)S(1)} %pad_maximum_fusion.2.refs_2_), channel_id=1, source_target_pairs={{0,1},{1,0},{2,3},{3,2},{4,5},{5,4},{6,7},{7,6},{8,9},{9,8},{10,11... | collective-permute-start | bytes 2433032 | tf_op jit(solution)/shard_map/ppermute | solution.py:31
  34.7 15.8 %copy-start.16 = (bf16[4,88,1152]{2,1,0:T(8,128)(2,1)}, bf16[4,88,1152]{2,1,0:T(8,128)(2,1)S(1)}, u32[]{:S(2)}) copy-start(bf16[4,88,1152]{2,1,0:T(8,128)(2,1)S(1)} %collective-permute-done.10.refs_1_) | copy-start | bytes 2433028
  34.7 4.0 %copy-start.17 = (bf16[4,88,1152]{2,1,0:T(8,128)(2,1)}, bf16[4,88,1152]{2,1,0:T(8,128)(2,1)S(1)}, u32[]{:S(2)}) copy-start(bf16[4,88,1152]{2,1,0:T(8,128)(2,1)S(1)} %collective-permute-done.4.refs_1_) | copy-start | bytes 2433028
  34.7 15.8 %collective-permute-start.11 = (bf16[4,88,1152]{2,1,0:T(8,128)(2,1)S(1)}, bf16[4,88,1152]{2,1,0:T(8,128)(2,1)S(1)}, u32[]{:S(2)}, u32[]{:S(2)}) collective-permute-start(bf16[4,88,1152]{2,1,0:T(8,128)(2,1)S(1)} %pad_maximum_fusion.1.refs_0_), channel_id=1, source_target_pairs={{0,64},{1,33},{2,66},{3,35},{4,68},{5,37},{6,70},{7,39},{8,72},{9,... | collective-permute-start | bytes 2433032 | tf_op jit(solution)/shard_map/ppermute | solution.py:31
  38.7 0.9 copy-start.18
  50.5 0.9 copy-start.19
  51.4 13.9 %copy-start.15 = (bf16[368,1152]{1,0:T(8,128)(2,1)S(1)}, bf16[368,1152]{1,0:T(8,128)(2,1)}, u32[]{:S(2)}) copy-start(bf16[368,1152]{1,0:T(8,128)(2,1)} %get-tuple-element.34) | copy-start | bytes 2543620
  64.9 12.2 %collective-permute-start.12 = (f32[352,1152]{1,0:T(8,128)}, f32[352,1152]{1,0:T(8,128)S(1)}, u32[]{:S(2)}, u32[]{:S(2)}) collective-permute-start(f32[352,1152]{1,0:T(8,128)} %get-tuple-element.33), channel_id=1, source_target_pairs={{0,1},{1,0},{2,3},{3,2},{4,5},{5,4},{6,7},{7,6},{8,9},{9,8},{10,11... | collective-permute-start | bytes 4866056 | tf_op jit(solution)/shard_map/ppermute | solution.py:31
  65.3 11.8 %collective-permute-start.13 = (bf16[368,1152]{1,0:T(8,128)(2,1)S(1)}, bf16[368,1152]{1,0:T(8,128)(2,1)S(1)}, u32[]{:S(2)}, u32[]{:S(2)}) collective-permute-start(bf16[368,1152]{1,0:T(8,128)(2,1)S(1)} %copy-done.15), channel_id=1, source_target_pairs={{0,2},{1,17},{2,0},{3,19},{4,6},{5,21},{6,4},{7,23},{8,10},{9,25},... | collective-permute-start | bytes 2543624 | tf_op jit(solution)/shard_map/ppermute | solution.py:31
  66.7 35.4 %collective-permute-start.18 = (bf16[368,1152]{1,0:T(8,128)(2,1)}, bf16[368,1152]{1,0:T(8,128)(2,1)S(1)}, u32[]{:S(2)}, u32[]{:S(2)}) collective-permute-start(bf16[368,1152]{1,0:T(8,128)(2,1)} %get-tuple-element.38), channel_id=1, source_target_pairs={{0,64},{1,33},{2,66},{3,35},{4,68},{5,37},{6,70},{7,39},{8,72},{9,... | collective-permute-start | bytes 2543624 | tf_op jit(solution)/shard_map/ppermute | solution.py:31
  68.8 33.3 %collective-permute-start.19 = (bf16[368,1152]{1,0:T(8,128)(2,1)}, bf16[368,1152]{1,0:T(8,128)(2,1)S(1)}, u32[]{:S(2)}, u32[]{:S(2)}) collective-permute-start(bf16[368,1152]{1,0:T(8,128)(2,1)} %get-tuple-element.39), channel_id=1, source_target_pairs={{0,66},{1,49},{2,64},{3,51},{4,70},{5,53},{6,68},{7,55},{8,74},{9,... | collective-permute-start | bytes 2543624 | tf_op jit(solution)/shard_map/ppermute | solution.py:31
  77.1 25.1 %copy-start.1 = (bf16[368,1152]{1,0:T(8,128)(2,1)}, bf16[368,1152]{1,0:T(8,128)(2,1)S(1)}, u32[]{:S(2)}) copy-start(bf16[368,1152]{1,0:T(8,128)(2,1)S(1)} %collective-permute-done.13.refs_0_) | copy-start | bytes 2543620
  77.1 1.2 copy-start
  78.3 4.7 %copy-start.13 = (f32[8,128]{1,0:T(8,128)S(1)}, f32[8,128]{1,0:T(8,128)}, u32[]{:S(2)}) copy-start(f32[8,128]{1,0:T(8,128)} %get-tuple-element.37.sums_ref) | copy-start | bytes 12292
  81.9 31.5 %collective-permute-start.23 = (bf16[104,1152]{1,0:T(8,128)(2,1)}, bf16[104,1152]{1,0:T(8,128)(2,1)S(1)}, u32[]{:S(2)}, u32[]{:S(2)}) collective-permute-start(bf16[104,1152]{1,0:T(8,128)(2,1)} %get-tuple-element.46), channel_id=1, source_target_pairs={{0,4},{1,5},{2,6},{3,7},{4,0},{5,1},{6,2},{7,3},{8,12},{9,13},{10,... | collective-permute-start | bytes 718856 | tf_op jit(solution)/shard_map/ppermute | solution.py:31
  83.1 5.4 %collective-permute-start.14 = (f32[8,128]{1,0:T(8,128)S(1)}, f32[8,128]{1,0:T(8,128)S(1)}, u32[]{:S(2)}, u32[]{:S(2)}) collective-permute-start(f32[8,128]{1,0:T(8,128)S(1)} %copy-done.13), channel_id=1, source_target_pairs={{0,4},{1,5},{2,6},{3,7},{4,0},{5,1},{6,2},{7,3},{8,12},{9,13},{10,... | collective-permute-start | bytes 12296 | tf_op jit(solution)/shard_map/ppermute | solution.py:31
  88.4 4.0 %collective-permute-start.15 = (f32[8,128]{1,0:T(8,128)S(1)}, f32[8,128]{1,0:T(8,128)S(1)}, u32[]{:S(2)}, u32[]{:S(2)}) collective-permute-start(f32[8,128]{1,0:T(8,128)S(1)} %add.21), channel_id=1, source_target_pairs={{0,8},{1,9},{2,10},{3,11},{4,12},{5,13},{6,14},{7,15},{8,0},{9,1},... | collective-permute-start | bytes 12296 | tf_op jit(solution)/shard_map/ppermute | solution.py:31
  92.4 2.7 %collective-permute-start.16 = (f32[8,128]{1,0:T(8,128)S(1)}, f32[8,128]{1,0:T(8,128)S(1)}, u32[]{:S(2)}, u32[]{:S(2)}) collective-permute-start(f32[8,128]{1,0:T(8,128)S(1)} %add.22), channel_id=1, source_target_pairs={{0,2},{1,17},{2,0},{3,19},{4,6},{5,21},{6,4},{7,23},{8,10},{9,25},... | collective-permute-start | bytes 12296 | tf_op jit(solution)/shard_map/ppermute | solution.py:31
  95.1 5.0 %collective-permute-start.17 = (f32[8,128]{1,0:T(8,128)S(1)}, f32[8,128]{1,0:T(8,128)S(1)}, u32[]{:S(2)}, u32[]{:S(2)}) collective-permute-start(f32[8,128]{1,0:T(8,128)S(1)} %add.23), channel_id=1, source_target_pairs={{0,64},{1,33},{2,66},{3,35},{4,68},{5,37},{6,70},{7,39},{8,72},{9,... | collective-permute-start | bytes 12296 | tf_op jit(solution)/shard_map/ppermute | solution.py:31
  97.3 16.8 %collective-permute-start.24 = (bf16[104,1152]{1,0:T(8,128)(2,1)}, bf16[104,1152]{1,0:T(8,128)(2,1)S(1)}, u32[]{:S(2)}, u32[]{:S(2)}) collective-permute-start(bf16[104,1152]{1,0:T(8,128)(2,1)} %get-tuple-element.47), channel_id=1, source_target_pairs={{0,8},{1,9},{2,10},{3,11},{4,12},{5,13},{6,14},{7,15},{8,0},{9,1},... | collective-permute-start | bytes 718856 | tf_op jit(solution)/shard_map/ppermute | solution.py:31
  100.1 14.0 %collective-permute-start.25 = (bf16[104,1152]{1,0:T(8,128)(2,1)}, bf16[104,1152]{1,0:T(8,128)(2,1)S(1)}, u32[]{:S(2)}, u32[]{:S(2)}) collective-permute-start(bf16[104,1152]{1,0:T(8,128)(2,1)} %get-tuple-element.48), channel_id=1, source_target_pairs={{0,12},{1,13},{2,14},{3,15},{4,8},{5,9},{6,10},{7,11},{8,4},{9,5},... | collective-permute-start | bytes 718856 | tf_op jit(solution)/shard_map/ppermute | solution.py:31
  102.2 0.9 copy-start.2
  102.2 1.2 copy-start.3
  110.2 8.5 %collective-permute-start.20 = (bf16[104,1152]{1,0:T(8,128)(2,1)}, bf16[104,1152]{1,0:T(8,128)(2,1)S(1)}, u32[]{:S(2)}, u32[]{:S(2)}) collective-permute-start(bf16[104,1152]{1,0:T(8,128)(2,1)} %get-tuple-element.41), channel_id=1, source_target_pairs={{0,16},{1,3},{2,18},{3,1},{4,20},{5,7},{6,22},{7,5},{8,24},{9,11},... | collective-permute-start | bytes 718856 | tf_op jit(solution)/shard_map/ppermute | solution.py:31
  110.8 9.0 %collective-permute-start.21 = (bf16[104,1152]{1,0:T(8,128)(2,1)}, bf16[104,1152]{1,0:T(8,128)(2,1)S(1)}, u32[]{:S(2)}, u32[]{:S(2)}) collective-permute-start(bf16[104,1152]{1,0:T(8,128)(2,1)} %get-tuple-element.42), channel_id=1, source_target_pairs={{0,32},{1,65},{2,34},{3,67},{4,36},{5,69},{6,38},{7,71},{8,40},{9,... | collective-permute-start | bytes 718856 | tf_op jit(solution)/shard_map/ppermute | solution.py:31
  113.4 0.7 copy-start.7
  113.4 8.9 %collective-permute-start.22 = (bf16[104,1152]{1,0:T(8,128)(2,1)}, bf16[104,1152]{1,0:T(8,128)(2,1)S(1)}, u32[]{:S(2)}, u32[]{:S(2)}) collective-permute-start(bf16[104,1152]{1,0:T(8,128)(2,1)} %get-tuple-element.43), channel_id=1, source_target_pairs={{0,48},{1,67},{2,50},{3,65},{4,52},{5,71},{6,54},{7,69},{8,56},{9,... | collective-permute-start | bytes 718856 | tf_op jit(solution)/shard_map/ppermute | solution.py:31
  114.1 0.7 copy-start.8
  114.1 0.8 copy-start.10
  117.5 9.2 %copy-start.6 = (f32[88,1152]{1,0:T(8,128)S(1)}, f32[88,1152]{1,0:T(8,128)}, u32[]{:S(2)}) copy-start(f32[88,1152]{1,0:T(8,128)} %get-tuple-element.49) | copy-start | bytes 1216516
  118.7 8.1 %collective-permute-start.26 = (f32[88,576]{1,0:T(8,128)S(1)}, f32[88,576]{1,0:T(8,128)S(1)}, u32[]{:S(2)}, u32[]{:S(2)}) collective-permute-start(f32[88,576]{1,0:T(8,128)S(1)} %slice.74), channel_id=1, source_target_pairs={{0,2},{1,3},{2,0},{3,1},{4,6},{5,7},{6,4},{7,5},{8,10},{9,11},{10,... | collective-permute-start | bytes 608264 | tf_op jit(solution)/shard_map/ppermute | solution.py:31
  118.8 3.5 %copy-start.9 = (bf16[104,1152]{1,0:T(8,128)(2,1)}, bf16[104,1152]{1,0:T(8,128)(2,1)S(1)}, u32[]{:S(2)}) copy-start(bf16[104,1152]{1,0:T(8,128)(2,1)S(1)} %collective-permute-done.20.r1_ref) | copy-start | bytes 718852
  119.8 2.5 %copy-start.11 = (bf16[104,1152]{1,0:T(8,128)(2,1)}, bf16[104,1152]{1,0:T(8,128)(2,1)S(1)}, u32[]{:S(2)}) copy-start(bf16[104,1152]{1,0:T(8,128)(2,1)S(1)} %collective-permute-done.21.r2_ref) | copy-start | bytes 718852
  122.3 0.7 copy-start.12
  126.8 0.7 copy-start.14
  127.7 8.4 %collective-permute-start.27 = (f32[360,288]{0,1:T(8,128)S(1)}, f32[360,288]{0,1:T(8,128)S(1)}, u32[]{:S(2)}, u32[]{:S(2)}) collective-permute-start(f32[360,288]{0,1:T(8,128)S(1)} %copy.17), channel_id=1, source_target_pairs={{0,1},{1,0},{2,3},{3,2},{4,5},{5,4},{6,7},{7,6},{8,9},{9,8},{10,11... | collective-permute-start | bytes 1244168 | tf_op jit(solution)/shard_map/ppermute | solution.py:31

commit v3 on v2

--- a/solution.py
+++ b/solution.py
@@ -97,9 +97,8 @@
         coeff_low[b * step : (b + 1) * step, :] = coeff.astype(BF)
         temp = temp + jnp.sum(coeff * part, axis=0, keepdims=True)
         bias = bias + jnp.sum(coeff, axis=0, keepdims=True)
-    sums = jnp.concatenate(
-        [jnp.broadcast_to(jnp.sum(v, axis=1, keepdims=True), (4, 128)) for v in (temp, bias)], axis=0
-    )
+    even = lax.broadcasted_iota(jnp.int32, (8, 128), 1) % 2 == 0
+    sums = jnp.where(even, jnp.sum(temp, axis=1, keepdims=True), jnp.sum(bias, axis=1, keepdims=True))
     text_part = jnp.dot(coeff_low[...], images[...], preferred_element_type=F32)
     for b in range(4):
         top = text_part[b * step : b * step + rows]
@@ -141,11 +140,11 @@
     for r in received:
         total = total + (decode(r[0:quarter], r[quarter : quarter + 16].astype(F32)[0:1, :]) if coded else r[...])
     out_ref[...] = total[0:rows]
-    scalars = [jnp.broadcast_to(v, (1, feats)) for at in (0, 4) for v in split3(sums_ref[at : at + 1, 0:1])]
+    scalars = [jnp.concatenate([v] * (feats // 128), axis=1) for v in split3(sums_ref[0:1, :])]
     for i, m_ref in ((1, m1_ref), (2, m2_ref), (3, m3_ref)):
         part = total[i * rows : (i + 1) * rows]
         m = top_of(jnp.max(jnp.max(jnp.abs(part), axis=0, keepdims=True), axis=1, keepdims=True))
-        m = jnp.broadcast_to(m, (10, feats))
+        m = jnp.broadcast_to(m, (13, feats))
         m_ref[...] = jnp.concatenate([encode(part, m[0:1]), *scalars, m], axis=0).astype(BF)
 
 
@@ -155,20 +154,17 @@
     for whole in wholes:
         total = total + decode(whole[0:rows], whole[rows + 8 : rows + 9])
     out_ref[...] = total * scale_ref[0]
-    extra = [whole[rows : rows + 8, 0:128] for whole in wholes]
-
-    def three(e, at):
-        return e[at : at + 1] + (e[at + 1 : at + 2] + e[at + 2 : at + 3])
-
-    for at, src in ((0, 0), (4, 3)):
-        a, b, c = (three(e, src) for e in extra)
-        sums_out[at : at + 4, :] = jnp.broadcast_to((sums_ref[at : at + 1, :] + a) + (b + c), (4, 128))
+    a, b, c = (w[rows : rows + 1, :128] + (w[rows + 1 : rows + 2, :128] + w[rows + 2 : rows + 3, :128]) for w in wholes)
+    sums_out[...] = jnp.broadcast_to((sums_ref[0:1, :] + a) + (b + c), (8, 128))
 
 
 VMEM = pl.BlockSpec(memory_space=pltpu.VMEM)
 SMEM = pl.BlockSpec(memory_space=pltpu.SMEM)
 HBM = pl.BlockSpec(memory_space=pl.ANY)
-BIG = pltpu.CompilerParams(vmem_limit_bytes=56 * 1024 * 1024)
+
+
+def grant(mib):
+    return pltpu.CompilerParams(vmem_limit_bytes=mib * 1024 * 1024)
 
 
 def after(array, *others):
@@ -224,7 +220,7 @@
         in_specs=[SMEM, SMEM] + [HBM] * 4,
         out_specs=(VMEM,) * 4,
         scratch_shapes=scratch,
-        compiler_params=BIG,
+        compiler_params=grant(40),
         cost_estimate=cost,
         name="tile_first",
     )(info, scales, stack, second1, images_own, images_other)
@@ -234,7 +230,7 @@
         in_specs=[SMEM, SMEM] + [HBM] * 4 + [VMEM] * 2,
         out_specs=(VMEM,) * 5,
         scratch_shapes=scratch,
-        compiler_params=BIG,
+        compiler_params=grant(40),
         cost_estimate=cost,
         name="tile_second",
     )(info, scales, second2, second3, images_own, images_other, acc, sums)
@@ -247,7 +243,7 @@
             out_shape=(jax.ShapeDtypeStruct((rows, feats), F32), message, message, message),
             in_specs=[VMEM] * len(args),
             out_specs=(VMEM,) * 4,
-            compiler_params=BIG,
+            compiler_params=grant(20),
             name=name,
         )(*args)
 
@@ -257,16 +253,19 @@
             out_shape=(jax.ShapeDtypeStruct((rows, feats), F32), sums_shape),
             in_specs=[SMEM] + [VMEM] * 5,
             out_specs=(VMEM, VMEM),
-            compiler_params=BIG,
+            compiler_params=grant(10),
             name=name,
         )(logit_scaler, *args)
 
     got1 = swap(m1, z_mask(1), y_mask(1))
-    img, i1, i2, i3 = first_sum("image_first", False, img_own, sums, after(swap(img_other, CORE), got1))
+    m2, m3, img_other, sums, got1 = lax.optimization_barrier((m2, m3, img_other, sums, got1))
     got2, got3 = swap(m2, z_mask(2), y_mask(2)), swap(m3, z_mask(3), y_mask(3))
-    i1, sums = lax.optimization_barrier((i1, sums))
+    img_got, one = swap(img_other, CORE), swap(sums, x_mask(1))
+    img, i1, i2, i3 = first_sum("image_first", False, img_own, sums, img_got)
+    i1, i2, i3, one = lax.optimization_barrier((i1, i2, i3, one))
+    sums = sums + one
     img_got = [swap(m, x_mask(k)) for k, m in ((1, i1), (2, i2), (3, i3))]
-    for mask in ((x_mask(1),), (x_mask(2),), (z_mask(1), y_mask(1)), (z_mask(2), y_mask(2))):
+    for mask in ((x_mask(2),), (z_mask(1), y_mask(1)), (z_mask(2), y_mask(2))):
         sums = sums + swap(sums, *mask)
 
     text, n1, n2, n3 = first_sum("text_first", True, text_own, sums, got1, got2, got3)
@@ -282,7 +281,7 @@
     text_grad = jnp.concatenate(by(on0, mine[:step], other[:step]), axis=0)
     image_grad = jnp.concatenate(by(on0, mine[step:], other[step : 2 * step]), axis=0)
     sums = sums + other[2 * step :, :128]
-    scalar_grads = jnp.stack([sums[0, 0], sums[4, 0]])
+    scalar_grads = sums[0, :2]
     return (image_grad, text_grad, scalar_grads)
 
 

time: 142 us -> 106 us (0.75)
  Pallas kernels: 40 us -> 22.5 us
  local copies, waits for them, and re-layouts: 14.4 us -> 6.2 us
  starting transfers between devices: 44.7 us -> 39.9 us
  other arithmetic: 5.12 us -> 1.63 us
    unnamed x49 -> x9, local copies, waits for them, and re-layouts: 8.87 us -> 2.82 us
    pallas_call x2, Pallas kernels: 10.4 us -> 5.04 us  [first_sum(): pl.pallas_call(functools.partial(first_sum_kernel, rows, feats, coded), o...]
    pallas_call x1, Pallas kernels: 13.5 us -> 8.67 us  [body(): pl.pallas_call(functools.partial(tile_kernel, False, rows, half, feats),...]
    ppermute x28, starting transfers between devices: 44.7 us -> 39.9 us  [swap(): lax.ppermute(array, AXES, [(i, i ^ (mask1 if i & 1 else mask0)) for i in...]
    pallas_call x2, Pallas kernels: 5.27 us -> 1.24 us  [last_sum(): pl.pallas_call(functools.partial(last_sum_kernel, rows), out_shape=(jax.S...]
    pallas_call x1, Pallas kernels: 10.8 us -> 7.5 us  [body(): pl.pallas_call(functools.partial(tile_kernel, True, rows, half, feats), o...]
    another operation x1 -> x0, other arithmetic: 1.85 us -> none  [body(): scalar_grads = jnp.stack([sums[0, 0], sums[4, 0]])]
    ppermute x28, waiting for transfers between devices: 34.8 us -> 33.4 us  [swap(): lax.ppermute(array, AXES, [(i, i ^ (mask1 if i & 1 else mask0)) for i in...]
  transfers between devices with their start and end apart: 28 -> 28, of which waited for: 11 -> 16; matrix products, arithmetic and copies ran while one was open for 3% -> 1% of each run, Pallas kernels for 19% -> 21%
where the time goes in v3:
time: 106 us
  starting transfers between devices  39.9 us (38%)
  waiting for transfers between devices  33.4 us (32%)
  Pallas kernels  22.5 us (21%)
  local copies, waits for them, and re-layouts  6.2 us (6%)
  between operations  2.18 us (2%)
  other arithmetic  1.63 us (2%)
    ppermute x28, starting transfers between devices, swap(): lax.ppermute(array, AXES, [(i, i ^ (mask1 if i & 1 else mask0)) for i in...  39.9 us
    ppermute x28, waiting for transfers between devices, swap(): lax.ppermute(array, AXES, [(i, i ^ (mask1 if i & 1 else mask0)) for i in...  33.4 us
    pallas_call x1, Pallas kernels, body(): pl.pallas_call(functools.partial(tile_kernel, False, rows, half, feats),...  8.67 us
    pallas_call x1, Pallas kernels, body(): pl.pallas_call(functools.partial(tile_kernel, True, rows, half, feats), o...  7.5 us
    pallas_call x2, Pallas kernels, first_sum(): pl.pallas_call(functools.partial(first_sum_kernel, rows, feats, coded), o...  5.04 us
    unnamed x9, local copies, waits for them, and re-layouts  2.82 us
  transfers between devices with their start and end apart: 28, of which 16 were waited for; matrix products, arithmetic and copies ran while one was open for 1% of the time, Pallas kernels for 21%

profile of v3, /device:TPU:1, one launch (start us, length us, event | category | flops | bytes accessed | tf_op | source)
XLA Modules:
  0.0 105.8 jit_solution(527893383002833050)
XLA Ops:
  0.6 1.1 %fusion.6 = (bf16[176,288]{0,1:T(8,128)(2,1)S(1)}, bf16[176,288]{0,1:T(8,128)(2,1)S(1)}) fusion(bf16[352,288]{0,1:T(8,128)(2,1)} %param.4), kind=kLoop, calls=%fused_computation.41 | loop fusion | bytes 405504 | tf_op jit(solution)/shard_map/slice | solution.py:186
  2.0 1.1 %fusion.5 = (bf16[176,288]{0,1:T(8,128)(2,1)S(1)}, bf16[176,288]{0,1:T(8,128)(2,1)S(1)}) fusion(bf16[352,288]{0,1:T(8,128)(2,1)} %param.5), kind=kLoop, calls=%fused_computation.40 | loop fusion | bytes 405504 | tf_op jit(solution)/shard_map/slice | solution.py:186
  3.5 1.5 %collective-permute-start = (bf16[352,288]{1,0:T(8,128)(2,1)S(1)}, bf16[352,288]{1,0:T(8,128)(2,1)S(1)}, u32[]{:S(2)}, u32[]{:S(2)}) collective-permute-start(bf16[352,288]{1,0:T(8,128)(2,1)S(1)} %broadcast_select_fusion.2), channel_id=1, source_target_pairs={{0,1},{1,0},{2,3},{3,2},{4,5},{5,4},{6,7},{7,6},{8,9},{9,8},{10,11... | collective-permute-start | bytes 608264 | tf_op jit(solution)/shard_map/ppermute | solution.py:31
  5.0 1.2 %collective-permute-done = bf16[352,288]{1,0:T(8,128)(2,1)S(1)} collective-permute-done((bf16[352,288]{1,0:T(8,128)(2,1)S(1)}, bf16[352,288]{1,0:T(8,128)(2,1)S(1)}, u32[]{:S(2)}, u32[]{:S(2)}) %collective-permute-start) | collective-permute-done | bytes 202784 | tf_op jit(solution)/shard_map/ppermute | solution.py:31
  6.6 1.8 %collective-permute-start.5 = (bf16[88,576]{1,0:T(8,128)(2,1)S(1)}, bf16[88,576]{1,0:T(8,128)(2,1)S(1)}, u32[]{:S(2)}, u32[]{:S(2)}) collective-permute-start(bf16[88,576]{1,0:T(8,128)(2,1)S(1)} %get-tuple-element.83), channel_id=1, source_target_pairs={{0,2},{1,3},{2,0},{3,1},{4,6},{5,7},{6,4},{7,5},{8,10},{9,11},{10,... | collective-permute-start | bytes 304136 | tf_op jit(solution)/shard_map/ppermute | solution.py:31
  8.6 3.4 %collective-permute-start.2 = (bf16[88,1152]{1,0:T(8,128)(2,1)S(1)}, bf16[88,1152]{1,0:T(8,128)(2,1)S(1)}, u32[]{:S(2)}, u32[]{:S(2)}) collective-permute-start(bf16[88,1152]{1,0:T(8,128)(2,1)S(1)} %pad_maximum_fusion.7), channel_id=1, source_target_pairs={{0,32},{1,65},{2,34},{3,67},{4,36},{5,69},{6,38},{7,71},{8,40},{9,... | collective-permute-start | bytes 608264 | tf_op jit(solution)/shard_map/ppermute | solution.py:31
  12.5 2.6 %collective-permute-start.8 = (bf16[88,1152]{1,0:T(8,128)(2,1)S(1)}, bf16[88,1152]{1,0:T(8,128)(2,1)S(1)}, u32[]{:S(2)}, u32[]{:S(2)}) collective-permute-start(bf16[88,1152]{1,0:T(8,128)(2,1)S(1)} %pad_maximum_fusion.8), channel_id=1, source_target_pairs={{0,12},{1,13},{2,14},{3,15},{4,8},{5,9},{6,10},{7,11},{8,4},{9,5},... | collective-permute-start | bytes 608264 | tf_op jit(solution)/shard_map/ppermute | solution.py:31
  15.0 0.5 collective-permute-start.7
  15.5 1.8 %collective-permute-done.2 = bf16[88,1152]{1,0:T(8,128)(2,1)S(1)} collective-permute-done((bf16[88,1152]{1,0:T(8,128)(2,1)S(1)}, bf16[88,1152]{1,0:T(8,128)(2,1)S(1)}, u32[]{:S(2)}, u32[]{:S(2)}) %collective-permute-start.2) | collective-permute-done | bytes 202784 | tf_op jit(solution)/shard_map/ppermute | solution.py:31
  17.3 1.2 %collective-permute-start.6 = (bf16[88,1152]{1,0:T(8,128)(2,1)S(1)}, bf16[88,1152]{1,0:T(8,128)(2,1)S(1)}, u32[]{:S(2)}, u32[]{:S(2)}) collective-permute-start(bf16[88,1152]{1,0:T(8,128)(2,1)S(1)} %pad_maximum_fusion.8), channel_id=1, source_target_pairs={{0,4},{1,5},{2,6},{3,7},{4,0},{5,1},{6,2},{7,3},{8,12},{9,13},{10,... | collective-permute-start | bytes 608264 | tf_op jit(solution)/shard_map/ppermute | solution.py:31
  18.5 1.0 collective-permute-done.3
  19.7 2.8 %collective-permute-start.10 = (bf16[4,88,1152]{2,1,0:T(8,128)(2,1)S(1)}, bf16[4,88,1152]{2,1,0:T(8,128)(2,1)S(1)}, u32[]{:S(2)}, u32[]{:S(2)}) collective-permute-start(bf16[4,88,1152]{2,1,0:T(8,128)(2,1)S(1)} %pad_maximum_fusion.1.refs_0_), channel_id=1, source_target_pairs={{0,66},{1,49},{2,64},{3,51},{4,70},{5,53},{6,68},{7,55},{8,74},{9,... | collective-permute-start | bytes 2433032 | tf_op jit(solution)/shard_map/ppermute | solution.py:31
  22.5 1.1 collective-permute-done.8
  23.6 0.8 collective-permute-done.6
  24.4 1.9 %collective-permute-start.9 = (bf16[352,1152]{1,0:T(8,128)(2,1)S(1)}, bf16[352,1152]{1,0:T(8,128)(2,1)S(1)}, u32[]{:S(2)}, u32[]{:S(2)}) collective-permute-start(bf16[352,1152]{1,0:T(8,128)(2,1)S(1)} %pad_maximum_fusion.2.refs_2_), channel_id=1, source_target_pairs={{0,1},{1,0},{2,3},{3,2},{4,5},{5,4},{6,7},{7,6},{8,9},{9,8},{10,11... | collective-permute-start | bytes 2433032 | tf_op jit(solution)/shard_map/ppermute | solution.py:31
  27.8 4.7 %collective-permute-done.10.refs_1_ = bf16[4,88,1152]{2,1,0:T(8,128)(2,1)S(1)} collective-permute-done((bf16[4,88,1152]{2,1,0:T(8,128)(2,1)S(1)}, bf16[4,88,1152]{2,1,0:T(8,128)(2,1)S(1)}, u32[]{:S(2)}, u32[]{:S(2)}) %collective-permute-start.10) | collective-permute-done | bytes 811040 | tf_op jit(solution)/shard_map/ppermute | solution.py:31
  32.4 1.5 %collective-permute-done.4.refs_1_ = bf16[4,88,1152]{2,1,0:T(8,128)(2,1)S(1)} collective-permute-done((bf16[4,88,1152]{2,1,0:T(8,128)(2,1)S(1)}, bf16[4,88,1152]{2,1,0:T(8,128)(2,1)S(1)}, u32[]{:S(2)}, u32[]{:S(2)}) %collective-permute-start.4) | collective-permute-done | bytes 811040 | tf_op jit(solution)/shard_map/ppermute | solution.py:31
  34.3 7.5 %tile_first.1 = (f32[352,1152]{1,0:T(8,128)S(1)}, bf16[368,1152]{1,0:T(8,128)(2,1)S(1)}, f32[704,1152]{1,0:T(8,128)S(1)}, f32[8,128]{1,0:T(8,128)S(1)}) custom-call(s32[2]{0:T(128)S(1)} %pad_add_fusion.info_ref, f32[2]{0:T(128)S(1)} %pad_maximum_fusion.10.scale_ref, bf16[4,88,1152]{2,1,0:T(8,128)(2,1)S(1)} %pad_maximum_fusion.1.refs_0_, ...), custom_call_target="tpu_custom_call" | custom-call | flops 3425697792 | bytes 9732096 | tf_op jit(solution)/shard_map/tile_first/pallas_call | solution.py:217
  41.8 1.4 %collective-permute-start.12 = (bf16[368,1152]{1,0:T(8,128)(2,1)S(1)}, bf16[368,1152]{1,0:T(8,128)(2,1)S(1)}, u32[]{:S(2)}, u32[]{:S(2)}) collective-permute-start(bf16[368,1152]{1,0:T(8,128)(2,1)S(1)} %get-tuple-element.41), channel_id=1, source_target_pairs={{0,2},{1,17},{2,0},{3,19},{4,6},{5,21},{6,4},{7,23},{8,10},{9,25},... | collective-permute-start | bytes 2543624 | tf_op jit(solution)/shard_map/ppermute | solution.py:31
  43.2 3.6 %collective-permute-done.11.refs_0_ = bf16[4,88,1152]{2,1,0:T(8,128)(2,1)S(1)} collective-permute-done((bf16[4,88,1152]{2,1,0:T(8,128)(2,1)S(1)}, bf16[4,88,1152]{2,1,0:T(8,128)(2,1)S(1)}, u32[]{:S(2)}, u32[]{:S(2)}) %collective-permute-start.11) | collective-permute-done | bytes 811040 | tf_op jit(solution)/shard_map/ppermute | solution.py:31
  46.8 8.7 %tile_second.1 = (bf16[368,1152]{1,0:T(8,128)(2,1)S(1)}, bf16[368,1152]{1,0:T(8,128)(2,1)S(1)}, f32[352,1152]{1,0:T(8,128)S(1)}, f32[352,1152]{1,0:T(8,128)S(1)}, f32[8,128]{1,0:T(8,128)S(1)}) custom-call(s32[2]{0:T(128)S(1)} %pad_add_fusion.info_ref, f32[2]{0:T(128)S(1)} %pad_maximum_fusion.10.scale_ref, ...), custom_call_target="tpu_custom_call" | custom-call | flops 3425697792 | bytes 9732096 | tf_op jit(solution)/shard_map/tile_second/pallas_call | solution.py:227
  55.5 2.2 %collective-permute-start.13 = (f32[352,1152]{1,0:T(8,128)S(1)}, f32[352,1152]{1,0:T(8,128)S(1)}, u32[]{:S(2)}, u32[]{:S(2)}) collective-permute-start(f32[352,1152]{1,0:T(8,128)S(1)} %get-tuple-element.44), channel_id=1, source_target_pairs={{0,1},{1,0},{2,3},{3,2},{4,5},{5,4},{6,7},{7,6},{8,9},{9,8},{10,11... | collective-permute-start | bytes 4866056 | tf_op jit(solution)/shard_map/ppermute | solution.py:31
  57.6 1.6 %collective-permute-start.18 = (bf16[368,1152]{1,0:T(8,128)(2,1)S(1)}, bf16[368,1152]{1,0:T(8,128)(2,1)S(1)}, u32[]{:S(2)}, u32[]{:S(2)}) collective-permute-start(bf16[368,1152]{1,0:T(8,128)(2,1)S(1)} %get-tuple-element.50), channel_id=1, source_target_pairs={{0,64},{1,33},{2,66},{3,35},{4,68},{5,37},{6,70},{7,39},{8,72},{9,... | collective-permute-start | bytes 2543624 | tf_op jit(solution)/shard_map/ppermute | solution.py:31
  59.3 0.8 collective-permute-start.19
  60.1 1.2 %collective-permute-start.14 = (f32[8,128]{1,0:T(8,128)S(1)}, f32[8,128]{1,0:T(8,128)S(1)}, u32[]{:S(2)}, u32[]{:S(2)}) collective-permute-start(f32[8,128]{1,0:T(8,128)S(1)} %get-tuple-element.42.sums_ref), channel_id=1, source_target_pairs={{0,4},{1,5},{2,6},{3,7},{4,0},{5,1},{6,2},{7,3},{8,12},{9,13},{10,... | collective-permute-start | bytes 12296 | tf_op jit(solution)/shard_map/ppermute | solution.py:31
  61.3 1.0 image_first.1
  62.2 0.6 collective-permute-done.14
  62.8 1.2 %collective-permute-start.23 = (bf16[104,1152]{1,0:T(8,128)(2,1)S(1)}, bf16[104,1152]{1,0:T(8,128)(2,1)S(1)}, u32[]{:S(2)}, u32[]{:S(2)}) collective-permute-start(bf16[104,1152]{1,0:T(8,128)(2,1)S(1)} %get-tuple-element.58), channel_id=1, source_target_pairs={{0,4},{1,5},{2,6},{3,7},{4,0},{5,1},{6,2},{7,3},{8,12},{9,13},{10,... | collective-permute-start | bytes 718856 | tf_op jit(solution)/shard_map/ppermute | solution.py:31
  64.0 2.5 %collective-permute-start.15 = (f32[8,128]{1,0:T(8,128)S(1)}, f32[8,128]{1,0:T(8,128)S(1)}, u32[]{:S(2)}, u32[]{:S(2)}) collective-permute-start(f32[8,128]{1,0:T(8,128)S(1)} %add.21), channel_id=1, source_target_pairs={{0,8},{1,9},{2,10},{3,11},{4,12},{5,13},{6,14},{7,15},{8,0},{9,1},... | collective-permute-start | bytes 12296 | tf_op jit(solution)/shard_map/ppermute | solution.py:31
  66.5 3.8 %collective-permute-done.15 = f32[8,128]{1,0:T(8,128)S(1)} collective-permute-done((f32[8,128]{1,0:T(8,128)S(1)}, f32[8,128]{1,0:T(8,128)S(1)}, u32[]{:S(2)}, u32[]{:S(2)}) %collective-permute-start.15) | collective-permute-done | bytes 4128 | tf_op jit(solution)/shard_map/ppermute | solution.py:31
  70.7 2.4 %collective-permute-done.16 = f32[8,128]{1,0:T(8,128)S(1)} collective-permute-done((f32[8,128]{1,0:T(8,128)S(1)}, f32[8,128]{1,0:T(8,128)S(1)}, u32[]{:S(2)}, u32[]{:S(2)}) %collective-permute-start.16) | collective-permute-done | bytes 4128 | tf_op jit(solution)/shard_map/ppermute | solution.py:31
  73.1 2.1 %collective-permute-start.17 = (f32[8,128]{1,0:T(8,128)S(1)}, f32[8,128]{1,0:T(8,128)S(1)}, u32[]{:S(2)}, u32[]{:S(2)}) collective-permute-start(f32[8,128]{1,0:T(8,128)S(1)} %add.23), channel_id=1, source_target_pairs={{0,64},{1,33},{2,66},{3,35},{4,68},{5,37},{6,70},{7,39},{8,72},{9,... | collective-permute-start | bytes 12296 | tf_op jit(solution)/shard_map/ppermute | solution.py:31
  75.7 1.5 %collective-permute-done.17 = f32[8,128]{1,0:T(8,128)S(1)} collective-permute-done((f32[8,128]{1,0:T(8,128)S(1)}, f32[8,128]{1,0:T(8,128)S(1)}, u32[]{:S(2)}, u32[]{:S(2)}) %collective-permute-start.17) | collective-permute-done | bytes 4128 | tf_op jit(solution)/shard_map/ppermute | solution.py:31
  77.5 2.6 %collective-permute-done.19.refs_2_ = bf16[368,1152]{1,0:T(8,128)(2,1)S(1)} collective-permute-done((bf16[368,1152]{1,0:T(8,128)(2,1)S(1)}, bf16[368,1152]{1,0:T(8,128)(2,1)S(1)}, u32[]{:S(2)}, u32[]{:S(2)}) %collective-permute-start.19) | collective-permute-done | bytes 847904 | tf_op jit(solution)/shard_map/ppermute | solution.py:31
  80.1 4.1 %text_first.1 = (f32[88,1152]{1,0:T(8,128)S(1)}, bf16[104,1152]{1,0:T(8,128)(2,1)S(1)}, bf16[104,1152]{1,0:T(8,128)(2,1)S(1)}, bf16[104,1152]{1,0:T(8,128)(2,1)S(1)}) custom-call(f32[352,1152]{1,0:T(8,128)S(1)} %get-tuple-element.33.own_ref, f32[8,128]{1,0:T(8,128)S(1)} %add.24.sums_ref, bf16[368,1152]{1,0:T(8,128)(2,1)S(1)} %collective-permute-done.12.refs_0_, ...), custom_call_target="tpu_custom_call" | custom-call | tf_op jit(solution)/shard_map/text_first/pallas_call | solution.py:241
  84.2 0.5 collective-permute-start.20
  84.7 2.0 %collective-permute-start.21 = (bf16[104,1152]{1,0:T(8,128)(2,1)S(1)}, bf16[104,1152]{1,0:T(8,128)(2,1)S(1)}, u32[]{:S(2)}, u32[]{:S(2)}) collective-permute-start(bf16[104,1152]{1,0:T(8,128)(2,1)S(1)} %get-tuple-element.54), channel_id=1, source_target_pairs={{0,32},{1,65},{2,34},{3,67},{4,36},{5,69},{6,38},{7,71},{8,40},{9,... | collective-permute-start | bytes 718856 | tf_op jit(solution)/shard_map/ppermute | solution.py:31
  86.7 1.4 %collective-permute-start.22 = (bf16[104,1152]{1,0:T(8,128)(2,1)S(1)}, bf16[104,1152]{1,0:T(8,128)(2,1)S(1)}, u32[]{:S(2)}, u32[]{:S(2)}) collective-permute-start(bf16[104,1152]{1,0:T(8,128)(2,1)S(1)} %get-tuple-element.55), channel_id=1, source_target_pairs={{0,48},{1,67},{2,50},{3,65},{4,52},{5,71},{6,54},{7,69},{8,56},{9,... | collective-permute-start | bytes 718856 | tf_op jit(solution)/shard_map/ppermute | solution.py:31
  88.1 0.6 image_last.1
  88.9 1.5 %collective-permute-start.26 = (f32[88,576]{1,0:T(8,128)S(1)}, f32[88,576]{1,0:T(8,128)S(1)}, u32[]{:S(2)}, u32[]{:S(2)}) collective-permute-start(f32[88,576]{1,0:T(8,128)S(1)} %slice.71), channel_id=1, source_target_pairs={{0,2},{1,3},{2,0},{3,1},{4,6},{5,7},{6,4},{7,5},{8,10},{9,11},{10,... | collective-permute-start | bytes 608264 | tf_op jit(solution)/shard_map/ppermute | solution.py:31
  90.3 2.6 %collective-permute-done.21.r2_ref = bf16[104,1152]{1,0:T(8,128)(2,1)S(1)} collective-permute-done((bf16[104,1152]{1,0:T(8,128)(2,1)S(1)}, bf16[104,1152]{1,0:T(8,128)(2,1)S(1)}, u32[]{:S(2)}, u32[]{:S(2)}) %collective-permute-start.21) | collective-permute-done | bytes 239648 | tf_op jit(solution)/shard_map/ppermute | solution.py:31
  92.9 2.8 %collective-permute-done.22.r3_ref = bf16[104,1152]{1,0:T(8,128)(2,1)S(1)} collective-permute-done((bf16[104,1152]{1,0:T(8,128)(2,1)S(1)}, bf16[104,1152]{1,0:T(8,128)(2,1)S(1)}, u32[]{:S(2)}, u32[]{:S(2)}) %collective-permute-start.22) | collective-permute-done | bytes 239648 | tf_op jit(solution)/shard_map/ppermute | solution.py:31
  95.7 0.6 text_last.1
  97.0 4.1 %collective-permute-start.27 = (f32[360,288]{0,1:T(8,128)S(1)}, f32[360,288]{0,1:T(8,128)S(1)}, u32[]{:S(2)}, u32[]{:S(2)}) collective-permute-start(f32[360,288]{0,1:T(8,128)S(1)} %copy.17), channel_id=1, source_target_pairs={{0,1},{1,0},{2,3},{3,2},{4,5},{5,4},{6,7},{7,6},{8,9},{9,8},{10,11... | collective-permute-start | bytes 1244168 | tf_op jit(solution)/shard_map/ppermute | solution.py:31
  101.1 1.4 %collective-permute-done.27 = f32[360,288]{0,1:T(8,128)S(1)} collective-permute-done((f32[360,288]{0,1:T(8,128)S(1)}, f32[360,288]{0,1:T(8,128)S(1)}, u32[]{:S(2)}, u32[]{:S(2)}) %collective-permute-start.27) | collective-permute-done | bytes 414752 | tf_op jit(solution)/shard_map/ppermute | solution.py:31
  102.7 0.5 slice_bitcast_fusion
  103.8 1.0 copy.21
  104.8 1.0 copy.22
  (53 shorter events, 5.1 us)
Async XLA Ops:
  3.5 2.7 %collective-permute-start = (bf16[352,288]{1,0:T(8,128)(2,1)S(1)}, bf16[352,288]{1,0:T(8,128)(2,1)S(1)}, u32[]{:S(2)}, u32[]{:S(2)}) collective-permute-start(bf16[352,288]{1,0:T(8,128)(2,1)S(1)} %broadcast_select_fusion.2), channel_id=1, source_target_pairs={{0,1},{1,0},{2,3},{3,2},{4,5},{5,4},{6,7},{7,6},{8,9},{9,8},{10,11... | collective-permute-start | bytes 608264 | tf_op jit(solution)/shard_map/ppermute | solution.py:31
  6.6 5.8 %collective-permute-start.5 = (bf16[88,576]{1,0:T(8,128)(2,1)S(1)}, bf16[88,576]{1,0:T(8,128)(2,1)S(1)}, u32[]{:S(2)}, u32[]{:S(2)}) collective-permute-start(bf16[88,576]{1,0:T(8,128)(2,1)S(1)} %get-tuple-element.83), channel_id=1, source_target_pairs={{0,2},{1,3},{2,0},{3,1},{4,6},{5,7},{6,4},{7,5},{8,10},{9,11},{10,... | collective-permute-start | bytes 304136 | tf_op jit(solution)/shard_map/ppermute | solution.py:31
  8.6 8.7 %collective-permute-start.2 = (bf16[88,1152]{1,0:T(8,128)(2,1)S(1)}, bf16[88,1152]{1,0:T(8,128)(2,1)S(1)}, u32[]{:S(2)}, u32[]{:S(2)}) collective-permute-start(bf16[88,1152]{1,0:T(8,128)(2,1)S(1)} %pad_maximum_fusion.7), channel_id=1, source_target_pairs={{0,32},{1,65},{2,34},{3,67},{4,36},{5,69},{6,38},{7,71},{8,40},{9,... | collective-permute-start | bytes 608264 | tf_op jit(solution)/shard_map/ppermute | solution.py:31
  12.0 6.6 %collective-permute-start.1 = (bf16[88,1152]{1,0:T(8,128)(2,1)S(1)}, bf16[88,1152]{1,0:T(8,128)(2,1)S(1)}, u32[]{:S(2)}, u32[]{:S(2)}) collective-permute-start(bf16[88,1152]{1,0:T(8,128)(2,1)S(1)} %pad_maximum_fusion.7), channel_id=1, source_target_pairs={{0,16},{1,3},{2,18},{3,1},{4,20},{5,7},{6,22},{7,5},{8,24},{9,11},... | collective-permute-start | bytes 608264 | tf_op jit(solution)/shard_map/ppermute | solution.py:31
  12.0 7.6 %collective-permute-start.3 = (bf16[88,1152]{1,0:T(8,128)(2,1)S(1)}, bf16[88,1152]{1,0:T(8,128)(2,1)S(1)}, u32[]{:S(2)}, u32[]{:S(2)}) collective-permute-start(bf16[88,1152]{1,0:T(8,128)(2,1)S(1)} %pad_maximum_fusion.7), channel_id=1, source_target_pairs={{0,48},{1,67},{2,50},{3,65},{4,52},{5,71},{6,54},{7,69},{8,56},{9,... | collective-permute-start | bytes 608264 | tf_op jit(solution)/shard_map/ppermute | solution.py:31
  12.5 11.1 %collective-permute-start.8 = (bf16[88,1152]{1,0:T(8,128)(2,1)S(1)}, bf16[88,1152]{1,0:T(8,128)(2,1)S(1)}, u32[]{:S(2)}, u32[]{:S(2)}) collective-permute-start(bf16[88,1152]{1,0:T(8,128)(2,1)S(1)} %pad_maximum_fusion.8), channel_id=1, source_target_pairs={{0,12},{1,13},{2,14},{3,15},{4,8},{5,9},{6,10},{7,11},{8,4},{9,5},... | collective-permute-start | bytes 608264 | tf_op jit(solution)/shard_map/ppermute | solution.py:31
  15.0 8.5 %collective-permute-start.7 = (bf16[88,1152]{1,0:T(8,128)(2,1)S(1)}, bf16[88,1152]{1,0:T(8,128)(2,1)S(1)}, u32[]{:S(2)}, u32[]{:S(2)}) collective-permute-start(bf16[88,1152]{1,0:T(8,128)(2,1)S(1)} %pad_maximum_fusion.8), channel_id=1, source_target_pairs={{0,8},{1,9},{2,10},{3,11},{4,12},{5,13},{6,14},{7,15},{8,0},{9,1},... | collective-permute-start | bytes 608264 | tf_op jit(solution)/shard_map/ppermute | solution.py:31
  17.3 7.0 %collective-permute-start.6 = (bf16[88,1152]{1,0:T(8,128)(2,1)S(1)}, bf16[88,1152]{1,0:T(8,128)(2,1)S(1)}, u32[]{:S(2)}, u32[]{:S(2)}) collective-permute-start(bf16[88,1152]{1,0:T(8,128)(2,1)S(1)} %pad_maximum_fusion.8), channel_id=1, source_target_pairs={{0,4},{1,5},{2,6},{3,7},{4,0},{5,1},{6,2},{7,3},{8,12},{9,13},{10,... | collective-permute-start | bytes 608264 | tf_op jit(solution)/shard_map/ppermute | solution.py:31
  19.7 12.8 %collective-permute-start.10 = (bf16[4,88,1152]{2,1,0:T(8,128)(2,1)S(1)}, bf16[4,88,1152]{2,1,0:T(8,128)(2,1)S(1)}, u32[]{:S(2)}, u32[]{:S(2)}) collective-permute-start(bf16[4,88,1152]{2,1,0:T(8,128)(2,1)S(1)} %pad_maximum_fusion.1.refs_0_), channel_id=1, source_target_pairs={{0,66},{1,49},{2,64},{3,51},{4,70},{5,53},{6,68},{7,55},{8,74},{9,... | collective-permute-start | bytes 2433032 | tf_op jit(solution)/shard_map/ppermute | solution.py:31
  22.5 11.4 %collective-permute-start.4 = (bf16[4,88,1152]{2,1,0:T(8,128)(2,1)S(1)}, bf16[4,88,1152]{2,1,0:T(8,128)(2,1)S(1)}, u32[]{:S(2)}, u32[]{:S(2)}) collective-permute-start(bf16[4,88,1152]{2,1,0:T(8,128)(2,1)S(1)} %pad_maximum_fusion.1.refs_0_), channel_id=1, source_target_pairs={{0,2},{1,17},{2,0},{3,19},{4,6},{5,21},{6,4},{7,23},{8,10},{9,25},... | collective-permute-start | bytes 2433032 | tf_op jit(solution)/shard_map/ppermute | solution.py:31
  24.4 9.8 %collective-permute-start.9 = (bf16[352,1152]{1,0:T(8,128)(2,1)S(1)}, bf16[352,1152]{1,0:T(8,128)(2,1)S(1)}, u32[]{:S(2)}, u32[]{:S(2)}) collective-permute-start(bf16[352,1152]{1,0:T(8,128)(2,1)S(1)} %pad_maximum_fusion.2.refs_2_), channel_id=1, source_target_pairs={{0,1},{1,0},{2,3},{3,2},{4,5},{5,4},{6,7},{7,6},{8,9},{9,8},{10,11... | collective-permute-start | bytes 2433032 | tf_op jit(solution)/shard_map/ppermute | solution.py:31
  33.9 12.9 %collective-permute-start.11 = (bf16[4,88,1152]{2,1,0:T(8,128)(2,1)S(1)}, bf16[4,88,1152]{2,1,0:T(8,128)(2,1)S(1)}, u32[]{:S(2)}, u32[]{:S(2)}) collective-permute-start(bf16[4,88,1152]{2,1,0:T(8,128)(2,1)S(1)} %pad_maximum_fusion.1.refs_0_), channel_id=1, source_target_pairs={{0,64},{1,33},{2,66},{3,35},{4,68},{5,37},{6,70},{7,39},{8,72},{9,... | collective-permute-start | bytes 2433032 | tf_op jit(solution)/shard_map/ppermute | solution.py:31
  41.8 13.7 %collective-permute-start.12 = (bf16[368,1152]{1,0:T(8,128)(2,1)S(1)}, bf16[368,1152]{1,0:T(8,128)(2,1)S(1)}, u32[]{:S(2)}, u32[]{:S(2)}) collective-permute-start(bf16[368,1152]{1,0:T(8,128)(2,1)S(1)} %get-tuple-element.41), channel_id=1, source_target_pairs={{0,2},{1,17},{2,0},{3,19},{4,6},{5,21},{6,4},{7,23},{8,10},{9,25},... | collective-permute-start | bytes 2543624 | tf_op jit(solution)/shard_map/ppermute | solution.py:31
  55.5 5.8 %collective-permute-start.13 = (f32[352,1152]{1,0:T(8,128)S(1)}, f32[352,1152]{1,0:T(8,128)S(1)}, u32[]{:S(2)}, u32[]{:S(2)}) collective-permute-start(f32[352,1152]{1,0:T(8,128)S(1)} %get-tuple-element.44), channel_id=1, source_target_pairs={{0,1},{1,0},{2,3},{3,2},{4,5},{5,4},{6,7},{7,6},{8,9},{9,8},{10,11... | collective-permute-start | bytes 4866056 | tf_op jit(solution)/shard_map/ppermute | solution.py:31
  57.6 19.8 %collective-permute-start.18 = (bf16[368,1152]{1,0:T(8,128)(2,1)S(1)}, bf16[368,1152]{1,0:T(8,128)(2,1)S(1)}, u32[]{:S(2)}, u32[]{:S(2)}) collective-permute-start(bf16[368,1152]{1,0:T(8,128)(2,1)S(1)} %get-tuple-element.50), channel_id=1, source_target_pairs={{0,64},{1,33},{2,66},{3,35},{4,68},{5,37},{6,70},{7,39},{8,72},{9,... | collective-permute-start | bytes 2543624 | tf_op jit(solution)/shard_map/ppermute | solution.py:31
  59.3 20.8 %collective-permute-start.19 = (bf16[368,1152]{1,0:T(8,128)(2,1)S(1)}, bf16[368,1152]{1,0:T(8,128)(2,1)S(1)}, u32[]{:S(2)}, u32[]{:S(2)}) collective-permute-start(bf16[368,1152]{1,0:T(8,128)(2,1)S(1)} %get-tuple-element.51), channel_id=1, source_target_pairs={{0,66},{1,49},{2,64},{3,51},{4,70},{5,53},{6,68},{7,55},{8,74},{9,... | collective-permute-start | bytes 2543624 | tf_op jit(solution)/shard_map/ppermute | solution.py:31
  60.1 2.8 %collective-permute-start.14 = (f32[8,128]{1,0:T(8,128)S(1)}, f32[8,128]{1,0:T(8,128)S(1)}, u32[]{:S(2)}, u32[]{:S(2)}) collective-permute-start(f32[8,128]{1,0:T(8,128)S(1)} %get-tuple-element.42.sums_ref), channel_id=1, source_target_pairs={{0,4},{1,5},{2,6},{3,7},{4,0},{5,1},{6,2},{7,3},{8,12},{9,13},{10,... | collective-permute-start | bytes 12296 | tf_op jit(solution)/shard_map/ppermute | solution.py:31
  62.8 23.9 %collective-permute-start.23 = (bf16[104,1152]{1,0:T(8,128)(2,1)S(1)}, bf16[104,1152]{1,0:T(8,128)(2,1)S(1)}, u32[]{:S(2)}, u32[]{:S(2)}) collective-permute-start(bf16[104,1152]{1,0:T(8,128)(2,1)S(1)} %get-tuple-element.58), channel_id=1, source_target_pairs={{0,4},{1,5},{2,6},{3,7},{4,0},{5,1},{6,2},{7,3},{8,12},{9,13},{10,... | collective-permute-start | bytes 718856 | tf_op jit(solution)/shard_map/ppermute | solution.py:31
  64.0 6.3 %collective-permute-start.15 = (f32[8,128]{1,0:T(8,128)S(1)}, f32[8,128]{1,0:T(8,128)S(1)}, u32[]{:S(2)}, u32[]{:S(2)}) collective-permute-start(f32[8,128]{1,0:T(8,128)S(1)} %add.21), channel_id=1, source_target_pairs={{0,8},{1,9},{2,10},{3,11},{4,12},{5,13},{6,14},{7,15},{8,0},{9,1},... | collective-permute-start | bytes 12296 | tf_op jit(solution)/shard_map/ppermute | solution.py:31
  70.3 2.8 %collective-permute-start.16 = (f32[8,128]{1,0:T(8,128)S(1)}, f32[8,128]{1,0:T(8,128)S(1)}, u32[]{:S(2)}, u32[]{:S(2)}) collective-permute-start(f32[8,128]{1,0:T(8,128)S(1)} %add.22), channel_id=1, source_target_pairs={{0,2},{1,17},{2,0},{3,19},{4,6},{5,21},{6,4},{7,23},{8,10},{9,25},... | collective-permute-start | bytes 12296 | tf_op jit(solution)/shard_map/ppermute | solution.py:31
  73.1 4.1 %collective-permute-start.17 = (f32[8,128]{1,0:T(8,128)S(1)}, f32[8,128]{1,0:T(8,128)S(1)}, u32[]{:S(2)}, u32[]{:S(2)}) collective-permute-start(f32[8,128]{1,0:T(8,128)S(1)} %add.23), channel_id=1, source_target_pairs={{0,64},{1,33},{2,66},{3,35},{4,68},{5,37},{6,70},{7,39},{8,72},{9,... | collective-permute-start | bytes 12296 | tf_op jit(solution)/shard_map/ppermute | solution.py:31
  75.1 13.0 %collective-permute-start.24 = (bf16[104,1152]{1,0:T(8,128)(2,1)S(1)}, bf16[104,1152]{1,0:T(8,128)(2,1)S(1)}, u32[]{:S(2)}, u32[]{:S(2)}) collective-permute-start(bf16[104,1152]{1,0:T(8,128)(2,1)S(1)} %get-tuple-element.59), channel_id=1, source_target_pairs={{0,8},{1,9},{2,10},{3,11},{4,12},{5,13},{6,14},{7,15},{8,0},{9,1},... | collective-permute-start | bytes 718856 | tf_op jit(solution)/shard_map/ppermute | solution.py:31
  77.2 11.0 %collective-permute-start.25 = (bf16[104,1152]{1,0:T(8,128)(2,1)S(1)}, bf16[104,1152]{1,0:T(8,128)(2,1)S(1)}, u32[]{:S(2)}, u32[]{:S(2)}) collective-permute-start(bf16[104,1152]{1,0:T(8,128)(2,1)S(1)} %get-tuple-element.60), channel_id=1, source_target_pairs={{0,12},{1,13},{2,14},{3,15},{4,8},{5,9},{6,10},{7,11},{8,4},{9,5},... | collective-permute-start | bytes 718856 | tf_op jit(solution)/shard_map/ppermute | solution.py:31
  84.2 6.2 %collective-permute-start.20 = (bf16[104,1152]{1,0:T(8,128)(2,1)S(1)}, bf16[104,1152]{1,0:T(8,128)(2,1)S(1)}, u32[]{:S(2)}, u32[]{:S(2)}) collective-permute-start(bf16[104,1152]{1,0:T(8,128)(2,1)S(1)} %get-tuple-element.53), channel_id=1, source_target_pairs={{0,16},{1,3},{2,18},{3,1},{4,20},{5,7},{6,22},{7,5},{8,24},{9,11},... | collective-permute-start | bytes 718856 | tf_op jit(solution)/shard_map/ppermute | solution.py:31
  84.7 8.2 %collective-permute-start.21 = (bf16[104,1152]{1,0:T(8,128)(2,1)S(1)}, bf16[104,1152]{1,0:T(8,128)(2,1)S(1)}, u32[]{:S(2)}, u32[]{:S(2)}) collective-permute-start(bf16[104,1152]{1,0:T(8,128)(2,1)S(1)} %get-tuple-element.54), channel_id=1, source_target_pairs={{0,32},{1,65},{2,34},{3,67},{4,36},{5,69},{6,38},{7,71},{8,40},{9,... | collective-permute-start | bytes 718856 | tf_op jit(solution)/shard_map/ppermute | solution.py:31
  86.7 8.9 %collective-permute-start.22 = (bf16[104,1152]{1,0:T(8,128)(2,1)S(1)}, bf16[104,1152]{1,0:T(8,128)(2,1)S(1)}, u32[]{:S(2)}, u32[]{:S(2)}) collective-permute-start(bf16[104,1152]{1,0:T(8,128)(2,1)S(1)} %get-tuple-element.55), channel_id=1, source_target_pairs={{0,48},{1,67},{2,50},{3,65},{4,52},{5,71},{6,54},{7,69},{8,56},{9,... | collective-permute-start | bytes 718856 | tf_op jit(solution)/shard_map/ppermute | solution.py:31
  88.9 7.6 %collective-permute-start.26 = (f32[88,576]{1,0:T(8,128)S(1)}, f32[88,576]{1,0:T(8,128)S(1)}, u32[]{:S(2)}, u32[]{:S(2)}) collective-permute-start(f32[88,576]{1,0:T(8,128)S(1)} %slice.71), channel_id=1, source_target_pairs={{0,2},{1,3},{2,0},{3,1},{4,6},{5,7},{6,4},{7,5},{8,10},{9,11},{10,... | collective-permute-start | bytes 608264 | tf_op jit(solution)/shard_map/ppermute | solution.py:31
  97.0 5.5 %collective-permute-start.27 = (f32[360,288]{0,1:T(8,128)S(1)}, f32[360,288]{0,1:T(8,128)S(1)}, u32[]{:S(2)}, u32[]{:S(2)}) collective-permute-start(f32[360,288]{0,1:T(8,128)S(1)} %copy.17), channel_id=1, source_target_pairs={{0,1},{1,0},{2,3},{3,2},{4,5},{5,4},{6,7},{7,6},{8,9},{9,8},{10,11... | collective-permute-start | bytes 1244168 | tf_op jit(solution)/shard_map/ppermute | solution.py:31

commit v4 on v3

v4 whole, which is shorter than its diff:
```python
import functools

import jax
import jax.numpy as jnp
from jax import lax
from jax.experimental import pallas as pl
from jax.experimental.pallas import tpu as pltpu
from jax.sharding import PartitionSpec as P

BF = jnp.bfloat16
F32 = jnp.float32
AXES = ("batch", "dim")
CORE = 1


def x_mask(k):
    return k << 2


def y_mask(k):
    return k << 4


def z_mask(k):
    return ((k >> 1) << 6) | ((k & 1) << 1)


def swap(array, mask0, mask1=None):
    mask1 = mask0 if mask1 is None else mask1
    n = lax.axis_size("batch") * lax.axis_size("dim")
    return lax.ppermute(array, AXES, [(i, i ^ (mask1 if i & 1 else mask0)) for i in range(n)])


LOW = 2.0**-3.5


def encode(v, m):
    a = jnp.abs(v) * (127.0 * LOW / m) + LOW
    for _ in range(5):
        a = a * a
    return jnp.where(v < 0, -a, a)


def decode(code, m):
    c = code.astype(F32)
    a = jnp.exp(jnp.log(jnp.abs(c)) * (1.0 / 32.0)) * (1.0 / LOW) - 1.0
    v = a * (m * (1.0 / 127.0))
    return jnp.where(c < 0, -v, v)


def top_of(largest):
    return (largest * 1.01 + 1e-30).astype(BF).astype(F32)


def tile_kernel(last, rows, half, feats, info_ref, scale_ref, t0_ref, t1_ref, t2_ref, t3_ref, im0_ref, im1_ref, *refs):
    if last:
        before_ref, sums_before, own_ref, m1_ref, m2_ref, m3_ref, img0_ref, img1_ref, sums_ref, *scratch = refs
    else:
        own_ref, m1_ref, m2_ref, m3_ref, acc_ref, sums_ref, *scratch = refs
    texts, images, t_rel, coeff_low, grads, sems = scratch
    core, z_lo = info_ref[0], info_ref[1]
    scaling, offset = scale_ref[0], scale_ref[1]
    quarter, step = 4 * rows, 2 * rows
    copies = [
        pltpu.make_async_copy(src, texts.at[j], sems.at[j]) for j, src in enumerate((t0_ref, t1_ref, t2_ref, t3_ref))
    ] + [
        pltpu.make_async_copy(src, images.at[pl.ds(o * quarter, quarter)], sems.at[4 + o])
        for o, src in enumerate((im0_ref, im1_ref))
    ]
    for copy in copies:
        copy.start()
    for copy in copies:
        copy.wait()

    def place(b, e):
        return jnp.where(core == 0, 2 * (b >> 1) + e, b), jnp.where(core == 0, b & 1, e)

    for b in range(4):
        p0, p1 = (texts[place(b, e)].astype(F32) for e in range(2))
        top = jnp.concatenate([p0[:, :half], p1[:, :half]], axis=1)
        bottom = jnp.concatenate([p0[:, half:], p1[:, half:]], axis=1)
        t_rel[b * step : (b + 1) * step, :] = jnp.concatenate([top, bottom], axis=0).astype(BF)
    similar = lax.dot_general(t_rel[...], images[...], (((1,), (1,)), ((), ())), preferred_element_type=F32)
    temp, bias = jnp.zeros((1, 2 * quarter), F32), jnp.zeros((1, 2 * quarter), F32)
    for b in range(4):
        part = similar[b * step : (b + 1) * step]
        logits = scaling * part + offset
        if last and b == 0:
            row = lax.broadcasted_iota(jnp.int32, part.shape, 0)
            column = lax.broadcasted_iota(jnp.int32, part.shape, 1)
            matched = (row - rows * z_lo == column) & (column < rows)
            sig = 1.0 / (1.0 + jnp.exp(jnp.where(matched, logits, -logits)))
            coeff = jnp.where(matched, -sig, sig)
        else:
            coeff = 1.0 / (1.0 + jnp.exp(-logits))
        coeff_low[b * step : (b + 1) * step, :] = coeff.astype(BF)
        temp = temp + jnp.sum(coeff * part, axis=0, keepdims=True)
        bias = bias + jnp.sum(coeff, axis=0, keepdims=True)
    even = lax.broadcasted_iota(jnp.int32, (8, 128), 1) % 2 == 0
    sums = jnp.where(even, jnp.sum(temp, axis=1, keepdims=True), jnp.sum(bias, axis=1, keepdims=True))
    text_part = jnp.dot(coeff_low[...], images[...], preferred_element_type=F32)
    for b in range(4):
        top = text_part[b * step : b * step + rows]
        bottom = text_part[b * step + rows : (b + 1) * step]
        grads[place(b, 0)] = jnp.concatenate([top[:, :half], bottom[:, :half]], axis=1)
        grads[place(b, 1)] = jnp.concatenate([top[:, half:], bottom[:, half:]], axis=1)
    acc = lax.dot_general(coeff_low[...], t_rel[...], (((0,), (0,)), ((), ())), preferred_element_type=F32)

    own_ref[...] = jnp.concatenate([grads[0, i] for i in range(2)], axis=0)
    for k, m_ref in ((1, m1_ref), (2, m2_ref), (3, m3_ref)):
        m_ref[...] = message([grads[k, i] for i in range(2)], feats)
    if last:
        acc = acc + before_ref[...]
        img0_ref[...] = acc[0:quarter]
        img1_ref[...] = acc[quarter : 2 * quarter]
        sums_ref[...] = sums + sums_before[...]
    else:
        acc_ref[...] = acc
        sums_ref[...] = sums


def message(blocks, feats, extra=()):
    part = jnp.concatenate(blocks, axis=0)
    m = top_of(jnp.max(jnp.max(jnp.abs(part), axis=0, keepdims=True), axis=1, keepdims=True))
    tail = jnp.broadcast_to(m, (8 - len(extra), feats))
    return jnp.concatenate([encode(part, m), *extra, tail], axis=0).astype(BF)


def decoded(ref):
    whole = ref[...].astype(F32)
    n = whole.shape[0] - 8
    return decode(whole[:n], whole[n + 7 : n + 8]), whole[n:]


def split3(v):
    hi = v.astype(BF).astype(F32)
    mid = (v - hi).astype(BF).astype(F32)
    return [hi, mid, v - hi - mid]


def image_first_kernel(rows, feats, own_ref, other_ref, sums_ref, out_ref, *messages):
    total = own_ref[...] + other_ref[...]
    out_ref[...] = total[0:rows]
    scalars = [jnp.concatenate([v] * (feats // 128), axis=1) for v in split3(sums_ref[0:1, :])]
    for i, m_ref in enumerate(messages):
        m_ref[...] = message([total[(i + 1) * rows : (i + 2) * rows]], feats, scalars)


def image_last_kernel(rows, feats, scale_ref, own_ref, sums_ref, r1_ref, r2_ref, r3_ref, out_ref):
    total, tails = own_ref[...], []
    for r in (r1_ref, r2_ref, r3_ref):
        value, tail = decoded(r)
        total = total + value
        tails.append(tail[0:1, :128] + (tail[1:2, :128] + tail[2:3, :128]))
    sums = (sums_ref[0:1, :] + tails[0]) + (tails[1] + tails[2])
    sums = jnp.broadcast_to(jnp.concatenate([sums] * (feats // 128), axis=1), (8, feats))
    out_ref[...] = jnp.concatenate([total * scale_ref[0], sums], axis=0)


def text_first_kernel(rows, feats, keep, own_ref, r1_ref, r2_ref, r3_ref, *out_refs):
    total = own_ref[...]
    for r in (r1_ref, r2_ref, r3_ref):
        total = total + decoded(r)[0]
    for i, out_ref in enumerate(out_refs):
        block = total[i * rows : (i + 1) * rows]
        out_ref[...] = block if keep and i == 0 else message([block], feats)


def text_last_kernel(scale_ref, own_ref, r1_ref, r2_ref, r3_ref, out_ref):
    total = own_ref[...]
    for r in (r1_ref, r2_ref, r3_ref):
        total = total + decoded(r)[0]
    out_ref[...] = total * scale_ref[0]


VMEM = pl.BlockSpec(memory_space=pltpu.VMEM)
SMEM = pl.BlockSpec(memory_space=pltpu.SMEM)
HBM = pl.BlockSpec(memory_space=pl.ANY)


def grant(mib):
    return pltpu.CompilerParams(vmem_limit_bytes=mib * 1024 * 1024)


def after(array, *others):
    return lax.optimization_barrier((array, *others))[0]


def body(picture_embeds, caption_embeds, logit_scaler, logit_offset_term):
    height, width = picture_embeds.shape
    rows, half, feats = height // 4, 2 * width, 4 * width
    step, quarter = 2 * rows, 4 * rows
    index = lax.axis_index("batch") * lax.axis_size("dim") + lax.axis_index("dim")
    core, z_lo = index & 1, (index >> 1) & 1
    on0, lo0 = core == 0, z_lo == 0
    scaling = logit_scaler[0]

    def by(first_one, own, other):
        return [jnp.where(first_one, own, other), jnp.where(first_one, other, own)]

    both = [jnp.concatenate([t[:step], i[:step]]) for t, i in ((caption_embeds, picture_embeds),)]
    both.append(jnp.concatenate([caption_embeds[step:], picture_embeds[step:]]))
    keep, send = by(on0, *both)
    chip = jnp.concatenate(by(on0, keep, swap(send, CORE)), axis=1)
    packed = jnp.concatenate([chip[:rows], chip[rows:step]], axis=1)
    keep, send = by(lo0, chip[step : step + rows], chip[step + rows :])
    first = [packed] + [swap(packed, y_mask(i), z_mask(i)) for i in range(1, 4)]
    image = after(jnp.concatenate([keep, swap(send, z_mask(1))], axis=1), first[1])
    images = [swap(image, x_mask(k)) for k in range(1, 4)]

    def fetch(stack):
        return [stack] + [swap(stack, z_mask(j), y_mask(j)) for j in range(1, 4)]

    texts_a = fetch(jnp.stack(first[2:]))
    images[0] = after(images[0], texts_a[1], texts_a[3])
    images_own = jnp.concatenate([image, *images], axis=0)
    images_other = swap(images_own, CORE)
    texts_b = fetch(after(jnp.stack(first[:2]), texts_a[1], texts_a[3]))

    def small(n, shape, dtype=F32):
        return [jax.ShapeDtypeStruct(shape, dtype)] * n

    def tile(last, *args):
        images = small(2, (quarter, feats)) if last else small(1, (2 * quarter, feats))
        out_shape = small(1, (step, feats)) + small(3, (step + 8, feats), BF) + images + small(1, (8, 128))
        return pl.pallas_call(
            functools.partial(tile_kernel, last, rows, half, feats),
            out_shape=out_shape,
            in_specs=[SMEM, SMEM] + [HBM] * 6 + [VMEM] * (len(args) - 6),
            out_specs=[VMEM] * len(out_shape),
            scratch_shapes=[
                pltpu.VMEM((4, 2, rows, feats), BF),
                pltpu.VMEM((2 * quarter, feats), BF),
                pltpu.VMEM((4 * step, feats), BF),
                pltpu.VMEM((4 * step, 2 * quarter), BF),
                pltpu.VMEM((4, 2, rows, feats), F32),
                pltpu.SemaphoreType.DMA((6,)),
            ],
            compiler_params=grant(40),
            cost_estimate=pl.CostEstimate(
                flops=3 * 2 * 4 * step * 2 * quarter * feats, bytes_accessed=12 * 4 * step * feats, transcendentals=8 * step * quarter
            ),
            name="tile_last" if last else "tile_first",
        )(info, scales, *args)

    def call(kernel, name, out_shape, *args, scale=False):
        return pl.pallas_call(
            kernel,
            out_shape=out_shape,
            in_specs=[SMEM] * scale + [VMEM] * (len(args) - scale),
            out_specs=[VMEM] * len(out_shape),
            compiler_params=grant(20),
            name=name,
        )(*args)

    def give(messages):
        return [swap(m, z_mask(j), y_mask(j)) for j, m in zip((1, 2, 3), messages)]

    info = jnp.stack([core, z_lo]).astype(jnp.int32)
    scales = jnp.stack([scaling, logit_offset_term[0]])
    own_a, *messages, acc, sums = tile(False, *texts_a, images_own, images_other)
    got_a = give(messages)
    own_b, *messages, img_own, img_other, sums = tile(True, *texts_b, images_own, images_other, acc, sums)
    *messages, img_other, sums, _ = lax.optimization_barrier((*messages, img_other, sums, got_a))
    got_b = give(messages)

    img_got = swap(img_other, CORE)
    sums = sums + swap(sums, y_mask(1))
    n2, n3 = call(
        functools.partial(text_first_kernel, rows, feats, False), "text_first_a", small(2, (rows + 8, feats), BF), after(own_a, sums), *got_a
    )
    sums = sums + swap(sums, y_mask(2))
    sums = after(sums, n2, n3)
    sums = sums + swap(sums, z_mask(2))
    img, *messages = call(
        functools.partial(image_first_kernel, rows, feats), "image_first",
        small(1, (rows, feats)) + small(3, (rows + 8, feats), BF), img_own, img_got, sums,
    )
    img_got = [swap(m, x_mask(k)) for k, m in zip((1, 2, 3), messages)]
    got2, got3 = swap(n2, y_mask(2), z_mask(2)), swap(n3, y_mask(3), z_mask(3))
    text, n1 = call(
        functools.partial(text_first_kernel, rows, feats, True), "text_first_b",
        small(1, (rows, feats)) + small(1, (rows + 8, feats), BF), after(own_b, *messages), *got_b,
    )
    got1 = swap(after(n1, got2, got3), y_mask(1), z_mask(1))

    (img,) = call(
        functools.partial(image_last_kernel, rows, feats), "image_last", small(1, (rows + 8, feats)),
        logit_scaler, img, sums, *img_got, scale=True,
    )
    keep, got = img[:, :half], swap(img[:, half:], z_mask(1))
    image = jnp.concatenate(by(lo0, keep[:rows], got[:rows]), axis=0)
    sums = keep[rows:] + got[rows:]
    (text,) = call(text_last_kernel, "text_last", small(1, (rows, feats)), logit_scaler, text, got1, got2, got3, scale=True)
    whole = jnp.concatenate([text[:, :half], text[:, half:], image, sums], axis=0)
    mine, other = by(on0, whole[:, :width], whole[:, width:])
    other = swap(other, CORE)
    text_grad = jnp.concatenate(by(on0, mine[:step], other[:step]), axis=0)
    image_grad = jnp.concatenate(by(on0, mine[step : 2 * step], other[step : 2 * step]), axis=0)
    scalar_grads = mine[2 * step, :2] + other[2 * step, :2]
    return (image_grad, text_grad, scalar_grads)


def solution(mesh):
    placed = (P("batch", "dim"), P("batch", "dim"), P(), P())
    return jax.shard_map(
        body,
        mesh=mesh,
        in_specs=placed,
        out_specs=(P("batch", "dim"), P("batch", "dim"), P()),
        check_vma=False,
    )
```

time: 106 us -> 124 us (1.17)
  waiting for transfers between devices: 33.4 us -> 45.5 us
  starting transfers between devices: 39.9 us -> 44.8 us
  Pallas kernels: 22.5 us -> 23.9 us
    ppermute x28 -> x33, waiting for transfers between devices: 33.4 us -> 45.5 us  [swap(): lax.ppermute(array, AXES, [(i, i ^ (mask1 if i & 1 else mask0)) for i in...]
    ppermute x28 -> x33, starting transfers between devices: 39.9 us -> 44.8 us  [swap(): lax.ppermute(array, AXES, [(i, i ^ (mask1 if i & 1 else mask0)) for i in...]
    pallas_call x6 -> x7, Pallas kernels: 22.5 us -> 23.9 us  [the longest x2 17.3 us: tile(): pl.pallas_call(functools.partial(tile_kernel, last, rows, half, feats), o...]
    unnamed x9 -> x14, local copies, waits for them, and re-layouts: 2.82 us -> 3.06 us
  transfers between devices with their start and end apart: 28 -> 33, of which waited for: 16 -> 16; matrix products, arithmetic and copies ran while one was open for 1% -> 1% of each run, Pallas kernels for 21% -> 19%
where the time goes in v4:
time: 124 us
  waiting for transfers between devices  45.5 us (37%)
  starting transfers between devices  44.8 us (36%)
  Pallas kernels  23.9 us (19%)
  local copies, waits for them, and re-layouts  5.8 us (5%)
  between operations  2.22 us (2%)
  other arithmetic  2 us (2%)
    ppermute x33, waiting for transfers between devices, swap(): lax.ppermute(array, AXES, [(i, i ^ (mask1 if i & 1 else mask0)) for i in...  45.5 us
    ppermute x33, starting transfers between devices, swap(): lax.ppermute(array, AXES, [(i, i ^ (mask1 if i & 1 else mask0)) for i in...  44.8 us
    pallas_call x2, Pallas kernels, tile(): pl.pallas_call(functools.partial(tile_kernel, last, rows, half, feats), o...  17.3 us
    pallas_call x5, Pallas kernels, call(): pl.pallas_call(kernel, out_shape=out_shape, in_specs=[SMEM] * scale + [VM...  6.61 us
    unnamed x14, local copies, waits for them, and re-layouts  3.06 us
  transfers between devices with their start and end apart: 33, of which 16 were waited for; matrix products, arithmetic and copies ran while one was open for 1% of the time, Pallas kernels for 19%

profile of v4, /device:TPU:1, one launch (start us, length us, event | category | flops | bytes accessed | tf_op | source)
XLA Modules:
  0.0 124.2 jit_solution(3039808094677229459)
XLA Ops:
  0.6 1.1 fusion.7
  2.0 1.1 fusion.6
  3.5 1.5 %collective-permute-start = (bf16[352,288]{1,0:T(8,128)(2,1)S(1)}, bf16[352,288]{1,0:T(8,128)(2,1)S(1)}, u32[]{:S(2)}, u32[]{:S(2)}) collective-permute-start(bf16[352,288]{1,0:T(8,128)(2,1)S(1)} %broadcast_select_fusion.2), channel_id=1, source_target_pairs={{0,1},{1,0},{2,3},{3,2},{4,5},{5,4},{6,7},{7,6},{8,9},{9,8},{10,11... | collective-permute-start | bytes 608264 | tf_op jit(solution)/shard_map/ppermute | solution.py:31
  5.0 1.2 collective-permute-done
  6.7 3.8 %collective-permute-start.2 = (bf16[88,1152]{1,0:T(8,128)(2,1)S(1)}, bf16[88,1152]{1,0:T(8,128)(2,1)S(1)}, u32[]{:S(2)}, u32[]{:S(2)}) collective-permute-start(bf16[88,1152]{1,0:T(8,128)(2,1)S(1)} %pad_maximum_fusion.6), channel_id=1, source_target_pairs={{0,32},{1,65},{2,34},{3,67},{4,36},{5,69},{6,38},{7,71},{8,40},{9,... | collective-permute-start | bytes 608264 | tf_op jit(solution)/shard_map/ppermute | solution.py:31
  11.2 1.2 collective-permute-start.9
  12.3 1.5 %collective-permute-done.2 = bf16[88,1152]{1,0:T(8,128)(2,1)S(1)} collective-permute-done((bf16[88,1152]{1,0:T(8,128)(2,1)S(1)}, bf16[88,1152]{1,0:T(8,128)(2,1)S(1)}, u32[]{:S(2)}, u32[]{:S(2)}) %collective-permute-start.2) | collective-permute-done | bytes 202784 | tf_op jit(solution)/shard_map/ppermute | solution.py:31
  13.9 2.7 %collective-permute-done.3 = bf16[88,1152]{1,0:T(8,128)(2,1)S(1)} collective-permute-done((bf16[88,1152]{1,0:T(8,128)(2,1)S(1)}, bf16[88,1152]{1,0:T(8,128)(2,1)S(1)}, u32[]{:S(2)}, u32[]{:S(2)}) %collective-permute-start.3) | collective-permute-done | bytes 202784 | tf_op jit(solution)/shard_map/ppermute | solution.py:31
  16.6 2.5 %collective-permute-start.5 = (bf16[2,88,1152]{2,1,0:T(8,128)(2,1)S(1)}, bf16[2,88,1152]{2,1,0:T(8,128)(2,1)S(1)}, u32[]{:S(2)}, u32[]{:S(2)}) collective-permute-start(bf16[2,88,1152]{2,1,0:T(8,128)(2,1)S(1)} %pad_maximum_fusion.3.t0_ref), channel_id=1, source_target_pairs={{0,66},{1,49},{2,64},{3,51},{4,70},{5,53},{6,68},{7,55},{8,74},{9,... | collective-permute-start | bytes 1216520 | tf_op jit(solution)/shard_map/ppermute | solution.py:31
  19.2 2.6 %collective-permute-start.12 = (bf16[88,1152]{1,0:T(8,128)(2,1)S(1)}, bf16[88,1152]{1,0:T(8,128)(2,1)S(1)}, u32[]{:S(2)}, u32[]{:S(2)}) collective-permute-start(bf16[88,1152]{1,0:T(8,128)(2,1)S(1)} %pad_maximum_fusion.7), channel_id=1, source_target_pairs={{0,12},{1,13},{2,14},{3,15},{4,8},{5,9},{6,10},{7,11},{8,4},{9,5},... | collective-permute-start | bytes 608264 | tf_op jit(solution)/shard_map/ppermute | solution.py:31
  22.6 6.8 %collective-permute-done.10 = bf16[88,1152]{1,0:T(8,128)(2,1)S(1)} collective-permute-done((bf16[88,1152]{1,0:T(8,128)(2,1)S(1)}, bf16[88,1152]{1,0:T(8,128)(2,1)S(1)}, u32[]{:S(2)}, u32[]{:S(2)}) %collective-permute-start.10) | collective-permute-done | bytes 202784 | tf_op jit(solution)/shard_map/ppermute | solution.py:31
  29.4 0.6 collective-permute-done.12
  30.1 3.0 %collective-permute-start.13 = (bf16[352,1152]{1,0:T(8,128)(2,1)S(1)}, bf16[352,1152]{1,0:T(8,128)(2,1)S(1)}, u32[]{:S(2)}, u32[]{:S(2)}) collective-permute-start(bf16[352,1152]{1,0:T(8,128)(2,1)S(1)} %constant_dynamic-update-slice_fusion.im0_ref), channel_id=1, source_target_pairs={{0,1},{1,0},{2,3},{3,2},{4,5},{5,4},{6,7},{7,6},{8,9},{9,8},{10,11... | collective-permute-start | bytes 2433032 | tf_op jit(solution)/shard_map/ppermute | solution.py:31
  34.5 2.8 %collective-permute-start.14 = (bf16[2,88,1152]{2,1,0:T(8,128)(2,1)S(1)}, bf16[2,88,1152]{2,1,0:T(8,128)(2,1)S(1)}, u32[]{:S(2)}, u32[]{:S(2)}) collective-permute-start(bf16[2,88,1152]{2,1,0:T(8,128)(2,1)S(1)} %pad_maximum_fusion.3.t0_ref), channel_id=1, source_target_pairs={{0,64},{1,33},{2,66},{3,35},{4,68},{5,37},{6,70},{7,39},{8,72},{9,... | collective-permute-start | bytes 1216520 | tf_op jit(solution)/shard_map/ppermute | solution.py:31
  37.4 1.2 collective-permute-start.8
  38.7 1.1 collective-permute-start.7
  39.8 1.1 collective-permute-start.6
  40.8 2.3 %collective-permute-done.14.t2_ref = bf16[2,88,1152]{2,1,0:T(8,128)(2,1)S(1)} collective-permute-done((bf16[2,88,1152]{2,1,0:T(8,128)(2,1)S(1)}, bf16[2,88,1152]{2,1,0:T(8,128)(2,1)S(1)}, u32[]{:S(2)}, u32[]{:S(2)}) %collective-permute-start.14) | collective-permute-done | bytes 405536 | tf_op jit(solution)/shard_map/ppermute | solution.py:31
  43.1 8.6 %tile_first.1 = (f32[176,1152]{1,0:T(8,128)S(1)}, bf16[184,1152]{1,0:T(8,128)(2,1)S(1)}, bf16[184,1152]{1,0:T(8,128)(2,1)S(1)}, bf16[184,1152]{1,0:T(8,128)(2,1)...) custom-call(s32[2]{0:T(128)S(1)} %pad_add_fusion.info_ref, f32[2]{0:T(128)S(1)} %pad_maximum_fusion.9.scale_ref, ...), custom_call_target="tpu_custom_call" | custom-call | flops 3425697792 | bytes 9732096 | tf_op jit(solution)/shard_map/tile_first/pallas_call | solution.py:226
  51.7 1.7 %collective-permute-start.15 = (bf16[184,1152]{1,0:T(8,128)(2,1)S(1)}, bf16[184,1152]{1,0:T(8,128)(2,1)S(1)}, u32[]{:S(2)}, u32[]{:S(2)}) collective-permute-start(bf16[184,1152]{1,0:T(8,128)(2,1)S(1)} %get-tuple-element.48), channel_id=1, source_target_pairs={{0,2},{1,17},{2,0},{3,19},{4,6},{5,21},{6,4},{7,23},{8,10},{9,25},... | collective-permute-start | bytes 1271816 | tf_op jit(solution)/shard_map/ppermute | solution.py:31
  53.4 2.3 %collective-permute-start.16 = (bf16[184,1152]{1,0:T(8,128)(2,1)S(1)}, bf16[184,1152]{1,0:T(8,128)(2,1)S(1)}, u32[]{:S(2)}, u32[]{:S(2)}) collective-permute-start(bf16[184,1152]{1,0:T(8,128)(2,1)S(1)} %get-tuple-element.49), channel_id=1, source_target_pairs={{0,64},{1,33},{2,66},{3,35},{4,68},{5,37},{6,70},{7,39},{8,72},{9,... | collective-permute-start | bytes 1271816 | tf_op jit(solution)/shard_map/ppermute | solution.py:31
  55.9 8.7 %tile_last.1 = (f32[176,1152]{1,0:T(8,128)S(1)}, bf16[184,1152]{1,0:T(8,128)(2,1)S(1)}, bf16[184,1152]{1,0:T(8,128)(2,1)S(1)}, bf16[184,1152]{1,0:T(8,128)(2,1)S...) custom-call(s32[2]{0:T(128)S(1)} %pad_add_fusion.info_ref, ...), custom_call_target="tpu_custom_call" | custom-call | flops 3425697792 | bytes 9732096 | tf_op jit(solution)/shard_map/tile_last/pallas_call | solution.py:226
  64.6 1.5 %collective-permute-done.16.r2_ref = bf16[184,1152]{1,0:T(8,128)(2,1)S(1)} collective-permute-done((bf16[184,1152]{1,0:T(8,128)(2,1)S(1)}, bf16[184,1152]{1,0:T(8,128)(2,1)S(1)}, u32[]{:S(2)}, u32[]{:S(2)}) %collective-permute-start.16) | collective-permute-done | bytes 423968 | tf_op jit(solution)/shard_map/ppermute | solution.py:31
  66.1 2.6 %collective-permute-done.17.r3_ref = bf16[184,1152]{1,0:T(8,128)(2,1)S(1)} collective-permute-done((bf16[184,1152]{1,0:T(8,128)(2,1)S(1)}, bf16[184,1152]{1,0:T(8,128)(2,1)S(1)}, u32[]{:S(2)}, u32[]{:S(2)}) %collective-permute-start.17) | collective-permute-done | bytes 423968 | tf_op jit(solution)/shard_map/ppermute | solution.py:31
  68.7 2.7 %collective-permute-start.18 = (f32[352,1152]{1,0:T(8,128)S(1)}, f32[352,1152]{1,0:T(8,128)S(1)}, u32[]{:S(2)}, u32[]{:S(2)}) collective-permute-start(f32[352,1152]{1,0:T(8,128)S(1)} %get-tuple-element.51), channel_id=1, source_target_pairs={{0,1},{1,0},{2,3},{3,2},{4,5},{5,4},{6,7},{7,6},{8,9},{9,8},{10,11... | collective-permute-start | bytes 4866056 | tf_op jit(solution)/shard_map/ppermute | solution.py:31
  71.4 0.9 collective-permute-start.22
  72.3 1.2 collective-permute-start.23
  73.4 1.8 %collective-permute-start.24 = (bf16[184,1152]{1,0:T(8,128)(2,1)S(1)}, bf16[184,1152]{1,0:T(8,128)(2,1)S(1)}, u32[]{:S(2)}, u32[]{:S(2)}) collective-permute-start(bf16[184,1152]{1,0:T(8,128)(2,1)S(1)} %get-tuple-element.64), channel_id=1, source_target_pairs={{0,66},{1,49},{2,64},{3,51},{4,70},{5,53},{6,68},{7,55},{8,74},{9,... | collective-permute-start | bytes 1271816 | tf_op jit(solution)/shard_map/ppermute | solution.py:31
  75.2 8.1 %collective-permute-done.19 = f32[8,128]{1,0:T(8,128)S(1)} collective-permute-done((f32[8,128]{1,0:T(8,128)S(1)}, f32[8,128]{1,0:T(8,128)S(1)}, u32[]{:S(2)}, u32[]{:S(2)}) %collective-permute-start.19) | collective-permute-done | bytes 4128 | tf_op jit(solution)/shard_map/ppermute | solution.py:31
  83.3 1.2 collective-permute-start.20
  84.5 2.2 %text_first_a.1 = (bf16[96,1152]{1,0:T(8,128)(2,1)S(1)}, bf16[96,1152]{1,0:T(8,128)(2,1)S(1)}) custom-call(f32[176,1152]{1,0:T(8,128)S(1)} %get-tuple-element.54.own_ref, bf16[184,1152]{1,0:T(8,128)(2,1)S(1)} %collective-permute-done.15.r1_ref, bf16[184,1152]{1,0:T(8,128)(2,1)S(1)} %collective-permute-done.16.r2_ref, ...), custom_call_target="tpu_custom_call" | custom-call | tf_op jit(solution)/shard_map/text_first_a/pallas_call | solution.py:247
  87.3 4.0 %collective-permute-done.21 = f32[8,128]{1,0:T(8,128)S(1)} collective-permute-done((f32[8,128]{1,0:T(8,128)S(1)}, f32[8,128]{1,0:T(8,128)S(1)}, u32[]{:S(2)}, u32[]{:S(2)}) %collective-permute-start.21) | collective-permute-done | bytes 4128 | tf_op jit(solution)/shard_map/ppermute | solution.py:31
  91.2 0.8 collective-permute-start.26
  92.1 1.0 image_first.1
  93.0 1.3 %collective-permute-start.28 = (bf16[96,1152]{1,0:T(8,128)(2,1)S(1)}, bf16[96,1152]{1,0:T(8,128)(2,1)S(1)}, u32[]{:S(2)}, u32[]{:S(2)}) collective-permute-start(bf16[96,1152]{1,0:T(8,128)(2,1)S(1)} %get-tuple-element.58), channel_id=1, source_target_pairs={{0,4},{1,5},{2,6},{3,7},{4,0},{5,1},{6,2},{7,3},{8,12},{9,13},{10,... | collective-permute-start | bytes 663560 | tf_op jit(solution)/shard_map/ppermute | solution.py:31
  94.3 2.5 %collective-permute-start.29 = (bf16[96,1152]{1,0:T(8,128)(2,1)S(1)}, bf16[96,1152]{1,0:T(8,128)(2,1)S(1)}, u32[]{:S(2)}, u32[]{:S(2)}) collective-permute-start(bf16[96,1152]{1,0:T(8,128)(2,1)S(1)} %get-tuple-element.59), channel_id=1, source_target_pairs={{0,8},{1,9},{2,10},{3,11},{4,12},{5,13},{6,14},{7,15},{8,0},{9,1},... | collective-permute-start | bytes 663560 | tf_op jit(solution)/shard_map/ppermute | solution.py:31
  97.0 2.2 %text_first_b.1 = (f32[88,1152]{1,0:T(8,128)S(1)}, bf16[96,1152]{1,0:T(8,128)(2,1)S(1)}) custom-call(f32[176,1152]{1,0:T(8,128)S(1)} %get-tuple-element.61.own_ref, bf16[184,1152]{1,0:T(8,128)(2,1)S(1)} %collective-permute-done.22.r1_ref, bf16[184,1152]{1,0:T(8,128)(2,1)S(1)} %collective-permute-done.23.r2_ref, ...), custom_call_target="tpu_custom_call" | custom-call | tf_op jit(solution)/shard_map/text_first_b/pallas_call | solution.py:247
  99.6 1.5 %collective-permute-start.27 = (bf16[96,1152]{1,0:T(8,128)(2,1)S(1)}, bf16[96,1152]{1,0:T(8,128)(2,1)S(1)}, u32[]{:S(2)}, u32[]{:S(2)}) collective-permute-start(bf16[96,1152]{1,0:T(8,128)(2,1)S(1)} %get-tuple-element.67), channel_id=1, source_target_pairs={{0,16},{1,3},{2,18},{3,1},{4,20},{5,7},{6,22},{7,5},{8,24},{9,11},... | collective-permute-start | bytes 663560 | tf_op jit(solution)/shard_map/ppermute | solution.py:31
  101.2 4.0 %collective-permute-done.29.r2_ref = bf16[96,1152]{1,0:T(8,128)(2,1)S(1)} collective-permute-done((bf16[96,1152]{1,0:T(8,128)(2,1)S(1)}, bf16[96,1152]{1,0:T(8,128)(2,1)S(1)}, u32[]{:S(2)}, u32[]{:S(2)}) %collective-permute-start.29) | collective-permute-done | bytes 221216 | tf_op jit(solution)/shard_map/ppermute | solution.py:31
  105.2 3.4 %collective-permute-done.30.r3_ref = bf16[96,1152]{1,0:T(8,128)(2,1)S(1)} collective-permute-done((bf16[96,1152]{1,0:T(8,128)(2,1)S(1)}, bf16[96,1152]{1,0:T(8,128)(2,1)S(1)}, u32[]{:S(2)}, u32[]{:S(2)}) %collective-permute-start.30) | collective-permute-done | bytes 221216 | tf_op jit(solution)/shard_map/ppermute | solution.py:31
  108.6 0.6 image_last.1
  109.3 2.7 %collective-permute-start.31 = (f32[96,576]{1,0:T(8,128)S(1)}, f32[96,576]{1,0:T(8,128)S(1)}, u32[]{:S(2)}, u32[]{:S(2)}) collective-permute-start(f32[96,576]{1,0:T(8,128)S(1)} %slice.104), channel_id=1, source_target_pairs={{0,2},{1,3},{2,0},{3,1},{4,6},{5,7},{6,4},{7,5},{8,10},{9,11},{10,... | collective-permute-start | bytes 663560 | tf_op jit(solution)/shard_map/ppermute | solution.py:31
  112.0 0.6 text_last.1
  112.8 4.6 %collective-permute-done.31 = f32[96,576]{1,0:T(8,128)S(1)} collective-permute-done((f32[96,576]{1,0:T(8,128)S(1)}, f32[96,576]{1,0:T(8,128)S(1)}, u32[]{:S(2)}, u32[]{:S(2)}) %collective-permute-start.31) | collective-permute-done | bytes 221216 | tf_op jit(solution)/shard_map/ppermute | solution.py:31
  117.9 1.6 %collective-permute-start.32 = (f32[360,288]{0,1:T(8,128)S(1)}, f32[360,288]{0,1:T(8,128)S(1)}, u32[]{:S(2)}, u32[]{:S(2)}) collective-permute-start(f32[360,288]{0,1:T(8,128)S(1)} %copy.17), channel_id=1, source_target_pairs={{0,1},{1,0},{2,3},{3,2},{4,5},{5,4},{6,7},{7,6},{8,9},{9,8},{10,11... | collective-permute-start | bytes 1244168 | tf_op jit(solution)/shard_map/ppermute | solution.py:31
  119.5 1.4 %collective-permute-done.32 = f32[360,288]{0,1:T(8,128)S(1)} collective-permute-done((f32[360,288]{0,1:T(8,128)S(1)}, f32[360,288]{0,1:T(8,128)S(1)}, u32[]{:S(2)}, u32[]{:S(2)}) %collective-permute-start.32) | collective-permute-done | bytes 414752 | tf_op jit(solution)/shard_map/ppermute | solution.py:31
  122.3 1.0 copy.21
  123.2 1.0 copy.22
  (67 shorter events, 6.6 us)
Async XLA Ops:
  3.5 2.7 %collective-permute-start = (bf16[352,288]{1,0:T(8,128)(2,1)S(1)}, bf16[352,288]{1,0:T(8,128)(2,1)S(1)}, u32[]{:S(2)}, u32[]{:S(2)}) collective-permute-start(bf16[352,288]{1,0:T(8,128)(2,1)S(1)} %broadcast_select_fusion.2), channel_id=1, source_target_pairs={{0,1},{1,0},{2,3},{3,2},{4,5},{5,4},{6,7},{7,6},{8,9},{9,8},{10,11... | collective-permute-start | bytes 608264 | tf_op jit(solution)/shard_map/ppermute | solution.py:31
  6.7 7.2 %collective-permute-start.2 = (bf16[88,1152]{1,0:T(8,128)(2,1)S(1)}, bf16[88,1152]{1,0:T(8,128)(2,1)S(1)}, u32[]{:S(2)}, u32[]{:S(2)}) collective-permute-start(bf16[88,1152]{1,0:T(8,128)(2,1)S(1)} %pad_maximum_fusion.6), channel_id=1, source_target_pairs={{0,32},{1,65},{2,34},{3,67},{4,36},{5,69},{6,38},{7,71},{8,40},{9,... | collective-permute-start | bytes 608264 | tf_op jit(solution)/shard_map/ppermute | solution.py:31
  10.4 6.1 %collective-permute-start.3 = (bf16[88,1152]{1,0:T(8,128)(2,1)S(1)}, bf16[88,1152]{1,0:T(8,128)(2,1)S(1)}, u32[]{:S(2)}, u32[]{:S(2)}) collective-permute-start(bf16[88,1152]{1,0:T(8,128)(2,1)S(1)} %pad_maximum_fusion.6), channel_id=1, source_target_pairs={{0,48},{1,67},{2,50},{3,65},{4,52},{5,71},{6,54},{7,69},{8,56},{9,... | collective-permute-start | bytes 608264 | tf_op jit(solution)/shard_map/ppermute | solution.py:31
  10.9 8.3 %collective-permute-start.1 = (bf16[88,1152]{1,0:T(8,128)(2,1)S(1)}, bf16[88,1152]{1,0:T(8,128)(2,1)S(1)}, u32[]{:S(2)}, u32[]{:S(2)}) collective-permute-start(bf16[88,1152]{1,0:T(8,128)(2,1)S(1)} %pad_maximum_fusion.6), channel_id=1, source_target_pairs={{0,16},{1,3},{2,18},{3,1},{4,20},{5,7},{6,22},{7,5},{8,24},{9,11},... | collective-permute-start | bytes 608264 | tf_op jit(solution)/shard_map/ppermute | solution.py:31
  11.2 7.9 %collective-permute-start.9 = (bf16[88,576]{1,0:T(8,128)(2,1)S(1)}, bf16[88,576]{1,0:T(8,128)(2,1)S(1)}, u32[]{:S(2)}, u32[]{:S(2)}) collective-permute-start(bf16[88,576]{1,0:T(8,128)(2,1)S(1)} %get-tuple-element.87), channel_id=1, source_target_pairs={{0,2},{1,3},{2,0},{3,1},{4,6},{5,7},{6,4},{7,5},{8,10},{9,11},{10,... | collective-permute-start | bytes 304136 | tf_op jit(solution)/shard_map/ppermute | solution.py:31
  16.6 12.8 %collective-permute-start.5 = (bf16[2,88,1152]{2,1,0:T(8,128)(2,1)S(1)}, bf16[2,88,1152]{2,1,0:T(8,128)(2,1)S(1)}, u32[]{:S(2)}, u32[]{:S(2)}) collective-permute-start(bf16[2,88,1152]{2,1,0:T(8,128)(2,1)S(1)} %pad_maximum_fusion.3.t0_ref), channel_id=1, source_target_pairs={{0,66},{1,49},{2,64},{3,51},{4,70},{5,53},{6,68},{7,55},{8,74},{9,... | collective-permute-start | bytes 1216520 | tf_op jit(solution)/shard_map/ppermute | solution.py:31
  19.1 10.3 %collective-permute-start.4 = (bf16[2,88,1152]{2,1,0:T(8,128)(2,1)S(1)}, bf16[2,88,1152]{2,1,0:T(8,128)(2,1)S(1)}, u32[]{:S(2)}, u32[]{:S(2)}) collective-permute-start(bf16[2,88,1152]{2,1,0:T(8,128)(2,1)S(1)} %pad_maximum_fusion.3.t0_ref), channel_id=1, source_target_pairs={{0,2},{1,17},{2,0},{3,19},{4,6},{5,21},{6,4},{7,23},{8,10},{9,25},... | collective-permute-start | bytes 1216520 | tf_op jit(solution)/shard_map/ppermute | solution.py:31
  19.2 10.8 %collective-permute-start.12 = (bf16[88,1152]{1,0:T(8,128)(2,1)S(1)}, bf16[88,1152]{1,0:T(8,128)(2,1)S(1)}, u32[]{:S(2)}, u32[]{:S(2)}) collective-permute-start(bf16[88,1152]{1,0:T(8,128)(2,1)S(1)} %pad_maximum_fusion.7), channel_id=1, source_target_pairs={{0,12},{1,13},{2,14},{3,15},{4,8},{5,9},{6,10},{7,11},{8,4},{9,5},... | collective-permute-start | bytes 608264 | tf_op jit(solution)/shard_map/ppermute | solution.py:31
  21.8 7.6 %collective-permute-start.11 = (bf16[88,1152]{1,0:T(8,128)(2,1)S(1)}, bf16[88,1152]{1,0:T(8,128)(2,1)S(1)}, u32[]{:S(2)}, u32[]{:S(2)}) collective-permute-start(bf16[88,1152]{1,0:T(8,128)(2,1)S(1)} %pad_maximum_fusion.7), channel_id=1, source_target_pairs={{0,8},{1,9},{2,10},{3,11},{4,12},{5,13},{6,14},{7,15},{8,0},{9,1},... | collective-permute-start | bytes 608264 | tf_op jit(solution)/shard_map/ppermute | solution.py:31
  22.3 7.0 %collective-permute-start.10 = (bf16[88,1152]{1,0:T(8,128)(2,1)S(1)}, bf16[88,1152]{1,0:T(8,128)(2,1)S(1)}, u32[]{:S(2)}, u32[]{:S(2)}) collective-permute-start(bf16[88,1152]{1,0:T(8,128)(2,1)S(1)} %pad_maximum_fusion.7), channel_id=1, source_target_pairs={{0,4},{1,5},{2,6},{3,7},{4,0},{5,1},{6,2},{7,3},{8,12},{9,13},{10,... | collective-permute-start | bytes 608264 | tf_op jit(solution)/shard_map/ppermute | solution.py:31
  30.1 13.0 %collective-permute-start.13 = (bf16[352,1152]{1,0:T(8,128)(2,1)S(1)}, bf16[352,1152]{1,0:T(8,128)(2,1)S(1)}, u32[]{:S(2)}, u32[]{:S(2)}) collective-permute-start(bf16[352,1152]{1,0:T(8,128)(2,1)S(1)} %constant_dynamic-update-slice_fusion.im0_ref), channel_id=1, source_target_pairs={{0,1},{1,0},{2,3},{3,2},{4,5},{5,4},{6,7},{7,6},{8,9},{9,8},{10,11... | collective-permute-start | bytes 2433032 | tf_op jit(solution)/shard_map/ppermute | solution.py:31
  34.5 8.6 %collective-permute-start.14 = (bf16[2,88,1152]{2,1,0:T(8,128)(2,1)S(1)}, bf16[2,88,1152]{2,1,0:T(8,128)(2,1)S(1)}, u32[]{:S(2)}, u32[]{:S(2)}) collective-permute-start(bf16[2,88,1152]{2,1,0:T(8,128)(2,1)S(1)} %pad_maximum_fusion.3.t0_ref), channel_id=1, source_target_pairs={{0,64},{1,33},{2,66},{3,35},{4,68},{5,37},{6,70},{7,39},{8,72},{9,... | collective-permute-start | bytes 1216520 | tf_op jit(solution)/shard_map/ppermute | solution.py:31
  37.4 18.3 %collective-permute-start.8 = (bf16[2,88,1152]{2,1,0:T(8,128)(2,1)S(1)}, bf16[2,88,1152]{2,1,0:T(8,128)(2,1)S(1)}, u32[]{:S(2)}, u32[]{:S(2)}) collective-permute-start(bf16[2,88,1152]{2,1,0:T(8,128)(2,1)S(1)} %pad_maximum_fusion.2.t0_ref), channel_id=1, source_target_pairs={{0,66},{1,49},{2,64},{3,51},{4,70},{5,53},{6,68},{7,55},{8,74},{9,... | collective-permute-start | bytes 1216520 | tf_op jit(solution)/shard_map/ppermute | solution.py:31
  38.7 17.2 %collective-permute-start.7 = (bf16[2,88,1152]{2,1,0:T(8,128)(2,1)S(1)}, bf16[2,88,1152]{2,1,0:T(8,128)(2,1)S(1)}, u32[]{:S(2)}, u32[]{:S(2)}) collective-permute-start(bf16[2,88,1152]{2,1,0:T(8,128)(2,1)S(1)} %pad_maximum_fusion.2.t0_ref), channel_id=1, source_target_pairs={{0,64},{1,33},{2,66},{3,35},{4,68},{5,37},{6,70},{7,39},{8,72},{9,... | collective-permute-start | bytes 1216520 | tf_op jit(solution)/shard_map/ppermute | solution.py:31
  39.8 16.2 %collective-permute-start.6 = (bf16[2,88,1152]{2,1,0:T(8,128)(2,1)S(1)}, bf16[2,88,1152]{2,1,0:T(8,128)(2,1)S(1)}, u32[]{:S(2)}, u32[]{:S(2)}) collective-permute-start(bf16[2,88,1152]{2,1,0:T(8,128)(2,1)S(1)} %pad_maximum_fusion.2.t0_ref), channel_id=1, source_target_pairs={{0,2},{1,17},{2,0},{3,19},{4,6},{5,21},{6,4},{7,23},{8,10},{9,25},... | collective-permute-start | bytes 1216520 | tf_op jit(solution)/shard_map/ppermute | solution.py:31
  51.7 12.9 %collective-permute-start.15 = (bf16[184,1152]{1,0:T(8,128)(2,1)S(1)}, bf16[184,1152]{1,0:T(8,128)(2,1)S(1)}, u32[]{:S(2)}, u32[]{:S(2)}) collective-permute-start(bf16[184,1152]{1,0:T(8,128)(2,1)S(1)} %get-tuple-element.48), channel_id=1, source_target_pairs={{0,2},{1,17},{2,0},{3,19},{4,6},{5,21},{6,4},{7,23},{8,10},{9,25},... | collective-permute-start | bytes 1271816 | tf_op jit(solution)/shard_map/ppermute | solution.py:31
  53.4 12.7 %collective-permute-start.16 = (bf16[184,1152]{1,0:T(8,128)(2,1)S(1)}, bf16[184,1152]{1,0:T(8,128)(2,1)S(1)}, u32[]{:S(2)}, u32[]{:S(2)}) collective-permute-start(bf16[184,1152]{1,0:T(8,128)(2,1)S(1)} %get-tuple-element.49), channel_id=1, source_target_pairs={{0,64},{1,33},{2,66},{3,35},{4,68},{5,37},{6,70},{7,39},{8,72},{9,... | collective-permute-start | bytes 1271816 | tf_op jit(solution)/shard_map/ppermute | solution.py:31
  55.7 13.0 %collective-permute-start.17 = (bf16[184,1152]{1,0:T(8,128)(2,1)S(1)}, bf16[184,1152]{1,0:T(8,128)(2,1)S(1)}, u32[]{:S(2)}, u32[]{:S(2)}) collective-permute-start(bf16[184,1152]{1,0:T(8,128)(2,1)S(1)} %get-tuple-element.50), channel_id=1, source_target_pairs={{0,66},{1,49},{2,64},{3,51},{4,70},{5,53},{6,68},{7,55},{8,74},{9,... | collective-permute-start | bytes 1271816 | tf_op jit(solution)/shard_map/ppermute | solution.py:31
  68.7 22.5 %collective-permute-start.18 = (f32[352,1152]{1,0:T(8,128)S(1)}, f32[352,1152]{1,0:T(8,128)S(1)}, u32[]{:S(2)}, u32[]{:S(2)}) collective-permute-start(f32[352,1152]{1,0:T(8,128)S(1)} %get-tuple-element.51), channel_id=1, source_target_pairs={{0,1},{1,0},{2,3},{3,2},{4,5},{5,4},{6,7},{7,6},{8,9},{9,8},{10,11... | collective-permute-start | bytes 4866056 | tf_op jit(solution)/shard_map/ppermute | solution.py:31
  71.4 21.6 %collective-permute-start.22 = (bf16[184,1152]{1,0:T(8,128)(2,1)S(1)}, bf16[184,1152]{1,0:T(8,128)(2,1)S(1)}, u32[]{:S(2)}, u32[]{:S(2)}) collective-permute-start(bf16[184,1152]{1,0:T(8,128)(2,1)S(1)} %get-tuple-element.62), channel_id=1, source_target_pairs={{0,2},{1,17},{2,0},{3,19},{4,6},{5,21},{6,4},{7,23},{8,10},{9,25},... | collective-permute-start | bytes 1271816 | tf_op jit(solution)/shard_map/ppermute | solution.py:31
  72.3 22.1 %collective-permute-start.23 = (bf16[184,1152]{1,0:T(8,128)(2,1)S(1)}, bf16[184,1152]{1,0:T(8,128)(2,1)S(1)}, u32[]{:S(2)}, u32[]{:S(2)}) collective-permute-start(bf16[184,1152]{1,0:T(8,128)(2,1)S(1)} %get-tuple-element.63), channel_id=1, source_target_pairs={{0,64},{1,33},{2,66},{3,35},{4,68},{5,37},{6,70},{7,39},{8,72},{9,... | collective-permute-start | bytes 1271816 | tf_op jit(solution)/shard_map/ppermute | solution.py:31
  73.4 23.4 %collective-permute-start.24 = (bf16[184,1152]{1,0:T(8,128)(2,1)S(1)}, bf16[184,1152]{1,0:T(8,128)(2,1)S(1)}, u32[]{:S(2)}, u32[]{:S(2)}) collective-permute-start(bf16[184,1152]{1,0:T(8,128)(2,1)S(1)} %get-tuple-element.64), channel_id=1, source_target_pairs={{0,66},{1,49},{2,64},{3,51},{4,70},{5,53},{6,68},{7,55},{8,74},{9,... | collective-permute-start | bytes 1271816 | tf_op jit(solution)/shard_map/ppermute | solution.py:31
  75.2 8.1 %collective-permute-start.19 = (f32[8,128]{1,0:T(8,128)S(1)}, f32[8,128]{1,0:T(8,128)S(1)}, u32[]{:S(2)}, u32[]{:S(2)}) collective-permute-start(f32[8,128]{1,0:T(8,128)S(1)} %get-tuple-element.52), channel_id=1, source_target_pairs={{0,16},{1,17},{2,18},{3,19},{4,20},{5,21},{6,22},{7,23},{8,24},{9,... | collective-permute-start | bytes 12296 | tf_op jit(solution)/shard_map/ppermute | solution.py:31
  83.3 4.0 %collective-permute-start.20 = (f32[8,128]{1,0:T(8,128)S(1)}, f32[8,128]{1,0:T(8,128)S(1)}, u32[]{:S(2)}, u32[]{:S(2)}) collective-permute-start(f32[8,128]{1,0:T(8,128)S(1)} %add.22), channel_id=1, source_target_pairs={{0,32},{1,33},{2,34},{3,35},{4,36},{5,37},{6,38},{7,39},{8,40},{9,... | collective-permute-start | bytes 12296 | tf_op jit(solution)/shard_map/ppermute | solution.py:31
  87.3 4.0 %collective-permute-start.21 = (f32[8,128]{1,0:T(8,128)S(1)}, f32[8,128]{1,0:T(8,128)S(1)}, u32[]{:S(2)}, u32[]{:S(2)}) collective-permute-start(f32[8,128]{1,0:T(8,128)S(1)} %add.23), channel_id=1, source_target_pairs={{0,64},{1,65},{2,66},{3,67},{4,68},{5,69},{6,70},{7,71},{8,72},{9,... | collective-permute-start | bytes 12296 | tf_op jit(solution)/shard_map/ppermute | solution.py:31
  91.2 8.0 %collective-permute-start.25 = (bf16[96,1152]{1,0:T(8,128)(2,1)S(1)}, bf16[96,1152]{1,0:T(8,128)(2,1)S(1)}, u32[]{:S(2)}, u32[]{:S(2)}) collective-permute-start(bf16[96,1152]{1,0:T(8,128)(2,1)S(1)} %get-tuple-element.55), channel_id=1, source_target_pairs={{0,32},{1,65},{2,34},{3,67},{4,36},{5,69},{6,38},{7,71},{8,40},{9,... | collective-permute-start | bytes 663560 | tf_op jit(solution)/shard_map/ppermute | solution.py:31
  91.2 8.4 %collective-permute-start.26 = (bf16[96,1152]{1,0:T(8,128)(2,1)S(1)}, bf16[96,1152]{1,0:T(8,128)(2,1)S(1)}, u32[]{:S(2)}, u32[]{:S(2)}) collective-permute-start(bf16[96,1152]{1,0:T(8,128)(2,1)S(1)} %get-tuple-element.56), channel_id=1, source_target_pairs={{0,48},{1,67},{2,50},{3,65},{4,52},{5,71},{6,54},{7,69},{8,56},{9,... | collective-permute-start | bytes 663560 | tf_op jit(solution)/shard_map/ppermute | solution.py:31
  93.0 8.1 %collective-permute-start.28 = (bf16[96,1152]{1,0:T(8,128)(2,1)S(1)}, bf16[96,1152]{1,0:T(8,128)(2,1)S(1)}, u32[]{:S(2)}, u32[]{:S(2)}) collective-permute-start(bf16[96,1152]{1,0:T(8,128)(2,1)S(1)} %get-tuple-element.58), channel_id=1, source_target_pairs={{0,4},{1,5},{2,6},{3,7},{4,0},{5,1},{6,2},{7,3},{8,12},{9,13},{10,... | collective-permute-start | bytes 663560 | tf_op jit(solution)/shard_map/ppermute | solution.py:31
  94.3 10.8 %collective-permute-start.29 = (bf16[96,1152]{1,0:T(8,128)(2,1)S(1)}, bf16[96,1152]{1,0:T(8,128)(2,1)S(1)}, u32[]{:S(2)}, u32[]{:S(2)}) collective-permute-start(bf16[96,1152]{1,0:T(8,128)(2,1)S(1)} %get-tuple-element.59), channel_id=1, source_target_pairs={{0,8},{1,9},{2,10},{3,11},{4,12},{5,13},{6,14},{7,15},{8,0},{9,1},... | collective-permute-start | bytes 663560 | tf_op jit(solution)/shard_map/ppermute | solution.py:31
  96.8 11.8 %collective-permute-start.30 = (bf16[96,1152]{1,0:T(8,128)(2,1)S(1)}, bf16[96,1152]{1,0:T(8,128)(2,1)S(1)}, u32[]{:S(2)}, u32[]{:S(2)}) collective-permute-start(bf16[96,1152]{1,0:T(8,128)(2,1)S(1)} %get-tuple-element.60), channel_id=1, source_target_pairs={{0,12},{1,13},{2,14},{3,15},{4,8},{5,9},{6,10},{7,11},{8,4},{9,5},... | collective-permute-start | bytes 663560 | tf_op jit(solution)/shard_map/ppermute | solution.py:31
  99.6 12.4 %collective-permute-start.27 = (bf16[96,1152]{1,0:T(8,128)(2,1)S(1)}, bf16[96,1152]{1,0:T(8,128)(2,1)S(1)}, u32[]{:S(2)}, u32[]{:S(2)}) collective-permute-start(bf16[96,1152]{1,0:T(8,128)(2,1)S(1)} %get-tuple-element.67), channel_id=1, source_target_pairs={{0,16},{1,3},{2,18},{3,1},{4,20},{5,7},{6,22},{7,5},{8,24},{9,11},... | collective-permute-start | bytes 663560 | tf_op jit(solution)/shard_map/ppermute | solution.py:31
  109.3 8.1 %collective-permute-start.31 = (f32[96,576]{1,0:T(8,128)S(1)}, f32[96,576]{1,0:T(8,128)S(1)}, u32[]{:S(2)}, u32[]{:S(2)}) collective-permute-start(f32[96,576]{1,0:T(8,128)S(1)} %slice.104), channel_id=1, source_target_pairs={{0,2},{1,3},{2,0},{3,1},{4,6},{5,7},{6,4},{7,5},{8,10},{9,11},{10,... | collective-permute-start | bytes 663560 | tf_op jit(solution)/shard_map/ppermute | solution.py:31
  117.9 3.0 %collective-permute-start.32 = (f32[360,288]{0,1:T(8,128)S(1)}, f32[360,288]{0,1:T(8,128)S(1)}, u32[]{:S(2)}, u32[]{:S(2)}) collective-permute-start(f32[360,288]{0,1:T(8,128)S(1)} %copy.17), channel_id=1, source_target_pairs={{0,1},{1,0},{2,3},{3,2},{4,5},{5,4},{6,7},{7,6},{8,9},{9,8},{10,11... | collective-permute-start | bytes 1244168 | tf_op jit(solution)/shard_map/ppermute | solution.py:31

commit v5 on v4

v5 whole, which is shorter than its diff:
```python
import functools

import jax
import jax.numpy as jnp
from jax import lax
from jax.experimental import pallas as pl
from jax.experimental.pallas import tpu as pltpu
from jax.sharding import PartitionSpec as P

BF = jnp.bfloat16
F32 = jnp.float32
AXES = ("batch", "dim")
CORE = 1


def x_mask(k):
    return k << 2


def y_mask(k):
    return k << 4


def z_mask(k):
    return ((k >> 1) << 6) | ((k & 1) << 1)


def swap(array, mask0, mask1=None):
    mask1 = mask0 if mask1 is None else mask1
    n = lax.axis_size("batch") * lax.axis_size("dim")
    return lax.ppermute(array, AXES, [(i, i ^ (mask1 if i & 1 else mask0)) for i in range(n)])


LOW = 2.0**-3.5


def encode(v, m):
    a = jnp.abs(v) * (127.0 * LOW / m) + LOW
    for _ in range(5):
        a = a * a
    return jnp.where(v < 0, -a, a)


def decode(code, m):
    c = code.astype(F32)
    a = jnp.exp(jnp.log(jnp.abs(c)) * (1.0 / 32.0)) * (1.0 / LOW) - 1.0
    v = a * (m * (1.0 / 127.0))
    return jnp.where(c < 0, -v, v)


def top_of(largest):
    return (largest * 1.01 + 1e-30).astype(BF).astype(F32)


def pairs(core_ref, rows, half, ta_ref, tb_ref, t_rel):
    on0, step = core_ref[0] == 0, 2 * rows
    for b in range(4):
        other = (ta_ref, tb_ref)[b >> 1]
        p0 = jnp.where(on0, ta_ref[b].astype(F32), other[2 * (b & 1)].astype(F32))
        p1 = jnp.where(on0, tb_ref[b].astype(F32), other[2 * (b & 1) + 1].astype(F32))
        top = jnp.concatenate([p0[:, :half], p1[:, :half]], axis=1)
        bottom = jnp.concatenate([p0[:, half:], p1[:, half:]], axis=1)
        t_rel[b * step : (b + 1) * step, :] = jnp.concatenate([top, bottom], axis=0).astype(BF)


def coefficients(near, rows, info_ref, scale_ref, t_rel, images, coeff_low):
    scaling, offset = scale_ref[0], scale_ref[1]
    step, columns = 2 * rows, images.shape[0]
    similar = lax.dot_general(t_rel[...], images[...], (((1,), (1,)), ((), ())), preferred_element_type=F32)
    temp, bias = jnp.zeros((1, columns), F32), jnp.zeros((1, columns), F32)
    for b in range(4):
        part = similar[b * step : (b + 1) * step]
        logits = scaling * part + offset
        if near and b == 0:
            row = lax.broadcasted_iota(jnp.int32, part.shape, 0)
            column = lax.broadcasted_iota(jnp.int32, part.shape, 1)
            matched = (row - rows * info_ref[1] == column) & (column < rows)
            sig = 1.0 / (1.0 + jnp.exp(jnp.where(matched, logits, -logits)))
            coeff = jnp.where(matched, -sig, sig)
        else:
            coeff = 1.0 / (1.0 + jnp.exp(-logits))
        coeff_low[b * step : (b + 1) * step, :] = coeff.astype(BF)
        temp = temp + jnp.sum(coeff * part, axis=0, keepdims=True)
        bias = bias + jnp.sum(coeff, axis=0, keepdims=True)
    even = lax.broadcasted_iota(jnp.int32, (8, 128), 1) % 2 == 0
    return jnp.where(even, jnp.sum(temp, axis=1, keepdims=True), jnp.sum(bias, axis=1, keepdims=True))


def text_parts(core_ref, rows, half, coeff_low, images, grads):
    on0, step = core_ref[0] == 0, 2 * rows
    part = jnp.dot(coeff_low[...], images[...], preferred_element_type=F32)
    for b in range(4):
        top, bottom = part[b * step : b * step + rows], part[b * step + rows : (b + 1) * step]
        for e, at in ((0, slice(0, half)), (1, slice(half, 2 * half))):
            place = jnp.where(on0, e, b >> 1), jnp.where(on0, b, 2 * (b & 1) + e)
            grads[place] = jnp.concatenate([top[:, at], bottom[:, at]], axis=1)


def image_parts(coeff_low, t_rel):
    return lax.dot_general(coeff_low[...], t_rel[...], (((0,), (0,)), ((), ())), preferred_element_type=F32)


def far_kernel(
    rows, half, feats, info_ref, scale_ref, ta_ref, tb_ref, im0_ref, im1_ref,
    ma_ref, mb_ref, acc_ref, sums_ref, images, t_rel, coeff_low, grads,
):
    quarter = 4 * rows
    images[0:quarter, :] = im0_ref[...]
    images[quarter : 2 * quarter, :] = im1_ref[...]
    pairs(info_ref, rows, half, ta_ref, tb_ref, t_rel)
    sums_ref[...] = coefficients(False, rows, info_ref, scale_ref, t_rel, images, coeff_low)
    text_parts(info_ref, rows, half, coeff_low, images, grads)
    for k, m_ref in ((0, ma_ref), (1, mb_ref)):
        m_ref[...] = message([grads[k, i] for i in range(4)], feats)
    acc_ref[...] = image_parts(coeff_low, t_rel)


def near_first_kernel(
    rows, half, feats, info_ref, scale_ref, ta_ref, tb_ref, im0_ref, im1_ref, sums_before,
    images, t_rel, coeff_low, sums_ref,
):
    quarter = 4 * rows
    images[0:quarter, :] = im0_ref[...]
    images[quarter : 2 * quarter, :] = im1_ref[...]
    pairs(info_ref, rows, half, ta_ref, tb_ref, t_rel)
    sums = coefficients(True, rows, info_ref, scale_ref, t_rel, images, coeff_low)
    sums_ref[...] = sums + sums_before[...]


def near_last_kernel(
    rows, half, feats, info_ref, images, t_rel, coeff_low, before_ref, own_ref, m_ref, img0_ref, *refs,
):
    others, grads = refs[:4], refs[4]
    quarter = 4 * rows
    text_parts(info_ref, rows, half, coeff_low, images, grads)
    own_ref[...] = jnp.concatenate([grads[0, i] for i in range(4)], axis=0)
    m_ref[...] = message([grads[1, i] for i in range(4)], feats)
    acc = image_parts(coeff_low, t_rel) + before_ref[...]
    img0_ref[...] = acc[0:quarter]
    for k, img_ref in enumerate(others):
        img_ref[...] = acc[quarter + k * rows : quarter + (k + 1) * rows]


def message(blocks, feats, extra=()):
    part = jnp.concatenate(blocks, axis=0)
    m = top_of(jnp.max(jnp.max(jnp.abs(part), axis=0, keepdims=True), axis=1, keepdims=True))
    tail = jnp.broadcast_to(m, (8 - len(extra), feats))
    return jnp.concatenate([encode(part, m), *extra, tail], axis=0).astype(BF)


def decoded(ref):
    whole = ref[...].astype(F32)
    n = whole.shape[0] - 8
    return decode(whole[:n], whole[n + 7 : n + 8]), whole[n:]


def split3(v):
    hi = v.astype(BF).astype(F32)
    mid = (v - hi).astype(BF).astype(F32)
    return [hi, mid, v - hi - mid]


def image_first_kernel(rows, feats, own_ref, *refs):
    others, (out_ref, *messages) = refs[:4], refs[4:]
    out_ref[...] = own_ref[0:rows] + others[0][...]
    for i, m_ref in enumerate(messages):
        m_ref[...] = message([own_ref[(i + 1) * rows : (i + 2) * rows] + others[i + 1][...]], feats)


def text_far_kernel(own_ref, r2_ref, out_ref):
    out_ref[...] = own_ref[...] + decoded(r2_ref)[0]


def text_first_kernel(rows, feats, own_ref, r1_ref, r3_ref, sums_ref, out_ref, *messages):
    total = own_ref[...] + decoded(r1_ref)[0] + decoded(r3_ref)[0]
    out_ref[...] = total[0:rows]
    scalars = [jnp.concatenate([v] * (feats // 128), axis=1) for v in split3(sums_ref[0:1, :])]
    for i, m_ref in enumerate(messages):
        m_ref[...] = message([total[(i + 1) * rows : (i + 2) * rows]], feats, scalars)


def image_last_kernel(scale_ref, own_ref, r1_ref, r2_ref, r3_ref, out_ref):
    total = own_ref[...]
    for r in (r1_ref, r2_ref, r3_ref):
        total = total + decoded(r)[0]
    out_ref[...] = total * scale_ref[0]


def text_last_kernel(rows, feats, scale_ref, own_ref, sums_ref, r1_ref, r2_ref, r3_ref, out_ref):
    total, tails = own_ref[...], []
    for r in (r1_ref, r2_ref, r3_ref):
        value, tail = decoded(r)
        total = total + value
        tails.append(tail[0:1, :128] + (tail[1:2, :128] + tail[2:3, :128]))
    sums = (sums_ref[0:1, :] + tails[0]) + (tails[1] + tails[2])
    sums = jnp.broadcast_to(jnp.concatenate([sums] * (feats // 128), axis=1), (8, feats))
    out_ref[...] = jnp.concatenate([total * scale_ref[0], sums], axis=0)


VMEM = pl.BlockSpec(memory_space=pltpu.VMEM)
SMEM = pl.BlockSpec(memory_space=pltpu.SMEM)


def grant(mib):
    return pltpu.CompilerParams(vmem_limit_bytes=mib * 1024 * 1024)


def after(array, *others):
    return lax.optimization_barrier((array, *others))[0]


def body(picture_embeds, caption_embeds, logit_scaler, logit_offset_term):
    height, width = picture_embeds.shape
    rows, half, feats = height // 4, 2 * width, 4 * width
    step, quarter = 2 * rows, 4 * rows
    index = lax.axis_index("batch") * lax.axis_size("dim") + lax.axis_index("dim")
    core, z_lo = index & 1, (index >> 1) & 1
    on0, lo0 = core == 0, z_lo == 0
    scaling = logit_scaler[0]

    def by(first_one, own, other):
        return [jnp.where(first_one, own, other), jnp.where(first_one, other, own)]

    both = [jnp.concatenate([t[:step], i[:step]]) for t, i in ((caption_embeds, picture_embeds),)]
    both.append(jnp.concatenate([caption_embeds[step:], picture_embeds[step:]]))
    keep, send = by(on0, *both)
    chip = jnp.concatenate(by(on0, keep, swap(send, CORE)), axis=1)
    packed = jnp.concatenate([chip[:rows], chip[rows:step]], axis=1)
    keep, send = by(lo0, chip[step : step + rows], chip[step + rows :])
    first = [packed] + [swap(packed, y_mask(i), z_mask(i)) for i in range(1, 4)]
    image = jnp.concatenate([keep, swap(send, z_mask(1))], axis=1)
    stack = jnp.stack(first)
    second = [stack] + [swap(stack, z_mask(j), y_mask(j)) for j in range(1, 4)]
    images_own = jnp.concatenate([image] + [swap(image, x_mask(k)) for k in range(1, 4)], axis=0)
    images_other = swap(images_own, CORE)

    def f32(*shape):
        return jax.ShapeDtypeStruct(shape, F32)

    def bf16(*shape):
        return jax.ShapeDtypeStruct(shape, BF)

    def call(kernel, name, out_shape, *args, scalars=0, scratch=(), mib=20, products=0):
        return pl.pallas_call(
            kernel,
            out_shape=out_shape,
            in_specs=[SMEM] * scalars + [VMEM] * (len(args) - scalars),
            out_specs=[VMEM] * len(out_shape),
            scratch_shapes=scratch,
            compiler_params=grant(mib),
            cost_estimate=pl.CostEstimate(
                flops=products * 2 * quarter * 2 * quarter * 2 * feats,
                bytes_accessed=sum(a.size * a.dtype.itemsize for a in (*args, *out_shape)),
                transcendentals=products * 4 * quarter * quarter,
            ),
            name=name,
        )(*args)

    sizes = (rows, half, feats)
    info = jnp.stack([core, z_lo]).astype(jnp.int32)
    scales = jnp.stack([scaling, logit_offset_term[0]])
    images_shape, coeff_shape = (2 * quarter, feats), (2 * quarter, 2 * quarter)
    grads = pltpu.VMEM((2, 4, rows, feats), F32)
    m2, m3, acc, sums = call(
        functools.partial(far_kernel, *sizes), "tile_far",
        [bf16(quarter + 8, feats), bf16(quarter + 8, feats), f32(*images_shape), f32(8, 128)],
        info, scales, second[2], second[3], images_own, images_other,
        scalars=2, mib=40, products=3,
        scratch=[pltpu.VMEM(images_shape, BF), pltpu.VMEM(images_shape, BF), pltpu.VMEM(coeff_shape, BF), grads],
    )
    images, t_rel, coeff_low, sums = call(
        functools.partial(near_first_kernel, *sizes), "tile_near_first",
        [bf16(*images_shape), bf16(*images_shape), bf16(*coeff_shape), f32(8, 128)],
        info, scales, second[0], second[1], images_own, images_other, sums,
        scalars=2, mib=30, products=1,
    )
    text, m1, img_own, *img_others = call(
        functools.partial(near_last_kernel, *sizes), "tile_near_last",
        [f32(quarter, feats), bf16(quarter + 8, feats), f32(quarter, feats)] + [f32(rows, feats)] * 4,
        info, images, t_rel, coeff_low, acc,
        scalars=1, mib=30, products=2, scratch=[grads],
    )

    one = sums + swap(sums, x_mask(1))
    got2 = swap(m2, z_mask(2), y_mask(2))
    m1, m3, img_others, one, got2 = lax.optimization_barrier((m1, m3, img_others, one, got2))
    got1, got3 = swap(m1, z_mask(1), y_mask(1)), swap(m3, z_mask(3), y_mask(3))
    img, *messages = call(
        functools.partial(image_first_kernel, rows, feats), "image_first",
        [f32(rows, feats)] + [bf16(rows + 8, feats)] * 3, img_own, *[swap(part, CORE) for part in img_others],
    )
    sums = one
    for mask in ((x_mask(3),), (z_mask(1), y_mask(1)), (z_mask(3), y_mask(3))):
        sums = sums + swap(sums, *mask)
    img_got = [swap(m, x_mask(k)) for k, m in zip((1, 2, 3), messages)]
    (far,) = call(text_far_kernel, "text_far", [f32(quarter, feats)], after(text, *messages), got2)
    text, *messages = call(
        functools.partial(text_first_kernel, rows, feats), "text_first",
        [f32(rows, feats)] + [bf16(rows + 8, feats)] * 3, far, got1, got3, sums,
    )
    got = [swap(m, y_mask(i), z_mask(i)) for i, m in zip((1, 2, 3), messages)]

    (img,) = call(image_last_kernel, "image_last", [f32(rows, feats)], logit_scaler, img, *img_got, scalars=1)
    image = jnp.concatenate(by(lo0, img[:, :half], swap(img[:, half:], z_mask(1))), axis=0)
    (text,) = call(
        functools.partial(text_last_kernel, rows, feats), "text_last", [f32(rows + 8, feats)],
        logit_scaler, after(text, image), sums, *got, scalars=1,
    )
    whole = jnp.concatenate([text[:rows, :half], text[:rows, half:], image, text[rows:, :half]], axis=0)
    mine, other = by(on0, whole[:, :width], whole[:, width:])
    other = swap(other, CORE)
    text_grad = jnp.concatenate(by(on0, mine[:step], other[:step]), axis=0)
    image_grad = jnp.concatenate(by(on0, mine[step : 2 * step], other[step : 2 * step]), axis=0)
    scalar_grads = mine[2 * step, :2] + other[2 * step, :2]
    return (image_grad, text_grad, scalar_grads)


def solution(mesh):
    placed = (P("batch", "dim"), P("batch", "dim"), P(), P())
    return jax.shard_map(
        body,
        mesh=mesh,
        in_specs=placed,
        out_specs=(P("batch", "dim"), P("batch", "dim"), P()),
        check_vma=False,
    )
```

time: 124 us -> 111 us (0.90)
  waiting for transfers between devices: 45.5 us -> 35 us
  starting transfers between devices: 44.8 us -> 42.9 us
  Pallas kernels: 23.9 us -> 22.4 us
    ppermute x33 -> x31, waiting for transfers between devices: 45.5 us -> 35 us  [swap(): lax.ppermute(array, AXES, [(i, i ^ (mask1 if i & 1 else mask0)) for i in...]
    ppermute x33 -> x31, starting transfers between devices: 44.8 us -> 42.9 us  [swap(): lax.ppermute(array, AXES, [(i, i ^ (mask1 if i & 1 else mask0)) for i in...]
    pallas_call x7 -> x8, Pallas kernels: 23.9 us -> 22.4 us  [call(): pl.pallas_call(kernel, out_shape=out_shape, in_specs=[SMEM] * scalars + [...]
    unnamed x14 -> x11, local copies, waits for them, and re-layouts: 3.06 us -> 2.99 us
  transfers between devices with their start and end apart: 33 -> 31, of which waited for: 16 -> 17; matrix products, arithmetic and copies ran while one was open for 1% -> 1% of each run, Pallas kernels for 19% -> 20%
where the time goes in v5:
time: 111 us; the launch traced here: 110 us
  starting transfers between devices  42.9 us (39%)
  waiting for transfers between devices  35 us (32%)
  Pallas kernels  22.4 us (20%)
  local copies, waits for them, and re-layouts  5.72 us (5%)
  between operations  2.19 us (2%)
  other arithmetic  2.11 us (2%)
    ppermute x31, starting transfers between devices, swap(): lax.ppermute(array, AXES, [(i, i ^ (mask1 if i & 1 else mask0)) for i in...  42.9 us
    ppermute x31, waiting for transfers between devices, swap(): lax.ppermute(array, AXES, [(i, i ^ (mask1 if i & 1 else mask0)) for i in...  35 us
    pallas_call x8, Pallas kernels, call(): pl.pallas_call(kernel, out_shape=out_shape, in_specs=[SMEM] * scalars + [...  22.4 us
    unnamed x11, local copies, waits for them, and re-layouts  2.99 us
  transfers between devices with their start and end apart: 31, of which 17 were waited for; matrix products, arithmetic and copies ran while one was open for 1% of the time, Pallas kernels for 20%

profile of v5, /device:TPU:1, one launch (start us, length us, event | category | flops | bytes accessed | tf_op | source)
XLA Modules:
  0.0 110.4 jit_solution(6465325830247569192)
XLA Ops:
  0.6 1.1 fusion.6
  2.0 1.1 fusion.5
  3.5 1.5 %collective-permute-start = (bf16[352,288]{1,0:T(8,128)(2,1)S(1)}, bf16[352,288]{1,0:T(8,128)(2,1)S(1)}, u32[]{:S(2)}, u32[]{:S(2)}) collective-permute-start(bf16[352,288]{1,0:T(8,128)(2,1)S(1)} %broadcast_select_fusion.2), channel_id=1, source_target_pairs={{0,1},{1,0},{2,3},{3,2},{4,5},{5,4},{6,7},{7,6},{8,9},{9,8},{10,11... | collective-permute-start | bytes 608264 | tf_op jit(solution)/shard_map/ppermute | solution.py:31
  5.0 1.2 %collective-permute-done = bf16[352,288]{1,0:T(8,128)(2,1)S(1)} collective-permute-done((bf16[352,288]{1,0:T(8,128)(2,1)S(1)}, bf16[352,288]{1,0:T(8,128)(2,1)S(1)}, u32[]{:S(2)}, u32[]{:S(2)}) %collective-permute-start) | collective-permute-done | bytes 202784 | tf_op jit(solution)/shard_map/ppermute | solution.py:31
  6.6 1.8 %collective-permute-start.5 = (bf16[88,576]{1,0:T(8,128)(2,1)S(1)}, bf16[88,576]{1,0:T(8,128)(2,1)S(1)}, u32[]{:S(2)}, u32[]{:S(2)}) collective-permute-start(bf16[88,576]{1,0:T(8,128)(2,1)S(1)} %get-tuple-element.85), channel_id=1, source_target_pairs={{0,2},{1,3},{2,0},{3,1},{4,6},{5,7},{6,4},{7,5},{8,10},{9,11},{10,... | collective-permute-start | bytes 304136 | tf_op jit(solution)/shard_map/ppermute | solution.py:31
  8.6 3.4 %collective-permute-start.2 = (bf16[88,1152]{1,0:T(8,128)(2,1)S(1)}, bf16[88,1152]{1,0:T(8,128)(2,1)S(1)}, u32[]{:S(2)}, u32[]{:S(2)}) collective-permute-start(bf16[88,1152]{1,0:T(8,128)(2,1)S(1)} %pad_maximum_fusion.6), channel_id=1, source_target_pairs={{0,32},{1,65},{2,34},{3,67},{4,36},{5,69},{6,38},{7,71},{8,40},{9,... | collective-permute-start | bytes 608264 | tf_op jit(solution)/shard_map/ppermute | solution.py:31
  12.5 2.6 %collective-permute-start.8 = (bf16[88,1152]{1,0:T(8,128)(2,1)S(1)}, bf16[88,1152]{1,0:T(8,128)(2,1)S(1)}, u32[]{:S(2)}, u32[]{:S(2)}) collective-permute-start(bf16[88,1152]{1,0:T(8,128)(2,1)S(1)} %pad_maximum_fusion.7), channel_id=1, source_target_pairs={{0,12},{1,13},{2,14},{3,15},{4,8},{5,9},{6,10},{7,11},{8,4},{9,5},... | collective-permute-start | bytes 608264 | tf_op jit(solution)/shard_map/ppermute | solution.py:31
  15.5 1.8 %collective-permute-done.2 = bf16[88,1152]{1,0:T(8,128)(2,1)S(1)} collective-permute-done((bf16[88,1152]{1,0:T(8,128)(2,1)S(1)}, bf16[88,1152]{1,0:T(8,128)(2,1)S(1)}, u32[]{:S(2)}, u32[]{:S(2)}) %collective-permute-start.2) | collective-permute-done | bytes 202784 | tf_op jit(solution)/shard_map/ppermute | solution.py:31
  17.3 1.2 %collective-permute-start.6 = (bf16[88,1152]{1,0:T(8,128)(2,1)S(1)}, bf16[88,1152]{1,0:T(8,128)(2,1)S(1)}, u32[]{:S(2)}, u32[]{:S(2)}) collective-permute-start(bf16[88,1152]{1,0:T(8,128)(2,1)S(1)} %pad_maximum_fusion.7), channel_id=1, source_target_pairs={{0,4},{1,5},{2,6},{3,7},{4,0},{5,1},{6,2},{7,3},{8,12},{9,13},{10,... | collective-permute-start | bytes 608264 | tf_op jit(solution)/shard_map/ppermute | solution.py:31
  18.5 1.0 collective-permute-done.3
  19.7 2.8 %collective-permute-start.11 = (bf16[4,88,1152]{2,1,0:T(8,128)(2,1)S(1)}, bf16[4,88,1152]{2,1,0:T(8,128)(2,1)S(1)}, u32[]{:S(2)}, u32[]{:S(2)}) collective-permute-start(bf16[4,88,1152]{2,1,0:T(8,128)(2,1)S(1)} %pad_maximum_fusion.ta_ref), channel_id=1, source_target_pairs={{0,66},{1,49},{2,64},{3,51},{4,70},{5,53},{6,68},{7,55},{8,74},{9,... | collective-permute-start | bytes 2433032 | tf_op jit(solution)/shard_map/ppermute | solution.py:31
  22.8 0.7 collective-permute-done.8
  23.6 0.8 collective-permute-done.6
  24.4 1.9 %collective-permute-start.9 = (bf16[352,1152]{1,0:T(8,128)(2,1)S(1)}, bf16[352,1152]{1,0:T(8,128)(2,1)S(1)}, u32[]{:S(2)}, u32[]{:S(2)}) collective-permute-start(bf16[352,1152]{1,0:T(8,128)(2,1)S(1)} %pad_maximum_fusion.1.im0_ref), channel_id=1, source_target_pairs={{0,1},{1,0},{2,3},{3,2},{4,5},{5,4},{6,7},{7,6},{8,9},{9,8},{10,11... | collective-permute-start | bytes 2433032 | tf_op jit(solution)/shard_map/ppermute | solution.py:31
  27.8 1.3 %collective-permute-start.4 = (bf16[4,88,1152]{2,1,0:T(8,128)(2,1)S(1)}, bf16[4,88,1152]{2,1,0:T(8,128)(2,1)S(1)}, u32[]{:S(2)}, u32[]{:S(2)}) collective-permute-start(bf16[4,88,1152]{2,1,0:T(8,128)(2,1)S(1)} %pad_maximum_fusion.ta_ref), channel_id=1, source_target_pairs={{0,2},{1,17},{2,0},{3,19},{4,6},{5,21},{6,4},{7,23},{8,10},{9,25},... | collective-permute-start | bytes 2433032 | tf_op jit(solution)/shard_map/ppermute | solution.py:31
  29.1 12.1 %collective-permute-done.11.tb_ref = bf16[4,88,1152]{2,1,0:T(8,128)(2,1)S(1)} collective-permute-done((bf16[4,88,1152]{2,1,0:T(8,128)(2,1)S(1)}, bf16[4,88,1152]{2,1,0:T(8,128)(2,1)S(1)}, u32[]{:S(2)}, u32[]{:S(2)}) %collective-permute-start.11) | collective-permute-done | bytes 811040 | tf_op jit(solution)/shard_map/ppermute | solution.py:31
  41.1 8.3 %tile_far.1 = (bf16[360,1152]{1,0:T(8,128)(2,1)S(1)}, bf16[360,1152]{1,0:T(8,128)(2,1)S(1)}, f32[704,1152]{1,0:T(8,128)S(1)}, f32[8,128]{1,0:T(8,128)S(1)}) custom-call(s32[2]{0:T(128)S(1)} %pad_add_fusion.info_ref, f32[2]{0:T(128)S(1)} %pad_maximum_fusion.9.scale_ref, bf16[4,88,1152]{2,1,0:T(8,128)(2,1)S(1)} %collective-permute-done.10.ta_ref, ...), custom_call_target="tpu_custom_call" | custom-call | flops 3425697792 | bytes 8151056 | tf_op jit(solution)/shard_map/tile_far/pallas_call | solution.py:244
  49.4 1.9 %collective-permute-start.13 = (bf16[360,1152]{1,0:T(8,128)(2,1)S(1)}, bf16[360,1152]{1,0:T(8,128)(2,1)S(1)}, u32[]{:S(2)}, u32[]{:S(2)}) collective-permute-start(bf16[360,1152]{1,0:T(8,128)(2,1)S(1)} %get-tuple-element.49), channel_id=1, source_target_pairs={{0,64},{1,33},{2,66},{3,35},{4,68},{5,37},{6,70},{7,39},{8,72},{9,... | collective-permute-start | bytes 2488328 | tf_op jit(solution)/shard_map/ppermute | solution.py:31
  51.4 3.0 %tile_near_first.1 = (bf16[704,1152]{1,0:T(8,128)(2,1)S(1)}, bf16[704,1152]{1,0:T(8,128)(2,1)S(1)}, bf16[704,704]{1,0:T(8,128)(2,1)S(1)}, f32[8,128]{1,0:T(8,128)S(1)}) custom-call(s32[2]{0:T(128)S(1)} %pad_add_fusion.info_ref, f32[2]{0:T(128)S(1)} %pad_maximum_fusion.9.scale_ref, bf16[4,88,1152]{2,1,0:T(8,128)(2,1)S(1)} %pad_maximum_fusion.ta_ref, ...), custom_call_target="tpu_custom_call" | custom-call | flops 1141899264 | bytes 7487504 | tf_op jit(solution)/shard_map/tile_near_first/pallas_call | solution.py:244
  54.3 0.9 collective-permute-start.12
  55.3 5.3 %tile_near_last.1 = (f32[352,1152]{1,0:T(8,128)S(1)}, bf16[360,1152]{1,0:T(8,128)(2,1)S(1)}, f32[352,1152]{1,0:T(8,128)S(1)}, f32[88,1152]{1,0:T(8,128)S(1)}, f3...) custom-call(s32[2]{0:T(128)S(1)} %pad_add_fusion.info_ref, ...), custom_call_target="tpu_custom_call" | custom-call | flops 2283798528 | bytes 13174792 | tf_op jit(solution)/shard_map/tile_near_last/pallas_call | solution.py:244
  60.6 2.3 %collective-permute-done.13.r2_ref = bf16[360,1152]{1,0:T(8,128)(2,1)S(1)} collective-permute-done((bf16[360,1152]{1,0:T(8,128)(2,1)S(1)}, bf16[360,1152]{1,0:T(8,128)(2,1)S(1)}, u32[]{:S(2)}, u32[]{:S(2)}) %collective-permute-start.13) | collective-permute-done | bytes 829472 | tf_op jit(solution)/shard_map/ppermute | solution.py:31
  62.8 2.2 %collective-permute-start.14 = (f32[88,1152]{1,0:T(8,128)S(1)}, f32[88,1152]{1,0:T(8,128)S(1)}, u32[]{:S(2)}, u32[]{:S(2)}) collective-permute-start(f32[88,1152]{1,0:T(8,128)S(1)} %get-tuple-element.50), channel_id=1, source_target_pairs={{0,1},{1,0},{2,3},{3,2},{4,5},{5,4},{6,7},{7,6},{8,9},{9,8},{10,11... | collective-permute-start | bytes 1216520 | tf_op jit(solution)/shard_map/ppermute | solution.py:31
  65.0 1.8 %collective-permute-start.19 = (bf16[360,1152]{1,0:T(8,128)(2,1)S(1)}, bf16[360,1152]{1,0:T(8,128)(2,1)S(1)}, u32[]{:S(2)}, u32[]{:S(2)}) collective-permute-start(bf16[360,1152]{1,0:T(8,128)(2,1)S(1)} %get-tuple-element.60), channel_id=1, source_target_pairs={{0,66},{1,49},{2,64},{3,51},{4,70},{5,53},{6,68},{7,55},{8,74},{9,... | collective-permute-start | bytes 2488328 | tf_op jit(solution)/shard_map/ppermute | solution.py:31
  66.8 1.1 %collective-permute-start.15 = (f32[88,1152]{1,0:T(8,128)S(1)}, f32[88,1152]{1,0:T(8,128)S(1)}, u32[]{:S(2)}, u32[]{:S(2)}) collective-permute-start(f32[88,1152]{1,0:T(8,128)S(1)} %get-tuple-element.51), channel_id=1, source_target_pairs={{0,1},{1,0},{2,3},{3,2},{4,5},{5,4},{6,7},{7,6},{8,9},{9,8},{10,11... | collective-permute-start | bytes 1216520 | tf_op jit(solution)/shard_map/ppermute | solution.py:31
  68.5 0.9 collective-permute-done.15.refs_1_
  70.5 0.9 image_first.1
  71.5 1.3 %collective-permute-start.26 = (bf16[96,1152]{1,0:T(8,128)(2,1)S(1)}, bf16[96,1152]{1,0:T(8,128)(2,1)S(1)}, u32[]{:S(2)}, u32[]{:S(2)}) collective-permute-start(bf16[96,1152]{1,0:T(8,128)(2,1)S(1)} %get-tuple-element.54), channel_id=1, source_target_pairs={{0,4},{1,5},{2,6},{3,7},{4,0},{5,1},{6,2},{7,3},{8,12},{9,13},{10,... | collective-permute-start | bytes 663560 | tf_op jit(solution)/shard_map/ppermute | solution.py:31
  72.7 1.8 %collective-permute-start.20 = (f32[8,128]{1,0:T(8,128)S(1)}, f32[8,128]{1,0:T(8,128)S(1)}, u32[]{:S(2)}, u32[]{:S(2)}) collective-permute-start(f32[8,128]{1,0:T(8,128)S(1)} %add.22), channel_id=1, source_target_pairs={{0,12},{1,13},{2,14},{3,15},{4,8},{5,9},{6,10},{7,11},{8,4},{9,5},... | collective-permute-start | bytes 12296 | tf_op jit(solution)/shard_map/ppermute | solution.py:31
  74.6 2.1 %collective-permute-done.20 = f32[8,128]{1,0:T(8,128)S(1)} collective-permute-done((f32[8,128]{1,0:T(8,128)S(1)}, f32[8,128]{1,0:T(8,128)S(1)}, u32[]{:S(2)}, u32[]{:S(2)}) %collective-permute-start.20) | collective-permute-done | bytes 4128 | tf_op jit(solution)/shard_map/ppermute | solution.py:31
  76.7 2.5 %collective-permute-done.21 = f32[8,128]{1,0:T(8,128)S(1)} collective-permute-done((f32[8,128]{1,0:T(8,128)S(1)}, f32[8,128]{1,0:T(8,128)S(1)}, u32[]{:S(2)}, u32[]{:S(2)}) %collective-permute-start.21) | collective-permute-done | bytes 4128 | tf_op jit(solution)/shard_map/ppermute | solution.py:31
  79.2 1.3 %collective-permute-start.22 = (f32[8,128]{1,0:T(8,128)S(1)}, f32[8,128]{1,0:T(8,128)S(1)}, u32[]{:S(2)}, u32[]{:S(2)}) collective-permute-start(f32[8,128]{1,0:T(8,128)S(1)} %add.24), channel_id=1, source_target_pairs={{0,66},{1,49},{2,64},{3,51},{4,70},{5,53},{6,68},{7,55},{8,74},{9,... | collective-permute-start | bytes 12296 | tf_op jit(solution)/shard_map/ppermute | solution.py:31
  80.5 2.3 %collective-permute-done.22 = f32[8,128]{1,0:T(8,128)S(1)} collective-permute-done((f32[8,128]{1,0:T(8,128)S(1)}, f32[8,128]{1,0:T(8,128)S(1)}, u32[]{:S(2)}, u32[]{:S(2)}) %collective-permute-start.22) | collective-permute-done | bytes 4128 | tf_op jit(solution)/shard_map/ppermute | solution.py:31
  82.8 1.5 %collective-permute-start.27 = (bf16[96,1152]{1,0:T(8,128)(2,1)S(1)}, bf16[96,1152]{1,0:T(8,128)(2,1)S(1)}, u32[]{:S(2)}, u32[]{:S(2)}) collective-permute-start(bf16[96,1152]{1,0:T(8,128)(2,1)S(1)} %get-tuple-element.55), channel_id=1, source_target_pairs={{0,8},{1,9},{2,10},{3,11},{4,12},{5,13},{6,14},{7,15},{8,0},{9,1},... | collective-permute-start | bytes 663560 | tf_op jit(solution)/shard_map/ppermute | solution.py:31
  85.0 0.8 text_far.1.own_ref
  85.8 3.0 %text_first.1 = (f32[88,1152]{1,0:T(8,128)S(1)}, bf16[96,1152]{1,0:T(8,128)(2,1)S(1)}, bf16[96,1152]{1,0:T(8,128)(2,1)S(1)}, bf16[96,1152]{1,0:T(8,128)(2,1)S(1)}) custom-call(f32[352,1152]{1,0:T(8,128)S(1)} %text_far.1.own_ref, bf16[360,1152]{1,0:T(8,128)(2,1)S(1)} %collective-permute-done.18.r1_ref, bf16[360,1152]{1,0:T(8,128)(2,1)S(1)} %collective-permute-done.19.r3_ref, ...), custom_call_target="tpu_custom_call" | custom-call | bytes 4354048 | tf_op jit(solution)/shard_map/text_first/pallas_call | solution.py:244
  88.7 0.8 collective-permute-start.23
  89.5 2.1 %collective-permute-start.24 = (bf16[96,1152]{1,0:T(8,128)(2,1)S(1)}, bf16[96,1152]{1,0:T(8,128)(2,1)S(1)}, u32[]{:S(2)}, u32[]{:S(2)}) collective-permute-start(bf16[96,1152]{1,0:T(8,128)(2,1)S(1)} %get-tuple-element.64), channel_id=1, source_target_pairs={{0,32},{1,65},{2,34},{3,67},{4,36},{5,69},{6,38},{7,71},{8,40},{9,... | collective-permute-start | bytes 663560 | tf_op jit(solution)/shard_map/ppermute | solution.py:31
  91.6 1.1 collective-permute-start.25
  92.7 1.8 %collective-permute-done.28.r3_ref = bf16[96,1152]{1,0:T(8,128)(2,1)S(1)} collective-permute-done((bf16[96,1152]{1,0:T(8,128)(2,1)S(1)}, bf16[96,1152]{1,0:T(8,128)(2,1)S(1)}, u32[]{:S(2)}, u32[]{:S(2)}) %collective-permute-start.28) | collective-permute-done | bytes 221216 | tf_op jit(solution)/shard_map/ppermute | solution.py:31
  94.5 0.6 image_last.1
  95.2 1.7 %collective-permute-start.29 = (f32[88,576]{1,0:T(8,128)S(1)}, f32[88,576]{1,0:T(8,128)S(1)}, u32[]{:S(2)}, u32[]{:S(2)}) collective-permute-start(f32[88,576]{1,0:T(8,128)S(1)} %slice.93), channel_id=1, source_target_pairs={{0,2},{1,3},{2,0},{3,1},{4,6},{5,7},{6,4},{7,5},{8,10},{9,11},{10,... | collective-permute-start | bytes 608264 | tf_op jit(solution)/shard_map/ppermute | solution.py:31
  97.4 2.6 %collective-permute-done.25.r3_ref = bf16[96,1152]{1,0:T(8,128)(2,1)S(1)} collective-permute-done((bf16[96,1152]{1,0:T(8,128)(2,1)S(1)}, bf16[96,1152]{1,0:T(8,128)(2,1)S(1)}, u32[]{:S(2)}, u32[]{:S(2)}) %collective-permute-start.25) | collective-permute-done | bytes 221216 | tf_op jit(solution)/shard_map/ppermute | solution.py:31
  100.0 0.6 text_last.1
  101.2 4.4 %collective-permute-start.30 = (f32[360,288]{0,1:T(8,128)S(1)}, f32[360,288]{0,1:T(8,128)S(1)}, u32[]{:S(2)}, u32[]{:S(2)}) collective-permute-start(f32[360,288]{0,1:T(8,128)S(1)} %copy.17), channel_id=1, source_target_pairs={{0,1},{1,0},{2,3},{3,2},{4,5},{5,4},{6,7},{7,6},{8,9},{9,8},{10,11... | collective-permute-start | bytes 1244168 | tf_op jit(solution)/shard_map/ppermute | solution.py:31
  105.7 1.4 %collective-permute-done.30 = f32[360,288]{0,1:T(8,128)S(1)} collective-permute-done((f32[360,288]{0,1:T(8,128)S(1)}, f32[360,288]{0,1:T(8,128)S(1)}, u32[]{:S(2)}, u32[]{:S(2)}) %collective-permute-start.30) | collective-permute-done | bytes 414752 | tf_op jit(solution)/shard_map/ppermute | solution.py:31
  108.4 1.0 copy.21
  109.4 1.0 copy.22
  (61 shorter events, 7.7 us)
Async XLA Ops:
  3.5 2.7 %collective-permute-start = (bf16[352,288]{1,0:T(8,128)(2,1)S(1)}, bf16[352,288]{1,0:T(8,128)(2,1)S(1)}, u32[]{:S(2)}, u32[]{:S(2)}) collective-permute-start(bf16[352,288]{1,0:T(8,128)(2,1)S(1)} %broadcast_select_fusion.2), channel_id=1, source_target_pairs={{0,1},{1,0},{2,3},{3,2},{4,5},{5,4},{6,7},{7,6},{8,9},{9,8},{10,11... | collective-permute-start | bytes 608264 | tf_op jit(solution)/shard_map/ppermute | solution.py:31
  6.6 5.8 %collective-permute-start.5 = (bf16[88,576]{1,0:T(8,128)(2,1)S(1)}, bf16[88,576]{1,0:T(8,128)(2,1)S(1)}, u32[]{:S(2)}, u32[]{:S(2)}) collective-permute-start(bf16[88,576]{1,0:T(8,128)(2,1)S(1)} %get-tuple-element.85), channel_id=1, source_target_pairs={{0,2},{1,3},{2,0},{3,1},{4,6},{5,7},{6,4},{7,5},{8,10},{9,11},{10,... | collective-permute-start | bytes 304136 | tf_op jit(solution)/shard_map/ppermute | solution.py:31
  8.6 8.7 %collective-permute-start.2 = (bf16[88,1152]{1,0:T(8,128)(2,1)S(1)}, bf16[88,1152]{1,0:T(8,128)(2,1)S(1)}, u32[]{:S(2)}, u32[]{:S(2)}) collective-permute-start(bf16[88,1152]{1,0:T(8,128)(2,1)S(1)} %pad_maximum_fusion.6), channel_id=1, source_target_pairs={{0,32},{1,65},{2,34},{3,67},{4,36},{5,69},{6,38},{7,71},{8,40},{9,... | collective-permute-start | bytes 608264 | tf_op jit(solution)/shard_map/ppermute | solution.py:31
  12.0 6.6 %collective-permute-start.1 = (bf16[88,1152]{1,0:T(8,128)(2,1)S(1)}, bf16[88,1152]{1,0:T(8,128)(2,1)S(1)}, u32[]{:S(2)}, u32[]{:S(2)}) collective-permute-start(bf16[88,1152]{1,0:T(8,128)(2,1)S(1)} %pad_maximum_fusion.6), channel_id=1, source_target_pairs={{0,16},{1,3},{2,18},{3,1},{4,20},{5,7},{6,22},{7,5},{8,24},{9,11},... | collective-permute-start | bytes 608264 | tf_op jit(solution)/shard_map/ppermute | solution.py:31
  12.0 7.6 %collective-permute-start.3 = (bf16[88,1152]{1,0:T(8,128)(2,1)S(1)}, bf16[88,1152]{1,0:T(8,128)(2,1)S(1)}, u32[]{:S(2)}, u32[]{:S(2)}) collective-permute-start(bf16[88,1152]{1,0:T(8,128)(2,1)S(1)} %pad_maximum_fusion.6), channel_id=1, source_target_pairs={{0,48},{1,67},{2,50},{3,65},{4,52},{5,71},{6,54},{7,69},{8,56},{9,... | collective-permute-start | bytes 608264 | tf_op jit(solution)/shard_map/ppermute | solution.py:31
  12.5 11.1 %collective-permute-start.8 = (bf16[88,1152]{1,0:T(8,128)(2,1)S(1)}, bf16[88,1152]{1,0:T(8,128)(2,1)S(1)}, u32[]{:S(2)}, u32[]{:S(2)}) collective-permute-start(bf16[88,1152]{1,0:T(8,128)(2,1)S(1)} %pad_maximum_fusion.7), channel_id=1, source_target_pairs={{0,12},{1,13},{2,14},{3,15},{4,8},{5,9},{6,10},{7,11},{8,4},{9,5},... | collective-permute-start | bytes 608264 | tf_op jit(solution)/shard_map/ppermute | solution.py:31
  15.0 8.5 %collective-permute-start.7 = (bf16[88,1152]{1,0:T(8,128)(2,1)S(1)}, bf16[88,1152]{1,0:T(8,128)(2,1)S(1)}, u32[]{:S(2)}, u32[]{:S(2)}) collective-permute-start(bf16[88,1152]{1,0:T(8,128)(2,1)S(1)} %pad_maximum_fusion.7), channel_id=1, source_target_pairs={{0,8},{1,9},{2,10},{3,11},{4,12},{5,13},{6,14},{7,15},{8,0},{9,1},... | collective-permute-start | bytes 608264 | tf_op jit(solution)/shard_map/ppermute | solution.py:31
  17.3 7.0 %collective-permute-start.6 = (bf16[88,1152]{1,0:T(8,128)(2,1)S(1)}, bf16[88,1152]{1,0:T(8,128)(2,1)S(1)}, u32[]{:S(2)}, u32[]{:S(2)}) collective-permute-start(bf16[88,1152]{1,0:T(8,128)(2,1)S(1)} %pad_maximum_fusion.7), channel_id=1, source_target_pairs={{0,4},{1,5},{2,6},{3,7},{4,0},{5,1},{6,2},{7,3},{8,12},{9,13},{10,... | collective-permute-start | bytes 608264 | tf_op jit(solution)/shard_map/ppermute | solution.py:31
  19.7 21.4 %collective-permute-start.11 = (bf16[4,88,1152]{2,1,0:T(8,128)(2,1)S(1)}, bf16[4,88,1152]{2,1,0:T(8,128)(2,1)S(1)}, u32[]{:S(2)}, u32[]{:S(2)}) collective-permute-start(bf16[4,88,1152]{2,1,0:T(8,128)(2,1)S(1)} %pad_maximum_fusion.ta_ref), channel_id=1, source_target_pairs={{0,66},{1,49},{2,64},{3,51},{4,70},{5,53},{6,68},{7,55},{8,74},{9,... | collective-permute-start | bytes 2433032 | tf_op jit(solution)/shard_map/ppermute | solution.py:31
  22.5 18.6 %collective-permute-start.10 = (bf16[4,88,1152]{2,1,0:T(8,128)(2,1)S(1)}, bf16[4,88,1152]{2,1,0:T(8,128)(2,1)S(1)}, u32[]{:S(2)}, u32[]{:S(2)}) collective-permute-start(bf16[4,88,1152]{2,1,0:T(8,128)(2,1)S(1)} %pad_maximum_fusion.ta_ref), channel_id=1, source_target_pairs={{0,64},{1,33},{2,66},{3,35},{4,68},{5,37},{6,70},{7,39},{8,72},{9,... | collective-permute-start | bytes 2433032 | tf_op jit(solution)/shard_map/ppermute | solution.py:31
  24.4 16.7 %collective-permute-start.9 = (bf16[352,1152]{1,0:T(8,128)(2,1)S(1)}, bf16[352,1152]{1,0:T(8,128)(2,1)S(1)}, u32[]{:S(2)}, u32[]{:S(2)}) collective-permute-start(bf16[352,1152]{1,0:T(8,128)(2,1)S(1)} %pad_maximum_fusion.1.im0_ref), channel_id=1, source_target_pairs={{0,1},{1,0},{2,3},{3,2},{4,5},{5,4},{6,7},{7,6},{8,9},{9,8},{10,11... | collective-permute-start | bytes 2433032 | tf_op jit(solution)/shard_map/ppermute | solution.py:31
  27.8 23.6 %collective-permute-start.4 = (bf16[4,88,1152]{2,1,0:T(8,128)(2,1)S(1)}, bf16[4,88,1152]{2,1,0:T(8,128)(2,1)S(1)}, u32[]{:S(2)}, u32[]{:S(2)}) collective-permute-start(bf16[4,88,1152]{2,1,0:T(8,128)(2,1)S(1)} %pad_maximum_fusion.ta_ref), channel_id=1, source_target_pairs={{0,2},{1,17},{2,0},{3,19},{4,6},{5,21},{6,4},{7,23},{8,10},{9,25},... | collective-permute-start | bytes 2433032 | tf_op jit(solution)/shard_map/ppermute | solution.py:31
  49.4 13.4 %collective-permute-start.13 = (bf16[360,1152]{1,0:T(8,128)(2,1)S(1)}, bf16[360,1152]{1,0:T(8,128)(2,1)S(1)}, u32[]{:S(2)}, u32[]{:S(2)}) collective-permute-start(bf16[360,1152]{1,0:T(8,128)(2,1)S(1)} %get-tuple-element.49), channel_id=1, source_target_pairs={{0,64},{1,33},{2,66},{3,35},{4,68},{5,37},{6,70},{7,39},{8,72},{9,... | collective-permute-start | bytes 2488328 | tf_op jit(solution)/shard_map/ppermute | solution.py:31
  54.3 6.2 %collective-permute-start.12 = (f32[8,128]{1,0:T(8,128)S(1)}, f32[8,128]{1,0:T(8,128)S(1)}, u32[]{:S(2)}, u32[]{:S(2)}) collective-permute-start(f32[8,128]{1,0:T(8,128)S(1)} %get-tuple-element.48), channel_id=1, source_target_pairs={{0,4},{1,5},{2,6},{3,7},{4,0},{5,1},{6,2},{7,3},{8,12},{9,13},{10,... | collective-permute-start | bytes 12296 | tf_op jit(solution)/shard_map/ppermute | solution.py:31
  62.8 5.2 %collective-permute-start.14 = (f32[88,1152]{1,0:T(8,128)S(1)}, f32[88,1152]{1,0:T(8,128)S(1)}, u32[]{:S(2)}, u32[]{:S(2)}) collective-permute-start(f32[88,1152]{1,0:T(8,128)S(1)} %get-tuple-element.50), channel_id=1, source_target_pairs={{0,1},{1,0},{2,3},{3,2},{4,5},{5,4},{6,7},{7,6},{8,9},{9,8},{10,11... | collective-permute-start | bytes 1216520 | tf_op jit(solution)/shard_map/ppermute | solution.py:31
  65.0 20.7 %collective-permute-start.18 = (bf16[360,1152]{1,0:T(8,128)(2,1)S(1)}, bf16[360,1152]{1,0:T(8,128)(2,1)S(1)}, u32[]{:S(2)}, u32[]{:S(2)}) collective-permute-start(bf16[360,1152]{1,0:T(8,128)(2,1)S(1)} %get-tuple-element.59), channel_id=1, source_target_pairs={{0,2},{1,17},{2,0},{3,19},{4,6},{5,21},{6,4},{7,23},{8,10},{9,25},... | collective-permute-start | bytes 2488328 | tf_op jit(solution)/shard_map/ppermute | solution.py:31
  65.0 20.7 %collective-permute-start.19 = (bf16[360,1152]{1,0:T(8,128)(2,1)S(1)}, bf16[360,1152]{1,0:T(8,128)(2,1)S(1)}, u32[]{:S(2)}, u32[]{:S(2)}) collective-permute-start(bf16[360,1152]{1,0:T(8,128)(2,1)S(1)} %get-tuple-element.60), channel_id=1, source_target_pairs={{0,66},{1,49},{2,64},{3,51},{4,70},{5,53},{6,68},{7,55},{8,74},{9,... | collective-permute-start | bytes 2488328 | tf_op jit(solution)/shard_map/ppermute | solution.py:31
  66.8 2.5 %collective-permute-start.15 = (f32[88,1152]{1,0:T(8,128)S(1)}, f32[88,1152]{1,0:T(8,128)S(1)}, u32[]{:S(2)}, u32[]{:S(2)}) collective-permute-start(f32[88,1152]{1,0:T(8,128)S(1)} %get-tuple-element.51), channel_id=1, source_target_pairs={{0,1},{1,0},{2,3},{3,2},{4,5},{5,4},{6,7},{7,6},{8,9},{9,8},{10,11... | collective-permute-start | bytes 1216520 | tf_op jit(solution)/shard_map/ppermute | solution.py:31
  68.0 1.9 %collective-permute-start.16 = (f32[88,1152]{1,0:T(8,128)S(1)}, f32[88,1152]{1,0:T(8,128)S(1)}, u32[]{:S(2)}, u32[]{:S(2)}) collective-permute-start(f32[88,1152]{1,0:T(8,128)S(1)} %get-tuple-element.52), channel_id=1, source_target_pairs={{0,1},{1,0},{2,3},{3,2},{4,5},{5,4},{6,7},{7,6},{8,9},{9,8},{10,11... | collective-permute-start | bytes 1216520 | tf_op jit(solution)/shard_map/ppermute | solution.py:31
  68.0 2.5 %collective-permute-start.17 = (f32[88,1152]{1,0:T(8,128)S(1)}, f32[88,1152]{1,0:T(8,128)S(1)}, u32[]{:S(2)}, u32[]{:S(2)}) collective-permute-start(f32[88,1152]{1,0:T(8,128)S(1)} %get-tuple-element.53), channel_id=1, source_target_pairs={{0,1},{1,0},{2,3},{3,2},{4,5},{5,4},{6,7},{7,6},{8,9},{9,8},{10,11... | collective-permute-start | bytes 1216520 | tf_op jit(solution)/shard_map/ppermute | solution.py:31
  71.5 20.2 %collective-permute-start.26 = (bf16[96,1152]{1,0:T(8,128)(2,1)S(1)}, bf16[96,1152]{1,0:T(8,128)(2,1)S(1)}, u32[]{:S(2)}, u32[]{:S(2)}) collective-permute-start(bf16[96,1152]{1,0:T(8,128)(2,1)S(1)} %get-tuple-element.54), channel_id=1, source_target_pairs={{0,4},{1,5},{2,6},{3,7},{4,0},{5,1},{6,2},{7,3},{8,12},{9,13},{10,... | collective-permute-start | bytes 663560 | tf_op jit(solution)/shard_map/ppermute | solution.py:31
  72.7 4.0 %collective-permute-start.20 = (f32[8,128]{1,0:T(8,128)S(1)}, f32[8,128]{1,0:T(8,128)S(1)}, u32[]{:S(2)}, u32[]{:S(2)}) collective-permute-start(f32[8,128]{1,0:T(8,128)S(1)} %add.22), channel_id=1, source_target_pairs={{0,12},{1,13},{2,14},{3,15},{4,8},{5,9},{6,10},{7,11},{8,4},{9,5},... | collective-permute-start | bytes 12296 | tf_op jit(solution)/shard_map/ppermute | solution.py:31
  76.7 2.5 %collective-permute-start.21 = (f32[8,128]{1,0:T(8,128)S(1)}, f32[8,128]{1,0:T(8,128)S(1)}, u32[]{:S(2)}, u32[]{:S(2)}) collective-permute-start(f32[8,128]{1,0:T(8,128)S(1)} %add.23), channel_id=1, source_target_pairs={{0,2},{1,17},{2,0},{3,19},{4,6},{5,21},{6,4},{7,23},{8,10},{9,25},... | collective-permute-start | bytes 12296 | tf_op jit(solution)/shard_map/ppermute | solution.py:31
  79.2 3.7 %collective-permute-start.22 = (f32[8,128]{1,0:T(8,128)S(1)}, f32[8,128]{1,0:T(8,128)S(1)}, u32[]{:S(2)}, u32[]{:S(2)}) collective-permute-start(f32[8,128]{1,0:T(8,128)S(1)} %add.24), channel_id=1, source_target_pairs={{0,66},{1,49},{2,64},{3,51},{4,70},{5,53},{6,68},{7,55},{8,74},{9,... | collective-permute-start | bytes 12296 | tf_op jit(solution)/shard_map/ppermute | solution.py:31
  82.8 9.8 %collective-permute-start.27 = (bf16[96,1152]{1,0:T(8,128)(2,1)S(1)}, bf16[96,1152]{1,0:T(8,128)(2,1)S(1)}, u32[]{:S(2)}, u32[]{:S(2)}) collective-permute-start(bf16[96,1152]{1,0:T(8,128)(2,1)S(1)} %get-tuple-element.55), channel_id=1, source_target_pairs={{0,8},{1,9},{2,10},{3,11},{4,12},{5,13},{6,14},{7,15},{8,0},{9,1},... | collective-permute-start | bytes 663560 | tf_op jit(solution)/shard_map/ppermute | solution.py:31
  84.4 10.1 %collective-permute-start.28 = (bf16[96,1152]{1,0:T(8,128)(2,1)S(1)}, bf16[96,1152]{1,0:T(8,128)(2,1)S(1)}, u32[]{:S(2)}, u32[]{:S(2)}) collective-permute-start(bf16[96,1152]{1,0:T(8,128)(2,1)S(1)} %get-tuple-element.56), channel_id=1, source_target_pairs={{0,12},{1,13},{2,14},{3,15},{4,8},{5,9},{6,10},{7,11},{8,4},{9,5},... | collective-permute-start | bytes 663560 | tf_op jit(solution)/shard_map/ppermute | solution.py:31
  88.7 8.2 %collective-permute-start.23 = (bf16[96,1152]{1,0:T(8,128)(2,1)S(1)}, bf16[96,1152]{1,0:T(8,128)(2,1)S(1)}, u32[]{:S(2)}, u32[]{:S(2)}) collective-permute-start(bf16[96,1152]{1,0:T(8,128)(2,1)S(1)} %get-tuple-element.63), channel_id=1, source_target_pairs={{0,16},{1,3},{2,18},{3,1},{4,20},{5,7},{6,22},{7,5},{8,24},{9,11},... | collective-permute-start | bytes 663560 | tf_op jit(solution)/shard_map/ppermute | solution.py:31
  89.5 7.8 %collective-permute-start.24 = (bf16[96,1152]{1,0:T(8,128)(2,1)S(1)}, bf16[96,1152]{1,0:T(8,128)(2,1)S(1)}, u32[]{:S(2)}, u32[]{:S(2)}) collective-permute-start(bf16[96,1152]{1,0:T(8,128)(2,1)S(1)} %get-tuple-element.64), channel_id=1, source_target_pairs={{0,32},{1,65},{2,34},{3,67},{4,36},{5,69},{6,38},{7,71},{8,40},{9,... | collective-permute-start | bytes 663560 | tf_op jit(solution)/shard_map/ppermute | solution.py:31
  91.6 8.3 %collective-permute-start.25 = (bf16[96,1152]{1,0:T(8,128)(2,1)S(1)}, bf16[96,1152]{1,0:T(8,128)(2,1)S(1)}, u32[]{:S(2)}, u32[]{:S(2)}) collective-permute-start(bf16[96,1152]{1,0:T(8,128)(2,1)S(1)} %get-tuple-element.65), channel_id=1, source_target_pairs={{0,48},{1,67},{2,50},{3,65},{4,52},{5,71},{6,54},{7,69},{8,56},{9,... | collective-permute-start | bytes 663560 | tf_op jit(solution)/shard_map/ppermute | solution.py:31
  95.2 5.5 %collective-permute-start.29 = (f32[88,576]{1,0:T(8,128)S(1)}, f32[88,576]{1,0:T(8,128)S(1)}, u32[]{:S(2)}, u32[]{:S(2)}) collective-permute-start(f32[88,576]{1,0:T(8,128)S(1)} %slice.93), channel_id=1, source_target_pairs={{0,2},{1,3},{2,0},{3,1},{4,6},{5,7},{6,4},{7,5},{8,10},{9,11},{10,... | collective-permute-start | bytes 608264 | tf_op jit(solution)/shard_map/ppermute | solution.py:31
  101.2 5.9 %collective-permute-start.30 = (f32[360,288]{0,1:T(8,128)S(1)}, f32[360,288]{0,1:T(8,128)S(1)}, u32[]{:S(2)}, u32[]{:S(2)}) collective-permute-start(f32[360,288]{0,1:T(8,128)S(1)} %copy.17), channel_id=1, source_target_pairs={{0,1},{1,0},{2,3},{3,2},{4,5},{5,4},{6,7},{7,6},{8,9},{9,8},{10,11... | collective-permute-start | bytes 1244168 | tf_op jit(solution)/shard_map/ppermute | solution.py:31

commit v6 on v5

--- a/solution.py
+++ b/solution.py
@@ -160,33 +160,15 @@
     return [hi, mid, v - hi - mid]
 
 
-def image_first_kernel(rows, feats, own_ref, *refs):
+def image_first_kernel(rows, feats, own_ref, sums_ref, *refs):
     others, (out_ref, *messages) = refs[:4], refs[4:]
     out_ref[...] = own_ref[0:rows] + others[0][...]
-    for i, m_ref in enumerate(messages):
-        m_ref[...] = message([own_ref[(i + 1) * rows : (i + 2) * rows] + others[i + 1][...]], feats)
-
-
-def text_far_kernel(own_ref, r2_ref, out_ref):
-    out_ref[...] = own_ref[...] + decoded(r2_ref)[0]
-
-
-def text_first_kernel(rows, feats, own_ref, r1_ref, r3_ref, sums_ref, out_ref, *messages):
-    total = own_ref[...] + decoded(r1_ref)[0] + decoded(r3_ref)[0]
-    out_ref[...] = total[0:rows]
     scalars = [jnp.concatenate([v] * (feats // 128), axis=1) for v in split3(sums_ref[0:1, :])]
     for i, m_ref in enumerate(messages):
-        m_ref[...] = message([total[(i + 1) * rows : (i + 2) * rows]], feats, scalars)
-
-
-def image_last_kernel(scale_ref, own_ref, r1_ref, r2_ref, r3_ref, out_ref):
-    total = own_ref[...]
-    for r in (r1_ref, r2_ref, r3_ref):
-        total = total + decoded(r)[0]
-    out_ref[...] = total * scale_ref[0]
-
-
-def text_last_kernel(rows, feats, scale_ref, own_ref, sums_ref, r1_ref, r2_ref, r3_ref, out_ref):
+        m_ref[...] = message([own_ref[(i + 1) * rows : (i + 2) * rows] + others[i + 1][...]], feats, scalars)
+
+
+def image_last_kernel(feats, scale_ref, own_ref, sums_ref, r1_ref, r2_ref, r3_ref, out_ref):
     total, tails = own_ref[...], []
     for r in (r1_ref, r2_ref, r3_ref):
         value, tail = decoded(r)
@@ -195,6 +177,24 @@
     sums = (sums_ref[0:1, :] + tails[0]) + (tails[1] + tails[2])
     sums = jnp.broadcast_to(jnp.concatenate([sums] * (feats // 128), axis=1), (8, feats))
     out_ref[...] = jnp.concatenate([total * scale_ref[0], sums], axis=0)
+
+
+def text_far_kernel(own_ref, r2_ref, out_ref):
+    out_ref[...] = own_ref[...] + decoded(r2_ref)[0]
+
+
+def text_first_kernel(rows, feats, own_ref, r1_ref, r3_ref, out_ref, *messages):
+    total = own_ref[...] + decoded(r1_ref)[0] + decoded(r3_ref)[0]
+    out_ref[...] = total[0:rows]
+    for i, m_ref in enumerate(messages):
+        m_ref[...] = message([total[(i + 1) * rows : (i + 2) * rows]], feats)
+
+
+def text_last_kernel(scale_ref, own_ref, r1_ref, r2_ref, r3_ref, out_ref):
+    total = own_ref[...]
+    for r in (r1_ref, r2_ref, r3_ref):
+        total = total + decoded(r)[0]
+    out_ref[...] = total * scale_ref[0]
 
 
 VMEM = pl.BlockSpec(memory_space=pltpu.VMEM)
@@ -281,38 +281,38 @@
         scalars=1, mib=30, products=2, scratch=[grads],
     )
 
-    one = sums + swap(sums, x_mask(1))
+    one = sums + swap(sums, y_mask(1))
     got2 = swap(m2, z_mask(2), y_mask(2))
     m1, m3, img_others, one, got2 = lax.optimization_barrier((m1, m3, img_others, one, got2))
     got1, got3 = swap(m1, z_mask(1), y_mask(1)), swap(m3, z_mask(3), y_mask(3))
+    sums = one + swap(one, y_mask(3))
     img, *messages = call(
         functools.partial(image_first_kernel, rows, feats), "image_first",
-        [f32(rows, feats)] + [bf16(rows + 8, feats)] * 3, img_own, *[swap(part, CORE) for part in img_others],
-    )
-    sums = one
-    for mask in ((x_mask(3),), (z_mask(1), y_mask(1)), (z_mask(3), y_mask(3))):
-        sums = sums + swap(sums, *mask)
+        [f32(rows, feats)] + [bf16(rows + 8, feats)] * 3, img_own, sums, *[swap(part, CORE) for part in img_others],
+    )
     img_got = [swap(m, x_mask(k)) for k, m in zip((1, 2, 3), messages)]
     (far,) = call(text_far_kernel, "text_far", [f32(quarter, feats)], after(text, *messages), got2)
     text, *messages = call(
         functools.partial(text_first_kernel, rows, feats), "text_first",
-        [f32(rows, feats)] + [bf16(rows + 8, feats)] * 3, far, got1, got3, sums,
+        [f32(rows, feats)] + [bf16(rows + 8, feats)] * 3, far, got1, got3,
     )
     got = [swap(m, y_mask(i), z_mask(i)) for i, m in zip((1, 2, 3), messages)]
 
-    (img,) = call(image_last_kernel, "image_last", [f32(rows, feats)], logit_scaler, img, *img_got, scalars=1)
-    image = jnp.concatenate(by(lo0, img[:, :half], swap(img[:, half:], z_mask(1))), axis=0)
-    (text,) = call(
-        functools.partial(text_last_kernel, rows, feats), "text_last", [f32(rows + 8, feats)],
-        logit_scaler, after(text, image), sums, *got, scalars=1,
-    )
-    whole = jnp.concatenate([text[:rows, :half], text[:rows, half:], image, text[rows:, :half]], axis=0)
+    img_got[0] = after(img_got[0], text)
+    (img,) = call(
+        functools.partial(image_last_kernel, feats), "image_last", [f32(rows + 8, feats)], logit_scaler, img, sums, *img_got, scalars=1
+    )
+    keep, back = img[:, :half], swap(img[:, half:], z_mask(1))
+    image = jnp.concatenate(by(lo0, keep[:rows], back[:rows]), axis=0)
+    sums = keep[rows:]
+    sums = (sums + back[rows:]) + (swap(sums, z_mask(2)) + swap(sums, z_mask(3)))
+    (text,) = call(text_last_kernel, "text_last", [f32(rows, feats)], logit_scaler, after(text, img, sums), *got, scalars=1)
+    whole = jnp.concatenate([text[:, :half], text[:, half:], image, sums], axis=0)
     mine, other = by(on0, whole[:, :width], whole[:, width:])
     other = swap(other, CORE)
     text_grad = jnp.concatenate(by(on0, mine[:step], other[:step]), axis=0)
     image_grad = jnp.concatenate(by(on0, mine[step : 2 * step], other[step : 2 * step]), axis=0)
-    scalar_grads = mine[2 * step, :2] + other[2 * step, :2]
-    return (image_grad, text_grad, scalar_grads)
+    return (image_grad, text_grad, mine[2 * step, :2] + other[2 * step, :2])
 
 
 def solution(mesh):

time: 111 us -> 124 us (1.12)
  waiting for transfers between devices: 35 us -> 48.1 us
    ppermute x31, waiting for transfers between devices: 35 us -> 48.1 us  [swap(): lax.ppermute(array, AXES, [(i, i ^ (mask1 if i & 1 else mask0)) for i in...]
  transfers between devices with their start and end apart: 31 -> 31, of which waited for: 17 -> 17; matrix products, arithmetic and copies ran while one was open for 1% -> 1% of each run, Pallas kernels for 20% -> 17%
where the time goes in v6:
time: 124 us
  waiting for transfers between devices  48.1 us (39%)
  starting transfers between devices  43.1 us (35%)
  Pallas kernels  22.5 us (18%)
  local copies, waits for them, and re-layouts  5.72 us (5%)
  between operations  2.19 us (2%)
  other arithmetic  2.11 us (2%)
    ppermute x31, waiting for transfers between devices, swap(): lax.ppermute(array, AXES, [(i, i ^ (mask1 if i & 1 else mask0)) for i in...  48.1 us
    ppermute x31, starting transfers between devices, swap(): lax.ppermute(array, AXES, [(i, i ^ (mask1 if i & 1 else mask0)) for i in...  43.1 us
    pallas_call x8, Pallas kernels, call(): pl.pallas_call(kernel, out_shape=out_shape, in_specs=[SMEM] * scalars + [...  22.5 us
    unnamed x11, local copies, waits for them, and re-layouts  2.99 us
  transfers between devices with their start and end apart: 31, of which 17 were waited for; matrix products, arithmetic and copies ran while one was open for 1% of the time, Pallas kernels for 17%

profile of v6, /device:TPU:1, one launch (start us, length us, event | category | flops | bytes accessed | tf_op | source)
XLA Modules:
  0.0 123.7 jit_solution(122845663963518543)
XLA Ops:
  0.6 1.1 fusion.7
  2.0 1.1 fusion.6
  3.5 1.5 %collective-permute-start = (bf16[352,288]{1,0:T(8,128)(2,1)S(1)}, bf16[352,288]{1,0:T(8,128)(2,1)S(1)}, u32[]{:S(2)}, u32[]{:S(2)}) collective-permute-start(bf16[352,288]{1,0:T(8,128)(2,1)S(1)} %broadcast_select_fusion.2), channel_id=1, source_target_pairs={{0,1},{1,0},{2,3},{3,2},{4,5},{5,4},{6,7},{7,6},{8,9},{9,8},{10,11... | collective-permute-start | bytes 608264 | tf_op jit(solution)/shard_map/ppermute | solution.py:31
  5.0 1.2 collective-permute-done
  6.6 1.8 %collective-permute-start.5 = (bf16[88,576]{1,0:T(8,128)(2,1)S(1)}, bf16[88,576]{1,0:T(8,128)(2,1)S(1)}, u32[]{:S(2)}, u32[]{:S(2)}) collective-permute-start(bf16[88,576]{1,0:T(8,128)(2,1)S(1)} %get-tuple-element.89), channel_id=1, source_target_pairs={{0,2},{1,3},{2,0},{3,1},{4,6},{5,7},{6,4},{7,5},{8,10},{9,11},{10,... | collective-permute-start | bytes 304136 | tf_op jit(solution)/shard_map/ppermute | solution.py:31
  8.6 3.4 %collective-permute-start.2 = (bf16[88,1152]{1,0:T(8,128)(2,1)S(1)}, bf16[88,1152]{1,0:T(8,128)(2,1)S(1)}, u32[]{:S(2)}, u32[]{:S(2)}) collective-permute-start(bf16[88,1152]{1,0:T(8,128)(2,1)S(1)} %pad_maximum_fusion.6), channel_id=1, source_target_pairs={{0,32},{1,65},{2,34},{3,67},{4,36},{5,69},{6,38},{7,71},{8,40},{9,... | collective-permute-start | bytes 608264 | tf_op jit(solution)/shard_map/ppermute | solution.py:31
  12.5 2.6 %collective-permute-start.8 = (bf16[88,1152]{1,0:T(8,128)(2,1)S(1)}, bf16[88,1152]{1,0:T(8,128)(2,1)S(1)}, u32[]{:S(2)}, u32[]{:S(2)}) collective-permute-start(bf16[88,1152]{1,0:T(8,128)(2,1)S(1)} %pad_maximum_fusion.7), channel_id=1, source_target_pairs={{0,12},{1,13},{2,14},{3,15},{4,8},{5,9},{6,10},{7,11},{8,4},{9,5},... | collective-permute-start | bytes 608264 | tf_op jit(solution)/shard_map/ppermute | solution.py:31
  15.5 1.8 %collective-permute-done.2 = bf16[88,1152]{1,0:T(8,128)(2,1)S(1)} collective-permute-done((bf16[88,1152]{1,0:T(8,128)(2,1)S(1)}, bf16[88,1152]{1,0:T(8,128)(2,1)S(1)}, u32[]{:S(2)}, u32[]{:S(2)}) %collective-permute-start.2) | collective-permute-done | bytes 202784 | tf_op jit(solution)/shard_map/ppermute | solution.py:31
  17.3 1.2 collective-permute-start.6
  18.5 1.0 collective-permute-done.3
  19.7 2.8 %collective-permute-start.11 = (bf16[4,88,1152]{2,1,0:T(8,128)(2,1)S(1)}, bf16[4,88,1152]{2,1,0:T(8,128)(2,1)S(1)}, u32[]{:S(2)}, u32[]{:S(2)}) collective-permute-start(bf16[4,88,1152]{2,1,0:T(8,128)(2,1)S(1)} %pad_maximum_fusion.ta_ref), channel_id=1, source_target_pairs={{0,66},{1,49},{2,64},{3,51},{4,70},{5,53},{6,68},{7,55},{8,74},{9,... | collective-permute-start | bytes 2433032 | tf_op jit(solution)/shard_map/ppermute | solution.py:31
  22.8 0.7 collective-permute-done.8
  23.6 0.8 collective-permute-done.6
  24.4 1.9 %collective-permute-start.9 = (bf16[352,1152]{1,0:T(8,128)(2,1)S(1)}, bf16[352,1152]{1,0:T(8,128)(2,1)S(1)}, u32[]{:S(2)}, u32[]{:S(2)}) collective-permute-start(bf16[352,1152]{1,0:T(8,128)(2,1)S(1)} %pad_maximum_fusion.1.im0_ref), channel_id=1, source_target_pairs={{0,1},{1,0},{2,3},{3,2},{4,5},{5,4},{6,7},{7,6},{8,9},{9,8},{10,11... | collective-permute-start | bytes 2433032 | tf_op jit(solution)/shard_map/ppermute | solution.py:31
  27.8 1.3 %collective-permute-start.4 = (bf16[4,88,1152]{2,1,0:T(8,128)(2,1)S(1)}, bf16[4,88,1152]{2,1,0:T(8,128)(2,1)S(1)}, u32[]{:S(2)}, u32[]{:S(2)}) collective-permute-start(bf16[4,88,1152]{2,1,0:T(8,128)(2,1)S(1)} %pad_maximum_fusion.ta_ref), channel_id=1, source_target_pairs={{0,2},{1,17},{2,0},{3,19},{4,6},{5,21},{6,4},{7,23},{8,10},{9,25},... | collective-permute-start | bytes 2433032 | tf_op jit(solution)/shard_map/ppermute | solution.py:31
  29.1 12.1 %collective-permute-done.11.tb_ref = bf16[4,88,1152]{2,1,0:T(8,128)(2,1)S(1)} collective-permute-done((bf16[4,88,1152]{2,1,0:T(8,128)(2,1)S(1)}, bf16[4,88,1152]{2,1,0:T(8,128)(2,1)S(1)}, u32[]{:S(2)}, u32[]{:S(2)}) %collective-permute-start.11) | collective-permute-done | bytes 811040 | tf_op jit(solution)/shard_map/ppermute | solution.py:31
  41.1 8.3 %tile_far.1 = (bf16[360,1152]{1,0:T(8,128)(2,1)S(1)}, bf16[360,1152]{1,0:T(8,128)(2,1)S(1)}, f32[704,1152]{1,0:T(8,128)S(1)}, f32[8,128]{1,0:T(8,128)S(1)}) custom-call(s32[2]{0:T(128)S(1)} %pad_add_fusion.info_ref, f32[2]{0:T(128)S(1)} %pad_maximum_fusion.9.scale_ref, bf16[4,88,1152]{2,1,0:T(8,128)(2,1)S(1)} %collective-permute-done.10.ta_ref, ...), custom_call_target="tpu_custom_call" | custom-call | flops 3425697792 | bytes 8151056 | tf_op jit(solution)/shard_map/tile_far/pallas_call | solution.py:244
  49.4 1.9 %collective-permute-start.13 = (bf16[360,1152]{1,0:T(8,128)(2,1)S(1)}, bf16[360,1152]{1,0:T(8,128)(2,1)S(1)}, u32[]{:S(2)}, u32[]{:S(2)}) collective-permute-start(bf16[360,1152]{1,0:T(8,128)(2,1)S(1)} %get-tuple-element.51), channel_id=1, source_target_pairs={{0,64},{1,33},{2,66},{3,35},{4,68},{5,37},{6,70},{7,39},{8,72},{9,... | collective-permute-start | bytes 2488328 | tf_op jit(solution)/shard_map/ppermute | solution.py:31
  51.4 3.0 %tile_near_first.1 = (bf16[704,1152]{1,0:T(8,128)(2,1)S(1)}, bf16[704,1152]{1,0:T(8,128)(2,1)S(1)}, bf16[704,704]{1,0:T(8,128)(2,1)S(1)}, f32[8,128]{1,0:T(8,128)S(1)}) custom-call(s32[2]{0:T(128)S(1)} %pad_add_fusion.info_ref, f32[2]{0:T(128)S(1)} %pad_maximum_fusion.9.scale_ref, bf16[4,88,1152]{2,1,0:T(8,128)(2,1)S(1)} %pad_maximum_fusion.ta_ref, ...), custom_call_target="tpu_custom_call" | custom-call | flops 1141899264 | bytes 7487504 | tf_op jit(solution)/shard_map/tile_near_first/pallas_call | solution.py:244
  54.3 1.3 %collective-permute-start.12 = (f32[8,128]{1,0:T(8,128)S(1)}, f32[8,128]{1,0:T(8,128)S(1)}, u32[]{:S(2)}, u32[]{:S(2)}) collective-permute-start(f32[8,128]{1,0:T(8,128)S(1)} %get-tuple-element.50), channel_id=1, source_target_pairs={{0,16},{1,17},{2,18},{3,19},{4,20},{5,21},{6,22},{7,23},{8,24},{9,... | collective-permute-start | bytes 12296 | tf_op jit(solution)/shard_map/ppermute | solution.py:31
  55.7 5.3 %tile_near_last.1 = (f32[352,1152]{1,0:T(8,128)S(1)}, bf16[360,1152]{1,0:T(8,128)(2,1)S(1)}, f32[352,1152]{1,0:T(8,128)S(1)}, f32[88,1152]{1,0:T(8,128)S(1)}, f3...) custom-call(s32[2]{0:T(128)S(1)} %pad_add_fusion.info_ref, ...), custom_call_target="tpu_custom_call" | custom-call | flops 2283798528 | bytes 13174792 | tf_op jit(solution)/shard_map/tile_near_last/pallas_call | solution.py:244
  60.9 2.0 %collective-permute-done.12 = f32[8,128]{1,0:T(8,128)S(1)} collective-permute-done((f32[8,128]{1,0:T(8,128)S(1)}, f32[8,128]{1,0:T(8,128)S(1)}, u32[]{:S(2)}, u32[]{:S(2)}) %collective-permute-start.12) | collective-permute-done | bytes 4128 | tf_op jit(solution)/shard_map/ppermute | solution.py:31
  62.9 2.1 %collective-permute-start.15 = (f32[88,1152]{1,0:T(8,128)S(1)}, f32[88,1152]{1,0:T(8,128)S(1)}, u32[]{:S(2)}, u32[]{:S(2)}) collective-permute-start(f32[88,1152]{1,0:T(8,128)S(1)} %get-tuple-element.53), channel_id=1, source_target_pairs={{0,1},{1,0},{2,3},{3,2},{4,5},{5,4},{6,7},{7,6},{8,9},{9,8},{10,11... | collective-permute-start | bytes 1216520 | tf_op jit(solution)/shard_map/ppermute | solution.py:31
  65.0 1.8 %collective-permute-start.20 = (bf16[360,1152]{1,0:T(8,128)(2,1)S(1)}, bf16[360,1152]{1,0:T(8,128)(2,1)S(1)}, u32[]{:S(2)}, u32[]{:S(2)}) collective-permute-start(bf16[360,1152]{1,0:T(8,128)(2,1)S(1)} %get-tuple-element.63), channel_id=1, source_target_pairs={{0,66},{1,49},{2,64},{3,51},{4,70},{5,53},{6,68},{7,55},{8,74},{9,... | collective-permute-start | bytes 2488328 | tf_op jit(solution)/shard_map/ppermute | solution.py:31
  66.8 0.9 collective-permute-start.14
  67.7 1.9 %collective-permute-start.16 = (f32[88,1152]{1,0:T(8,128)S(1)}, f32[88,1152]{1,0:T(8,128)S(1)}, u32[]{:S(2)}, u32[]{:S(2)}) collective-permute-start(f32[88,1152]{1,0:T(8,128)S(1)} %get-tuple-element.54), channel_id=1, source_target_pairs={{0,1},{1,0},{2,3},{3,2},{4,5},{5,4},{6,7},{7,6},{8,9},{9,8},{10,11... | collective-permute-start | bytes 1216520 | tf_op jit(solution)/shard_map/ppermute | solution.py:31
  69.6 8.4 %collective-permute-done.14 = f32[8,128]{1,0:T(8,128)S(1)} collective-permute-done((f32[8,128]{1,0:T(8,128)S(1)}, f32[8,128]{1,0:T(8,128)S(1)}, u32[]{:S(2)}, u32[]{:S(2)}) %collective-permute-start.14) | collective-permute-done | bytes 4128 | tf_op jit(solution)/shard_map/ppermute | solution.py:31
  78.5 1.2 collective-permute-done.17.refs_2_
  79.7 0.6 collective-permute-done.18.refs_3_
  80.3 0.9 image_first.1
  81.2 1.3 %collective-permute-start.21 = (bf16[96,1152]{1,0:T(8,128)(2,1)S(1)}, bf16[96,1152]{1,0:T(8,128)(2,1)S(1)}, u32[]{:S(2)}, u32[]{:S(2)}) collective-permute-start(bf16[96,1152]{1,0:T(8,128)(2,1)S(1)} %get-tuple-element.57), channel_id=1, source_target_pairs={{0,4},{1,5},{2,6},{3,7},{4,0},{5,1},{6,2},{7,3},{8,12},{9,13},{10,... | collective-permute-start | bytes 663560 | tf_op jit(solution)/shard_map/ppermute | solution.py:31
  82.5 2.4 %collective-permute-start.22 = (bf16[96,1152]{1,0:T(8,128)(2,1)S(1)}, bf16[96,1152]{1,0:T(8,128)(2,1)S(1)}, u32[]{:S(2)}, u32[]{:S(2)}) collective-permute-start(bf16[96,1152]{1,0:T(8,128)(2,1)S(1)} %get-tuple-element.58), channel_id=1, source_target_pairs={{0,8},{1,9},{2,10},{3,11},{4,12},{5,13},{6,14},{7,15},{8,0},{9,1},... | collective-permute-start | bytes 663560 | tf_op jit(solution)/shard_map/ppermute | solution.py:31
  85.1 0.8 text_far.1.own_ref
  85.9 3.0 %text_first.1 = (f32[88,1152]{1,0:T(8,128)S(1)}, bf16[96,1152]{1,0:T(8,128)(2,1)S(1)}, bf16[96,1152]{1,0:T(8,128)(2,1)S(1)}, bf16[96,1152]{1,0:T(8,128)(2,1)S(1)}) custom-call(f32[352,1152]{1,0:T(8,128)S(1)} %text_far.1.own_ref, bf16[360,1152]{1,0:T(8,128)(2,1)S(1)} %collective-permute-done.19.r1_ref, bf16[360,1152]{1,0:T(8,128)(2,1)S(1)} %collective-permute-done.20.r3_ref), custom_call_target="tpu_custom_call" | custom-call | bytes 4349952 | tf_op jit(solution)/shard_map/text_first/pallas_call | solution.py:244
  88.9 6.2 %collective-permute-done.22.r2_ref = bf16[96,1152]{1,0:T(8,128)(2,1)S(1)} collective-permute-done((bf16[96,1152]{1,0:T(8,128)(2,1)S(1)}, bf16[96,1152]{1,0:T(8,128)(2,1)S(1)}, u32[]{:S(2)}, u32[]{:S(2)}) %collective-permute-start.22) | collective-permute-done | bytes 221216 | tf_op jit(solution)/shard_map/ppermute | solution.py:31
  95.1 2.0 %collective-permute-done.23.r3_ref = bf16[96,1152]{1,0:T(8,128)(2,1)S(1)} collective-permute-done((bf16[96,1152]{1,0:T(8,128)(2,1)S(1)}, bf16[96,1152]{1,0:T(8,128)(2,1)S(1)}, u32[]{:S(2)}, u32[]{:S(2)}) %collective-permute-start.23) | collective-permute-done | bytes 221216 | tf_op jit(solution)/shard_map/ppermute | solution.py:31
  97.1 0.6 image_last.1
  98.0 3.4 %collective-permute-start.25 = (f32[8,576]{1,0:T(8,128)S(1)}, f32[8,576]{1,0:T(8,128)S(1)}, u32[]{:S(2)}, u32[]{:S(2)}) collective-permute-start(f32[8,576]{1,0:T(8,128)S(1)} %slice.101), channel_id=1, source_target_pairs={{0,64},{1,65},{2,66},{3,67},{4,68},{5,69},{6,70},{7,71},{8,72},{9,... | collective-permute-start | bytes 55304 | tf_op jit(solution)/shard_map/ppermute | solution.py:31
  101.8 3.4 %collective-permute-start.28 = (bf16[96,1152]{1,0:T(8,128)(2,1)S(1)}, bf16[96,1152]{1,0:T(8,128)(2,1)S(1)}, u32[]{:S(2)}, u32[]{:S(2)}) collective-permute-start(bf16[96,1152]{1,0:T(8,128)(2,1)S(1)} %get-tuple-element.69), channel_id=1, source_target_pairs={{0,32},{1,65},{2,34},{3,67},{4,36},{5,69},{6,38},{7,71},{8,40},{9,... | collective-permute-start | bytes 663560 | tf_op jit(solution)/shard_map/ppermute | solution.py:31
  105.3 0.7 collective-permute-done.25
  106.4 2.4 %collective-permute-done.27.r1_ref = bf16[96,1152]{1,0:T(8,128)(2,1)S(1)} collective-permute-done((bf16[96,1152]{1,0:T(8,128)(2,1)S(1)}, bf16[96,1152]{1,0:T(8,128)(2,1)S(1)}, u32[]{:S(2)}, u32[]{:S(2)}) %collective-permute-start.27) | collective-permute-done | bytes 221216 | tf_op jit(solution)/shard_map/ppermute | solution.py:31
  108.8 4.4 %collective-permute-done.28.r2_ref = bf16[96,1152]{1,0:T(8,128)(2,1)S(1)} collective-permute-done((bf16[96,1152]{1,0:T(8,128)(2,1)S(1)}, bf16[96,1152]{1,0:T(8,128)(2,1)S(1)}, u32[]{:S(2)}, u32[]{:S(2)}) %collective-permute-start.28) | collective-permute-done | bytes 221216 | tf_op jit(solution)/shard_map/ppermute | solution.py:31
  113.1 1.3 %collective-permute-done.29.r3_ref = bf16[96,1152]{1,0:T(8,128)(2,1)S(1)} collective-permute-done((bf16[96,1152]{1,0:T(8,128)(2,1)S(1)}, bf16[96,1152]{1,0:T(8,128)(2,1)S(1)}, u32[]{:S(2)}, u32[]{:S(2)}) %collective-permute-start.29) | collective-permute-done | bytes 221216 | tf_op jit(solution)/shard_map/ppermute | solution.py:31
  114.4 0.6 text_last.1
  115.7 3.3 %collective-permute-start.30 = (f32[360,288]{0,1:T(8,128)S(1)}, f32[360,288]{0,1:T(8,128)S(1)}, u32[]{:S(2)}, u32[]{:S(2)}) collective-permute-start(f32[360,288]{0,1:T(8,128)S(1)} %copy.17), channel_id=1, source_target_pairs={{0,1},{1,0},{2,3},{3,2},{4,5},{5,4},{6,7},{7,6},{8,9},{9,8},{10,11... | collective-permute-start | bytes 1244168 | tf_op jit(solution)/shard_map/ppermute | solution.py:31
  119.0 1.4 %collective-permute-done.30 = f32[360,288]{0,1:T(8,128)S(1)} collective-permute-done((f32[360,288]{0,1:T(8,128)S(1)}, f32[360,288]{0,1:T(8,128)S(1)}, u32[]{:S(2)}, u32[]{:S(2)}) %collective-permute-start.30) | collective-permute-done | bytes 414752 | tf_op jit(solution)/shard_map/ppermute | solution.py:31
  121.7 1.0 copy.21
  122.7 1.0 copy.22
  (61 shorter events, 6.6 us)
Async XLA Ops:
  3.5 2.7 %collective-permute-start = (bf16[352,288]{1,0:T(8,128)(2,1)S(1)}, bf16[352,288]{1,0:T(8,128)(2,1)S(1)}, u32[]{:S(2)}, u32[]{:S(2)}) collective-permute-start(bf16[352,288]{1,0:T(8,128)(2,1)S(1)} %broadcast_select_fusion.2), channel_id=1, source_target_pairs={{0,1},{1,0},{2,3},{3,2},{4,5},{5,4},{6,7},{7,6},{8,9},{9,8},{10,11... | collective-permute-start | bytes 608264 | tf_op jit(solution)/shard_map/ppermute | solution.py:31
  6.6 5.8 %collective-permute-start.5 = (bf16[88,576]{1,0:T(8,128)(2,1)S(1)}, bf16[88,576]{1,0:T(8,128)(2,1)S(1)}, u32[]{:S(2)}, u32[]{:S(2)}) collective-permute-start(bf16[88,576]{1,0:T(8,128)(2,1)S(1)} %get-tuple-element.89), channel_id=1, source_target_pairs={{0,2},{1,3},{2,0},{3,1},{4,6},{5,7},{6,4},{7,5},{8,10},{9,11},{10,... | collective-permute-start | bytes 304136 | tf_op jit(solution)/shard_map/ppermute | solution.py:31
  8.6 8.7 %collective-permute-start.2 = (bf16[88,1152]{1,0:T(8,128)(2,1)S(1)}, bf16[88,1152]{1,0:T(8,128)(2,1)S(1)}, u32[]{:S(2)}, u32[]{:S(2)}) collective-permute-start(bf16[88,1152]{1,0:T(8,128)(2,1)S(1)} %pad_maximum_fusion.6), channel_id=1, source_target_pairs={{0,32},{1,65},{2,34},{3,67},{4,36},{5,69},{6,38},{7,71},{8,40},{9,... | collective-permute-start | bytes 608264 | tf_op jit(solution)/shard_map/ppermute | solution.py:31
  12.0 6.6 %collective-permute-start.1 = (bf16[88,1152]{1,0:T(8,128)(2,1)S(1)}, bf16[88,1152]{1,0:T(8,128)(2,1)S(1)}, u32[]{:S(2)}, u32[]{:S(2)}) collective-permute-start(bf16[88,1152]{1,0:T(8,128)(2,1)S(1)} %pad_maximum_fusion.6), channel_id=1, source_target_pairs={{0,16},{1,3},{2,18},{3,1},{4,20},{5,7},{6,22},{7,5},{8,24},{9,11},... | collective-permute-start | bytes 608264 | tf_op jit(solution)/shard_map/ppermute | solution.py:31
  12.0 7.6 %collective-permute-start.3 = (bf16[88,1152]{1,0:T(8,128)(2,1)S(1)}, bf16[88,1152]{1,0:T(8,128)(2,1)S(1)}, u32[]{:S(2)}, u32[]{:S(2)}) collective-permute-start(bf16[88,1152]{1,0:T(8,128)(2,1)S(1)} %pad_maximum_fusion.6), channel_id=1, source_target_pairs={{0,48},{1,67},{2,50},{3,65},{4,52},{5,71},{6,54},{7,69},{8,56},{9,... | collective-permute-start | bytes 608264 | tf_op jit(solution)/shard_map/ppermute | solution.py:31
  12.5 11.1 %collective-permute-start.8 = (bf16[88,1152]{1,0:T(8,128)(2,1)S(1)}, bf16[88,1152]{1,0:T(8,128)(2,1)S(1)}, u32[]{:S(2)}, u32[]{:S(2)}) collective-permute-start(bf16[88,1152]{1,0:T(8,128)(2,1)S(1)} %pad_maximum_fusion.7), channel_id=1, source_target_pairs={{0,12},{1,13},{2,14},{3,15},{4,8},{5,9},{6,10},{7,11},{8,4},{9,5},... | collective-permute-start | bytes 608264 | tf_op jit(solution)/shard_map/ppermute | solution.py:31
  15.0 8.5 %collective-permute-start.7 = (bf16[88,1152]{1,0:T(8,128)(2,1)S(1)}, bf16[88,1152]{1,0:T(8,128)(2,1)S(1)}, u32[]{:S(2)}, u32[]{:S(2)}) collective-permute-start(bf16[88,1152]{1,0:T(8,128)(2,1)S(1)} %pad_maximum_fusion.7), channel_id=1, source_target_pairs={{0,8},{1,9},{2,10},{3,11},{4,12},{5,13},{6,14},{7,15},{8,0},{9,1},... | collective-permute-start | bytes 608264 | tf_op jit(solution)/shard_map/ppermute | solution.py:31
  17.3 7.0 %collective-permute-start.6 = (bf16[88,1152]{1,0:T(8,128)(2,1)S(1)}, bf16[88,1152]{1,0:T(8,128)(2,1)S(1)}, u32[]{:S(2)}, u32[]{:S(2)}) collective-permute-start(bf16[88,1152]{1,0:T(8,128)(2,1)S(1)} %pad_maximum_fusion.7), channel_id=1, source_target_pairs={{0,4},{1,5},{2,6},{3,7},{4,0},{5,1},{6,2},{7,3},{8,12},{9,13},{10,... | collective-permute-start | bytes 608264 | tf_op jit(solution)/shard_map/ppermute | solution.py:31
  19.7 21.4 %collective-permute-start.11 = (bf16[4,88,1152]{2,1,0:T(8,128)(2,1)S(1)}, bf16[4,88,1152]{2,1,0:T(8,128)(2,1)S(1)}, u32[]{:S(2)}, u32[]{:S(2)}) collective-permute-start(bf16[4,88,1152]{2,1,0:T(8,128)(2,1)S(1)} %pad_maximum_fusion.ta_ref), channel_id=1, source_target_pairs={{0,66},{1,49},{2,64},{3,51},{4,70},{5,53},{6,68},{7,55},{8,74},{9,... | collective-permute-start | bytes 2433032 | tf_op jit(solution)/shard_map/ppermute | solution.py:31
  22.5 18.6 %collective-permute-start.10 = (bf16[4,88,1152]{2,1,0:T(8,128)(2,1)S(1)}, bf16[4,88,1152]{2,1,0:T(8,128)(2,1)S(1)}, u32[]{:S(2)}, u32[]{:S(2)}) collective-permute-start(bf16[4,88,1152]{2,1,0:T(8,128)(2,1)S(1)} %pad_maximum_fusion.ta_ref), channel_id=1, source_target_pairs={{0,64},{1,33},{2,66},{3,35},{4,68},{5,37},{6,70},{7,39},{8,72},{9,... | collective-permute-start | bytes 2433032 | tf_op jit(solution)/shard_map/ppermute | solution.py:31
  24.4 16.7 %collective-permute-start.9 = (bf16[352,1152]{1,0:T(8,128)(2,1)S(1)}, bf16[352,1152]{1,0:T(8,128)(2,1)S(1)}, u32[]{:S(2)}, u32[]{:S(2)}) collective-permute-start(bf16[352,1152]{1,0:T(8,128)(2,1)S(1)} %pad_maximum_fusion.1.im0_ref), channel_id=1, source_target_pairs={{0,1},{1,0},{2,3},{3,2},{4,5},{5,4},{6,7},{7,6},{8,9},{9,8},{10,11... | collective-permute-start | bytes 2433032 | tf_op jit(solution)/shard_map/ppermute | solution.py:31
  27.8 23.6 %collective-permute-start.4 = (bf16[4,88,1152]{2,1,0:T(8,128)(2,1)S(1)}, bf16[4,88,1152]{2,1,0:T(8,128)(2,1)S(1)}, u32[]{:S(2)}, u32[]{:S(2)}) collective-permute-start(bf16[4,88,1152]{2,1,0:T(8,128)(2,1)S(1)} %pad_maximum_fusion.ta_ref), channel_id=1, source_target_pairs={{0,2},{1,17},{2,0},{3,19},{4,6},{5,21},{6,4},{7,23},{8,10},{9,25},... | collective-permute-start | bytes 2433032 | tf_op jit(solution)/shard_map/ppermute | solution.py:31
  49.4 13.4 %collective-permute-start.13 = (bf16[360,1152]{1,0:T(8,128)(2,1)S(1)}, bf16[360,1152]{1,0:T(8,128)(2,1)S(1)}, u32[]{:S(2)}, u32[]{:S(2)}) collective-permute-start(bf16[360,1152]{1,0:T(8,128)(2,1)S(1)} %get-tuple-element.51), channel_id=1, source_target_pairs={{0,64},{1,33},{2,66},{3,35},{4,68},{5,37},{6,70},{7,39},{8,72},{9,... | collective-permute-start | bytes 2488328 | tf_op jit(solution)/shard_map/ppermute | solution.py:31
  54.3 8.6 %collective-permute-start.12 = (f32[8,128]{1,0:T(8,128)S(1)}, f32[8,128]{1,0:T(8,128)S(1)}, u32[]{:S(2)}, u32[]{:S(2)}) collective-permute-start(f32[8,128]{1,0:T(8,128)S(1)} %get-tuple-element.50), channel_id=1, source_target_pairs={{0,16},{1,17},{2,18},{3,19},{4,20},{5,21},{6,22},{7,23},{8,24},{9,... | collective-permute-start | bytes 12296 | tf_op jit(solution)/shard_map/ppermute | solution.py:31
  62.9 15.1 %collective-permute-start.15 = (f32[88,1152]{1,0:T(8,128)S(1)}, f32[88,1152]{1,0:T(8,128)S(1)}, u32[]{:S(2)}, u32[]{:S(2)}) collective-permute-start(f32[88,1152]{1,0:T(8,128)S(1)} %get-tuple-element.53), channel_id=1, source_target_pairs={{0,1},{1,0},{2,3},{3,2},{4,5},{5,4},{6,7},{7,6},{8,9},{9,8},{10,11... | collective-permute-start | bytes 1216520 | tf_op jit(solution)/shard_map/ppermute | solution.py:31
  65.0 20.9 %collective-permute-start.19 = (bf16[360,1152]{1,0:T(8,128)(2,1)S(1)}, bf16[360,1152]{1,0:T(8,128)(2,1)S(1)}, u32[]{:S(2)}, u32[]{:S(2)}) collective-permute-start(bf16[360,1152]{1,0:T(8,128)(2,1)S(1)} %get-tuple-element.62), channel_id=1, source_target_pairs={{0,2},{1,17},{2,0},{3,19},{4,6},{5,21},{6,4},{7,23},{8,10},{9,25},... | collective-permute-start | bytes 2488328 | tf_op jit(solution)/shard_map/ppermute | solution.py:31
  65.0 20.9 %collective-permute-start.20 = (bf16[360,1152]{1,0:T(8,128)(2,1)S(1)}, bf16[360,1152]{1,0:T(8,128)(2,1)S(1)}, u32[]{:S(2)}, u32[]{:S(2)}) collective-permute-start(bf16[360,1152]{1,0:T(8,128)(2,1)S(1)} %get-tuple-element.63), channel_id=1, source_target_pairs={{0,66},{1,49},{2,64},{3,51},{4,70},{5,53},{6,68},{7,55},{8,74},{9,... | collective-permute-start | bytes 2488328 | tf_op jit(solution)/shard_map/ppermute | solution.py:31
  66.8 11.1 %collective-permute-start.14 = (f32[8,128]{1,0:T(8,128)S(1)}, f32[8,128]{1,0:T(8,128)S(1)}, u32[]{:S(2)}, u32[]{:S(2)}) collective-permute-start(f32[8,128]{1,0:T(8,128)S(1)} %add.25), channel_id=1, source_target_pairs={{0,48},{1,49},{2,50},{3,51},{4,52},{5,53},{6,54},{7,55},{8,56},{9,... | collective-permute-start | bytes 12296 | tf_op jit(solution)/shard_map/ppermute | solution.py:31
  67.7 10.7 %collective-permute-start.16 = (f32[88,1152]{1,0:T(8,128)S(1)}, f32[88,1152]{1,0:T(8,128)S(1)}, u32[]{:S(2)}, u32[]{:S(2)}) collective-permute-start(f32[88,1152]{1,0:T(8,128)S(1)} %get-tuple-element.54), channel_id=1, source_target_pairs={{0,1},{1,0},{2,3},{3,2},{4,5},{5,4},{6,7},{7,6},{8,9},{9,8},{10,11... | collective-permute-start | bytes 1216520 | tf_op jit(solution)/shard_map/ppermute | solution.py:31
  77.9 1.7 %collective-permute-start.17 = (f32[88,1152]{1,0:T(8,128)S(1)}, f32[88,1152]{1,0:T(8,128)S(1)}, u32[]{:S(2)}, u32[]{:S(2)}) collective-permute-start(f32[88,1152]{1,0:T(8,128)S(1)} %get-tuple-element.55), channel_id=1, source_target_pairs={{0,1},{1,0},{2,3},{3,2},{4,5},{5,4},{6,7},{7,6},{8,9},{9,8},{10,11... | collective-permute-start | bytes 1216520 | tf_op jit(solution)/shard_map/ppermute | solution.py:31
  77.9 2.3 %collective-permute-start.18 = (f32[88,1152]{1,0:T(8,128)S(1)}, f32[88,1152]{1,0:T(8,128)S(1)}, u32[]{:S(2)}, u32[]{:S(2)}) collective-permute-start(f32[88,1152]{1,0:T(8,128)S(1)} %get-tuple-element.56), channel_id=1, source_target_pairs={{0,1},{1,0},{2,3},{3,2},{4,5},{5,4},{6,7},{7,6},{8,9},{9,8},{10,11... | collective-permute-start | bytes 1216520 | tf_op jit(solution)/shard_map/ppermute | solution.py:31
  81.2 7.7 %collective-permute-start.21 = (bf16[96,1152]{1,0:T(8,128)(2,1)S(1)}, bf16[96,1152]{1,0:T(8,128)(2,1)S(1)}, u32[]{:S(2)}, u32[]{:S(2)}) collective-permute-start(bf16[96,1152]{1,0:T(8,128)(2,1)S(1)} %get-tuple-element.57), channel_id=1, source_target_pairs={{0,4},{1,5},{2,6},{3,7},{4,0},{5,1},{6,2},{7,3},{8,12},{9,13},{10,... | collective-permute-start | bytes 663560 | tf_op jit(solution)/shard_map/ppermute | solution.py:31
  82.5 12.7 %collective-permute-start.22 = (bf16[96,1152]{1,0:T(8,128)(2,1)S(1)}, bf16[96,1152]{1,0:T(8,128)(2,1)S(1)}, u32[]{:S(2)}, u32[]{:S(2)}) collective-permute-start(bf16[96,1152]{1,0:T(8,128)(2,1)S(1)} %get-tuple-element.58), channel_id=1, source_target_pairs={{0,8},{1,9},{2,10},{3,11},{4,12},{5,13},{6,14},{7,15},{8,0},{9,1},... | collective-permute-start | bytes 663560 | tf_op jit(solution)/shard_map/ppermute | solution.py:31
  84.9 12.2 %collective-permute-start.23 = (bf16[96,1152]{1,0:T(8,128)(2,1)S(1)}, bf16[96,1152]{1,0:T(8,128)(2,1)S(1)}, u32[]{:S(2)}, u32[]{:S(2)}) collective-permute-start(bf16[96,1152]{1,0:T(8,128)(2,1)S(1)} %get-tuple-element.59), channel_id=1, source_target_pairs={{0,12},{1,13},{2,14},{3,15},{4,8},{5,9},{6,10},{7,11},{8,4},{9,5},... | collective-permute-start | bytes 663560 | tf_op jit(solution)/shard_map/ppermute | solution.py:31
  97.9 8.5 %collective-permute-start.24 = (f32[96,576]{1,0:T(8,128)S(1)}, f32[96,576]{1,0:T(8,128)S(1)}, u32[]{:S(2)}, u32[]{:S(2)}) collective-permute-start(f32[96,576]{1,0:T(8,128)S(1)} %slice.102), channel_id=1, source_target_pairs={{0,2},{1,3},{2,0},{3,1},{4,6},{5,7},{6,4},{7,5},{8,10},{9,11},{10,... | collective-permute-start | bytes 663560 | tf_op jit(solution)/shard_map/ppermute | solution.py:31
  98.0 7.9 %collective-permute-start.25 = (f32[8,576]{1,0:T(8,128)S(1)}, f32[8,576]{1,0:T(8,128)S(1)}, u32[]{:S(2)}, u32[]{:S(2)}) collective-permute-start(f32[8,576]{1,0:T(8,128)S(1)} %slice.101), channel_id=1, source_target_pairs={{0,64},{1,65},{2,66},{3,67},{4,68},{5,69},{6,70},{7,71},{8,72},{9,... | collective-permute-start | bytes 55304 | tf_op jit(solution)/shard_map/ppermute | solution.py:31
  101.4 5.0 %collective-permute-start.26 = (f32[8,576]{1,0:T(8,128)S(1)}, f32[8,576]{1,0:T(8,128)S(1)}, u32[]{:S(2)}, u32[]{:S(2)}) collective-permute-start(f32[8,576]{1,0:T(8,128)S(1)} %slice.101), channel_id=1, source_target_pairs={{0,66},{1,67},{2,64},{3,65},{4,70},{5,71},{6,68},{7,69},{8,74},{9,... | collective-permute-start | bytes 55304 | tf_op jit(solution)/shard_map/ppermute | solution.py:31
  101.8 6.9 %collective-permute-start.27 = (bf16[96,1152]{1,0:T(8,128)(2,1)S(1)}, bf16[96,1152]{1,0:T(8,128)(2,1)S(1)}, u32[]{:S(2)}, u32[]{:S(2)}) collective-permute-start(bf16[96,1152]{1,0:T(8,128)(2,1)S(1)} %get-tuple-element.68), channel_id=1, source_target_pairs={{0,16},{1,3},{2,18},{3,1},{4,20},{5,7},{6,22},{7,5},{8,24},{9,11},... | collective-permute-start | bytes 663560 | tf_op jit(solution)/shard_map/ppermute | solution.py:31
  101.8 11.3 %collective-permute-start.28 = (bf16[96,1152]{1,0:T(8,128)(2,1)S(1)}, bf16[96,1152]{1,0:T(8,128)(2,1)S(1)}, u32[]{:S(2)}, u32[]{:S(2)}) collective-permute-start(bf16[96,1152]{1,0:T(8,128)(2,1)S(1)} %get-tuple-element.69), channel_id=1, source_target_pairs={{0,32},{1,65},{2,34},{3,67},{4,36},{5,69},{6,38},{7,71},{8,40},{9,... | collective-permute-start | bytes 663560 | tf_op jit(solution)/shard_map/ppermute | solution.py:31
  105.9 8.5 %collective-permute-start.29 = (bf16[96,1152]{1,0:T(8,128)(2,1)S(1)}, bf16[96,1152]{1,0:T(8,128)(2,1)S(1)}, u32[]{:S(2)}, u32[]{:S(2)}) collective-permute-start(bf16[96,1152]{1,0:T(8,128)(2,1)S(1)} %get-tuple-element.70), channel_id=1, source_target_pairs={{0,48},{1,67},{2,50},{3,65},{4,52},{5,71},{6,54},{7,69},{8,56},{9,... | collective-permute-start | bytes 663560 | tf_op jit(solution)/shard_map/ppermute | solution.py:31
  115.7 4.7 %collective-permute-start.30 = (f32[360,288]{0,1:T(8,128)S(1)}, f32[360,288]{0,1:T(8,128)S(1)}, u32[]{:S(2)}, u32[]{:S(2)}) collective-permute-start(f32[360,288]{0,1:T(8,128)S(1)} %copy.17), channel_id=1, source_target_pairs={{0,1},{1,0},{2,3},{3,2},{4,5},{5,4},{6,7},{7,6},{8,9},{9,8},{10,11... | collective-permute-start | bytes 1244168 | tf_op jit(solution)/shard_map/ppermute | solution.py:31

commit v7 on v6

--- a/solution.py
+++ b/solution.py
@@ -127,16 +127,16 @@
     sums_ref[...] = sums + sums_before[...]
 
 
-def near_last_kernel(
-    rows, half, feats, info_ref, images, t_rel, coeff_low, before_ref, own_ref, m_ref, img0_ref, *refs,
-):
-    others, grads = refs[:4], refs[4]
-    quarter = 4 * rows
+def near_text_kernel(rows, half, feats, info_ref, images, coeff_low, own_ref, m_ref, grads):
     text_parts(info_ref, rows, half, coeff_low, images, grads)
     own_ref[...] = jnp.concatenate([grads[0, i] for i in range(4)], axis=0)
     m_ref[...] = message([grads[1, i] for i in range(4)], feats)
+
+
+def near_image_kernel(rows, t_rel, coeff_low, before_ref, own_ref, *others):
+    quarter = 4 * rows
     acc = image_parts(coeff_low, t_rel) + before_ref[...]
-    img0_ref[...] = acc[0:quarter]
+    own_ref[...] = acc[0:quarter]
     for k, img_ref in enumerate(others):
         img_ref[...] = acc[quarter + k * rows : quarter + (k + 1) * rows]
 
@@ -274,21 +274,24 @@
         info, scales, second[0], second[1], images_own, images_other, sums,
         scalars=2, mib=30, products=1,
     )
-    text, m1, img_own, *img_others = call(
-        functools.partial(near_last_kernel, *sizes), "tile_near_last",
-        [f32(quarter, feats), bf16(quarter + 8, feats), f32(quarter, feats)] + [f32(rows, feats)] * 4,
-        info, images, t_rel, coeff_low, acc,
-        scalars=1, mib=30, products=2, scratch=[grads],
-    )
-
-    one = sums + swap(sums, y_mask(1))
+    two = sums + swap(sums, y_mask(1))
+    img_own, *img_others = call(
+        functools.partial(near_image_kernel, rows), "tile_near_image", [f32(quarter, feats)] + [f32(rows, feats)] * 4,
+        t_rel, coeff_low, acc, mib=30, products=1,
+    )
+    coeff_low, two, img_own, img_others = lax.optimization_barrier((coeff_low, two, img_own, img_others))
+    img_others = [swap(part, CORE) for part in img_others]
+    sums = two + swap(two, y_mask(3))
+    text, m1 = call(
+        functools.partial(near_text_kernel, *sizes), "tile_near_text", [f32(quarter, feats), bf16(quarter + 8, feats)],
+        info, images, coeff_low, scalars=1, mib=30, products=1, scratch=[grads],
+    )
     got2 = swap(m2, z_mask(2), y_mask(2))
-    m1, m3, img_others, one, got2 = lax.optimization_barrier((m1, m3, img_others, one, got2))
+    m1, m3, sums, got2, img_others = lax.optimization_barrier((m1, m3, sums, got2, img_others))
     got1, got3 = swap(m1, z_mask(1), y_mask(1)), swap(m3, z_mask(3), y_mask(3))
-    sums = one + swap(one, y_mask(3))
     img, *messages = call(
         functools.partial(image_first_kernel, rows, feats), "image_first",
-        [f32(rows, feats)] + [bf16(rows + 8, feats)] * 3, img_own, sums, *[swap(part, CORE) for part in img_others],
+        [f32(rows, feats)] + [bf16(rows + 8, feats)] * 3, img_own, sums, *img_others,
     )
     img_got = [swap(m, x_mask(k)) for k, m in zip((1, 2, 3), messages)]
     (far,) = call(text_far_kernel, "text_far", [f32(quarter, feats)], after(text, *messages), got2)
@@ -300,13 +303,13 @@
 
     img_got[0] = after(img_got[0], text)
     (img,) = call(
-        functools.partial(image_last_kernel, feats), "image_last", [f32(rows + 8, feats)], logit_scaler, img, sums, *img_got, scalars=1
-    )
-    keep, back = img[:, :half], swap(img[:, half:], z_mask(1))
+        functools.partial(image_last_kernel, feats), "image_last", [f32(rows + 8, feats)], logit_scaler, img, sums, *img_got, scalars=1, products=1
+    )
+    (text,) = call(text_last_kernel, "text_last", [f32(rows, feats)], logit_scaler, text, *got, scalars=1, products=2)
+    keep, back = img[:, :half], after(swap(img[:, half:], z_mask(1)), text)
     image = jnp.concatenate(by(lo0, keep[:rows], back[:rows]), axis=0)
     sums = keep[rows:]
     sums = (sums + back[rows:]) + (swap(sums, z_mask(2)) + swap(sums, z_mask(3)))
-    (text,) = call(text_last_kernel, "text_last", [f32(rows, feats)], logit_scaler, after(text, img, sums), *got, scalars=1)
     whole = jnp.concatenate([text[:, :half], text[:, half:], image, sums], axis=0)
     mine, other = by(on0, whole[:, :width], whole[:, width:])
     other = swap(other, CORE)

time: 124 us -> 109 us (0.88)
  waiting for transfers between devices: 48.1 us -> 37.9 us
  starting transfers between devices: 43.1 us -> 37.9 us
    ppermute x31, waiting for transfers between devices: 48.1 us -> 37.9 us  [swap(): lax.ppermute(array, AXES, [(i, i ^ (mask1 if i & 1 else mask0)) for i in...]
    ppermute x31, starting transfers between devices: 43.1 us -> 37.9 us  [swap(): lax.ppermute(array, AXES, [(i, i ^ (mask1 if i & 1 else mask0)) for i in...]
    pallas_call x8 -> x9, Pallas kernels: 22.5 us -> 22.8 us  [call(): pl.pallas_call(kernel, out_shape=out_shape, in_specs=[SMEM] * scalars + [...]
  transfers between devices with their start and end apart: 31 -> 31, of which waited for: 17 -> 14; matrix products, arithmetic and copies ran while one was open for 1% -> 1% of each run, Pallas kernels for 17% -> 21%
where the time goes in v7:
time: 109 us
  starting transfers between devices  37.9 us (35%)
  waiting for transfers between devices  37.9 us (35%)
  Pallas kernels  22.8 us (21%)
  local copies, waits for them, and re-layouts  5.72 us (5%)
  between operations  2.26 us (2%)
  other arithmetic  2.11 us (2%)
    ppermute x31, waiting for transfers between devices, swap(): lax.ppermute(array, AXES, [(i, i ^ (mask1 if i & 1 else mask0)) for i in...  37.9 us
    ppermute x31, starting transfers between devices, swap(): lax.ppermute(array, AXES, [(i, i ^ (mask1 if i & 1 else mask0)) for i in...  37.9 us
    pallas_call x9, Pallas kernels, call(): pl.pallas_call(kernel, out_shape=out_shape, in_specs=[SMEM] * scalars + [...  22.8 us
    unnamed x11, local copies, waits for them, and re-layouts  2.99 us
  transfers between devices with their start and end apart: 31, of which 14 were waited for; matrix products, arithmetic and copies ran while one was open for 1% of the time, Pallas kernels for 21%

profile of v7, /device:TPU:1, one launch (start us, length us, event | category | flops | bytes accessed | tf_op | source)
XLA Modules:
  0.0 108.7 jit_solution(8473732600191478670)
XLA Ops:
  0.6 1.1 %fusion.6 = (bf16[176,288]{0,1:T(8,128)(2,1)S(1)}, bf16[176,288]{0,1:T(8,128)(2,1)S(1)}) fusion(bf16[352,288]{0,1:T(8,128)(2,1)} %param.4), kind=kLoop, calls=%fused_computation.41 | loop fusion | bytes 405504 | tf_op jit(solution)/shard_map/slice | solution.py:224
  2.0 1.1 %fusion.5 = (bf16[176,288]{0,1:T(8,128)(2,1)S(1)}, bf16[176,288]{0,1:T(8,128)(2,1)S(1)}) fusion(bf16[352,288]{0,1:T(8,128)(2,1)} %param.5), kind=kLoop, calls=%fused_computation.40 | loop fusion | bytes 405504 | tf_op jit(solution)/shard_map/slice | solution.py:224
  3.5 1.5 %collective-permute-start = (bf16[352,288]{1,0:T(8,128)(2,1)S(1)}, bf16[352,288]{1,0:T(8,128)(2,1)S(1)}, u32[]{:S(2)}, u32[]{:S(2)}) collective-permute-start(bf16[352,288]{1,0:T(8,128)(2,1)S(1)} %broadcast_select_fusion.2), channel_id=1, source_target_pairs={{0,1},{1,0},{2,3},{3,2},{4,5},{5,4},{6,7},{7,6},{8,9},{9,8},{10,11... | collective-permute-start | bytes 608264 | tf_op jit(solution)/shard_map/ppermute | solution.py:31
  5.0 1.2 %collective-permute-done = bf16[352,288]{1,0:T(8,128)(2,1)S(1)} collective-permute-done((bf16[352,288]{1,0:T(8,128)(2,1)S(1)}, bf16[352,288]{1,0:T(8,128)(2,1)S(1)}, u32[]{:S(2)}, u32[]{:S(2)}) %collective-permute-start) | collective-permute-done | bytes 202784 | tf_op jit(solution)/shard_map/ppermute | solution.py:31
  6.6 1.8 %collective-permute-start.5 = (bf16[88,576]{1,0:T(8,128)(2,1)S(1)}, bf16[88,576]{1,0:T(8,128)(2,1)S(1)}, u32[]{:S(2)}, u32[]{:S(2)}) collective-permute-start(bf16[88,576]{1,0:T(8,128)(2,1)S(1)} %get-tuple-element.103), channel_id=1, source_target_pairs={{0,2},{1,3},{2,0},{3,1},{4,6},{5,7},{6,4},{7,5},{8,10},{9,11},{10,... | collective-permute-start | bytes 304136 | tf_op jit(solution)/shard_map/ppermute | solution.py:31
  8.6 3.4 %collective-permute-start.2 = (bf16[88,1152]{1,0:T(8,128)(2,1)S(1)}, bf16[88,1152]{1,0:T(8,128)(2,1)S(1)}, u32[]{:S(2)}, u32[]{:S(2)}) collective-permute-start(bf16[88,1152]{1,0:T(8,128)(2,1)S(1)} %pad_maximum_fusion.6), channel_id=1, source_target_pairs={{0,32},{1,65},{2,34},{3,67},{4,36},{5,69},{6,38},{7,71},{8,40},{9,... | collective-permute-start | bytes 608264 | tf_op jit(solution)/shard_map/ppermute | solution.py:31
  12.5 2.6 %collective-permute-start.8 = (bf16[88,1152]{1,0:T(8,128)(2,1)S(1)}, bf16[88,1152]{1,0:T(8,128)(2,1)S(1)}, u32[]{:S(2)}, u32[]{:S(2)}) collective-permute-start(bf16[88,1152]{1,0:T(8,128)(2,1)S(1)} %pad_maximum_fusion.7), channel_id=1, source_target_pairs={{0,12},{1,13},{2,14},{3,15},{4,8},{5,9},{6,10},{7,11},{8,4},{9,5},... | collective-permute-start | bytes 608264 | tf_op jit(solution)/shard_map/ppermute | solution.py:31
  15.0 0.5 collective-permute-start.7
  15.5 1.8 %collective-permute-done.2 = bf16[88,1152]{1,0:T(8,128)(2,1)S(1)} collective-permute-done((bf16[88,1152]{1,0:T(8,128)(2,1)S(1)}, bf16[88,1152]{1,0:T(8,128)(2,1)S(1)}, u32[]{:S(2)}, u32[]{:S(2)}) %collective-permute-start.2) | collective-permute-done | bytes 202784 | tf_op jit(solution)/shard_map/ppermute | solution.py:31
  17.3 1.2 %collective-permute-start.6 = (bf16[88,1152]{1,0:T(8,128)(2,1)S(1)}, bf16[88,1152]{1,0:T(8,128)(2,1)S(1)}, u32[]{:S(2)}, u32[]{:S(2)}) collective-permute-start(bf16[88,1152]{1,0:T(8,128)(2,1)S(1)} %pad_maximum_fusion.7), channel_id=1, source_target_pairs={{0,4},{1,5},{2,6},{3,7},{4,0},{5,1},{6,2},{7,3},{8,12},{9,13},{10,... | collective-permute-start | bytes 608264 | tf_op jit(solution)/shard_map/ppermute | solution.py:31
  18.5 1.0 collective-permute-done.3
  19.7 2.8 %collective-permute-start.11 = (bf16[4,88,1152]{2,1,0:T(8,128)(2,1)S(1)}, bf16[4,88,1152]{2,1,0:T(8,128)(2,1)S(1)}, u32[]{:S(2)}, u32[]{:S(2)}) collective-permute-start(bf16[4,88,1152]{2,1,0:T(8,128)(2,1)S(1)} %pad_maximum_fusion.ta_ref), channel_id=1, source_target_pairs={{0,66},{1,49},{2,64},{3,51},{4,70},{5,53},{6,68},{7,55},{8,74},{9,... | collective-permute-start | bytes 2433032 | tf_op jit(solution)/shard_map/ppermute | solution.py:31
  22.8 0.7 collective-permute-done.8
  23.6 0.8 collective-permute-done.6
  24.4 1.9 %collective-permute-start.9 = (bf16[352,1152]{1,0:T(8,128)(2,1)S(1)}, bf16[352,1152]{1,0:T(8,128)(2,1)S(1)}, u32[]{:S(2)}, u32[]{:S(2)}) collective-permute-start(bf16[352,1152]{1,0:T(8,128)(2,1)S(1)} %pad_maximum_fusion.1.im0_ref), channel_id=1, source_target_pairs={{0,1},{1,0},{2,3},{3,2},{4,5},{5,4},{6,7},{7,6},{8,9},{9,8},{10,11... | collective-permute-start | bytes 2433032 | tf_op jit(solution)/shard_map/ppermute | solution.py:31
  26.3 1.3 %collective-permute-start.4 = (bf16[4,88,1152]{2,1,0:T(8,128)(2,1)S(1)}, bf16[4,88,1152]{2,1,0:T(8,128)(2,1)S(1)}, u32[]{:S(2)}, u32[]{:S(2)}) collective-permute-start(bf16[4,88,1152]{2,1,0:T(8,128)(2,1)S(1)} %pad_maximum_fusion.ta_ref), channel_id=1, source_target_pairs={{0,2},{1,17},{2,0},{3,19},{4,6},{5,21},{6,4},{7,23},{8,10},{9,25},... | collective-permute-start | bytes 2433032 | tf_op jit(solution)/shard_map/ppermute | solution.py:31
  29.1 12.1 %collective-permute-done.11.tb_ref = bf16[4,88,1152]{2,1,0:T(8,128)(2,1)S(1)} collective-permute-done((bf16[4,88,1152]{2,1,0:T(8,128)(2,1)S(1)}, bf16[4,88,1152]{2,1,0:T(8,128)(2,1)S(1)}, u32[]{:S(2)}, u32[]{:S(2)}) %collective-permute-start.11) | collective-permute-done | bytes 811040 | tf_op jit(solution)/shard_map/ppermute | solution.py:31
  41.1 8.3 %tile_far.1 = (bf16[360,1152]{1,0:T(8,128)(2,1)S(1)}, bf16[360,1152]{1,0:T(8,128)(2,1)S(1)}, f32[704,1152]{1,0:T(8,128)S(1)}, f32[8,128]{1,0:T(8,128)S(1)}) custom-call(s32[2]{0:T(128)S(1)} %pad_add_fusion.info_ref, f32[2]{0:T(128)S(1)} %pad_maximum_fusion.9.scale_ref, bf16[4,88,1152]{2,1,0:T(8,128)(2,1)S(1)} %collective-permute-done.10.ta_ref, ...), custom_call_target="tpu_custom_call" | custom-call | flops 3425697792 | bytes 8151056 | tf_op jit(solution)/shard_map/tile_far/pallas_call | solution.py:244
  49.4 1.9 %collective-permute-start.14 = (bf16[360,1152]{1,0:T(8,128)(2,1)S(1)}, bf16[360,1152]{1,0:T(8,128)(2,1)S(1)}, u32[]{:S(2)}, u32[]{:S(2)}) collective-permute-start(bf16[360,1152]{1,0:T(8,128)(2,1)S(1)} %get-tuple-element.61), channel_id=1, source_target_pairs={{0,64},{1,33},{2,66},{3,35},{4,68},{5,37},{6,70},{7,39},{8,72},{9,... | collective-permute-start | bytes 2488328 | tf_op jit(solution)/shard_map/ppermute | solution.py:31
  51.3 3.0 %tile_near_first.1 = (bf16[704,1152]{1,0:T(8,128)(2,1)S(1)}, bf16[704,1152]{1,0:T(8,128)(2,1)S(1)}, bf16[704,704]{1,0:T(8,128)(2,1)S(1)}, f32[8,128]{1,0:T(8,128)S(1)}) custom-call(s32[2]{0:T(128)S(1)} %pad_add_fusion.info_ref, f32[2]{0:T(128)S(1)} %pad_maximum_fusion.9.scale_ref, bf16[4,88,1152]{2,1,0:T(8,128)(2,1)S(1)} %pad_maximum_fusion.ta_ref, ...), custom_call_target="tpu_custom_call" | custom-call | flops 1141899264 | bytes 7487504 | tf_op jit(solution)/shard_map/tile_near_first/pallas_call | solution.py:244
  54.3 1.3 %collective-permute-start.12 = (f32[8,128]{1,0:T(8,128)S(1)}, f32[8,128]{1,0:T(8,128)S(1)}, u32[]{:S(2)}, u32[]{:S(2)}) collective-permute-start(f32[8,128]{1,0:T(8,128)S(1)} %get-tuple-element.47), channel_id=1, source_target_pairs={{0,16},{1,17},{2,18},{3,19},{4,20},{5,21},{6,22},{7,23},{8,24},{9,... | collective-permute-start | bytes 12296 | tf_op jit(solution)/shard_map/ppermute | solution.py:31
  55.6 1.6 %tile_near_image.1 = (f32[352,1152]{1,0:T(8,128)S(1)}, f32[88,1152]{1,0:T(8,128)S(1)}, f32[88,1152]{1,0:T(8,128)S(1)}, f32[88,1152]{1,0:T(8,128)S(1)}, f32[88,1152]{1,0:T(8,128)S(1)}) custom-call(bf16[704,1152]{1,0:T(8,128)(2,1)S(1)} %get-tuple-element.48.t_rel, bf16[704,704]{1,0:T(8,128)(2,1)S(1)} %get-tuple-element.55.coeff_low, ...), custom_call_target="tpu_custom_call" | custom-call | flops 1141899264 | bytes 9101312 | tf_op jit(solution)/shard_map/tile_near_image/pallas_call | solution.py:244
  57.3 5.6 %collective-permute-done.12 = f32[8,128]{1,0:T(8,128)S(1)} collective-permute-done((f32[8,128]{1,0:T(8,128)S(1)}, f32[8,128]{1,0:T(8,128)S(1)}, u32[]{:S(2)}, u32[]{:S(2)}) %collective-permute-start.12) | collective-permute-done | bytes 4128 | tf_op jit(solution)/shard_map/ppermute | solution.py:31
  63.2 0.5 collective-permute-start.16
  63.7 2.9 %collective-permute-done.13 = f32[8,128]{1,0:T(8,128)S(1)} collective-permute-done((f32[8,128]{1,0:T(8,128)S(1)}, f32[8,128]{1,0:T(8,128)S(1)}, u32[]{:S(2)}, u32[]{:S(2)}) %collective-permute-start.13) | collective-permute-done | bytes 4128 | tf_op jit(solution)/shard_map/ppermute | solution.py:31
  66.6 4.0 %tile_near_text.1 = (f32[352,1152]{1,0:T(8,128)S(1)}, bf16[360,1152]{1,0:T(8,128)(2,1)S(1)}) custom-call(s32[2]{0:T(128)S(1)} %pad_add_fusion.info_ref, bf16[704,1152]{1,0:T(8,128)(2,1)S(1)} %get-tuple-element.45.images, bf16[704,704]{1,0:T(8,128)(2,1)S(1)} %get-tuple-element.55.coeff_low), custom_call_target="tpu_custom_call" | custom-call | flops 1141899264 | bytes 5064712 | tf_op jit(solution)/shard_map/tile_near_text/pallas_call | solution.py:244
  70.7 0.4 collective-permute-start.20
  71.1 0.9 image_first.1
  72.0 1.2 %collective-permute-start.24 = (bf16[96,1152]{1,0:T(8,128)(2,1)S(1)}, bf16[96,1152]{1,0:T(8,128)(2,1)S(1)}, u32[]{:S(2)}, u32[]{:S(2)}) collective-permute-start(bf16[96,1152]{1,0:T(8,128)(2,1)S(1)} %get-tuple-element.71), channel_id=1, source_target_pairs={{0,4},{1,5},{2,6},{3,7},{4,0},{5,1},{6,2},{7,3},{8,12},{9,13},{10,... | collective-permute-start | bytes 663560 | tf_op jit(solution)/shard_map/ppermute | solution.py:31
  73.2 2.5 %collective-permute-start.25 = (bf16[96,1152]{1,0:T(8,128)(2,1)S(1)}, bf16[96,1152]{1,0:T(8,128)(2,1)S(1)}, u32[]{:S(2)}, u32[]{:S(2)}) collective-permute-start(bf16[96,1152]{1,0:T(8,128)(2,1)S(1)} %get-tuple-element.72), channel_id=1, source_target_pairs={{0,8},{1,9},{2,10},{3,11},{4,12},{5,13},{6,14},{7,15},{8,0},{9,1},... | collective-permute-start | bytes 663560 | tf_op jit(solution)/shard_map/ppermute | solution.py:31
  76.0 0.8 text_far.1.own_ref
  76.7 5.6 %collective-permute-done.19.r1_ref = bf16[360,1152]{1,0:T(8,128)(2,1)S(1)} collective-permute-done((bf16[360,1152]{1,0:T(8,128)(2,1)S(1)}, bf16[360,1152]{1,0:T(8,128)(2,1)S(1)}, u32[]{:S(2)}, u32[]{:S(2)}) %collective-permute-start.19) | collective-permute-done | bytes 829472 | tf_op jit(solution)/shard_map/ppermute | solution.py:31
  82.3 1.3 %collective-permute-done.20.r3_ref = bf16[360,1152]{1,0:T(8,128)(2,1)S(1)} collective-permute-done((bf16[360,1152]{1,0:T(8,128)(2,1)S(1)}, bf16[360,1152]{1,0:T(8,128)(2,1)S(1)}, u32[]{:S(2)}, u32[]{:S(2)}) %collective-permute-start.20) | collective-permute-done | bytes 829472 | tf_op jit(solution)/shard_map/ppermute | solution.py:31
  83.6 3.0 %text_first.1 = (f32[88,1152]{1,0:T(8,128)S(1)}, bf16[96,1152]{1,0:T(8,128)(2,1)S(1)}, bf16[96,1152]{1,0:T(8,128)(2,1)S(1)}, bf16[96,1152]{1,0:T(8,128)(2,1)S(1)}) custom-call(f32[352,1152]{1,0:T(8,128)S(1)} %text_far.1.own_ref, bf16[360,1152]{1,0:T(8,128)(2,1)S(1)} %collective-permute-done.19.r1_ref, bf16[360,1152]{1,0:T(8,128)(2,1)S(1)} %collective-permute-done.20.r3_ref), custom_call_target="tpu_custom_call" | custom-call | bytes 4349952 | tf_op jit(solution)/shard_map/text_first/pallas_call | solution.py:244
  86.7 1.9 %collective-permute-start.22 = (bf16[96,1152]{1,0:T(8,128)(2,1)S(1)}, bf16[96,1152]{1,0:T(8,128)(2,1)S(1)}, u32[]{:S(2)}, u32[]{:S(2)}) collective-permute-start(bf16[96,1152]{1,0:T(8,128)(2,1)S(1)} %get-tuple-element.80), channel_id=1, source_target_pairs={{0,32},{1,65},{2,34},{3,67},{4,36},{5,69},{6,38},{7,71},{8,40},{9,... | collective-permute-start | bytes 663560 | tf_op jit(solution)/shard_map/ppermute | solution.py:31
  88.6 1.9 %collective-permute-start.23 = (bf16[96,1152]{1,0:T(8,128)(2,1)S(1)}, bf16[96,1152]{1,0:T(8,128)(2,1)S(1)}, u32[]{:S(2)}, u32[]{:S(2)}) collective-permute-start(bf16[96,1152]{1,0:T(8,128)(2,1)S(1)} %get-tuple-element.81), channel_id=1, source_target_pairs={{0,48},{1,67},{2,50},{3,65},{4,52},{5,71},{6,54},{7,69},{8,56},{9,... | collective-permute-start | bytes 663560 | tf_op jit(solution)/shard_map/ppermute | solution.py:31
  90.6 0.6 image_last.1
  91.3 1.3 %collective-permute-start.29 = (f32[8,576]{1,0:T(8,128)S(1)}, f32[8,576]{1,0:T(8,128)S(1)}, u32[]{:S(2)}, u32[]{:S(2)}) collective-permute-start(f32[8,576]{1,0:T(8,128)S(1)} %slice.105), channel_id=1, source_target_pairs={{0,66},{1,67},{2,64},{3,65},{4,70},{5,71},{6,68},{7,69},{8,74},{9,... | collective-permute-start | bytes 55304 | tf_op jit(solution)/shard_map/ppermute | solution.py:31
  92.7 1.5 %collective-permute-start.27 = (f32[96,576]{1,0:T(8,128)S(1)}, f32[96,576]{1,0:T(8,128)S(1)}, u32[]{:S(2)}, u32[]{:S(2)}) collective-permute-start(f32[96,576]{1,0:T(8,128)S(1)} %slice.104), channel_id=1, source_target_pairs={{0,2},{1,3},{2,0},{3,1},{4,6},{5,7},{6,4},{7,5},{8,10},{9,11},{10,... | collective-permute-start | bytes 663560 | tf_op jit(solution)/shard_map/ppermute | solution.py:31
  94.1 0.5 collective-permute-done.22.r2_ref
  94.6 2.5 %collective-permute-done.23.r3_ref = bf16[96,1152]{1,0:T(8,128)(2,1)S(1)} collective-permute-done((bf16[96,1152]{1,0:T(8,128)(2,1)S(1)}, bf16[96,1152]{1,0:T(8,128)(2,1)S(1)}, u32[]{:S(2)}, u32[]{:S(2)}) %collective-permute-start.23) | collective-permute-done | bytes 221216 | tf_op jit(solution)/shard_map/ppermute | solution.py:31
  97.2 0.6 text_last.1
  97.8 0.5 collective-permute-done.27
  99.0 5.0 %collective-permute-start.30 = (f32[360,288]{0,1:T(8,128)S(1)}, f32[360,288]{0,1:T(8,128)S(1)}, u32[]{:S(2)}, u32[]{:S(2)}) collective-permute-start(f32[360,288]{0,1:T(8,128)S(1)} %copy.17), channel_id=1, source_target_pairs={{0,1},{1,0},{2,3},{3,2},{4,5},{5,4},{6,7},{7,6},{8,9},{9,8},{10,11... | collective-permute-start | bytes 1244168 | tf_op jit(solution)/shard_map/ppermute | solution.py:31
  104.0 1.4 %collective-permute-done.30 = f32[360,288]{0,1:T(8,128)S(1)} collective-permute-done((f32[360,288]{0,1:T(8,128)S(1)}, f32[360,288]{0,1:T(8,128)S(1)}, u32[]{:S(2)}, u32[]{:S(2)}) %collective-permute-start.30) | collective-permute-done | bytes 414752 | tf_op jit(solution)/shard_map/ppermute | solution.py:31
  106.0 0.5 fusion.3
  106.7 1.0 copy.21
  107.7 1.0 copy.22
  (61 shorter events, 4.7 us)
Async XLA Ops:
  3.5 2.7 %collective-permute-start = (bf16[352,288]{1,0:T(8,128)(2,1)S(1)}, bf16[352,288]{1,0:T(8,128)(2,1)S(1)}, u32[]{:S(2)}, u32[]{:S(2)}) collective-permute-start(bf16[352,288]{1,0:T(8,128)(2,1)S(1)} %broadcast_select_fusion.2), channel_id=1, source_target_pairs={{0,1},{1,0},{2,3},{3,2},{4,5},{5,4},{6,7},{7,6},{8,9},{9,8},{10,11... | collective-permute-start | bytes 608264 | tf_op jit(solution)/shard_map/ppermute | solution.py:31
  6.6 5.8 %collective-permute-start.5 = (bf16[88,576]{1,0:T(8,128)(2,1)S(1)}, bf16[88,576]{1,0:T(8,128)(2,1)S(1)}, u32[]{:S(2)}, u32[]{:S(2)}) collective-permute-start(bf16[88,576]{1,0:T(8,128)(2,1)S(1)} %get-tuple-element.103), channel_id=1, source_target_pairs={{0,2},{1,3},{2,0},{3,1},{4,6},{5,7},{6,4},{7,5},{8,10},{9,11},{10,... | collective-permute-start | bytes 304136 | tf_op jit(solution)/shard_map/ppermute | solution.py:31
  8.6 8.7 %collective-permute-start.2 = (bf16[88,1152]{1,0:T(8,128)(2,1)S(1)}, bf16[88,1152]{1,0:T(8,128)(2,1)S(1)}, u32[]{:S(2)}, u32[]{:S(2)}) collective-permute-start(bf16[88,1152]{1,0:T(8,128)(2,1)S(1)} %pad_maximum_fusion.6), channel_id=1, source_target_pairs={{0,32},{1,65},{2,34},{3,67},{4,36},{5,69},{6,38},{7,71},{8,40},{9,... | collective-permute-start | bytes 608264 | tf_op jit(solution)/shard_map/ppermute | solution.py:31
  12.0 6.6 %collective-permute-start.1 = (bf16[88,1152]{1,0:T(8,128)(2,1)S(1)}, bf16[88,1152]{1,0:T(8,128)(2,1)S(1)}, u32[]{:S(2)}, u32[]{:S(2)}) collective-permute-start(bf16[88,1152]{1,0:T(8,128)(2,1)S(1)} %pad_maximum_fusion.6), channel_id=1, source_target_pairs={{0,16},{1,3},{2,18},{3,1},{4,20},{5,7},{6,22},{7,5},{8,24},{9,11},... | collective-permute-start | bytes 608264 | tf_op jit(solution)/shard_map/ppermute | solution.py:31
  12.0 7.6 %collective-permute-start.3 = (bf16[88,1152]{1,0:T(8,128)(2,1)S(1)}, bf16[88,1152]{1,0:T(8,128)(2,1)S(1)}, u32[]{:S(2)}, u32[]{:S(2)}) collective-permute-start(bf16[88,1152]{1,0:T(8,128)(2,1)S(1)} %pad_maximum_fusion.6), channel_id=1, source_target_pairs={{0,48},{1,67},{2,50},{3,65},{4,52},{5,71},{6,54},{7,69},{8,56},{9,... | collective-permute-start | bytes 608264 | tf_op jit(solution)/shard_map/ppermute | solution.py:31
  12.5 11.1 %collective-permute-start.8 = (bf16[88,1152]{1,0:T(8,128)(2,1)S(1)}, bf16[88,1152]{1,0:T(8,128)(2,1)S(1)}, u32[]{:S(2)}, u32[]{:S(2)}) collective-permute-start(bf16[88,1152]{1,0:T(8,128)(2,1)S(1)} %pad_maximum_fusion.7), channel_id=1, source_target_pairs={{0,12},{1,13},{2,14},{3,15},{4,8},{5,9},{6,10},{7,11},{8,4},{9,5},... | collective-permute-start | bytes 608264 | tf_op jit(solution)/shard_map/ppermute | solution.py:31
  15.0 8.5 %collective-permute-start.7 = (bf16[88,1152]{1,0:T(8,128)(2,1)S(1)}, bf16[88,1152]{1,0:T(8,128)(2,1)S(1)}, u32[]{:S(2)}, u32[]{:S(2)}) collective-permute-start(bf16[88,1152]{1,0:T(8,128)(2,1)S(1)} %pad_maximum_fusion.7), channel_id=1, source_target_pairs={{0,8},{1,9},{2,10},{3,11},{4,12},{5,13},{6,14},{7,15},{8,0},{9,1},... | collective-permute-start | bytes 608264 | tf_op jit(solution)/shard_map/ppermute | solution.py:31
  17.3 7.0 %collective-permute-start.6 = (bf16[88,1152]{1,0:T(8,128)(2,1)S(1)}, bf16[88,1152]{1,0:T(8,128)(2,1)S(1)}, u32[]{:S(2)}, u32[]{:S(2)}) collective-permute-start(bf16[88,1152]{1,0:T(8,128)(2,1)S(1)} %pad_maximum_fusion.7), channel_id=1, source_target_pairs={{0,4},{1,5},{2,6},{3,7},{4,0},{5,1},{6,2},{7,3},{8,12},{9,13},{10,... | collective-permute-start | bytes 608264 | tf_op jit(solution)/shard_map/ppermute | solution.py:31
  19.7 21.4 %collective-permute-start.11 = (bf16[4,88,1152]{2,1,0:T(8,128)(2,1)S(1)}, bf16[4,88,1152]{2,1,0:T(8,128)(2,1)S(1)}, u32[]{:S(2)}, u32[]{:S(2)}) collective-permute-start(bf16[4,88,1152]{2,1,0:T(8,128)(2,1)S(1)} %pad_maximum_fusion.ta_ref), channel_id=1, source_target_pairs={{0,66},{1,49},{2,64},{3,51},{4,70},{5,53},{6,68},{7,55},{8,74},{9,... | collective-permute-start | bytes 2433032 | tf_op jit(solution)/shard_map/ppermute | solution.py:31
  22.5 18.6 %collective-permute-start.10 = (bf16[4,88,1152]{2,1,0:T(8,128)(2,1)S(1)}, bf16[4,88,1152]{2,1,0:T(8,128)(2,1)S(1)}, u32[]{:S(2)}, u32[]{:S(2)}) collective-permute-start(bf16[4,88,1152]{2,1,0:T(8,128)(2,1)S(1)} %pad_maximum_fusion.ta_ref), channel_id=1, source_target_pairs={{0,64},{1,33},{2,66},{3,35},{4,68},{5,37},{6,70},{7,39},{8,72},{9,... | collective-permute-start | bytes 2433032 | tf_op jit(solution)/shard_map/ppermute | solution.py:31
  24.4 16.7 %collective-permute-start.9 = (bf16[352,1152]{1,0:T(8,128)(2,1)S(1)}, bf16[352,1152]{1,0:T(8,128)(2,1)S(1)}, u32[]{:S(2)}, u32[]{:S(2)}) collective-permute-start(bf16[352,1152]{1,0:T(8,128)(2,1)S(1)} %pad_maximum_fusion.1.im0_ref), channel_id=1, source_target_pairs={{0,1},{1,0},{2,3},{3,2},{4,5},{5,4},{6,7},{7,6},{8,9},{9,8},{10,11... | collective-permute-start | bytes 2433032 | tf_op jit(solution)/shard_map/ppermute | solution.py:31
  26.3 25.0 %collective-permute-start.4 = (bf16[4,88,1152]{2,1,0:T(8,128)(2,1)S(1)}, bf16[4,88,1152]{2,1,0:T(8,128)(2,1)S(1)}, u32[]{:S(2)}, u32[]{:S(2)}) collective-permute-start(bf16[4,88,1152]{2,1,0:T(8,128)(2,1)S(1)} %pad_maximum_fusion.ta_ref), channel_id=1, source_target_pairs={{0,2},{1,17},{2,0},{3,19},{4,6},{5,21},{6,4},{7,23},{8,10},{9,25},... | collective-permute-start | bytes 2433032 | tf_op jit(solution)/shard_map/ppermute | solution.py:31
  49.4 21.2 %collective-permute-start.14 = (bf16[360,1152]{1,0:T(8,128)(2,1)S(1)}, bf16[360,1152]{1,0:T(8,128)(2,1)S(1)}, u32[]{:S(2)}, u32[]{:S(2)}) collective-permute-start(bf16[360,1152]{1,0:T(8,128)(2,1)S(1)} %get-tuple-element.61), channel_id=1, source_target_pairs={{0,64},{1,33},{2,66},{3,35},{4,68},{5,37},{6,70},{7,39},{8,72},{9,... | collective-permute-start | bytes 2488328 | tf_op jit(solution)/shard_map/ppermute | solution.py:31
  54.3 8.6 %collective-permute-start.12 = (f32[8,128]{1,0:T(8,128)S(1)}, f32[8,128]{1,0:T(8,128)S(1)}, u32[]{:S(2)}, u32[]{:S(2)}) collective-permute-start(f32[8,128]{1,0:T(8,128)S(1)} %get-tuple-element.47), channel_id=1, source_target_pairs={{0,16},{1,17},{2,18},{3,19},{4,20},{5,21},{6,22},{7,23},{8,24},{9,... | collective-permute-start | bytes 12296 | tf_op jit(solution)/shard_map/ppermute | solution.py:31
  62.9 3.7 %collective-permute-start.13 = (f32[8,128]{1,0:T(8,128)S(1)}, f32[8,128]{1,0:T(8,128)S(1)}, u32[]{:S(2)}, u32[]{:S(2)}) collective-permute-start(f32[8,128]{1,0:T(8,128)S(1)} %add.25), channel_id=1, source_target_pairs={{0,48},{1,49},{2,50},{3,51},{4,52},{5,53},{6,54},{7,55},{8,56},{9,... | collective-permute-start | bytes 12296 | tf_op jit(solution)/shard_map/ppermute | solution.py:31
  63.2 7.4 %collective-permute-start.15 = (f32[88,1152]{1,0:T(8,128)S(1)}, f32[88,1152]{1,0:T(8,128)S(1)}, u32[]{:S(2)}, u32[]{:S(2)}) collective-permute-start(f32[88,1152]{1,0:T(8,128)S(1)} %get-tuple-element.62), channel_id=1, source_target_pairs={{0,1},{1,0},{2,3},{3,2},{4,5},{5,4},{6,7},{7,6},{8,9},{9,8},{10,11... | collective-permute-start | bytes 1216520 | tf_op jit(solution)/shard_map/ppermute | solution.py:31
  63.2 7.4 %collective-permute-start.16 = (f32[88,1152]{1,0:T(8,128)S(1)}, f32[88,1152]{1,0:T(8,128)S(1)}, u32[]{:S(2)}, u32[]{:S(2)}) collective-permute-start(f32[88,1152]{1,0:T(8,128)S(1)} %get-tuple-element.63), channel_id=1, source_target_pairs={{0,1},{1,0},{2,3},{3,2},{4,5},{5,4},{6,7},{7,6},{8,9},{9,8},{10,11... | collective-permute-start | bytes 1216520 | tf_op jit(solution)/shard_map/ppermute | solution.py:31
  63.7 6.9 %collective-permute-start.17 = (f32[88,1152]{1,0:T(8,128)S(1)}, f32[88,1152]{1,0:T(8,128)S(1)}, u32[]{:S(2)}, u32[]{:S(2)}) collective-permute-start(f32[88,1152]{1,0:T(8,128)S(1)} %get-tuple-element.64), channel_id=1, source_target_pairs={{0,1},{1,0},{2,3},{3,2},{4,5},{5,4},{6,7},{7,6},{8,9},{9,8},{10,11... | collective-permute-start | bytes 1216520 | tf_op jit(solution)/shard_map/ppermute | solution.py:31
  66.5 4.0 %collective-permute-start.18 = (f32[88,1152]{1,0:T(8,128)S(1)}, f32[88,1152]{1,0:T(8,128)S(1)}, u32[]{:S(2)}, u32[]{:S(2)}) collective-permute-start(f32[88,1152]{1,0:T(8,128)S(1)} %get-tuple-element.65), channel_id=1, source_target_pairs={{0,1},{1,0},{2,3},{3,2},{4,5},{5,4},{6,7},{7,6},{8,9},{9,8},{10,11... | collective-permute-start | bytes 1216520 | tf_op jit(solution)/shard_map/ppermute | solution.py:31
  70.6 11.7 %collective-permute-start.19 = (bf16[360,1152]{1,0:T(8,128)(2,1)S(1)}, bf16[360,1152]{1,0:T(8,128)(2,1)S(1)}, u32[]{:S(2)}, u32[]{:S(2)}) collective-permute-start(bf16[360,1152]{1,0:T(8,128)(2,1)S(1)} %get-tuple-element.76), channel_id=1, source_target_pairs={{0,2},{1,17},{2,0},{3,19},{4,6},{5,21},{6,4},{7,23},{8,10},{9,25},... | collective-permute-start | bytes 2488328 | tf_op jit(solution)/shard_map/ppermute | solution.py:31
  70.7 12.9 %collective-permute-start.20 = (bf16[360,1152]{1,0:T(8,128)(2,1)S(1)}, bf16[360,1152]{1,0:T(8,128)(2,1)S(1)}, u32[]{:S(2)}, u32[]{:S(2)}) collective-permute-start(bf16[360,1152]{1,0:T(8,128)(2,1)S(1)} %get-tuple-element.77), channel_id=1, source_target_pairs={{0,66},{1,49},{2,64},{3,51},{4,70},{5,53},{6,68},{7,55},{8,74},{9,... | collective-permute-start | bytes 2488328 | tf_op jit(solution)/shard_map/ppermute | solution.py:31
  72.0 16.6 %collective-permute-start.24 = (bf16[96,1152]{1,0:T(8,128)(2,1)S(1)}, bf16[96,1152]{1,0:T(8,128)(2,1)S(1)}, u32[]{:S(2)}, u32[]{:S(2)}) collective-permute-start(bf16[96,1152]{1,0:T(8,128)(2,1)S(1)} %get-tuple-element.71), channel_id=1, source_target_pairs={{0,4},{1,5},{2,6},{3,7},{4,0},{5,1},{6,2},{7,3},{8,12},{9,13},{10,... | collective-permute-start | bytes 663560 | tf_op jit(solution)/shard_map/ppermute | solution.py:31
  73.2 17.3 %collective-permute-start.25 = (bf16[96,1152]{1,0:T(8,128)(2,1)S(1)}, bf16[96,1152]{1,0:T(8,128)(2,1)S(1)}, u32[]{:S(2)}, u32[]{:S(2)}) collective-permute-start(bf16[96,1152]{1,0:T(8,128)(2,1)S(1)} %get-tuple-element.72), channel_id=1, source_target_pairs={{0,8},{1,9},{2,10},{3,11},{4,12},{5,13},{6,14},{7,15},{8,0},{9,1},... | collective-permute-start | bytes 663560 | tf_op jit(solution)/shard_map/ppermute | solution.py:31
  75.8 14.8 %collective-permute-start.26 = (bf16[96,1152]{1,0:T(8,128)(2,1)S(1)}, bf16[96,1152]{1,0:T(8,128)(2,1)S(1)}, u32[]{:S(2)}, u32[]{:S(2)}) collective-permute-start(bf16[96,1152]{1,0:T(8,128)(2,1)S(1)} %get-tuple-element.73), channel_id=1, source_target_pairs={{0,12},{1,13},{2,14},{3,15},{4,8},{5,9},{6,10},{7,11},{8,4},{9,5},... | collective-permute-start | bytes 663560 | tf_op jit(solution)/shard_map/ppermute | solution.py:31
  86.6 6.1 %collective-permute-start.21 = (bf16[96,1152]{1,0:T(8,128)(2,1)S(1)}, bf16[96,1152]{1,0:T(8,128)(2,1)S(1)}, u32[]{:S(2)}, u32[]{:S(2)}) collective-permute-start(bf16[96,1152]{1,0:T(8,128)(2,1)S(1)} %get-tuple-element.79), channel_id=1, source_target_pairs={{0,16},{1,3},{2,18},{3,1},{4,20},{5,7},{6,22},{7,5},{8,24},{9,11},... | collective-permute-start | bytes 663560 | tf_op jit(solution)/shard_map/ppermute | solution.py:31
  86.7 7.9 %collective-permute-start.22 = (bf16[96,1152]{1,0:T(8,128)(2,1)S(1)}, bf16[96,1152]{1,0:T(8,128)(2,1)S(1)}, u32[]{:S(2)}, u32[]{:S(2)}) collective-permute-start(bf16[96,1152]{1,0:T(8,128)(2,1)S(1)} %get-tuple-element.80), channel_id=1, source_target_pairs={{0,32},{1,65},{2,34},{3,67},{4,36},{5,69},{6,38},{7,71},{8,40},{9,... | collective-permute-start | bytes 663560 | tf_op jit(solution)/shard_map/ppermute | solution.py:31
  88.6 8.6 %collective-permute-start.23 = (bf16[96,1152]{1,0:T(8,128)(2,1)S(1)}, bf16[96,1152]{1,0:T(8,128)(2,1)S(1)}, u32[]{:S(2)}, u32[]{:S(2)}) collective-permute-start(bf16[96,1152]{1,0:T(8,128)(2,1)S(1)} %get-tuple-element.81), channel_id=1, source_target_pairs={{0,48},{1,67},{2,50},{3,65},{4,52},{5,71},{6,54},{7,69},{8,56},{9,... | collective-permute-start | bytes 663560 | tf_op jit(solution)/shard_map/ppermute | solution.py:31
  91.2 7.3 %collective-permute-start.28 = (f32[8,576]{1,0:T(8,128)S(1)}, f32[8,576]{1,0:T(8,128)S(1)}, u32[]{:S(2)}, u32[]{:S(2)}) collective-permute-start(f32[8,576]{1,0:T(8,128)S(1)} %slice.105), channel_id=1, source_target_pairs={{0,64},{1,65},{2,66},{3,67},{4,68},{5,69},{6,70},{7,71},{8,72},{9,... | collective-permute-start | bytes 55304 | tf_op jit(solution)/shard_map/ppermute | solution.py:31
  91.3 7.2 %collective-permute-start.29 = (f32[8,576]{1,0:T(8,128)S(1)}, f32[8,576]{1,0:T(8,128)S(1)}, u32[]{:S(2)}, u32[]{:S(2)}) collective-permute-start(f32[8,576]{1,0:T(8,128)S(1)} %slice.105), channel_id=1, source_target_pairs={{0,66},{1,67},{2,64},{3,65},{4,70},{5,71},{6,68},{7,69},{8,74},{9,... | collective-permute-start | bytes 55304 | tf_op jit(solution)/shard_map/ppermute | solution.py:31
  92.7 5.6 %collective-permute-start.27 = (f32[96,576]{1,0:T(8,128)S(1)}, f32[96,576]{1,0:T(8,128)S(1)}, u32[]{:S(2)}, u32[]{:S(2)}) collective-permute-start(f32[96,576]{1,0:T(8,128)S(1)} %slice.104), channel_id=1, source_target_pairs={{0,2},{1,3},{2,0},{3,1},{4,6},{5,7},{6,4},{7,5},{8,10},{9,11},{10,... | collective-permute-start | bytes 663560 | tf_op jit(solution)/shard_map/ppermute | solution.py:31
  99.0 6.4 %collective-permute-start.30 = (f32[360,288]{0,1:T(8,128)S(1)}, f32[360,288]{0,1:T(8,128)S(1)}, u32[]{:S(2)}, u32[]{:S(2)}) collective-permute-start(f32[360,288]{0,1:T(8,128)S(1)} %copy.17), channel_id=1, source_target_pairs={{0,1},{1,0},{2,3},{3,2},{4,5},{5,4},{6,7},{7,6},{8,9},{9,8},{10,11... | collective-permute-start | bytes 1244168 | tf_op jit(solution)/shard_map/ppermute | solution.py:31

commit v8 on v5

--- a/solution.py
+++ b/solution.py
@@ -100,45 +100,36 @@
     return lax.dot_general(coeff_low[...], t_rel[...], (((0,), (0,)), ((), ())), preferred_element_type=F32)
 
 
-def far_kernel(
+def near_kernel(
     rows, half, feats, info_ref, scale_ref, ta_ref, tb_ref, im0_ref, im1_ref,
-    ma_ref, mb_ref, acc_ref, sums_ref, images, t_rel, coeff_low, grads,
+    own_ref, m_ref, acc_ref, sums_ref, images, t_rel, coeff_low, grads,
 ):
     quarter = 4 * rows
     images[0:quarter, :] = im0_ref[...]
     images[quarter : 2 * quarter, :] = im1_ref[...]
     pairs(info_ref, rows, half, ta_ref, tb_ref, t_rel)
-    sums_ref[...] = coefficients(False, rows, info_ref, scale_ref, t_rel, images, coeff_low)
+    sums_ref[...] = coefficients(True, rows, info_ref, scale_ref, t_rel, images, coeff_low)
     text_parts(info_ref, rows, half, coeff_low, images, grads)
-    for k, m_ref in ((0, ma_ref), (1, mb_ref)):
-        m_ref[...] = message([grads[k, i] for i in range(4)], feats)
+    own_ref[...] = jnp.concatenate([grads[0, i] for i in range(4)], axis=0)
+    m_ref[...] = message([grads[1, i] for i in range(4)], feats)
     acc_ref[...] = image_parts(coeff_low, t_rel)
 
 
-def near_first_kernel(
-    rows, half, feats, info_ref, scale_ref, ta_ref, tb_ref, im0_ref, im1_ref, sums_before,
-    images, t_rel, coeff_low, sums_ref,
+def far_kernel(
+    rows, half, feats, info_ref, scale_ref, ta_ref, tb_ref, im0_ref, im1_ref, before_ref, sums_before,
+    ma_ref, mb_ref, own_ref, other_ref, sums_ref, images, t_rel, coeff_low, grads,
 ):
     quarter = 4 * rows
     images[0:quarter, :] = im0_ref[...]
     images[quarter : 2 * quarter, :] = im1_ref[...]
     pairs(info_ref, rows, half, ta_ref, tb_ref, t_rel)
-    sums = coefficients(True, rows, info_ref, scale_ref, t_rel, images, coeff_low)
-    sums_ref[...] = sums + sums_before[...]
-
-
-def near_last_kernel(
-    rows, half, feats, info_ref, images, t_rel, coeff_low, before_ref, own_ref, m_ref, img0_ref, *refs,
-):
-    others, grads = refs[:4], refs[4]
-    quarter = 4 * rows
+    sums_ref[...] = coefficients(False, rows, info_ref, scale_ref, t_rel, images, coeff_low) + sums_before[...]
     text_parts(info_ref, rows, half, coeff_low, images, grads)
-    own_ref[...] = jnp.concatenate([grads[0, i] for i in range(4)], axis=0)
-    m_ref[...] = message([grads[1, i] for i in range(4)], feats)
+    for k, m_ref in ((0, ma_ref), (1, mb_ref)):
+        m_ref[...] = message([grads[k, i] for i in range(4)], feats)
     acc = image_parts(coeff_low, t_rel) + before_ref[...]
-    img0_ref[...] = acc[0:quarter]
-    for k, img_ref in enumerate(others):
-        img_ref[...] = acc[quarter + k * rows : quarter + (k + 1) * rows]
+    own_ref[...] = acc[0:quarter]
+    other_ref[...] = acc[quarter : 2 * quarter]
 
 
 def message(blocks, feats, extra=()):
@@ -160,23 +151,11 @@
     return [hi, mid, v - hi - mid]
 
 
-def image_first_kernel(rows, feats, own_ref, *refs):
-    others, (out_ref, *messages) = refs[:4], refs[4:]
-    out_ref[...] = own_ref[0:rows] + others[0][...]
+def image_first_kernel(rows, feats, own_ref, other_ref, out_ref, *messages):
+    total = own_ref[...] + other_ref[...]
+    out_ref[...] = total[0:rows]
     for i, m_ref in enumerate(messages):
-        m_ref[...] = message([own_ref[(i + 1) * rows : (i + 2) * rows] + others[i + 1][...]], feats)
-
-
-def text_far_kernel(own_ref, r2_ref, out_ref):
-    out_ref[...] = own_ref[...] + decoded(r2_ref)[0]
-
-
-def text_first_kernel(rows, feats, own_ref, r1_ref, r3_ref, sums_ref, out_ref, *messages):
-    total = own_ref[...] + decoded(r1_ref)[0] + decoded(r3_ref)[0]
-    out_ref[...] = total[0:rows]
-    scalars = [jnp.concatenate([v] * (feats // 128), axis=1) for v in split3(sums_ref[0:1, :])]
-    for i, m_ref in enumerate(messages):
-        m_ref[...] = message([total[(i + 1) * rows : (i + 2) * rows]], feats, scalars)
+        m_ref[...] = message([total[(i + 1) * rows : (i + 2) * rows]], feats)
 
 
 def image_last_kernel(scale_ref, own_ref, r1_ref, r2_ref, r3_ref, out_ref):
@@ -186,7 +165,19 @@
     out_ref[...] = total * scale_ref[0]
 
 
-def text_last_kernel(rows, feats, scale_ref, own_ref, sums_ref, r1_ref, r2_ref, r3_ref, out_ref):
+def text_near_kernel(own_ref, r1_ref, out_ref):
+    out_ref[...] = own_ref[...] + decoded(r1_ref)[0]
+
+
+def text_first_kernel(rows, feats, own_ref, r2_ref, r3_ref, sums_ref, out_ref, *messages):
+    total = own_ref[...] + decoded(r2_ref)[0] + decoded(r3_ref)[0]
+    out_ref[...] = total[0:rows]
+    scalars = [jnp.concatenate([v] * (feats // 128), axis=1) for v in split3(sums_ref[0:1, :])]
+    for i, m_ref in enumerate(messages):
+        m_ref[...] = message([total[(i + 1) * rows : (i + 2) * rows]], feats, scalars)
+
+
+def text_last_kernel(feats, scale_ref, own_ref, sums_ref, r1_ref, r2_ref, r3_ref, out_ref):
     total, tails = own_ref[...], []
     for r in (r1_ref, r2_ref, r3_ref):
         value, tail = decoded(r)
@@ -230,9 +221,10 @@
     first = [packed] + [swap(packed, y_mask(i), z_mask(i)) for i in range(1, 4)]
     image = jnp.concatenate([keep, swap(send, z_mask(1))], axis=1)
     stack = jnp.stack(first)
-    second = [stack] + [swap(stack, z_mask(j), y_mask(j)) for j in range(1, 4)]
+    second1, second3 = (swap(stack, z_mask(j), y_mask(j)) for j in (1, 3))
     images_own = jnp.concatenate([image] + [swap(image, x_mask(k)) for k in range(1, 4)], axis=0)
     images_other = swap(images_own, CORE)
+    second2 = swap(after(stack, images_own), z_mask(2), y_mask(2))
 
     def f32(*shape):
         return jax.ShapeDtypeStruct(shape, F32)
@@ -240,7 +232,7 @@
     def bf16(*shape):
         return jax.ShapeDtypeStruct(shape, BF)
 
-    def call(kernel, name, out_shape, *args, scalars=0, scratch=(), mib=20, products=0):
+    def call(kernel, name, out_shape, *args, scalars=0, scratch=(), mib=20, products=0, brief=False):
         return pl.pallas_call(
             kernel,
             out_shape=out_shape,
@@ -250,7 +242,7 @@
             compiler_params=grant(mib),
             cost_estimate=pl.CostEstimate(
                 flops=products * 2 * quarter * 2 * quarter * 2 * feats,
-                bytes_accessed=sum(a.size * a.dtype.itemsize for a in (*args, *out_shape)),
+                bytes_accessed=0 if brief else sum(a.size * a.dtype.itemsize for a in (*args, *out_shape)),
                 transcendentals=products * 4 * quarter * quarter,
             ),
             name=name,
@@ -261,58 +253,53 @@
     scales = jnp.stack([scaling, logit_offset_term[0]])
     images_shape, coeff_shape = (2 * quarter, feats), (2 * quarter, 2 * quarter)
     grads = pltpu.VMEM((2, 4, rows, feats), F32)
-    m2, m3, acc, sums = call(
+    scratch = [pltpu.VMEM(images_shape, BF), pltpu.VMEM(images_shape, BF), pltpu.VMEM(coeff_shape, BF), grads]
+    text, m1, acc, sums = call(
+        functools.partial(near_kernel, *sizes), "tile_near",
+        [f32(quarter, feats), bf16(quarter + 8, feats), f32(*images_shape), f32(8, 128)],
+        info, scales, stack, second1, images_own, images_other,
+        scalars=2, mib=40, products=3, scratch=scratch,
+    )
+    m2, m3, img_own, img_other, sums = call(
         functools.partial(far_kernel, *sizes), "tile_far",
-        [bf16(quarter + 8, feats), bf16(quarter + 8, feats), f32(*images_shape), f32(8, 128)],
-        info, scales, second[2], second[3], images_own, images_other,
-        scalars=2, mib=40, products=3,
-        scratch=[pltpu.VMEM(images_shape, BF), pltpu.VMEM(images_shape, BF), pltpu.VMEM(coeff_shape, BF), grads],
-    )
-    images, t_rel, coeff_low, sums = call(
-        functools.partial(near_first_kernel, *sizes), "tile_near_first",
-        [bf16(*images_shape), bf16(*images_shape), bf16(*coeff_shape), f32(8, 128)],
-        info, scales, second[0], second[1], images_own, images_other, sums,
-        scalars=2, mib=30, products=1,
-    )
-    text, m1, img_own, *img_others = call(
-        functools.partial(near_last_kernel, *sizes), "tile_near_last",
-        [f32(quarter, feats), bf16(quarter + 8, feats), f32(quarter, feats)] + [f32(rows, feats)] * 4,
-        info, images, t_rel, coeff_low, acc,
-        scalars=1, mib=30, products=2, scratch=[grads],
-    )
-
-    one = sums + swap(sums, x_mask(1))
-    got2 = swap(m2, z_mask(2), y_mask(2))
-    m1, m3, img_others, one, got2 = lax.optimization_barrier((m1, m3, img_others, one, got2))
-    got1, got3 = swap(m1, z_mask(1), y_mask(1)), swap(m3, z_mask(3), y_mask(3))
+        [bf16(quarter + 8, feats), bf16(quarter + 8, feats), f32(quarter, feats), f32(quarter, feats), f32(8, 128)],
+        info, scales, second2, second3, images_own, images_other, acc, sums,
+        scalars=2, mib=40, products=3, scratch=scratch,
+    )
+    got1 = swap(m1, z_mask(1), y_mask(1))
+    m2, m3, img_other, sums, got1 = lax.optimization_barrier((m2, m3, img_other, sums, got1))
+    got2, got3 = swap(m2, z_mask(2), y_mask(2)), swap(m3, z_mask(3), y_mask(3))
+    one = swap(sums, x_mask(1))
     img, *messages = call(
         functools.partial(image_first_kernel, rows, feats), "image_first",
-        [f32(rows, feats)] + [bf16(rows + 8, feats)] * 3, img_own, *[swap(part, CORE) for part in img_others],
-    )
-    sums = one
-    for mask in ((x_mask(3),), (z_mask(1), y_mask(1)), (z_mask(3), y_mask(3))):
-        sums = sums + swap(sums, *mask)
+        [f32(rows, feats)] + [bf16(rows + 8, feats)] * 3, img_own, swap(img_other, CORE),
+    )
+    *messages, one = lax.optimization_barrier((*messages, one))
+    two = sums + one
+    four = two + swap(two, x_mask(3))
     img_got = [swap(m, x_mask(k)) for k, m in zip((1, 2, 3), messages)]
-    (far,) = call(text_far_kernel, "text_far", [f32(quarter, feats)], after(text, *messages), got2)
+    (text,) = call(text_near_kernel, "text_near", [f32(quarter, feats)], after(text, *messages, four), got1, products=3)
+    s1, s2, s3 = (after(swap(four, z_mask(k), y_mask(k)), got2, got3) for k in (1, 2, 3))
+    sums = (four + s1) + (s2 + s3)
     text, *messages = call(
         functools.partial(text_first_kernel, rows, feats), "text_first",
-        [f32(rows, feats)] + [bf16(rows + 8, feats)] * 3, far, got1, got3, sums,
+        [f32(rows, feats)] + [bf16(rows + 8, feats)] * 3, text, got2, got3, sums, brief=True,
     )
     got = [swap(m, y_mask(i), z_mask(i)) for i, m in zip((1, 2, 3), messages)]
 
-    (img,) = call(image_last_kernel, "image_last", [f32(rows, feats)], logit_scaler, img, *img_got, scalars=1)
-    image = jnp.concatenate(by(lo0, img[:, :half], swap(img[:, half:], z_mask(1))), axis=0)
+    img_got[0] = after(img_got[0], text)
+    (img,) = call(image_last_kernel, "image_last", [f32(rows, feats)], logit_scaler, img, *img_got, scalars=1, products=3)
     (text,) = call(
-        functools.partial(text_last_kernel, rows, feats), "text_last", [f32(rows + 8, feats)],
-        logit_scaler, after(text, image), sums, *got, scalars=1,
-    )
+        functools.partial(text_last_kernel, feats), "text_last", [f32(rows + 8, feats)],
+        logit_scaler, text, sums, *got, scalars=1, products=4,
+    )
+    image = jnp.concatenate(by(lo0, img[:, :half], after(swap(img[:, half:], z_mask(1)), text)), axis=0)
     whole = jnp.concatenate([text[:rows, :half], text[:rows, half:], image, text[rows:, :half]], axis=0)
     mine, other = by(on0, whole[:, :width], whole[:, width:])
     other = swap(other, CORE)
     text_grad = jnp.concatenate(by(on0, mine[:step], other[:step]), axis=0)
     image_grad = jnp.concatenate(by(on0, mine[step : 2 * step], other[step : 2 * step]), axis=0)
-    scalar_grads = mine[2 * step, :2] + other[2 * step, :2]
-    return (image_grad, text_grad, scalar_grads)
+    return (image_grad, text_grad, mine[2 * step, :2] + other[2 * step, :2])
 
 
 def solution(mesh):

time: 111 us -> 108 us (0.973)
  starting transfers between devices: 42.9 us -> 39.6 us
  waiting for transfers between devices: 35 us -> 36.9 us
    ppermute x31 -> x29, starting transfers between devices: 42.9 us -> 39.6 us  [swap(): lax.ppermute(array, AXES, [(i, i ^ (mask1 if i & 1 else mask0)) for i in...]
    ppermute x31 -> x29, waiting for transfers between devices: 35 us -> 36.9 us  [swap(): lax.ppermute(array, AXES, [(i, i ^ (mask1 if i & 1 else mask0)) for i in...]
    pallas_call x8 -> x7, Pallas kernels: 22.4 us -> 21.5 us  [call(): pl.pallas_call(kernel, out_shape=out_shape, in_specs=[SMEM] * scalars + [...]
  transfers between devices with their start and end apart: 31 -> 29, of which waited for: 17 -> 15; matrix products, arithmetic and copies ran while one was open for 1% -> 1% of each run, Pallas kernels for 20% -> 20%
where the time goes in v8:
time: 108 us
  starting transfers between devices  39.6 us (37%)
  waiting for transfers between devices  36.9 us (34%)
  Pallas kernels  21.5 us (20%)
  local copies, waits for them, and re-layouts  5.72 us (5%)
  between operations  2.19 us (2%)
  other arithmetic  2.1 us (2%)
    ppermute x29, starting transfers between devices, swap(): lax.ppermute(array, AXES, [(i, i ^ (mask1 if i & 1 else mask0)) for i in...  39.6 us
    ppermute x29, waiting for transfers between devices, swap(): lax.ppermute(array, AXES, [(i, i ^ (mask1 if i & 1 else mask0)) for i in...  36.9 us
    pallas_call x7, Pallas kernels, call(): pl.pallas_call(kernel, out_shape=out_shape, in_specs=[SMEM] * scalars + [...  21.5 us
    unnamed x11, local copies, waits for them, and re-layouts  2.99 us
  transfers between devices with their start and end apart: 29, of which 15 were waited for; matrix products, arithmetic and copies ran while one was open for 1% of the time, Pallas kernels for 20%

profile of v8, /device:TPU:1, one launch (start us, length us, event | category | flops | bytes accessed | tf_op | source)
XLA Modules:
  0.0 108.0 jit_solution(5616799568419497597)
XLA Ops:
  0.6 1.1 %fusion.6 = (bf16[176,288]{0,1:T(8,128)(2,1)S(1)}, bf16[176,288]{0,1:T(8,128)(2,1)S(1)}) fusion(bf16[352,288]{0,1:T(8,128)(2,1)} %param.4), kind=kLoop, calls=%fused_computation.42 | loop fusion | bytes 405504 | tf_op jit(solution)/shard_map/slice | solution.py:215
  2.0 1.1 %fusion.5 = (bf16[176,288]{0,1:T(8,128)(2,1)S(1)}, bf16[176,288]{0,1:T(8,128)(2,1)S(1)}) fusion(bf16[352,288]{0,1:T(8,128)(2,1)} %param.5), kind=kLoop, calls=%fused_computation.41 | loop fusion | bytes 405504 | tf_op jit(solution)/shard_map/slice | solution.py:215
  3.5 1.5 %collective-permute-start = (bf16[352,288]{1,0:T(8,128)(2,1)S(1)}, bf16[352,288]{1,0:T(8,128)(2,1)S(1)}, u32[]{:S(2)}, u32[]{:S(2)}) collective-permute-start(bf16[352,288]{1,0:T(8,128)(2,1)S(1)} %broadcast_select_fusion.2), channel_id=1, source_target_pairs={{0,1},{1,0},{2,3},{3,2},{4,5},{5,4},{6,7},{7,6},{8,9},{9,8},{10,11... | collective-permute-start | bytes 608264 | tf_op jit(solution)/shard_map/ppermute | solution.py:31
  5.0 1.2 %collective-permute-done = bf16[352,288]{1,0:T(8,128)(2,1)S(1)} collective-permute-done((bf16[352,288]{1,0:T(8,128)(2,1)S(1)}, bf16[352,288]{1,0:T(8,128)(2,1)S(1)}, u32[]{:S(2)}, u32[]{:S(2)}) %collective-permute-start) | collective-permute-done | bytes 202784 | tf_op jit(solution)/shard_map/ppermute | solution.py:31
  6.6 1.8 %collective-permute-start.5 = (bf16[88,576]{1,0:T(8,128)(2,1)S(1)}, bf16[88,576]{1,0:T(8,128)(2,1)S(1)}, u32[]{:S(2)}, u32[]{:S(2)}) collective-permute-start(bf16[88,576]{1,0:T(8,128)(2,1)S(1)} %get-tuple-element.87), channel_id=1, source_target_pairs={{0,2},{1,3},{2,0},{3,1},{4,6},{5,7},{6,4},{7,5},{8,10},{9,11},{10,... | collective-permute-start | bytes 304136 | tf_op jit(solution)/shard_map/ppermute | solution.py:31
  8.6 3.4 %collective-permute-start.2 = (bf16[88,1152]{1,0:T(8,128)(2,1)S(1)}, bf16[88,1152]{1,0:T(8,128)(2,1)S(1)}, u32[]{:S(2)}, u32[]{:S(2)}) collective-permute-start(bf16[88,1152]{1,0:T(8,128)(2,1)S(1)} %pad_maximum_fusion.6), channel_id=1, source_target_pairs={{0,32},{1,65},{2,34},{3,67},{4,36},{5,69},{6,38},{7,71},{8,40},{9,... | collective-permute-start | bytes 608264 | tf_op jit(solution)/shard_map/ppermute | solution.py:31
  12.0 0.4 collective-permute-start.3
  12.5 2.6 %collective-permute-start.8 = (bf16[88,1152]{1,0:T(8,128)(2,1)S(1)}, bf16[88,1152]{1,0:T(8,128)(2,1)S(1)}, u32[]{:S(2)}, u32[]{:S(2)}) collective-permute-start(bf16[88,1152]{1,0:T(8,128)(2,1)S(1)} %pad_maximum_fusion.7), channel_id=1, source_target_pairs={{0,12},{1,13},{2,14},{3,15},{4,8},{5,9},{6,10},{7,11},{8,4},{9,5},... | collective-permute-start | bytes 608264 | tf_op jit(solution)/shard_map/ppermute | solution.py:31
  15.0 0.5 collective-permute-start.7
  15.5 1.8 %collective-permute-done.2 = bf16[88,1152]{1,0:T(8,128)(2,1)S(1)} collective-permute-done((bf16[88,1152]{1,0:T(8,128)(2,1)S(1)}, bf16[88,1152]{1,0:T(8,128)(2,1)S(1)}, u32[]{:S(2)}, u32[]{:S(2)}) %collective-permute-start.2) | collective-permute-done | bytes 202784 | tf_op jit(solution)/shard_map/ppermute | solution.py:31
  17.3 1.2 %collective-permute-start.6 = (bf16[88,1152]{1,0:T(8,128)(2,1)S(1)}, bf16[88,1152]{1,0:T(8,128)(2,1)S(1)}, u32[]{:S(2)}, u32[]{:S(2)}) collective-permute-start(bf16[88,1152]{1,0:T(8,128)(2,1)S(1)} %pad_maximum_fusion.7), channel_id=1, source_target_pairs={{0,4},{1,5},{2,6},{3,7},{4,0},{5,1},{6,2},{7,3},{8,12},{9,13},{10,... | collective-permute-start | bytes 608264 | tf_op jit(solution)/shard_map/ppermute | solution.py:31
  18.5 1.0 collective-permute-done.3
  19.7 1.4 %collective-permute-start.4 = (bf16[4,88,1152]{2,1,0:T(8,128)(2,1)S(1)}, bf16[4,88,1152]{2,1,0:T(8,128)(2,1)S(1)}, u32[]{:S(2)}, u32[]{:S(2)}) collective-permute-start(bf16[4,88,1152]{2,1,0:T(8,128)(2,1)S(1)} %pad_maximum_fusion.ta_ref), channel_id=1, source_target_pairs={{0,2},{1,17},{2,0},{3,19},{4,6},{5,21},{6,4},{7,23},{8,10},{9,25},... | collective-permute-start | bytes 2433032 | tf_op jit(solution)/shard_map/ppermute | solution.py:31
  21.1 2.5 %collective-permute-done.8 = bf16[88,1152]{1,0:T(8,128)(2,1)S(1)} collective-permute-done((bf16[88,1152]{1,0:T(8,128)(2,1)S(1)}, bf16[88,1152]{1,0:T(8,128)(2,1)S(1)}, u32[]{:S(2)}, u32[]{:S(2)}) %collective-permute-start.8) | collective-permute-done | bytes 202784 | tf_op jit(solution)/shard_map/ppermute | solution.py:31
  23.6 0.8 collective-permute-done.6
  24.4 1.9 %collective-permute-start.9 = (bf16[352,1152]{1,0:T(8,128)(2,1)S(1)}, bf16[352,1152]{1,0:T(8,128)(2,1)S(1)}, u32[]{:S(2)}, u32[]{:S(2)}) collective-permute-start(bf16[352,1152]{1,0:T(8,128)(2,1)S(1)} %pad_maximum_fusion.1.im0_ref), channel_id=1, source_target_pairs={{0,1},{1,0},{2,3},{3,2},{4,5},{5,4},{6,7},{7,6},{8,9},{9,8},{10,11... | collective-permute-start | bytes 2433032 | tf_op jit(solution)/shard_map/ppermute | solution.py:31
  27.8 2.7 %collective-permute-start.11 = (bf16[4,88,1152]{2,1,0:T(8,128)(2,1)S(1)}, bf16[4,88,1152]{2,1,0:T(8,128)(2,1)S(1)}, u32[]{:S(2)}, u32[]{:S(2)}) collective-permute-start(bf16[4,88,1152]{2,1,0:T(8,128)(2,1)S(1)} %pad_maximum_fusion.ta_ref), channel_id=1, source_target_pairs={{0,66},{1,49},{2,64},{3,51},{4,70},{5,53},{6,68},{7,55},{8,74},{9,... | collective-permute-start | bytes 2433032 | tf_op jit(solution)/shard_map/ppermute | solution.py:31
  31.2 7.2 %tile_near.1 = (f32[352,1152]{1,0:T(8,128)S(1)}, bf16[360,1152]{1,0:T(8,128)(2,1)S(1)}, f32[704,1152]{1,0:T(8,128)S(1)}, f32[8,128]{1,0:T(8,128)S(1)}) custom-call(s32[2]{0:T(128)S(1)} %pad_add_fusion.info_ref, f32[2]{0:T(128)S(1)} %pad_maximum_fusion.9.scale_ref, bf16[4,88,1152]{2,1,0:T(8,128)(2,1)S(1)} %pad_maximum_fusion.ta_ref, ...), custom_call_target="tpu_custom_call" | custom-call | flops 3425697792 | bytes 8943632 | tf_op jit(solution)/shard_map/tile_near/pallas_call | solution.py:236
  38.4 1.3 %collective-permute-start.12 = (bf16[360,1152]{1,0:T(8,128)(2,1)S(1)}, bf16[360,1152]{1,0:T(8,128)(2,1)S(1)}, u32[]{:S(2)}, u32[]{:S(2)}) collective-permute-start(bf16[360,1152]{1,0:T(8,128)(2,1)S(1)} %get-tuple-element.45), channel_id=1, source_target_pairs={{0,2},{1,17},{2,0},{3,19},{4,6},{5,21},{6,4},{7,23},{8,10},{9,25},... | collective-permute-start | bytes 2488328 | tf_op jit(solution)/shard_map/ppermute | solution.py:31
  39.7 9.4 %collective-permute-done.11.tb_ref = bf16[4,88,1152]{2,1,0:T(8,128)(2,1)S(1)} collective-permute-done((bf16[4,88,1152]{2,1,0:T(8,128)(2,1)S(1)}, bf16[4,88,1152]{2,1,0:T(8,128)(2,1)S(1)}, u32[]{:S(2)}, u32[]{:S(2)}) %collective-permute-start.11) | collective-permute-done | bytes 811040 | tf_op jit(solution)/shard_map/ppermute | solution.py:31
  49.1 8.4 %tile_far.1 = (bf16[360,1152]{1,0:T(8,128)(2,1)S(1)}, bf16[360,1152]{1,0:T(8,128)(2,1)S(1)}, f32[352,1152]{1,0:T(8,128)S(1)}, f32[352,1152]{1,0:T(8,128)S(1)}, f32[8,128]{1,0:T(8,128)S(1)}) custom-call(s32[2]{0:T(128)S(1)} %pad_add_fusion.info_ref, f32[2]{0:T(128)S(1)} %pad_maximum_fusion.9.scale_ref, ...), custom_call_target="tpu_custom_call" | custom-call | flops 3425697792 | bytes 11399184 | tf_op jit(solution)/shard_map/tile_far/pallas_call | solution.py:236
  57.5 0.9 collective-permute-start.13
  58.4 2.9 %collective-permute-start.16 = (bf16[360,1152]{1,0:T(8,128)(2,1)S(1)}, bf16[360,1152]{1,0:T(8,128)(2,1)S(1)}, u32[]{:S(2)}, u32[]{:S(2)}) collective-permute-start(bf16[360,1152]{1,0:T(8,128)(2,1)S(1)} %get-tuple-element.57), channel_id=1, source_target_pairs={{0,64},{1,33},{2,66},{3,35},{4,68},{5,37},{6,70},{7,39},{8,72},{9,... | collective-permute-start | bytes 2488328 | tf_op jit(solution)/shard_map/ppermute | solution.py:31
  61.3 0.8 collective-permute-start.17
  62.1 1.2 %collective-permute-start.14 = (f32[8,128]{1,0:T(8,128)S(1)}, f32[8,128]{1,0:T(8,128)S(1)}, u32[]{:S(2)}, u32[]{:S(2)}) collective-permute-start(f32[8,128]{1,0:T(8,128)S(1)} %get-tuple-element.50), channel_id=1, source_target_pairs={{0,4},{1,5},{2,6},{3,7},{4,0},{5,1},{6,2},{7,3},{8,12},{9,13},{10,... | collective-permute-start | bytes 12296 | tf_op jit(solution)/shard_map/ppermute | solution.py:31
  63.3 0.9 image_first.1
  64.3 0.6 collective-permute-done.14
  64.9 2.5 %collective-permute-start.15 = (f32[8,128]{1,0:T(8,128)S(1)}, f32[8,128]{1,0:T(8,128)S(1)}, u32[]{:S(2)}, u32[]{:S(2)}) collective-permute-start(f32[8,128]{1,0:T(8,128)S(1)} %add.25), channel_id=1, source_target_pairs={{0,12},{1,13},{2,14},{3,15},{4,8},{5,9},{6,10},{7,11},{8,4},{9,5},... | collective-permute-start | bytes 12296 | tf_op jit(solution)/shard_map/ppermute | solution.py:31
  67.3 1.5 %collective-permute-done.15 = f32[8,128]{1,0:T(8,128)S(1)} collective-permute-done((f32[8,128]{1,0:T(8,128)S(1)}, f32[8,128]{1,0:T(8,128)S(1)}, u32[]{:S(2)}, u32[]{:S(2)}) %collective-permute-start.15) | collective-permute-done | bytes 4128 | tf_op jit(solution)/shard_map/ppermute | solution.py:31
  68.8 1.9 %collective-permute-start.20 = (f32[8,128]{1,0:T(8,128)S(1)}, f32[8,128]{1,0:T(8,128)S(1)}, u32[]{:S(2)}, u32[]{:S(2)}) collective-permute-start(f32[8,128]{1,0:T(8,128)S(1)} %add.26), channel_id=1, source_target_pairs={{0,66},{1,49},{2,64},{3,51},{4,70},{5,53},{6,68},{7,55},{8,74},{9,... | collective-permute-start | bytes 12296 | tf_op jit(solution)/shard_map/ppermute | solution.py:31
  70.7 1.4 %collective-permute-start.18 = (f32[8,128]{1,0:T(8,128)S(1)}, f32[8,128]{1,0:T(8,128)S(1)}, u32[]{:S(2)}, u32[]{:S(2)}) collective-permute-start(f32[8,128]{1,0:T(8,128)S(1)} %add.26), channel_id=1, source_target_pairs={{0,2},{1,17},{2,0},{3,19},{4,6},{5,21},{6,4},{7,23},{8,10},{9,25},... | collective-permute-start | bytes 12296 | tf_op jit(solution)/shard_map/ppermute | solution.py:31
  72.1 0.8 text_near.1.own_ref
  72.9 7.5 %collective-permute-done.17.r3_ref = bf16[360,1152]{1,0:T(8,128)(2,1)S(1)} collective-permute-done((bf16[360,1152]{1,0:T(8,128)(2,1)S(1)}, bf16[360,1152]{1,0:T(8,128)(2,1)S(1)}, u32[]{:S(2)}, u32[]{:S(2)}) %collective-permute-start.17) | collective-permute-done | bytes 829472 | tf_op jit(solution)/shard_map/ppermute | solution.py:31
  80.4 2.7 %collective-permute-start.25 = (bf16[96,1152]{1,0:T(8,128)(2,1)S(1)}, bf16[96,1152]{1,0:T(8,128)(2,1)S(1)}, u32[]{:S(2)}, u32[]{:S(2)}) collective-permute-start(bf16[96,1152]{1,0:T(8,128)(2,1)S(1)} %get-tuple-element.52), channel_id=1, source_target_pairs={{0,8},{1,9},{2,10},{3,11},{4,12},{5,13},{6,14},{7,15},{8,0},{9,1},... | collective-permute-start | bytes 663560 | tf_op jit(solution)/shard_map/ppermute | solution.py:31
  83.2 0.9 collective-permute-start.26
  84.1 3.0 %text_first.1 = (f32[88,1152]{1,0:T(8,128)S(1)}, bf16[96,1152]{1,0:T(8,128)(2,1)S(1)}, bf16[96,1152]{1,0:T(8,128)(2,1)S(1)}, bf16[96,1152]{1,0:T(8,128)(2,1)S(1)}) custom-call(f32[352,1152]{1,0:T(8,128)S(1)} %text_near.1.own_ref, bf16[360,1152]{1,0:T(8,128)(2,1)S(1)} %collective-permute-done.16.r2_ref, bf16[360,1152]{1,0:T(8,128)(2,1)S(1)} %collective-permute-done.17.r3_ref, ...), custom_call_target="tpu_custom_call" | custom-call | tf_op jit(solution)/shard_map/text_first/pallas_call | solution.py:236
  87.1 3.6 %collective-permute-start.22 = (bf16[96,1152]{1,0:T(8,128)(2,1)S(1)}, bf16[96,1152]{1,0:T(8,128)(2,1)S(1)}, u32[]{:S(2)}, u32[]{:S(2)}) collective-permute-start(bf16[96,1152]{1,0:T(8,128)(2,1)S(1)} %get-tuple-element.64), channel_id=1, source_target_pairs={{0,32},{1,65},{2,34},{3,67},{4,36},{5,69},{6,38},{7,71},{8,40},{9,... | collective-permute-start | bytes 663560 | tf_op jit(solution)/shard_map/ppermute | solution.py:31
  91.0 3.1 %collective-permute-done.26.r3_ref = bf16[96,1152]{1,0:T(8,128)(2,1)S(1)} collective-permute-done((bf16[96,1152]{1,0:T(8,128)(2,1)S(1)}, bf16[96,1152]{1,0:T(8,128)(2,1)S(1)}, u32[]{:S(2)}, u32[]{:S(2)}) %collective-permute-start.26) | collective-permute-done | bytes 221216 | tf_op jit(solution)/shard_map/ppermute | solution.py:31
  94.0 0.6 image_last.1
  94.9 1.9 %collective-permute-done.22.r2_ref = bf16[96,1152]{1,0:T(8,128)(2,1)S(1)} collective-permute-done((bf16[96,1152]{1,0:T(8,128)(2,1)S(1)}, bf16[96,1152]{1,0:T(8,128)(2,1)S(1)}, u32[]{:S(2)}, u32[]{:S(2)}) %collective-permute-start.22) | collective-permute-done | bytes 221216 | tf_op jit(solution)/shard_map/ppermute | solution.py:31
  96.8 2.3 %collective-permute-done.23.r3_ref = bf16[96,1152]{1,0:T(8,128)(2,1)S(1)} collective-permute-done((bf16[96,1152]{1,0:T(8,128)(2,1)S(1)}, bf16[96,1152]{1,0:T(8,128)(2,1)S(1)}, u32[]{:S(2)}, u32[]{:S(2)}) %collective-permute-start.23) | collective-permute-done | bytes 221216 | tf_op jit(solution)/shard_map/ppermute | solution.py:31
  99.1 0.6 text_last.1
  99.9 1.6 %collective-permute-done.27 = f32[88,576]{1,0:T(8,128)S(1)} collective-permute-done((f32[88,576]{1,0:T(8,128)S(1)}, f32[88,576]{1,0:T(8,128)S(1)}, u32[]{:S(2)}, u32[]{:S(2)}) %collective-permute-start.27) | collective-permute-done | bytes 202784 | tf_op jit(solution)/shard_map/ppermute | solution.py:31
  102.0 1.4 %collective-permute-start.28 = (f32[360,288]{0,1:T(8,128)S(1)}, f32[360,288]{0,1:T(8,128)S(1)}, u32[]{:S(2)}, u32[]{:S(2)}) collective-permute-start(f32[360,288]{0,1:T(8,128)S(1)} %copy.17), channel_id=1, source_target_pairs={{0,1},{1,0},{2,3},{3,2},{4,5},{5,4},{6,7},{7,6},{8,9},{9,8},{10,11... | collective-permute-start | bytes 1244168 | tf_op jit(solution)/shard_map/ppermute | solution.py:31
  103.4 1.4 %collective-permute-done.28 = f32[360,288]{0,1:T(8,128)S(1)} collective-permute-done((f32[360,288]{0,1:T(8,128)S(1)}, f32[360,288]{0,1:T(8,128)S(1)}, u32[]{:S(2)}, u32[]{:S(2)}) %collective-permute-start.28) | collective-permute-done | bytes 414752 | tf_op jit(solution)/shard_map/ppermute | solution.py:31
  105.4 0.5 fusion.3
  106.1 1.0 copy.21
  107.1 1.0 copy.22
  (55 shorter events, 4.3 us)
Async XLA Ops:
  3.5 2.7 %collective-permute-start = (bf16[352,288]{1,0:T(8,128)(2,1)S(1)}, bf16[352,288]{1,0:T(8,128)(2,1)S(1)}, u32[]{:S(2)}, u32[]{:S(2)}) collective-permute-start(bf16[352,288]{1,0:T(8,128)(2,1)S(1)} %broadcast_select_fusion.2), channel_id=1, source_target_pairs={{0,1},{1,0},{2,3},{3,2},{4,5},{5,4},{6,7},{7,6},{8,9},{9,8},{10,11... | collective-permute-start | bytes 608264 | tf_op jit(solution)/shard_map/ppermute | solution.py:31
  6.6 5.8 %collective-permute-start.5 = (bf16[88,576]{1,0:T(8,128)(2,1)S(1)}, bf16[88,576]{1,0:T(8,128)(2,1)S(1)}, u32[]{:S(2)}, u32[]{:S(2)}) collective-permute-start(bf16[88,576]{1,0:T(8,128)(2,1)S(1)} %get-tuple-element.87), channel_id=1, source_target_pairs={{0,2},{1,3},{2,0},{3,1},{4,6},{5,7},{6,4},{7,5},{8,10},{9,11},{10,... | collective-permute-start | bytes 304136 | tf_op jit(solution)/shard_map/ppermute | solution.py:31
  8.6 8.7 %collective-permute-start.2 = (bf16[88,1152]{1,0:T(8,128)(2,1)S(1)}, bf16[88,1152]{1,0:T(8,128)(2,1)S(1)}, u32[]{:S(2)}, u32[]{:S(2)}) collective-permute-start(bf16[88,1152]{1,0:T(8,128)(2,1)S(1)} %pad_maximum_fusion.6), channel_id=1, source_target_pairs={{0,32},{1,65},{2,34},{3,67},{4,36},{5,69},{6,38},{7,71},{8,40},{9,... | collective-permute-start | bytes 608264 | tf_op jit(solution)/shard_map/ppermute | solution.py:31
  12.0 6.6 %collective-permute-start.1 = (bf16[88,1152]{1,0:T(8,128)(2,1)S(1)}, bf16[88,1152]{1,0:T(8,128)(2,1)S(1)}, u32[]{:S(2)}, u32[]{:S(2)}) collective-permute-start(bf16[88,1152]{1,0:T(8,128)(2,1)S(1)} %pad_maximum_fusion.6), channel_id=1, source_target_pairs={{0,16},{1,3},{2,18},{3,1},{4,20},{5,7},{6,22},{7,5},{8,24},{9,11},... | collective-permute-start | bytes 608264 | tf_op jit(solution)/shard_map/ppermute | solution.py:31
  12.0 7.6 %collective-permute-start.3 = (bf16[88,1152]{1,0:T(8,128)(2,1)S(1)}, bf16[88,1152]{1,0:T(8,128)(2,1)S(1)}, u32[]{:S(2)}, u32[]{:S(2)}) collective-permute-start(bf16[88,1152]{1,0:T(8,128)(2,1)S(1)} %pad_maximum_fusion.6), channel_id=1, source_target_pairs={{0,48},{1,67},{2,50},{3,65},{4,52},{5,71},{6,54},{7,69},{8,56},{9,... | collective-permute-start | bytes 608264 | tf_op jit(solution)/shard_map/ppermute | solution.py:31
  12.5 11.1 %collective-permute-start.8 = (bf16[88,1152]{1,0:T(8,128)(2,1)S(1)}, bf16[88,1152]{1,0:T(8,128)(2,1)S(1)}, u32[]{:S(2)}, u32[]{:S(2)}) collective-permute-start(bf16[88,1152]{1,0:T(8,128)(2,1)S(1)} %pad_maximum_fusion.7), channel_id=1, source_target_pairs={{0,12},{1,13},{2,14},{3,15},{4,8},{5,9},{6,10},{7,11},{8,4},{9,5},... | collective-permute-start | bytes 608264 | tf_op jit(solution)/shard_map/ppermute | solution.py:31
  15.0 8.5 %collective-permute-start.7 = (bf16[88,1152]{1,0:T(8,128)(2,1)S(1)}, bf16[88,1152]{1,0:T(8,128)(2,1)S(1)}, u32[]{:S(2)}, u32[]{:S(2)}) collective-permute-start(bf16[88,1152]{1,0:T(8,128)(2,1)S(1)} %pad_maximum_fusion.7), channel_id=1, source_target_pairs={{0,8},{1,9},{2,10},{3,11},{4,12},{5,13},{6,14},{7,15},{8,0},{9,1},... | collective-permute-start | bytes 608264 | tf_op jit(solution)/shard_map/ppermute | solution.py:31
  17.3 7.0 %collective-permute-start.6 = (bf16[88,1152]{1,0:T(8,128)(2,1)S(1)}, bf16[88,1152]{1,0:T(8,128)(2,1)S(1)}, u32[]{:S(2)}, u32[]{:S(2)}) collective-permute-start(bf16[88,1152]{1,0:T(8,128)(2,1)S(1)} %pad_maximum_fusion.7), channel_id=1, source_target_pairs={{0,4},{1,5},{2,6},{3,7},{4,0},{5,1},{6,2},{7,3},{8,12},{9,13},{10,... | collective-permute-start | bytes 608264 | tf_op jit(solution)/shard_map/ppermute | solution.py:31
  19.7 11.5 %collective-permute-start.4 = (bf16[4,88,1152]{2,1,0:T(8,128)(2,1)S(1)}, bf16[4,88,1152]{2,1,0:T(8,128)(2,1)S(1)}, u32[]{:S(2)}, u32[]{:S(2)}) collective-permute-start(bf16[4,88,1152]{2,1,0:T(8,128)(2,1)S(1)} %pad_maximum_fusion.ta_ref), channel_id=1, source_target_pairs={{0,2},{1,17},{2,0},{3,19},{4,6},{5,21},{6,4},{7,23},{8,10},{9,25},... | collective-permute-start | bytes 2433032 | tf_op jit(solution)/shard_map/ppermute | solution.py:31
  24.4 6.7 %collective-permute-start.9 = (bf16[352,1152]{1,0:T(8,128)(2,1)S(1)}, bf16[352,1152]{1,0:T(8,128)(2,1)S(1)}, u32[]{:S(2)}, u32[]{:S(2)}) collective-permute-start(bf16[352,1152]{1,0:T(8,128)(2,1)S(1)} %pad_maximum_fusion.1.im0_ref), channel_id=1, source_target_pairs={{0,1},{1,0},{2,3},{3,2},{4,5},{5,4},{6,7},{7,6},{8,9},{9,8},{10,11... | collective-permute-start | bytes 2433032 | tf_op jit(solution)/shard_map/ppermute | solution.py:31
  27.8 21.4 %collective-permute-start.11 = (bf16[4,88,1152]{2,1,0:T(8,128)(2,1)S(1)}, bf16[4,88,1152]{2,1,0:T(8,128)(2,1)S(1)}, u32[]{:S(2)}, u32[]{:S(2)}) collective-permute-start(bf16[4,88,1152]{2,1,0:T(8,128)(2,1)S(1)} %pad_maximum_fusion.ta_ref), channel_id=1, source_target_pairs={{0,66},{1,49},{2,64},{3,51},{4,70},{5,53},{6,68},{7,55},{8,74},{9,... | collective-permute-start | bytes 2433032 | tf_op jit(solution)/shard_map/ppermute | solution.py:31
  30.5 18.6 %collective-permute-start.10 = (bf16[4,88,1152]{2,1,0:T(8,128)(2,1)S(1)}, bf16[4,88,1152]{2,1,0:T(8,128)(2,1)S(1)}, u32[]{:S(2)}, u32[]{:S(2)}) collective-permute-start(bf16[4,88,1152]{2,1,0:T(8,128)(2,1)S(1)} %pad_maximum_fusion.ta_ref), channel_id=1, source_target_pairs={{0,64},{1,33},{2,66},{3,35},{4,68},{5,37},{6,70},{7,39},{8,72},{9,... | collective-permute-start | bytes 2433032 | tf_op jit(solution)/shard_map/ppermute | solution.py:31
  38.4 19.1 %collective-permute-start.12 = (bf16[360,1152]{1,0:T(8,128)(2,1)S(1)}, bf16[360,1152]{1,0:T(8,128)(2,1)S(1)}, u32[]{:S(2)}, u32[]{:S(2)}) collective-permute-start(bf16[360,1152]{1,0:T(8,128)(2,1)S(1)} %get-tuple-element.45), channel_id=1, source_target_pairs={{0,2},{1,17},{2,0},{3,19},{4,6},{5,21},{6,4},{7,23},{8,10},{9,25},... | collective-permute-start | bytes 2488328 | tf_op jit(solution)/shard_map/ppermute | solution.py:31
  57.5 5.8 %collective-permute-start.13 = (f32[352,1152]{1,0:T(8,128)S(1)}, f32[352,1152]{1,0:T(8,128)S(1)}, u32[]{:S(2)}, u32[]{:S(2)}) collective-permute-start(f32[352,1152]{1,0:T(8,128)S(1)} %get-tuple-element.46), channel_id=1, source_target_pairs={{0,1},{1,0},{2,3},{3,2},{4,5},{5,4},{6,7},{7,6},{8,9},{9,8},{10,11... | collective-permute-start | bytes 4866056 | tf_op jit(solution)/shard_map/ppermute | solution.py:31
  58.4 14.4 %collective-permute-start.16 = (bf16[360,1152]{1,0:T(8,128)(2,1)S(1)}, bf16[360,1152]{1,0:T(8,128)(2,1)S(1)}, u32[]{:S(2)}, u32[]{:S(2)}) collective-permute-start(bf16[360,1152]{1,0:T(8,128)(2,1)S(1)} %get-tuple-element.57), channel_id=1, source_target_pairs={{0,64},{1,33},{2,66},{3,35},{4,68},{5,37},{6,70},{7,39},{8,72},{9,... | collective-permute-start | bytes 2488328 | tf_op jit(solution)/shard_map/ppermute | solution.py:31
  61.3 19.1 %collective-permute-start.17 = (bf16[360,1152]{1,0:T(8,128)(2,1)S(1)}, bf16[360,1152]{1,0:T(8,128)(2,1)S(1)}, u32[]{:S(2)}, u32[]{:S(2)}) collective-permute-start(bf16[360,1152]{1,0:T(8,128)(2,1)S(1)} %get-tuple-element.58), channel_id=1, source_target_pairs={{0,66},{1,49},{2,64},{3,51},{4,70},{5,53},{6,68},{7,55},{8,74},{9,... | collective-permute-start | bytes 2488328 | tf_op jit(solution)/shard_map/ppermute | solution.py:31
  62.1 2.8 %collective-permute-start.14 = (f32[8,128]{1,0:T(8,128)S(1)}, f32[8,128]{1,0:T(8,128)S(1)}, u32[]{:S(2)}, u32[]{:S(2)}) collective-permute-start(f32[8,128]{1,0:T(8,128)S(1)} %get-tuple-element.50), channel_id=1, source_target_pairs={{0,4},{1,5},{2,6},{3,7},{4,0},{5,1},{6,2},{7,3},{8,12},{9,13},{10,... | collective-permute-start | bytes 12296 | tf_op jit(solution)/shard_map/ppermute | solution.py:31
  64.9 4.0 %collective-permute-start.15 = (f32[8,128]{1,0:T(8,128)S(1)}, f32[8,128]{1,0:T(8,128)S(1)}, u32[]{:S(2)}, u32[]{:S(2)}) collective-permute-start(f32[8,128]{1,0:T(8,128)S(1)} %add.25), channel_id=1, source_target_pairs={{0,12},{1,13},{2,14},{3,15},{4,8},{5,9},{6,10},{7,11},{8,4},{9,5},... | collective-permute-start | bytes 12296 | tf_op jit(solution)/shard_map/ppermute | solution.py:31
  68.8 14.4 %collective-permute-start.20 = (f32[8,128]{1,0:T(8,128)S(1)}, f32[8,128]{1,0:T(8,128)S(1)}, u32[]{:S(2)}, u32[]{:S(2)}) collective-permute-start(f32[8,128]{1,0:T(8,128)S(1)} %add.26), channel_id=1, source_target_pairs={{0,66},{1,49},{2,64},{3,51},{4,70},{5,53},{6,68},{7,55},{8,74},{9,... | collective-permute-start | bytes 12296 | tf_op jit(solution)/shard_map/ppermute | solution.py:31
  70.7 13.3 %collective-permute-start.19 = (f32[8,128]{1,0:T(8,128)S(1)}, f32[8,128]{1,0:T(8,128)S(1)}, u32[]{:S(2)}, u32[]{:S(2)}) collective-permute-start(f32[8,128]{1,0:T(8,128)S(1)} %add.26), channel_id=1, source_target_pairs={{0,64},{1,33},{2,66},{3,35},{4,68},{5,37},{6,70},{7,39},{8,72},{9,... | collective-permute-start | bytes 12296 | tf_op jit(solution)/shard_map/ppermute | solution.py:31
  70.7 13.3 %collective-permute-start.18 = (f32[8,128]{1,0:T(8,128)S(1)}, f32[8,128]{1,0:T(8,128)S(1)}, u32[]{:S(2)}, u32[]{:S(2)}) collective-permute-start(f32[8,128]{1,0:T(8,128)S(1)} %add.26), channel_id=1, source_target_pairs={{0,2},{1,17},{2,0},{3,19},{4,6},{5,21},{6,4},{7,23},{8,10},{9,25},... | collective-permute-start | bytes 12296 | tf_op jit(solution)/shard_map/ppermute | solution.py:31
  72.9 17.9 %collective-permute-start.24 = (bf16[96,1152]{1,0:T(8,128)(2,1)S(1)}, bf16[96,1152]{1,0:T(8,128)(2,1)S(1)}, u32[]{:S(2)}, u32[]{:S(2)}) collective-permute-start(bf16[96,1152]{1,0:T(8,128)(2,1)S(1)} %get-tuple-element.51), channel_id=1, source_target_pairs={{0,4},{1,5},{2,6},{3,7},{4,0},{5,1},{6,2},{7,3},{8,12},{9,13},{10,... | collective-permute-start | bytes 663560 | tf_op jit(solution)/shard_map/ppermute | solution.py:31
  80.4 10.5 %collective-permute-start.25 = (bf16[96,1152]{1,0:T(8,128)(2,1)S(1)}, bf16[96,1152]{1,0:T(8,128)(2,1)S(1)}, u32[]{:S(2)}, u32[]{:S(2)}) collective-permute-start(bf16[96,1152]{1,0:T(8,128)(2,1)S(1)} %get-tuple-element.52), channel_id=1, source_target_pairs={{0,8},{1,9},{2,10},{3,11},{4,12},{5,13},{6,14},{7,15},{8,0},{9,1},... | collective-permute-start | bytes 663560 | tf_op jit(solution)/shard_map/ppermute | solution.py:31
  83.2 10.8 %collective-permute-start.26 = (bf16[96,1152]{1,0:T(8,128)(2,1)S(1)}, bf16[96,1152]{1,0:T(8,128)(2,1)S(1)}, u32[]{:S(2)}, u32[]{:S(2)}) collective-permute-start(bf16[96,1152]{1,0:T(8,128)(2,1)S(1)} %get-tuple-element.53), channel_id=1, source_target_pairs={{0,12},{1,13},{2,14},{3,15},{4,8},{5,9},{6,10},{7,11},{8,4},{9,5},... | collective-permute-start | bytes 663560 | tf_op jit(solution)/shard_map/ppermute | solution.py:31
  87.0 7.8 %collective-permute-start.21 = (bf16[96,1152]{1,0:T(8,128)(2,1)S(1)}, bf16[96,1152]{1,0:T(8,128)(2,1)S(1)}, u32[]{:S(2)}, u32[]{:S(2)}) collective-permute-start(bf16[96,1152]{1,0:T(8,128)(2,1)S(1)} %get-tuple-element.63), channel_id=1, source_target_pairs={{0,16},{1,3},{2,18},{3,1},{4,20},{5,7},{6,22},{7,5},{8,24},{9,11},... | collective-permute-start | bytes 663560 | tf_op jit(solution)/shard_map/ppermute | solution.py:31
  87.1 9.7 %collective-permute-start.22 = (bf16[96,1152]{1,0:T(8,128)(2,1)S(1)}, bf16[96,1152]{1,0:T(8,128)(2,1)S(1)}, u32[]{:S(2)}, u32[]{:S(2)}) collective-permute-start(bf16[96,1152]{1,0:T(8,128)(2,1)S(1)} %get-tuple-element.64), channel_id=1, source_target_pairs={{0,32},{1,65},{2,34},{3,67},{4,36},{5,69},{6,38},{7,71},{8,40},{9,... | collective-permute-start | bytes 663560 | tf_op jit(solution)/shard_map/ppermute | solution.py:31
  90.8 8.3 %collective-permute-start.23 = (bf16[96,1152]{1,0:T(8,128)(2,1)S(1)}, bf16[96,1152]{1,0:T(8,128)(2,1)S(1)}, u32[]{:S(2)}, u32[]{:S(2)}) collective-permute-start(bf16[96,1152]{1,0:T(8,128)(2,1)S(1)} %get-tuple-element.65), channel_id=1, source_target_pairs={{0,48},{1,67},{2,50},{3,65},{4,52},{5,71},{6,54},{7,69},{8,56},{9,... | collective-permute-start | bytes 663560 | tf_op jit(solution)/shard_map/ppermute | solution.py:31
  94.8 6.7 %collective-permute-start.27 = (f32[88,576]{1,0:T(8,128)S(1)}, f32[88,576]{1,0:T(8,128)S(1)}, u32[]{:S(2)}, u32[]{:S(2)}) collective-permute-start(f32[88,576]{1,0:T(8,128)S(1)} %slice.93), channel_id=1, source_target_pairs={{0,2},{1,3},{2,0},{3,1},{4,6},{5,7},{6,4},{7,5},{8,10},{9,11},{10,... | collective-permute-start | bytes 608264 | tf_op jit(solution)/shard_map/ppermute | solution.py:31
  102.0 2.8 %collective-permute-start.28 = (f32[360,288]{0,1:T(8,128)S(1)}, f32[360,288]{0,1:T(8,128)S(1)}, u32[]{:S(2)}, u32[]{:S(2)}) collective-permute-start(f32[360,288]{0,1:T(8,128)S(1)} %copy.17), channel_id=1, source_target_pairs={{0,1},{1,0},{2,3},{3,2},{4,5},{5,4},{6,7},{7,6},{8,9},{9,8},{10,11... | collective-permute-start | bytes 1244168 | tf_op jit(solution)/shard_map/ppermute | solution.py:31

commit v9 on v8

--- a/solution.py
+++ b/solution.py
@@ -117,19 +117,20 @@
 
 def far_kernel(
     rows, half, feats, info_ref, scale_ref, ta_ref, tb_ref, im0_ref, im1_ref, before_ref, sums_before,
-    ma_ref, mb_ref, own_ref, other_ref, sums_ref, images, t_rel, coeff_low, grads,
+    ma_ref, mb_ref, own_ref, other_ref, images, t_rel, coeff_low, grads,
 ):
     quarter = 4 * rows
     images[0:quarter, :] = im0_ref[...]
     images[quarter : 2 * quarter, :] = im1_ref[...]
     pairs(info_ref, rows, half, ta_ref, tb_ref, t_rel)
-    sums_ref[...] = coefficients(False, rows, info_ref, scale_ref, t_rel, images, coeff_low) + sums_before[...]
+    sums = coefficients(False, rows, info_ref, scale_ref, t_rel, images, coeff_low) + sums_before[...]
     text_parts(info_ref, rows, half, coeff_low, images, grads)
     for k, m_ref in ((0, ma_ref), (1, mb_ref)):
         m_ref[...] = message([grads[k, i] for i in range(4)], feats)
     acc = image_parts(coeff_low, t_rel) + before_ref[...]
-    own_ref[...] = acc[0:quarter]
-    other_ref[...] = acc[quarter : 2 * quarter]
+    wide = jnp.concatenate([sums] * (feats // 128), axis=1)
+    own_ref[...] = jnp.concatenate([acc[0:quarter], wide], axis=0)
+    other_ref[...] = jnp.concatenate([acc[quarter : 2 * quarter], wide], axis=0)
 
 
 def message(blocks, feats, extra=()):
@@ -153,16 +154,26 @@
 
 def image_first_kernel(rows, feats, own_ref, other_ref, out_ref, *messages):
     total = own_ref[...] + other_ref[...]
-    out_ref[...] = total[0:rows]
+    sums = total[4 * rows :]
+    out_ref[...] = jnp.concatenate([total[0:rows], sums], axis=0)
     for i, m_ref in enumerate(messages):
-        m_ref[...] = message([total[(i + 1) * rows : (i + 2) * rows]], feats)
-
-
-def image_last_kernel(scale_ref, own_ref, r1_ref, r2_ref, r3_ref, out_ref):
-    total = own_ref[...]
-    for r in (r1_ref, r2_ref, r3_ref):
-        total = total + decoded(r)[0]
+        m_ref[...] = message([total[(i + 1) * rows : (i + 2) * rows]], feats, split3(sums[0:1]))
+
+
+def with_scalars(own_ref, refs):
+    n = own_ref.shape[0] - 8
+    total, tails = own_ref[0:n, :], []
+    for r in refs:
+        value, tail = decoded(r)
+        total = total + value
+        tails.append(tail[0:1] + (tail[1:2] + tail[2:3]))
+    return total, (own_ref[n : n + 1, :] + tails[0]) + (tails[1] + tails[2])
+
+
+def image_last_kernel(feats, scale_ref, own_ref, r1_ref, r2_ref, r3_ref, out_ref, sums_ref):
+    total, sums = with_scalars(own_ref, (r1_ref, r2_ref, r3_ref))
     out_ref[...] = total * scale_ref[0]
+    sums_ref[...] = jnp.broadcast_to(sums, (8, feats))
 
 
 def text_near_kernel(own_ref, r1_ref, out_ref):
@@ -171,21 +182,15 @@
 
 def text_first_kernel(rows, feats, own_ref, r2_ref, r3_ref, sums_ref, out_ref, *messages):
     total = own_ref[...] + decoded(r2_ref)[0] + decoded(r3_ref)[0]
-    out_ref[...] = total[0:rows]
-    scalars = [jnp.concatenate([v] * (feats // 128), axis=1) for v in split3(sums_ref[0:1, :])]
+    out_ref[...] = jnp.concatenate([total[0:rows], sums_ref[...]], axis=0)
     for i, m_ref in enumerate(messages):
-        m_ref[...] = message([total[(i + 1) * rows : (i + 2) * rows]], feats, scalars)
-
-
-def text_last_kernel(feats, scale_ref, own_ref, sums_ref, r1_ref, r2_ref, r3_ref, out_ref):
-    total, tails = own_ref[...], []
-    for r in (r1_ref, r2_ref, r3_ref):
-        value, tail = decoded(r)
-        total = total + value
-        tails.append(tail[0:1, :128] + (tail[1:2, :128] + tail[2:3, :128]))
-    sums = (sums_ref[0:1, :] + tails[0]) + (tails[1] + tails[2])
-    sums = jnp.broadcast_to(jnp.concatenate([sums] * (feats // 128), axis=1), (8, feats))
-    out_ref[...] = jnp.concatenate([total * scale_ref[0], sums], axis=0)
+        m_ref[...] = message([total[(i + 1) * rows : (i + 2) * rows]], feats, split3(sums_ref[0:1, :]))
+
+
+def text_last_kernel(scale_ref, own_ref, r1_ref, r2_ref, r3_ref, out_ref, sums_ref):
+    total, sums = with_scalars(own_ref, (r1_ref, r2_ref, r3_ref))
+    out_ref[...] = total * scale_ref[0]
+    sums_ref[...] = jnp.broadcast_to(sums[:, :128], (8, 128))
 
 
 VMEM = pl.BlockSpec(memory_space=pltpu.VMEM)
@@ -225,6 +230,7 @@
     images_own = jnp.concatenate([image] + [swap(image, x_mask(k)) for k in range(1, 4)], axis=0)
     images_other = swap(images_own, CORE)
     second2 = swap(after(stack, images_own), z_mask(2), y_mask(2))
+    second1, second3 = lax.optimization_barrier((second1, second3))
 
     def f32(*shape):
         return jax.ShapeDtypeStruct(shape, F32)
@@ -260,46 +266,43 @@
         info, scales, stack, second1, images_own, images_other,
         scalars=2, mib=40, products=3, scratch=scratch,
     )
-    m2, m3, img_own, img_other, sums = call(
+    m2, m3, img_own, img_other = call(
         functools.partial(far_kernel, *sizes), "tile_far",
-        [bf16(quarter + 8, feats), bf16(quarter + 8, feats), f32(quarter, feats), f32(quarter, feats), f32(8, 128)],
+        [bf16(quarter + 8, feats), bf16(quarter + 8, feats), f32(quarter + 8, feats), f32(quarter + 8, feats)],
         info, scales, second2, second3, images_own, images_other, acc, sums,
         scalars=2, mib=40, products=3, scratch=scratch,
     )
     got1 = swap(m1, z_mask(1), y_mask(1))
-    m2, m3, img_other, sums, got1 = lax.optimization_barrier((m2, m3, img_other, sums, got1))
+    m2, m3, img_other, got1 = lax.optimization_barrier((m2, m3, img_other, got1))
     got2, got3 = swap(m2, z_mask(2), y_mask(2)), swap(m3, z_mask(3), y_mask(3))
-    one = swap(sums, x_mask(1))
     img, *messages = call(
         functools.partial(image_first_kernel, rows, feats), "image_first",
-        [f32(rows, feats)] + [bf16(rows + 8, feats)] * 3, img_own, swap(img_other, CORE),
-    )
-    *messages, one = lax.optimization_barrier((*messages, one))
-    two = sums + one
-    four = two + swap(two, x_mask(3))
+        [f32(rows + 8, feats)] + [bf16(rows + 8, feats)] * 3, img_own, swap(img_other, CORE),
+    )
     img_got = [swap(m, x_mask(k)) for k, m in zip((1, 2, 3), messages)]
-    (text,) = call(text_near_kernel, "text_near", [f32(quarter, feats)], after(text, *messages, four), got1, products=3)
-    s1, s2, s3 = (after(swap(four, z_mask(k), y_mask(k)), got2, got3) for k in (1, 2, 3))
-    sums = (four + s1) + (s2 + s3)
+    (text,) = call(text_near_kernel, "text_near", [f32(quarter, feats)], after(text, *messages), got1)
+    img, sums = call(
+        functools.partial(image_last_kernel, feats), "image_last", [f32(rows, feats), f32(8, feats)],
+        logit_scaler, img, *img_got, scalars=1,
+    )
     text, *messages = call(
         functools.partial(text_first_kernel, rows, feats), "text_first",
-        [f32(rows, feats)] + [bf16(rows + 8, feats)] * 3, text, got2, got3, sums, brief=True,
+        [f32(rows + 8, feats)] + [bf16(rows + 8, feats)] * 3, text, got2, got3, sums,
     )
     got = [swap(m, y_mask(i), z_mask(i)) for i, m in zip((1, 2, 3), messages)]
-
-    img_got[0] = after(img_got[0], text)
-    (img,) = call(image_last_kernel, "image_last", [f32(rows, feats)], logit_scaler, img, *img_got, scalars=1, products=3)
-    (text,) = call(
-        functools.partial(text_last_kernel, feats), "text_last", [f32(rows + 8, feats)],
-        logit_scaler, text, sums, *got, scalars=1, products=4,
+    text, sums = call(
+        text_last_kernel, "text_last", [f32(rows, feats), f32(8, 128)], logit_scaler, text, *got, scalars=1, products=2
     )
     image = jnp.concatenate(by(lo0, img[:, :half], after(swap(img[:, half:], z_mask(1)), text)), axis=0)
-    whole = jnp.concatenate([text[:rows, :half], text[:rows, half:], image, text[rows:, :half]], axis=0)
+    whole = jnp.concatenate([text[:, :half], text[:, half:], image], axis=0)
     mine, other = by(on0, whole[:, :width], whole[:, width:])
+    sums = after(sums, other)
     other = swap(other, CORE)
     text_grad = jnp.concatenate(by(on0, mine[:step], other[:step]), axis=0)
-    image_grad = jnp.concatenate(by(on0, mine[step : 2 * step], other[step : 2 * step]), axis=0)
-    return (image_grad, text_grad, mine[2 * step, :2] + other[2 * step, :2])
+    image_grad = jnp.concatenate(by(on0, mine[step:], other[step:]), axis=0)
+    s1, s2, s3 = (swap(sums, z_mask(k), y_mask(k)) for k in (1, 2, 3))
+    sums = (sums + s1) + (s2 + s3)
+    return (image_grad, text_grad, sums[0, :2])
 
 
 def solution(mesh):

time: 108 us -> 103 us (0.954)
  waiting for transfers between devices: 36.9 us -> 32.7 us
  starting transfers between devices: 39.6 us -> 38.2 us
    ppermute x29 -> x27, waiting for transfers between devices: 36.9 us -> 32.7 us  [swap(): lax.ppermute(array, AXES, [(i, i ^ (mask1 if i & 1 else mask0)) for i in...]
    ppermute x29 -> x27, starting transfers between devices: 39.6 us -> 38.2 us  [swap(): lax.ppermute(array, AXES, [(i, i ^ (mask1 if i & 1 else mask0)) for i in...]
    unnamed x11 -> x8, local copies, waits for them, and re-layouts: 2.99 us -> 2.77 us
  transfers between devices with their start and end apart: 29 -> 27, of which waited for: 15 -> 18; matrix products, arithmetic and copies ran while one was open for 1% -> 1% of each run, Pallas kernels for 20% -> 18%
where the time goes in v9:
time: 103 us; the launch traced here: 102 us
  starting transfers between devices  38.2 us (37%)
  waiting for transfers between devices  32.7 us (32%)
  Pallas kernels  21.7 us (21%)
  local copies, waits for them, and re-layouts  5.92 us (6%)
  between operations  2.18 us (2%)
  other arithmetic  1.68 us (2%)
    ppermute x27, starting transfers between devices, swap(): lax.ppermute(array, AXES, [(i, i ^ (mask1 if i & 1 else mask0)) for i in...  38.2 us
    ppermute x27, waiting for transfers between devices, swap(): lax.ppermute(array, AXES, [(i, i ^ (mask1 if i & 1 else mask0)) for i in...  32.7 us
    pallas_call x7, Pallas kernels, call(): pl.pallas_call(kernel, out_shape=out_shape, in_specs=[SMEM] * scalars + [...  21.7 us
    unnamed x8, local copies, waits for them, and re-layouts  2.77 us
  transfers between devices with their start and end apart: 27, of which 18 were waited for; matrix products, arithmetic and copies ran while one was open for 1% of the time, Pallas kernels for 18%

profile of v9, /device:TPU:1, one launch (start us, length us, event | category | flops | bytes accessed | tf_op | source)
XLA Modules:
  0.0 102.4 jit_solution(5182048251441859054)
XLA Ops:
  0.6 1.1 %fusion.6 = (bf16[176,288]{0,1:T(8,128)(2,1)S(1)}, bf16[176,288]{0,1:T(8,128)(2,1)S(1)}) fusion(bf16[352,288]{0,1:T(8,128)(2,1)} %param.4), kind=kLoop, calls=%fused_computation.40 | loop fusion | bytes 405504 | tf_op jit(solution)/shard_map/slice | solution.py:220
  2.0 1.1 %fusion.5 = (bf16[176,288]{0,1:T(8,128)(2,1)S(1)}, bf16[176,288]{0,1:T(8,128)(2,1)S(1)}) fusion(bf16[352,288]{0,1:T(8,128)(2,1)} %param.5), kind=kLoop, calls=%fused_computation.39 | loop fusion | bytes 405504 | tf_op jit(solution)/shard_map/slice | solution.py:220
  3.5 1.5 %collective-permute-start = (bf16[352,288]{1,0:T(8,128)(2,1)S(1)}, bf16[352,288]{1,0:T(8,128)(2,1)S(1)}, u32[]{:S(2)}, u32[]{:S(2)}) collective-permute-start(bf16[352,288]{1,0:T(8,128)(2,1)S(1)} %broadcast_select_fusion.2), channel_id=1, source_target_pairs={{0,1},{1,0},{2,3},{3,2},{4,5},{5,4},{6,7},{7,6},{8,9},{9,8},{10,11... | collective-permute-start | bytes 608264 | tf_op jit(solution)/shard_map/ppermute | solution.py:31
  5.0 1.2 %collective-permute-done = bf16[352,288]{1,0:T(8,128)(2,1)S(1)} collective-permute-done((bf16[352,288]{1,0:T(8,128)(2,1)S(1)}, bf16[352,288]{1,0:T(8,128)(2,1)S(1)}, u32[]{:S(2)}, u32[]{:S(2)}) %collective-permute-start) | collective-permute-done | bytes 202784 | tf_op jit(solution)/shard_map/ppermute | solution.py:31
  6.6 1.8 %collective-permute-start.6 = (bf16[88,576]{1,0:T(8,128)(2,1)S(1)}, bf16[88,576]{1,0:T(8,128)(2,1)S(1)}, u32[]{:S(2)}, u32[]{:S(2)}) collective-permute-start(bf16[88,576]{1,0:T(8,128)(2,1)S(1)} %get-tuple-element.83), channel_id=1, source_target_pairs={{0,2},{1,3},{2,0},{3,1},{4,6},{5,7},{6,4},{7,5},{8,10},{9,11},{10,... | collective-permute-start | bytes 304136 | tf_op jit(solution)/shard_map/ppermute | solution.py:31
  8.6 3.4 %collective-permute-start.2 = (bf16[88,1152]{1,0:T(8,128)(2,1)S(1)}, bf16[88,1152]{1,0:T(8,128)(2,1)S(1)}, u32[]{:S(2)}, u32[]{:S(2)}) collective-permute-start(bf16[88,1152]{1,0:T(8,128)(2,1)S(1)} %pad_maximum_fusion.7), channel_id=1, source_target_pairs={{0,32},{1,65},{2,34},{3,67},{4,36},{5,69},{6,38},{7,71},{8,40},{9,... | collective-permute-start | bytes 608264 | tf_op jit(solution)/shard_map/ppermute | solution.py:31
  12.5 2.6 %collective-permute-start.9 = (bf16[88,1152]{1,0:T(8,128)(2,1)S(1)}, bf16[88,1152]{1,0:T(8,128)(2,1)S(1)}, u32[]{:S(2)}, u32[]{:S(2)}) collective-permute-start(bf16[88,1152]{1,0:T(8,128)(2,1)S(1)} %pad_maximum_fusion.8), channel_id=1, source_target_pairs={{0,12},{1,13},{2,14},{3,15},{4,8},{5,9},{6,10},{7,11},{8,4},{9,5},... | collective-permute-start | bytes 608264 | tf_op jit(solution)/shard_map/ppermute | solution.py:31
  15.5 1.8 %collective-permute-done.2 = bf16[88,1152]{1,0:T(8,128)(2,1)S(1)} collective-permute-done((bf16[88,1152]{1,0:T(8,128)(2,1)S(1)}, bf16[88,1152]{1,0:T(8,128)(2,1)S(1)}, u32[]{:S(2)}, u32[]{:S(2)}) %collective-permute-start.2) | collective-permute-done | bytes 202784 | tf_op jit(solution)/shard_map/ppermute | solution.py:31
  17.3 1.2 %collective-permute-start.7 = (bf16[88,1152]{1,0:T(8,128)(2,1)S(1)}, bf16[88,1152]{1,0:T(8,128)(2,1)S(1)}, u32[]{:S(2)}, u32[]{:S(2)}) collective-permute-start(bf16[88,1152]{1,0:T(8,128)(2,1)S(1)} %pad_maximum_fusion.8), channel_id=1, source_target_pairs={{0,4},{1,5},{2,6},{3,7},{4,0},{5,1},{6,2},{7,3},{8,12},{9,13},{10,... | collective-permute-start | bytes 608264 | tf_op jit(solution)/shard_map/ppermute | solution.py:31
  18.5 1.0 collective-permute-done.3
  19.7 2.8 %collective-permute-start.5 = (bf16[4,88,1152]{2,1,0:T(8,128)(2,1)S(1)}, bf16[4,88,1152]{2,1,0:T(8,128)(2,1)S(1)}, u32[]{:S(2)}, u32[]{:S(2)}) collective-permute-start(bf16[4,88,1152]{2,1,0:T(8,128)(2,1)S(1)} %pad_maximum_fusion.1.ta_ref), channel_id=1, source_target_pairs={{0,66},{1,49},{2,64},{3,51},{4,70},{5,53},{6,68},{7,55},{8,74},{9,... | collective-permute-start | bytes 2433032 | tf_op jit(solution)/shard_map/ppermute | solution.py:31
  22.5 1.1 %collective-permute-done.9 = bf16[88,1152]{1,0:T(8,128)(2,1)S(1)} collective-permute-done((bf16[88,1152]{1,0:T(8,128)(2,1)S(1)}, bf16[88,1152]{1,0:T(8,128)(2,1)S(1)}, u32[]{:S(2)}, u32[]{:S(2)}) %collective-permute-start.9) | collective-permute-done | bytes 202784 | tf_op jit(solution)/shard_map/ppermute | solution.py:31
  23.6 0.8 collective-permute-done.7
  24.4 1.9 %collective-permute-start.10 = (bf16[352,1152]{1,0:T(8,128)(2,1)S(1)}, bf16[352,1152]{1,0:T(8,128)(2,1)S(1)}, u32[]{:S(2)}, u32[]{:S(2)}) collective-permute-start(bf16[352,1152]{1,0:T(8,128)(2,1)S(1)} %pad_maximum_fusion.2.im0_ref), channel_id=1, source_target_pairs={{0,1},{1,0},{2,3},{3,2},{4,5},{5,4},{6,7},{7,6},{8,9},{9,8},{10,11... | collective-permute-start | bytes 2433032 | tf_op jit(solution)/shard_map/ppermute | solution.py:31
  27.8 2.9 %collective-permute-start.11 = (bf16[4,88,1152]{2,1,0:T(8,128)(2,1)S(1)}, bf16[4,88,1152]{2,1,0:T(8,128)(2,1)S(1)}, u32[]{:S(2)}, u32[]{:S(2)}) collective-permute-start(bf16[4,88,1152]{2,1,0:T(8,128)(2,1)S(1)} %pad_maximum_fusion.1.ta_ref), channel_id=1, source_target_pairs={{0,64},{1,33},{2,66},{3,35},{4,68},{5,37},{6,70},{7,39},{8,72},{9,... | collective-permute-start | bytes 2433032 | tf_op jit(solution)/shard_map/ppermute | solution.py:31
  30.7 1.8 %collective-permute-done.5.tb_ref = bf16[4,88,1152]{2,1,0:T(8,128)(2,1)S(1)} collective-permute-done((bf16[4,88,1152]{2,1,0:T(8,128)(2,1)S(1)}, bf16[4,88,1152]{2,1,0:T(8,128)(2,1)S(1)}, u32[]{:S(2)}, u32[]{:S(2)}) %collective-permute-start.5) | collective-permute-done | bytes 811040 | tf_op jit(solution)/shard_map/ppermute | solution.py:31
  32.4 1.5 %collective-permute-done.4.tb_ref = bf16[4,88,1152]{2,1,0:T(8,128)(2,1)S(1)} collective-permute-done((bf16[4,88,1152]{2,1,0:T(8,128)(2,1)S(1)}, bf16[4,88,1152]{2,1,0:T(8,128)(2,1)S(1)}, u32[]{:S(2)}, u32[]{:S(2)}) %collective-permute-start.4) | collective-permute-done | bytes 811040 | tf_op jit(solution)/shard_map/ppermute | solution.py:31
  33.9 7.2 %tile_near.1 = (f32[352,1152]{1,0:T(8,128)S(1)}, bf16[360,1152]{1,0:T(8,128)(2,1)S(1)}, f32[704,1152]{1,0:T(8,128)S(1)}, f32[8,128]{1,0:T(8,128)S(1)}) custom-call(s32[2]{0:T(128)S(1)} %pad_add_fusion.info_ref, f32[2]{0:T(128)S(1)} %pad_maximum_fusion.10.scale_ref, bf16[4,88,1152]{2,1,0:T(8,128)(2,1)S(1)} %pad_maximum_fusion.1.ta_ref, ...), custom_call_target="tpu_custom_call" | custom-call | flops 3425697792 | bytes 8943632 | tf_op jit(solution)/shard_map/tile_near/pallas_call | solution.py:242
  41.4 1.0 collective-permute-done.11.ta_ref
  42.4 8.4 %tile_far.1 = (bf16[360,1152]{1,0:T(8,128)(2,1)S(1)}, bf16[360,1152]{1,0:T(8,128)(2,1)S(1)}, f32[360,1152]{1,0:T(8,128)S(1)}, f32[360,1152]{1,0:T(8,128)S(1)}) custom-call(s32[2]{0:T(128)S(1)} %pad_add_fusion.info_ref, f32[2]{0:T(128)S(1)} %pad_maximum_fusion.10.scale_ref, bf16[4,88,1152]{2,1,0:T(8,128)(2,1)S(1)} %collective-permute-done.11.ta_ref, ...), custom_call_target="tpu_custom_call" | custom-call | flops 3425697792 | bytes 11468816 | tf_op jit(solution)/shard_map/tile_far/pallas_call | solution.py:242
  50.8 2.2 %collective-permute-done.12.r1_ref = bf16[360,1152]{1,0:T(8,128)(2,1)S(1)} collective-permute-done((bf16[360,1152]{1,0:T(8,128)(2,1)S(1)}, bf16[360,1152]{1,0:T(8,128)(2,1)S(1)}, u32[]{:S(2)}, u32[]{:S(2)}) %collective-permute-start.12) | collective-permute-done | bytes 829472 | tf_op jit(solution)/shard_map/ppermute | solution.py:31
  53.0 2.1 %collective-permute-start.13 = (f32[360,1152]{1,0:T(8,128)S(1)}, f32[360,1152]{1,0:T(8,128)S(1)}, u32[]{:S(2)}, u32[]{:S(2)}) collective-permute-start(f32[360,1152]{1,0:T(8,128)S(1)} %get-tuple-element.44), channel_id=1, source_target_pairs={{0,1},{1,0},{2,3},{3,2},{4,5},{5,4},{6,7},{7,6},{8,9},{9,8},{10,11... | collective-permute-start | bytes 4976648 | tf_op jit(solution)/shard_map/ppermute | solution.py:31
  55.1 1.6 %collective-permute-start.14 = (bf16[360,1152]{1,0:T(8,128)(2,1)S(1)}, bf16[360,1152]{1,0:T(8,128)(2,1)S(1)}, u32[]{:S(2)}, u32[]{:S(2)}) collective-permute-start(bf16[360,1152]{1,0:T(8,128)(2,1)S(1)} %get-tuple-element.50), channel_id=1, source_target_pairs={{0,64},{1,33},{2,66},{3,35},{4,68},{5,37},{6,70},{7,39},{8,72},{9,... | collective-permute-start | bytes 2488328 | tf_op jit(solution)/shard_map/ppermute | solution.py:31
  56.7 0.8 collective-permute-start.15
  57.5 0.7 collective-permute-done.13.other_ref
  58.2 1.0 image_first.1
  59.2 1.3 %collective-permute-start.16 = (bf16[96,1152]{1,0:T(8,128)(2,1)S(1)}, bf16[96,1152]{1,0:T(8,128)(2,1)S(1)}, u32[]{:S(2)}, u32[]{:S(2)}) collective-permute-start(bf16[96,1152]{1,0:T(8,128)(2,1)S(1)} %get-tuple-element.45), channel_id=1, source_target_pairs={{0,4},{1,5},{2,6},{3,7},{4,0},{5,1},{6,2},{7,3},{8,12},{9,13},{10,... | collective-permute-start | bytes 663560 | tf_op jit(solution)/shard_map/ppermute | solution.py:31
  60.5 2.5 %collective-permute-start.17 = (bf16[96,1152]{1,0:T(8,128)(2,1)S(1)}, bf16[96,1152]{1,0:T(8,128)(2,1)S(1)}, u32[]{:S(2)}, u32[]{:S(2)}) collective-permute-start(bf16[96,1152]{1,0:T(8,128)(2,1)S(1)} %get-tuple-element.46), channel_id=1, source_target_pairs={{0,8},{1,9},{2,10},{3,11},{4,12},{5,13},{6,14},{7,15},{8,0},{9,1},... | collective-permute-start | bytes 663560 | tf_op jit(solution)/shard_map/ppermute | solution.py:31
  63.2 0.8 text_near.1.own_ref
  63.9 1.8 %collective-permute-done.16.r1_ref = bf16[96,1152]{1,0:T(8,128)(2,1)S(1)} collective-permute-done((bf16[96,1152]{1,0:T(8,128)(2,1)S(1)}, bf16[96,1152]{1,0:T(8,128)(2,1)S(1)}, u32[]{:S(2)}, u32[]{:S(2)}) %collective-permute-start.16) | collective-permute-done | bytes 221216 | tf_op jit(solution)/shard_map/ppermute | solution.py:31
  65.7 7.0 %collective-permute-done.17.r2_ref = bf16[96,1152]{1,0:T(8,128)(2,1)S(1)} collective-permute-done((bf16[96,1152]{1,0:T(8,128)(2,1)S(1)}, bf16[96,1152]{1,0:T(8,128)(2,1)S(1)}, u32[]{:S(2)}, u32[]{:S(2)}) %collective-permute-start.17) | collective-permute-done | bytes 221216 | tf_op jit(solution)/shard_map/ppermute | solution.py:31
  72.7 2.3 %collective-permute-done.18.r3_ref = bf16[96,1152]{1,0:T(8,128)(2,1)S(1)} collective-permute-done((bf16[96,1152]{1,0:T(8,128)(2,1)S(1)}, bf16[96,1152]{1,0:T(8,128)(2,1)S(1)}, u32[]{:S(2)}, u32[]{:S(2)}) %collective-permute-start.18) | collective-permute-done | bytes 221216 | tf_op jit(solution)/shard_map/ppermute | solution.py:31
  75.0 0.6 image_last.1
  75.6 1.4 %collective-permute-done.15.r3_ref = bf16[360,1152]{1,0:T(8,128)(2,1)S(1)} collective-permute-done((bf16[360,1152]{1,0:T(8,128)(2,1)S(1)}, bf16[360,1152]{1,0:T(8,128)(2,1)S(1)}, u32[]{:S(2)}, u32[]{:S(2)}) %collective-permute-start.15) | collective-permute-done | bytes 829472 | tf_op jit(solution)/shard_map/ppermute | solution.py:31
  77.1 3.1 %text_first.1 = (f32[96,1152]{1,0:T(8,128)S(1)}, bf16[96,1152]{1,0:T(8,128)(2,1)S(1)}, bf16[96,1152]{1,0:T(8,128)(2,1)S(1)}, bf16[96,1152]{1,0:T(8,128)(2,1)S(1)}) custom-call(f32[352,1152]{1,0:T(8,128)S(1)} %text_near.1.own_ref, bf16[360,1152]{1,0:T(8,128)(2,1)S(1)} %collective-permute-done.14.r2_ref, bf16[360,1152]{1,0:T(8,128)(2,1)S(1)} %collective-permute-done.15.r3_ref, ...), custom_call_target="tpu_custom_call" | custom-call | bytes 4423680 | tf_op jit(solution)/shard_map/text_first/pallas_call | solution.py:242
  80.7 1.7 %collective-permute-start.20 = (bf16[96,1152]{1,0:T(8,128)(2,1)S(1)}, bf16[96,1152]{1,0:T(8,128)(2,1)S(1)}, u32[]{:S(2)}, u32[]{:S(2)}) collective-permute-start(bf16[96,1152]{1,0:T(8,128)(2,1)S(1)} %get-tuple-element.56), channel_id=1, source_target_pairs={{0,32},{1,65},{2,34},{3,67},{4,36},{5,69},{6,38},{7,71},{8,40},{9,... | collective-permute-start | bytes 663560 | tf_op jit(solution)/shard_map/ppermute | solution.py:31
  82.3 1.7 %collective-permute-start.21 = (bf16[96,1152]{1,0:T(8,128)(2,1)S(1)}, bf16[96,1152]{1,0:T(8,128)(2,1)S(1)}, u32[]{:S(2)}, u32[]{:S(2)}) collective-permute-start(bf16[96,1152]{1,0:T(8,128)(2,1)S(1)} %get-tuple-element.57), channel_id=1, source_target_pairs={{0,48},{1,67},{2,50},{3,65},{4,52},{5,71},{6,54},{7,69},{8,56},{9,... | collective-permute-start | bytes 663560 | tf_op jit(solution)/shard_map/ppermute | solution.py:31
  84.3 1.0 collective-permute-done.19.r1_ref
  85.3 3.1 %collective-permute-done.20.r2_ref = bf16[96,1152]{1,0:T(8,128)(2,1)S(1)} collective-permute-done((bf16[96,1152]{1,0:T(8,128)(2,1)S(1)}, bf16[96,1152]{1,0:T(8,128)(2,1)S(1)}, u32[]{:S(2)}, u32[]{:S(2)}) %collective-permute-start.20) | collective-permute-done | bytes 221216 | tf_op jit(solution)/shard_map/ppermute | solution.py:31
  88.4 2.3 %collective-permute-done.21.r3_ref = bf16[96,1152]{1,0:T(8,128)(2,1)S(1)} collective-permute-done((bf16[96,1152]{1,0:T(8,128)(2,1)S(1)}, bf16[96,1152]{1,0:T(8,128)(2,1)S(1)}, u32[]{:S(2)}, u32[]{:S(2)}) %collective-permute-start.21) | collective-permute-done | bytes 221216 | tf_op jit(solution)/shard_map/ppermute | solution.py:31
  90.7 0.6 text_last.1
  91.8 1.5 %collective-permute-start.26 = (f32[8,128]{1,0:T(8,128)S(1)}, f32[8,128]{1,0:T(8,128)S(1)}, u32[]{:S(2)}, u32[]{:S(2)}) collective-permute-start(f32[8,128]{1,0:T(8,128)S(1)} %get-tuple-element.62), channel_id=1, source_target_pairs={{0,66},{1,49},{2,64},{3,51},{4,70},{5,53},{6,68},{7,55},{8,74},{9,... | collective-permute-start | bytes 12296 | tf_op jit(solution)/shard_map/ppermute | solution.py:31
  93.3 1.3 %collective-permute-start.25 = (f32[8,128]{1,0:T(8,128)S(1)}, f32[8,128]{1,0:T(8,128)S(1)}, u32[]{:S(2)}, u32[]{:S(2)}) collective-permute-start(f32[8,128]{1,0:T(8,128)S(1)} %get-tuple-element.62), channel_id=1, source_target_pairs={{0,64},{1,33},{2,66},{3,35},{4,68},{5,37},{6,70},{7,39},{8,72},{9,... | collective-permute-start | bytes 12296 | tf_op jit(solution)/shard_map/ppermute | solution.py:31
  94.6 0.5 collective-permute-start.24
  95.3 3.1 %collective-permute-start.23 = (f32[352,288]{0,1:T(8,128)S(1)}, f32[352,288]{0,1:T(8,128)S(1)}, u32[]{:S(2)}, u32[]{:S(2)}) collective-permute-start(f32[352,288]{0,1:T(8,128)S(1)} %copy.17), channel_id=1, source_target_pairs={{0,1},{1,0},{2,3},{3,2},{4,5},{5,4},{6,7},{7,6},{8,9},{9,8},{10,11... | collective-permute-start | bytes 1216520 | tf_op jit(solution)/shard_map/ppermute | solution.py:31
  99.0 0.9 collective-permute-done.23
  100.4 1.0 copy.21
  101.4 1.0 copy.20
  (45 shorter events, 5.5 us)
Async XLA Ops:
  3.5 2.7 %collective-permute-start = (bf16[352,288]{1,0:T(8,128)(2,1)S(1)}, bf16[352,288]{1,0:T(8,128)(2,1)S(1)}, u32[]{:S(2)}, u32[]{:S(2)}) collective-permute-start(bf16[352,288]{1,0:T(8,128)(2,1)S(1)} %broadcast_select_fusion.2), channel_id=1, source_target_pairs={{0,1},{1,0},{2,3},{3,2},{4,5},{5,4},{6,7},{7,6},{8,9},{9,8},{10,11... | collective-permute-start | bytes 608264 | tf_op jit(solution)/shard_map/ppermute | solution.py:31
  6.6 5.8 %collective-permute-start.6 = (bf16[88,576]{1,0:T(8,128)(2,1)S(1)}, bf16[88,576]{1,0:T(8,128)(2,1)S(1)}, u32[]{:S(2)}, u32[]{:S(2)}) collective-permute-start(bf16[88,576]{1,0:T(8,128)(2,1)S(1)} %get-tuple-element.83), channel_id=1, source_target_pairs={{0,2},{1,3},{2,0},{3,1},{4,6},{5,7},{6,4},{7,5},{8,10},{9,11},{10,... | collective-permute-start | bytes 304136 | tf_op jit(solution)/shard_map/ppermute | solution.py:31
  8.6 8.7 %collective-permute-start.2 = (bf16[88,1152]{1,0:T(8,128)(2,1)S(1)}, bf16[88,1152]{1,0:T(8,128)(2,1)S(1)}, u32[]{:S(2)}, u32[]{:S(2)}) collective-permute-start(bf16[88,1152]{1,0:T(8,128)(2,1)S(1)} %pad_maximum_fusion.7), channel_id=1, source_target_pairs={{0,32},{1,65},{2,34},{3,67},{4,36},{5,69},{6,38},{7,71},{8,40},{9,... | collective-permute-start | bytes 608264 | tf_op jit(solution)/shard_map/ppermute | solution.py:31
  12.0 6.6 %collective-permute-start.1 = (bf16[88,1152]{1,0:T(8,128)(2,1)S(1)}, bf16[88,1152]{1,0:T(8,128)(2,1)S(1)}, u32[]{:S(2)}, u32[]{:S(2)}) collective-permute-start(bf16[88,1152]{1,0:T(8,128)(2,1)S(1)} %pad_maximum_fusion.7), channel_id=1, source_target_pairs={{0,16},{1,3},{2,18},{3,1},{4,20},{5,7},{6,22},{7,5},{8,24},{9,11},... | collective-permute-start | bytes 608264 | tf_op jit(solution)/shard_map/ppermute | solution.py:31
  12.0 7.6 %collective-permute-start.3 = (bf16[88,1152]{1,0:T(8,128)(2,1)S(1)}, bf16[88,1152]{1,0:T(8,128)(2,1)S(1)}, u32[]{:S(2)}, u32[]{:S(2)}) collective-permute-start(bf16[88,1152]{1,0:T(8,128)(2,1)S(1)} %pad_maximum_fusion.7), channel_id=1, source_target_pairs={{0,48},{1,67},{2,50},{3,65},{4,52},{5,71},{6,54},{7,69},{8,56},{9,... | collective-permute-start | bytes 608264 | tf_op jit(solution)/shard_map/ppermute | solution.py:31
  12.5 11.1 %collective-permute-start.9 = (bf16[88,1152]{1,0:T(8,128)(2,1)S(1)}, bf16[88,1152]{1,0:T(8,128)(2,1)S(1)}, u32[]{:S(2)}, u32[]{:S(2)}) collective-permute-start(bf16[88,1152]{1,0:T(8,128)(2,1)S(1)} %pad_maximum_fusion.8), channel_id=1, source_target_pairs={{0,12},{1,13},{2,14},{3,15},{4,8},{5,9},{6,10},{7,11},{8,4},{9,5},... | collective-permute-start | bytes 608264 | tf_op jit(solution)/shard_map/ppermute | solution.py:31
  15.0 8.5 %collective-permute-start.8 = (bf16[88,1152]{1,0:T(8,128)(2,1)S(1)}, bf16[88,1152]{1,0:T(8,128)(2,1)S(1)}, u32[]{:S(2)}, u32[]{:S(2)}) collective-permute-start(bf16[88,1152]{1,0:T(8,128)(2,1)S(1)} %pad_maximum_fusion.8), channel_id=1, source_target_pairs={{0,8},{1,9},{2,10},{3,11},{4,12},{5,13},{6,14},{7,15},{8,0},{9,1},... | collective-permute-start | bytes 608264 | tf_op jit(solution)/shard_map/ppermute | solution.py:31
  17.3 7.0 %collective-permute-start.7 = (bf16[88,1152]{1,0:T(8,128)(2,1)S(1)}, bf16[88,1152]{1,0:T(8,128)(2,1)S(1)}, u32[]{:S(2)}, u32[]{:S(2)}) collective-permute-start(bf16[88,1152]{1,0:T(8,128)(2,1)S(1)} %pad_maximum_fusion.8), channel_id=1, source_target_pairs={{0,4},{1,5},{2,6},{3,7},{4,0},{5,1},{6,2},{7,3},{8,12},{9,13},{10,... | collective-permute-start | bytes 608264 | tf_op jit(solution)/shard_map/ppermute | solution.py:31
  19.7 12.8 %collective-permute-start.5 = (bf16[4,88,1152]{2,1,0:T(8,128)(2,1)S(1)}, bf16[4,88,1152]{2,1,0:T(8,128)(2,1)S(1)}, u32[]{:S(2)}, u32[]{:S(2)}) collective-permute-start(bf16[4,88,1152]{2,1,0:T(8,128)(2,1)S(1)} %pad_maximum_fusion.1.ta_ref), channel_id=1, source_target_pairs={{0,66},{1,49},{2,64},{3,51},{4,70},{5,53},{6,68},{7,55},{8,74},{9,... | collective-permute-start | bytes 2433032 | tf_op jit(solution)/shard_map/ppermute | solution.py:31
  22.5 11.4 %collective-permute-start.4 = (bf16[4,88,1152]{2,1,0:T(8,128)(2,1)S(1)}, bf16[4,88,1152]{2,1,0:T(8,128)(2,1)S(1)}, u32[]{:S(2)}, u32[]{:S(2)}) collective-permute-start(bf16[4,88,1152]{2,1,0:T(8,128)(2,1)S(1)} %pad_maximum_fusion.1.ta_ref), channel_id=1, source_target_pairs={{0,2},{1,17},{2,0},{3,19},{4,6},{5,21},{6,4},{7,23},{8,10},{9,25},... | collective-permute-start | bytes 2433032 | tf_op jit(solution)/shard_map/ppermute | solution.py:31
  24.4 9.5 %collective-permute-start.10 = (bf16[352,1152]{1,0:T(8,128)(2,1)S(1)}, bf16[352,1152]{1,0:T(8,128)(2,1)S(1)}, u32[]{:S(2)}, u32[]{:S(2)}) collective-permute-start(bf16[352,1152]{1,0:T(8,128)(2,1)S(1)} %pad_maximum_fusion.2.im0_ref), channel_id=1, source_target_pairs={{0,1},{1,0},{2,3},{3,2},{4,5},{5,4},{6,7},{7,6},{8,9},{9,8},{10,11... | collective-permute-start | bytes 2433032 | tf_op jit(solution)/shard_map/ppermute | solution.py:31
  27.8 14.6 %collective-permute-start.11 = (bf16[4,88,1152]{2,1,0:T(8,128)(2,1)S(1)}, bf16[4,88,1152]{2,1,0:T(8,128)(2,1)S(1)}, u32[]{:S(2)}, u32[]{:S(2)}) collective-permute-start(bf16[4,88,1152]{2,1,0:T(8,128)(2,1)S(1)} %pad_maximum_fusion.1.ta_ref), channel_id=1, source_target_pairs={{0,64},{1,33},{2,66},{3,35},{4,68},{5,37},{6,70},{7,39},{8,72},{9,... | collective-permute-start | bytes 2433032 | tf_op jit(solution)/shard_map/ppermute | solution.py:31
  41.1 11.9 %collective-permute-start.12 = (bf16[360,1152]{1,0:T(8,128)(2,1)S(1)}, bf16[360,1152]{1,0:T(8,128)(2,1)S(1)}, u32[]{:S(2)}, u32[]{:S(2)}) collective-permute-start(bf16[360,1152]{1,0:T(8,128)(2,1)S(1)} %get-tuple-element.43), channel_id=1, source_target_pairs={{0,2},{1,17},{2,0},{3,19},{4,6},{5,21},{6,4},{7,23},{8,10},{9,25},... | collective-permute-start | bytes 2488328 | tf_op jit(solution)/shard_map/ppermute | solution.py:31
  53.0 5.2 %collective-permute-start.13 = (f32[360,1152]{1,0:T(8,128)S(1)}, f32[360,1152]{1,0:T(8,128)S(1)}, u32[]{:S(2)}, u32[]{:S(2)}) collective-permute-start(f32[360,1152]{1,0:T(8,128)S(1)} %get-tuple-element.44), channel_id=1, source_target_pairs={{0,1},{1,0},{2,3},{3,2},{4,5},{5,4},{6,7},{7,6},{8,9},{9,8},{10,11... | collective-permute-start | bytes 4976648 | tf_op jit(solution)/shard_map/ppermute | solution.py:31
  55.1 20.6 %collective-permute-start.14 = (bf16[360,1152]{1,0:T(8,128)(2,1)S(1)}, bf16[360,1152]{1,0:T(8,128)(2,1)S(1)}, u32[]{:S(2)}, u32[]{:S(2)}) collective-permute-start(bf16[360,1152]{1,0:T(8,128)(2,1)S(1)} %get-tuple-element.50), channel_id=1, source_target_pairs={{0,64},{1,33},{2,66},{3,35},{4,68},{5,37},{6,70},{7,39},{8,72},{9,... | collective-permute-start | bytes 2488328 | tf_op jit(solution)/shard_map/ppermute | solution.py:31
  56.7 20.3 %collective-permute-start.15 = (bf16[360,1152]{1,0:T(8,128)(2,1)S(1)}, bf16[360,1152]{1,0:T(8,128)(2,1)S(1)}, u32[]{:S(2)}, u32[]{:S(2)}) collective-permute-start(bf16[360,1152]{1,0:T(8,128)(2,1)S(1)} %get-tuple-element.51), channel_id=1, source_target_pairs={{0,66},{1,49},{2,64},{3,51},{4,70},{5,53},{6,68},{7,55},{8,74},{9,... | collective-permute-start | bytes 2488328 | tf_op jit(solution)/shard_map/ppermute | solution.py:31
  59.2 6.5 %collective-permute-start.16 = (bf16[96,1152]{1,0:T(8,128)(2,1)S(1)}, bf16[96,1152]{1,0:T(8,128)(2,1)S(1)}, u32[]{:S(2)}, u32[]{:S(2)}) collective-permute-start(bf16[96,1152]{1,0:T(8,128)(2,1)S(1)} %get-tuple-element.45), channel_id=1, source_target_pairs={{0,4},{1,5},{2,6},{3,7},{4,0},{5,1},{6,2},{7,3},{8,12},{9,13},{10,... | collective-permute-start | bytes 663560 | tf_op jit(solution)/shard_map/ppermute | solution.py:31
  60.5 12.2 %collective-permute-start.17 = (bf16[96,1152]{1,0:T(8,128)(2,1)S(1)}, bf16[96,1152]{1,0:T(8,128)(2,1)S(1)}, u32[]{:S(2)}, u32[]{:S(2)}) collective-permute-start(bf16[96,1152]{1,0:T(8,128)(2,1)S(1)} %get-tuple-element.46), channel_id=1, source_target_pairs={{0,8},{1,9},{2,10},{3,11},{4,12},{5,13},{6,14},{7,15},{8,0},{9,1},... | collective-permute-start | bytes 663560 | tf_op jit(solution)/shard_map/ppermute | solution.py:31
  63.0 12.0 %collective-permute-start.18 = (bf16[96,1152]{1,0:T(8,128)(2,1)S(1)}, bf16[96,1152]{1,0:T(8,128)(2,1)S(1)}, u32[]{:S(2)}, u32[]{:S(2)}) collective-permute-start(bf16[96,1152]{1,0:T(8,128)(2,1)S(1)} %get-tuple-element.47), channel_id=1, source_target_pairs={{0,12},{1,13},{2,14},{3,15},{4,8},{5,9},{6,10},{7,11},{8,4},{9,5},... | collective-permute-start | bytes 663560 | tf_op jit(solution)/shard_map/ppermute | solution.py:31
  80.1 5.2 %collective-permute-start.19 = (bf16[96,1152]{1,0:T(8,128)(2,1)S(1)}, bf16[96,1152]{1,0:T(8,128)(2,1)S(1)}, u32[]{:S(2)}, u32[]{:S(2)}) collective-permute-start(bf16[96,1152]{1,0:T(8,128)(2,1)S(1)} %get-tuple-element.55), channel_id=1, source_target_pairs={{0,16},{1,3},{2,18},{3,1},{4,20},{5,7},{6,22},{7,5},{8,24},{9,11},... | collective-permute-start | bytes 663560 | tf_op jit(solution)/shard_map/ppermute | solution.py:31
  80.7 7.7 %collective-permute-start.20 = (bf16[96,1152]{1,0:T(8,128)(2,1)S(1)}, bf16[96,1152]{1,0:T(8,128)(2,1)S(1)}, u32[]{:S(2)}, u32[]{:S(2)}) collective-permute-start(bf16[96,1152]{1,0:T(8,128)(2,1)S(1)} %get-tuple-element.56), channel_id=1, source_target_pairs={{0,32},{1,65},{2,34},{3,67},{4,36},{5,69},{6,38},{7,71},{8,40},{9,... | collective-permute-start | bytes 663560 | tf_op jit(solution)/shard_map/ppermute | solution.py:31
  82.3 8.4 %collective-permute-start.21 = (bf16[96,1152]{1,0:T(8,128)(2,1)S(1)}, bf16[96,1152]{1,0:T(8,128)(2,1)S(1)}, u32[]{:S(2)}, u32[]{:S(2)}) collective-permute-start(bf16[96,1152]{1,0:T(8,128)(2,1)S(1)} %get-tuple-element.57), channel_id=1, source_target_pairs={{0,48},{1,67},{2,50},{3,65},{4,52},{5,71},{6,54},{7,69},{8,56},{9,... | collective-permute-start | bytes 663560 | tf_op jit(solution)/shard_map/ppermute | solution.py:31
  84.2 7.1 %collective-permute-start.22 = (f32[88,576]{1,0:T(8,128)S(1)}, f32[88,576]{1,0:T(8,128)S(1)}, u32[]{:S(2)}, u32[]{:S(2)}) collective-permute-start(f32[88,576]{1,0:T(8,128)S(1)} %slice.68), channel_id=1, source_target_pairs={{0,2},{1,3},{2,0},{3,1},{4,6},{5,7},{6,4},{7,5},{8,10},{9,11},{10,... | collective-permute-start | bytes 608264 | tf_op jit(solution)/shard_map/ppermute | solution.py:31
  91.8 6.7 %collective-permute-start.26 = (f32[8,128]{1,0:T(8,128)S(1)}, f32[8,128]{1,0:T(8,128)S(1)}, u32[]{:S(2)}, u32[]{:S(2)}) collective-permute-start(f32[8,128]{1,0:T(8,128)S(1)} %get-tuple-element.62), channel_id=1, source_target_pairs={{0,66},{1,49},{2,64},{3,51},{4,70},{5,53},{6,68},{7,55},{8,74},{9,... | collective-permute-start | bytes 12296 | tf_op jit(solution)/shard_map/ppermute | solution.py:31
  93.3 5.1 %collective-permute-start.25 = (f32[8,128]{1,0:T(8,128)S(1)}, f32[8,128]{1,0:T(8,128)S(1)}, u32[]{:S(2)}, u32[]{:S(2)}) collective-permute-start(f32[8,128]{1,0:T(8,128)S(1)} %get-tuple-element.62), channel_id=1, source_target_pairs={{0,64},{1,33},{2,66},{3,35},{4,68},{5,37},{6,70},{7,39},{8,72},{9,... | collective-permute-start | bytes 12296 | tf_op jit(solution)/shard_map/ppermute | solution.py:31
  94.6 3.9 %collective-permute-start.24 = (f32[8,128]{1,0:T(8,128)S(1)}, f32[8,128]{1,0:T(8,128)S(1)}, u32[]{:S(2)}, u32[]{:S(2)}) collective-permute-start(f32[8,128]{1,0:T(8,128)S(1)} %get-tuple-element.62), channel_id=1, source_target_pairs={{0,2},{1,17},{2,0},{3,19},{4,6},{5,21},{6,4},{7,23},{8,10},{9,25},... | collective-permute-start | bytes 12296 | tf_op jit(solution)/shard_map/ppermute | solution.py:31
  95.3 4.6 %collective-permute-start.23 = (f32[352,288]{0,1:T(8,128)S(1)}, f32[352,288]{0,1:T(8,128)S(1)}, u32[]{:S(2)}, u32[]{:S(2)}) collective-permute-start(f32[352,288]{0,1:T(8,128)S(1)} %copy.17), channel_id=1, source_target_pairs={{0,1},{1,0},{2,3},{3,2},{4,5},{5,4},{6,7},{7,6},{8,9},{9,8},{10,11... | collective-permute-start | bytes 1216520 | tf_op jit(solution)/shard_map/ppermute | solution.py:31

commit v10 on v9

--- a/solution.py
+++ b/solution.py
@@ -100,6 +100,22 @@
     return lax.dot_general(coeff_low[...], t_rel[...], (((0,), (0,)), ((), ())), preferred_element_type=F32)
 
 
+def split_kernel(rows, info_ref, texts_ref, images_ref, keep_ref, send_ref):
+    on0, step = info_ref[0] == 0, 2 * rows
+    for at, ref in ((0, texts_ref), (step, images_ref)):
+        whole = ref[...].astype(F32).T
+        first, second = whole[:step], whole[step:]
+        keep_ref[at : at + step, :] = jnp.where(on0, first, second).astype(BF)
+        send_ref[at : at + step, :] = jnp.where(on0, second, first).astype(BF)
+
+
+def join_kernel(rows, info_ref, own_ref, got_ref, texts_ref, images_ref):
+    on0, step = info_ref[0] == 0, 2 * rows
+    for at, ref in ((0, texts_ref), (step, images_ref)):
+        own, got = own_ref[at : at + step, :], got_ref[at : at + step, :]
+        ref[...] = jnp.concatenate([jnp.where(on0, own, got), jnp.where(on0, got, own)], axis=0).T
+
+
 def near_kernel(
     rows, half, feats, info_ref, scale_ref, ta_ref, tb_ref, im0_ref, im1_ref,
     own_ref, m_ref, acc_ref, sums_ref, images, t_rel, coeff_low, grads,
@@ -217,21 +233,6 @@
     def by(first_one, own, other):
         return [jnp.where(first_one, own, other), jnp.where(first_one, other, own)]
 
-    both = [jnp.concatenate([t[:step], i[:step]]) for t, i in ((caption_embeds, picture_embeds),)]
-    both.append(jnp.concatenate([caption_embeds[step:], picture_embeds[step:]]))
-    keep, send = by(on0, *both)
-    chip = jnp.concatenate(by(on0, keep, swap(send, CORE)), axis=1)
-    packed = jnp.concatenate([chip[:rows], chip[rows:step]], axis=1)
-    keep, send = by(lo0, chip[step : step + rows], chip[step + rows :])
-    first = [packed] + [swap(packed, y_mask(i), z_mask(i)) for i in range(1, 4)]
-    image = jnp.concatenate([keep, swap(send, z_mask(1))], axis=1)
-    stack = jnp.stack(first)
-    second1, second3 = (swap(stack, z_mask(j), y_mask(j)) for j in (1, 3))
-    images_own = jnp.concatenate([image] + [swap(image, x_mask(k)) for k in range(1, 4)], axis=0)
-    images_other = swap(images_own, CORE)
-    second2 = swap(after(stack, images_own), z_mask(2), y_mask(2))
-    second1, second3 = lax.optimization_barrier((second1, second3))
-
     def f32(*shape):
         return jax.ShapeDtypeStruct(shape, F32)
 
@@ -254,8 +255,23 @@
             name=name,
         )(*args)
 
+    info = jnp.stack([core, z_lo]).astype(jnp.int32)
+    keep, send = call(
+        functools.partial(split_kernel, rows), "split", [bf16(height, width)] * 2, info, caption_embeds.T, picture_embeds.T, scalars=1
+    )
+    chip = jnp.concatenate(by(on0, keep, swap(send, CORE)), axis=1)
+    packed = jnp.concatenate([chip[:rows], chip[rows:step]], axis=1)
+    keep, send = by(lo0, chip[step : step + rows], chip[step + rows :])
+    first = [packed] + [swap(packed, y_mask(i), z_mask(i)) for i in range(1, 4)]
+    image = jnp.concatenate([keep, swap(send, z_mask(1))], axis=1)
+    stack = jnp.stack(first)
+    second1, second3 = (swap(stack, z_mask(j), y_mask(j)) for j in (1, 3))
+    images_own = jnp.concatenate([image] + [swap(image, x_mask(k)) for k in range(1, 4)], axis=0)
+    images_other = swap(images_own, CORE)
+    second2 = swap(after(stack, images_own), z_mask(2), y_mask(2))
+    second1, second3 = lax.optimization_barrier((second1, second3))
+
     sizes = (rows, half, feats)
-    info = jnp.stack([core, z_lo]).astype(jnp.int32)
     scales = jnp.stack([scaling, logit_offset_term[0]])
     images_shape, coeff_shape = (2 * quarter, feats), (2 * quarter, 2 * quarter)
     grads = pltpu.VMEM((2, 4, rows, feats), F32)
@@ -273,7 +289,7 @@
         scalars=2, mib=40, products=3, scratch=scratch,
     )
     got1 = swap(m1, z_mask(1), y_mask(1))
-    m2, m3, img_other, got1 = lax.optimization_barrier((m2, m3, img_other, got1))
+    img_other, got1 = lax.optimization_barrier((img_other, got1))
     got2, got3 = swap(m2, z_mask(2), y_mask(2)), swap(m3, z_mask(3), y_mask(3))
     img, *messages = call(
         functools.partial(image_first_kernel, rows, feats), "image_first",
@@ -298,11 +314,13 @@
     mine, other = by(on0, whole[:, :width], whole[:, width:])
     sums = after(sums, other)
     other = swap(other, CORE)
-    text_grad = jnp.concatenate(by(on0, mine[:step], other[:step]), axis=0)
-    image_grad = jnp.concatenate(by(on0, mine[step:], other[step:]), axis=0)
-    s1, s2, s3 = (swap(sums, z_mask(k), y_mask(k)) for k in (1, 2, 3))
-    sums = (sums + s1) + (s2 + s3)
-    return (image_grad, text_grad, sums[0, :2])
+    sums = sums + swap(sums, z_mask(1), y_mask(1))
+    mine = after(mine, sums)
+    text_grad, image_grad = call(
+        functools.partial(join_kernel, rows), "join", [f32(width, height)] * 2, info, mine, other, scalars=1
+    )
+    sums = sums + after(swap(sums, z_mask(3), y_mask(3)), text_grad, image_grad)
+    return (image_grad.T, text_grad.T, sums[0, :2])
 
 
 def solution(mesh):

time: 103 us -> 102 us (level)
  local copies, waits for them, and re-layouts: 5.92 us -> 2.92 us
  starting transfers between devices: 38.2 us -> 35.2 us
  Pallas kernels: 21.7 us -> 24.2 us
  waiting for transfers between devices: 32.7 us -> 34.9 us
    ppermute x27 -> x26, starting transfers between devices: 38.2 us -> 35.2 us  [swap(): lax.ppermute(array, AXES, [(i, i ^ (mask1 if i & 1 else mask0)) for i in...]
    pallas_call x7 -> x9, Pallas kernels: 21.7 us -> 24.2 us  [call(): pl.pallas_call(kernel, out_shape=out_shape, in_specs=[SMEM] * scalars + [...]
    slice x3 -> x0, local copies, waits for them, and re-layouts: 2.33 us -> none  [the longest x1 1.1 us: body(): t[:step]]
    ppermute x27 -> x26, waiting for transfers between devices: 32.7 us -> 34.9 us  [swap(): lax.ppermute(array, AXES, [(i, i ^ (mask1 if i & 1 else mask0)) for i in...]
    unnamed x8 -> x4, local copies, waits for them, and re-layouts: 2.77 us -> 1.87 us
  transfers between devices with their start and end apart: 27 -> 26, of which waited for: 18 -> 19; matrix products, arithmetic and copies ran while one was open for 1% -> 1% of each run, Pallas kernels for 18% -> 20%
where the time goes in v10:
time: 102 us; the launch traced here: 101 us
  starting transfers between devices  35.2 us (35%)
  waiting for transfers between devices  34.9 us (34%)
  Pallas kernels  24.2 us (24%)
  local copies, waits for them, and re-layouts  2.92 us (3%)
  between operations  2.1 us (2%)
  other arithmetic  1.34 us (1%)
    ppermute x26, starting transfers between devices, swap(): lax.ppermute(array, AXES, [(i, i ^ (mask1 if i & 1 else mask0)) for i in...  35.2 us
    ppermute x26, waiting for transfers between devices, swap(): lax.ppermute(array, AXES, [(i, i ^ (mask1 if i & 1 else mask0)) for i in...  34.9 us
    pallas_call x9, Pallas kernels, call(): pl.pallas_call(kernel, out_shape=out_shape, in_specs=[SMEM] * scalars + [...  24.2 us
  transfers between devices with their start and end apart: 26, of which 19 were waited for; matrix products, arithmetic and copies ran while one was open for 1% of the time, Pallas kernels for 20%

profile of v10, /device:TPU:1, one launch (start us, length us, event | category | flops | bytes accessed | tf_op | source)
XLA Modules:
  0.0 100.7 jit_solution(7876624532819858703)
XLA Ops:
  0.7 0.9 copy-done
  1.7 0.9 copy-done.1
  2.6 0.8 split.1
  3.4 1.5 %collective-permute-start = (bf16[352,288]{1,0:T(8,128)(2,1)S(1)}, bf16[352,288]{1,0:T(8,128)(2,1)S(1)}, u32[]{:S(2)}, u32[]{:S(2)}) collective-permute-start(bf16[352,288]{1,0:T(8,128)(2,1)S(1)} %get-tuple-element.38), channel_id=1, source_target_pairs={{0,1},{1,0},{2,3},{3,2},{4,5},{5,4},{6,7},{7,6},{8,9},{9,8},{10,11... | collective-permute-start | bytes 608264 | tf_op jit(solution)/shard_map/ppermute | solution.py:31
  4.9 1.2 %collective-permute-done = bf16[352,288]{1,0:T(8,128)(2,1)S(1)} collective-permute-done((bf16[352,288]{1,0:T(8,128)(2,1)S(1)}, bf16[352,288]{1,0:T(8,128)(2,1)S(1)}, u32[]{:S(2)}, u32[]{:S(2)}) %collective-permute-start) | collective-permute-done | bytes 202784 | tf_op jit(solution)/shard_map/ppermute | solution.py:31
  6.3 1.8 %collective-permute-start.6 = (bf16[88,576]{1,0:T(8,128)(2,1)S(1)}, bf16[88,576]{1,0:T(8,128)(2,1)S(1)}, u32[]{:S(2)}, u32[]{:S(2)}) collective-permute-start(bf16[88,576]{1,0:T(8,128)(2,1)S(1)} %get-tuple-element.77), channel_id=1, source_target_pairs={{0,2},{1,3},{2,0},{3,1},{4,6},{5,7},{6,4},{7,5},{8,10},{9,11},{10,... | collective-permute-start | bytes 304136 | tf_op jit(solution)/shard_map/ppermute | solution.py:31
  8.4 3.4 %collective-permute-start.2 = (bf16[88,1152]{1,0:T(8,128)(2,1)S(1)}, bf16[88,1152]{1,0:T(8,128)(2,1)S(1)}, u32[]{:S(2)}, u32[]{:S(2)}) collective-permute-start(bf16[88,1152]{1,0:T(8,128)(2,1)S(1)} %pad_maximum_fusion.3), channel_id=1, source_target_pairs={{0,32},{1,65},{2,34},{3,67},{4,36},{5,69},{6,38},{7,71},{8,40},{9,... | collective-permute-start | bytes 608264 | tf_op jit(solution)/shard_map/ppermute | solution.py:31
  12.2 2.6 %collective-permute-start.9 = (bf16[88,1152]{1,0:T(8,128)(2,1)S(1)}, bf16[88,1152]{1,0:T(8,128)(2,1)S(1)}, u32[]{:S(2)}, u32[]{:S(2)}) collective-permute-start(bf16[88,1152]{1,0:T(8,128)(2,1)S(1)} %pad_maximum_fusion.4), channel_id=1, source_target_pairs={{0,12},{1,13},{2,14},{3,15},{4,8},{5,9},{6,10},{7,11},{8,4},{9,5},... | collective-permute-start | bytes 608264 | tf_op jit(solution)/shard_map/ppermute | solution.py:31
  15.3 1.8 %collective-permute-done.2 = bf16[88,1152]{1,0:T(8,128)(2,1)S(1)} collective-permute-done((bf16[88,1152]{1,0:T(8,128)(2,1)S(1)}, bf16[88,1152]{1,0:T(8,128)(2,1)S(1)}, u32[]{:S(2)}, u32[]{:S(2)}) %collective-permute-start.2) | collective-permute-done | bytes 202784 | tf_op jit(solution)/shard_map/ppermute | solution.py:31
  17.1 1.2 %collective-permute-start.7 = (bf16[88,1152]{1,0:T(8,128)(2,1)S(1)}, bf16[88,1152]{1,0:T(8,128)(2,1)S(1)}, u32[]{:S(2)}, u32[]{:S(2)}) collective-permute-start(bf16[88,1152]{1,0:T(8,128)(2,1)S(1)} %pad_maximum_fusion.4), channel_id=1, source_target_pairs={{0,4},{1,5},{2,6},{3,7},{4,0},{5,1},{6,2},{7,3},{8,12},{9,13},{10,... | collective-permute-start | bytes 608264 | tf_op jit(solution)/shard_map/ppermute | solution.py:31
  18.3 1.0 %collective-permute-done.3 = bf16[88,1152]{1,0:T(8,128)(2,1)S(1)} collective-permute-done((bf16[88,1152]{1,0:T(8,128)(2,1)S(1)}, bf16[88,1152]{1,0:T(8,128)(2,1)S(1)}, u32[]{:S(2)}, u32[]{:S(2)}) %collective-permute-start.3) | collective-permute-done | bytes 202784 | tf_op jit(solution)/shard_map/ppermute | solution.py:31
  19.5 2.8 %collective-permute-start.5 = (bf16[4,88,1152]{2,1,0:T(8,128)(2,1)S(1)}, bf16[4,88,1152]{2,1,0:T(8,128)(2,1)S(1)}, u32[]{:S(2)}, u32[]{:S(2)}) collective-permute-start(bf16[4,88,1152]{2,1,0:T(8,128)(2,1)S(1)} %pad_maximum_fusion.1.ta_ref), channel_id=1, source_target_pairs={{0,66},{1,49},{2,64},{3,51},{4,70},{5,53},{6,68},{7,55},{8,74},{9,... | collective-permute-start | bytes 2433032 | tf_op jit(solution)/shard_map/ppermute | solution.py:31
  22.3 1.1 %collective-permute-done.9 = bf16[88,1152]{1,0:T(8,128)(2,1)S(1)} collective-permute-done((bf16[88,1152]{1,0:T(8,128)(2,1)S(1)}, bf16[88,1152]{1,0:T(8,128)(2,1)S(1)}, u32[]{:S(2)}, u32[]{:S(2)}) %collective-permute-start.9) | collective-permute-done | bytes 202784 | tf_op jit(solution)/shard_map/ppermute | solution.py:31
  23.3 0.8 collective-permute-done.7
  24.2 1.9 %collective-permute-start.10 = (bf16[352,1152]{1,0:T(8,128)(2,1)S(1)}, bf16[352,1152]{1,0:T(8,128)(2,1)S(1)}, u32[]{:S(2)}, u32[]{:S(2)}) collective-permute-start(bf16[352,1152]{1,0:T(8,128)(2,1)S(1)} %pad_maximum_fusion.2.im0_ref), channel_id=1, source_target_pairs={{0,1},{1,0},{2,3},{3,2},{4,5},{5,4},{6,7},{7,6},{8,9},{9,8},{10,11... | collective-permute-start | bytes 2433032 | tf_op jit(solution)/shard_map/ppermute | solution.py:31
  27.5 2.9 %collective-permute-start.11 = (bf16[4,88,1152]{2,1,0:T(8,128)(2,1)S(1)}, bf16[4,88,1152]{2,1,0:T(8,128)(2,1)S(1)}, u32[]{:S(2)}, u32[]{:S(2)}) collective-permute-start(bf16[4,88,1152]{2,1,0:T(8,128)(2,1)S(1)} %pad_maximum_fusion.1.ta_ref), channel_id=1, source_target_pairs={{0,64},{1,33},{2,66},{3,35},{4,68},{5,37},{6,70},{7,39},{8,72},{9,... | collective-permute-start | bytes 2433032 | tf_op jit(solution)/shard_map/ppermute | solution.py:31
  30.4 1.8 %collective-permute-done.5.tb_ref = bf16[4,88,1152]{2,1,0:T(8,128)(2,1)S(1)} collective-permute-done((bf16[4,88,1152]{2,1,0:T(8,128)(2,1)S(1)}, bf16[4,88,1152]{2,1,0:T(8,128)(2,1)S(1)}, u32[]{:S(2)}, u32[]{:S(2)}) %collective-permute-start.5) | collective-permute-done | bytes 811040 | tf_op jit(solution)/shard_map/ppermute | solution.py:31
  32.2 1.5 %collective-permute-done.4.tb_ref = bf16[4,88,1152]{2,1,0:T(8,128)(2,1)S(1)} collective-permute-done((bf16[4,88,1152]{2,1,0:T(8,128)(2,1)S(1)}, bf16[4,88,1152]{2,1,0:T(8,128)(2,1)S(1)}, u32[]{:S(2)}, u32[]{:S(2)}) %collective-permute-start.4) | collective-permute-done | bytes 811040 | tf_op jit(solution)/shard_map/ppermute | solution.py:31
  33.7 7.2 %tile_near.1 = (f32[352,1152]{1,0:T(8,128)S(1)}, bf16[360,1152]{1,0:T(8,128)(2,1)S(1)}, f32[704,1152]{1,0:T(8,128)S(1)}, f32[8,128]{1,0:T(8,128)S(1)}) custom-call(s32[2]{0:T(128)S(1)} %pad_add_fusion.info_ref, f32[2]{0:T(128)S(1)} %pad_maximum_fusion.6.scale_ref, bf16[4,88,1152]{2,1,0:T(8,128)(2,1)S(1)} %pad_maximum_fusion.1.ta_ref, ...), custom_call_target="tpu_custom_call" | custom-call | flops 3425697792 | bytes 8943632 | tf_op jit(solution)/shard_map/tile_near/pallas_call | solution.py:243
  41.2 1.0 collective-permute-done.11.ta_ref
  42.2 8.4 %tile_far.1 = (bf16[360,1152]{1,0:T(8,128)(2,1)S(1)}, bf16[360,1152]{1,0:T(8,128)(2,1)S(1)}, f32[360,1152]{1,0:T(8,128)S(1)}, f32[360,1152]{1,0:T(8,128)S(1)}) custom-call(s32[2]{0:T(128)S(1)} %pad_add_fusion.info_ref, f32[2]{0:T(128)S(1)} %pad_maximum_fusion.6.scale_ref, bf16[4,88,1152]{2,1,0:T(8,128)(2,1)S(1)} %collective-permute-done.11.ta_ref, ...), custom_call_target="tpu_custom_call" | custom-call | flops 3425697792 | bytes 11468816 | tf_op jit(solution)/shard_map/tile_far/pallas_call | solution.py:243
  50.6 2.2 %collective-permute-done.12.r1_ref = bf16[360,1152]{1,0:T(8,128)(2,1)S(1)} collective-permute-done((bf16[360,1152]{1,0:T(8,128)(2,1)S(1)}, bf16[360,1152]{1,0:T(8,128)(2,1)S(1)}, u32[]{:S(2)}, u32[]{:S(2)}) %collective-permute-start.12) | collective-permute-done | bytes 829472 | tf_op jit(solution)/shard_map/ppermute | solution.py:31
  52.8 2.1 %collective-permute-start.13 = (f32[360,1152]{1,0:T(8,128)S(1)}, f32[360,1152]{1,0:T(8,128)S(1)}, u32[]{:S(2)}, u32[]{:S(2)}) collective-permute-start(f32[360,1152]{1,0:T(8,128)S(1)} %get-tuple-element.48), channel_id=1, source_target_pairs={{0,1},{1,0},{2,3},{3,2},{4,5},{5,4},{6,7},{7,6},{8,9},{9,8},{10,11... | collective-permute-start | bytes 4976648 | tf_op jit(solution)/shard_map/ppermute | solution.py:31
  54.8 1.6 %collective-permute-start.14 = (bf16[360,1152]{1,0:T(8,128)(2,1)S(1)}, bf16[360,1152]{1,0:T(8,128)(2,1)S(1)}, u32[]{:S(2)}, u32[]{:S(2)}) collective-permute-start(bf16[360,1152]{1,0:T(8,128)(2,1)S(1)} %get-tuple-element.54), channel_id=1, source_target_pairs={{0,64},{1,33},{2,66},{3,35},{4,68},{5,37},{6,70},{7,39},{8,72},{9,... | collective-permute-start | bytes 2488328 | tf_op jit(solution)/shard_map/ppermute | solution.py:31
  56.5 0.8 collective-permute-start.15
  57.3 0.7 collective-permute-done.13.other_ref
  58.0 1.0 image_first.1
  59.0 1.3 %collective-permute-start.16 = (bf16[96,1152]{1,0:T(8,128)(2,1)S(1)}, bf16[96,1152]{1,0:T(8,128)(2,1)S(1)}, u32[]{:S(2)}, u32[]{:S(2)}) collective-permute-start(bf16[96,1152]{1,0:T(8,128)(2,1)S(1)} %get-tuple-element.49), channel_id=1, source_target_pairs={{0,4},{1,5},{2,6},{3,7},{4,0},{5,1},{6,2},{7,3},{8,12},{9,13},{10,... | collective-permute-start | bytes 663560 | tf_op jit(solution)/shard_map/ppermute | solution.py:31
  60.3 2.4 %collective-permute-start.17 = (bf16[96,1152]{1,0:T(8,128)(2,1)S(1)}, bf16[96,1152]{1,0:T(8,128)(2,1)S(1)}, u32[]{:S(2)}, u32[]{:S(2)}) collective-permute-start(bf16[96,1152]{1,0:T(8,128)(2,1)S(1)} %get-tuple-element.50), channel_id=1, source_target_pairs={{0,8},{1,9},{2,10},{3,11},{4,12},{5,13},{6,14},{7,15},{8,0},{9,1},... | collective-permute-start | bytes 663560 | tf_op jit(solution)/shard_map/ppermute | solution.py:31
  62.9 0.8 text_near.1.own_ref
  63.7 1.8 %collective-permute-done.16.r1_ref = bf16[96,1152]{1,0:T(8,128)(2,1)S(1)} collective-permute-done((bf16[96,1152]{1,0:T(8,128)(2,1)S(1)}, bf16[96,1152]{1,0:T(8,128)(2,1)S(1)}, u32[]{:S(2)}, u32[]{:S(2)}) %collective-permute-start.16) | collective-permute-done | bytes 221216 | tf_op jit(solution)/shard_map/ppermute | solution.py:31
  65.5 7.0 %collective-permute-done.17.r2_ref = bf16[96,1152]{1,0:T(8,128)(2,1)S(1)} collective-permute-done((bf16[96,1152]{1,0:T(8,128)(2,1)S(1)}, bf16[96,1152]{1,0:T(8,128)(2,1)S(1)}, u32[]{:S(2)}, u32[]{:S(2)}) %collective-permute-start.17) | collective-permute-done | bytes 221216 | tf_op jit(solution)/shard_map/ppermute | solution.py:31
  72.5 2.3 %collective-permute-done.18.r3_ref = bf16[96,1152]{1,0:T(8,128)(2,1)S(1)} collective-permute-done((bf16[96,1152]{1,0:T(8,128)(2,1)S(1)}, bf16[96,1152]{1,0:T(8,128)(2,1)S(1)}, u32[]{:S(2)}, u32[]{:S(2)}) %collective-permute-start.18) | collective-permute-done | bytes 221216 | tf_op jit(solution)/shard_map/ppermute | solution.py:31
  74.8 0.6 image_last.1
  75.4 1.4 %collective-permute-done.15.r3_ref = bf16[360,1152]{1,0:T(8,128)(2,1)S(1)} collective-permute-done((bf16[360,1152]{1,0:T(8,128)(2,1)S(1)}, bf16[360,1152]{1,0:T(8,128)(2,1)S(1)}, u32[]{:S(2)}, u32[]{:S(2)}) %collective-permute-start.15) | collective-permute-done | bytes 829472 | tf_op jit(solution)/shard_map/ppermute | solution.py:31
  76.8 3.1 %text_first.1 = (f32[96,1152]{1,0:T(8,128)S(1)}, bf16[96,1152]{1,0:T(8,128)(2,1)S(1)}, bf16[96,1152]{1,0:T(8,128)(2,1)S(1)}, bf16[96,1152]{1,0:T(8,128)(2,1)S(1)}) custom-call(f32[352,1152]{1,0:T(8,128)S(1)} %text_near.1.own_ref, bf16[360,1152]{1,0:T(8,128)(2,1)S(1)} %collective-permute-done.14.r2_ref, bf16[360,1152]{1,0:T(8,128)(2,1)S(1)} %collective-permute-done.15.r3_ref, ...), custom_call_target="tpu_custom_call" | custom-call | bytes 4423680 | tf_op jit(solution)/shard_map/text_first/pallas_call | solution.py:243
  79.9 0.5 collective-permute-start.19
  80.4 1.7 %collective-permute-start.20 = (bf16[96,1152]{1,0:T(8,128)(2,1)S(1)}, bf16[96,1152]{1,0:T(8,128)(2,1)S(1)}, u32[]{:S(2)}, u32[]{:S(2)}) collective-permute-start(bf16[96,1152]{1,0:T(8,128)(2,1)S(1)} %get-tuple-element.60), channel_id=1, source_target_pairs={{0,32},{1,65},{2,34},{3,67},{4,36},{5,69},{6,38},{7,71},{8,40},{9,... | collective-permute-start | bytes 663560 | tf_op jit(solution)/shard_map/ppermute | solution.py:31
  82.1 1.7 %collective-permute-start.21 = (bf16[96,1152]{1,0:T(8,128)(2,1)S(1)}, bf16[96,1152]{1,0:T(8,128)(2,1)S(1)}, u32[]{:S(2)}, u32[]{:S(2)}) collective-permute-start(bf16[96,1152]{1,0:T(8,128)(2,1)S(1)} %get-tuple-element.61), channel_id=1, source_target_pairs={{0,48},{1,67},{2,50},{3,65},{4,52},{5,71},{6,54},{7,69},{8,56},{9,... | collective-permute-start | bytes 663560 | tf_op jit(solution)/shard_map/ppermute | solution.py:31
  84.1 1.0 collective-permute-done.19.r1_ref
  85.1 3.1 %collective-permute-done.20.r2_ref = bf16[96,1152]{1,0:T(8,128)(2,1)S(1)} collective-permute-done((bf16[96,1152]{1,0:T(8,128)(2,1)S(1)}, bf16[96,1152]{1,0:T(8,128)(2,1)S(1)}, u32[]{:S(2)}, u32[]{:S(2)}) %collective-permute-start.20) | collective-permute-done | bytes 221216 | tf_op jit(solution)/shard_map/ppermute | solution.py:31
  88.1 2.3 %collective-permute-done.21.r3_ref = bf16[96,1152]{1,0:T(8,128)(2,1)S(1)} collective-permute-done((bf16[96,1152]{1,0:T(8,128)(2,1)S(1)}, bf16[96,1152]{1,0:T(8,128)(2,1)S(1)}, u32[]{:S(2)}, u32[]{:S(2)}) %collective-permute-start.21) | collective-permute-done | bytes 221216 | tf_op jit(solution)/shard_map/ppermute | solution.py:31
  90.5 0.6 text_last.1
  91.7 2.3 %collective-permute-start.24 = (f32[352,288]{0,1:T(8,128)S(1)}, f32[352,288]{0,1:T(8,128)S(1)}, u32[]{:S(2)}, u32[]{:S(2)}) collective-permute-start(f32[352,288]{0,1:T(8,128)S(1)} %copy.7), channel_id=1, source_target_pairs={{0,1},{1,0},{2,3},{3,2},{4,5},{5,4},{6,7},{7,6},{8,9},{9,8},{10,11... | collective-permute-start | bytes 1216520 | tf_op jit(solution)/shard_map/ppermute | solution.py:31
  94.0 2.5 %collective-permute-done.23 = f32[8,128]{1,0:T(8,128)S(1)} collective-permute-done((f32[8,128]{1,0:T(8,128)S(1)}, f32[8,128]{1,0:T(8,128)S(1)}, u32[]{:S(2)}, u32[]{:S(2)}) %collective-permute-start.23) | collective-permute-done | bytes 4128 | tf_op jit(solution)/shard_map/ppermute | solution.py:31
  96.5 1.2 %collective-permute-start.25 = (f32[8,128]{1,0:T(8,128)S(1)}, f32[8,128]{1,0:T(8,128)S(1)}, u32[]{:S(2)}, u32[]{:S(2)}) collective-permute-start(f32[8,128]{1,0:T(8,128)S(1)} %add.10), channel_id=1, source_target_pairs={{0,66},{1,49},{2,64},{3,51},{4,70},{5,53},{6,68},{7,55},{8,74},{9,... | collective-permute-start | bytes 12296 | tf_op jit(solution)/shard_map/ppermute | solution.py:31
  97.9 1.7 %join.1 = (f32[288,352]{1,0:T(8,128)}, f32[288,352]{1,0:T(8,128)}) custom-call(s32[2]{0:T(128)S(1)} %pad_add_fusion.info_ref, f32[352,288]{1,0:T(8,128)S(1)} %get-tuple-element.67.own_ref, f32[352,288]{1,0:T(8,128)S(1)} %copy.8.got_ref), custom_call_target="tpu_custom_call" | custom-call | bytes 1622024 | tf_op jit(solution)/shard_map/join/pallas_call | solution.py:243
  99.6 0.5 collective-permute-done.25
  (36 shorter events, 3.9 us)
Async XLA Ops:
  0.7 0.9 copy-start
  1.6 0.9 copy-start.1
  3.4 2.7 %collective-permute-start = (bf16[352,288]{1,0:T(8,128)(2,1)S(1)}, bf16[352,288]{1,0:T(8,128)(2,1)S(1)}, u32[]{:S(2)}, u32[]{:S(2)}) collective-permute-start(bf16[352,288]{1,0:T(8,128)(2,1)S(1)} %get-tuple-element.38), channel_id=1, source_target_pairs={{0,1},{1,0},{2,3},{3,2},{4,5},{5,4},{6,7},{7,6},{8,9},{9,8},{10,11... | collective-permute-start | bytes 608264 | tf_op jit(solution)/shard_map/ppermute | solution.py:31
  6.3 5.8 %collective-permute-start.6 = (bf16[88,576]{1,0:T(8,128)(2,1)S(1)}, bf16[88,576]{1,0:T(8,128)(2,1)S(1)}, u32[]{:S(2)}, u32[]{:S(2)}) collective-permute-start(bf16[88,576]{1,0:T(8,128)(2,1)S(1)} %get-tuple-element.77), channel_id=1, source_target_pairs={{0,2},{1,3},{2,0},{3,1},{4,6},{5,7},{6,4},{7,5},{8,10},{9,11},{10,... | collective-permute-start | bytes 304136 | tf_op jit(solution)/shard_map/ppermute | solution.py:31
  8.4 8.7 %collective-permute-start.2 = (bf16[88,1152]{1,0:T(8,128)(2,1)S(1)}, bf16[88,1152]{1,0:T(8,128)(2,1)S(1)}, u32[]{:S(2)}, u32[]{:S(2)}) collective-permute-start(bf16[88,1152]{1,0:T(8,128)(2,1)S(1)} %pad_maximum_fusion.3), channel_id=1, source_target_pairs={{0,32},{1,65},{2,34},{3,67},{4,36},{5,69},{6,38},{7,71},{8,40},{9,... | collective-permute-start | bytes 608264 | tf_op jit(solution)/shard_map/ppermute | solution.py:31
  11.7 6.6 %collective-permute-start.1 = (bf16[88,1152]{1,0:T(8,128)(2,1)S(1)}, bf16[88,1152]{1,0:T(8,128)(2,1)S(1)}, u32[]{:S(2)}, u32[]{:S(2)}) collective-permute-start(bf16[88,1152]{1,0:T(8,128)(2,1)S(1)} %pad_maximum_fusion.3), channel_id=1, source_target_pairs={{0,16},{1,3},{2,18},{3,1},{4,20},{5,7},{6,22},{7,5},{8,24},{9,11},... | collective-permute-start | bytes 608264 | tf_op jit(solution)/shard_map/ppermute | solution.py:31
  11.7 7.6 %collective-permute-start.3 = (bf16[88,1152]{1,0:T(8,128)(2,1)S(1)}, bf16[88,1152]{1,0:T(8,128)(2,1)S(1)}, u32[]{:S(2)}, u32[]{:S(2)}) collective-permute-start(bf16[88,1152]{1,0:T(8,128)(2,1)S(1)} %pad_maximum_fusion.3), channel_id=1, source_target_pairs={{0,48},{1,67},{2,50},{3,65},{4,52},{5,71},{6,54},{7,69},{8,56},{9,... | collective-permute-start | bytes 608264 | tf_op jit(solution)/shard_map/ppermute | solution.py:31
  12.2 11.1 %collective-permute-start.9 = (bf16[88,1152]{1,0:T(8,128)(2,1)S(1)}, bf16[88,1152]{1,0:T(8,128)(2,1)S(1)}, u32[]{:S(2)}, u32[]{:S(2)}) collective-permute-start(bf16[88,1152]{1,0:T(8,128)(2,1)S(1)} %pad_maximum_fusion.4), channel_id=1, source_target_pairs={{0,12},{1,13},{2,14},{3,15},{4,8},{5,9},{6,10},{7,11},{8,4},{9,5},... | collective-permute-start | bytes 608264 | tf_op jit(solution)/shard_map/ppermute | solution.py:31
  14.8 8.5 %collective-permute-start.8 = (bf16[88,1152]{1,0:T(8,128)(2,1)S(1)}, bf16[88,1152]{1,0:T(8,128)(2,1)S(1)}, u32[]{:S(2)}, u32[]{:S(2)}) collective-permute-start(bf16[88,1152]{1,0:T(8,128)(2,1)S(1)} %pad_maximum_fusion.4), channel_id=1, source_target_pairs={{0,8},{1,9},{2,10},{3,11},{4,12},{5,13},{6,14},{7,15},{8,0},{9,1},... | collective-permute-start | bytes 608264 | tf_op jit(solution)/shard_map/ppermute | solution.py:31
  17.1 7.0 %collective-permute-start.7 = (bf16[88,1152]{1,0:T(8,128)(2,1)S(1)}, bf16[88,1152]{1,0:T(8,128)(2,1)S(1)}, u32[]{:S(2)}, u32[]{:S(2)}) collective-permute-start(bf16[88,1152]{1,0:T(8,128)(2,1)S(1)} %pad_maximum_fusion.4), channel_id=1, source_target_pairs={{0,4},{1,5},{2,6},{3,7},{4,0},{5,1},{6,2},{7,3},{8,12},{9,13},{10,... | collective-permute-start | bytes 608264 | tf_op jit(solution)/shard_map/ppermute | solution.py:31
  19.5 12.8 %collective-permute-start.5 = (bf16[4,88,1152]{2,1,0:T(8,128)(2,1)S(1)}, bf16[4,88,1152]{2,1,0:T(8,128)(2,1)S(1)}, u32[]{:S(2)}, u32[]{:S(2)}) collective-permute-start(bf16[4,88,1152]{2,1,0:T(8,128)(2,1)S(1)} %pad_maximum_fusion.1.ta_ref), channel_id=1, source_target_pairs={{0,66},{1,49},{2,64},{3,51},{4,70},{5,53},{6,68},{7,55},{8,74},{9,... | collective-permute-start | bytes 2433032 | tf_op jit(solution)/shard_map/ppermute | solution.py:31
  22.3 11.4 %collective-permute-start.4 = (bf16[4,88,1152]{2,1,0:T(8,128)(2,1)S(1)}, bf16[4,88,1152]{2,1,0:T(8,128)(2,1)S(1)}, u32[]{:S(2)}, u32[]{:S(2)}) collective-permute-start(bf16[4,88,1152]{2,1,0:T(8,128)(2,1)S(1)} %pad_maximum_fusion.1.ta_ref), channel_id=1, source_target_pairs={{0,2},{1,17},{2,0},{3,19},{4,6},{5,21},{6,4},{7,23},{8,10},{9,25},... | collective-permute-start | bytes 2433032 | tf_op jit(solution)/shard_map/ppermute | solution.py:31
  24.2 9.5 %collective-permute-start.10 = (bf16[352,1152]{1,0:T(8,128)(2,1)S(1)}, bf16[352,1152]{1,0:T(8,128)(2,1)S(1)}, u32[]{:S(2)}, u32[]{:S(2)}) collective-permute-start(bf16[352,1152]{1,0:T(8,128)(2,1)S(1)} %pad_maximum_fusion.2.im0_ref), channel_id=1, source_target_pairs={{0,1},{1,0},{2,3},{3,2},{4,5},{5,4},{6,7},{7,6},{8,9},{9,8},{10,11... | collective-permute-start | bytes 2433032 | tf_op jit(solution)/shard_map/ppermute | solution.py:31
  27.5 14.7 %collective-permute-start.11 = (bf16[4,88,1152]{2,1,0:T(8,128)(2,1)S(1)}, bf16[4,88,1152]{2,1,0:T(8,128)(2,1)S(1)}, u32[]{:S(2)}, u32[]{:S(2)}) collective-permute-start(bf16[4,88,1152]{2,1,0:T(8,128)(2,1)S(1)} %pad_maximum_fusion.1.ta_ref), channel_id=1, source_target_pairs={{0,64},{1,33},{2,66},{3,35},{4,68},{5,37},{6,70},{7,39},{8,72},{9,... | collective-permute-start | bytes 2433032 | tf_op jit(solution)/shard_map/ppermute | solution.py:31
  40.9 11.9 %collective-permute-start.12 = (bf16[360,1152]{1,0:T(8,128)(2,1)S(1)}, bf16[360,1152]{1,0:T(8,128)(2,1)S(1)}, u32[]{:S(2)}, u32[]{:S(2)}) collective-permute-start(bf16[360,1152]{1,0:T(8,128)(2,1)S(1)} %get-tuple-element.47), channel_id=1, source_target_pairs={{0,2},{1,17},{2,0},{3,19},{4,6},{5,21},{6,4},{7,23},{8,10},{9,25},... | collective-permute-start | bytes 2488328 | tf_op jit(solution)/shard_map/ppermute | solution.py:31
  52.8 5.2 %collective-permute-start.13 = (f32[360,1152]{1,0:T(8,128)S(1)}, f32[360,1152]{1,0:T(8,128)S(1)}, u32[]{:S(2)}, u32[]{:S(2)}) collective-permute-start(f32[360,1152]{1,0:T(8,128)S(1)} %get-tuple-element.48), channel_id=1, source_target_pairs={{0,1},{1,0},{2,3},{3,2},{4,5},{5,4},{6,7},{7,6},{8,9},{9,8},{10,11... | collective-permute-start | bytes 4976648 | tf_op jit(solution)/shard_map/ppermute | solution.py:31
  54.8 20.6 %collective-permute-start.14 = (bf16[360,1152]{1,0:T(8,128)(2,1)S(1)}, bf16[360,1152]{1,0:T(8,128)(2,1)S(1)}, u32[]{:S(2)}, u32[]{:S(2)}) collective-permute-start(bf16[360,1152]{1,0:T(8,128)(2,1)S(1)} %get-tuple-element.54), channel_id=1, source_target_pairs={{0,64},{1,33},{2,66},{3,35},{4,68},{5,37},{6,70},{7,39},{8,72},{9,... | collective-permute-start | bytes 2488328 | tf_op jit(solution)/shard_map/ppermute | solution.py:31
  56.5 20.4 %collective-permute-start.15 = (bf16[360,1152]{1,0:T(8,128)(2,1)S(1)}, bf16[360,1152]{1,0:T(8,128)(2,1)S(1)}, u32[]{:S(2)}, u32[]{:S(2)}) collective-permute-start(bf16[360,1152]{1,0:T(8,128)(2,1)S(1)} %get-tuple-element.55), channel_id=1, source_target_pairs={{0,66},{1,49},{2,64},{3,51},{4,70},{5,53},{6,68},{7,55},{8,74},{9,... | collective-permute-start | bytes 2488328 | tf_op jit(solution)/shard_map/ppermute | solution.py:31
  59.0 6.5 %collective-permute-start.16 = (bf16[96,1152]{1,0:T(8,128)(2,1)S(1)}, bf16[96,1152]{1,0:T(8,128)(2,1)S(1)}, u32[]{:S(2)}, u32[]{:S(2)}) collective-permute-start(bf16[96,1152]{1,0:T(8,128)(2,1)S(1)} %get-tuple-element.49), channel_id=1, source_target_pairs={{0,4},{1,5},{2,6},{3,7},{4,0},{5,1},{6,2},{7,3},{8,12},{9,13},{10,... | collective-permute-start | bytes 663560 | tf_op jit(solution)/shard_map/ppermute | solution.py:31
  60.3 12.2 %collective-permute-start.17 = (bf16[96,1152]{1,0:T(8,128)(2,1)S(1)}, bf16[96,1152]{1,0:T(8,128)(2,1)S(1)}, u32[]{:S(2)}, u32[]{:S(2)}) collective-permute-start(bf16[96,1152]{1,0:T(8,128)(2,1)S(1)} %get-tuple-element.50), channel_id=1, source_target_pairs={{0,8},{1,9},{2,10},{3,11},{4,12},{5,13},{6,14},{7,15},{8,0},{9,1},... | collective-permute-start | bytes 663560 | tf_op jit(solution)/shard_map/ppermute | solution.py:31
  62.7 12.0 %collective-permute-start.18 = (bf16[96,1152]{1,0:T(8,128)(2,1)S(1)}, bf16[96,1152]{1,0:T(8,128)(2,1)S(1)}, u32[]{:S(2)}, u32[]{:S(2)}) collective-permute-start(bf16[96,1152]{1,0:T(8,128)(2,1)S(1)} %get-tuple-element.51), channel_id=1, source_target_pairs={{0,12},{1,13},{2,14},{3,15},{4,8},{5,9},{6,10},{7,11},{8,4},{9,5},... | collective-permute-start | bytes 663560 | tf_op jit(solution)/shard_map/ppermute | solution.py:31
  79.9 5.2 %collective-permute-start.19 = (bf16[96,1152]{1,0:T(8,128)(2,1)S(1)}, bf16[96,1152]{1,0:T(8,128)(2,1)S(1)}, u32[]{:S(2)}, u32[]{:S(2)}) collective-permute-start(bf16[96,1152]{1,0:T(8,128)(2,1)S(1)} %get-tuple-element.59), channel_id=1, source_target_pairs={{0,16},{1,3},{2,18},{3,1},{4,20},{5,7},{6,22},{7,5},{8,24},{9,11},... | collective-permute-start | bytes 663560 | tf_op jit(solution)/shard_map/ppermute | solution.py:31
  80.4 7.7 %collective-permute-start.20 = (bf16[96,1152]{1,0:T(8,128)(2,1)S(1)}, bf16[96,1152]{1,0:T(8,128)(2,1)S(1)}, u32[]{:S(2)}, u32[]{:S(2)}) collective-permute-start(bf16[96,1152]{1,0:T(8,128)(2,1)S(1)} %get-tuple-element.60), channel_id=1, source_target_pairs={{0,32},{1,65},{2,34},{3,67},{4,36},{5,69},{6,38},{7,71},{8,40},{9,... | collective-permute-start | bytes 663560 | tf_op jit(solution)/shard_map/ppermute | solution.py:31
  82.1 8.4 %collective-permute-start.21 = (bf16[96,1152]{1,0:T(8,128)(2,1)S(1)}, bf16[96,1152]{1,0:T(8,128)(2,1)S(1)}, u32[]{:S(2)}, u32[]{:S(2)}) collective-permute-start(bf16[96,1152]{1,0:T(8,128)(2,1)S(1)} %get-tuple-element.61), channel_id=1, source_target_pairs={{0,48},{1,67},{2,50},{3,65},{4,52},{5,71},{6,54},{7,69},{8,56},{9,... | collective-permute-start | bytes 663560 | tf_op jit(solution)/shard_map/ppermute | solution.py:31
  84.0 7.1 %collective-permute-start.22 = (f32[88,576]{1,0:T(8,128)S(1)}, f32[88,576]{1,0:T(8,128)S(1)}, u32[]{:S(2)}, u32[]{:S(2)}) collective-permute-start(f32[88,576]{1,0:T(8,128)S(1)} %slice.40), channel_id=1, source_target_pairs={{0,2},{1,3},{2,0},{3,1},{4,6},{5,7},{6,4},{7,5},{8,10},{9,11},{10,... | collective-permute-start | bytes 608264 | tf_op jit(solution)/shard_map/ppermute | solution.py:31
  91.7 6.0 %collective-permute-start.24 = (f32[352,288]{0,1:T(8,128)S(1)}, f32[352,288]{0,1:T(8,128)S(1)}, u32[]{:S(2)}, u32[]{:S(2)}) collective-permute-start(f32[352,288]{0,1:T(8,128)S(1)} %copy.7), channel_id=1, source_target_pairs={{0,1},{1,0},{2,3},{3,2},{4,5},{5,4},{6,7},{7,6},{8,9},{9,8},{10,11... | collective-permute-start | bytes 1216520 | tf_op jit(solution)/shard_map/ppermute | solution.py:31
  94.0 2.5 %collective-permute-start.23 = (f32[8,128]{1,0:T(8,128)S(1)}, f32[8,128]{1,0:T(8,128)S(1)}, u32[]{:S(2)}, u32[]{:S(2)}) collective-permute-start(f32[8,128]{1,0:T(8,128)S(1)} %get-tuple-element.66), channel_id=1, source_target_pairs={{0,2},{1,17},{2,0},{3,19},{4,6},{5,21},{6,4},{7,23},{8,10},{9,25},... | collective-permute-start | bytes 12296 | tf_op jit(solution)/shard_map/ppermute | solution.py:31
  96.5 3.7 %collective-permute-start.25 = (f32[8,128]{1,0:T(8,128)S(1)}, f32[8,128]{1,0:T(8,128)S(1)}, u32[]{:S(2)}, u32[]{:S(2)}) collective-permute-start(f32[8,128]{1,0:T(8,128)S(1)} %add.10), channel_id=1, source_target_pairs={{0,66},{1,49},{2,64},{3,51},{4,70},{5,53},{6,68},{7,55},{8,74},{9,... | collective-permute-start | bytes 12296 | tf_op jit(solution)/shard_map/ppermute | solution.py:31

commit v11 on v10

--- a/solution.py
+++ b/solution.py
@@ -118,7 +118,7 @@
 
 def near_kernel(
     rows, half, feats, info_ref, scale_ref, ta_ref, tb_ref, im0_ref, im1_ref,
-    own_ref, m_ref, acc_ref, sums_ref, images, t_rel, coeff_low, grads,
+    own_ref, m_ref, t_rel, coeff_low, sums_ref, images, grads,
 ):
     quarter = 4 * rows
     images[0:quarter, :] = im0_ref[...]
@@ -128,6 +128,9 @@
     text_parts(info_ref, rows, half, coeff_low, images, grads)
     own_ref[...] = jnp.concatenate([grads[0, i] for i in range(4)], axis=0)
     m_ref[...] = message([grads[1, i] for i in range(4)], feats)
+
+
+def near_image_kernel(t_rel, coeff_low, acc_ref):
     acc_ref[...] = image_parts(coeff_low, t_rel)
 
 
@@ -276,19 +279,21 @@
     images_shape, coeff_shape = (2 * quarter, feats), (2 * quarter, 2 * quarter)
     grads = pltpu.VMEM((2, 4, rows, feats), F32)
     scratch = [pltpu.VMEM(images_shape, BF), pltpu.VMEM(images_shape, BF), pltpu.VMEM(coeff_shape, BF), grads]
-    text, m1, acc, sums = call(
+    text, m1, t_near, c_near, sums = call(
         functools.partial(near_kernel, *sizes), "tile_near",
-        [f32(quarter, feats), bf16(quarter + 8, feats), f32(*images_shape), f32(8, 128)],
+        [f32(quarter, feats), bf16(quarter + 8, feats), bf16(*images_shape), bf16(*coeff_shape), f32(8, 128)],
         info, scales, stack, second1, images_own, images_other,
-        scalars=2, mib=40, products=3, scratch=scratch,
-    )
+        scalars=2, mib=36, products=2, scratch=[scratch[0], grads],
+    )
+    got1 = swap(m1, z_mask(1), y_mask(1))
+    (acc,) = call(near_image_kernel, "image_near", [f32(*images_shape)], t_near, c_near, mib=30, products=1)
+    second2 = after(second2, acc)
     m2, m3, img_own, img_other = call(
         functools.partial(far_kernel, *sizes), "tile_far",
         [bf16(quarter + 8, feats), bf16(quarter + 8, feats), f32(quarter + 8, feats), f32(quarter + 8, feats)],
         info, scales, second2, second3, images_own, images_other, acc, sums,
         scalars=2, mib=40, products=3, scratch=scratch,
     )
-    got1 = swap(m1, z_mask(1), y_mask(1))
     img_other, got1 = lax.optimization_barrier((img_other, got1))
     got2, got3 = swap(m2, z_mask(2), y_mask(2)), swap(m3, z_mask(3), y_mask(3))
     img, *messages = call(
@@ -314,12 +319,11 @@
     mine, other = by(on0, whole[:, :width], whole[:, width:])
     sums = after(sums, other)
     other = swap(other, CORE)
-    sums = sums + swap(sums, z_mask(1), y_mask(1))
-    mine = after(mine, sums)
     text_grad, image_grad = call(
         functools.partial(join_kernel, rows), "join", [f32(width, height)] * 2, info, mine, other, scalars=1
     )
-    sums = sums + after(swap(sums, z_mask(3), y_mask(3)), text_grad, image_grad)
+    s1, s2, s3 = (after(swap(sums, z_mask(k), y_mask(k)), text_grad, image_grad) for k in (1, 2, 3))
+    sums = (sums + s1) + (s2 + s3)
     return (image_grad.T, text_grad.T, sums[0, :2])
 
 

time: 102 us -> 98.6 us (0.967); the launches traced: 101 us -> 98.4 us
  waiting for transfers between devices: 34.9 us -> 30.3 us
  starting transfers between devices: 35.2 us -> 37.2 us
    ppermute x26 -> x27, waiting for transfers between devices: 34.9 us -> 30.3 us  [swap(): lax.ppermute(array, AXES, [(i, i ^ (mask1 if i & 1 else mask0)) for i in...]
    ppermute x26 -> x27, starting transfers between devices: 35.2 us -> 37.2 us  [swap(): lax.ppermute(array, AXES, [(i, i ^ (mask1 if i & 1 else mask0)) for i in...]
    pallas_call x9 -> x10, Pallas kernels: 24.2 us -> 24.4 us  [call(): pl.pallas_call(kernel, out_shape=out_shape, in_specs=[SMEM] * scalars + [...]
  transfers between devices with their start and end apart: 26 -> 27, of which waited for: 19 -> 17; matrix products, arithmetic and copies ran while one was open for 1% -> 1% of each run, Pallas kernels for 20% -> 21%
where the time goes in v11:
time: 98.6 us; the launch traced here: 98.4 us
  starting transfers between devices  37.2 us (38%)
  waiting for transfers between devices  30.3 us (31%)
  Pallas kernels  24.4 us (25%)
  local copies, waits for them, and re-layouts  2.92 us (3%)
  between operations  2.1 us (2%)
  other arithmetic  1.34 us (1%)
    ppermute x27, starting transfers between devices, swap(): lax.ppermute(array, AXES, [(i, i ^ (mask1 if i & 1 else mask0)) for i in...  37.2 us
    ppermute x27, waiting for transfers between devices, swap(): lax.ppermute(array, AXES, [(i, i ^ (mask1 if i & 1 else mask0)) for i in...  30.3 us
    pallas_call x10, Pallas kernels, call(): pl.pallas_call(kernel, out_shape=out_shape, in_specs=[SMEM] * scalars + [...  24.4 us
  transfers between devices with their start and end apart: 27, of which 17 were waited for; matrix products, arithmetic and copies ran while one was open for 1% of the time, Pallas kernels for 21%

profile of v11, /device:TPU:1, one launch (start us, length us, event | category | flops | bytes accessed | tf_op | source)
XLA Modules:
  0.0 98.4 jit_solution(11883523140590864720)
XLA Ops:
  0.7 0.9 copy-done
  1.7 0.9 copy-done.1
  2.6 0.8 split.1
  3.4 1.5 %collective-permute-start = (bf16[352,288]{1,0:T(8,128)(2,1)S(1)}, bf16[352,288]{1,0:T(8,128)(2,1)S(1)}, u32[]{:S(2)}, u32[]{:S(2)}) collective-permute-start(bf16[352,288]{1,0:T(8,128)(2,1)S(1)} %get-tuple-element.41), channel_id=1, source_target_pairs={{0,1},{1,0},{2,3},{3,2},{4,5},{5,4},{6,7},{7,6},{8,9},{9,8},{10,11... | collective-permute-start | bytes 608264 | tf_op jit(solution)/shard_map/ppermute | solution.py:31
  4.9 1.2 %collective-permute-done = bf16[352,288]{1,0:T(8,128)(2,1)S(1)} collective-permute-done((bf16[352,288]{1,0:T(8,128)(2,1)S(1)}, bf16[352,288]{1,0:T(8,128)(2,1)S(1)}, u32[]{:S(2)}, u32[]{:S(2)}) %collective-permute-start) | collective-permute-done | bytes 202784 | tf_op jit(solution)/shard_map/ppermute | solution.py:31
  6.3 1.8 %collective-permute-start.6 = (bf16[88,576]{1,0:T(8,128)(2,1)S(1)}, bf16[88,576]{1,0:T(8,128)(2,1)S(1)}, u32[]{:S(2)}, u32[]{:S(2)}) collective-permute-start(bf16[88,576]{1,0:T(8,128)(2,1)S(1)} %get-tuple-element.83), channel_id=1, source_target_pairs={{0,2},{1,3},{2,0},{3,1},{4,6},{5,7},{6,4},{7,5},{8,10},{9,11},{10,... | collective-permute-start | bytes 304136 | tf_op jit(solution)/shard_map/ppermute | solution.py:31
  8.4 3.4 %collective-permute-start.2 = (bf16[88,1152]{1,0:T(8,128)(2,1)S(1)}, bf16[88,1152]{1,0:T(8,128)(2,1)S(1)}, u32[]{:S(2)}, u32[]{:S(2)}) collective-permute-start(bf16[88,1152]{1,0:T(8,128)(2,1)S(1)} %pad_maximum_fusion.3), channel_id=1, source_target_pairs={{0,32},{1,65},{2,34},{3,67},{4,36},{5,69},{6,38},{7,71},{8,40},{9,... | collective-permute-start | bytes 608264 | tf_op jit(solution)/shard_map/ppermute | solution.py:31
  12.2 2.6 %collective-permute-start.9 = (bf16[88,1152]{1,0:T(8,128)(2,1)S(1)}, bf16[88,1152]{1,0:T(8,128)(2,1)S(1)}, u32[]{:S(2)}, u32[]{:S(2)}) collective-permute-start(bf16[88,1152]{1,0:T(8,128)(2,1)S(1)} %pad_maximum_fusion.4), channel_id=1, source_target_pairs={{0,12},{1,13},{2,14},{3,15},{4,8},{5,9},{6,10},{7,11},{8,4},{9,5},... | collective-permute-start | bytes 608264 | tf_op jit(solution)/shard_map/ppermute | solution.py:31
  15.3 1.8 %collective-permute-done.2 = bf16[88,1152]{1,0:T(8,128)(2,1)S(1)} collective-permute-done((bf16[88,1152]{1,0:T(8,128)(2,1)S(1)}, bf16[88,1152]{1,0:T(8,128)(2,1)S(1)}, u32[]{:S(2)}, u32[]{:S(2)}) %collective-permute-start.2) | collective-permute-done | bytes 202784 | tf_op jit(solution)/shard_map/ppermute | solution.py:31
  17.1 1.2 %collective-permute-start.7 = (bf16[88,1152]{1,0:T(8,128)(2,1)S(1)}, bf16[88,1152]{1,0:T(8,128)(2,1)S(1)}, u32[]{:S(2)}, u32[]{:S(2)}) collective-permute-start(bf16[88,1152]{1,0:T(8,128)(2,1)S(1)} %pad_maximum_fusion.4), channel_id=1, source_target_pairs={{0,4},{1,5},{2,6},{3,7},{4,0},{5,1},{6,2},{7,3},{8,12},{9,13},{10,... | collective-permute-start | bytes 608264 | tf_op jit(solution)/shard_map/ppermute | solution.py:31
  18.3 1.0 %collective-permute-done.3 = bf16[88,1152]{1,0:T(8,128)(2,1)S(1)} collective-permute-done((bf16[88,1152]{1,0:T(8,128)(2,1)S(1)}, bf16[88,1152]{1,0:T(8,128)(2,1)S(1)}, u32[]{:S(2)}, u32[]{:S(2)}) %collective-permute-start.3) | collective-permute-done | bytes 202784 | tf_op jit(solution)/shard_map/ppermute | solution.py:31
  19.5 2.8 %collective-permute-start.5 = (bf16[4,88,1152]{2,1,0:T(8,128)(2,1)S(1)}, bf16[4,88,1152]{2,1,0:T(8,128)(2,1)S(1)}, u32[]{:S(2)}, u32[]{:S(2)}) collective-permute-start(bf16[4,88,1152]{2,1,0:T(8,128)(2,1)S(1)} %pad_maximum_fusion.1.ta_ref), channel_id=1, source_target_pairs={{0,66},{1,49},{2,64},{3,51},{4,70},{5,53},{6,68},{7,55},{8,74},{9,... | collective-permute-start | bytes 2433032 | tf_op jit(solution)/shard_map/ppermute | solution.py:31
  22.3 1.1 %collective-permute-done.9 = bf16[88,1152]{1,0:T(8,128)(2,1)S(1)} collective-permute-done((bf16[88,1152]{1,0:T(8,128)(2,1)S(1)}, bf16[88,1152]{1,0:T(8,128)(2,1)S(1)}, u32[]{:S(2)}, u32[]{:S(2)}) %collective-permute-start.9) | collective-permute-done | bytes 202784 | tf_op jit(solution)/shard_map/ppermute | solution.py:31
  23.3 0.8 collective-permute-done.7
  24.2 1.9 %collective-permute-start.10 = (bf16[352,1152]{1,0:T(8,128)(2,1)S(1)}, bf16[352,1152]{1,0:T(8,128)(2,1)S(1)}, u32[]{:S(2)}, u32[]{:S(2)}) collective-permute-start(bf16[352,1152]{1,0:T(8,128)(2,1)S(1)} %pad_maximum_fusion.2.im0_ref), channel_id=1, source_target_pairs={{0,1},{1,0},{2,3},{3,2},{4,5},{5,4},{6,7},{7,6},{8,9},{9,8},{10,11... | collective-permute-start | bytes 2433032 | tf_op jit(solution)/shard_map/ppermute | solution.py:31
  27.4 3.0 %collective-permute-start.11 = (bf16[4,88,1152]{2,1,0:T(8,128)(2,1)S(1)}, bf16[4,88,1152]{2,1,0:T(8,128)(2,1)S(1)}, u32[]{:S(2)}, u32[]{:S(2)}) collective-permute-start(bf16[4,88,1152]{2,1,0:T(8,128)(2,1)S(1)} %pad_maximum_fusion.1.ta_ref), channel_id=1, source_target_pairs={{0,64},{1,33},{2,66},{3,35},{4,68},{5,37},{6,70},{7,39},{8,72},{9,... | collective-permute-start | bytes 2433032 | tf_op jit(solution)/shard_map/ppermute | solution.py:31
  30.4 1.8 %collective-permute-done.5.tb_ref = bf16[4,88,1152]{2,1,0:T(8,128)(2,1)S(1)} collective-permute-done((bf16[4,88,1152]{2,1,0:T(8,128)(2,1)S(1)}, bf16[4,88,1152]{2,1,0:T(8,128)(2,1)S(1)}, u32[]{:S(2)}, u32[]{:S(2)}) %collective-permute-start.5) | collective-permute-done | bytes 811040 | tf_op jit(solution)/shard_map/ppermute | solution.py:31
  32.2 1.5 %collective-permute-done.4.tb_ref = bf16[4,88,1152]{2,1,0:T(8,128)(2,1)S(1)} collective-permute-done((bf16[4,88,1152]{2,1,0:T(8,128)(2,1)S(1)}, bf16[4,88,1152]{2,1,0:T(8,128)(2,1)S(1)}, u32[]{:S(2)}, u32[]{:S(2)}) %collective-permute-start.4) | collective-permute-done | bytes 811040 | tf_op jit(solution)/shard_map/ppermute | solution.py:31
  33.7 5.9 %tile_near.1 = (f32[352,1152]{1,0:T(8,128)S(1)}, bf16[360,1152]{1,0:T(8,128)(2,1)S(1)}, bf16[704,1152]{1,0:T(8,128)(2,1)S(1)}, bf16[704,704]{1,0:T(8,128)(2,1)S(1)}, f32[8,128]{1,0:T(8,128)S(1)}) custom-call(s32[2]{0:T(128)S(1)} %pad_add_fusion.info_ref, f32[2]{0:T(128)S(1)} %pad_maximum_fusion.6.scale_ref, ...), custom_call_target="tpu_custom_call" | custom-call | flops 2283798528 | bytes 8312848 | tf_op jit(solution)/shard_map/tile_near/pallas_call | solution.py:246
  39.8 1.6 %image_near.1.before_ref = f32[704,1152]{1,0:T(8,128)S(1)} custom-call(bf16[704,1152]{1,0:T(8,128)(2,1)S(1)} %get-tuple-element.45.t_rel, bf16[704,704]{1,0:T(8,128)(2,1)S(1)} %get-tuple-element.46.coeff_low), custom_call_target="tpu_custom_call" | custom-call | flops 1141899264 | bytes 5857280 | tf_op jit(solution)/shard_map/image_near/pallas_call | solution.py:246
  41.4 0.7 collective-permute-done.11.ta_ref
  42.2 8.4 %tile_far.1 = (bf16[360,1152]{1,0:T(8,128)(2,1)S(1)}, bf16[360,1152]{1,0:T(8,128)(2,1)S(1)}, f32[360,1152]{1,0:T(8,128)S(1)}, f32[360,1152]{1,0:T(8,128)S(1)}) custom-call(s32[2]{0:T(128)S(1)} %pad_add_fusion.info_ref, f32[2]{0:T(128)S(1)} %pad_maximum_fusion.6.scale_ref, bf16[4,88,1152]{2,1,0:T(8,128)(2,1)S(1)} %collective-permute-done.11.ta_ref, ...), custom_call_target="tpu_custom_call" | custom-call | flops 3425697792 | bytes 11468816 | tf_op jit(solution)/shard_map/tile_far/pallas_call | solution.py:246
  50.6 0.8 collective-permute-done.12.r1_ref
  51.4 2.1 %collective-permute-start.13 = (f32[360,1152]{1,0:T(8,128)S(1)}, f32[360,1152]{1,0:T(8,128)S(1)}, u32[]{:S(2)}, u32[]{:S(2)}) collective-permute-start(f32[360,1152]{1,0:T(8,128)S(1)} %get-tuple-element.53), channel_id=1, source_target_pairs={{0,1},{1,0},{2,3},{3,2},{4,5},{5,4},{6,7},{7,6},{8,9},{9,8},{10,11... | collective-permute-start | bytes 4976648 | tf_op jit(solution)/shard_map/ppermute | solution.py:31
  53.5 1.6 %collective-permute-start.14 = (bf16[360,1152]{1,0:T(8,128)(2,1)S(1)}, bf16[360,1152]{1,0:T(8,128)(2,1)S(1)}, u32[]{:S(2)}, u32[]{:S(2)}) collective-permute-start(bf16[360,1152]{1,0:T(8,128)(2,1)S(1)} %get-tuple-element.59), channel_id=1, source_target_pairs={{0,64},{1,33},{2,66},{3,35},{4,68},{5,37},{6,70},{7,39},{8,72},{9,... | collective-permute-start | bytes 2488328 | tf_op jit(solution)/shard_map/ppermute | solution.py:31
  55.1 0.8 collective-permute-start.15
  55.9 0.7 collective-permute-done.13.other_ref
  56.6 1.0 image_first.1
  57.6 1.3 %collective-permute-start.16 = (bf16[96,1152]{1,0:T(8,128)(2,1)S(1)}, bf16[96,1152]{1,0:T(8,128)(2,1)S(1)}, u32[]{:S(2)}, u32[]{:S(2)}) collective-permute-start(bf16[96,1152]{1,0:T(8,128)(2,1)S(1)} %get-tuple-element.54), channel_id=1, source_target_pairs={{0,4},{1,5},{2,6},{3,7},{4,0},{5,1},{6,2},{7,3},{8,12},{9,13},{10,... | collective-permute-start | bytes 663560 | tf_op jit(solution)/shard_map/ppermute | solution.py:31
  58.9 2.4 %collective-permute-start.17 = (bf16[96,1152]{1,0:T(8,128)(2,1)S(1)}, bf16[96,1152]{1,0:T(8,128)(2,1)S(1)}, u32[]{:S(2)}, u32[]{:S(2)}) collective-permute-start(bf16[96,1152]{1,0:T(8,128)(2,1)S(1)} %get-tuple-element.55), channel_id=1, source_target_pairs={{0,8},{1,9},{2,10},{3,11},{4,12},{5,13},{6,14},{7,15},{8,0},{9,1},... | collective-permute-start | bytes 663560 | tf_op jit(solution)/shard_map/ppermute | solution.py:31
  61.6 0.8 text_near.1.own_ref
  62.3 1.8 %collective-permute-done.16.r1_ref = bf16[96,1152]{1,0:T(8,128)(2,1)S(1)} collective-permute-done((bf16[96,1152]{1,0:T(8,128)(2,1)S(1)}, bf16[96,1152]{1,0:T(8,128)(2,1)S(1)}, u32[]{:S(2)}, u32[]{:S(2)}) %collective-permute-start.16) | collective-permute-done | bytes 221216 | tf_op jit(solution)/shard_map/ppermute | solution.py:31
  64.1 7.0 %collective-permute-done.17.r2_ref = bf16[96,1152]{1,0:T(8,128)(2,1)S(1)} collective-permute-done((bf16[96,1152]{1,0:T(8,128)(2,1)S(1)}, bf16[96,1152]{1,0:T(8,128)(2,1)S(1)}, u32[]{:S(2)}, u32[]{:S(2)}) %collective-permute-start.17) | collective-permute-done | bytes 221216 | tf_op jit(solution)/shard_map/ppermute | solution.py:31
  71.1 2.2 %collective-permute-done.18.r3_ref = bf16[96,1152]{1,0:T(8,128)(2,1)S(1)} collective-permute-done((bf16[96,1152]{1,0:T(8,128)(2,1)S(1)}, bf16[96,1152]{1,0:T(8,128)(2,1)S(1)}, u32[]{:S(2)}, u32[]{:S(2)}) %collective-permute-start.18) | collective-permute-done | bytes 221216 | tf_op jit(solution)/shard_map/ppermute | solution.py:31
  73.4 0.6 image_last.1
  74.0 1.4 %collective-permute-done.15.r3_ref = bf16[360,1152]{1,0:T(8,128)(2,1)S(1)} collective-permute-done((bf16[360,1152]{1,0:T(8,128)(2,1)S(1)}, bf16[360,1152]{1,0:T(8,128)(2,1)S(1)}, u32[]{:S(2)}, u32[]{:S(2)}) %collective-permute-start.15) | collective-permute-done | bytes 829472 | tf_op jit(solution)/shard_map/ppermute | solution.py:31
  75.5 3.1 %text_first.1 = (f32[96,1152]{1,0:T(8,128)S(1)}, bf16[96,1152]{1,0:T(8,128)(2,1)S(1)}, bf16[96,1152]{1,0:T(8,128)(2,1)S(1)}, bf16[96,1152]{1,0:T(8,128)(2,1)S(1)}) custom-call(f32[352,1152]{1,0:T(8,128)S(1)} %text_near.1.own_ref, bf16[360,1152]{1,0:T(8,128)(2,1)S(1)} %collective-permute-done.14.r2_ref, bf16[360,1152]{1,0:T(8,128)(2,1)S(1)} %collective-permute-done.15.r3_ref, ...), custom_call_target="tpu_custom_call" | custom-call | bytes 4423680 | tf_op jit(solution)/shard_map/text_first/pallas_call | solution.py:246
  78.5 0.5 collective-permute-start.19
  79.1 1.8 %collective-permute-start.20 = (bf16[96,1152]{1,0:T(8,128)(2,1)S(1)}, bf16[96,1152]{1,0:T(8,128)(2,1)S(1)}, u32[]{:S(2)}, u32[]{:S(2)}) collective-permute-start(bf16[96,1152]{1,0:T(8,128)(2,1)S(1)} %get-tuple-element.65), channel_id=1, source_target_pairs={{0,32},{1,65},{2,34},{3,67},{4,36},{5,69},{6,38},{7,71},{8,40},{9,... | collective-permute-start | bytes 663560 | tf_op jit(solution)/shard_map/ppermute | solution.py:31
  80.8 1.6 %collective-permute-start.21 = (bf16[96,1152]{1,0:T(8,128)(2,1)S(1)}, bf16[96,1152]{1,0:T(8,128)(2,1)S(1)}, u32[]{:S(2)}, u32[]{:S(2)}) collective-permute-start(bf16[96,1152]{1,0:T(8,128)(2,1)S(1)} %get-tuple-element.66), channel_id=1, source_target_pairs={{0,48},{1,67},{2,50},{3,65},{4,52},{5,71},{6,54},{7,69},{8,56},{9,... | collective-permute-start | bytes 663560 | tf_op jit(solution)/shard_map/ppermute | solution.py:31
  82.7 1.0 %collective-permute-done.19.r1_ref = bf16[96,1152]{1,0:T(8,128)(2,1)S(1)} collective-permute-done((bf16[96,1152]{1,0:T(8,128)(2,1)S(1)}, bf16[96,1152]{1,0:T(8,128)(2,1)S(1)}, u32[]{:S(2)}, u32[]{:S(2)}) %collective-permute-start.19) | collective-permute-done | bytes 221216 | tf_op jit(solution)/shard_map/ppermute | solution.py:31
  83.7 3.2 %collective-permute-done.20.r2_ref = bf16[96,1152]{1,0:T(8,128)(2,1)S(1)} collective-permute-done((bf16[96,1152]{1,0:T(8,128)(2,1)S(1)}, bf16[96,1152]{1,0:T(8,128)(2,1)S(1)}, u32[]{:S(2)}, u32[]{:S(2)}) %collective-permute-start.20) | collective-permute-done | bytes 221216 | tf_op jit(solution)/shard_map/ppermute | solution.py:31
  86.9 2.3 %collective-permute-done.21.r3_ref = bf16[96,1152]{1,0:T(8,128)(2,1)S(1)} collective-permute-done((bf16[96,1152]{1,0:T(8,128)(2,1)S(1)}, bf16[96,1152]{1,0:T(8,128)(2,1)S(1)}, u32[]{:S(2)}, u32[]{:S(2)}) %collective-permute-start.21) | collective-permute-done | bytes 221216 | tf_op jit(solution)/shard_map/ppermute | solution.py:31
  89.2 0.6 text_last.1
  90.5 2.2 %collective-permute-start.23 = (f32[352,288]{0,1:T(8,128)S(1)}, f32[352,288]{0,1:T(8,128)S(1)}, u32[]{:S(2)}, u32[]{:S(2)}) collective-permute-start(f32[352,288]{0,1:T(8,128)S(1)} %copy.7), channel_id=1, source_target_pairs={{0,1},{1,0},{2,3},{3,2},{4,5},{5,4},{6,7},{7,6},{8,9},{9,8},{10,11... | collective-permute-start | bytes 1216520 | tf_op jit(solution)/shard_map/ppermute | solution.py:31
  92.7 1.2 %collective-permute-start.26 = (f32[8,128]{1,0:T(8,128)S(1)}, f32[8,128]{1,0:T(8,128)S(1)}, u32[]{:S(2)}, u32[]{:S(2)}) collective-permute-start(f32[8,128]{1,0:T(8,128)S(1)} %get-tuple-element.73), channel_id=1, source_target_pairs={{0,66},{1,49},{2,64},{3,51},{4,70},{5,53},{6,68},{7,55},{8,74},{9,... | collective-permute-start | bytes 12296 | tf_op jit(solution)/shard_map/ppermute | solution.py:31
  94.0 2.0 %collective-permute-start.24 = (f32[8,128]{1,0:T(8,128)S(1)}, f32[8,128]{1,0:T(8,128)S(1)}, u32[]{:S(2)}, u32[]{:S(2)}) collective-permute-start(f32[8,128]{1,0:T(8,128)S(1)} %get-tuple-element.73), channel_id=1, source_target_pairs={{0,2},{1,17},{2,0},{3,19},{4,6},{5,21},{6,4},{7,23},{8,10},{9,25},... | collective-permute-start | bytes 12296 | tf_op jit(solution)/shard_map/ppermute | solution.py:31
  96.1 1.7 %join.1 = (f32[288,352]{1,0:T(8,128)}, f32[288,352]{1,0:T(8,128)}) custom-call(s32[2]{0:T(128)S(1)} %pad_add_fusion.info_ref, f32[352,288]{1,0:T(8,128)S(1)} %get-tuple-element.80.own_ref, f32[352,288]{1,0:T(8,128)S(1)} %copy.8.got_ref), custom_call_target="tpu_custom_call" | custom-call | bytes 1622024 | tf_op jit(solution)/shard_map/join/pallas_call | solution.py:246
  (38 shorter events, 4.0 us)
Async XLA Ops:
  0.7 0.9 copy-start
  1.6 0.9 copy-start.1
  3.4 2.7 %collective-permute-start = (bf16[352,288]{1,0:T(8,128)(2,1)S(1)}, bf16[352,288]{1,0:T(8,128)(2,1)S(1)}, u32[]{:S(2)}, u32[]{:S(2)}) collective-permute-start(bf16[352,288]{1,0:T(8,128)(2,1)S(1)} %get-tuple-element.41), channel_id=1, source_target_pairs={{0,1},{1,0},{2,3},{3,2},{4,5},{5,4},{6,7},{7,6},{8,9},{9,8},{10,11... | collective-permute-start | bytes 608264 | tf_op jit(solution)/shard_map/ppermute | solution.py:31
  6.3 5.8 %collective-permute-start.6 = (bf16[88,576]{1,0:T(8,128)(2,1)S(1)}, bf16[88,576]{1,0:T(8,128)(2,1)S(1)}, u32[]{:S(2)}, u32[]{:S(2)}) collective-permute-start(bf16[88,576]{1,0:T(8,128)(2,1)S(1)} %get-tuple-element.83), channel_id=1, source_target_pairs={{0,2},{1,3},{2,0},{3,1},{4,6},{5,7},{6,4},{7,5},{8,10},{9,11},{10,... | collective-permute-start | bytes 304136 | tf_op jit(solution)/shard_map/ppermute | solution.py:31
  8.4 8.7 %collective-permute-start.2 = (bf16[88,1152]{1,0:T(8,128)(2,1)S(1)}, bf16[88,1152]{1,0:T(8,128)(2,1)S(1)}, u32[]{:S(2)}, u32[]{:S(2)}) collective-permute-start(bf16[88,1152]{1,0:T(8,128)(2,1)S(1)} %pad_maximum_fusion.3), channel_id=1, source_target_pairs={{0,32},{1,65},{2,34},{3,67},{4,36},{5,69},{6,38},{7,71},{8,40},{9,... | collective-permute-start | bytes 608264 | tf_op jit(solution)/shard_map/ppermute | solution.py:31
  11.7 6.6 %collective-permute-start.1 = (bf16[88,1152]{1,0:T(8,128)(2,1)S(1)}, bf16[88,1152]{1,0:T(8,128)(2,1)S(1)}, u32[]{:S(2)}, u32[]{:S(2)}) collective-permute-start(bf16[88,1152]{1,0:T(8,128)(2,1)S(1)} %pad_maximum_fusion.3), channel_id=1, source_target_pairs={{0,16},{1,3},{2,18},{3,1},{4,20},{5,7},{6,22},{7,5},{8,24},{9,11},... | collective-permute-start | bytes 608264 | tf_op jit(solution)/shard_map/ppermute | solution.py:31
  11.7 7.6 %collective-permute-start.3 = (bf16[88,1152]{1,0:T(8,128)(2,1)S(1)}, bf16[88,1152]{1,0:T(8,128)(2,1)S(1)}, u32[]{:S(2)}, u32[]{:S(2)}) collective-permute-start(bf16[88,1152]{1,0:T(8,128)(2,1)S(1)} %pad_maximum_fusion.3), channel_id=1, source_target_pairs={{0,48},{1,67},{2,50},{3,65},{4,52},{5,71},{6,54},{7,69},{8,56},{9,... | collective-permute-start | bytes 608264 | tf_op jit(solution)/shard_map/ppermute | solution.py:31
  12.2 11.1 %collective-permute-start.9 = (bf16[88,1152]{1,0:T(8,128)(2,1)S(1)}, bf16[88,1152]{1,0:T(8,128)(2,1)S(1)}, u32[]{:S(2)}, u32[]{:S(2)}) collective-permute-start(bf16[88,1152]{1,0:T(8,128)(2,1)S(1)} %pad_maximum_fusion.4), channel_id=1, source_target_pairs={{0,12},{1,13},{2,14},{3,15},{4,8},{5,9},{6,10},{7,11},{8,4},{9,5},... | collective-permute-start | bytes 608264 | tf_op jit(solution)/shard_map/ppermute | solution.py:31
  14.8 8.5 %collective-permute-start.8 = (bf16[88,1152]{1,0:T(8,128)(2,1)S(1)}, bf16[88,1152]{1,0:T(8,128)(2,1)S(1)}, u32[]{:S(2)}, u32[]{:S(2)}) collective-permute-start(bf16[88,1152]{1,0:T(8,128)(2,1)S(1)} %pad_maximum_fusion.4), channel_id=1, source_target_pairs={{0,8},{1,9},{2,10},{3,11},{4,12},{5,13},{6,14},{7,15},{8,0},{9,1},... | collective-permute-start | bytes 608264 | tf_op jit(solution)/shard_map/ppermute | solution.py:31
  17.1 7.0 %collective-permute-start.7 = (bf16[88,1152]{1,0:T(8,128)(2,1)S(1)}, bf16[88,1152]{1,0:T(8,128)(2,1)S(1)}, u32[]{:S(2)}, u32[]{:S(2)}) collective-permute-start(bf16[88,1152]{1,0:T(8,128)(2,1)S(1)} %pad_maximum_fusion.4), channel_id=1, source_target_pairs={{0,4},{1,5},{2,6},{3,7},{4,0},{5,1},{6,2},{7,3},{8,12},{9,13},{10,... | collective-permute-start | bytes 608264 | tf_op jit(solution)/shard_map/ppermute | solution.py:31
  19.5 12.8 %collective-permute-start.5 = (bf16[4,88,1152]{2,1,0:T(8,128)(2,1)S(1)}, bf16[4,88,1152]{2,1,0:T(8,128)(2,1)S(1)}, u32[]{:S(2)}, u32[]{:S(2)}) collective-permute-start(bf16[4,88,1152]{2,1,0:T(8,128)(2,1)S(1)} %pad_maximum_fusion.1.ta_ref), channel_id=1, source_target_pairs={{0,66},{1,49},{2,64},{3,51},{4,70},{5,53},{6,68},{7,55},{8,74},{9,... | collective-permute-start | bytes 2433032 | tf_op jit(solution)/shard_map/ppermute | solution.py:31
  22.3 11.4 %collective-permute-start.4 = (bf16[4,88,1152]{2,1,0:T(8,128)(2,1)S(1)}, bf16[4,88,1152]{2,1,0:T(8,128)(2,1)S(1)}, u32[]{:S(2)}, u32[]{:S(2)}) collective-permute-start(bf16[4,88,1152]{2,1,0:T(8,128)(2,1)S(1)} %pad_maximum_fusion.1.ta_ref), channel_id=1, source_target_pairs={{0,2},{1,17},{2,0},{3,19},{4,6},{5,21},{6,4},{7,23},{8,10},{9,25},... | collective-permute-start | bytes 2433032 | tf_op jit(solution)/shard_map/ppermute | solution.py:31
  24.2 9.5 %collective-permute-start.10 = (bf16[352,1152]{1,0:T(8,128)(2,1)S(1)}, bf16[352,1152]{1,0:T(8,128)(2,1)S(1)}, u32[]{:S(2)}, u32[]{:S(2)}) collective-permute-start(bf16[352,1152]{1,0:T(8,128)(2,1)S(1)} %pad_maximum_fusion.2.im0_ref), channel_id=1, source_target_pairs={{0,1},{1,0},{2,3},{3,2},{4,5},{5,4},{6,7},{7,6},{8,9},{9,8},{10,11... | collective-permute-start | bytes 2433032 | tf_op jit(solution)/shard_map/ppermute | solution.py:31
  27.4 14.8 %collective-permute-start.11 = (bf16[4,88,1152]{2,1,0:T(8,128)(2,1)S(1)}, bf16[4,88,1152]{2,1,0:T(8,128)(2,1)S(1)}, u32[]{:S(2)}, u32[]{:S(2)}) collective-permute-start(bf16[4,88,1152]{2,1,0:T(8,128)(2,1)S(1)} %pad_maximum_fusion.1.ta_ref), channel_id=1, source_target_pairs={{0,64},{1,33},{2,66},{3,35},{4,68},{5,37},{6,70},{7,39},{8,72},{9,... | collective-permute-start | bytes 2433032 | tf_op jit(solution)/shard_map/ppermute | solution.py:31
  39.5 11.9 %collective-permute-start.12 = (bf16[360,1152]{1,0:T(8,128)(2,1)S(1)}, bf16[360,1152]{1,0:T(8,128)(2,1)S(1)}, u32[]{:S(2)}, u32[]{:S(2)}) collective-permute-start(bf16[360,1152]{1,0:T(8,128)(2,1)S(1)} %get-tuple-element.52), channel_id=1, source_target_pairs={{0,2},{1,17},{2,0},{3,19},{4,6},{5,21},{6,4},{7,23},{8,10},{9,25},... | collective-permute-start | bytes 2488328 | tf_op jit(solution)/shard_map/ppermute | solution.py:31
  51.4 5.2 %collective-permute-start.13 = (f32[360,1152]{1,0:T(8,128)S(1)}, f32[360,1152]{1,0:T(8,128)S(1)}, u32[]{:S(2)}, u32[]{:S(2)}) collective-permute-start(f32[360,1152]{1,0:T(8,128)S(1)} %get-tuple-element.53), channel_id=1, source_target_pairs={{0,1},{1,0},{2,3},{3,2},{4,5},{5,4},{6,7},{7,6},{8,9},{9,8},{10,11... | collective-permute-start | bytes 4976648 | tf_op jit(solution)/shard_map/ppermute | solution.py:31
  53.5 20.5 %collective-permute-start.14 = (bf16[360,1152]{1,0:T(8,128)(2,1)S(1)}, bf16[360,1152]{1,0:T(8,128)(2,1)S(1)}, u32[]{:S(2)}, u32[]{:S(2)}) collective-permute-start(bf16[360,1152]{1,0:T(8,128)(2,1)S(1)} %get-tuple-element.59), channel_id=1, source_target_pairs={{0,64},{1,33},{2,66},{3,35},{4,68},{5,37},{6,70},{7,39},{8,72},{9,... | collective-permute-start | bytes 2488328 | tf_op jit(solution)/shard_map/ppermute | solution.py:31
  55.1 20.3 %collective-permute-start.15 = (bf16[360,1152]{1,0:T(8,128)(2,1)S(1)}, bf16[360,1152]{1,0:T(8,128)(2,1)S(1)}, u32[]{:S(2)}, u32[]{:S(2)}) collective-permute-start(bf16[360,1152]{1,0:T(8,128)(2,1)S(1)} %get-tuple-element.60), channel_id=1, source_target_pairs={{0,66},{1,49},{2,64},{3,51},{4,70},{5,53},{6,68},{7,55},{8,74},{9,... | collective-permute-start | bytes 2488328 | tf_op jit(solution)/shard_map/ppermute | solution.py:31
  57.6 6.5 %collective-permute-start.16 = (bf16[96,1152]{1,0:T(8,128)(2,1)S(1)}, bf16[96,1152]{1,0:T(8,128)(2,1)S(1)}, u32[]{:S(2)}, u32[]{:S(2)}) collective-permute-start(bf16[96,1152]{1,0:T(8,128)(2,1)S(1)} %get-tuple-element.54), channel_id=1, source_target_pairs={{0,4},{1,5},{2,6},{3,7},{4,0},{5,1},{6,2},{7,3},{8,12},{9,13},{10,... | collective-permute-start | bytes 663560 | tf_op jit(solution)/shard_map/ppermute | solution.py:31
  58.9 12.2 %collective-permute-start.17 = (bf16[96,1152]{1,0:T(8,128)(2,1)S(1)}, bf16[96,1152]{1,0:T(8,128)(2,1)S(1)}, u32[]{:S(2)}, u32[]{:S(2)}) collective-permute-start(bf16[96,1152]{1,0:T(8,128)(2,1)S(1)} %get-tuple-element.55), channel_id=1, source_target_pairs={{0,8},{1,9},{2,10},{3,11},{4,12},{5,13},{6,14},{7,15},{8,0},{9,1},... | collective-permute-start | bytes 663560 | tf_op jit(solution)/shard_map/ppermute | solution.py:31
  61.4 12.0 %collective-permute-start.18 = (bf16[96,1152]{1,0:T(8,128)(2,1)S(1)}, bf16[96,1152]{1,0:T(8,128)(2,1)S(1)}, u32[]{:S(2)}, u32[]{:S(2)}) collective-permute-start(bf16[96,1152]{1,0:T(8,128)(2,1)S(1)} %get-tuple-element.56), channel_id=1, source_target_pairs={{0,12},{1,13},{2,14},{3,15},{4,8},{5,9},{6,10},{7,11},{8,4},{9,5},... | collective-permute-start | bytes 663560 | tf_op jit(solution)/shard_map/ppermute | solution.py:31
  78.5 5.2 %collective-permute-start.19 = (bf16[96,1152]{1,0:T(8,128)(2,1)S(1)}, bf16[96,1152]{1,0:T(8,128)(2,1)S(1)}, u32[]{:S(2)}, u32[]{:S(2)}) collective-permute-start(bf16[96,1152]{1,0:T(8,128)(2,1)S(1)} %get-tuple-element.64), channel_id=1, source_target_pairs={{0,16},{1,3},{2,18},{3,1},{4,20},{5,7},{6,22},{7,5},{8,24},{9,11},... | collective-permute-start | bytes 663560 | tf_op jit(solution)/shard_map/ppermute | solution.py:31
  79.1 7.8 %collective-permute-start.20 = (bf16[96,1152]{1,0:T(8,128)(2,1)S(1)}, bf16[96,1152]{1,0:T(8,128)(2,1)S(1)}, u32[]{:S(2)}, u32[]{:S(2)}) collective-permute-start(bf16[96,1152]{1,0:T(8,128)(2,1)S(1)} %get-tuple-element.65), channel_id=1, source_target_pairs={{0,32},{1,65},{2,34},{3,67},{4,36},{5,69},{6,38},{7,71},{8,40},{9,... | collective-permute-start | bytes 663560 | tf_op jit(solution)/shard_map/ppermute | solution.py:31
  80.8 8.4 %collective-permute-start.21 = (bf16[96,1152]{1,0:T(8,128)(2,1)S(1)}, bf16[96,1152]{1,0:T(8,128)(2,1)S(1)}, u32[]{:S(2)}, u32[]{:S(2)}) collective-permute-start(bf16[96,1152]{1,0:T(8,128)(2,1)S(1)} %get-tuple-element.66), channel_id=1, source_target_pairs={{0,48},{1,67},{2,50},{3,65},{4,52},{5,71},{6,54},{7,69},{8,56},{9,... | collective-permute-start | bytes 663560 | tf_op jit(solution)/shard_map/ppermute | solution.py:31
  82.6 7.2 %collective-permute-start.22 = (f32[88,576]{1,0:T(8,128)S(1)}, f32[88,576]{1,0:T(8,128)S(1)}, u32[]{:S(2)}, u32[]{:S(2)}) collective-permute-start(f32[88,576]{1,0:T(8,128)S(1)} %slice.40), channel_id=1, source_target_pairs={{0,2},{1,3},{2,0},{3,1},{4,6},{5,7},{6,4},{7,5},{8,10},{9,11},{10,... | collective-permute-start | bytes 608264 | tf_op jit(solution)/shard_map/ppermute | solution.py:31
  90.5 5.5 %collective-permute-start.23 = (f32[352,288]{0,1:T(8,128)S(1)}, f32[352,288]{0,1:T(8,128)S(1)}, u32[]{:S(2)}, u32[]{:S(2)}) collective-permute-start(f32[352,288]{0,1:T(8,128)S(1)} %copy.7), channel_id=1, source_target_pairs={{0,1},{1,0},{2,3},{3,2},{4,5},{5,4},{6,7},{7,6},{8,9},{9,8},{10,11... | collective-permute-start | bytes 1216520 | tf_op jit(solution)/shard_map/ppermute | solution.py:31
  92.7 5.2 %collective-permute-start.26 = (f32[8,128]{1,0:T(8,128)S(1)}, f32[8,128]{1,0:T(8,128)S(1)}, u32[]{:S(2)}, u32[]{:S(2)}) collective-permute-start(f32[8,128]{1,0:T(8,128)S(1)} %get-tuple-element.73), channel_id=1, source_target_pairs={{0,66},{1,49},{2,64},{3,51},{4,70},{5,53},{6,68},{7,55},{8,74},{9,... | collective-permute-start | bytes 12296 | tf_op jit(solution)/shard_map/ppermute | solution.py:31
  93.9 4.0 %collective-permute-start.25 = (f32[8,128]{1,0:T(8,128)S(1)}, f32[8,128]{1,0:T(8,128)S(1)}, u32[]{:S(2)}, u32[]{:S(2)}) collective-permute-start(f32[8,128]{1,0:T(8,128)S(1)} %get-tuple-element.73), channel_id=1, source_target_pairs={{0,64},{1,33},{2,66},{3,35},{4,68},{5,37},{6,70},{7,39},{8,72},{9,... | collective-permute-start | bytes 12296 | tf_op jit(solution)/shard_map/ppermute | solution.py:31
  94.0 3.9 %collective-permute-start.24 = (f32[8,128]{1,0:T(8,128)S(1)}, f32[8,128]{1,0:T(8,128)S(1)}, u32[]{:S(2)}, u32[]{:S(2)}) collective-permute-start(f32[8,128]{1,0:T(8,128)S(1)} %get-tuple-element.73), channel_id=1, source_target_pairs={{0,2},{1,17},{2,0},{3,19},{4,6},{5,21},{6,4},{7,23},{8,10},{9,25},... | collective-permute-start | bytes 12296 | tf_op jit(solution)/shard_map/ppermute | solution.py:31

commit v12 on v11

--- a/solution.py
+++ b/solution.py
@@ -100,10 +100,14 @@
     return lax.dot_general(coeff_low[...], t_rel[...], (((0,), (0,)), ((), ())), preferred_element_type=F32)
 
 
-def split_kernel(rows, info_ref, texts_ref, images_ref, keep_ref, send_ref):
+def split_kernel(rows, info_ref, texts_ref, images_ref, keep_ref, send_ref, both, sems):
     on0, step = info_ref[0] == 0, 2 * rows
-    for at, ref in ((0, texts_ref), (step, images_ref)):
-        whole = ref[...].astype(F32).T
+    copies = [pltpu.make_async_copy(ref, both.at[k], sems.at[k]) for k, ref in enumerate((texts_ref, images_ref))]
+    for copy in copies:
+        copy.start()
+    for k, at in ((0, 0), (1, step)):
+        copies[k].wait()
+        whole = both[k].astype(F32).T
         first, second = whole[:step], whole[step:]
         keep_ref[at : at + step, :] = jnp.where(on0, first, second).astype(BF)
         send_ref[at : at + step, :] = jnp.where(on0, second, first).astype(BF)
@@ -112,8 +116,8 @@
 def join_kernel(rows, info_ref, own_ref, got_ref, texts_ref, images_ref):
     on0, step = info_ref[0] == 0, 2 * rows
     for at, ref in ((0, texts_ref), (step, images_ref)):
-        own, got = own_ref[at : at + step, :], got_ref[at : at + step, :]
-        ref[...] = jnp.concatenate([jnp.where(on0, own, got), jnp.where(on0, got, own)], axis=0).T
+        own, got = own_ref[:, at : at + step], got_ref[:, at : at + step]
+        ref[...] = jnp.concatenate([jnp.where(on0, own, got), jnp.where(on0, got, own)], axis=1)
 
 
 def near_kernel(
@@ -199,20 +203,36 @@
     out_ref[...] = own_ref[...] + decoded(r1_ref)[0]
 
 
-def text_first_kernel(rows, feats, own_ref, r2_ref, r3_ref, sums_ref, out_ref, *messages):
-    total = own_ref[...] + decoded(r2_ref)[0] + decoded(r3_ref)[0]
-    out_ref[...] = jnp.concatenate([total[0:rows], sums_ref[...]], axis=0)
-    for i, m_ref in enumerate(messages):
-        m_ref[...] = message([total[(i + 1) * rows : (i + 2) * rows]], feats, split3(sums_ref[0:1, :]))
-
-
-def text_last_kernel(scale_ref, own_ref, r1_ref, r2_ref, r3_ref, out_ref, sums_ref):
+def text_first_kernel(rows, feats, own_ref, r2_ref, r3_ref, sums_ref, out_ref, m1_ref, m2_ref, m3_ref, total):
+    tops = [r[4 * rows :, :].astype(F32)[7:8] for r in (r2_ref, r3_ref)]
+
+    def add(step, carry):
+        at = pl.ds(pl.multiple_of(step * 32, 32), 32)
+        total[at, :] = own_ref[at, :] + decode(r2_ref[at, :], tops[0]) + decode(r3_ref[at, :], tops[1])
+        return carry
+
+    lax.fori_loop(0, 4 * rows // 32, add, 0)
+    out_ref[...] = jnp.concatenate([total[0:rows, :], sums_ref[...]], axis=0)
+    for i, m_ref in enumerate((m1_ref, m2_ref, m3_ref)):
+        m_ref[...] = message([total[(i + 1) * rows : (i + 2) * rows, :]], feats, split3(sums_ref[0:1, :]))
+
+
+def close_kernel(rows, width, info_ref, scale_ref, own_ref, r1_ref, r2_ref, r3_ref, img_ref, back_ref, mine_ref, other_ref, sums_ref):
+    half = 2 * width
+    on0, lo0 = info_ref[0] == 0, info_ref[1] == 0
     total, sums = with_scalars(own_ref, (r1_ref, r2_ref, r3_ref))
-    out_ref[...] = total * scale_ref[0]
+    text = total * scale_ref[0]
     sums_ref[...] = jnp.broadcast_to(sums[:, :128], (8, 128))
+    keep, back = img_ref[:, :half], back_ref[...]
+    parts = (text[:, :half], text[:, half:], jnp.where(lo0, keep, back), jnp.where(lo0, back, keep))
+    whole = jnp.concatenate(parts, axis=0)
+    left, right = whole[:, :width], whole[:, width:]
+    mine_ref[...] = jnp.where(on0, left, right).T
+    other_ref[...] = jnp.where(on0, right, left).T
 
 
 VMEM = pl.BlockSpec(memory_space=pltpu.VMEM)
+HBM = pl.BlockSpec(memory_space=pltpu.HBM)
 SMEM = pl.BlockSpec(memory_space=pltpu.SMEM)
 
 
@@ -242,17 +262,17 @@
     def bf16(*shape):
         return jax.ShapeDtypeStruct(shape, BF)
 
-    def call(kernel, name, out_shape, *args, scalars=0, scratch=(), mib=20, products=0, brief=False):
+    def call(kernel, name, out_shape, *args, scalars=0, scratch=(), mib=20, products=0, where=VMEM):
         return pl.pallas_call(
             kernel,
             out_shape=out_shape,
-            in_specs=[SMEM] * scalars + [VMEM] * (len(args) - scalars),
+            in_specs=[SMEM] * scalars + [where] * (len(args) - scalars),
             out_specs=[VMEM] * len(out_shape),
             scratch_shapes=scratch,
             compiler_params=grant(mib),
             cost_estimate=pl.CostEstimate(
                 flops=products * 2 * quarter * 2 * quarter * 2 * feats,
-                bytes_accessed=0 if brief else sum(a.size * a.dtype.itemsize for a in (*args, *out_shape)),
+                bytes_accessed=sum(a.size * a.dtype.itemsize for a in (*args, *out_shape)),
                 transcendentals=products * 4 * quarter * quarter,
             ),
             name=name,
@@ -260,7 +280,8 @@
 
     info = jnp.stack([core, z_lo]).astype(jnp.int32)
     keep, send = call(
-        functools.partial(split_kernel, rows), "split", [bf16(height, width)] * 2, info, caption_embeds.T, picture_embeds.T, scalars=1
+        functools.partial(split_kernel, rows), "split", [bf16(height, width)] * 2, info, caption_embeds.T, picture_embeds.T, scalars=1,
+        where=HBM, mib=62, scratch=[pltpu.VMEM((2, width, height), BF), pltpu.SemaphoreType.DMA((2,))],
     )
     chip = jnp.concatenate(by(on0, keep, swap(send, CORE)), axis=1)
     packed = jnp.concatenate([chip[:rows], chip[rows:step]], axis=1)
@@ -309,14 +330,14 @@
     text, *messages = call(
         functools.partial(text_first_kernel, rows, feats), "text_first",
         [f32(rows + 8, feats)] + [bf16(rows + 8, feats)] * 3, text, got2, got3, sums,
+        scratch=[pltpu.VMEM((quarter, feats), F32)],
     )
     got = [swap(m, y_mask(i), z_mask(i)) for i, m in zip((1, 2, 3), messages)]
-    text, sums = call(
-        text_last_kernel, "text_last", [f32(rows, feats), f32(8, 128)], logit_scaler, text, *got, scalars=1, products=2
-    )
-    image = jnp.concatenate(by(lo0, img[:, :half], after(swap(img[:, half:], z_mask(1)), text)), axis=0)
-    whole = jnp.concatenate([text[:, :half], text[:, half:], image], axis=0)
-    mine, other = by(on0, whole[:, :width], whole[:, width:])
+    back = swap(img[:, half:], z_mask(1))
+    mine, other, sums = call(
+        functools.partial(close_kernel, rows, width), "close", [f32(width, height), f32(width, height), f32(8, 128)],
+        info, logit_scaler, text, *got, img, back, scalars=2,
+    )
     sums = after(sums, other)
     other = swap(other, CORE)
     text_grad, image_grad = call(

time: 98.6 us -> 101 us (1.024)
  Pallas kernels: 24.4 us -> 27.1 us
  local copies, waits for them, and re-layouts: 2.92 us -> 0.63 us
  other arithmetic: 1.34 us -> 2.41 us
    pallas_call x10, Pallas kernels: 24.4 us -> 27.1 us  [call(): pl.pallas_call(kernel, out_shape=out_shape, in_specs=[SMEM] * scalars + [...]
    unnamed x4 -> x2, local copies, waits for them, and re-layouts: 1.87 us -> 0.01 us
  transfers between devices with their start and end apart: 27 -> 27, of which waited for: 17 -> 16; matrix products, arithmetic and copies ran while one was open for 1% -> 1% of each run, Pallas kernels for 21% -> 20%
where the time goes in v12:
time: 101 us
  starting transfers between devices  37 us (37%)
  waiting for transfers between devices  31.3 us (31%)
  Pallas kernels  27.1 us (27%)
  other arithmetic  2.41 us (2%)
  between operations  2.09 us (2%)
    ppermute x27, starting transfers between devices, swap(): lax.ppermute(array, AXES, [(i, i ^ (mask1 if i & 1 else mask0)) for i in...  37 us
    ppermute x27, waiting for transfers between devices, swap(): lax.ppermute(array, AXES, [(i, i ^ (mask1 if i & 1 else mask0)) for i in...  31.3 us
    pallas_call x10, Pallas kernels, call(): pl.pallas_call(kernel, out_shape=out_shape, in_specs=[SMEM] * scalars + [...  27.1 us
  transfers between devices with their start and end apart: 27, of which 16 were waited for; matrix products, arithmetic and copies ran while one was open for 1% of the time, Pallas kernels for 20%

profile of v12, /device:TPU:1, one launch (start us, length us, event | category | flops | bytes accessed | tf_op | source)
XLA Modules:
  0.0 100.6 jit_solution(1118788039562797021)
XLA Ops:
  0.6 0.6 pad_add_fusion.info_ref
  1.2 2.7 %split.1 = (bf16[352,288]{1,0:T(8,128)(2,1)}, bf16[352,288]{1,0:T(8,128)(2,1)}) custom-call(s32[2]{0:T(128)} %pad_add_fusion.info_ref, bf16[288,352]{1,0:T(8,128)(2,1)} %bitcast.13, bf16[288,352]{1,0:T(8,128)(2,1)} %bitcast.14), custom_call_target="tpu_custom_call" | custom-call | bytes 811016 | tf_op jit(solution)/shard_map/split/pallas_call | solution.py:266
  4.0 1.5 %collective-permute-start = (bf16[352,288]{1,0:T(8,128)(2,1)}, bf16[352,288]{1,0:T(8,128)(2,1)S(1)}, u32[]{:S(2)}, u32[]{:S(2)}) collective-permute-start(bf16[352,288]{1,0:T(8,128)(2,1)} %get-tuple-element.41), channel_id=1, source_target_pairs={{0,1},{1,0},{2,3},{3,2},{4,5},{5,4},{6,7},{7,6},{8,9},{9,8},{10,11... | collective-permute-start | bytes 608264 | tf_op jit(solution)/shard_map/ppermute | solution.py:31
  5.5 1.4 %collective-permute-done = bf16[352,288]{1,0:T(8,128)(2,1)S(1)} collective-permute-done((bf16[352,288]{1,0:T(8,128)(2,1)}, bf16[352,288]{1,0:T(8,128)(2,1)S(1)}, u32[]{:S(2)}, u32[]{:S(2)}) %collective-permute-start) | collective-permute-done | bytes 202784 | tf_op jit(solution)/shard_map/ppermute | solution.py:31
  6.9 1.0 %broadcast_select_fusion = (bf16[352,288]{1,0:T(8,128)(2,1)S(1)}, bf16[352,288]{1,0:T(8,128)(2,1)S(1)}) fusion(bf16[352,288]{1,0:T(8,128)(2,1)S(1)} %collective-permute-done, bf16[352,288]{1,0:T(8,128)(2,1)} %get-tuple-element.40, pred[]{:T(512)S(6)} %eq.6), kind=kLoop, calls=%fused_computation.8 | loop fusion | flops 202752 | bytes 811009 | tf_op jit(solution)/shard_map/jit(_where)/select_n | solution.py:257
  8.1 1.8 %collective-permute-start.6 = (bf16[88,576]{1,0:T(8,128)(2,1)S(1)}, bf16[88,576]{1,0:T(8,128)(2,1)S(1)}, u32[]{:S(2)}, u32[]{:S(2)}) collective-permute-start(bf16[88,576]{1,0:T(8,128)(2,1)S(1)} %get-tuple-element.79), channel_id=1, source_target_pairs={{0,2},{1,3},{2,0},{3,1},{4,6},{5,7},{6,4},{7,5},{8,10},{9,11},{10,... | collective-permute-start | bytes 304136 | tf_op jit(solution)/shard_map/ppermute | solution.py:31
  10.1 3.4 %collective-permute-start.2 = (bf16[88,1152]{1,0:T(8,128)(2,1)S(1)}, bf16[88,1152]{1,0:T(8,128)(2,1)S(1)}, u32[]{:S(2)}, u32[]{:S(2)}) collective-permute-start(bf16[88,1152]{1,0:T(8,128)(2,1)S(1)} %pad_maximum_fusion.2), channel_id=1, source_target_pairs={{0,32},{1,65},{2,34},{3,67},{4,36},{5,69},{6,38},{7,71},{8,40},{9,... | collective-permute-start | bytes 608264 | tf_op jit(solution)/shard_map/ppermute | solution.py:31
  14.0 2.6 %collective-permute-start.9 = (bf16[88,1152]{1,0:T(8,128)(2,1)S(1)}, bf16[88,1152]{1,0:T(8,128)(2,1)S(1)}, u32[]{:S(2)}, u32[]{:S(2)}) collective-permute-start(bf16[88,1152]{1,0:T(8,128)(2,1)S(1)} %pad_maximum_fusion.3), channel_id=1, source_target_pairs={{0,12},{1,13},{2,14},{3,15},{4,8},{5,9},{6,10},{7,11},{8,4},{9,5},... | collective-permute-start | bytes 608264 | tf_op jit(solution)/shard_map/ppermute | solution.py:31
  16.6 0.5 collective-permute-start.8
  17.1 1.8 %collective-permute-done.2 = bf16[88,1152]{1,0:T(8,128)(2,1)S(1)} collective-permute-done((bf16[88,1152]{1,0:T(8,128)(2,1)S(1)}, bf16[88,1152]{1,0:T(8,128)(2,1)S(1)}, u32[]{:S(2)}, u32[]{:S(2)}) %collective-permute-start.2) | collective-permute-done | bytes 202784 | tf_op jit(solution)/shard_map/ppermute | solution.py:31
  18.9 1.2 %collective-permute-start.7 = (bf16[88,1152]{1,0:T(8,128)(2,1)S(1)}, bf16[88,1152]{1,0:T(8,128)(2,1)S(1)}, u32[]{:S(2)}, u32[]{:S(2)}) collective-permute-start(bf16[88,1152]{1,0:T(8,128)(2,1)S(1)} %pad_maximum_fusion.3), channel_id=1, source_target_pairs={{0,4},{1,5},{2,6},{3,7},{4,0},{5,1},{6,2},{7,3},{8,12},{9,13},{10,... | collective-permute-start | bytes 608264 | tf_op jit(solution)/shard_map/ppermute | solution.py:31
  20.1 1.0 %collective-permute-done.3 = bf16[88,1152]{1,0:T(8,128)(2,1)S(1)} collective-permute-done((bf16[88,1152]{1,0:T(8,128)(2,1)S(1)}, bf16[88,1152]{1,0:T(8,128)(2,1)S(1)}, u32[]{:S(2)}, u32[]{:S(2)}) %collective-permute-start.3) | collective-permute-done | bytes 202784 | tf_op jit(solution)/shard_map/ppermute | solution.py:31
  21.2 2.8 %collective-permute-start.5 = (bf16[4,88,1152]{2,1,0:T(8,128)(2,1)S(1)}, bf16[4,88,1152]{2,1,0:T(8,128)(2,1)S(1)}, u32[]{:S(2)}, u32[]{:S(2)}) collective-permute-start(bf16[4,88,1152]{2,1,0:T(8,128)(2,1)S(1)} %pad_maximum_fusion.ta_ref), channel_id=1, source_target_pairs={{0,66},{1,49},{2,64},{3,51},{4,70},{5,53},{6,68},{7,55},{8,74},{9,... | collective-permute-start | bytes 2433032 | tf_op jit(solution)/shard_map/ppermute | solution.py:31
  24.1 1.0 %collective-permute-done.9 = bf16[88,1152]{1,0:T(8,128)(2,1)S(1)} collective-permute-done((bf16[88,1152]{1,0:T(8,128)(2,1)S(1)}, bf16[88,1152]{1,0:T(8,128)(2,1)S(1)}, u32[]{:S(2)}, u32[]{:S(2)}) %collective-permute-start.9) | collective-permute-done | bytes 202784 | tf_op jit(solution)/shard_map/ppermute | solution.py:31
  25.1 0.8 collective-permute-done.7
  26.0 1.9 %collective-permute-start.10 = (bf16[352,1152]{1,0:T(8,128)(2,1)S(1)}, bf16[352,1152]{1,0:T(8,128)(2,1)S(1)}, u32[]{:S(2)}, u32[]{:S(2)}) collective-permute-start(bf16[352,1152]{1,0:T(8,128)(2,1)S(1)} %pad_maximum_fusion.1.im0_ref), channel_id=1, source_target_pairs={{0,1},{1,0},{2,3},{3,2},{4,5},{5,4},{6,7},{7,6},{8,9},{9,8},{10,11... | collective-permute-start | bytes 2433032 | tf_op jit(solution)/shard_map/ppermute | solution.py:31
  29.2 3.0 %collective-permute-start.11 = (bf16[4,88,1152]{2,1,0:T(8,128)(2,1)S(1)}, bf16[4,88,1152]{2,1,0:T(8,128)(2,1)S(1)}, u32[]{:S(2)}, u32[]{:S(2)}) collective-permute-start(bf16[4,88,1152]{2,1,0:T(8,128)(2,1)S(1)} %pad_maximum_fusion.ta_ref), channel_id=1, source_target_pairs={{0,64},{1,33},{2,66},{3,35},{4,68},{5,37},{6,70},{7,39},{8,72},{9,... | collective-permute-start | bytes 2433032 | tf_op jit(solution)/shard_map/ppermute | solution.py:31
  32.2 1.8 %collective-permute-done.5.tb_ref = bf16[4,88,1152]{2,1,0:T(8,128)(2,1)S(1)} collective-permute-done((bf16[4,88,1152]{2,1,0:T(8,128)(2,1)S(1)}, bf16[4,88,1152]{2,1,0:T(8,128)(2,1)S(1)}, u32[]{:S(2)}, u32[]{:S(2)}) %collective-permute-start.5) | collective-permute-done | bytes 811040 | tf_op jit(solution)/shard_map/ppermute | solution.py:31
  34.0 1.5 %collective-permute-done.4.tb_ref = bf16[4,88,1152]{2,1,0:T(8,128)(2,1)S(1)} collective-permute-done((bf16[4,88,1152]{2,1,0:T(8,128)(2,1)S(1)}, bf16[4,88,1152]{2,1,0:T(8,128)(2,1)S(1)}, u32[]{:S(2)}, u32[]{:S(2)}) %collective-permute-start.4) | collective-permute-done | bytes 811040 | tf_op jit(solution)/shard_map/ppermute | solution.py:31
  35.5 5.9 %tile_near.1 = (f32[352,1152]{1,0:T(8,128)S(1)}, bf16[360,1152]{1,0:T(8,128)(2,1)S(1)}, bf16[704,1152]{1,0:T(8,128)(2,1)S(1)}, bf16[704,704]{1,0:T(8,128)(2,1)S(1)}, f32[8,128]{1,0:T(8,128)S(1)}) custom-call(s32[2]{0:T(128)S(1)} %copy-done, f32[2]{0:T(128)S(1)} %pad_maximum_fusion.5.scale_ref, bf16[4,88,1152]{2,1,0:T(8,128)(2,1)S(1)} %pad_maximum_fusion.ta_ref, ...), custom_call_target="tpu_custom_call" | custom-call | flops 2283798528 | bytes 8312848 | tf_op jit(solution)/shard_map/tile_near/pallas_call | solution.py:266
  41.6 1.6 %image_near.1.before_ref = f32[704,1152]{1,0:T(8,128)S(1)} custom-call(bf16[704,1152]{1,0:T(8,128)(2,1)S(1)} %get-tuple-element.45.t_rel, bf16[704,704]{1,0:T(8,128)(2,1)S(1)} %get-tuple-element.46.coeff_low), custom_call_target="tpu_custom_call" | custom-call | flops 1141899264 | bytes 5857280 | tf_op jit(solution)/shard_map/image_near/pallas_call | solution.py:266
  43.2 0.7 collective-permute-done.11.ta_ref
  44.0 8.4 %tile_far.1 = (bf16[360,1152]{1,0:T(8,128)(2,1)S(1)}, bf16[360,1152]{1,0:T(8,128)(2,1)S(1)}, f32[360,1152]{1,0:T(8,128)S(1)}, f32[360,1152]{1,0:T(8,128)S(1)}) custom-call(s32[2]{0:T(128)S(1)} %copy-done, f32[2]{0:T(128)S(1)} %pad_maximum_fusion.5.scale_ref, bf16[4,88,1152]{2,1,0:T(8,128)(2,1)S(1)} %collective-permute-done.11.ta_ref, ...), custom_call_target="tpu_custom_call" | custom-call | flops 3425697792 | bytes 11468816 | tf_op jit(solution)/shard_map/tile_far/pallas_call | solution.py:266
  52.4 0.8 collective-permute-done.12.r1_ref
  53.2 2.1 %collective-permute-start.13 = (f32[360,1152]{1,0:T(8,128)S(1)}, f32[360,1152]{1,0:T(8,128)S(1)}, u32[]{:S(2)}, u32[]{:S(2)}) collective-permute-start(f32[360,1152]{1,0:T(8,128)S(1)} %get-tuple-element.53), channel_id=1, source_target_pairs={{0,1},{1,0},{2,3},{3,2},{4,5},{5,4},{6,7},{7,6},{8,9},{9,8},{10,11... | collective-permute-start | bytes 4976648 | tf_op jit(solution)/shard_map/ppermute | solution.py:31
  55.2 1.6 %collective-permute-start.14 = (bf16[360,1152]{1,0:T(8,128)(2,1)S(1)}, bf16[360,1152]{1,0:T(8,128)(2,1)S(1)}, u32[]{:S(2)}, u32[]{:S(2)}) collective-permute-start(bf16[360,1152]{1,0:T(8,128)(2,1)S(1)} %get-tuple-element.59), channel_id=1, source_target_pairs={{0,64},{1,33},{2,66},{3,35},{4,68},{5,37},{6,70},{7,39},{8,72},{9,... | collective-permute-start | bytes 2488328 | tf_op jit(solution)/shard_map/ppermute | solution.py:31
  56.9 0.8 collective-permute-start.15
  57.7 0.7 collective-permute-done.13.other_ref
  58.4 1.0 image_first.1
  59.4 1.3 %collective-permute-start.16 = (bf16[96,1152]{1,0:T(8,128)(2,1)S(1)}, bf16[96,1152]{1,0:T(8,128)(2,1)S(1)}, u32[]{:S(2)}, u32[]{:S(2)}) collective-permute-start(bf16[96,1152]{1,0:T(8,128)(2,1)S(1)} %get-tuple-element.54), channel_id=1, source_target_pairs={{0,4},{1,5},{2,6},{3,7},{4,0},{5,1},{6,2},{7,3},{8,12},{9,13},{10,... | collective-permute-start | bytes 663560 | tf_op jit(solution)/shard_map/ppermute | solution.py:31
  60.7 2.5 %collective-permute-start.17 = (bf16[96,1152]{1,0:T(8,128)(2,1)S(1)}, bf16[96,1152]{1,0:T(8,128)(2,1)S(1)}, u32[]{:S(2)}, u32[]{:S(2)}) collective-permute-start(bf16[96,1152]{1,0:T(8,128)(2,1)S(1)} %get-tuple-element.55), channel_id=1, source_target_pairs={{0,8},{1,9},{2,10},{3,11},{4,12},{5,13},{6,14},{7,15},{8,0},{9,1},... | collective-permute-start | bytes 663560 | tf_op jit(solution)/shard_map/ppermute | solution.py:31
  63.3 0.8 text_near.1.own_ref
  64.1 1.8 %collective-permute-done.16.r1_ref = bf16[96,1152]{1,0:T(8,128)(2,1)S(1)} collective-permute-done((bf16[96,1152]{1,0:T(8,128)(2,1)S(1)}, bf16[96,1152]{1,0:T(8,128)(2,1)S(1)}, u32[]{:S(2)}, u32[]{:S(2)}) %collective-permute-start.16) | collective-permute-done | bytes 221216 | tf_op jit(solution)/shard_map/ppermute | solution.py:31
  65.9 7.0 %collective-permute-done.17.r2_ref = bf16[96,1152]{1,0:T(8,128)(2,1)S(1)} collective-permute-done((bf16[96,1152]{1,0:T(8,128)(2,1)S(1)}, bf16[96,1152]{1,0:T(8,128)(2,1)S(1)}, u32[]{:S(2)}, u32[]{:S(2)}) %collective-permute-start.17) | collective-permute-done | bytes 221216 | tf_op jit(solution)/shard_map/ppermute | solution.py:31
  72.9 2.3 %collective-permute-done.18.r3_ref = bf16[96,1152]{1,0:T(8,128)(2,1)S(1)} collective-permute-done((bf16[96,1152]{1,0:T(8,128)(2,1)S(1)}, bf16[96,1152]{1,0:T(8,128)(2,1)S(1)}, u32[]{:S(2)}, u32[]{:S(2)}) %collective-permute-start.18) | collective-permute-done | bytes 221216 | tf_op jit(solution)/shard_map/ppermute | solution.py:31
  75.2 0.6 image_last.1
  75.8 1.4 %collective-permute-done.15.r3_ref = bf16[360,1152]{1,0:T(8,128)(2,1)S(1)} collective-permute-done((bf16[360,1152]{1,0:T(8,128)(2,1)S(1)}, bf16[360,1152]{1,0:T(8,128)(2,1)S(1)}, u32[]{:S(2)}, u32[]{:S(2)}) %collective-permute-start.15) | collective-permute-done | bytes 829472 | tf_op jit(solution)/shard_map/ppermute | solution.py:31
  77.2 2.6 %text_first.1 = (f32[96,1152]{1,0:T(8,128)S(1)}, bf16[96,1152]{1,0:T(8,128)(2,1)S(1)}, bf16[96,1152]{1,0:T(8,128)(2,1)S(1)}, bf16[96,1152]{1,0:T(8,128)(2,1)S(1)}) custom-call(f32[352,1152]{1,0:T(8,128)S(1)} %text_near.1.own_ref, bf16[360,1152]{1,0:T(8,128)(2,1)S(1)} %collective-permute-done.14.r2_ref, bf16[360,1152]{1,0:T(8,128)(2,1)S(1)} %collective-permute-done.15.r3_ref, ...), custom_call_target="tpu_custom_call" | custom-call | bytes 4423680 | tf_op jit(solution)/shard_map/text_first/pallas_call | solution.py:266
  79.9 0.5 collective-permute-start.19
  80.4 1.8 %collective-permute-start.20 = (bf16[96,1152]{1,0:T(8,128)(2,1)S(1)}, bf16[96,1152]{1,0:T(8,128)(2,1)S(1)}, u32[]{:S(2)}, u32[]{:S(2)}) collective-permute-start(bf16[96,1152]{1,0:T(8,128)(2,1)S(1)} %get-tuple-element.65), channel_id=1, source_target_pairs={{0,32},{1,65},{2,34},{3,67},{4,36},{5,69},{6,38},{7,71},{8,40},{9,... | collective-permute-start | bytes 663560 | tf_op jit(solution)/shard_map/ppermute | solution.py:31
  82.2 1.6 %collective-permute-start.21 = (bf16[96,1152]{1,0:T(8,128)(2,1)S(1)}, bf16[96,1152]{1,0:T(8,128)(2,1)S(1)}, u32[]{:S(2)}, u32[]{:S(2)}) collective-permute-start(bf16[96,1152]{1,0:T(8,128)(2,1)S(1)} %get-tuple-element.66), channel_id=1, source_target_pairs={{0,48},{1,67},{2,50},{3,65},{4,52},{5,71},{6,54},{7,69},{8,56},{9,... | collective-permute-start | bytes 663560 | tf_op jit(solution)/shard_map/ppermute | solution.py:31
  84.0 6.7 %collective-permute-done.22.back_ref = f32[88,576]{1,0:T(8,128)S(1)} collective-permute-done((f32[88,576]{1,0:T(8,128)S(1)}, f32[88,576]{1,0:T(8,128)S(1)}, u32[]{:S(2)}, u32[]{:S(2)}) %collective-permute-start.22) | collective-permute-done | bytes 202784 | tf_op jit(solution)/shard_map/ppermute | solution.py:31
  90.8 1.8 %close.1 = (f32[288,352]{1,0:T(8,128)S(1)}, f32[288,352]{1,0:T(8,128)S(1)}, f32[8,128]{1,0:T(8,128)S(1)}) custom-call(s32[2]{0:T(128)S(1)} %copy-done, f32[1]{0:T(128)S(6)} %copy.7.scale_ref, f32[96,1152]{1,0:T(8,128)S(1)} %get-tuple-element.63.own_ref, bf16[96,1152]{1,0:T(8,128)(2,1)S(1)} %collective-permute-done.19.r1_ref, ...), custom_call_target="tpu_custom_call" | custom-call | bytes 2529292 | tf_op jit(solution)/shard_map/close/pallas_call | solution.py:266
  92.6 2.0 %collective-permute-start.23 = (f32[288,352]{1,0:T(8,128)S(1)}, f32[288,352]{1,0:T(8,128)S(1)}, u32[]{:S(2)}, u32[]{:S(2)}) collective-permute-start(f32[288,352]{1,0:T(8,128)S(1)} %get-tuple-element.69), channel_id=1, source_target_pairs={{0,1},{1,0},{2,3},{3,2},{4,5},{5,4},{6,7},{7,6},{8,9},{9,8},{10,11... | collective-permute-start | bytes 1216520 | tf_op jit(solution)/shard_map/ppermute | solution.py:31
  94.6 1.5 %collective-permute-start.26 = (f32[8,128]{1,0:T(8,128)S(1)}, f32[8,128]{1,0:T(8,128)S(1)}, u32[]{:S(2)}, u32[]{:S(2)}) collective-permute-start(f32[8,128]{1,0:T(8,128)S(1)} %get-tuple-element.73), channel_id=1, source_target_pairs={{0,66},{1,49},{2,64},{3,51},{4,70},{5,53},{6,68},{7,55},{8,74},{9,... | collective-permute-start | bytes 12296 | tf_op jit(solution)/shard_map/ppermute | solution.py:31
  96.4 1.4 %collective-permute-start.24 = (f32[8,128]{1,0:T(8,128)S(1)}, f32[8,128]{1,0:T(8,128)S(1)}, u32[]{:S(2)}, u32[]{:S(2)}) collective-permute-start(f32[8,128]{1,0:T(8,128)S(1)} %get-tuple-element.73), channel_id=1, source_target_pairs={{0,2},{1,17},{2,0},{3,19},{4,6},{5,21},{6,4},{7,23},{8,10},{9,25},... | collective-permute-start | bytes 12296 | tf_op jit(solution)/shard_map/ppermute | solution.py:31
  97.9 1.6 %join.1 = (f32[288,352]{1,0:T(8,128)}, f32[288,352]{1,0:T(8,128)}) custom-call(s32[2]{0:T(128)S(1)} %copy-done, f32[288,352]{1,0:T(8,128)S(1)} %get-tuple-element.68.own_ref, f32[288,352]{1,0:T(8,128)S(1)} %collective-permute-done.23.got_ref), custom_call_target="tpu_custom_call" | custom-call | bytes 1622024 | tf_op jit(solution)/shard_map/join/pallas_call | solution.py:266
  99.5 0.6 collective-permute-done.25
  (31 shorter events, 2.7 us)
Async XLA Ops:
  4.0 2.9 %collective-permute-start = (bf16[352,288]{1,0:T(8,128)(2,1)}, bf16[352,288]{1,0:T(8,128)(2,1)S(1)}, u32[]{:S(2)}, u32[]{:S(2)}) collective-permute-start(bf16[352,288]{1,0:T(8,128)(2,1)} %get-tuple-element.41), channel_id=1, source_target_pairs={{0,1},{1,0},{2,3},{3,2},{4,5},{5,4},{6,7},{7,6},{8,9},{9,8},{10,11... | collective-permute-start | bytes 608264 | tf_op jit(solution)/shard_map/ppermute | solution.py:31
  8.1 5.8 %collective-permute-start.6 = (bf16[88,576]{1,0:T(8,128)(2,1)S(1)}, bf16[88,576]{1,0:T(8,128)(2,1)S(1)}, u32[]{:S(2)}, u32[]{:S(2)}) collective-permute-start(bf16[88,576]{1,0:T(8,128)(2,1)S(1)} %get-tuple-element.79), channel_id=1, source_target_pairs={{0,2},{1,3},{2,0},{3,1},{4,6},{5,7},{6,4},{7,5},{8,10},{9,11},{10,... | collective-permute-start | bytes 304136 | tf_op jit(solution)/shard_map/ppermute | solution.py:31
  10.1 8.7 %collective-permute-start.2 = (bf16[88,1152]{1,0:T(8,128)(2,1)S(1)}, bf16[88,1152]{1,0:T(8,128)(2,1)S(1)}, u32[]{:S(2)}, u32[]{:S(2)}) collective-permute-start(bf16[88,1152]{1,0:T(8,128)(2,1)S(1)} %pad_maximum_fusion.2), channel_id=1, source_target_pairs={{0,32},{1,65},{2,34},{3,67},{4,36},{5,69},{6,38},{7,71},{8,40},{9,... | collective-permute-start | bytes 608264 | tf_op jit(solution)/shard_map/ppermute | solution.py:31
  13.5 6.6 %collective-permute-start.1 = (bf16[88,1152]{1,0:T(8,128)(2,1)S(1)}, bf16[88,1152]{1,0:T(8,128)(2,1)S(1)}, u32[]{:S(2)}, u32[]{:S(2)}) collective-permute-start(bf16[88,1152]{1,0:T(8,128)(2,1)S(1)} %pad_maximum_fusion.2), channel_id=1, source_target_pairs={{0,16},{1,3},{2,18},{3,1},{4,20},{5,7},{6,22},{7,5},{8,24},{9,11},... | collective-permute-start | bytes 608264 | tf_op jit(solution)/shard_map/ppermute | solution.py:31
  13.5 7.6 %collective-permute-start.3 = (bf16[88,1152]{1,0:T(8,128)(2,1)S(1)}, bf16[88,1152]{1,0:T(8,128)(2,1)S(1)}, u32[]{:S(2)}, u32[]{:S(2)}) collective-permute-start(bf16[88,1152]{1,0:T(8,128)(2,1)S(1)} %pad_maximum_fusion.2), channel_id=1, source_target_pairs={{0,48},{1,67},{2,50},{3,65},{4,52},{5,71},{6,54},{7,69},{8,56},{9,... | collective-permute-start | bytes 608264 | tf_op jit(solution)/shard_map/ppermute | solution.py:31
  14.0 11.1 %collective-permute-start.9 = (bf16[88,1152]{1,0:T(8,128)(2,1)S(1)}, bf16[88,1152]{1,0:T(8,128)(2,1)S(1)}, u32[]{:S(2)}, u32[]{:S(2)}) collective-permute-start(bf16[88,1152]{1,0:T(8,128)(2,1)S(1)} %pad_maximum_fusion.3), channel_id=1, source_target_pairs={{0,12},{1,13},{2,14},{3,15},{4,8},{5,9},{6,10},{7,11},{8,4},{9,5},... | collective-permute-start | bytes 608264 | tf_op jit(solution)/shard_map/ppermute | solution.py:31
  16.6 8.5 %collective-permute-start.8 = (bf16[88,1152]{1,0:T(8,128)(2,1)S(1)}, bf16[88,1152]{1,0:T(8,128)(2,1)S(1)}, u32[]{:S(2)}, u32[]{:S(2)}) collective-permute-start(bf16[88,1152]{1,0:T(8,128)(2,1)S(1)} %pad_maximum_fusion.3), channel_id=1, source_target_pairs={{0,8},{1,9},{2,10},{3,11},{4,12},{5,13},{6,14},{7,15},{8,0},{9,1},... | collective-permute-start | bytes 608264 | tf_op jit(solution)/shard_map/ppermute | solution.py:31
  18.9 7.0 %collective-permute-start.7 = (bf16[88,1152]{1,0:T(8,128)(2,1)S(1)}, bf16[88,1152]{1,0:T(8,128)(2,1)S(1)}, u32[]{:S(2)}, u32[]{:S(2)}) collective-permute-start(bf16[88,1152]{1,0:T(8,128)(2,1)S(1)} %pad_maximum_fusion.3), channel_id=1, source_target_pairs={{0,4},{1,5},{2,6},{3,7},{4,0},{5,1},{6,2},{7,3},{8,12},{9,13},{10,... | collective-permute-start | bytes 608264 | tf_op jit(solution)/shard_map/ppermute | solution.py:31
  21.1 14.3 %copy-start = (s32[2]{0:T(128)S(1)}, s32[2]{0:T(128)}, u32[]{:S(2)}) copy-start(s32[2]{0:T(128)} %pad_add_fusion.info_ref) | copy-start | bytes 28
  21.2 12.8 %collective-permute-start.5 = (bf16[4,88,1152]{2,1,0:T(8,128)(2,1)S(1)}, bf16[4,88,1152]{2,1,0:T(8,128)(2,1)S(1)}, u32[]{:S(2)}, u32[]{:S(2)}) collective-permute-start(bf16[4,88,1152]{2,1,0:T(8,128)(2,1)S(1)} %pad_maximum_fusion.ta_ref), channel_id=1, source_target_pairs={{0,66},{1,49},{2,64},{3,51},{4,70},{5,53},{6,68},{7,55},{8,74},{9,... | collective-permute-start | bytes 2433032 | tf_op jit(solution)/shard_map/ppermute | solution.py:31
  24.1 11.4 %collective-permute-start.4 = (bf16[4,88,1152]{2,1,0:T(8,128)(2,1)S(1)}, bf16[4,88,1152]{2,1,0:T(8,128)(2,1)S(1)}, u32[]{:S(2)}, u32[]{:S(2)}) collective-permute-start(bf16[4,88,1152]{2,1,0:T(8,128)(2,1)S(1)} %pad_maximum_fusion.ta_ref), channel_id=1, source_target_pairs={{0,2},{1,17},{2,0},{3,19},{4,6},{5,21},{6,4},{7,23},{8,10},{9,25},... | collective-permute-start | bytes 2433032 | tf_op jit(solution)/shard_map/ppermute | solution.py:31
  26.0 9.5 %collective-permute-start.10 = (bf16[352,1152]{1,0:T(8,128)(2,1)S(1)}, bf16[352,1152]{1,0:T(8,128)(2,1)S(1)}, u32[]{:S(2)}, u32[]{:S(2)}) collective-permute-start(bf16[352,1152]{1,0:T(8,128)(2,1)S(1)} %pad_maximum_fusion.1.im0_ref), channel_id=1, source_target_pairs={{0,1},{1,0},{2,3},{3,2},{4,5},{5,4},{6,7},{7,6},{8,9},{9,8},{10,11... | collective-permute-start | bytes 2433032 | tf_op jit(solution)/shard_map/ppermute | solution.py:31
  29.2 14.8 %collective-permute-start.11 = (bf16[4,88,1152]{2,1,0:T(8,128)(2,1)S(1)}, bf16[4,88,1152]{2,1,0:T(8,128)(2,1)S(1)}, u32[]{:S(2)}, u32[]{:S(2)}) collective-permute-start(bf16[4,88,1152]{2,1,0:T(8,128)(2,1)S(1)} %pad_maximum_fusion.ta_ref), channel_id=1, source_target_pairs={{0,64},{1,33},{2,66},{3,35},{4,68},{5,37},{6,70},{7,39},{8,72},{9,... | collective-permute-start | bytes 2433032 | tf_op jit(solution)/shard_map/ppermute | solution.py:31
  41.3 11.9 %collective-permute-start.12 = (bf16[360,1152]{1,0:T(8,128)(2,1)S(1)}, bf16[360,1152]{1,0:T(8,128)(2,1)S(1)}, u32[]{:S(2)}, u32[]{:S(2)}) collective-permute-start(bf16[360,1152]{1,0:T(8,128)(2,1)S(1)} %get-tuple-element.52), channel_id=1, source_target_pairs={{0,2},{1,17},{2,0},{3,19},{4,6},{5,21},{6,4},{7,23},{8,10},{9,25},... | collective-permute-start | bytes 2488328 | tf_op jit(solution)/shard_map/ppermute | solution.py:31
  53.2 5.2 %collective-permute-start.13 = (f32[360,1152]{1,0:T(8,128)S(1)}, f32[360,1152]{1,0:T(8,128)S(1)}, u32[]{:S(2)}, u32[]{:S(2)}) collective-permute-start(f32[360,1152]{1,0:T(8,128)S(1)} %get-tuple-element.53), channel_id=1, source_target_pairs={{0,1},{1,0},{2,3},{3,2},{4,5},{5,4},{6,7},{7,6},{8,9},{9,8},{10,11... | collective-permute-start | bytes 4976648 | tf_op jit(solution)/shard_map/ppermute | solution.py:31
  55.2 20.6 %collective-permute-start.14 = (bf16[360,1152]{1,0:T(8,128)(2,1)S(1)}, bf16[360,1152]{1,0:T(8,128)(2,1)S(1)}, u32[]{:S(2)}, u32[]{:S(2)}) collective-permute-start(bf16[360,1152]{1,0:T(8,128)(2,1)S(1)} %get-tuple-element.59), channel_id=1, source_target_pairs={{0,64},{1,33},{2,66},{3,35},{4,68},{5,37},{6,70},{7,39},{8,72},{9,... | collective-permute-start | bytes 2488328 | tf_op jit(solution)/shard_map/ppermute | solution.py:31
  56.9 20.3 %collective-permute-start.15 = (bf16[360,1152]{1,0:T(8,128)(2,1)S(1)}, bf16[360,1152]{1,0:T(8,128)(2,1)S(1)}, u32[]{:S(2)}, u32[]{:S(2)}) collective-permute-start(bf16[360,1152]{1,0:T(8,128)(2,1)S(1)} %get-tuple-element.60), channel_id=1, source_target_pairs={{0,66},{1,49},{2,64},{3,51},{4,70},{5,53},{6,68},{7,55},{8,74},{9,... | collective-permute-start | bytes 2488328 | tf_op jit(solution)/shard_map/ppermute | solution.py:31
  59.4 6.5 %collective-permute-start.16 = (bf16[96,1152]{1,0:T(8,128)(2,1)S(1)}, bf16[96,1152]{1,0:T(8,128)(2,1)S(1)}, u32[]{:S(2)}, u32[]{:S(2)}) collective-permute-start(bf16[96,1152]{1,0:T(8,128)(2,1)S(1)} %get-tuple-element.54), channel_id=1, source_target_pairs={{0,4},{1,5},{2,6},{3,7},{4,0},{5,1},{6,2},{7,3},{8,12},{9,13},{10,... | collective-permute-start | bytes 663560 | tf_op jit(solution)/shard_map/ppermute | solution.py:31
  60.7 12.2 %collective-permute-start.17 = (bf16[96,1152]{1,0:T(8,128)(2,1)S(1)}, bf16[96,1152]{1,0:T(8,128)(2,1)S(1)}, u32[]{:S(2)}, u32[]{:S(2)}) collective-permute-start(bf16[96,1152]{1,0:T(8,128)(2,1)S(1)} %get-tuple-element.55), channel_id=1, source_target_pairs={{0,8},{1,9},{2,10},{3,11},{4,12},{5,13},{6,14},{7,15},{8,0},{9,1},... | collective-permute-start | bytes 663560 | tf_op jit(solution)/shard_map/ppermute | solution.py:31
  63.1 12.0 %collective-permute-start.18 = (bf16[96,1152]{1,0:T(8,128)(2,1)S(1)}, bf16[96,1152]{1,0:T(8,128)(2,1)S(1)}, u32[]{:S(2)}, u32[]{:S(2)}) collective-permute-start(bf16[96,1152]{1,0:T(8,128)(2,1)S(1)} %get-tuple-element.56), channel_id=1, source_target_pairs={{0,12},{1,13},{2,14},{3,15},{4,8},{5,9},{6,10},{7,11},{8,4},{9,5},... | collective-permute-start | bytes 663560 | tf_op jit(solution)/shard_map/ppermute | solution.py:31
  79.9 10.9 %collective-permute-start.19 = (bf16[96,1152]{1,0:T(8,128)(2,1)S(1)}, bf16[96,1152]{1,0:T(8,128)(2,1)S(1)}, u32[]{:S(2)}, u32[]{:S(2)}) collective-permute-start(bf16[96,1152]{1,0:T(8,128)(2,1)S(1)} %get-tuple-element.64), channel_id=1, source_target_pairs={{0,16},{1,3},{2,18},{3,1},{4,20},{5,7},{6,22},{7,5},{8,24},{9,11},... | collective-permute-start | bytes 663560 | tf_op jit(solution)/shard_map/ppermute | solution.py:31
  80.4 10.4 %collective-permute-start.20 = (bf16[96,1152]{1,0:T(8,128)(2,1)S(1)}, bf16[96,1152]{1,0:T(8,128)(2,1)S(1)}, u32[]{:S(2)}, u32[]{:S(2)}) collective-permute-start(bf16[96,1152]{1,0:T(8,128)(2,1)S(1)} %get-tuple-element.65), channel_id=1, source_target_pairs={{0,32},{1,65},{2,34},{3,67},{4,36},{5,69},{6,38},{7,71},{8,40},{9,... | collective-permute-start | bytes 663560 | tf_op jit(solution)/shard_map/ppermute | solution.py:31
  82.2 8.6 %collective-permute-start.21 = (bf16[96,1152]{1,0:T(8,128)(2,1)S(1)}, bf16[96,1152]{1,0:T(8,128)(2,1)S(1)}, u32[]{:S(2)}, u32[]{:S(2)}) collective-permute-start(bf16[96,1152]{1,0:T(8,128)(2,1)S(1)} %get-tuple-element.66), channel_id=1, source_target_pairs={{0,48},{1,67},{2,50},{3,65},{4,52},{5,71},{6,54},{7,69},{8,56},{9,... | collective-permute-start | bytes 663560 | tf_op jit(solution)/shard_map/ppermute | solution.py:31
  84.0 6.8 %collective-permute-start.22 = (f32[88,576]{1,0:T(8,128)S(1)}, f32[88,576]{1,0:T(8,128)S(1)}, u32[]{:S(2)}, u32[]{:S(2)}) collective-permute-start(f32[88,576]{1,0:T(8,128)S(1)} %slice.22), channel_id=1, source_target_pairs={{0,2},{1,3},{2,0},{3,1},{4,6},{5,7},{6,4},{7,5},{8,10},{9,11},{10,... | collective-permute-start | bytes 608264 | tf_op jit(solution)/shard_map/ppermute | solution.py:31
  92.6 5.2 %collective-permute-start.23 = (f32[288,352]{1,0:T(8,128)S(1)}, f32[288,352]{1,0:T(8,128)S(1)}, u32[]{:S(2)}, u32[]{:S(2)}) collective-permute-start(f32[288,352]{1,0:T(8,128)S(1)} %get-tuple-element.69), channel_id=1, source_target_pairs={{0,1},{1,0},{2,3},{3,2},{4,5},{5,4},{6,7},{7,6},{8,9},{9,8},{10,11... | collective-permute-start | bytes 1216520 | tf_op jit(solution)/shard_map/ppermute | solution.py:31
  94.6 4.9 %collective-permute-start.26 = (f32[8,128]{1,0:T(8,128)S(1)}, f32[8,128]{1,0:T(8,128)S(1)}, u32[]{:S(2)}, u32[]{:S(2)}) collective-permute-start(f32[8,128]{1,0:T(8,128)S(1)} %get-tuple-element.73), channel_id=1, source_target_pairs={{0,66},{1,49},{2,64},{3,51},{4,70},{5,53},{6,68},{7,55},{8,74},{9,... | collective-permute-start | bytes 12296 | tf_op jit(solution)/shard_map/ppermute | solution.py:31
  96.1 4.0 %collective-permute-start.25 = (f32[8,128]{1,0:T(8,128)S(1)}, f32[8,128]{1,0:T(8,128)S(1)}, u32[]{:S(2)}, u32[]{:S(2)}) collective-permute-start(f32[8,128]{1,0:T(8,128)S(1)} %get-tuple-element.73), channel_id=1, source_target_pairs={{0,64},{1,33},{2,66},{3,35},{4,68},{5,37},{6,70},{7,39},{8,72},{9,... | collective-permute-start | bytes 12296 | tf_op jit(solution)/shard_map/ppermute | solution.py:31
  96.4 3.6 %collective-permute-start.24 = (f32[8,128]{1,0:T(8,128)S(1)}, f32[8,128]{1,0:T(8,128)S(1)}, u32[]{:S(2)}, u32[]{:S(2)}) collective-permute-start(f32[8,128]{1,0:T(8,128)S(1)} %get-tuple-element.73), channel_id=1, source_target_pairs={{0,2},{1,17},{2,0},{3,19},{4,6},{5,21},{6,4},{7,23},{8,10},{9,25},... | collective-permute-start | bytes 12296 | tf_op jit(solution)/shard_map/ppermute | solution.py:31

commit v13 on v11

--- a/solution.py
+++ b/solution.py
@@ -109,8 +109,11 @@
         send_ref[at : at + step, :] = jnp.where(on0, second, first).astype(BF)
 
 
-def join_kernel(rows, info_ref, own_ref, got_ref, texts_ref, images_ref):
+def join_kernel(rows, info_ref, own_ref, got_ref, sums_ref, s1_ref, s2_ref, s3_ref, texts_ref, images_ref, scalars_ref):
     on0, step = info_ref[0] == 0, 2 * rows
+    sums = (sums_ref[0:1, :] + s1_ref[0:1, :]) + (s2_ref[0:1, :] + s3_ref[0:1, :])
+    scalars_ref[0] = jnp.sum(sums[:, 0:1])
+    scalars_ref[1] = jnp.sum(sums[:, 1:2])
     for at, ref in ((0, texts_ref), (step, images_ref)):
         own, got = own_ref[at : at + step, :], got_ref[at : at + step, :]
         ref[...] = jnp.concatenate([jnp.where(on0, own, got), jnp.where(on0, got, own)], axis=0).T
@@ -199,11 +202,18 @@
     out_ref[...] = own_ref[...] + decoded(r1_ref)[0]
 
 
-def text_first_kernel(rows, feats, own_ref, r2_ref, r3_ref, sums_ref, out_ref, *messages):
-    total = own_ref[...] + decoded(r2_ref)[0] + decoded(r3_ref)[0]
-    out_ref[...] = jnp.concatenate([total[0:rows], sums_ref[...]], axis=0)
-    for i, m_ref in enumerate(messages):
-        m_ref[...] = message([total[(i + 1) * rows : (i + 2) * rows]], feats, split3(sums_ref[0:1, :]))
+def text_first_kernel(rows, feats, own_ref, r2_ref, r3_ref, sums_ref, out_ref, m1_ref, m2_ref, m3_ref, total):
+    tops = [r[4 * rows :, :].astype(F32)[7:8] for r in (r2_ref, r3_ref)]
+
+    def add(step, carry):
+        at = pl.ds(pl.multiple_of(step * 32, 32), 32)
+        total[at, :] = own_ref[at, :] + decode(r2_ref[at, :], tops[0]) + decode(r3_ref[at, :], tops[1])
+        return carry
+
+    lax.fori_loop(0, 4 * rows // 32, add, 0)
+    out_ref[...] = jnp.concatenate([total[0:rows, :], sums_ref[...]], axis=0)
+    for i, m_ref in enumerate((m1_ref, m2_ref, m3_ref)):
+        m_ref[...] = message([total[(i + 1) * rows : (i + 2) * rows, :]], feats, split3(sums_ref[0:1, :]))
 
 
 def text_last_kernel(scale_ref, own_ref, r1_ref, r2_ref, r3_ref, out_ref, sums_ref):
@@ -242,17 +252,17 @@
     def bf16(*shape):
         return jax.ShapeDtypeStruct(shape, BF)
 
-    def call(kernel, name, out_shape, *args, scalars=0, scratch=(), mib=20, products=0, brief=False):
+    def call(kernel, name, out_shape, *args, scalars=0, scratch=(), mib=20, products=0, out_specs=None):
         return pl.pallas_call(
             kernel,
             out_shape=out_shape,
             in_specs=[SMEM] * scalars + [VMEM] * (len(args) - scalars),
-            out_specs=[VMEM] * len(out_shape),
+            out_specs=out_specs or [VMEM] * len(out_shape),
             scratch_shapes=scratch,
             compiler_params=grant(mib),
             cost_estimate=pl.CostEstimate(
                 flops=products * 2 * quarter * 2 * quarter * 2 * feats,
-                bytes_accessed=0 if brief else sum(a.size * a.dtype.itemsize for a in (*args, *out_shape)),
+                bytes_accessed=sum(a.size * a.dtype.itemsize for a in (*args, *out_shape)),
                 transcendentals=products * 4 * quarter * quarter,
             ),
             name=name,
@@ -309,6 +319,7 @@
     text, *messages = call(
         functools.partial(text_first_kernel, rows, feats), "text_first",
         [f32(rows + 8, feats)] + [bf16(rows + 8, feats)] * 3, text, got2, got3, sums,
+        scratch=[pltpu.VMEM((quarter, feats), F32)],
     )
     got = [swap(m, y_mask(i), z_mask(i)) for i, m in zip((1, 2, 3), messages)]
     text, sums = call(
@@ -319,12 +330,12 @@
     mine, other = by(on0, whole[:, :width], whole[:, width:])
     sums = after(sums, other)
     other = swap(other, CORE)
-    text_grad, image_grad = call(
-        functools.partial(join_kernel, rows), "join", [f32(width, height)] * 2, info, mine, other, scalars=1
-    )
-    s1, s2, s3 = (after(swap(sums, z_mask(k), y_mask(k)), text_grad, image_grad) for k in (1, 2, 3))
-    sums = (sums + s1) + (s2 + s3)
-    return (image_grad.T, text_grad.T, sums[0, :2])
+    lasts = [swap(sums, z_mask(k), y_mask(k)) for k in (1, 2, 3)]
+    text_grad, image_grad, scalar_grads = call(
+        functools.partial(join_kernel, rows), "join", [f32(width, height), f32(width, height), f32(2)],
+        info, mine, other, sums, *lasts, scalars=1, out_specs=[VMEM, VMEM, SMEM],
+    )
+    return (image_grad.T, text_grad.T, scalar_grads)
 
 
 def solution(mesh):

time: 98.6 us -> 99.5 us (level)
  waiting for transfers between devices: 30.3 us -> 32 us
    ppermute x27, waiting for transfers between devices: 30.3 us -> 32 us  [swap(): lax.ppermute(array, AXES, [(i, i ^ (mask1 if i & 1 else mask0)) for i in...]
  transfers between devices with their start and end apart: 27 -> 27, of which waited for: 17 -> 19; matrix products, arithmetic and copies ran while one was open for 1% -> 1% of each run, Pallas kernels for 21% -> 19%
where the time goes in v13:
time: 99.5 us; the launch traced here: 99.3 us
  starting transfers between devices  37.2 us (37%)
  waiting for transfers between devices  32 us (32%)
  Pallas kernels  24.1 us (24%)
  local copies, waits for them, and re-layouts  2.41 us (2%)
  between operations  2.28 us (2%)
  other arithmetic  1.34 us (1%)
    ppermute x27, starting transfers between devices, swap(): lax.ppermute(array, AXES, [(i, i ^ (mask1 if i & 1 else mask0)) for i in...  37.2 us
    ppermute x27, waiting for transfers between devices, swap(): lax.ppermute(array, AXES, [(i, i ^ (mask1 if i & 1 else mask0)) for i in...  32 us
    pallas_call x10, Pallas kernels, call(): pl.pallas_call(kernel, out_shape=out_shape, in_specs=[SMEM] * scalars + [...  24.1 us
  transfers between devices with their start and end apart: 27, of which 19 were waited for; matrix products, arithmetic and copies ran while one was open for 1% of the time, Pallas kernels for 19%

profile of v13, /device:TPU:1, one launch (start us, length us, event | category | flops | bytes accessed | tf_op | source)
XLA Modules:
  0.0 99.3 jit_solution(5895132874527741067)
XLA Ops:
  0.7 0.9 copy-done
  1.7 0.9 copy-done.1
  2.6 0.8 split.1
  3.4 1.5 %collective-permute-start = (bf16[352,288]{1,0:T(8,128)(2,1)S(1)}, bf16[352,288]{1,0:T(8,128)(2,1)S(1)}, u32[]{:S(2)}, u32[]{:S(2)}) collective-permute-start(bf16[352,288]{1,0:T(8,128)(2,1)S(1)} %get-tuple-element.39), channel_id=1, source_target_pairs={{0,1},{1,0},{2,3},{3,2},{4,5},{5,4},{6,7},{7,6},{8,9},{9,8},{10,11... | collective-permute-start | bytes 608264 | tf_op jit(solution)/shard_map/ppermute | solution.py:31
  4.9 1.2 %collective-permute-done = bf16[352,288]{1,0:T(8,128)(2,1)S(1)} collective-permute-done((bf16[352,288]{1,0:T(8,128)(2,1)S(1)}, bf16[352,288]{1,0:T(8,128)(2,1)S(1)}, u32[]{:S(2)}, u32[]{:S(2)}) %collective-permute-start) | collective-permute-done | bytes 202784 | tf_op jit(solution)/shard_map/ppermute | solution.py:31
  6.3 1.8 %collective-permute-start.6 = (bf16[88,576]{1,0:T(8,128)(2,1)S(1)}, bf16[88,576]{1,0:T(8,128)(2,1)S(1)}, u32[]{:S(2)}, u32[]{:S(2)}) collective-permute-start(bf16[88,576]{1,0:T(8,128)(2,1)S(1)} %get-tuple-element.79), channel_id=1, source_target_pairs={{0,2},{1,3},{2,0},{3,1},{4,6},{5,7},{6,4},{7,5},{8,10},{9,11},{10,... | collective-permute-start | bytes 304136 | tf_op jit(solution)/shard_map/ppermute | solution.py:31
  8.4 3.4 %collective-permute-start.2 = (bf16[88,1152]{1,0:T(8,128)(2,1)S(1)}, bf16[88,1152]{1,0:T(8,128)(2,1)S(1)}, u32[]{:S(2)}, u32[]{:S(2)}) collective-permute-start(bf16[88,1152]{1,0:T(8,128)(2,1)S(1)} %pad_maximum_fusion.3), channel_id=1, source_target_pairs={{0,32},{1,65},{2,34},{3,67},{4,36},{5,69},{6,38},{7,71},{8,40},{9,... | collective-permute-start | bytes 608264 | tf_op jit(solution)/shard_map/ppermute | solution.py:31
  12.2 2.6 %collective-permute-start.9 = (bf16[88,1152]{1,0:T(8,128)(2,1)S(1)}, bf16[88,1152]{1,0:T(8,128)(2,1)S(1)}, u32[]{:S(2)}, u32[]{:S(2)}) collective-permute-start(bf16[88,1152]{1,0:T(8,128)(2,1)S(1)} %pad_maximum_fusion.4), channel_id=1, source_target_pairs={{0,12},{1,13},{2,14},{3,15},{4,8},{5,9},{6,10},{7,11},{8,4},{9,5},... | collective-permute-start | bytes 608264 | tf_op jit(solution)/shard_map/ppermute | solution.py:31
  15.3 1.8 %collective-permute-done.2 = bf16[88,1152]{1,0:T(8,128)(2,1)S(1)} collective-permute-done((bf16[88,1152]{1,0:T(8,128)(2,1)S(1)}, bf16[88,1152]{1,0:T(8,128)(2,1)S(1)}, u32[]{:S(2)}, u32[]{:S(2)}) %collective-permute-start.2) | collective-permute-done | bytes 202784 | tf_op jit(solution)/shard_map/ppermute | solution.py:31
  17.1 1.2 %collective-permute-start.7 = (bf16[88,1152]{1,0:T(8,128)(2,1)S(1)}, bf16[88,1152]{1,0:T(8,128)(2,1)S(1)}, u32[]{:S(2)}, u32[]{:S(2)}) collective-permute-start(bf16[88,1152]{1,0:T(8,128)(2,1)S(1)} %pad_maximum_fusion.4), channel_id=1, source_target_pairs={{0,4},{1,5},{2,6},{3,7},{4,0},{5,1},{6,2},{7,3},{8,12},{9,13},{10,... | collective-permute-start | bytes 608264 | tf_op jit(solution)/shard_map/ppermute | solution.py:31
  18.3 1.0 %collective-permute-done.3 = bf16[88,1152]{1,0:T(8,128)(2,1)S(1)} collective-permute-done((bf16[88,1152]{1,0:T(8,128)(2,1)S(1)}, bf16[88,1152]{1,0:T(8,128)(2,1)S(1)}, u32[]{:S(2)}, u32[]{:S(2)}) %collective-permute-start.3) | collective-permute-done | bytes 202784 | tf_op jit(solution)/shard_map/ppermute | solution.py:31
  19.5 2.8 %collective-permute-start.5 = (bf16[4,88,1152]{2,1,0:T(8,128)(2,1)S(1)}, bf16[4,88,1152]{2,1,0:T(8,128)(2,1)S(1)}, u32[]{:S(2)}, u32[]{:S(2)}) collective-permute-start(bf16[4,88,1152]{2,1,0:T(8,128)(2,1)S(1)} %pad_maximum_fusion.1.ta_ref), channel_id=1, source_target_pairs={{0,66},{1,49},{2,64},{3,51},{4,70},{5,53},{6,68},{7,55},{8,74},{9,... | collective-permute-start | bytes 2433032 | tf_op jit(solution)/shard_map/ppermute | solution.py:31
  22.3 1.1 %collective-permute-done.9 = bf16[88,1152]{1,0:T(8,128)(2,1)S(1)} collective-permute-done((bf16[88,1152]{1,0:T(8,128)(2,1)S(1)}, bf16[88,1152]{1,0:T(8,128)(2,1)S(1)}, u32[]{:S(2)}, u32[]{:S(2)}) %collective-permute-start.9) | collective-permute-done | bytes 202784 | tf_op jit(solution)/shard_map/ppermute | solution.py:31
  23.3 0.8 collective-permute-done.7
  24.2 1.9 %collective-permute-start.10 = (bf16[352,1152]{1,0:T(8,128)(2,1)S(1)}, bf16[352,1152]{1,0:T(8,128)(2,1)S(1)}, u32[]{:S(2)}, u32[]{:S(2)}) collective-permute-start(bf16[352,1152]{1,0:T(8,128)(2,1)S(1)} %pad_maximum_fusion.2.im0_ref), channel_id=1, source_target_pairs={{0,1},{1,0},{2,3},{3,2},{4,5},{5,4},{6,7},{7,6},{8,9},{9,8},{10,11... | collective-permute-start | bytes 2433032 | tf_op jit(solution)/shard_map/ppermute | solution.py:31
  27.4 3.0 %collective-permute-start.11 = (bf16[4,88,1152]{2,1,0:T(8,128)(2,1)S(1)}, bf16[4,88,1152]{2,1,0:T(8,128)(2,1)S(1)}, u32[]{:S(2)}, u32[]{:S(2)}) collective-permute-start(bf16[4,88,1152]{2,1,0:T(8,128)(2,1)S(1)} %pad_maximum_fusion.1.ta_ref), channel_id=1, source_target_pairs={{0,64},{1,33},{2,66},{3,35},{4,68},{5,37},{6,70},{7,39},{8,72},{9,... | collective-permute-start | bytes 2433032 | tf_op jit(solution)/shard_map/ppermute | solution.py:31
  30.4 1.8 %collective-permute-done.5.tb_ref = bf16[4,88,1152]{2,1,0:T(8,128)(2,1)S(1)} collective-permute-done((bf16[4,88,1152]{2,1,0:T(8,128)(2,1)S(1)}, bf16[4,88,1152]{2,1,0:T(8,128)(2,1)S(1)}, u32[]{:S(2)}, u32[]{:S(2)}) %collective-permute-start.5) | collective-permute-done | bytes 811040 | tf_op jit(solution)/shard_map/ppermute | solution.py:31
  32.2 1.5 %collective-permute-done.4.tb_ref = bf16[4,88,1152]{2,1,0:T(8,128)(2,1)S(1)} collective-permute-done((bf16[4,88,1152]{2,1,0:T(8,128)(2,1)S(1)}, bf16[4,88,1152]{2,1,0:T(8,128)(2,1)S(1)}, u32[]{:S(2)}, u32[]{:S(2)}) %collective-permute-start.4) | collective-permute-done | bytes 811040 | tf_op jit(solution)/shard_map/ppermute | solution.py:31
  33.7 5.9 %tile_near.1 = (f32[352,1152]{1,0:T(8,128)S(1)}, bf16[360,1152]{1,0:T(8,128)(2,1)S(1)}, bf16[704,1152]{1,0:T(8,128)(2,1)S(1)}, bf16[704,704]{1,0:T(8,128)(2,1)S(1)}, f32[8,128]{1,0:T(8,128)S(1)}) custom-call(s32[2]{0:T(128)S(1)} %pad_add_fusion.info_ref, f32[2]{0:T(128)S(1)} %pad_maximum_fusion.6.scale_ref, ...), custom_call_target="tpu_custom_call" | custom-call | flops 2283798528 | bytes 8312848 | tf_op jit(solution)/shard_map/tile_near/pallas_call | solution.py:256
  39.8 1.6 %image_near.1.before_ref = f32[704,1152]{1,0:T(8,128)S(1)} custom-call(bf16[704,1152]{1,0:T(8,128)(2,1)S(1)} %get-tuple-element.43.t_rel, bf16[704,704]{1,0:T(8,128)(2,1)S(1)} %get-tuple-element.44.coeff_low), custom_call_target="tpu_custom_call" | custom-call | flops 1141899264 | bytes 5857280 | tf_op jit(solution)/shard_map/image_near/pallas_call | solution.py:256
  41.4 0.7 collective-permute-done.11.ta_ref
  42.2 8.4 %tile_far.1 = (bf16[360,1152]{1,0:T(8,128)(2,1)S(1)}, bf16[360,1152]{1,0:T(8,128)(2,1)S(1)}, f32[360,1152]{1,0:T(8,128)S(1)}, f32[360,1152]{1,0:T(8,128)S(1)}) custom-call(s32[2]{0:T(128)S(1)} %pad_add_fusion.info_ref, f32[2]{0:T(128)S(1)} %pad_maximum_fusion.6.scale_ref, bf16[4,88,1152]{2,1,0:T(8,128)(2,1)S(1)} %collective-permute-done.11.ta_ref, ...), custom_call_target="tpu_custom_call" | custom-call | flops 3425697792 | bytes 11468816 | tf_op jit(solution)/shard_map/tile_far/pallas_call | solution.py:256
  50.6 0.8 collective-permute-done.12.r1_ref
  51.4 2.1 %collective-permute-start.13 = (f32[360,1152]{1,0:T(8,128)S(1)}, f32[360,1152]{1,0:T(8,128)S(1)}, u32[]{:S(2)}, u32[]{:S(2)}) collective-permute-start(f32[360,1152]{1,0:T(8,128)S(1)} %get-tuple-element.51), channel_id=1, source_target_pairs={{0,1},{1,0},{2,3},{3,2},{4,5},{5,4},{6,7},{7,6},{8,9},{9,8},{10,11... | collective-permute-start | bytes 4976648 | tf_op jit(solution)/shard_map/ppermute | solution.py:31
  53.5 1.6 %collective-permute-start.14 = (bf16[360,1152]{1,0:T(8,128)(2,1)S(1)}, bf16[360,1152]{1,0:T(8,128)(2,1)S(1)}, u32[]{:S(2)}, u32[]{:S(2)}) collective-permute-start(bf16[360,1152]{1,0:T(8,128)(2,1)S(1)} %get-tuple-element.57), channel_id=1, source_target_pairs={{0,64},{1,33},{2,66},{3,35},{4,68},{5,37},{6,70},{7,39},{8,72},{9,... | collective-permute-start | bytes 2488328 | tf_op jit(solution)/shard_map/ppermute | solution.py:31
  55.1 0.8 collective-permute-start.15
  55.9 0.7 collective-permute-done.13.other_ref
  56.6 1.0 image_first.1
  57.6 1.3 %collective-permute-start.16 = (bf16[96,1152]{1,0:T(8,128)(2,1)S(1)}, bf16[96,1152]{1,0:T(8,128)(2,1)S(1)}, u32[]{:S(2)}, u32[]{:S(2)}) collective-permute-start(bf16[96,1152]{1,0:T(8,128)(2,1)S(1)} %get-tuple-element.52), channel_id=1, source_target_pairs={{0,4},{1,5},{2,6},{3,7},{4,0},{5,1},{6,2},{7,3},{8,12},{9,13},{10,... | collective-permute-start | bytes 663560 | tf_op jit(solution)/shard_map/ppermute | solution.py:31
  58.9 2.4 %collective-permute-start.17 = (bf16[96,1152]{1,0:T(8,128)(2,1)S(1)}, bf16[96,1152]{1,0:T(8,128)(2,1)S(1)}, u32[]{:S(2)}, u32[]{:S(2)}) collective-permute-start(bf16[96,1152]{1,0:T(8,128)(2,1)S(1)} %get-tuple-element.53), channel_id=1, source_target_pairs={{0,8},{1,9},{2,10},{3,11},{4,12},{5,13},{6,14},{7,15},{8,0},{9,1},... | collective-permute-start | bytes 663560 | tf_op jit(solution)/shard_map/ppermute | solution.py:31
  61.6 0.8 text_near.1.own_ref
  62.3 1.8 %collective-permute-done.16.r1_ref = bf16[96,1152]{1,0:T(8,128)(2,1)S(1)} collective-permute-done((bf16[96,1152]{1,0:T(8,128)(2,1)S(1)}, bf16[96,1152]{1,0:T(8,128)(2,1)S(1)}, u32[]{:S(2)}, u32[]{:S(2)}) %collective-permute-start.16) | collective-permute-done | bytes 221216 | tf_op jit(solution)/shard_map/ppermute | solution.py:31
  64.1 7.0 %collective-permute-done.17.r2_ref = bf16[96,1152]{1,0:T(8,128)(2,1)S(1)} collective-permute-done((bf16[96,1152]{1,0:T(8,128)(2,1)S(1)}, bf16[96,1152]{1,0:T(8,128)(2,1)S(1)}, u32[]{:S(2)}, u32[]{:S(2)}) %collective-permute-start.17) | collective-permute-done | bytes 221216 | tf_op jit(solution)/shard_map/ppermute | solution.py:31
  71.1 2.2 %collective-permute-done.18.r3_ref = bf16[96,1152]{1,0:T(8,128)(2,1)S(1)} collective-permute-done((bf16[96,1152]{1,0:T(8,128)(2,1)S(1)}, bf16[96,1152]{1,0:T(8,128)(2,1)S(1)}, u32[]{:S(2)}, u32[]{:S(2)}) %collective-permute-start.18) | collective-permute-done | bytes 221216 | tf_op jit(solution)/shard_map/ppermute | solution.py:31
  73.4 0.6 image_last.1
  74.0 1.4 %collective-permute-done.15.r3_ref = bf16[360,1152]{1,0:T(8,128)(2,1)S(1)} collective-permute-done((bf16[360,1152]{1,0:T(8,128)(2,1)S(1)}, bf16[360,1152]{1,0:T(8,128)(2,1)S(1)}, u32[]{:S(2)}, u32[]{:S(2)}) %collective-permute-start.15) | collective-permute-done | bytes 829472 | tf_op jit(solution)/shard_map/ppermute | solution.py:31
  75.5 2.6 %text_first.1 = (f32[96,1152]{1,0:T(8,128)S(1)}, bf16[96,1152]{1,0:T(8,128)(2,1)S(1)}, bf16[96,1152]{1,0:T(8,128)(2,1)S(1)}, bf16[96,1152]{1,0:T(8,128)(2,1)S(1)}) custom-call(f32[352,1152]{1,0:T(8,128)S(1)} %text_near.1.own_ref, bf16[360,1152]{1,0:T(8,128)(2,1)S(1)} %collective-permute-done.14.r2_ref, bf16[360,1152]{1,0:T(8,128)(2,1)S(1)} %collective-permute-done.15.r3_ref, ...), custom_call_target="tpu_custom_call" | custom-call | bytes 4423680 | tf_op jit(solution)/shard_map/text_first/pallas_call | solution.py:256
  78.6 1.8 %collective-permute-start.20 = (bf16[96,1152]{1,0:T(8,128)(2,1)S(1)}, bf16[96,1152]{1,0:T(8,128)(2,1)S(1)}, u32[]{:S(2)}, u32[]{:S(2)}) collective-permute-start(bf16[96,1152]{1,0:T(8,128)(2,1)S(1)} %get-tuple-element.63), channel_id=1, source_target_pairs={{0,32},{1,65},{2,34},{3,67},{4,36},{5,69},{6,38},{7,71},{8,40},{9,... | collective-permute-start | bytes 663560 | tf_op jit(solution)/shard_map/ppermute | solution.py:31
  80.4 1.6 %collective-permute-start.21 = (bf16[96,1152]{1,0:T(8,128)(2,1)S(1)}, bf16[96,1152]{1,0:T(8,128)(2,1)S(1)}, u32[]{:S(2)}, u32[]{:S(2)}) collective-permute-start(bf16[96,1152]{1,0:T(8,128)(2,1)S(1)} %get-tuple-element.64), channel_id=1, source_target_pairs={{0,48},{1,67},{2,50},{3,65},{4,52},{5,71},{6,54},{7,69},{8,56},{9,... | collective-permute-start | bytes 663560 | tf_op jit(solution)/shard_map/ppermute | solution.py:31
  82.3 1.0 %collective-permute-done.19.r1_ref = bf16[96,1152]{1,0:T(8,128)(2,1)S(1)} collective-permute-done((bf16[96,1152]{1,0:T(8,128)(2,1)S(1)}, bf16[96,1152]{1,0:T(8,128)(2,1)S(1)}, u32[]{:S(2)}, u32[]{:S(2)}) %collective-permute-start.19) | collective-permute-done | bytes 221216 | tf_op jit(solution)/shard_map/ppermute | solution.py:31
  83.3 3.2 %collective-permute-done.20.r2_ref = bf16[96,1152]{1,0:T(8,128)(2,1)S(1)} collective-permute-done((bf16[96,1152]{1,0:T(8,128)(2,1)S(1)}, bf16[96,1152]{1,0:T(8,128)(2,1)S(1)}, u32[]{:S(2)}, u32[]{:S(2)}) %collective-permute-start.20) | collective-permute-done | bytes 221216 | tf_op jit(solution)/shard_map/ppermute | solution.py:31
  86.4 2.3 %collective-permute-done.21.r3_ref = bf16[96,1152]{1,0:T(8,128)(2,1)S(1)} collective-permute-done((bf16[96,1152]{1,0:T(8,128)(2,1)S(1)}, bf16[96,1152]{1,0:T(8,128)(2,1)S(1)}, u32[]{:S(2)}, u32[]{:S(2)}) %collective-permute-start.21) | collective-permute-done | bytes 221216 | tf_op jit(solution)/shard_map/ppermute | solution.py:31
  88.8 0.6 text_last.1
  90.0 2.2 %collective-permute-start.23 = (f32[352,288]{0,1:T(8,128)S(1)}, f32[352,288]{0,1:T(8,128)S(1)}, u32[]{:S(2)}, u32[]{:S(2)}) collective-permute-start(f32[352,288]{0,1:T(8,128)S(1)} %copy.7), channel_id=1, source_target_pairs={{0,1},{1,0},{2,3},{3,2},{4,5},{5,4},{6,7},{7,6},{8,9},{9,8},{10,11... | collective-permute-start | bytes 1216520 | tf_op jit(solution)/shard_map/ppermute | solution.py:31
  92.2 1.2 %collective-permute-start.26 = (f32[8,128]{1,0:T(8,128)S(1)}, f32[8,128]{1,0:T(8,128)S(1)}, u32[]{:S(2)}, u32[]{:S(2)}) collective-permute-start(f32[8,128]{1,0:T(8,128)S(1)} %get-tuple-element.69.sums_ref), channel_id=1, source_target_pairs={{0,66},{1,49},{2,64},{3,51},{4,70},{5,53},{6,68},{7,55},{8,74},{9,... | collective-permute-start | bytes 12296 | tf_op jit(solution)/shard_map/ppermute | solution.py:31
  93.5 2.0 %collective-permute-start.24 = (f32[8,128]{1,0:T(8,128)S(1)}, f32[8,128]{1,0:T(8,128)S(1)}, u32[]{:S(2)}, u32[]{:S(2)}) collective-permute-start(f32[8,128]{1,0:T(8,128)S(1)} %get-tuple-element.69.sums_ref), channel_id=1, source_target_pairs={{0,2},{1,17},{2,0},{3,19},{4,6},{5,21},{6,4},{7,23},{8,10},{9,25},... | collective-permute-start | bytes 12296 | tf_op jit(solution)/shard_map/ppermute | solution.py:31
  95.9 1.5 %collective-permute-done.25.s2_ref = f32[8,128]{1,0:T(8,128)S(1)} collective-permute-done((f32[8,128]{1,0:T(8,128)S(1)}, f32[8,128]{1,0:T(8,128)S(1)}, u32[]{:S(2)}, u32[]{:S(2)}) %collective-permute-start.25) | collective-permute-done | bytes 4128 | tf_op jit(solution)/shard_map/ppermute | solution.py:31
  97.4 1.7 %join.1 = (f32[288,352]{1,0:T(8,128)}, f32[288,352]{1,0:T(8,128)}, f32[2]{0:T(128)}) custom-call(s32[2]{0:T(128)S(1)} %pad_add_fusion.info_ref, f32[352,288]{1,0:T(8,128)S(1)} %get-tuple-element.76.own_ref, f32[352,288]{1,0:T(8,128)S(1)} %copy.8.got_ref, f32[8,128]{1,0:T(8,128)S(1)} %get-tuple-element.69.sums_ref, ...), custom_call_target="tpu_custom_call" | custom-call | bytes 1638416 | tf_op jit(solution)/shard_map/join/pallas_call | solution.py:256
  (36 shorter events, 4.1 us)
Async XLA Ops:
  0.7 0.9 copy-start
  1.6 0.9 copy-start.1
  3.4 2.7 %collective-permute-start = (bf16[352,288]{1,0:T(8,128)(2,1)S(1)}, bf16[352,288]{1,0:T(8,128)(2,1)S(1)}, u32[]{:S(2)}, u32[]{:S(2)}) collective-permute-start(bf16[352,288]{1,0:T(8,128)(2,1)S(1)} %get-tuple-element.39), channel_id=1, source_target_pairs={{0,1},{1,0},{2,3},{3,2},{4,5},{5,4},{6,7},{7,6},{8,9},{9,8},{10,11... | collective-permute-start | bytes 608264 | tf_op jit(solution)/shard_map/ppermute | solution.py:31
  6.3 5.8 %collective-permute-start.6 = (bf16[88,576]{1,0:T(8,128)(2,1)S(1)}, bf16[88,576]{1,0:T(8,128)(2,1)S(1)}, u32[]{:S(2)}, u32[]{:S(2)}) collective-permute-start(bf16[88,576]{1,0:T(8,128)(2,1)S(1)} %get-tuple-element.79), channel_id=1, source_target_pairs={{0,2},{1,3},{2,0},{3,1},{4,6},{5,7},{6,4},{7,5},{8,10},{9,11},{10,... | collective-permute-start | bytes 304136 | tf_op jit(solution)/shard_map/ppermute | solution.py:31
  8.4 8.7 %collective-permute-start.2 = (bf16[88,1152]{1,0:T(8,128)(2,1)S(1)}, bf16[88,1152]{1,0:T(8,128)(2,1)S(1)}, u32[]{:S(2)}, u32[]{:S(2)}) collective-permute-start(bf16[88,1152]{1,0:T(8,128)(2,1)S(1)} %pad_maximum_fusion.3), channel_id=1, source_target_pairs={{0,32},{1,65},{2,34},{3,67},{4,36},{5,69},{6,38},{7,71},{8,40},{9,... | collective-permute-start | bytes 608264 | tf_op jit(solution)/shard_map/ppermute | solution.py:31
  11.7 6.6 %collective-permute-start.1 = (bf16[88,1152]{1,0:T(8,128)(2,1)S(1)}, bf16[88,1152]{1,0:T(8,128)(2,1)S(1)}, u32[]{:S(2)}, u32[]{:S(2)}) collective-permute-start(bf16[88,1152]{1,0:T(8,128)(2,1)S(1)} %pad_maximum_fusion.3), channel_id=1, source_target_pairs={{0,16},{1,3},{2,18},{3,1},{4,20},{5,7},{6,22},{7,5},{8,24},{9,11},... | collective-permute-start | bytes 608264 | tf_op jit(solution)/shard_map/ppermute | solution.py:31
  11.7 7.6 %collective-permute-start.3 = (bf16[88,1152]{1,0:T(8,128)(2,1)S(1)}, bf16[88,1152]{1,0:T(8,128)(2,1)S(1)}, u32[]{:S(2)}, u32[]{:S(2)}) collective-permute-start(bf16[88,1152]{1,0:T(8,128)(2,1)S(1)} %pad_maximum_fusion.3), channel_id=1, source_target_pairs={{0,48},{1,67},{2,50},{3,65},{4,52},{5,71},{6,54},{7,69},{8,56},{9,... | collective-permute-start | bytes 608264 | tf_op jit(solution)/shard_map/ppermute | solution.py:31
  12.2 11.1 %collective-permute-start.9 = (bf16[88,1152]{1,0:T(8,128)(2,1)S(1)}, bf16[88,1152]{1,0:T(8,128)(2,1)S(1)}, u32[]{:S(2)}, u32[]{:S(2)}) collective-permute-start(bf16[88,1152]{1,0:T(8,128)(2,1)S(1)} %pad_maximum_fusion.4), channel_id=1, source_target_pairs={{0,12},{1,13},{2,14},{3,15},{4,8},{5,9},{6,10},{7,11},{8,4},{9,5},... | collective-permute-start | bytes 608264 | tf_op jit(solution)/shard_map/ppermute | solution.py:31
  14.8 8.5 %collective-permute-start.8 = (bf16[88,1152]{1,0:T(8,128)(2,1)S(1)}, bf16[88,1152]{1,0:T(8,128)(2,1)S(1)}, u32[]{:S(2)}, u32[]{:S(2)}) collective-permute-start(bf16[88,1152]{1,0:T(8,128)(2,1)S(1)} %pad_maximum_fusion.4), channel_id=1, source_target_pairs={{0,8},{1,9},{2,10},{3,11},{4,12},{5,13},{6,14},{7,15},{8,0},{9,1},... | collective-permute-start | bytes 608264 | tf_op jit(solution)/shard_map/ppermute | solution.py:31
  17.1 7.0 %collective-permute-start.7 = (bf16[88,1152]{1,0:T(8,128)(2,1)S(1)}, bf16[88,1152]{1,0:T(8,128)(2,1)S(1)}, u32[]{:S(2)}, u32[]{:S(2)}) collective-permute-start(bf16[88,1152]{1,0:T(8,128)(2,1)S(1)} %pad_maximum_fusion.4), channel_id=1, source_target_pairs={{0,4},{1,5},{2,6},{3,7},{4,0},{5,1},{6,2},{7,3},{8,12},{9,13},{10,... | collective-permute-start | bytes 608264 | tf_op jit(solution)/shard_map/ppermute | solution.py:31
  19.5 12.8 %collective-permute-start.5 = (bf16[4,88,1152]{2,1,0:T(8,128)(2,1)S(1)}, bf16[4,88,1152]{2,1,0:T(8,128)(2,1)S(1)}, u32[]{:S(2)}, u32[]{:S(2)}) collective-permute-start(bf16[4,88,1152]{2,1,0:T(8,128)(2,1)S(1)} %pad_maximum_fusion.1.ta_ref), channel_id=1, source_target_pairs={{0,66},{1,49},{2,64},{3,51},{4,70},{5,53},{6,68},{7,55},{8,74},{9,... | collective-permute-start | bytes 2433032 | tf_op jit(solution)/shard_map/ppermute | solution.py:31
  22.3 11.4 %collective-permute-start.4 = (bf16[4,88,1152]{2,1,0:T(8,128)(2,1)S(1)}, bf16[4,88,1152]{2,1,0:T(8,128)(2,1)S(1)}, u32[]{:S(2)}, u32[]{:S(2)}) collective-permute-start(bf16[4,88,1152]{2,1,0:T(8,128)(2,1)S(1)} %pad_maximum_fusion.1.ta_ref), channel_id=1, source_target_pairs={{0,2},{1,17},{2,0},{3,19},{4,6},{5,21},{6,4},{7,23},{8,10},{9,25},... | collective-permute-start | bytes 2433032 | tf_op jit(solution)/shard_map/ppermute | solution.py:31
  24.2 9.5 %collective-permute-start.10 = (bf16[352,1152]{1,0:T(8,128)(2,1)S(1)}, bf16[352,1152]{1,0:T(8,128)(2,1)S(1)}, u32[]{:S(2)}, u32[]{:S(2)}) collective-permute-start(bf16[352,1152]{1,0:T(8,128)(2,1)S(1)} %pad_maximum_fusion.2.im0_ref), channel_id=1, source_target_pairs={{0,1},{1,0},{2,3},{3,2},{4,5},{5,4},{6,7},{7,6},{8,9},{9,8},{10,11... | collective-permute-start | bytes 2433032 | tf_op jit(solution)/shard_map/ppermute | solution.py:31
  27.4 14.8 %collective-permute-start.11 = (bf16[4,88,1152]{2,1,0:T(8,128)(2,1)S(1)}, bf16[4,88,1152]{2,1,0:T(8,128)(2,1)S(1)}, u32[]{:S(2)}, u32[]{:S(2)}) collective-permute-start(bf16[4,88,1152]{2,1,0:T(8,128)(2,1)S(1)} %pad_maximum_fusion.1.ta_ref), channel_id=1, source_target_pairs={{0,64},{1,33},{2,66},{3,35},{4,68},{5,37},{6,70},{7,39},{8,72},{9,... | collective-permute-start | bytes 2433032 | tf_op jit(solution)/shard_map/ppermute | solution.py:31
  39.5 11.9 %collective-permute-start.12 = (bf16[360,1152]{1,0:T(8,128)(2,1)S(1)}, bf16[360,1152]{1,0:T(8,128)(2,1)S(1)}, u32[]{:S(2)}, u32[]{:S(2)}) collective-permute-start(bf16[360,1152]{1,0:T(8,128)(2,1)S(1)} %get-tuple-element.50), channel_id=1, source_target_pairs={{0,2},{1,17},{2,0},{3,19},{4,6},{5,21},{6,4},{7,23},{8,10},{9,25},... | collective-permute-start | bytes 2488328 | tf_op jit(solution)/shard_map/ppermute | solution.py:31
  51.4 5.2 %collective-permute-start.13 = (f32[360,1152]{1,0:T(8,128)S(1)}, f32[360,1152]{1,0:T(8,128)S(1)}, u32[]{:S(2)}, u32[]{:S(2)}) collective-permute-start(f32[360,1152]{1,0:T(8,128)S(1)} %get-tuple-element.51), channel_id=1, source_target_pairs={{0,1},{1,0},{2,3},{3,2},{4,5},{5,4},{6,7},{7,6},{8,9},{9,8},{10,11... | collective-permute-start | bytes 4976648 | tf_op jit(solution)/shard_map/ppermute | solution.py:31
  53.5 20.5 %collective-permute-start.14 = (bf16[360,1152]{1,0:T(8,128)(2,1)S(1)}, bf16[360,1152]{1,0:T(8,128)(2,1)S(1)}, u32[]{:S(2)}, u32[]{:S(2)}) collective-permute-start(bf16[360,1152]{1,0:T(8,128)(2,1)S(1)} %get-tuple-element.57), channel_id=1, source_target_pairs={{0,64},{1,33},{2,66},{3,35},{4,68},{5,37},{6,70},{7,39},{8,72},{9,... | collective-permute-start | bytes 2488328 | tf_op jit(solution)/shard_map/ppermute | solution.py:31
  55.1 20.3 %collective-permute-start.15 = (bf16[360,1152]{1,0:T(8,128)(2,1)S(1)}, bf16[360,1152]{1,0:T(8,128)(2,1)S(1)}, u32[]{:S(2)}, u32[]{:S(2)}) collective-permute-start(bf16[360,1152]{1,0:T(8,128)(2,1)S(1)} %get-tuple-element.58), channel_id=1, source_target_pairs={{0,66},{1,49},{2,64},{3,51},{4,70},{5,53},{6,68},{7,55},{8,74},{9,... | collective-permute-start | bytes 2488328 | tf_op jit(solution)/shard_map/ppermute | solution.py:31
  57.6 6.5 %collective-permute-start.16 = (bf16[96,1152]{1,0:T(8,128)(2,1)S(1)}, bf16[96,1152]{1,0:T(8,128)(2,1)S(1)}, u32[]{:S(2)}, u32[]{:S(2)}) collective-permute-start(bf16[96,1152]{1,0:T(8,128)(2,1)S(1)} %get-tuple-element.52), channel_id=1, source_target_pairs={{0,4},{1,5},{2,6},{3,7},{4,0},{5,1},{6,2},{7,3},{8,12},{9,13},{10,... | collective-permute-start | bytes 663560 | tf_op jit(solution)/shard_map/ppermute | solution.py:31
  58.9 12.2 %collective-permute-start.17 = (bf16[96,1152]{1,0:T(8,128)(2,1)S(1)}, bf16[96,1152]{1,0:T(8,128)(2,1)S(1)}, u32[]{:S(2)}, u32[]{:S(2)}) collective-permute-start(bf16[96,1152]{1,0:T(8,128)(2,1)S(1)} %get-tuple-element.53), channel_id=1, source_target_pairs={{0,8},{1,9},{2,10},{3,11},{4,12},{5,13},{6,14},{7,15},{8,0},{9,1},... | collective-permute-start | bytes 663560 | tf_op jit(solution)/shard_map/ppermute | solution.py:31
  61.4 12.0 %collective-permute-start.18 = (bf16[96,1152]{1,0:T(8,128)(2,1)S(1)}, bf16[96,1152]{1,0:T(8,128)(2,1)S(1)}, u32[]{:S(2)}, u32[]{:S(2)}) collective-permute-start(bf16[96,1152]{1,0:T(8,128)(2,1)S(1)} %get-tuple-element.54), channel_id=1, source_target_pairs={{0,12},{1,13},{2,14},{3,15},{4,8},{5,9},{6,10},{7,11},{8,4},{9,5},... | collective-permute-start | bytes 663560 | tf_op jit(solution)/shard_map/ppermute | solution.py:31
  78.1 5.2 %collective-permute-start.19 = (bf16[96,1152]{1,0:T(8,128)(2,1)S(1)}, bf16[96,1152]{1,0:T(8,128)(2,1)S(1)}, u32[]{:S(2)}, u32[]{:S(2)}) collective-permute-start(bf16[96,1152]{1,0:T(8,128)(2,1)S(1)} %get-tuple-element.62), channel_id=1, source_target_pairs={{0,16},{1,3},{2,18},{3,1},{4,20},{5,7},{6,22},{7,5},{8,24},{9,11},... | collective-permute-start | bytes 663560 | tf_op jit(solution)/shard_map/ppermute | solution.py:31
  78.6 7.8 %collective-permute-start.20 = (bf16[96,1152]{1,0:T(8,128)(2,1)S(1)}, bf16[96,1152]{1,0:T(8,128)(2,1)S(1)}, u32[]{:S(2)}, u32[]{:S(2)}) collective-permute-start(bf16[96,1152]{1,0:T(8,128)(2,1)S(1)} %get-tuple-element.63), channel_id=1, source_target_pairs={{0,32},{1,65},{2,34},{3,67},{4,36},{5,69},{6,38},{7,71},{8,40},{9,... | collective-permute-start | bytes 663560 | tf_op jit(solution)/shard_map/ppermute | solution.py:31
  80.4 8.4 %collective-permute-start.21 = (bf16[96,1152]{1,0:T(8,128)(2,1)S(1)}, bf16[96,1152]{1,0:T(8,128)(2,1)S(1)}, u32[]{:S(2)}, u32[]{:S(2)}) collective-permute-start(bf16[96,1152]{1,0:T(8,128)(2,1)S(1)} %get-tuple-element.64), channel_id=1, source_target_pairs={{0,48},{1,67},{2,50},{3,65},{4,52},{5,71},{6,54},{7,69},{8,56},{9,... | collective-permute-start | bytes 663560 | tf_op jit(solution)/shard_map/ppermute | solution.py:31
  82.2 7.2 %collective-permute-start.22 = (f32[88,576]{1,0:T(8,128)S(1)}, f32[88,576]{1,0:T(8,128)S(1)}, u32[]{:S(2)}, u32[]{:S(2)}) collective-permute-start(f32[88,576]{1,0:T(8,128)S(1)} %slice.37), channel_id=1, source_target_pairs={{0,2},{1,3},{2,0},{3,1},{4,6},{5,7},{6,4},{7,5},{8,10},{9,11},{10,... | collective-permute-start | bytes 608264 | tf_op jit(solution)/shard_map/ppermute | solution.py:31
  90.0 5.5 %collective-permute-start.23 = (f32[352,288]{0,1:T(8,128)S(1)}, f32[352,288]{0,1:T(8,128)S(1)}, u32[]{:S(2)}, u32[]{:S(2)}) collective-permute-start(f32[352,288]{0,1:T(8,128)S(1)} %copy.7), channel_id=1, source_target_pairs={{0,1},{1,0},{2,3},{3,2},{4,5},{5,4},{6,7},{7,6},{8,9},{9,8},{10,11... | collective-permute-start | bytes 1216520 | tf_op jit(solution)/shard_map/ppermute | solution.py:31
  92.2 3.7 %collective-permute-start.26 = (f32[8,128]{1,0:T(8,128)S(1)}, f32[8,128]{1,0:T(8,128)S(1)}, u32[]{:S(2)}, u32[]{:S(2)}) collective-permute-start(f32[8,128]{1,0:T(8,128)S(1)} %get-tuple-element.69.sums_ref), channel_id=1, source_target_pairs={{0,66},{1,49},{2,64},{3,51},{4,70},{5,53},{6,68},{7,55},{8,74},{9,... | collective-permute-start | bytes 12296 | tf_op jit(solution)/shard_map/ppermute | solution.py:31
  93.5 4.0 %collective-permute-start.25 = (f32[8,128]{1,0:T(8,128)S(1)}, f32[8,128]{1,0:T(8,128)S(1)}, u32[]{:S(2)}, u32[]{:S(2)}) collective-permute-start(f32[8,128]{1,0:T(8,128)S(1)} %get-tuple-element.69.sums_ref), channel_id=1, source_target_pairs={{0,64},{1,33},{2,66},{3,35},{4,68},{5,37},{6,70},{7,39},{8,72},{9,... | collective-permute-start | bytes 12296 | tf_op jit(solution)/shard_map/ppermute | solution.py:31
  93.5 3.9 %collective-permute-start.24 = (f32[8,128]{1,0:T(8,128)S(1)}, f32[8,128]{1,0:T(8,128)S(1)}, u32[]{:S(2)}, u32[]{:S(2)}) collective-permute-start(f32[8,128]{1,0:T(8,128)S(1)} %get-tuple-element.69.sums_ref), channel_id=1, source_target_pairs={{0,2},{1,17},{2,0},{3,19},{4,6},{5,21},{6,4},{7,23},{8,10},{9,25},... | collective-permute-start | bytes 12296 | tf_op jit(solution)/shard_map/ppermute | solution.py:31

commit v14 on v11

v14 whole, which is shorter than its diff:
```python
import functools

import jax
import jax.numpy as jnp
from jax import lax
from jax.experimental import pallas as pl
from jax.experimental.pallas import tpu as pltpu
from jax.sharding import PartitionSpec as P

BF = jnp.bfloat16
F32 = jnp.float32
AXES = ("batch", "dim")
CORE = 1


def x_mask(k):
    return k << 2


def y_mask(k):
    return k << 4


def z_mask(k):
    return ((k >> 1) << 6) | ((k & 1) << 1)


def swap(array, mask0, mask1=None):
    mask1 = mask0 if mask1 is None else mask1
    n = lax.axis_size("batch") * lax.axis_size("dim")
    return lax.ppermute(array, AXES, [(i, i ^ (mask1 if i & 1 else mask0)) for i in range(n)])


LOW = 2.0**-3.5


def encode(v, m):
    a = jnp.abs(v) * (127.0 * LOW / m) + LOW
    for _ in range(5):
        a = a * a
    return jnp.where(v < 0, -a, a)


def decode(code, m):
    c = code.astype(F32)
    a = jnp.exp(jnp.log(jnp.abs(c)) * (1.0 / 32.0)) * (1.0 / LOW) - 1.0
    v = a * (m * (1.0 / 127.0))
    return jnp.where(c < 0, -v, v)


def top_of(largest):
    return (largest * 1.01 + 1e-30).astype(BF).astype(F32)


def pairs(core_ref, rows, half, texts, t_rel):
    on0, step = core_ref[0] == 0, 2 * rows
    for b in range(4):
        p0, p1 = (
            jnp.where(on0, texts[2 * (b >> 1) + e][b & 1].astype(F32), texts[b][e].astype(F32)) for e in range(2)
        )
        top = jnp.concatenate([p0[:, :half], p1[:, :half]], axis=1)
        bottom = jnp.concatenate([p0[:, half:], p1[:, half:]], axis=1)
        t_rel[b * step : (b + 1) * step, :] = jnp.concatenate([top, bottom], axis=0).astype(BF)


def coefficients(near, rows, info_ref, scale_ref, t_rel, images, coeff_low):
    scaling, offset = scale_ref[0], scale_ref[1]
    step, columns = 2 * rows, images.shape[0]
    similar = lax.dot_general(t_rel[...], images[...], (((1,), (1,)), ((), ())), preferred_element_type=F32)
    temp, bias = jnp.zeros((1, columns), F32), jnp.zeros((1, columns), F32)
    for b in range(4):
        part = similar[b * step : (b + 1) * step]
        logits = scaling * part + offset
        if near and b == 0:
            row = lax.broadcasted_iota(jnp.int32, part.shape, 0)
            column = lax.broadcasted_iota(jnp.int32, part.shape, 1)
            matched = (row - rows * info_ref[1] == column) & (column < rows)
            sig = 1.0 / (1.0 + jnp.exp(jnp.where(matched, logits, -logits)))
            coeff = jnp.where(matched, -sig, sig)
        else:
            coeff = 1.0 / (1.0 + jnp.exp(-logits))
        coeff_low[b * step : (b + 1) * step, :] = coeff.astype(BF)
        temp = temp + jnp.sum(coeff * part, axis=0, keepdims=True)
        bias = bias + jnp.sum(coeff, axis=0, keepdims=True)
    even = lax.broadcasted_iota(jnp.int32, (8, 128), 1) % 2 == 0
    return jnp.where(even, jnp.sum(temp, axis=1, keepdims=True), jnp.sum(bias, axis=1, keepdims=True))


def text_parts(core_ref, rows, half, coeff_low, images, grads):
    on0, step = core_ref[0] == 0, 2 * rows
    part = jnp.dot(coeff_low[...], images[...], preferred_element_type=F32)
    for b in range(4):
        top, bottom = part[b * step : b * step + rows], part[b * step + rows : (b + 1) * step]
        for e, at in ((0, slice(0, half)), (1, slice(half, 2 * half))):
            place = jnp.where(on0, 2 * (b >> 1) + e, b), jnp.where(on0, b & 1, e)
            grads[place] = jnp.concatenate([top[:, at], bottom[:, at]], axis=1)


def image_parts(coeff_low, t_rel):
    return lax.dot_general(coeff_low[...], t_rel[...], (((0,), (0,)), ((), ())), preferred_element_type=F32)


def split_kernel(rows, info_ref, texts_ref, images_ref, keep_ref, send_ref):
    on0, step = info_ref[0] == 0, 2 * rows
    for at, ref in ((0, texts_ref), (step, images_ref)):
        whole = ref[...].astype(F32).T
        first, second = whole[:step], whole[step:]
        keep_ref[at : at + step, :] = jnp.where(on0, first, second).astype(BF)
        send_ref[at : at + step, :] = jnp.where(on0, second, first).astype(BF)


def join_kernel(rows, info_ref, own_ref, got_ref, texts_ref, images_ref):
    on0, step = info_ref[0] == 0, 2 * rows
    for at, ref in ((0, texts_ref), (step, images_ref)):
        own, got = own_ref[at : at + step, :], got_ref[at : at + step, :]
        ref[...] = jnp.concatenate([jnp.where(on0, own, got), jnp.where(on0, got, own)], axis=0).T


def tile_kernel(last, rows, half, feats, info_ref, scale_ref, *refs):
    texts, (im0_ref, im1_ref), refs = refs[:4], refs[4:6], refs[6:]
    if last:
        acc_ref, sums_before, own_ref, *refs = refs
        messages, (mine_ref, *others), (images, t_rel, coeff_low, grads) = refs[:3], refs[3:8], refs[8:]
    else:
        own_ref, *refs = refs
        messages, (t_rel, coeff_low, sums_ref), (images, grads) = refs[:3], refs[3:6], refs[6:]
    quarter = 4 * rows
    images[0:quarter, :] = im0_ref[...]
    images[quarter : 2 * quarter, :] = im1_ref[...]
    pairs(info_ref, rows, half, texts, t_rel)
    sums = coefficients(last, rows, info_ref, scale_ref, t_rel, images, coeff_low)
    text_parts(info_ref, rows, half, coeff_low, images, grads)
    own_ref[...] = jnp.concatenate([grads[0, i] for i in range(2)], axis=0)
    for k, m_ref in enumerate(messages):
        m_ref[...] = message([grads[k + 1, i] for i in range(2)], feats)
    if last:
        acc = image_parts(coeff_low, t_rel) + acc_ref[...]
        wide = jnp.concatenate([sums + sums_before[...]] * (feats // 128), axis=1)
        mine_ref[...] = jnp.concatenate([acc[0:quarter], wide], axis=0)
        for k, ref in enumerate(others):
            value = acc[quarter + k * rows : quarter + (k + 1) * rows]
            ref[...] = jnp.concatenate([value, wide], axis=0) if k == 0 else value
    else:
        sums_ref[...] = sums


def image_kernel(t_rel, coeff_low, acc_ref):
    acc_ref[...] = image_parts(coeff_low, t_rel)


def message(blocks, feats, extra=()):
    part = jnp.concatenate(blocks, axis=0)
    m = top_of(jnp.max(jnp.max(jnp.abs(part), axis=0, keepdims=True), axis=1, keepdims=True))
    tail = jnp.broadcast_to(m, (8 - len(extra), feats))
    return jnp.concatenate([encode(part, m), *extra, tail], axis=0).astype(BF)


def decoded(ref):
    whole = ref[...].astype(F32)
    n = whole.shape[0] - 8
    return decode(whole[:n], whole[n + 7 : n + 8]), whole[n:]


def split3(v):
    hi = v.astype(BF).astype(F32)
    mid = (v - hi).astype(BF).astype(F32)
    return [hi, mid, v - hi - mid]


def image_first_kernel(rows, feats, own_ref, *refs):
    others, (out_ref, *messages) = refs[:4], refs[4:]
    sums = own_ref[4 * rows :, :] + others[0][rows:, :]
    out_ref[...] = jnp.concatenate([own_ref[0:rows, :] + others[0][0:rows, :], sums], axis=0)
    for i, m_ref in enumerate(messages):
        m_ref[...] = message([own_ref[(i + 1) * rows : (i + 2) * rows, :] + others[i + 1][...]], feats, split3(sums[0:1]))


def with_scalars(own_ref, refs):
    n = own_ref.shape[0] - 8
    total, tails = own_ref[0:n, :], []
    for r in refs:
        value, tail = decoded(r)
        total = total + value
        tails.append(tail[0:1] + (tail[1:2] + tail[2:3]))
    return total, (own_ref[n : n + 1, :] + tails[0]) + (tails[1] + tails[2])


def image_last_kernel(feats, scale_ref, own_ref, r1_ref, r2_ref, r3_ref, out_ref):
    total, sums = with_scalars(own_ref, (r1_ref, r2_ref, r3_ref))
    out_ref[...] = jnp.concatenate([total * scale_ref[0], jnp.broadcast_to(sums, (8, feats))], axis=0)


def text_first_kernel(rows, feats, owna_ref, ownb_ref, a1_ref, a2_ref, a3_ref, b1_ref, b2_ref, b3_ref, out_ref, m1_ref, m2_ref, m3_ref, total):
    step = 2 * rows
    for at, own_ref, refs in ((step, owna_ref, (a1_ref, a2_ref, a3_ref)), (0, ownb_ref, (b1_ref, b2_ref, b3_ref))):
        tops = [r[...].astype(F32)[step + 7 : step + 8] for r in refs]

        def add(k, carry):
            part = pl.ds(pl.multiple_of(k * 16, 16), 16)
            value = own_ref[part, :]
            for r, top in zip(refs, tops):
                value = value + decode(r[part, :], top)
            total[pl.ds(pl.multiple_of(at + k * 16, 16), 16), :] = value
            return carry

        lax.fori_loop(0, step // 16, add, 0, unroll=2)
    out_ref[...] = total[0:rows, :]
    for i, m_ref in enumerate((m1_ref, m2_ref, m3_ref)):
        m_ref[...] = message([total[(i + 1) * rows : (i + 2) * rows, :]], feats)


def text_last_kernel(scale_ref, own_ref, r1_ref, r2_ref, r3_ref, out_ref):
    total = own_ref[...]
    for r in (r1_ref, r2_ref, r3_ref):
        total = total + decoded(r)[0]
    out_ref[...] = total * scale_ref[0]


VMEM = pl.BlockSpec(memory_space=pltpu.VMEM)
SMEM = pl.BlockSpec(memory_space=pltpu.SMEM)


def grant(mib):
    return pltpu.CompilerParams(vmem_limit_bytes=mib * 1024 * 1024)


def after(array, *others):
    return lax.optimization_barrier((array, *others))[0]


def body(picture_embeds, caption_embeds, logit_scaler, logit_offset_term):
    height, width = picture_embeds.shape
    rows, half, feats = height // 4, 2 * width, 4 * width
    step, quarter = 2 * rows, 4 * rows
    index = lax.axis_index("batch") * lax.axis_size("dim") + lax.axis_index("dim")
    core, z_lo = index & 1, (index >> 1) & 1
    on0, lo0 = core == 0, z_lo == 0
    scaling = logit_scaler[0]

    def by(first_one, own, other):
        return [jnp.where(first_one, own, other), jnp.where(first_one, other, own)]

    def f32(*shape):
        return jax.ShapeDtypeStruct(shape, F32)

    def bf16(*shape):
        return jax.ShapeDtypeStruct(shape, BF)

    def call(kernel, name, out_shape, *args, scalars=0, scratch=(), mib=20, products=0):
        return pl.pallas_call(
            kernel,
            out_shape=out_shape,
            in_specs=[SMEM] * scalars + [VMEM] * (len(args) - scalars),
            out_specs=[VMEM] * len(out_shape),
            scratch_shapes=scratch,
            compiler_params=grant(mib),
            cost_estimate=pl.CostEstimate(
                flops=products * 2 * quarter * 2 * quarter * 2 * feats,
                bytes_accessed=sum(a.size * a.dtype.itemsize for a in (*args, *out_shape)),
                transcendentals=products * 4 * quarter * quarter,
            ),
            name=name,
        )(*args)

    info = jnp.stack([core, z_lo]).astype(jnp.int32)
    keep, send = call(
        functools.partial(split_kernel, rows), "split", [bf16(height, width)] * 2, info, caption_embeds.T, picture_embeds.T, scalars=1
    )
    chip = jnp.concatenate(by(on0, keep, swap(send, CORE)), axis=1)
    packed = jnp.concatenate([chip[:rows], chip[rows:step]], axis=1)
    keep, send = by(lo0, chip[step : step + rows], chip[step + rows :])
    first = [packed] + [swap(packed, y_mask(i), z_mask(i)) for i in range(1, 4)]
    image = jnp.concatenate([keep, swap(send, z_mask(1))], axis=1)
    pieces = [image] + [swap(image, x_mask(k)) for k in range(1, 4)]
    images_own = jnp.concatenate(pieces, axis=0)
    images_other = jnp.concatenate([swap(p, CORE) for p in pieces], axis=0)

    def fetch(stack):
        return [stack] + [swap(stack, z_mask(j), y_mask(j)) for j in range(1, 4)]

    texts_a, texts_b = fetch(jnp.stack(first[2:])), fetch(jnp.stack(first[:2]))
    sizes = (rows, half, feats)
    scales = jnp.stack([scaling, logit_offset_term[0]])
    images_shape, coeff_shape = (2 * quarter, feats), (2 * quarter, 2 * quarter)
    grads = pltpu.VMEM((4, 2, rows, feats), F32)
    images_scratch, coeff_scratch = pltpu.VMEM(images_shape, BF), pltpu.VMEM(coeff_shape, BF)
    parts_shape = [f32(step, feats)] + [bf16(step + 8, feats)] * 3

    def give(messages):
        return [swap(m, z_mask(j), y_mask(j)) for j, m in zip((1, 2, 3), messages)]

    own_a, *messages, t_rel, coeff_low, sums = call(
        functools.partial(tile_kernel, False, *sizes), "tile_first",
        parts_shape + [bf16(*images_shape), bf16(*coeff_shape), f32(8, 128)],
        info, scales, *texts_a, images_own, images_other, scalars=2, mib=36, products=2, scratch=[images_scratch, grads],
    )
    got_a = give(messages)
    (acc,) = call(image_kernel, "image_part", [f32(*images_shape)], t_rel, coeff_low, mib=30, products=1)
    texts_b[0] = after(texts_b[0], acc)
    parts = call(
        functools.partial(tile_kernel, True, *sizes), "tile_last",
        parts_shape + [f32(quarter + 8, feats), f32(rows + 8, feats)] + [f32(rows, feats)] * 3,
        info, scales, *texts_b, images_own, images_other, acc, sums,
        scalars=2, mib=36, products=3, scratch=[images_scratch, images_scratch, coeff_scratch, grads],
    )
    own_b, messages, img_own, img_others = parts[0], parts[1:4], parts[4], parts[5:]
    img_others, got_a = lax.optimization_barrier((img_others, got_a))
    got_b = give(messages)
    img, *messages = call(
        functools.partial(image_first_kernel, rows, feats), "image_first",
        [f32(rows + 8, feats)] + [bf16(rows + 8, feats)] * 3, img_own, *[swap(part, CORE) for part in img_others],
    )
    img_got = [swap(m, x_mask(k)) for k, m in zip((1, 2, 3), messages)]
    text, *messages = call(
        functools.partial(text_first_kernel, rows, feats), "text_first",
        [f32(rows, feats)] + [bf16(rows + 8, feats)] * 3, after(own_a, *messages), own_b, *got_a, *got_b,
        scratch=[pltpu.VMEM((quarter, feats), F32)],
    )
    got = [swap(m, y_mask(i), z_mask(i)) for i, m in zip((1, 2, 3), messages)]
    img_got[0] = after(img_got[0], text)
    (img,) = call(functools.partial(image_last_kernel, feats), "image_last", [f32(rows + 8, feats)], logit_scaler, img, *img_got, scalars=1)
    (text,) = call(text_last_kernel, "text_last", [f32(rows, feats)], logit_scaler, text, *got, scalars=1, products=2)
    keep, back = img[:, :half], after(swap(img[:, half:], z_mask(1)), text)
    image = jnp.concatenate(by(lo0, keep[:rows], back[:rows]), axis=0)
    sums = keep[rows:]
    sums = (sums + back[rows:]) + (swap(sums, z_mask(2)) + swap(sums, z_mask(3)))
    sums = sums[:, :128]
    whole = jnp.concatenate([text[:, :half], text[:, half:], image], axis=0)
    mine, other = by(on0, whole[:, :width], whole[:, width:])
    sums, other = lax.optimization_barrier((sums, other))
    other = swap(other, CORE)
    text_grad, image_grad = call(
        functools.partial(join_kernel, rows), "join", [f32(width, height)] * 2, info, mine, other, scalars=1
    )
    s1, s2, s3 = (after(swap(sums, y_mask(k)), text_grad, image_grad) for k in (1, 2, 3))
    sums = (sums + s1) + (s2 + s3)
    return (image_grad.T, text_grad.T, sums[0, :2])


def solution(mesh):
    placed = (P("batch", "dim"), P("batch", "dim"), P(), P())
    return jax.shard_map(
        body,
        mesh=mesh,
        in_specs=placed,
        out_specs=(P("batch", "dim"), P("batch", "dim"), P()),
        check_vma=False,
    )
```

time: 98.6 us -> 108 us (1.095)
  starting transfers between devices: 37.2 us -> 55.9 us
  waiting for transfers between devices: 30.3 us -> 21.1 us
    ppermute x27 -> x41, starting transfers between devices: 37.2 us -> 55.9 us  [swap(): lax.ppermute(array, AXES, [(i, i ^ (mask1 if i & 1 else mask0)) for i in...]
    ppermute x27 -> x41, waiting for transfers between devices: 30.3 us -> 21.1 us  [swap(): lax.ppermute(array, AXES, [(i, i ^ (mask1 if i & 1 else mask0)) for i in...]
    pallas_call x10 -> x9, Pallas kernels: 24.4 us -> 23.7 us  [call(): pl.pallas_call(kernel, out_shape=out_shape, in_specs=[SMEM] * scalars + [...]
  transfers between devices with their start and end apart: 27 -> 41, of which waited for: 17 -> 13; matrix products, arithmetic and copies ran while one was open for 1% -> 1% of each run, Pallas kernels for 21% -> 21%
where the time goes in v14:
time: 108 us; the launch traced here: 107 us
  starting transfers between devices  55.9 us (52%)
  Pallas kernels  23.7 us (22%)
  waiting for transfers between devices  21.1 us (20%)
  local copies, waits for them, and re-layouts  3.13 us (3%)
  between operations  2.23 us (2%)
  other arithmetic  1.21 us (1%)
    ppermute x41, starting transfers between devices, swap(): lax.ppermute(array, AXES, [(i, i ^ (mask1 if i & 1 else mask0)) for i in...  55.9 us
    pallas_call x9, Pallas kernels, call(): pl.pallas_call(kernel, out_shape=out_shape, in_specs=[SMEM] * scalars + [...  23.7 us
    ppermute x41, waiting for transfers between devices, swap(): lax.ppermute(array, AXES, [(i, i ^ (mask1 if i & 1 else mask0)) for i in...  21.1 us
  transfers between devices with their start and end apart: 41, of which 13 were waited for; matrix products, arithmetic and copies ran while one was open for 1% of the time, Pallas kernels for 21%

profile of v14, /device:TPU:1, one launch (start us, length us, event | category | flops | bytes accessed | tf_op | source)
XLA Modules:
  0.0 107.3 jit_solution(9861016649061066762)
XLA Ops:
  0.7 0.9 copy-done
  1.7 0.9 copy-done.1
  2.6 0.8 split.1
  3.4 1.5 %collective-permute-start = (bf16[352,288]{1,0:T(8,128)(2,1)S(1)}, bf16[352,288]{1,0:T(8,128)(2,1)S(1)}, u32[]{:S(2)}, u32[]{:S(2)}) collective-permute-start(bf16[352,288]{1,0:T(8,128)(2,1)S(1)} %get-tuple-element.48), channel_id=1, source_target_pairs={{0,1},{1,0},{2,3},{3,2},{4,5},{5,4},{6,7},{7,6},{8,9},{9,8},{10,11... | collective-permute-start | bytes 608264 | tf_op jit(solution)/shard_map/ppermute | solution.py:31
  6.5 1.8 %collective-permute-start.6 = (bf16[88,576]{1,0:T(8,128)(2,1)S(1)}, bf16[88,576]{1,0:T(8,128)(2,1)S(1)}, u32[]{:S(2)}, u32[]{:S(2)}) collective-permute-start(bf16[88,576]{1,0:T(8,128)(2,1)S(1)} %get-tuple-element.97), channel_id=1, source_target_pairs={{0,2},{1,3},{2,0},{3,1},{4,6},{5,7},{6,4},{7,5},{8,10},{9,11},{10,... | collective-permute-start | bytes 304136 | tf_op jit(solution)/shard_map/ppermute | solution.py:31
  8.7 3.6 %collective-permute-start.2 = (bf16[88,1152]{1,0:T(8,128)(2,1)S(1)}, bf16[88,1152]{1,0:T(8,128)(2,1)S(1)}, u32[]{:S(2)}, u32[]{:S(2)}) collective-permute-start(bf16[88,1152]{1,0:T(8,128)(2,1)S(1)} %pad_maximum_fusion.4), channel_id=1, source_target_pairs={{0,48},{1,67},{2,50},{3,65},{4,52},{5,71},{6,54},{7,69},{8,56},{9,... | collective-permute-start | bytes 608264 | tf_op jit(solution)/shard_map/ppermute | solution.py:31
  12.3 1.4 %collective-permute-start.10 = (bf16[88,1152]{1,0:T(8,128)(2,1)S(1)}, bf16[88,1152]{1,0:T(8,128)(2,1)S(1)}, u32[]{:S(2)}, u32[]{:S(2)}) collective-permute-start(bf16[88,1152]{1,0:T(8,128)(2,1)S(1)} %pad_maximum_fusion.5), channel_id=1, source_target_pairs={{0,1},{1,0},{2,3},{3,2},{4,5},{5,4},{6,7},{7,6},{8,9},{9,8},{10,11... | collective-permute-start | bytes 608264 | tf_op jit(solution)/shard_map/ppermute | solution.py:31
  13.8 2.5 %collective-permute-start.9 = (bf16[88,1152]{1,0:T(8,128)(2,1)S(1)}, bf16[88,1152]{1,0:T(8,128)(2,1)S(1)}, u32[]{:S(2)}, u32[]{:S(2)}) collective-permute-start(bf16[88,1152]{1,0:T(8,128)(2,1)S(1)} %pad_maximum_fusion.5), channel_id=1, source_target_pairs={{0,12},{1,13},{2,14},{3,15},{4,8},{5,9},{6,10},{7,11},{8,4},{9,5},... | collective-permute-start | bytes 608264 | tf_op jit(solution)/shard_map/ppermute | solution.py:31
  16.3 0.8 collective-permute-done.2
  17.1 2.7 %collective-permute-start.8 = (bf16[88,1152]{1,0:T(8,128)(2,1)S(1)}, bf16[88,1152]{1,0:T(8,128)(2,1)S(1)}, u32[]{:S(2)}, u32[]{:S(2)}) collective-permute-start(bf16[88,1152]{1,0:T(8,128)(2,1)S(1)} %pad_maximum_fusion.5), channel_id=1, source_target_pairs={{0,8},{1,9},{2,10},{3,11},{4,12},{5,13},{6,14},{7,15},{8,0},{9,1},... | collective-permute-start | bytes 608264 | tf_op jit(solution)/shard_map/ppermute | solution.py:31
  19.8 1.0 collective-permute-start.7
  20.9 2.5 %collective-permute-start.5 = (bf16[2,88,1152]{2,1,0:T(8,128)(2,1)S(1)}, bf16[2,88,1152]{2,1,0:T(8,128)(2,1)S(1)}, u32[]{:S(2)}, u32[]{:S(2)}) collective-permute-start(bf16[2,88,1152]{2,1,0:T(8,128)(2,1)S(1)} %pad_maximum_fusion.2.refs_0_), channel_id=1, source_target_pairs={{0,66},{1,49},{2,64},{3,51},{4,70},{5,53},{6,68},{7,55},{8,74},{9,... | collective-permute-start | bytes 1216520 | tf_op jit(solution)/shard_map/ppermute | solution.py:31
  23.5 1.6 %collective-permute-done.9 = bf16[88,1152]{1,0:T(8,128)(2,1)S(1)} collective-permute-done((bf16[88,1152]{1,0:T(8,128)(2,1)S(1)}, bf16[88,1152]{1,0:T(8,128)(2,1)S(1)}, u32[]{:S(2)}, u32[]{:S(2)}) %collective-permute-start.9) | collective-permute-done | bytes 202784 | tf_op jit(solution)/shard_map/ppermute | solution.py:31
  25.1 1.2 %collective-permute-start.3 = (bf16[2,88,1152]{2,1,0:T(8,128)(2,1)S(1)}, bf16[2,88,1152]{2,1,0:T(8,128)(2,1)S(1)}, u32[]{:S(2)}, u32[]{:S(2)}) collective-permute-start(bf16[2,88,1152]{2,1,0:T(8,128)(2,1)S(1)} %pad_maximum_fusion.2.refs_0_), channel_id=1, source_target_pairs={{0,2},{1,17},{2,0},{3,19},{4,6},{5,21},{6,4},{7,23},{8,10},{9,25},... | collective-permute-start | bytes 1216520 | tf_op jit(solution)/shard_map/ppermute | solution.py:31
  26.2 2.2 %collective-permute-done.7 = bf16[88,1152]{1,0:T(8,128)(2,1)S(1)} collective-permute-done((bf16[88,1152]{1,0:T(8,128)(2,1)S(1)}, bf16[88,1152]{1,0:T(8,128)(2,1)S(1)}, u32[]{:S(2)}, u32[]{:S(2)}) %collective-permute-start.7) | collective-permute-done | bytes 202784 | tf_op jit(solution)/shard_map/ppermute | solution.py:31
  28.4 2.1 %collective-permute-start.17 = (bf16[2,88,1152]{2,1,0:T(8,128)(2,1)S(1)}, bf16[2,88,1152]{2,1,0:T(8,128)(2,1)S(1)}, u32[]{:S(2)}, u32[]{:S(2)}) collective-permute-start(bf16[2,88,1152]{2,1,0:T(8,128)(2,1)S(1)} %pad_maximum_fusion.3.refs_0_), channel_id=1, source_target_pairs={{0,66},{1,49},{2,64},{3,51},{4,70},{5,53},{6,68},{7,55},{8,74},{9,... | collective-permute-start | bytes 1216520 | tf_op jit(solution)/shard_map/ppermute | solution.py:31
  30.6 3.8 %collective-permute-start.11 = (bf16[88,1152]{1,0:T(8,128)(2,1)S(1)}, bf16[88,1152]{1,0:T(8,128)(2,1)S(1)}, u32[]{:S(2)}, u32[]{:S(2)}) collective-permute-start(bf16[88,1152]{1,0:T(8,128)(2,1)S(1)} %collective-permute-done.7), channel_id=1, source_target_pairs={{0,1},{1,0},{2,3},{3,2},{4,5},{5,4},{6,7},{7,6},{8,9},{9,8},{10,11... | collective-permute-start | bytes 608264 | tf_op jit(solution)/shard_map/ppermute | solution.py:31
  34.4 1.1 collective-permute-done.11
  35.8 1.1 collective-permute-done.12
  37.3 1.1 collective-permute-done.13
  38.3 2.6 %collective-permute-start.16 = (bf16[2,88,1152]{2,1,0:T(8,128)(2,1)S(1)}, bf16[2,88,1152]{2,1,0:T(8,128)(2,1)S(1)}, u32[]{:S(2)}, u32[]{:S(2)}) collective-permute-start(bf16[2,88,1152]{2,1,0:T(8,128)(2,1)S(1)} %pad_maximum_fusion.3.refs_0_), channel_id=1, source_target_pairs={{0,64},{1,33},{2,66},{3,35},{4,68},{5,37},{6,70},{7,39},{8,72},{9,... | collective-permute-start | bytes 1216520 | tf_op jit(solution)/shard_map/ppermute | solution.py:31
  41.0 0.7 collective-permute-start.15
  41.7 6.1 %tile_first.1 = (f32[176,1152]{1,0:T(8,128)S(1)}, bf16[184,1152]{1,0:T(8,128)(2,1)S(1)}, bf16[184,1152]{1,0:T(8,128)(2,1)S(1)}, bf16[184,1152]{1,0:T(8,128)(2,1)...) custom-call(s32[2]{0:T(128)S(1)} %pad_add_fusion.info_ref, ...), custom_call_target="tpu_custom_call" | custom-call | flops 2283798528 | bytes 7944208 | tf_op jit(solution)/shard_map/tile_first/pallas_call | solution.py:250
  47.8 0.9 collective-permute-start.18
  49.1 2.7 %collective-permute-start.20 = (bf16[184,1152]{1,0:T(8,128)(2,1)S(1)}, bf16[184,1152]{1,0:T(8,128)(2,1)S(1)}, u32[]{:S(2)}, u32[]{:S(2)}) collective-permute-start(bf16[184,1152]{1,0:T(8,128)(2,1)S(1)} %get-tuple-element.61), channel_id=1, source_target_pairs={{0,66},{1,49},{2,64},{3,51},{4,70},{5,53},{6,68},{7,55},{8,74},{9,... | collective-permute-start | bytes 1271816 | tf_op jit(solution)/shard_map/ppermute | solution.py:31
  51.8 1.6 %image_part.1.refs_6_ = f32[704,1152]{1,0:T(8,128)S(1)} custom-call(bf16[704,1152]{1,0:T(8,128)(2,1)S(1)} %get-tuple-element.50.t_rel, bf16[704,704]{1,0:T(8,128)(2,1)S(1)} %get-tuple-element.51.coeff_low), custom_call_target="tpu_custom_call" | custom-call | flops 1141899264 | bytes 5857280 | tf_op jit(solution)/shard_map/image_part/pallas_call | solution.py:250
  53.4 7.8 %tile_last.1 = (f32[176,1152]{1,0:T(8,128)S(1)}, bf16[184,1152]{1,0:T(8,128)(2,1)S(1)}, bf16[184,1152]{1,0:T(8,128)(2,1)S(1)}, bf16[184,1152]{1,0:T(8,128)(2,1)S...) custom-call(s32[2]{0:T(128)S(1)} %pad_add_fusion.info_ref, ...), custom_call_target="tpu_custom_call" | custom-call | flops 3425697792 | bytes 11892752 | tf_op jit(solution)/shard_map/tile_last/pallas_call | solution.py:250
  61.3 0.8 collective-permute-done.20.a3_ref
  62.1 2.3 %collective-permute-start.22 = (f32[88,1152]{1,0:T(8,128)S(1)}, f32[88,1152]{1,0:T(8,128)S(1)}, u32[]{:S(2)}, u32[]{:S(2)}) collective-permute-start(f32[88,1152]{1,0:T(8,128)S(1)} %get-tuple-element.63), channel_id=1, source_target_pairs={{0,1},{1,0},{2,3},{3,2},{4,5},{5,4},{6,7},{7,6},{8,9},{9,8},{10,11... | collective-permute-start | bytes 1216520 | tf_op jit(solution)/shard_map/ppermute | solution.py:31
  64.9 0.7 collective-permute-start.25
  65.8 3.1 %collective-permute-start.26 = (bf16[184,1152]{1,0:T(8,128)(2,1)S(1)}, bf16[184,1152]{1,0:T(8,128)(2,1)S(1)}, u32[]{:S(2)}, u32[]{:S(2)}) collective-permute-start(bf16[184,1152]{1,0:T(8,128)(2,1)S(1)} %get-tuple-element.75), channel_id=1, source_target_pairs={{0,64},{1,33},{2,66},{3,35},{4,68},{5,37},{6,70},{7,39},{8,72},{9,... | collective-permute-start | bytes 1271816 | tf_op jit(solution)/shard_map/ppermute | solution.py:31
  69.1 1.0 image_first.1
  70.1 1.2 %collective-permute-start.31 = (bf16[96,1152]{1,0:T(8,128)(2,1)S(1)}, bf16[96,1152]{1,0:T(8,128)(2,1)S(1)}, u32[]{:S(2)}, u32[]{:S(2)}) collective-permute-start(bf16[96,1152]{1,0:T(8,128)(2,1)S(1)} %get-tuple-element.66), channel_id=1, source_target_pairs={{0,4},{1,5},{2,6},{3,7},{4,0},{5,1},{6,2},{7,3},{8,12},{9,13},{10,... | collective-permute-start | bytes 663560 | tf_op jit(solution)/shard_map/ppermute | solution.py:31
  71.3 1.2 %collective-permute-start.32 = (bf16[96,1152]{1,0:T(8,128)(2,1)S(1)}, bf16[96,1152]{1,0:T(8,128)(2,1)S(1)}, u32[]{:S(2)}, u32[]{:S(2)}) collective-permute-start(bf16[96,1152]{1,0:T(8,128)(2,1)S(1)} %get-tuple-element.67), channel_id=1, source_target_pairs={{0,8},{1,9},{2,10},{3,11},{4,12},{5,13},{6,14},{7,15},{8,0},{9,1},... | collective-permute-start | bytes 663560 | tf_op jit(solution)/shard_map/ppermute | solution.py:31
  72.5 1.5 %collective-permute-start.33 = (bf16[96,1152]{1,0:T(8,128)(2,1)S(1)}, bf16[96,1152]{1,0:T(8,128)(2,1)S(1)}, u32[]{:S(2)}, u32[]{:S(2)}) collective-permute-start(bf16[96,1152]{1,0:T(8,128)(2,1)S(1)} %get-tuple-element.68), channel_id=1, source_target_pairs={{0,12},{1,13},{2,14},{3,15},{4,8},{5,9},{6,10},{7,11},{8,4},{9,5},... | collective-permute-start | bytes 663560 | tf_op jit(solution)/shard_map/ppermute | solution.py:31
  74.0 5.0 %collective-permute-done.26.b2_ref = bf16[184,1152]{1,0:T(8,128)(2,1)S(1)} collective-permute-done((bf16[184,1152]{1,0:T(8,128)(2,1)S(1)}, bf16[184,1152]{1,0:T(8,128)(2,1)S(1)}, u32[]{:S(2)}, u32[]{:S(2)}) %collective-permute-start.26) | collective-permute-done | bytes 423968 | tf_op jit(solution)/shard_map/ppermute | solution.py:31
  79.0 2.9 %collective-permute-done.27.b3_ref = bf16[184,1152]{1,0:T(8,128)(2,1)S(1)} collective-permute-done((bf16[184,1152]{1,0:T(8,128)(2,1)S(1)}, bf16[184,1152]{1,0:T(8,128)(2,1)S(1)}, u32[]{:S(2)}, u32[]{:S(2)}) %collective-permute-start.27) | collective-permute-done | bytes 423968 | tf_op jit(solution)/shard_map/ppermute | solution.py:31
  81.9 3.5 %text_first.1 = (f32[88,1152]{1,0:T(8,128)S(1)}, bf16[96,1152]{1,0:T(8,128)(2,1)S(1)}, bf16[96,1152]{1,0:T(8,128)(2,1)S(1)}, bf16[96,1152]{1,0:T(8,128)(2,1)S(1)}) custom-call(f32[176,1152]{1,0:T(8,128)S(1)} %get-tuple-element.69.owna_ref, f32[176,1152]{1,0:T(8,128)S(1)} %get-tuple-element.70.ownb_ref, bf16[184,1152]{1,0:T(8,128)(2,1)S(1)} %collective-permute-done.18.a1_ref, ...), custom_call_target="tpu_custom_call" | custom-call | bytes 5234688 | tf_op jit(solution)/shard_map/text_first/pallas_call | solution.py:250
  85.4 2.0 %collective-permute-start.29 = (bf16[96,1152]{1,0:T(8,128)(2,1)S(1)}, bf16[96,1152]{1,0:T(8,128)(2,1)S(1)}, u32[]{:S(2)}, u32[]{:S(2)}) collective-permute-start(bf16[96,1152]{1,0:T(8,128)(2,1)S(1)} %get-tuple-element.79), channel_id=1, source_target_pairs={{0,32},{1,65},{2,34},{3,67},{4,36},{5,69},{6,38},{7,71},{8,40},{9,... | collective-permute-start | bytes 663560 | tf_op jit(solution)/shard_map/ppermute | solution.py:31
  87.5 1.8 %collective-permute-start.30 = (bf16[96,1152]{1,0:T(8,128)(2,1)S(1)}, bf16[96,1152]{1,0:T(8,128)(2,1)S(1)}, u32[]{:S(2)}, u32[]{:S(2)}) collective-permute-start(bf16[96,1152]{1,0:T(8,128)(2,1)S(1)} %get-tuple-element.80), channel_id=1, source_target_pairs={{0,48},{1,67},{2,50},{3,65},{4,52},{5,71},{6,54},{7,69},{8,56},{9,... | collective-permute-start | bytes 663560 | tf_op jit(solution)/shard_map/ppermute | solution.py:31
  90.0 1.0 collective-permute-start.36
  91.1 2.5 %collective-permute-start.34 = (f32[96,576]{1,0:T(8,128)S(1)}, f32[96,576]{1,0:T(8,128)S(1)}, u32[]{:S(2)}, u32[]{:S(2)}) collective-permute-start(f32[96,576]{1,0:T(8,128)S(1)} %slice.72), channel_id=1, source_target_pairs={{0,2},{1,3},{2,0},{3,1},{4,6},{5,7},{6,4},{7,5},{8,10},{9,11},{10,... | collective-permute-start | bytes 663560 | tf_op jit(solution)/shard_map/ppermute | solution.py:31
  93.5 2.8 %collective-permute-done.30.r3_ref = bf16[96,1152]{1,0:T(8,128)(2,1)S(1)} collective-permute-done((bf16[96,1152]{1,0:T(8,128)(2,1)S(1)}, bf16[96,1152]{1,0:T(8,128)(2,1)S(1)}, u32[]{:S(2)}, u32[]{:S(2)}) %collective-permute-start.30) | collective-permute-done | bytes 221216 | tf_op jit(solution)/shard_map/ppermute | solution.py:31
  97.0 1.3 %collective-permute-done.34 = f32[96,576]{1,0:T(8,128)S(1)} collective-permute-done((f32[96,576]{1,0:T(8,128)S(1)}, f32[96,576]{1,0:T(8,128)S(1)}, u32[]{:S(2)}, u32[]{:S(2)}) %collective-permute-start.34) | collective-permute-done | bytes 221216 | tf_op jit(solution)/shard_map/ppermute | solution.py:31
  98.9 2.3 %collective-permute-start.37 = (f32[352,288]{0,1:T(8,128)S(1)}, f32[352,288]{0,1:T(8,128)S(1)}, u32[]{:S(2)}, u32[]{:S(2)}) collective-permute-start(f32[352,288]{0,1:T(8,128)S(1)} %copy.7), channel_id=1, source_target_pairs={{0,1},{1,0},{2,3},{3,2},{4,5},{5,4},{6,7},{7,6},{8,9},{9,8},{10,11... | collective-permute-start | bytes 1216520 | tf_op jit(solution)/shard_map/ppermute | solution.py:31
  101.3 1.5 %collective-permute-start.40 = (f32[8,128]{1,0:T(8,128)S(1)}, f32[8,128]{1,0:T(8,128)S(1)}, u32[]{:S(2)}, u32[]{:S(2)}) collective-permute-start(f32[8,128]{1,0:T(8,128)S(1)} %fusion.3), channel_id=1, source_target_pairs={{0,48},{1,49},{2,50},{3,51},{4,52},{5,53},{6,54},{7,55},{8,56},{9,... | collective-permute-start | bytes 12296 | tf_op jit(solution)/shard_map/ppermute | solution.py:31
  102.8 1.7 %collective-permute-start.38 = (f32[8,128]{1,0:T(8,128)S(1)}, f32[8,128]{1,0:T(8,128)S(1)}, u32[]{:S(2)}, u32[]{:S(2)}) collective-permute-start(f32[8,128]{1,0:T(8,128)S(1)} %fusion.3), channel_id=1, source_target_pairs={{0,16},{1,17},{2,18},{3,19},{4,20},{5,21},{6,22},{7,23},{8,24},{9,... | collective-permute-start | bytes 12296 | tf_op jit(solution)/shard_map/ppermute | solution.py:31
  104.8 1.7 %join.1 = (f32[288,352]{1,0:T(8,128)}, f32[288,352]{1,0:T(8,128)}) custom-call(s32[2]{0:T(128)S(1)} %pad_add_fusion.info_ref, f32[352,288]{1,0:T(8,128)S(1)} %get-tuple-element.94.own_ref, f32[352,288]{1,0:T(8,128)S(1)} %copy.8.got_ref), custom_call_target="tpu_custom_call" | custom-call | bytes 1622024 | tf_op jit(solution)/shard_map/join/pallas_call | solution.py:250
  (74 shorter events, 6.3 us)
Async XLA Ops:
  0.7 0.9 copy-start
  1.6 0.9 copy-start.1
  3.4 2.9 %collective-permute-start = (bf16[352,288]{1,0:T(8,128)(2,1)S(1)}, bf16[352,288]{1,0:T(8,128)(2,1)S(1)}, u32[]{:S(2)}, u32[]{:S(2)}) collective-permute-start(bf16[352,288]{1,0:T(8,128)(2,1)S(1)} %get-tuple-element.48), channel_id=1, source_target_pairs={{0,1},{1,0},{2,3},{3,2},{4,5},{5,4},{6,7},{7,6},{8,9},{9,8},{10,11... | collective-permute-start | bytes 608264 | tf_op jit(solution)/shard_map/ppermute | solution.py:31
  6.5 5.7 %collective-permute-start.6 = (bf16[88,576]{1,0:T(8,128)(2,1)S(1)}, bf16[88,576]{1,0:T(8,128)(2,1)S(1)}, u32[]{:S(2)}, u32[]{:S(2)}) collective-permute-start(bf16[88,576]{1,0:T(8,128)(2,1)S(1)} %get-tuple-element.97), channel_id=1, source_target_pairs={{0,2},{1,3},{2,0},{3,1},{4,6},{5,7},{6,4},{7,5},{8,10},{9,11},{10,... | collective-permute-start | bytes 304136 | tf_op jit(solution)/shard_map/ppermute | solution.py:31
  8.6 12.4 %collective-permute-start.14 = (bf16[88,1152]{1,0:T(8,128)(2,1)S(1)}, bf16[88,1152]{1,0:T(8,128)(2,1)S(1)}, u32[]{:S(2)}, u32[]{:S(2)}) collective-permute-start(bf16[88,1152]{1,0:T(8,128)(2,1)S(1)} %pad_maximum_fusion.4), channel_id=1, source_target_pairs={{0,16},{1,3},{2,18},{3,1},{4,20},{5,7},{6,22},{7,5},{8,24},{9,11},... | collective-permute-start | bytes 608264 | tf_op jit(solution)/shard_map/ppermute | solution.py:31
  8.7 8.4 %collective-permute-start.2 = (bf16[88,1152]{1,0:T(8,128)(2,1)S(1)}, bf16[88,1152]{1,0:T(8,128)(2,1)S(1)}, u32[]{:S(2)}, u32[]{:S(2)}) collective-permute-start(bf16[88,1152]{1,0:T(8,128)(2,1)S(1)} %pad_maximum_fusion.4), channel_id=1, source_target_pairs={{0,48},{1,67},{2,50},{3,65},{4,52},{5,71},{6,54},{7,69},{8,56},{9,... | collective-permute-start | bytes 608264 | tf_op jit(solution)/shard_map/ppermute | solution.py:31
  12.2 7.6 %collective-permute-start.1 = (bf16[88,1152]{1,0:T(8,128)(2,1)S(1)}, bf16[88,1152]{1,0:T(8,128)(2,1)S(1)}, u32[]{:S(2)}, u32[]{:S(2)}) collective-permute-start(bf16[88,1152]{1,0:T(8,128)(2,1)S(1)} %pad_maximum_fusion.4), channel_id=1, source_target_pairs={{0,32},{1,65},{2,34},{3,67},{4,36},{5,69},{6,38},{7,71},{8,40},{9,... | collective-permute-start | bytes 608264 | tf_op jit(solution)/shard_map/ppermute | solution.py:31
  12.3 18.2 %collective-permute-start.10 = (bf16[88,1152]{1,0:T(8,128)(2,1)S(1)}, bf16[88,1152]{1,0:T(8,128)(2,1)S(1)}, u32[]{:S(2)}, u32[]{:S(2)}) collective-permute-start(bf16[88,1152]{1,0:T(8,128)(2,1)S(1)} %pad_maximum_fusion.5), channel_id=1, source_target_pairs={{0,1},{1,0},{2,3},{3,2},{4,5},{5,4},{6,7},{7,6},{8,9},{9,8},{10,11... | collective-permute-start | bytes 608264 | tf_op jit(solution)/shard_map/ppermute | solution.py:31
  13.8 11.3 %collective-permute-start.9 = (bf16[88,1152]{1,0:T(8,128)(2,1)S(1)}, bf16[88,1152]{1,0:T(8,128)(2,1)S(1)}, u32[]{:S(2)}, u32[]{:S(2)}) collective-permute-start(bf16[88,1152]{1,0:T(8,128)(2,1)S(1)} %pad_maximum_fusion.5), channel_id=1, source_target_pairs={{0,12},{1,13},{2,14},{3,15},{4,8},{5,9},{6,10},{7,11},{8,4},{9,5},... | collective-permute-start | bytes 608264 | tf_op jit(solution)/shard_map/ppermute | solution.py:31
  17.1 8.0 %collective-permute-start.8 = (bf16[88,1152]{1,0:T(8,128)(2,1)S(1)}, bf16[88,1152]{1,0:T(8,128)(2,1)S(1)}, u32[]{:S(2)}, u32[]{:S(2)}) collective-permute-start(bf16[88,1152]{1,0:T(8,128)(2,1)S(1)} %pad_maximum_fusion.5), channel_id=1, source_target_pairs={{0,8},{1,9},{2,10},{3,11},{4,12},{5,13},{6,14},{7,15},{8,0},{9,1},... | collective-permute-start | bytes 608264 | tf_op jit(solution)/shard_map/ppermute | solution.py:31
  19.8 8.6 %collective-permute-start.7 = (bf16[88,1152]{1,0:T(8,128)(2,1)S(1)}, bf16[88,1152]{1,0:T(8,128)(2,1)S(1)}, u32[]{:S(2)}, u32[]{:S(2)}) collective-permute-start(bf16[88,1152]{1,0:T(8,128)(2,1)S(1)} %pad_maximum_fusion.5), channel_id=1, source_target_pairs={{0,4},{1,5},{2,6},{3,7},{4,0},{5,1},{6,2},{7,3},{8,12},{9,13},{10,... | collective-permute-start | bytes 608264 | tf_op jit(solution)/shard_map/ppermute | solution.py:31
  20.9 20.0 %collective-permute-start.5 = (bf16[2,88,1152]{2,1,0:T(8,128)(2,1)S(1)}, bf16[2,88,1152]{2,1,0:T(8,128)(2,1)S(1)}, u32[]{:S(2)}, u32[]{:S(2)}) collective-permute-start(bf16[2,88,1152]{2,1,0:T(8,128)(2,1)S(1)} %pad_maximum_fusion.2.refs_0_), channel_id=1, source_target_pairs={{0,66},{1,49},{2,64},{3,51},{4,70},{5,53},{6,68},{7,55},{8,74},{9,... | collective-permute-start | bytes 1216520 | tf_op jit(solution)/shard_map/ppermute | solution.py:31
  25.1 16.6 %collective-permute-start.4 = (bf16[2,88,1152]{2,1,0:T(8,128)(2,1)S(1)}, bf16[2,88,1152]{2,1,0:T(8,128)(2,1)S(1)}, u32[]{:S(2)}, u32[]{:S(2)}) collective-permute-start(bf16[2,88,1152]{2,1,0:T(8,128)(2,1)S(1)} %pad_maximum_fusion.2.refs_0_), channel_id=1, source_target_pairs={{0,64},{1,33},{2,66},{3,35},{4,68},{5,37},{6,70},{7,39},{8,72},{9,... | collective-permute-start | bytes 1216520 | tf_op jit(solution)/shard_map/ppermute | solution.py:31
  25.1 16.6 %collective-permute-start.3 = (bf16[2,88,1152]{2,1,0:T(8,128)(2,1)S(1)}, bf16[2,88,1152]{2,1,0:T(8,128)(2,1)S(1)}, u32[]{:S(2)}, u32[]{:S(2)}) collective-permute-start(bf16[2,88,1152]{2,1,0:T(8,128)(2,1)S(1)} %pad_maximum_fusion.2.refs_0_), channel_id=1, source_target_pairs={{0,2},{1,17},{2,0},{3,19},{4,6},{5,21},{6,4},{7,23},{8,10},{9,25},... | collective-permute-start | bytes 1216520 | tf_op jit(solution)/shard_map/ppermute | solution.py:31
  28.4 20.6 %collective-permute-start.17 = (bf16[2,88,1152]{2,1,0:T(8,128)(2,1)S(1)}, bf16[2,88,1152]{2,1,0:T(8,128)(2,1)S(1)}, u32[]{:S(2)}, u32[]{:S(2)}) collective-permute-start(bf16[2,88,1152]{2,1,0:T(8,128)(2,1)S(1)} %pad_maximum_fusion.3.refs_0_), channel_id=1, source_target_pairs={{0,66},{1,49},{2,64},{3,51},{4,70},{5,53},{6,68},{7,55},{8,74},{9,... | collective-permute-start | bytes 1216520 | tf_op jit(solution)/shard_map/ppermute | solution.py:31
  30.6 4.9 %collective-permute-start.11 = (bf16[88,1152]{1,0:T(8,128)(2,1)S(1)}, bf16[88,1152]{1,0:T(8,128)(2,1)S(1)}, u32[]{:S(2)}, u32[]{:S(2)}) collective-permute-start(bf16[88,1152]{1,0:T(8,128)(2,1)S(1)} %collective-permute-done.7), channel_id=1, source_target_pairs={{0,1},{1,0},{2,3},{3,2},{4,5},{5,4},{6,7},{7,6},{8,9},{9,8},{10,11... | collective-permute-start | bytes 608264 | tf_op jit(solution)/shard_map/ppermute | solution.py:31
  35.4 1.5 %collective-permute-start.12 = (bf16[88,1152]{1,0:T(8,128)(2,1)S(1)}, bf16[88,1152]{1,0:T(8,128)(2,1)S(1)}, u32[]{:S(2)}, u32[]{:S(2)}) collective-permute-start(bf16[88,1152]{1,0:T(8,128)(2,1)S(1)} %collective-permute-done.8), channel_id=1, source_target_pairs={{0,1},{1,0},{2,3},{3,2},{4,5},{5,4},{6,7},{7,6},{8,9},{9,8},{10,11... | collective-permute-start | bytes 608264 | tf_op jit(solution)/shard_map/ppermute | solution.py:31
  36.9 1.5 %collective-permute-start.13 = (bf16[88,1152]{1,0:T(8,128)(2,1)S(1)}, bf16[88,1152]{1,0:T(8,128)(2,1)S(1)}, u32[]{:S(2)}, u32[]{:S(2)}) collective-permute-start(bf16[88,1152]{1,0:T(8,128)(2,1)S(1)} %collective-permute-done.9), channel_id=1, source_target_pairs={{0,1},{1,0},{2,3},{3,2},{4,5},{5,4},{6,7},{7,6},{8,9},{9,8},{10,11... | collective-permute-start | bytes 608264 | tf_op jit(solution)/shard_map/ppermute | solution.py:31
  38.3 15.1 %collective-permute-start.16 = (bf16[2,88,1152]{2,1,0:T(8,128)(2,1)S(1)}, bf16[2,88,1152]{2,1,0:T(8,128)(2,1)S(1)}, u32[]{:S(2)}, u32[]{:S(2)}) collective-permute-start(bf16[2,88,1152]{2,1,0:T(8,128)(2,1)S(1)} %pad_maximum_fusion.3.refs_0_), channel_id=1, source_target_pairs={{0,64},{1,33},{2,66},{3,35},{4,68},{5,37},{6,70},{7,39},{8,72},{9,... | collective-permute-start | bytes 1216520 | tf_op jit(solution)/shard_map/ppermute | solution.py:31
  41.0 12.5 %collective-permute-start.15 = (bf16[2,88,1152]{2,1,0:T(8,128)(2,1)S(1)}, bf16[2,88,1152]{2,1,0:T(8,128)(2,1)S(1)}, u32[]{:S(2)}, u32[]{:S(2)}) collective-permute-start(bf16[2,88,1152]{2,1,0:T(8,128)(2,1)S(1)} %pad_maximum_fusion.3.refs_0_), channel_id=1, source_target_pairs={{0,2},{1,17},{2,0},{3,19},{4,6},{5,21},{6,4},{7,23},{8,10},{9,25},... | collective-permute-start | bytes 1216520 | tf_op jit(solution)/shard_map/ppermute | solution.py:31
  47.8 13.4 %collective-permute-start.18 = (bf16[184,1152]{1,0:T(8,128)(2,1)S(1)}, bf16[184,1152]{1,0:T(8,128)(2,1)S(1)}, u32[]{:S(2)}, u32[]{:S(2)}) collective-permute-start(bf16[184,1152]{1,0:T(8,128)(2,1)S(1)} %get-tuple-element.59), channel_id=1, source_target_pairs={{0,2},{1,17},{2,0},{3,19},{4,6},{5,21},{6,4},{7,23},{8,10},{9,25},... | collective-permute-start | bytes 1271816 | tf_op jit(solution)/shard_map/ppermute | solution.py:31
  48.7 12.6 %collective-permute-start.19 = (bf16[184,1152]{1,0:T(8,128)(2,1)S(1)}, bf16[184,1152]{1,0:T(8,128)(2,1)S(1)}, u32[]{:S(2)}, u32[]{:S(2)}) collective-permute-start(bf16[184,1152]{1,0:T(8,128)(2,1)S(1)} %get-tuple-element.60), channel_id=1, source_target_pairs={{0,64},{1,33},{2,66},{3,35},{4,68},{5,37},{6,70},{7,39},{8,72},{9,... | collective-permute-start | bytes 1271816 | tf_op jit(solution)/shard_map/ppermute | solution.py:31
  49.1 13.1 %collective-permute-start.20 = (bf16[184,1152]{1,0:T(8,128)(2,1)S(1)}, bf16[184,1152]{1,0:T(8,128)(2,1)S(1)}, u32[]{:S(2)}, u32[]{:S(2)}) collective-permute-start(bf16[184,1152]{1,0:T(8,128)(2,1)S(1)} %get-tuple-element.61), channel_id=1, source_target_pairs={{0,66},{1,49},{2,64},{3,51},{4,70},{5,53},{6,68},{7,55},{8,74},{9,... | collective-permute-start | bytes 1271816 | tf_op jit(solution)/shard_map/ppermute | solution.py:31
  62.1 3.7 %collective-permute-start.22 = (f32[88,1152]{1,0:T(8,128)S(1)}, f32[88,1152]{1,0:T(8,128)S(1)}, u32[]{:S(2)}, u32[]{:S(2)}) collective-permute-start(f32[88,1152]{1,0:T(8,128)S(1)} %get-tuple-element.63), channel_id=1, source_target_pairs={{0,1},{1,0},{2,3},{3,2},{4,5},{5,4},{6,7},{7,6},{8,9},{9,8},{10,11... | collective-permute-start | bytes 1216520 | tf_op jit(solution)/shard_map/ppermute | solution.py:31
  64.4 4.4 %collective-permute-start.23 = (f32[88,1152]{1,0:T(8,128)S(1)}, f32[88,1152]{1,0:T(8,128)S(1)}, u32[]{:S(2)}, u32[]{:S(2)}) collective-permute-start(f32[88,1152]{1,0:T(8,128)S(1)} %get-tuple-element.64), channel_id=1, source_target_pairs={{0,1},{1,0},{2,3},{3,2},{4,5},{5,4},{6,7},{7,6},{8,9},{9,8},{10,11... | collective-permute-start | bytes 1216520 | tf_op jit(solution)/shard_map/ppermute | solution.py:31
  64.4 4.7 %collective-permute-start.21 = (f32[96,1152]{1,0:T(8,128)S(1)}, f32[96,1152]{1,0:T(8,128)S(1)}, u32[]{:S(2)}, u32[]{:S(2)}) collective-permute-start(f32[96,1152]{1,0:T(8,128)S(1)} %get-tuple-element.62), channel_id=1, source_target_pairs={{0,1},{1,0},{2,3},{3,2},{4,5},{5,4},{6,7},{7,6},{8,9},{9,8},{10,11... | collective-permute-start | bytes 1327112 | tf_op jit(solution)/shard_map/ppermute | solution.py:31
  64.9 4.2 %collective-permute-start.24 = (f32[88,1152]{1,0:T(8,128)S(1)}, f32[88,1152]{1,0:T(8,128)S(1)}, u32[]{:S(2)}, u32[]{:S(2)}) collective-permute-start(f32[88,1152]{1,0:T(8,128)S(1)} %get-tuple-element.65), channel_id=1, source_target_pairs={{0,1},{1,0},{2,3},{3,2},{4,5},{5,4},{6,7},{7,6},{8,9},{9,8},{10,11... | collective-permute-start | bytes 1216520 | tf_op jit(solution)/shard_map/ppermute | solution.py:31
  64.9 7.6 %collective-permute-start.25 = (bf16[184,1152]{1,0:T(8,128)(2,1)S(1)}, bf16[184,1152]{1,0:T(8,128)(2,1)S(1)}, u32[]{:S(2)}, u32[]{:S(2)}) collective-permute-start(bf16[184,1152]{1,0:T(8,128)(2,1)S(1)} %get-tuple-element.74), channel_id=1, source_target_pairs={{0,2},{1,17},{2,0},{3,19},{4,6},{5,21},{6,4},{7,23},{8,10},{9,25},... | collective-permute-start | bytes 1271816 | tf_op jit(solution)/shard_map/ppermute | solution.py:31
  65.8 13.2 %collective-permute-start.26 = (bf16[184,1152]{1,0:T(8,128)(2,1)S(1)}, bf16[184,1152]{1,0:T(8,128)(2,1)S(1)}, u32[]{:S(2)}, u32[]{:S(2)}) collective-permute-start(bf16[184,1152]{1,0:T(8,128)(2,1)S(1)} %get-tuple-element.75), channel_id=1, source_target_pairs={{0,64},{1,33},{2,66},{3,35},{4,68},{5,37},{6,70},{7,39},{8,72},{9,... | collective-permute-start | bytes 1271816 | tf_op jit(solution)/shard_map/ppermute | solution.py:31
  68.8 13.0 %collective-permute-start.27 = (bf16[184,1152]{1,0:T(8,128)(2,1)S(1)}, bf16[184,1152]{1,0:T(8,128)(2,1)S(1)}, u32[]{:S(2)}, u32[]{:S(2)}) collective-permute-start(bf16[184,1152]{1,0:T(8,128)(2,1)S(1)} %get-tuple-element.76), channel_id=1, source_target_pairs={{0,66},{1,49},{2,64},{3,51},{4,70},{5,53},{6,68},{7,55},{8,74},{9,... | collective-permute-start | bytes 1271816 | tf_op jit(solution)/shard_map/ppermute | solution.py:31
  70.1 17.4 %collective-permute-start.31 = (bf16[96,1152]{1,0:T(8,128)(2,1)S(1)}, bf16[96,1152]{1,0:T(8,128)(2,1)S(1)}, u32[]{:S(2)}, u32[]{:S(2)}) collective-permute-start(bf16[96,1152]{1,0:T(8,128)(2,1)S(1)} %get-tuple-element.66), channel_id=1, source_target_pairs={{0,4},{1,5},{2,6},{3,7},{4,0},{5,1},{6,2},{7,3},{8,12},{9,13},{10,... | collective-permute-start | bytes 663560 | tf_op jit(solution)/shard_map/ppermute | solution.py:31
  71.3 18.0 %collective-permute-start.32 = (bf16[96,1152]{1,0:T(8,128)(2,1)S(1)}, bf16[96,1152]{1,0:T(8,128)(2,1)S(1)}, u32[]{:S(2)}, u32[]{:S(2)}) collective-permute-start(bf16[96,1152]{1,0:T(8,128)(2,1)S(1)} %get-tuple-element.67), channel_id=1, source_target_pairs={{0,8},{1,9},{2,10},{3,11},{4,12},{5,13},{6,14},{7,15},{8,0},{9,1},... | collective-permute-start | bytes 663560 | tf_op jit(solution)/shard_map/ppermute | solution.py:31
  72.5 16.8 %collective-permute-start.33 = (bf16[96,1152]{1,0:T(8,128)(2,1)S(1)}, bf16[96,1152]{1,0:T(8,128)(2,1)S(1)}, u32[]{:S(2)}, u32[]{:S(2)}) collective-permute-start(bf16[96,1152]{1,0:T(8,128)(2,1)S(1)} %get-tuple-element.68), channel_id=1, source_target_pairs={{0,12},{1,13},{2,14},{3,15},{4,8},{5,9},{6,10},{7,11},{8,4},{9,5},... | collective-permute-start | bytes 663560 | tf_op jit(solution)/shard_map/ppermute | solution.py:31
  85.4 5.7 %collective-permute-start.28 = (bf16[96,1152]{1,0:T(8,128)(2,1)S(1)}, bf16[96,1152]{1,0:T(8,128)(2,1)S(1)}, u32[]{:S(2)}, u32[]{:S(2)}) collective-permute-start(bf16[96,1152]{1,0:T(8,128)(2,1)S(1)} %get-tuple-element.78), channel_id=1, source_target_pairs={{0,16},{1,3},{2,18},{3,1},{4,20},{5,7},{6,22},{7,5},{8,24},{9,11},... | collective-permute-start | bytes 663560 | tf_op jit(solution)/shard_map/ppermute | solution.py:31
  85.4 8.1 %collective-permute-start.29 = (bf16[96,1152]{1,0:T(8,128)(2,1)S(1)}, bf16[96,1152]{1,0:T(8,128)(2,1)S(1)}, u32[]{:S(2)}, u32[]{:S(2)}) collective-permute-start(bf16[96,1152]{1,0:T(8,128)(2,1)S(1)} %get-tuple-element.79), channel_id=1, source_target_pairs={{0,32},{1,65},{2,34},{3,67},{4,36},{5,69},{6,38},{7,71},{8,40},{9,... | collective-permute-start | bytes 663560 | tf_op jit(solution)/shard_map/ppermute | solution.py:31
  87.5 8.8 %collective-permute-start.30 = (bf16[96,1152]{1,0:T(8,128)(2,1)S(1)}, bf16[96,1152]{1,0:T(8,128)(2,1)S(1)}, u32[]{:S(2)}, u32[]{:S(2)}) collective-permute-start(bf16[96,1152]{1,0:T(8,128)(2,1)S(1)} %get-tuple-element.80), channel_id=1, source_target_pairs={{0,48},{1,67},{2,50},{3,65},{4,52},{5,71},{6,54},{7,69},{8,56},{9,... | collective-permute-start | bytes 663560 | tf_op jit(solution)/shard_map/ppermute | solution.py:31
  90.0 8.7 %collective-permute-start.36 = (f32[8,576]{1,0:T(8,128)S(1)}, f32[8,576]{1,0:T(8,128)S(1)}, u32[]{:S(2)}, u32[]{:S(2)}) collective-permute-start(f32[8,576]{1,0:T(8,128)S(1)} %slice.75), channel_id=1, source_target_pairs={{0,66},{1,67},{2,64},{3,65},{4,70},{5,71},{6,68},{7,69},{8,74},{9,... | collective-permute-start | bytes 55304 | tf_op jit(solution)/shard_map/ppermute | solution.py:31
  90.9 7.8 %collective-permute-start.35 = (f32[8,576]{1,0:T(8,128)S(1)}, f32[8,576]{1,0:T(8,128)S(1)}, u32[]{:S(2)}, u32[]{:S(2)}) collective-permute-start(f32[8,576]{1,0:T(8,128)S(1)} %slice.75), channel_id=1, source_target_pairs={{0,64},{1,65},{2,66},{3,67},{4,68},{5,69},{6,70},{7,71},{8,72},{9,... | collective-permute-start | bytes 55304 | tf_op jit(solution)/shard_map/ppermute | solution.py:31
  91.1 7.3 %collective-permute-start.34 = (f32[96,576]{1,0:T(8,128)S(1)}, f32[96,576]{1,0:T(8,128)S(1)}, u32[]{:S(2)}, u32[]{:S(2)}) collective-permute-start(f32[96,576]{1,0:T(8,128)S(1)} %slice.72), channel_id=1, source_target_pairs={{0,2},{1,3},{2,0},{3,1},{4,6},{5,7},{6,4},{7,5},{8,10},{9,11},{10,... | collective-permute-start | bytes 663560 | tf_op jit(solution)/shard_map/ppermute | solution.py:31
  98.9 5.6 %collective-permute-start.37 = (f32[352,288]{0,1:T(8,128)S(1)}, f32[352,288]{0,1:T(8,128)S(1)}, u32[]{:S(2)}, u32[]{:S(2)}) collective-permute-start(f32[352,288]{0,1:T(8,128)S(1)} %copy.7), channel_id=1, source_target_pairs={{0,1},{1,0},{2,3},{3,2},{4,5},{5,4},{6,7},{7,6},{8,9},{9,8},{10,11... | collective-permute-start | bytes 1216520 | tf_op jit(solution)/shard_map/ppermute | solution.py:31
  101.3 5.2 %collective-permute-start.40 = (f32[8,128]{1,0:T(8,128)S(1)}, f32[8,128]{1,0:T(8,128)S(1)}, u32[]{:S(2)}, u32[]{:S(2)}) collective-permute-start(f32[8,128]{1,0:T(8,128)S(1)} %fusion.3), channel_id=1, source_target_pairs={{0,48},{1,49},{2,50},{3,51},{4,52},{5,53},{6,54},{7,55},{8,56},{9,... | collective-permute-start | bytes 12296 | tf_op jit(solution)/shard_map/ppermute | solution.py:31
  102.8 4.0 %collective-permute-start.39 = (f32[8,128]{1,0:T(8,128)S(1)}, f32[8,128]{1,0:T(8,128)S(1)}, u32[]{:S(2)}, u32[]{:S(2)}) collective-permute-start(f32[8,128]{1,0:T(8,128)S(1)} %fusion.3), channel_id=1, source_target_pairs={{0,32},{1,33},{2,34},{3,35},{4,36},{5,37},{6,38},{7,39},{8,40},{9,... | collective-permute-start | bytes 12296 | tf_op jit(solution)/shard_map/ppermute | solution.py:31
  102.8 4.0 %collective-permute-start.38 = (f32[8,128]{1,0:T(8,128)S(1)}, f32[8,128]{1,0:T(8,128)S(1)}, u32[]{:S(2)}, u32[]{:S(2)}) collective-permute-start(f32[8,128]{1,0:T(8,128)S(1)} %fusion.3), channel_id=1, source_target_pairs={{0,16},{1,17},{2,18},{3,19},{4,20},{5,21},{6,22},{7,23},{8,24},{9,... | collective-permute-start | bytes 12296 | tf_op jit(solution)/shard_map/ppermute | solution.py:31

commit v15 on v13

--- a/solution.py
+++ b/solution.py
@@ -109,19 +109,16 @@
         send_ref[at : at + step, :] = jnp.where(on0, second, first).astype(BF)
 
 
-def join_kernel(rows, info_ref, own_ref, got_ref, sums_ref, s1_ref, s2_ref, s3_ref, texts_ref, images_ref, scalars_ref):
+def join_kernel(rows, info_ref, own_ref, got_ref, texts_ref, images_ref):
     on0, step = info_ref[0] == 0, 2 * rows
-    sums = (sums_ref[0:1, :] + s1_ref[0:1, :]) + (s2_ref[0:1, :] + s3_ref[0:1, :])
-    scalars_ref[0] = jnp.sum(sums[:, 0:1])
-    scalars_ref[1] = jnp.sum(sums[:, 1:2])
     for at, ref in ((0, texts_ref), (step, images_ref)):
-        own, got = own_ref[at : at + step, :], got_ref[at : at + step, :]
-        ref[...] = jnp.concatenate([jnp.where(on0, own, got), jnp.where(on0, got, own)], axis=0).T
+        own, got = own_ref[:, at : at + step], got_ref[:, at : at + step]
+        ref[...] = jnp.concatenate([jnp.where(on0, own, got), jnp.where(on0, got, own)], axis=1)
 
 
 def near_kernel(
     rows, half, feats, info_ref, scale_ref, ta_ref, tb_ref, im0_ref, im1_ref,
-    own_ref, m_ref, t_rel, coeff_low, sums_ref, images, grads,
+    grads, m_ref, t_rel, coeff_low, sums_ref, images,
 ):
     quarter = 4 * rows
     images[0:quarter, :] = im0_ref[...]
@@ -129,7 +126,6 @@
     pairs(info_ref, rows, half, ta_ref, tb_ref, t_rel)
     sums_ref[...] = coefficients(True, rows, info_ref, scale_ref, t_rel, images, coeff_low)
     text_parts(info_ref, rows, half, coeff_low, images, grads)
-    own_ref[...] = jnp.concatenate([grads[0, i] for i in range(4)], axis=0)
     m_ref[...] = message([grads[1, i] for i in range(4)], feats)
 
 
@@ -198,8 +194,8 @@
     sums_ref[...] = jnp.broadcast_to(sums, (8, feats))
 
 
-def text_near_kernel(own_ref, r1_ref, out_ref):
-    out_ref[...] = own_ref[...] + decoded(r1_ref)[0]
+def text_near_kernel(grads_ref, r1_ref, out_ref):
+    out_ref[...] = jnp.concatenate([grads_ref[0, i] for i in range(4)], axis=0) + decoded(r1_ref)[0]
 
 
 def text_first_kernel(rows, feats, own_ref, r2_ref, r3_ref, sums_ref, out_ref, m1_ref, m2_ref, m3_ref, total):
@@ -252,12 +248,12 @@
     def bf16(*shape):
         return jax.ShapeDtypeStruct(shape, BF)
 
-    def call(kernel, name, out_shape, *args, scalars=0, scratch=(), mib=20, products=0, out_specs=None):
+    def call(kernel, name, out_shape, *args, scalars=0, scratch=(), mib=20, products=0):
         return pl.pallas_call(
             kernel,
             out_shape=out_shape,
             in_specs=[SMEM] * scalars + [VMEM] * (len(args) - scalars),
-            out_specs=out_specs or [VMEM] * len(out_shape),
+            out_specs=[VMEM] * len(out_shape),
             scratch_shapes=scratch,
             compiler_params=grant(mib),
             cost_estimate=pl.CostEstimate(
@@ -291,9 +287,9 @@
     scratch = [pltpu.VMEM(images_shape, BF), pltpu.VMEM(images_shape, BF), pltpu.VMEM(coeff_shape, BF), grads]
     text, m1, t_near, c_near, sums = call(
         functools.partial(near_kernel, *sizes), "tile_near",
-        [f32(quarter, feats), bf16(quarter + 8, feats), bf16(*images_shape), bf16(*coeff_shape), f32(8, 128)],
+        [f32(2, 4, rows, feats), bf16(quarter + 8, feats), bf16(*images_shape), bf16(*coeff_shape), f32(8, 128)],
         info, scales, stack, second1, images_own, images_other,
-        scalars=2, mib=36, products=2, scratch=[scratch[0], grads],
+        scalars=2, mib=36, products=2, scratch=[scratch[0]],
     )
     got1 = swap(m1, z_mask(1), y_mask(1))
     (acc,) = call(near_image_kernel, "image_near", [f32(*images_shape)], t_near, c_near, mib=30, products=1)
@@ -329,13 +325,13 @@
     whole = jnp.concatenate([text[:, :half], text[:, half:], image], axis=0)
     mine, other = by(on0, whole[:, :width], whole[:, width:])
     sums = after(sums, other)
-    other = swap(other, CORE)
-    lasts = [swap(sums, z_mask(k), y_mask(k)) for k in (1, 2, 3)]
-    text_grad, image_grad, scalar_grads = call(
-        functools.partial(join_kernel, rows), "join", [f32(width, height), f32(width, height), f32(2)],
-        info, mine, other, sums, *lasts, scalars=1, out_specs=[VMEM, VMEM, SMEM],
-    )
-    return (image_grad.T, text_grad.T, scalar_grads)
+    other = swap(other.T, CORE)
+    text_grad, image_grad = call(
+        functools.partial(join_kernel, rows), "join", [f32(width, height)] * 2, info, mine.T, other, scalars=1
+    )
+    s1, s2, s3 = (after(swap(sums, z_mask(k), y_mask(k)), text_grad, image_grad) for k in (1, 2, 3))
+    sums = (sums + s1) + (s2 + s3)
+    return (image_grad.T, text_grad.T, sums[0, :2])
 
 
 def solution(mesh):

time: 99.5 us -> 110 us (1.11); the launches traced: 99.3 us -> 108 us
  local copies, waits for them, and re-layouts: 2.41 us -> 8.77 us
  other arithmetic: 1.34 us -> 4.08 us
  waiting for transfers between devices: 32 us -> 30.6 us
    concatenate x1, other arithmetic: 0.06 us -> 2.6 us  [body(): jnp.concatenate([image] + [swap(image, x_mask(k)) for k in range(1, 4)],...]
    optimization_barrier x0 -> x1, local copies, waits for them, and re-layouts: none -> 2.29 us  [after(): return lax.optimization_barrier((array, *others))[0]]
    concatenate x0 -> x1, local copies, waits for them, and re-layouts: none -> 1.57 us  [body(): jnp.concatenate([image] + [swap(image, x_mask(k)) for k in range(1, 4)],...]
    ppermute x27, waiting for transfers between devices: 32 us -> 30.6 us  [swap(): lax.ppermute(array, AXES, [(i, i ^ (mask1 if i & 1 else mask0)) for i in...]
    unnamed x4 -> x6, local copies, waits for them, and re-layouts: 1.87 us -> 2.91 us
  transfers between devices with their start and end apart: 27 -> 27, of which waited for: 19 -> 15; matrix products, arithmetic and copies ran while one was open for 1% -> 8% of each run, Pallas kernels for 19% -> 20%
where the time goes in v15:
time: 110 us; the launch traced here: 108 us
  starting transfers between devices  37.8 us (34%)
  waiting for transfers between devices  30.6 us (28%)
  Pallas kernels  25 us (23%)
  local copies, waits for them, and re-layouts  8.77 us (8%)
  other arithmetic  4.08 us (4%)
  between operations  2.12 us (2%)
    ppermute x27, starting transfers between devices, swap(): lax.ppermute(array, AXES, [(i, i ^ (mask1 if i & 1 else mask0)) for i in...  37.8 us
    ppermute x27, waiting for transfers between devices, swap(): lax.ppermute(array, AXES, [(i, i ^ (mask1 if i & 1 else mask0)) for i in...  30.6 us
    pallas_call x10, Pallas kernels, call(): pl.pallas_call(kernel, out_shape=out_shape, in_specs=[SMEM] * scalars + [...  25 us
    unnamed x6, local copies, waits for them, and re-layouts  2.91 us
    concatenate x1, other arithmetic, body(): jnp.concatenate([image] + [swap(image, x_mask(k)) for k in range(1, 4)],...  2.6 us
    optimization_barrier x1, local copies, waits for them, and re-layouts, after(): return lax.optimization_barrier((array, *others))[0]  2.29 us
  transfers between devices with their start and end apart: 27, of which 15 were waited for; matrix products, arithmetic and copies ran while one was open for 8% of the time, Pallas kernels for 20%

profile of v15, /device:TPU:1, one launch (start us, length us, event | category | flops | bytes accessed | tf_op | source)
XLA Modules:
  0.0 108.4 jit_solution(14080360673698755047)
XLA Ops:
  0.7 0.9 copy-done
  1.7 0.9 copy-done.1
  2.6 0.8 split.1
  3.6 1.5 %collective-permute-start = (bf16[352,288]{0,1:T(8,128)(2,1)S(1)}, bf16[352,288]{0,1:T(8,128)(2,1)S(1)}, u32[]{:S(2)}, u32[]{:S(2)}) collective-permute-start(bf16[352,288]{0,1:T(8,128)(2,1)S(1)} %copy.22), channel_id=1, source_target_pairs={{0,1},{1,0},{2,3},{3,2},{4,5},{5,4},{6,7},{7,6},{8,9},{9,8},{10,11... | collective-permute-start | bytes 608264 | tf_op jit(solution)/shard_map/ppermute | solution.py:31
  5.2 0.9 collective-permute-done
  6.4 1.8 %collective-permute-start.6 = (bf16[88,576]{0,1:T(8,128)(2,1)S(1)}, bf16[88,576]{0,1:T(8,128)(2,1)S(1)}, u32[]{:S(2)}, u32[]{:S(2)}) collective-permute-start(bf16[88,576]{0,1:T(8,128)(2,1)S(1)} %get-tuple-element.86), channel_id=1, source_target_pairs={{0,2},{1,3},{2,0},{3,1},{4,6},{5,7},{6,4},{7,5},{8,10},{9,11},{10,... | collective-permute-start | bytes 304136 | tf_op jit(solution)/shard_map/ppermute | solution.py:31
  8.3 3.4 %collective-permute-start.2 = (bf16[88,1152]{0,1:T(8,128)(2,1)S(1)}, bf16[88,1152]{0,1:T(8,128)(2,1)S(1)}, u32[]{:S(2)}, u32[]{:S(2)}) collective-permute-start(bf16[88,1152]{0,1:T(8,128)(2,1)S(1)} %get-tuple-element.90), channel_id=1, source_target_pairs={{0,32},{1,65},{2,34},{3,67},{4,36},{5,69},{6,38},{7,71},{8,40},{9,... | collective-permute-start | bytes 608264 | tf_op jit(solution)/shard_map/ppermute | solution.py:31
  12.2 2.5 %collective-permute-start.9 = (bf16[88,1152]{0,1:T(8,128)(2,1)S(1)}, bf16[88,1152]{0,1:T(8,128)(2,1)}, u32[]{:S(2)}, u32[]{:S(2)}) collective-permute-start(bf16[88,1152]{0,1:T(8,128)(2,1)S(1)} %pad_maximum_fusion.4), channel_id=1, source_target_pairs={{0,12},{1,13},{2,14},{3,15},{4,8},{5,9},{6,10},{7,11},{8,4},{9,5},... | collective-permute-start | bytes 608264 | tf_op jit(solution)/shard_map/ppermute | solution.py:31
  15.2 3.7 %collective-permute-done.2 = bf16[88,1152]{0,1:T(8,128)(2,1)S(1)} collective-permute-done((bf16[88,1152]{0,1:T(8,128)(2,1)S(1)}, bf16[88,1152]{0,1:T(8,128)(2,1)S(1)}, u32[]{:S(2)}, u32[]{:S(2)}) %collective-permute-start.2) | collective-permute-done | bytes 202784 | tf_op jit(solution)/shard_map/ppermute | solution.py:31
  18.9 1.2 %collective-permute-start.7 = (bf16[88,1152]{0,1:T(8,128)(2,1)S(1)}, bf16[88,1152]{0,1:T(8,128)(2,1)}, u32[]{:S(2)}, u32[]{:S(2)}) collective-permute-start(bf16[88,1152]{0,1:T(8,128)(2,1)S(1)} %pad_maximum_fusion.4), channel_id=1, source_target_pairs={{0,4},{1,5},{2,6},{3,7},{4,0},{5,1},{6,2},{7,3},{8,12},{9,13},{10,... | collective-permute-start | bytes 608264 | tf_op jit(solution)/shard_map/ppermute | solution.py:31
  20.1 1.7 %collective-permute-done.3 = bf16[88,1152]{0,1:T(8,128)(2,1)S(1)} collective-permute-done((bf16[88,1152]{0,1:T(8,128)(2,1)S(1)}, bf16[88,1152]{0,1:T(8,128)(2,1)S(1)}, u32[]{:S(2)}, u32[]{:S(2)}) %collective-permute-start.3) | collective-permute-done | bytes 202784 | tf_op jit(solution)/shard_map/ppermute | solution.py:31
  22.1 1.0 copy-done.2
  23.2 0.6 copy.28.ta_ref
  23.8 2.8 %collective-permute-start.5 = (bf16[4,88,1152]{2,1,0:T(8,128)(2,1)S(1)}, bf16[4,88,1152]{2,1,0:T(8,128)(2,1)S(1)}, u32[]{:S(2)}, u32[]{:S(2)}) collective-permute-start(bf16[4,88,1152]{2,1,0:T(8,128)(2,1)S(1)} %copy.28.ta_ref), channel_id=1, source_target_pairs={{0,66},{1,49},{2,64},{3,51},{4,70},{5,53},{6,68},{7,55},{8,74},{9,... | collective-permute-start | bytes 2433032 | tf_op jit(solution)/shard_map/ppermute | solution.py:31
  27.2 0.9 collective-permute-done.7
  28.1 2.6 %pad_maximum_fusion.1 = bf16[352,1152]{0,1:T(8,128)(2,1)} fusion(bf16[88,1152]{0,1:T(8,128)(2,1)} %collective-permute-done.9, bf16[88,1152]{0,1:T(8,128)(2,1)} %collective-permute-done.8, bf16[88,1152]{0,1:T(8,128)(2,1)} %collective-permute-done.7, bf16[88,576]{0,1:T(8,128)(2,1)S(1)} %collective-permute-done.6, bf16[88,576]{0,1:T(8,128)(2,1)S(1)} %get-tuple-element.83), kind=kLoop, calls=%fused_computation.1 | loop fusion | flops 4055040 | bytes 1622016 | tf_op jit(solution)/shard_map/concatenate | solution.py:278
  30.7 1.6 %copy.29.im0_ref = bf16[352,1152]{1,0:T(8,128)(2,1)S(1)} copy(bf16[352,1152]{0,1:T(8,128)(2,1)} %pad_maximum_fusion.1) | data formatting | bytes 1622016 | tf_op jit(solution)/shard_map/concatenate | solution.py:278
  32.3 1.9 %collective-permute-start.10 = (bf16[352,1152]{1,0:T(8,128)(2,1)S(1)}, bf16[352,1152]{1,0:T(8,128)(2,1)}, u32[]{:S(2)}, u32[]{:S(2)}) collective-permute-start(bf16[352,1152]{1,0:T(8,128)(2,1)S(1)} %copy.29.im0_ref), channel_id=1, source_target_pairs={{0,1},{1,0},{2,3},{3,2},{4,5},{5,4},{6,7},{7,6},{8,9},{9,8},{10,11... | collective-permute-start | bytes 2433032 | tf_op jit(solution)/shard_map/ppermute | solution.py:31
  35.5 2.3 %copy.30 = bf16[4,88,1152]{2,1,0:T(8,128)(2,1)} copy(bf16[4,88,1152]{1,2,0:T(8,128)(2,1)} %copy-done.2) | data formatting | bytes 1622016 | tf_op jit(solution)/shard_map/optimization_barrier | solution.py:230
  37.8 2.9 %collective-permute-start.11 = (bf16[4,88,1152]{2,1,0:T(8,128)(2,1)}, bf16[4,88,1152]{2,1,0:T(8,128)(2,1)S(1)}, u32[]{:S(2)}, u32[]{:S(2)}) collective-permute-start(bf16[4,88,1152]{2,1,0:T(8,128)(2,1)} %copy.30), channel_id=1, source_target_pairs={{0,64},{1,33},{2,66},{3,35},{4,68},{5,37},{6,70},{7,39},{8,72},{9,... | collective-permute-start | bytes 2433032 | tf_op jit(solution)/shard_map/ppermute | solution.py:31
  40.8 6.3 %tile_near.1 = (f32[2,4,88,1152]{3,2,1,0:T(8,128)S(1)}, bf16[360,1152]{1,0:T(8,128)(2,1)S(1)}, bf16[704,1152]{1,0:T(8,128)(2,1)S(1)}, bf16[704,704]{1,0:T(8,128)(2,1)S(1)}, f32[8,128]{1,0:T(8,128)S(1)}) custom-call(s32[2]{0:T(128)S(1)} %pad_add_fusion.info_ref, f32[2]{0:T(128)S(1)} %pad_maximum_fusion.6.scale_ref, bf16[4,88,1152]{2,1,0:T(8,128)(2,1)S(1)} %copy.28.ta_ref, ...), custom_call_target="tpu_custom_call" | custom-call | flops 2283798528 | bytes 9934864 | tf_op jit(solution)/shard_map/tile_near/pallas_call | solution.py:252
  47.1 0.7 collective-permute-start.12
  47.7 1.6 %image_near.1.before_ref = f32[704,1152]{1,0:T(8,128)S(1)} custom-call(bf16[704,1152]{1,0:T(8,128)(2,1)S(1)} %get-tuple-element.45.t_rel, bf16[704,704]{1,0:T(8,128)(2,1)S(1)} %get-tuple-element.46.coeff_low), custom_call_target="tpu_custom_call" | custom-call | flops 1141899264 | bytes 5857280 | tf_op jit(solution)/shard_map/image_near/pallas_call | solution.py:252
  49.4 1.6 %collective-permute-done.11.ta_ref = bf16[4,88,1152]{2,1,0:T(8,128)(2,1)S(1)} collective-permute-done((bf16[4,88,1152]{2,1,0:T(8,128)(2,1)}, bf16[4,88,1152]{2,1,0:T(8,128)(2,1)S(1)}, u32[]{:S(2)}, u32[]{:S(2)}) %collective-permute-start.11) | collective-permute-done | bytes 811040 | tf_op jit(solution)/shard_map/ppermute | solution.py:31
  50.9 9.1 %tile_far.1 = (bf16[360,1152]{1,0:T(8,128)(2,1)S(1)}, bf16[360,1152]{1,0:T(8,128)(2,1)S(1)}, f32[360,1152]{1,0:T(8,128)S(1)}, f32[360,1152]{1,0:T(8,128)S(1)}) custom-call(s32[2]{0:T(128)S(1)} %pad_add_fusion.info_ref, f32[2]{0:T(128)S(1)} %pad_maximum_fusion.6.scale_ref, bf16[4,88,1152]{2,1,0:T(8,128)(2,1)S(1)} %collective-permute-done.11.ta_ref, ...), custom_call_target="tpu_custom_call" | custom-call | flops 3425697792 | bytes 11468816 | tf_op jit(solution)/shard_map/tile_far/pallas_call | solution.py:252
  60.1 1.5 %collective-permute-start.13 = (f32[360,1152]{1,0:T(8,128)S(1)}, f32[360,1152]{1,0:T(8,128)S(1)}, u32[]{:S(2)}, u32[]{:S(2)}) collective-permute-start(f32[360,1152]{1,0:T(8,128)S(1)} %get-tuple-element.53), channel_id=1, source_target_pairs={{0,1},{1,0},{2,3},{3,2},{4,5},{5,4},{6,7},{7,6},{8,9},{9,8},{10,11... | collective-permute-start | bytes 4976648 | tf_op jit(solution)/shard_map/ppermute | solution.py:31
  61.6 2.9 %collective-permute-start.14 = (bf16[360,1152]{1,0:T(8,128)(2,1)S(1)}, bf16[360,1152]{1,0:T(8,128)(2,1)S(1)}, u32[]{:S(2)}, u32[]{:S(2)}) collective-permute-start(bf16[360,1152]{1,0:T(8,128)(2,1)S(1)} %get-tuple-element.59), channel_id=1, source_target_pairs={{0,64},{1,33},{2,66},{3,35},{4,68},{5,37},{6,70},{7,39},{8,72},{9,... | collective-permute-start | bytes 2488328 | tf_op jit(solution)/shard_map/ppermute | solution.py:31
  64.5 0.8 collective-permute-start.15
  65.3 1.0 image_first.1
  66.3 1.3 %collective-permute-start.16 = (bf16[96,1152]{1,0:T(8,128)(2,1)S(1)}, bf16[96,1152]{1,0:T(8,128)(2,1)S(1)}, u32[]{:S(2)}, u32[]{:S(2)}) collective-permute-start(bf16[96,1152]{1,0:T(8,128)(2,1)S(1)} %get-tuple-element.54), channel_id=1, source_target_pairs={{0,4},{1,5},{2,6},{3,7},{4,0},{5,1},{6,2},{7,3},{8,12},{9,13},{10,... | collective-permute-start | bytes 663560 | tf_op jit(solution)/shard_map/ppermute | solution.py:31
  67.6 2.5 %collective-permute-start.17 = (bf16[96,1152]{1,0:T(8,128)(2,1)S(1)}, bf16[96,1152]{1,0:T(8,128)(2,1)S(1)}, u32[]{:S(2)}, u32[]{:S(2)}) collective-permute-start(bf16[96,1152]{1,0:T(8,128)(2,1)S(1)} %get-tuple-element.55), channel_id=1, source_target_pairs={{0,8},{1,9},{2,10},{3,11},{4,12},{5,13},{6,14},{7,15},{8,0},{9,1},... | collective-permute-start | bytes 663560 | tf_op jit(solution)/shard_map/ppermute | solution.py:31
  70.2 0.8 text_near.1.own_ref
  71.0 2.4 %collective-permute-done.16.r1_ref = bf16[96,1152]{1,0:T(8,128)(2,1)S(1)} collective-permute-done((bf16[96,1152]{1,0:T(8,128)(2,1)S(1)}, bf16[96,1152]{1,0:T(8,128)(2,1)S(1)}, u32[]{:S(2)}, u32[]{:S(2)}) %collective-permute-start.16) | collective-permute-done | bytes 221216 | tf_op jit(solution)/shard_map/ppermute | solution.py:31
  73.4 7.0 %collective-permute-done.17.r2_ref = bf16[96,1152]{1,0:T(8,128)(2,1)S(1)} collective-permute-done((bf16[96,1152]{1,0:T(8,128)(2,1)S(1)}, bf16[96,1152]{1,0:T(8,128)(2,1)S(1)}, u32[]{:S(2)}, u32[]{:S(2)}) %collective-permute-start.17) | collective-permute-done | bytes 221216 | tf_op jit(solution)/shard_map/ppermute | solution.py:31
  80.4 2.0 %collective-permute-done.18.r3_ref = bf16[96,1152]{1,0:T(8,128)(2,1)S(1)} collective-permute-done((bf16[96,1152]{1,0:T(8,128)(2,1)S(1)}, bf16[96,1152]{1,0:T(8,128)(2,1)S(1)}, u32[]{:S(2)}, u32[]{:S(2)}) %collective-permute-start.18) | collective-permute-done | bytes 221216 | tf_op jit(solution)/shard_map/ppermute | solution.py:31
  82.4 0.6 image_last.1
  83.6 2.6 %text_first.1 = (f32[96,1152]{1,0:T(8,128)S(1)}, bf16[96,1152]{1,0:T(8,128)(2,1)S(1)}, bf16[96,1152]{1,0:T(8,128)(2,1)S(1)}, bf16[96,1152]{1,0:T(8,128)(2,1)S(1)}) custom-call(f32[352,1152]{1,0:T(8,128)S(1)} %text_near.1.own_ref, bf16[360,1152]{1,0:T(8,128)(2,1)S(1)} %collective-permute-done.14.r2_ref, bf16[360,1152]{1,0:T(8,128)(2,1)S(1)} %collective-permute-done.15.r3_ref, ...), custom_call_target="tpu_custom_call" | custom-call | bytes 4423680 | tf_op jit(solution)/shard_map/text_first/pallas_call | solution.py:252
  86.2 0.7 collective-permute-start.19
  86.9 3.3 %collective-permute-start.20 = (bf16[96,1152]{1,0:T(8,128)(2,1)S(1)}, bf16[96,1152]{1,0:T(8,128)(2,1)S(1)}, u32[]{:S(2)}, u32[]{:S(2)}) collective-permute-start(bf16[96,1152]{1,0:T(8,128)(2,1)S(1)} %get-tuple-element.65), channel_id=1, source_target_pairs={{0,32},{1,65},{2,34},{3,67},{4,36},{5,69},{6,38},{7,71},{8,40},{9,... | collective-permute-start | bytes 663560 | tf_op jit(solution)/shard_map/ppermute | solution.py:31
  90.5 0.9 collective-permute-done.19.r1_ref
  91.4 4.8 %collective-permute-done.20.r2_ref = bf16[96,1152]{1,0:T(8,128)(2,1)S(1)} collective-permute-done((bf16[96,1152]{1,0:T(8,128)(2,1)S(1)}, bf16[96,1152]{1,0:T(8,128)(2,1)S(1)}, u32[]{:S(2)}, u32[]{:S(2)}) %collective-permute-start.20) | collective-permute-done | bytes 221216 | tf_op jit(solution)/shard_map/ppermute | solution.py:31
  96.2 2.3 %collective-permute-done.21.r3_ref = bf16[96,1152]{1,0:T(8,128)(2,1)S(1)} collective-permute-done((bf16[96,1152]{1,0:T(8,128)(2,1)S(1)}, bf16[96,1152]{1,0:T(8,128)(2,1)S(1)}, u32[]{:S(2)}, u32[]{:S(2)}) %collective-permute-start.21) | collective-permute-done | bytes 221216 | tf_op jit(solution)/shard_map/ppermute | solution.py:31
  98.5 0.6 text_last.1
  100.0 1.9 %collective-permute-start.23 = (f32[288,352]{1,0:T(8,128)S(1)}, f32[288,352]{1,0:T(8,128)S(1)}, u32[]{:S(2)}, u32[]{:S(2)}) collective-permute-start(f32[288,352]{1,0:T(8,128)S(1)} %bitcast.18), channel_id=1, source_target_pairs={{0,1},{1,0},{2,3},{3,2},{4,5},{5,4},{6,7},{7,6},{8,9},{9,8},{10,11... | collective-permute-start | bytes 1216520 | tf_op jit(solution)/shard_map/ppermute | solution.py:31
  101.9 2.1 %collective-permute-start.26 = (f32[8,128]{1,0:T(8,128)S(1)}, f32[8,128]{1,0:T(8,128)S(1)}, u32[]{:S(2)}, u32[]{:S(2)}) collective-permute-start(f32[8,128]{1,0:T(8,128)S(1)} %get-tuple-element.73), channel_id=1, source_target_pairs={{0,66},{1,49},{2,64},{3,51},{4,70},{5,53},{6,68},{7,55},{8,74},{9,... | collective-permute-start | bytes 12296 | tf_op jit(solution)/shard_map/ppermute | solution.py:31
  104.3 0.8 collective-permute-start.24
  105.1 1.6 %join.1 = (f32[288,352]{1,0:T(8,128)}, f32[288,352]{1,0:T(8,128)}) custom-call(s32[2]{0:T(128)S(1)} %pad_add_fusion.info_ref, f32[288,352]{1,0:T(8,128)S(1)} %get-tuple-element.78.own_ref, f32[288,352]{1,0:T(8,128)S(1)} %collective-permute-done.23.got_ref), custom_call_target="tpu_custom_call" | custom-call | bytes 1622024 | tf_op jit(solution)/shard_map/join/pallas_call | solution.py:252
  106.7 1.2 %collective-permute-done.25 = f32[8,128]{1,0:T(8,128)S(1)} collective-permute-done((f32[8,128]{1,0:T(8,128)S(1)}, f32[8,128]{1,0:T(8,128)S(1)}, u32[]{:S(2)}, u32[]{:S(2)}) %collective-permute-start.25) | collective-permute-done | bytes 4128 | tf_op jit(solution)/shard_map/ppermute | solution.py:31
  (43 shorter events, 5.7 us)
Async XLA Ops:
  0.7 0.9 copy-start
  1.6 0.9 copy-start.1
  3.6 2.6 %collective-permute-start = (bf16[352,288]{0,1:T(8,128)(2,1)S(1)}, bf16[352,288]{0,1:T(8,128)(2,1)S(1)}, u32[]{:S(2)}, u32[]{:S(2)}) collective-permute-start(bf16[352,288]{0,1:T(8,128)(2,1)S(1)} %copy.22), channel_id=1, source_target_pairs={{0,1},{1,0},{2,3},{3,2},{4,5},{5,4},{6,7},{7,6},{8,9},{9,8},{10,11... | collective-permute-start | bytes 608264 | tf_op jit(solution)/shard_map/ppermute | solution.py:31
  6.4 5.7 %collective-permute-start.6 = (bf16[88,576]{0,1:T(8,128)(2,1)S(1)}, bf16[88,576]{0,1:T(8,128)(2,1)S(1)}, u32[]{:S(2)}, u32[]{:S(2)}) collective-permute-start(bf16[88,576]{0,1:T(8,128)(2,1)S(1)} %get-tuple-element.86), channel_id=1, source_target_pairs={{0,2},{1,3},{2,0},{3,1},{4,6},{5,7},{6,4},{7,5},{8,10},{9,11},{10,... | collective-permute-start | bytes 304136 | tf_op jit(solution)/shard_map/ppermute | solution.py:31
  8.3 10.6 %collective-permute-start.2 = (bf16[88,1152]{0,1:T(8,128)(2,1)S(1)}, bf16[88,1152]{0,1:T(8,128)(2,1)S(1)}, u32[]{:S(2)}, u32[]{:S(2)}) collective-permute-start(bf16[88,1152]{0,1:T(8,128)(2,1)S(1)} %get-tuple-element.90), channel_id=1, source_target_pairs={{0,32},{1,65},{2,34},{3,67},{4,36},{5,69},{6,38},{7,71},{8,40},{9,... | collective-permute-start | bytes 608264 | tf_op jit(solution)/shard_map/ppermute | solution.py:31
  11.7 8.4 %collective-permute-start.1 = (bf16[88,1152]{0,1:T(8,128)(2,1)S(1)}, bf16[88,1152]{0,1:T(8,128)(2,1)S(1)}, u32[]{:S(2)}, u32[]{:S(2)}) collective-permute-start(bf16[88,1152]{0,1:T(8,128)(2,1)S(1)} %get-tuple-element.90), channel_id=1, source_target_pairs={{0,16},{1,3},{2,18},{3,1},{4,20},{5,7},{6,22},{7,5},{8,24},{9,11},... | collective-permute-start | bytes 608264 | tf_op jit(solution)/shard_map/ppermute | solution.py:31
  11.7 10.1 %collective-permute-start.3 = (bf16[88,1152]{0,1:T(8,128)(2,1)S(1)}, bf16[88,1152]{0,1:T(8,128)(2,1)S(1)}, u32[]{:S(2)}, u32[]{:S(2)}) collective-permute-start(bf16[88,1152]{0,1:T(8,128)(2,1)S(1)} %get-tuple-element.90), channel_id=1, source_target_pairs={{0,48},{1,67},{2,50},{3,65},{4,52},{5,71},{6,54},{7,69},{8,56},{9,... | collective-permute-start | bytes 608264 | tf_op jit(solution)/shard_map/ppermute | solution.py:31
  12.2 15.0 %collective-permute-start.9 = (bf16[88,1152]{0,1:T(8,128)(2,1)S(1)}, bf16[88,1152]{0,1:T(8,128)(2,1)}, u32[]{:S(2)}, u32[]{:S(2)}) collective-permute-start(bf16[88,1152]{0,1:T(8,128)(2,1)S(1)} %pad_maximum_fusion.4), channel_id=1, source_target_pairs={{0,12},{1,13},{2,14},{3,15},{4,8},{5,9},{6,10},{7,11},{8,4},{9,5},... | collective-permute-start | bytes 608264 | tf_op jit(solution)/shard_map/ppermute | solution.py:31
  14.7 12.5 %collective-permute-start.8 = (bf16[88,1152]{0,1:T(8,128)(2,1)S(1)}, bf16[88,1152]{0,1:T(8,128)(2,1)}, u32[]{:S(2)}, u32[]{:S(2)}) collective-permute-start(bf16[88,1152]{0,1:T(8,128)(2,1)S(1)} %pad_maximum_fusion.4), channel_id=1, source_target_pairs={{0,8},{1,9},{2,10},{3,11},{4,12},{5,13},{6,14},{7,15},{8,0},{9,1},... | collective-permute-start | bytes 608264 | tf_op jit(solution)/shard_map/ppermute | solution.py:31
  18.9 9.2 %collective-permute-start.7 = (bf16[88,1152]{0,1:T(8,128)(2,1)S(1)}, bf16[88,1152]{0,1:T(8,128)(2,1)}, u32[]{:S(2)}, u32[]{:S(2)}) collective-permute-start(bf16[88,1152]{0,1:T(8,128)(2,1)S(1)} %pad_maximum_fusion.4), channel_id=1, source_target_pairs={{0,4},{1,5},{2,6},{3,7},{4,0},{5,1},{6,2},{7,3},{8,12},{9,13},{10,... | collective-permute-start | bytes 608264 | tf_op jit(solution)/shard_map/ppermute | solution.py:31
  22.1 1.0 copy-start.2
  23.8 16.9 %collective-permute-start.5 = (bf16[4,88,1152]{2,1,0:T(8,128)(2,1)S(1)}, bf16[4,88,1152]{2,1,0:T(8,128)(2,1)S(1)}, u32[]{:S(2)}, u32[]{:S(2)}) collective-permute-start(bf16[4,88,1152]{2,1,0:T(8,128)(2,1)S(1)} %copy.28.ta_ref), channel_id=1, source_target_pairs={{0,66},{1,49},{2,64},{3,51},{4,70},{5,53},{6,68},{7,55},{8,74},{9,... | collective-permute-start | bytes 2433032 | tf_op jit(solution)/shard_map/ppermute | solution.py:31
  26.6 14.1 %collective-permute-start.4 = (bf16[4,88,1152]{2,1,0:T(8,128)(2,1)S(1)}, bf16[4,88,1152]{2,1,0:T(8,128)(2,1)S(1)}, u32[]{:S(2)}, u32[]{:S(2)}) collective-permute-start(bf16[4,88,1152]{2,1,0:T(8,128)(2,1)S(1)} %copy.28.ta_ref), channel_id=1, source_target_pairs={{0,2},{1,17},{2,0},{3,19},{4,6},{5,21},{6,4},{7,23},{8,10},{9,25},... | collective-permute-start | bytes 2433032 | tf_op jit(solution)/shard_map/ppermute | solution.py:31
  32.3 8.5 %collective-permute-start.10 = (bf16[352,1152]{1,0:T(8,128)(2,1)S(1)}, bf16[352,1152]{1,0:T(8,128)(2,1)}, u32[]{:S(2)}, u32[]{:S(2)}) collective-permute-start(bf16[352,1152]{1,0:T(8,128)(2,1)S(1)} %copy.29.im0_ref), channel_id=1, source_target_pairs={{0,1},{1,0},{2,3},{3,2},{4,5},{5,4},{6,7},{7,6},{8,9},{9,8},{10,11... | collective-permute-start | bytes 2433032 | tf_op jit(solution)/shard_map/ppermute | solution.py:31
  37.8 13.1 %collective-permute-start.11 = (bf16[4,88,1152]{2,1,0:T(8,128)(2,1)}, bf16[4,88,1152]{2,1,0:T(8,128)(2,1)S(1)}, u32[]{:S(2)}, u32[]{:S(2)}) collective-permute-start(bf16[4,88,1152]{2,1,0:T(8,128)(2,1)} %copy.30), channel_id=1, source_target_pairs={{0,64},{1,33},{2,66},{3,35},{4,68},{5,37},{6,70},{7,39},{8,72},{9,... | collective-permute-start | bytes 2433032 | tf_op jit(solution)/shard_map/ppermute | solution.py:31
  47.1 13.0 %collective-permute-start.12 = (bf16[360,1152]{1,0:T(8,128)(2,1)S(1)}, bf16[360,1152]{1,0:T(8,128)(2,1)S(1)}, u32[]{:S(2)}, u32[]{:S(2)}) collective-permute-start(bf16[360,1152]{1,0:T(8,128)(2,1)S(1)} %get-tuple-element.52), channel_id=1, source_target_pairs={{0,2},{1,17},{2,0},{3,19},{4,6},{5,21},{6,4},{7,23},{8,10},{9,25},... | collective-permute-start | bytes 2488328 | tf_op jit(solution)/shard_map/ppermute | solution.py:31
  60.1 5.2 %collective-permute-start.13 = (f32[360,1152]{1,0:T(8,128)S(1)}, f32[360,1152]{1,0:T(8,128)S(1)}, u32[]{:S(2)}, u32[]{:S(2)}) collective-permute-start(f32[360,1152]{1,0:T(8,128)S(1)} %get-tuple-element.53), channel_id=1, source_target_pairs={{0,1},{1,0},{2,3},{3,2},{4,5},{5,4},{6,7},{7,6},{8,9},{9,8},{10,11... | collective-permute-start | bytes 4976648 | tf_op jit(solution)/shard_map/ppermute | solution.py:31
  61.6 21.5 %collective-permute-start.14 = (bf16[360,1152]{1,0:T(8,128)(2,1)S(1)}, bf16[360,1152]{1,0:T(8,128)(2,1)S(1)}, u32[]{:S(2)}, u32[]{:S(2)}) collective-permute-start(bf16[360,1152]{1,0:T(8,128)(2,1)S(1)} %get-tuple-element.59), channel_id=1, source_target_pairs={{0,64},{1,33},{2,66},{3,35},{4,68},{5,37},{6,70},{7,39},{8,72},{9,... | collective-permute-start | bytes 2488328 | tf_op jit(solution)/shard_map/ppermute | solution.py:31
  64.5 19.1 %collective-permute-start.15 = (bf16[360,1152]{1,0:T(8,128)(2,1)S(1)}, bf16[360,1152]{1,0:T(8,128)(2,1)S(1)}, u32[]{:S(2)}, u32[]{:S(2)}) collective-permute-start(bf16[360,1152]{1,0:T(8,128)(2,1)S(1)} %get-tuple-element.60), channel_id=1, source_target_pairs={{0,66},{1,49},{2,64},{3,51},{4,70},{5,53},{6,68},{7,55},{8,74},{9,... | collective-permute-start | bytes 2488328 | tf_op jit(solution)/shard_map/ppermute | solution.py:31
  66.3 7.1 %collective-permute-start.16 = (bf16[96,1152]{1,0:T(8,128)(2,1)S(1)}, bf16[96,1152]{1,0:T(8,128)(2,1)S(1)}, u32[]{:S(2)}, u32[]{:S(2)}) collective-permute-start(bf16[96,1152]{1,0:T(8,128)(2,1)S(1)} %get-tuple-element.54), channel_id=1, source_target_pairs={{0,4},{1,5},{2,6},{3,7},{4,0},{5,1},{6,2},{7,3},{8,12},{9,13},{10,... | collective-permute-start | bytes 663560 | tf_op jit(solution)/shard_map/ppermute | solution.py:31
  67.6 12.8 %collective-permute-start.17 = (bf16[96,1152]{1,0:T(8,128)(2,1)S(1)}, bf16[96,1152]{1,0:T(8,128)(2,1)S(1)}, u32[]{:S(2)}, u32[]{:S(2)}) collective-permute-start(bf16[96,1152]{1,0:T(8,128)(2,1)S(1)} %get-tuple-element.55), channel_id=1, source_target_pairs={{0,8},{1,9},{2,10},{3,11},{4,12},{5,13},{6,14},{7,15},{8,0},{9,1},... | collective-permute-start | bytes 663560 | tf_op jit(solution)/shard_map/ppermute | solution.py:31
  70.0 12.4 %collective-permute-start.18 = (bf16[96,1152]{1,0:T(8,128)(2,1)S(1)}, bf16[96,1152]{1,0:T(8,128)(2,1)S(1)}, u32[]{:S(2)}, u32[]{:S(2)}) collective-permute-start(bf16[96,1152]{1,0:T(8,128)(2,1)S(1)} %get-tuple-element.56), channel_id=1, source_target_pairs={{0,12},{1,13},{2,14},{3,15},{4,8},{5,9},{6,10},{7,11},{8,4},{9,5},... | collective-permute-start | bytes 663560 | tf_op jit(solution)/shard_map/ppermute | solution.py:31
  86.2 5.2 %collective-permute-start.19 = (bf16[96,1152]{1,0:T(8,128)(2,1)S(1)}, bf16[96,1152]{1,0:T(8,128)(2,1)S(1)}, u32[]{:S(2)}, u32[]{:S(2)}) collective-permute-start(bf16[96,1152]{1,0:T(8,128)(2,1)S(1)} %get-tuple-element.64), channel_id=1, source_target_pairs={{0,16},{1,3},{2,18},{3,1},{4,20},{5,7},{6,22},{7,5},{8,24},{9,11},... | collective-permute-start | bytes 663560 | tf_op jit(solution)/shard_map/ppermute | solution.py:31
  86.9 9.3 %collective-permute-start.20 = (bf16[96,1152]{1,0:T(8,128)(2,1)S(1)}, bf16[96,1152]{1,0:T(8,128)(2,1)S(1)}, u32[]{:S(2)}, u32[]{:S(2)}) collective-permute-start(bf16[96,1152]{1,0:T(8,128)(2,1)S(1)} %get-tuple-element.65), channel_id=1, source_target_pairs={{0,32},{1,65},{2,34},{3,67},{4,36},{5,69},{6,38},{7,71},{8,40},{9,... | collective-permute-start | bytes 663560 | tf_op jit(solution)/shard_map/ppermute | solution.py:31
  90.1 8.4 %collective-permute-start.21 = (bf16[96,1152]{1,0:T(8,128)(2,1)S(1)}, bf16[96,1152]{1,0:T(8,128)(2,1)S(1)}, u32[]{:S(2)}, u32[]{:S(2)}) collective-permute-start(bf16[96,1152]{1,0:T(8,128)(2,1)S(1)} %get-tuple-element.66), channel_id=1, source_target_pairs={{0,48},{1,67},{2,50},{3,65},{4,52},{5,71},{6,54},{7,69},{8,56},{9,... | collective-permute-start | bytes 663560 | tf_op jit(solution)/shard_map/ppermute | solution.py:31
  90.4 8.9 %collective-permute-start.22 = (f32[88,576]{0,1:T(8,128)S(1)}, f32[88,576]{0,1:T(8,128)S(1)}, u32[]{:S(2)}, u32[]{:S(2)}) collective-permute-start(f32[88,576]{0,1:T(8,128)S(1)} %slice.53), channel_id=1, source_target_pairs={{0,2},{1,3},{2,0},{3,1},{4,6},{5,7},{6,4},{7,5},{8,10},{9,11},{10,... | collective-permute-start | bytes 608264 | tf_op jit(solution)/shard_map/ppermute | solution.py:31
  100.0 5.1 %collective-permute-start.23 = (f32[288,352]{1,0:T(8,128)S(1)}, f32[288,352]{1,0:T(8,128)S(1)}, u32[]{:S(2)}, u32[]{:S(2)}) collective-permute-start(f32[288,352]{1,0:T(8,128)S(1)} %bitcast.18), channel_id=1, source_target_pairs={{0,1},{1,0},{2,3},{3,2},{4,5},{5,4},{6,7},{7,6},{8,9},{9,8},{10,11... | collective-permute-start | bytes 1216520 | tf_op jit(solution)/shard_map/ppermute | solution.py:31
  101.9 4.9 %collective-permute-start.26 = (f32[8,128]{1,0:T(8,128)S(1)}, f32[8,128]{1,0:T(8,128)S(1)}, u32[]{:S(2)}, u32[]{:S(2)}) collective-permute-start(f32[8,128]{1,0:T(8,128)S(1)} %get-tuple-element.73), channel_id=1, source_target_pairs={{0,66},{1,49},{2,64},{3,51},{4,70},{5,53},{6,68},{7,55},{8,74},{9,... | collective-permute-start | bytes 12296 | tf_op jit(solution)/shard_map/ppermute | solution.py:31
  103.9 4.0 %collective-permute-start.25 = (f32[8,128]{1,0:T(8,128)S(1)}, f32[8,128]{1,0:T(8,128)S(1)}, u32[]{:S(2)}, u32[]{:S(2)}) collective-permute-start(f32[8,128]{1,0:T(8,128)S(1)} %get-tuple-element.73), channel_id=1, source_target_pairs={{0,64},{1,33},{2,66},{3,35},{4,68},{5,37},{6,70},{7,39},{8,72},{9,... | collective-permute-start | bytes 12296 | tf_op jit(solution)/shard_map/ppermute | solution.py:31
  104.3 3.6 %collective-permute-start.24 = (f32[8,128]{1,0:T(8,128)S(1)}, f32[8,128]{1,0:T(8,128)S(1)}, u32[]{:S(2)}, u32[]{:S(2)}) collective-permute-start(f32[8,128]{1,0:T(8,128)S(1)} %get-tuple-element.73), channel_id=1, source_target_pairs={{0,2},{1,17},{2,0},{3,19},{4,6},{5,21},{6,4},{7,23},{8,10},{9,25},... | collective-permute-start | bytes 12296 | tf_op jit(solution)/shard_map/ppermute | solution.py:31

commit v16 on v15

--- a/solution.py
+++ b/solution.py
@@ -112,8 +112,8 @@
 def join_kernel(rows, info_ref, own_ref, got_ref, texts_ref, images_ref):
     on0, step = info_ref[0] == 0, 2 * rows
     for at, ref in ((0, texts_ref), (step, images_ref)):
-        own, got = own_ref[:, at : at + step], got_ref[:, at : at + step]
-        ref[...] = jnp.concatenate([jnp.where(on0, own, got), jnp.where(on0, got, own)], axis=1)
+        own, got = own_ref[at : at + step, :], got_ref[at : at + step, :]
+        ref[...] = jnp.concatenate([jnp.where(on0, own, got), jnp.where(on0, got, own)], axis=0).T
 
 
 def near_kernel(
@@ -325,9 +325,9 @@
     whole = jnp.concatenate([text[:, :half], text[:, half:], image], axis=0)
     mine, other = by(on0, whole[:, :width], whole[:, width:])
     sums = after(sums, other)
-    other = swap(other.T, CORE)
+    other = swap(other, CORE)
     text_grad, image_grad = call(
-        functools.partial(join_kernel, rows), "join", [f32(width, height)] * 2, info, mine.T, other, scalars=1
+        functools.partial(join_kernel, rows), "join", [f32(width, height)] * 2, info, mine, other, scalars=1
     )
     s1, s2, s3 = (after(swap(sums, z_mask(k), y_mask(k)), text_grad, image_grad) for k in (1, 2, 3))
     sums = (sums + s1) + (s2 + s3)

time: 110 us -> 98.1 us (0.89); the launches traced: 108 us -> 97.8 us
  local copies, waits for them, and re-layouts: 8.77 us -> 2.92 us
  other arithmetic: 4.08 us -> 1.34 us
  Pallas kernels: 25 us -> 23.9 us
    concatenate x1, other arithmetic: 2.6 us -> 0.06 us  [body(): jnp.concatenate([image] + [swap(image, x_mask(k)) for k in range(1, 4)],...]
    optimization_barrier x1 -> x0, local copies, waits for them, and re-layouts: 2.29 us -> none  [after(): return lax.optimization_barrier((array, *others))[0]]
    concatenate x1 -> x0, local copies, waits for them, and re-layouts: 1.57 us -> none  [body(): jnp.concatenate([image] + [swap(image, x_mask(k)) for k in range(1, 4)],...]
    pallas_call x10, Pallas kernels: 25 us -> 23.9 us  [call(): pl.pallas_call(kernel, out_shape=out_shape, in_specs=[SMEM] * scalars + [...]
    unnamed x6 -> x4, local copies, waits for them, and re-layouts: 2.91 us -> 1.87 us
  transfers between devices with their start and end apart: 27 -> 27, of which waited for: 15 -> 17; matrix products, arithmetic and copies ran while one was open for 8% -> 1% of each run, Pallas kernels for 20% -> 21%
where the time goes in v16:
time: 98.1 us; the launch traced here: 97.8 us
  starting transfers between devices  37 us (38%)
  waiting for transfers between devices  30.5 us (31%)
  Pallas kernels  23.9 us (24%)
  local copies, waits for them, and re-layouts  2.92 us (3%)
  between operations  2.11 us (2%)
  other arithmetic  1.34 us (1%)
    ppermute x27, starting transfers between devices, swap(): lax.ppermute(array, AXES, [(i, i ^ (mask1 if i & 1 else mask0)) for i in...  37 us
    ppermute x27, waiting for transfers between devices, swap(): lax.ppermute(array, AXES, [(i, i ^ (mask1 if i & 1 else mask0)) for i in...  30.5 us
    pallas_call x10, Pallas kernels, call(): pl.pallas_call(kernel, out_shape=out_shape, in_specs=[SMEM] * scalars + [...  23.9 us
  transfers between devices with their start and end apart: 27, of which 17 were waited for; matrix products, arithmetic and copies ran while one was open for 1% of the time, Pallas kernels for 21%

profile of v16, /device:TPU:1, one launch (start us, length us, event | category | flops | bytes accessed | tf_op | source)
XLA Modules:
  0.0 97.8 jit_solution(5635940351115585406)
XLA Ops:
  0.7 0.9 copy-done
  1.7 0.9 copy-done.1
  2.6 0.8 split.1
  3.4 1.5 %collective-permute-start = (bf16[352,288]{1,0:T(8,128)(2,1)S(1)}, bf16[352,288]{1,0:T(8,128)(2,1)S(1)}, u32[]{:S(2)}, u32[]{:S(2)}) collective-permute-start(bf16[352,288]{1,0:T(8,128)(2,1)S(1)} %get-tuple-element.41), channel_id=1, source_target_pairs={{0,1},{1,0},{2,3},{3,2},{4,5},{5,4},{6,7},{7,6},{8,9},{9,8},{10,11... | collective-permute-start | bytes 608264 | tf_op jit(solution)/shard_map/ppermute | solution.py:31
  4.9 1.2 %collective-permute-done = bf16[352,288]{1,0:T(8,128)(2,1)S(1)} collective-permute-done((bf16[352,288]{1,0:T(8,128)(2,1)S(1)}, bf16[352,288]{1,0:T(8,128)(2,1)S(1)}, u32[]{:S(2)}, u32[]{:S(2)}) %collective-permute-start) | collective-permute-done | bytes 202784 | tf_op jit(solution)/shard_map/ppermute | solution.py:31
  6.3 1.8 %collective-permute-start.6 = (bf16[88,576]{1,0:T(8,128)(2,1)S(1)}, bf16[88,576]{1,0:T(8,128)(2,1)S(1)}, u32[]{:S(2)}, u32[]{:S(2)}) collective-permute-start(bf16[88,576]{1,0:T(8,128)(2,1)S(1)} %get-tuple-element.83), channel_id=1, source_target_pairs={{0,2},{1,3},{2,0},{3,1},{4,6},{5,7},{6,4},{7,5},{8,10},{9,11},{10,... | collective-permute-start | bytes 304136 | tf_op jit(solution)/shard_map/ppermute | solution.py:31
  8.4 3.4 %collective-permute-start.2 = (bf16[88,1152]{1,0:T(8,128)(2,1)S(1)}, bf16[88,1152]{1,0:T(8,128)(2,1)S(1)}, u32[]{:S(2)}, u32[]{:S(2)}) collective-permute-start(bf16[88,1152]{1,0:T(8,128)(2,1)S(1)} %pad_maximum_fusion.3), channel_id=1, source_target_pairs={{0,32},{1,65},{2,34},{3,67},{4,36},{5,69},{6,38},{7,71},{8,40},{9,... | collective-permute-start | bytes 608264 | tf_op jit(solution)/shard_map/ppermute | solution.py:31
  12.2 2.6 %collective-permute-start.9 = (bf16[88,1152]{1,0:T(8,128)(2,1)S(1)}, bf16[88,1152]{1,0:T(8,128)(2,1)S(1)}, u32[]{:S(2)}, u32[]{:S(2)}) collective-permute-start(bf16[88,1152]{1,0:T(8,128)(2,1)S(1)} %pad_maximum_fusion.4), channel_id=1, source_target_pairs={{0,12},{1,13},{2,14},{3,15},{4,8},{5,9},{6,10},{7,11},{8,4},{9,5},... | collective-permute-start | bytes 608264 | tf_op jit(solution)/shard_map/ppermute | solution.py:31
  15.3 1.8 %collective-permute-done.2 = bf16[88,1152]{1,0:T(8,128)(2,1)S(1)} collective-permute-done((bf16[88,1152]{1,0:T(8,128)(2,1)S(1)}, bf16[88,1152]{1,0:T(8,128)(2,1)S(1)}, u32[]{:S(2)}, u32[]{:S(2)}) %collective-permute-start.2) | collective-permute-done | bytes 202784 | tf_op jit(solution)/shard_map/ppermute | solution.py:31
  17.1 1.2 %collective-permute-start.7 = (bf16[88,1152]{1,0:T(8,128)(2,1)S(1)}, bf16[88,1152]{1,0:T(8,128)(2,1)S(1)}, u32[]{:S(2)}, u32[]{:S(2)}) collective-permute-start(bf16[88,1152]{1,0:T(8,128)(2,1)S(1)} %pad_maximum_fusion.4), channel_id=1, source_target_pairs={{0,4},{1,5},{2,6},{3,7},{4,0},{5,1},{6,2},{7,3},{8,12},{9,13},{10,... | collective-permute-start | bytes 608264 | tf_op jit(solution)/shard_map/ppermute | solution.py:31
  18.3 1.0 %collective-permute-done.3 = bf16[88,1152]{1,0:T(8,128)(2,1)S(1)} collective-permute-done((bf16[88,1152]{1,0:T(8,128)(2,1)S(1)}, bf16[88,1152]{1,0:T(8,128)(2,1)S(1)}, u32[]{:S(2)}, u32[]{:S(2)}) %collective-permute-start.3) | collective-permute-done | bytes 202784 | tf_op jit(solution)/shard_map/ppermute | solution.py:31
  19.5 2.8 %collective-permute-start.5 = (bf16[4,88,1152]{2,1,0:T(8,128)(2,1)S(1)}, bf16[4,88,1152]{2,1,0:T(8,128)(2,1)S(1)}, u32[]{:S(2)}, u32[]{:S(2)}) collective-permute-start(bf16[4,88,1152]{2,1,0:T(8,128)(2,1)S(1)} %pad_maximum_fusion.1.ta_ref), channel_id=1, source_target_pairs={{0,66},{1,49},{2,64},{3,51},{4,70},{5,53},{6,68},{7,55},{8,74},{9,... | collective-permute-start | bytes 2433032 | tf_op jit(solution)/shard_map/ppermute | solution.py:31
  22.3 1.1 %collective-permute-done.9 = bf16[88,1152]{1,0:T(8,128)(2,1)S(1)} collective-permute-done((bf16[88,1152]{1,0:T(8,128)(2,1)S(1)}, bf16[88,1152]{1,0:T(8,128)(2,1)S(1)}, u32[]{:S(2)}, u32[]{:S(2)}) %collective-permute-start.9) | collective-permute-done | bytes 202784 | tf_op jit(solution)/shard_map/ppermute | solution.py:31
  23.3 0.8 collective-permute-done.7
  24.2 1.9 %collective-permute-start.10 = (bf16[352,1152]{1,0:T(8,128)(2,1)S(1)}, bf16[352,1152]{1,0:T(8,128)(2,1)S(1)}, u32[]{:S(2)}, u32[]{:S(2)}) collective-permute-start(bf16[352,1152]{1,0:T(8,128)(2,1)S(1)} %pad_maximum_fusion.2.im0_ref), channel_id=1, source_target_pairs={{0,1},{1,0},{2,3},{3,2},{4,5},{5,4},{6,7},{7,6},{8,9},{9,8},{10,11... | collective-permute-start | bytes 2433032 | tf_op jit(solution)/shard_map/ppermute | solution.py:31
  27.4 3.0 %collective-permute-start.11 = (bf16[4,88,1152]{2,1,0:T(8,128)(2,1)S(1)}, bf16[4,88,1152]{2,1,0:T(8,128)(2,1)S(1)}, u32[]{:S(2)}, u32[]{:S(2)}) collective-permute-start(bf16[4,88,1152]{2,1,0:T(8,128)(2,1)S(1)} %pad_maximum_fusion.1.ta_ref), channel_id=1, source_target_pairs={{0,64},{1,33},{2,66},{3,35},{4,68},{5,37},{6,70},{7,39},{8,72},{9,... | collective-permute-start | bytes 2433032 | tf_op jit(solution)/shard_map/ppermute | solution.py:31
  30.4 1.8 %collective-permute-done.5.tb_ref = bf16[4,88,1152]{2,1,0:T(8,128)(2,1)S(1)} collective-permute-done((bf16[4,88,1152]{2,1,0:T(8,128)(2,1)S(1)}, bf16[4,88,1152]{2,1,0:T(8,128)(2,1)S(1)}, u32[]{:S(2)}, u32[]{:S(2)}) %collective-permute-start.5) | collective-permute-done | bytes 811040 | tf_op jit(solution)/shard_map/ppermute | solution.py:31
  32.2 1.5 %collective-permute-done.4.tb_ref = bf16[4,88,1152]{2,1,0:T(8,128)(2,1)S(1)} collective-permute-done((bf16[4,88,1152]{2,1,0:T(8,128)(2,1)S(1)}, bf16[4,88,1152]{2,1,0:T(8,128)(2,1)S(1)}, u32[]{:S(2)}, u32[]{:S(2)}) %collective-permute-start.4) | collective-permute-done | bytes 811040 | tf_op jit(solution)/shard_map/ppermute | solution.py:31
  33.7 5.7 %tile_near.1 = (f32[2,4,88,1152]{3,2,1,0:T(8,128)S(1)}, bf16[360,1152]{1,0:T(8,128)(2,1)S(1)}, bf16[704,1152]{1,0:T(8,128)(2,1)S(1)}, bf16[704,704]{1,0:T(8,128)(2,1)S(1)}, f32[8,128]{1,0:T(8,128)S(1)}) custom-call(s32[2]{0:T(128)S(1)} %pad_add_fusion.info_ref, f32[2]{0:T(128)S(1)} %pad_maximum_fusion.6.scale_ref, ...), custom_call_target="tpu_custom_call" | custom-call | flops 2283798528 | bytes 9934864 | tf_op jit(solution)/shard_map/tile_near/pallas_call | solution.py:252
  39.7 1.6 %image_near.1.before_ref = f32[704,1152]{1,0:T(8,128)S(1)} custom-call(bf16[704,1152]{1,0:T(8,128)(2,1)S(1)} %get-tuple-element.45.t_rel, bf16[704,704]{1,0:T(8,128)(2,1)S(1)} %get-tuple-element.46.coeff_low), custom_call_target="tpu_custom_call" | custom-call | flops 1141899264 | bytes 5857280 | tf_op jit(solution)/shard_map/image_near/pallas_call | solution.py:252
  41.3 0.9 collective-permute-done.11.ta_ref
  42.2 8.5 %tile_far.1 = (bf16[360,1152]{1,0:T(8,128)(2,1)S(1)}, bf16[360,1152]{1,0:T(8,128)(2,1)S(1)}, f32[360,1152]{1,0:T(8,128)S(1)}, f32[360,1152]{1,0:T(8,128)S(1)}) custom-call(s32[2]{0:T(128)S(1)} %pad_add_fusion.info_ref, f32[2]{0:T(128)S(1)} %pad_maximum_fusion.6.scale_ref, bf16[4,88,1152]{2,1,0:T(8,128)(2,1)S(1)} %collective-permute-done.11.ta_ref, ...), custom_call_target="tpu_custom_call" | custom-call | flops 3425697792 | bytes 11468816 | tf_op jit(solution)/shard_map/tile_far/pallas_call | solution.py:252
  50.6 0.6 collective-permute-done.12.r1_ref
  51.2 2.1 %collective-permute-start.13 = (f32[360,1152]{1,0:T(8,128)S(1)}, f32[360,1152]{1,0:T(8,128)S(1)}, u32[]{:S(2)}, u32[]{:S(2)}) collective-permute-start(f32[360,1152]{1,0:T(8,128)S(1)} %get-tuple-element.53), channel_id=1, source_target_pairs={{0,1},{1,0},{2,3},{3,2},{4,5},{5,4},{6,7},{7,6},{8,9},{9,8},{10,11... | collective-permute-start | bytes 4976648 | tf_op jit(solution)/shard_map/ppermute | solution.py:31
  53.3 1.6 %collective-permute-start.14 = (bf16[360,1152]{1,0:T(8,128)(2,1)S(1)}, bf16[360,1152]{1,0:T(8,128)(2,1)S(1)}, u32[]{:S(2)}, u32[]{:S(2)}) collective-permute-start(bf16[360,1152]{1,0:T(8,128)(2,1)S(1)} %get-tuple-element.59), channel_id=1, source_target_pairs={{0,64},{1,33},{2,66},{3,35},{4,68},{5,37},{6,70},{7,39},{8,72},{9,... | collective-permute-start | bytes 2488328 | tf_op jit(solution)/shard_map/ppermute | solution.py:31
  55.0 0.8 collective-permute-start.15
  55.7 0.7 collective-permute-done.13.other_ref
  56.5 1.0 image_first.1
  57.5 1.3 %collective-permute-start.16 = (bf16[96,1152]{1,0:T(8,128)(2,1)S(1)}, bf16[96,1152]{1,0:T(8,128)(2,1)S(1)}, u32[]{:S(2)}, u32[]{:S(2)}) collective-permute-start(bf16[96,1152]{1,0:T(8,128)(2,1)S(1)} %get-tuple-element.54), channel_id=1, source_target_pairs={{0,4},{1,5},{2,6},{3,7},{4,0},{5,1},{6,2},{7,3},{8,12},{9,13},{10,... | collective-permute-start | bytes 663560 | tf_op jit(solution)/shard_map/ppermute | solution.py:31
  58.8 2.5 %collective-permute-start.17 = (bf16[96,1152]{1,0:T(8,128)(2,1)S(1)}, bf16[96,1152]{1,0:T(8,128)(2,1)S(1)}, u32[]{:S(2)}, u32[]{:S(2)}) collective-permute-start(bf16[96,1152]{1,0:T(8,128)(2,1)S(1)} %get-tuple-element.55), channel_id=1, source_target_pairs={{0,8},{1,9},{2,10},{3,11},{4,12},{5,13},{6,14},{7,15},{8,0},{9,1},... | collective-permute-start | bytes 663560 | tf_op jit(solution)/shard_map/ppermute | solution.py:31
  61.4 0.8 text_near.1.own_ref
  62.2 1.8 %collective-permute-done.16.r1_ref = bf16[96,1152]{1,0:T(8,128)(2,1)S(1)} collective-permute-done((bf16[96,1152]{1,0:T(8,128)(2,1)S(1)}, bf16[96,1152]{1,0:T(8,128)(2,1)S(1)}, u32[]{:S(2)}, u32[]{:S(2)}) %collective-permute-start.16) | collective-permute-done | bytes 221216 | tf_op jit(solution)/shard_map/ppermute | solution.py:31
  64.0 7.0 %collective-permute-done.17.r2_ref = bf16[96,1152]{1,0:T(8,128)(2,1)S(1)} collective-permute-done((bf16[96,1152]{1,0:T(8,128)(2,1)S(1)}, bf16[96,1152]{1,0:T(8,128)(2,1)S(1)}, u32[]{:S(2)}, u32[]{:S(2)}) %collective-permute-start.17) | collective-permute-done | bytes 221216 | tf_op jit(solution)/shard_map/ppermute | solution.py:31
  71.0 2.3 %collective-permute-done.18.r3_ref = bf16[96,1152]{1,0:T(8,128)(2,1)S(1)} collective-permute-done((bf16[96,1152]{1,0:T(8,128)(2,1)S(1)}, bf16[96,1152]{1,0:T(8,128)(2,1)S(1)}, u32[]{:S(2)}, u32[]{:S(2)}) %collective-permute-start.18) | collective-permute-done | bytes 221216 | tf_op jit(solution)/shard_map/ppermute | solution.py:31
  73.2 0.6 image_last.1
  73.9 1.4 %collective-permute-done.15.r3_ref = bf16[360,1152]{1,0:T(8,128)(2,1)S(1)} collective-permute-done((bf16[360,1152]{1,0:T(8,128)(2,1)S(1)}, bf16[360,1152]{1,0:T(8,128)(2,1)S(1)}, u32[]{:S(2)}, u32[]{:S(2)}) %collective-permute-start.15) | collective-permute-done | bytes 829472 | tf_op jit(solution)/shard_map/ppermute | solution.py:31
  75.3 2.6 %text_first.1 = (f32[96,1152]{1,0:T(8,128)S(1)}, bf16[96,1152]{1,0:T(8,128)(2,1)S(1)}, bf16[96,1152]{1,0:T(8,128)(2,1)S(1)}, bf16[96,1152]{1,0:T(8,128)(2,1)S(1)}) custom-call(f32[352,1152]{1,0:T(8,128)S(1)} %text_near.1.own_ref, bf16[360,1152]{1,0:T(8,128)(2,1)S(1)} %collective-permute-done.14.r2_ref, bf16[360,1152]{1,0:T(8,128)(2,1)S(1)} %collective-permute-done.15.r3_ref, ...), custom_call_target="tpu_custom_call" | custom-call | bytes 4423680 | tf_op jit(solution)/shard_map/text_first/pallas_call | solution.py:252
  78.0 0.5 collective-permute-start.19
  78.5 1.9 %collective-permute-start.20 = (bf16[96,1152]{1,0:T(8,128)(2,1)S(1)}, bf16[96,1152]{1,0:T(8,128)(2,1)S(1)}, u32[]{:S(2)}, u32[]{:S(2)}) collective-permute-start(bf16[96,1152]{1,0:T(8,128)(2,1)S(1)} %get-tuple-element.65), channel_id=1, source_target_pairs={{0,32},{1,65},{2,34},{3,67},{4,36},{5,69},{6,38},{7,71},{8,40},{9,... | collective-permute-start | bytes 663560 | tf_op jit(solution)/shard_map/ppermute | solution.py:31
  80.4 1.5 %collective-permute-start.21 = (bf16[96,1152]{1,0:T(8,128)(2,1)S(1)}, bf16[96,1152]{1,0:T(8,128)(2,1)S(1)}, u32[]{:S(2)}, u32[]{:S(2)}) collective-permute-start(bf16[96,1152]{1,0:T(8,128)(2,1)S(1)} %get-tuple-element.66), channel_id=1, source_target_pairs={{0,48},{1,67},{2,50},{3,65},{4,52},{5,71},{6,54},{7,69},{8,56},{9,... | collective-permute-start | bytes 663560 | tf_op jit(solution)/shard_map/ppermute | solution.py:31
  82.1 1.0 %collective-permute-done.19.r1_ref = bf16[96,1152]{1,0:T(8,128)(2,1)S(1)} collective-permute-done((bf16[96,1152]{1,0:T(8,128)(2,1)S(1)}, bf16[96,1152]{1,0:T(8,128)(2,1)S(1)}, u32[]{:S(2)}, u32[]{:S(2)}) %collective-permute-start.19) | collective-permute-done | bytes 221216 | tf_op jit(solution)/shard_map/ppermute | solution.py:31
  83.1 3.3 %collective-permute-done.20.r2_ref = bf16[96,1152]{1,0:T(8,128)(2,1)S(1)} collective-permute-done((bf16[96,1152]{1,0:T(8,128)(2,1)S(1)}, bf16[96,1152]{1,0:T(8,128)(2,1)S(1)}, u32[]{:S(2)}, u32[]{:S(2)}) %collective-permute-start.20) | collective-permute-done | bytes 221216 | tf_op jit(solution)/shard_map/ppermute | solution.py:31
  86.5 2.3 %collective-permute-done.21.r3_ref = bf16[96,1152]{1,0:T(8,128)(2,1)S(1)} collective-permute-done((bf16[96,1152]{1,0:T(8,128)(2,1)S(1)}, bf16[96,1152]{1,0:T(8,128)(2,1)S(1)}, u32[]{:S(2)}, u32[]{:S(2)}) %collective-permute-start.21) | collective-permute-done | bytes 221216 | tf_op jit(solution)/shard_map/ppermute | solution.py:31
  88.8 0.6 text_last.1
  90.1 2.0 %collective-permute-start.23 = (f32[352,288]{0,1:T(8,128)S(1)}, f32[352,288]{0,1:T(8,128)S(1)}, u32[]{:S(2)}, u32[]{:S(2)}) collective-permute-start(f32[352,288]{0,1:T(8,128)S(1)} %copy.7), channel_id=1, source_target_pairs={{0,1},{1,0},{2,3},{3,2},{4,5},{5,4},{6,7},{7,6},{8,9},{9,8},{10,11... | collective-permute-start | bytes 1216520 | tf_op jit(solution)/shard_map/ppermute | solution.py:31
  92.1 1.2 %collective-permute-start.26 = (f32[8,128]{1,0:T(8,128)S(1)}, f32[8,128]{1,0:T(8,128)S(1)}, u32[]{:S(2)}, u32[]{:S(2)}) collective-permute-start(f32[8,128]{1,0:T(8,128)S(1)} %get-tuple-element.73), channel_id=1, source_target_pairs={{0,66},{1,49},{2,64},{3,51},{4,70},{5,53},{6,68},{7,55},{8,74},{9,... | collective-permute-start | bytes 12296 | tf_op jit(solution)/shard_map/ppermute | solution.py:31
  93.4 2.0 %collective-permute-start.24 = (f32[8,128]{1,0:T(8,128)S(1)}, f32[8,128]{1,0:T(8,128)S(1)}, u32[]{:S(2)}, u32[]{:S(2)}) collective-permute-start(f32[8,128]{1,0:T(8,128)S(1)} %get-tuple-element.73), channel_id=1, source_target_pairs={{0,2},{1,17},{2,0},{3,19},{4,6},{5,21},{6,4},{7,23},{8,10},{9,25},... | collective-permute-start | bytes 12296 | tf_op jit(solution)/shard_map/ppermute | solution.py:31
  95.6 1.7 %join.1 = (f32[288,352]{1,0:T(8,128)}, f32[288,352]{1,0:T(8,128)}) custom-call(s32[2]{0:T(128)S(1)} %pad_add_fusion.info_ref, f32[352,288]{1,0:T(8,128)S(1)} %get-tuple-element.80.own_ref, f32[352,288]{1,0:T(8,128)S(1)} %copy.8.got_ref), custom_call_target="tpu_custom_call" | custom-call | bytes 1622024 | tf_op jit(solution)/shard_map/join/pallas_call | solution.py:252
  (38 shorter events, 4.0 us)
Async XLA Ops:
  0.7 0.9 copy-start
  1.6 0.9 copy-start.1
  3.4 2.7 %collective-permute-start = (bf16[352,288]{1,0:T(8,128)(2,1)S(1)}, bf16[352,288]{1,0:T(8,128)(2,1)S(1)}, u32[]{:S(2)}, u32[]{:S(2)}) collective-permute-start(bf16[352,288]{1,0:T(8,128)(2,1)S(1)} %get-tuple-element.41), channel_id=1, source_target_pairs={{0,1},{1,0},{2,3},{3,2},{4,5},{5,4},{6,7},{7,6},{8,9},{9,8},{10,11... | collective-permute-start | bytes 608264 | tf_op jit(solution)/shard_map/ppermute | solution.py:31
  6.3 5.8 %collective-permute-start.6 = (bf16[88,576]{1,0:T(8,128)(2,1)S(1)}, bf16[88,576]{1,0:T(8,128)(2,1)S(1)}, u32[]{:S(2)}, u32[]{:S(2)}) collective-permute-start(bf16[88,576]{1,0:T(8,128)(2,1)S(1)} %get-tuple-element.83), channel_id=1, source_target_pairs={{0,2},{1,3},{2,0},{3,1},{4,6},{5,7},{6,4},{7,5},{8,10},{9,11},{10,... | collective-permute-start | bytes 304136 | tf_op jit(solution)/shard_map/ppermute | solution.py:31
  8.4 8.7 %collective-permute-start.2 = (bf16[88,1152]{1,0:T(8,128)(2,1)S(1)}, bf16[88,1152]{1,0:T(8,128)(2,1)S(1)}, u32[]{:S(2)}, u32[]{:S(2)}) collective-permute-start(bf16[88,1152]{1,0:T(8,128)(2,1)S(1)} %pad_maximum_fusion.3), channel_id=1, source_target_pairs={{0,32},{1,65},{2,34},{3,67},{4,36},{5,69},{6,38},{7,71},{8,40},{9,... | collective-permute-start | bytes 608264 | tf_op jit(solution)/shard_map/ppermute | solution.py:31
  11.7 6.6 %collective-permute-start.1 = (bf16[88,1152]{1,0:T(8,128)(2,1)S(1)}, bf16[88,1152]{1,0:T(8,128)(2,1)S(1)}, u32[]{:S(2)}, u32[]{:S(2)}) collective-permute-start(bf16[88,1152]{1,0:T(8,128)(2,1)S(1)} %pad_maximum_fusion.3), channel_id=1, source_target_pairs={{0,16},{1,3},{2,18},{3,1},{4,20},{5,7},{6,22},{7,5},{8,24},{9,11},... | collective-permute-start | bytes 608264 | tf_op jit(solution)/shard_map/ppermute | solution.py:31
  11.7 7.6 %collective-permute-start.3 = (bf16[88,1152]{1,0:T(8,128)(2,1)S(1)}, bf16[88,1152]{1,0:T(8,128)(2,1)S(1)}, u32[]{:S(2)}, u32[]{:S(2)}) collective-permute-start(bf16[88,1152]{1,0:T(8,128)(2,1)S(1)} %pad_maximum_fusion.3), channel_id=1, source_target_pairs={{0,48},{1,67},{2,50},{3,65},{4,52},{5,71},{6,54},{7,69},{8,56},{9,... | collective-permute-start | bytes 608264 | tf_op jit(solution)/shard_map/ppermute | solution.py:31
  12.2 11.1 %collective-permute-start.9 = (bf16[88,1152]{1,0:T(8,128)(2,1)S(1)}, bf16[88,1152]{1,0:T(8,128)(2,1)S(1)}, u32[]{:S(2)}, u32[]{:S(2)}) collective-permute-start(bf16[88,1152]{1,0:T(8,128)(2,1)S(1)} %pad_maximum_fusion.4), channel_id=1, source_target_pairs={{0,12},{1,13},{2,14},{3,15},{4,8},{5,9},{6,10},{7,11},{8,4},{9,5},... | collective-permute-start | bytes 608264 | tf_op jit(solution)/shard_map/ppermute | solution.py:31
  14.8 8.5 %collective-permute-start.8 = (bf16[88,1152]{1,0:T(8,128)(2,1)S(1)}, bf16[88,1152]{1,0:T(8,128)(2,1)S(1)}, u32[]{:S(2)}, u32[]{:S(2)}) collective-permute-start(bf16[88,1152]{1,0:T(8,128)(2,1)S(1)} %pad_maximum_fusion.4), channel_id=1, source_target_pairs={{0,8},{1,9},{2,10},{3,11},{4,12},{5,13},{6,14},{7,15},{8,0},{9,1},... | collective-permute-start | bytes 608264 | tf_op jit(solution)/shard_map/ppermute | solution.py:31
  17.1 7.0 %collective-permute-start.7 = (bf16[88,1152]{1,0:T(8,128)(2,1)S(1)}, bf16[88,1152]{1,0:T(8,128)(2,1)S(1)}, u32[]{:S(2)}, u32[]{:S(2)}) collective-permute-start(bf16[88,1152]{1,0:T(8,128)(2,1)S(1)} %pad_maximum_fusion.4), channel_id=1, source_target_pairs={{0,4},{1,5},{2,6},{3,7},{4,0},{5,1},{6,2},{7,3},{8,12},{9,13},{10,... | collective-permute-start | bytes 608264 | tf_op jit(solution)/shard_map/ppermute | solution.py:31
  19.5 12.8 %collective-permute-start.5 = (bf16[4,88,1152]{2,1,0:T(8,128)(2,1)S(1)}, bf16[4,88,1152]{2,1,0:T(8,128)(2,1)S(1)}, u32[]{:S(2)}, u32[]{:S(2)}) collective-permute-start(bf16[4,88,1152]{2,1,0:T(8,128)(2,1)S(1)} %pad_maximum_fusion.1.ta_ref), channel_id=1, source_target_pairs={{0,66},{1,49},{2,64},{3,51},{4,70},{5,53},{6,68},{7,55},{8,74},{9,... | collective-permute-start | bytes 2433032 | tf_op jit(solution)/shard_map/ppermute | solution.py:31
  22.3 11.4 %collective-permute-start.4 = (bf16[4,88,1152]{2,1,0:T(8,128)(2,1)S(1)}, bf16[4,88,1152]{2,1,0:T(8,128)(2,1)S(1)}, u32[]{:S(2)}, u32[]{:S(2)}) collective-permute-start(bf16[4,88,1152]{2,1,0:T(8,128)(2,1)S(1)} %pad_maximum_fusion.1.ta_ref), channel_id=1, source_target_pairs={{0,2},{1,17},{2,0},{3,19},{4,6},{5,21},{6,4},{7,23},{8,10},{9,25},... | collective-permute-start | bytes 2433032 | tf_op jit(solution)/shard_map/ppermute | solution.py:31
  24.2 9.5 %collective-permute-start.10 = (bf16[352,1152]{1,0:T(8,128)(2,1)S(1)}, bf16[352,1152]{1,0:T(8,128)(2,1)S(1)}, u32[]{:S(2)}, u32[]{:S(2)}) collective-permute-start(bf16[352,1152]{1,0:T(8,128)(2,1)S(1)} %pad_maximum_fusion.2.im0_ref), channel_id=1, source_target_pairs={{0,1},{1,0},{2,3},{3,2},{4,5},{5,4},{6,7},{7,6},{8,9},{9,8},{10,11... | collective-permute-start | bytes 2433032 | tf_op jit(solution)/shard_map/ppermute | solution.py:31
  27.4 14.8 %collective-permute-start.11 = (bf16[4,88,1152]{2,1,0:T(8,128)(2,1)S(1)}, bf16[4,88,1152]{2,1,0:T(8,128)(2,1)S(1)}, u32[]{:S(2)}, u32[]{:S(2)}) collective-permute-start(bf16[4,88,1152]{2,1,0:T(8,128)(2,1)S(1)} %pad_maximum_fusion.1.ta_ref), channel_id=1, source_target_pairs={{0,64},{1,33},{2,66},{3,35},{4,68},{5,37},{6,70},{7,39},{8,72},{9,... | collective-permute-start | bytes 2433032 | tf_op jit(solution)/shard_map/ppermute | solution.py:31
  39.4 11.9 %collective-permute-start.12 = (bf16[360,1152]{1,0:T(8,128)(2,1)S(1)}, bf16[360,1152]{1,0:T(8,128)(2,1)S(1)}, u32[]{:S(2)}, u32[]{:S(2)}) collective-permute-start(bf16[360,1152]{1,0:T(8,128)(2,1)S(1)} %get-tuple-element.52), channel_id=1, source_target_pairs={{0,2},{1,17},{2,0},{3,19},{4,6},{5,21},{6,4},{7,23},{8,10},{9,25},... | collective-permute-start | bytes 2488328 | tf_op jit(solution)/shard_map/ppermute | solution.py:31
  51.2 5.2 %collective-permute-start.13 = (f32[360,1152]{1,0:T(8,128)S(1)}, f32[360,1152]{1,0:T(8,128)S(1)}, u32[]{:S(2)}, u32[]{:S(2)}) collective-permute-start(f32[360,1152]{1,0:T(8,128)S(1)} %get-tuple-element.53), channel_id=1, source_target_pairs={{0,1},{1,0},{2,3},{3,2},{4,5},{5,4},{6,7},{7,6},{8,9},{9,8},{10,11... | collective-permute-start | bytes 4976648 | tf_op jit(solution)/shard_map/ppermute | solution.py:31
  53.3 20.6 %collective-permute-start.14 = (bf16[360,1152]{1,0:T(8,128)(2,1)S(1)}, bf16[360,1152]{1,0:T(8,128)(2,1)S(1)}, u32[]{:S(2)}, u32[]{:S(2)}) collective-permute-start(bf16[360,1152]{1,0:T(8,128)(2,1)S(1)} %get-tuple-element.59), channel_id=1, source_target_pairs={{0,64},{1,33},{2,66},{3,35},{4,68},{5,37},{6,70},{7,39},{8,72},{9,... | collective-permute-start | bytes 2488328 | tf_op jit(solution)/shard_map/ppermute | solution.py:31
  55.0 20.3 %collective-permute-start.15 = (bf16[360,1152]{1,0:T(8,128)(2,1)S(1)}, bf16[360,1152]{1,0:T(8,128)(2,1)S(1)}, u32[]{:S(2)}, u32[]{:S(2)}) collective-permute-start(bf16[360,1152]{1,0:T(8,128)(2,1)S(1)} %get-tuple-element.60), channel_id=1, source_target_pairs={{0,66},{1,49},{2,64},{3,51},{4,70},{5,53},{6,68},{7,55},{8,74},{9,... | collective-permute-start | bytes 2488328 | tf_op jit(solution)/shard_map/ppermute | solution.py:31
  57.5 6.5 %collective-permute-start.16 = (bf16[96,1152]{1,0:T(8,128)(2,1)S(1)}, bf16[96,1152]{1,0:T(8,128)(2,1)S(1)}, u32[]{:S(2)}, u32[]{:S(2)}) collective-permute-start(bf16[96,1152]{1,0:T(8,128)(2,1)S(1)} %get-tuple-element.54), channel_id=1, source_target_pairs={{0,4},{1,5},{2,6},{3,7},{4,0},{5,1},{6,2},{7,3},{8,12},{9,13},{10,... | collective-permute-start | bytes 663560 | tf_op jit(solution)/shard_map/ppermute | solution.py:31
  58.8 12.2 %collective-permute-start.17 = (bf16[96,1152]{1,0:T(8,128)(2,1)S(1)}, bf16[96,1152]{1,0:T(8,128)(2,1)S(1)}, u32[]{:S(2)}, u32[]{:S(2)}) collective-permute-start(bf16[96,1152]{1,0:T(8,128)(2,1)S(1)} %get-tuple-element.55), channel_id=1, source_target_pairs={{0,8},{1,9},{2,10},{3,11},{4,12},{5,13},{6,14},{7,15},{8,0},{9,1},... | collective-permute-start | bytes 663560 | tf_op jit(solution)/shard_map/ppermute | solution.py:31
  61.2 12.0 %collective-permute-start.18 = (bf16[96,1152]{1,0:T(8,128)(2,1)S(1)}, bf16[96,1152]{1,0:T(8,128)(2,1)S(1)}, u32[]{:S(2)}, u32[]{:S(2)}) collective-permute-start(bf16[96,1152]{1,0:T(8,128)(2,1)S(1)} %get-tuple-element.56), channel_id=1, source_target_pairs={{0,12},{1,13},{2,14},{3,15},{4,8},{5,9},{6,10},{7,11},{8,4},{9,5},... | collective-permute-start | bytes 663560 | tf_op jit(solution)/shard_map/ppermute | solution.py:31
  78.0 5.2 %collective-permute-start.19 = (bf16[96,1152]{1,0:T(8,128)(2,1)S(1)}, bf16[96,1152]{1,0:T(8,128)(2,1)S(1)}, u32[]{:S(2)}, u32[]{:S(2)}) collective-permute-start(bf16[96,1152]{1,0:T(8,128)(2,1)S(1)} %get-tuple-element.64), channel_id=1, source_target_pairs={{0,16},{1,3},{2,18},{3,1},{4,20},{5,7},{6,22},{7,5},{8,24},{9,11},... | collective-permute-start | bytes 663560 | tf_op jit(solution)/shard_map/ppermute | solution.py:31
  78.5 8.0 %collective-permute-start.20 = (bf16[96,1152]{1,0:T(8,128)(2,1)S(1)}, bf16[96,1152]{1,0:T(8,128)(2,1)S(1)}, u32[]{:S(2)}, u32[]{:S(2)}) collective-permute-start(bf16[96,1152]{1,0:T(8,128)(2,1)S(1)} %get-tuple-element.65), channel_id=1, source_target_pairs={{0,32},{1,65},{2,34},{3,67},{4,36},{5,69},{6,38},{7,71},{8,40},{9,... | collective-permute-start | bytes 663560 | tf_op jit(solution)/shard_map/ppermute | solution.py:31
  80.4 8.4 %collective-permute-start.21 = (bf16[96,1152]{1,0:T(8,128)(2,1)S(1)}, bf16[96,1152]{1,0:T(8,128)(2,1)S(1)}, u32[]{:S(2)}, u32[]{:S(2)}) collective-permute-start(bf16[96,1152]{1,0:T(8,128)(2,1)S(1)} %get-tuple-element.66), channel_id=1, source_target_pairs={{0,48},{1,67},{2,50},{3,65},{4,52},{5,71},{6,54},{7,69},{8,56},{9,... | collective-permute-start | bytes 663560 | tf_op jit(solution)/shard_map/ppermute | solution.py:31
  82.0 7.4 %collective-permute-start.22 = (f32[88,576]{1,0:T(8,128)S(1)}, f32[88,576]{1,0:T(8,128)S(1)}, u32[]{:S(2)}, u32[]{:S(2)}) collective-permute-start(f32[88,576]{1,0:T(8,128)S(1)} %slice.40), channel_id=1, source_target_pairs={{0,2},{1,3},{2,0},{3,1},{4,6},{5,7},{6,4},{7,5},{8,10},{9,11},{10,... | collective-permute-start | bytes 608264 | tf_op jit(solution)/shard_map/ppermute | solution.py:31
  90.1 5.3 %collective-permute-start.23 = (f32[352,288]{0,1:T(8,128)S(1)}, f32[352,288]{0,1:T(8,128)S(1)}, u32[]{:S(2)}, u32[]{:S(2)}) collective-permute-start(f32[352,288]{0,1:T(8,128)S(1)} %copy.7), channel_id=1, source_target_pairs={{0,1},{1,0},{2,3},{3,2},{4,5},{5,4},{6,7},{7,6},{8,9},{9,8},{10,11... | collective-permute-start | bytes 1216520 | tf_op jit(solution)/shard_map/ppermute | solution.py:31
  92.1 5.2 %collective-permute-start.26 = (f32[8,128]{1,0:T(8,128)S(1)}, f32[8,128]{1,0:T(8,128)S(1)}, u32[]{:S(2)}, u32[]{:S(2)}) collective-permute-start(f32[8,128]{1,0:T(8,128)S(1)} %get-tuple-element.73), channel_id=1, source_target_pairs={{0,66},{1,49},{2,64},{3,51},{4,70},{5,53},{6,68},{7,55},{8,74},{9,... | collective-permute-start | bytes 12296 | tf_op jit(solution)/shard_map/ppermute | solution.py:31
  93.3 4.0 %collective-permute-start.25 = (f32[8,128]{1,0:T(8,128)S(1)}, f32[8,128]{1,0:T(8,128)S(1)}, u32[]{:S(2)}, u32[]{:S(2)}) collective-permute-start(f32[8,128]{1,0:T(8,128)S(1)} %get-tuple-element.73), channel_id=1, source_target_pairs={{0,64},{1,33},{2,66},{3,35},{4,68},{5,37},{6,70},{7,39},{8,72},{9,... | collective-permute-start | bytes 12296 | tf_op jit(solution)/shard_map/ppermute | solution.py:31
  93.4 3.9 %collective-permute-start.24 = (f32[8,128]{1,0:T(8,128)S(1)}, f32[8,128]{1,0:T(8,128)S(1)}, u32[]{:S(2)}, u32[]{:S(2)}) collective-permute-start(f32[8,128]{1,0:T(8,128)S(1)} %get-tuple-element.73), channel_id=1, source_target_pairs={{0,2},{1,17},{2,0},{3,19},{4,6},{5,21},{6,4},{7,23},{8,10},{9,25},... | collective-permute-start | bytes 12296 | tf_op jit(solution)/shard_map/ppermute | solution.py:31

commit v17 on v16

--- a/solution.py
+++ b/solution.py
@@ -109,11 +109,16 @@
         send_ref[at : at + step, :] = jnp.where(on0, second, first).astype(BF)
 
 
-def join_kernel(rows, info_ref, own_ref, got_ref, texts_ref, images_ref):
+def join_kernel(rows, info_ref, own_ref, got_ref, texts_ref, images_ref, whole, sems):
     on0, step = info_ref[0] == 0, 2 * rows
-    for at, ref in ((0, texts_ref), (step, images_ref)):
-        own, got = own_ref[at : at + step, :], got_ref[at : at + step, :]
-        ref[...] = jnp.concatenate([jnp.where(on0, own, got), jnp.where(on0, got, own)], axis=0).T
+    copies = []
+    for k, ref in enumerate((texts_ref, images_ref)):
+        own, got = own_ref[k * step : (k + 1) * step, :], got_ref[k * step : (k + 1) * step, :]
+        whole[k] = jnp.concatenate([jnp.where(on0, own, got), jnp.where(on0, got, own)], axis=0).T
+        copies.append(pltpu.make_async_copy(whole.at[k], ref, sems.at[k]))
+        copies[k].start()
+    for copy in copies:
+        copy.wait()
 
 
 def near_kernel(
@@ -206,7 +211,7 @@
         total[at, :] = own_ref[at, :] + decode(r2_ref[at, :], tops[0]) + decode(r3_ref[at, :], tops[1])
         return carry
 
-    lax.fori_loop(0, 4 * rows // 32, add, 0)
+    lax.fori_loop(0, 4 * rows // 32, add, 0, unroll=2)
     out_ref[...] = jnp.concatenate([total[0:rows, :], sums_ref[...]], axis=0)
     for i, m_ref in enumerate((m1_ref, m2_ref, m3_ref)):
         m_ref[...] = message([total[(i + 1) * rows : (i + 2) * rows, :]], feats, split3(sums_ref[0:1, :]))
@@ -219,6 +224,7 @@
 
 
 VMEM = pl.BlockSpec(memory_space=pltpu.VMEM)
+HBM = pl.BlockSpec(memory_space=pl.ANY)
 SMEM = pl.BlockSpec(memory_space=pltpu.SMEM)
 
 
@@ -248,12 +254,12 @@
     def bf16(*shape):
         return jax.ShapeDtypeStruct(shape, BF)
 
-    def call(kernel, name, out_shape, *args, scalars=0, scratch=(), mib=20, products=0):
+    def call(kernel, name, out_shape, *args, scalars=0, scratch=(), mib=20, products=0, out=VMEM):
         return pl.pallas_call(
             kernel,
             out_shape=out_shape,
             in_specs=[SMEM] * scalars + [VMEM] * (len(args) - scalars),
-            out_specs=[VMEM] * len(out_shape),
+            out_specs=[out] * len(out_shape),
             scratch_shapes=scratch,
             compiler_params=grant(mib),
             cost_estimate=pl.CostEstimate(
@@ -327,7 +333,8 @@
     sums = after(sums, other)
     other = swap(other, CORE)
     text_grad, image_grad = call(
-        functools.partial(join_kernel, rows), "join", [f32(width, height)] * 2, info, mine, other, scalars=1
+        functools.partial(join_kernel, rows), "join", [f32(width, height)] * 2, info, mine, other, scalars=1,
+        out=HBM, scratch=[pltpu.VMEM((2, width, height), F32), pltpu.SemaphoreType.DMA((2,))],
     )
     s1, s2, s3 = (after(swap(sums, z_mask(k), y_mask(k)), text_grad, image_grad) for k in (1, 2, 3))
     sums = (sums + s1) + (s2 + s3)

time: 98.1 us -> 98.2 us (level)
  no operation moved by 1% of the time
where the time goes in v17:
time: 98.2 us; the launch traced here: 97.9 us
  starting transfers between devices  37 us (38%)
  waiting for transfers between devices  30.5 us (31%)
  Pallas kernels  23.9 us (24%)
  local copies, waits for them, and re-layouts  2.92 us (3%)
  between operations  2.14 us (2%)
  other arithmetic  1.34 us (1%)
    ppermute x27, starting transfers between devices, swap(): lax.ppermute(array, AXES, [(i, i ^ (mask1 if i & 1 else mask0)) for i in...  37 us
    ppermute x27, waiting for transfers between devices, swap(): lax.ppermute(array, AXES, [(i, i ^ (mask1 if i & 1 else mask0)) for i in...  30.5 us
    pallas_call x10, Pallas kernels, call(): pl.pallas_call(kernel, out_shape=out_shape, in_specs=[SMEM] * scalars + [...  23.9 us
  transfers between devices with their start and end apart: 27, of which 17 were waited for; matrix products, arithmetic and copies ran while one was open for 1% of the time, Pallas kernels for 21%

profile of v17, /device:TPU:1, one launch (start us, length us, event | category | flops | bytes accessed | tf_op | source)
XLA Modules:
  0.0 97.9 jit_solution(8224767928642303646)
XLA Ops:
  0.7 0.9 copy-done
  1.7 0.9 copy-done.1
  2.6 0.8 split.1
  3.4 1.5 %collective-permute-start = (bf16[352,288]{1,0:T(8,128)(2,1)S(1)}, bf16[352,288]{1,0:T(8,128)(2,1)S(1)}, u32[]{:S(2)}, u32[]{:S(2)}) collective-permute-start(bf16[352,288]{1,0:T(8,128)(2,1)S(1)} %get-tuple-element.41), channel_id=1, source_target_pairs={{0,1},{1,0},{2,3},{3,2},{4,5},{5,4},{6,7},{7,6},{8,9},{9,8},{10,11... | collective-permute-start | bytes 608264 | tf_op jit(solution)/shard_map/ppermute | solution.py:31
  4.9 1.2 %collective-permute-done = bf16[352,288]{1,0:T(8,128)(2,1)S(1)} collective-permute-done((bf16[352,288]{1,0:T(8,128)(2,1)S(1)}, bf16[352,288]{1,0:T(8,128)(2,1)S(1)}, u32[]{:S(2)}, u32[]{:S(2)}) %collective-permute-start) | collective-permute-done | bytes 202784 | tf_op jit(solution)/shard_map/ppermute | solution.py:31
  6.3 1.8 %collective-permute-start.6 = (bf16[88,576]{1,0:T(8,128)(2,1)S(1)}, bf16[88,576]{1,0:T(8,128)(2,1)S(1)}, u32[]{:S(2)}, u32[]{:S(2)}) collective-permute-start(bf16[88,576]{1,0:T(8,128)(2,1)S(1)} %get-tuple-element.83), channel_id=1, source_target_pairs={{0,2},{1,3},{2,0},{3,1},{4,6},{5,7},{6,4},{7,5},{8,10},{9,11},{10,... | collective-permute-start | bytes 304136 | tf_op jit(solution)/shard_map/ppermute | solution.py:31
  8.4 3.4 %collective-permute-start.2 = (bf16[88,1152]{1,0:T(8,128)(2,1)S(1)}, bf16[88,1152]{1,0:T(8,128)(2,1)S(1)}, u32[]{:S(2)}, u32[]{:S(2)}) collective-permute-start(bf16[88,1152]{1,0:T(8,128)(2,1)S(1)} %pad_maximum_fusion.3), channel_id=1, source_target_pairs={{0,32},{1,65},{2,34},{3,67},{4,36},{5,69},{6,38},{7,71},{8,40},{9,... | collective-permute-start | bytes 608264 | tf_op jit(solution)/shard_map/ppermute | solution.py:31
  12.2 2.6 %collective-permute-start.9 = (bf16[88,1152]{1,0:T(8,128)(2,1)S(1)}, bf16[88,1152]{1,0:T(8,128)(2,1)S(1)}, u32[]{:S(2)}, u32[]{:S(2)}) collective-permute-start(bf16[88,1152]{1,0:T(8,128)(2,1)S(1)} %pad_maximum_fusion.4), channel_id=1, source_target_pairs={{0,12},{1,13},{2,14},{3,15},{4,8},{5,9},{6,10},{7,11},{8,4},{9,5},... | collective-permute-start | bytes 608264 | tf_op jit(solution)/shard_map/ppermute | solution.py:31
  15.3 1.8 %collective-permute-done.2 = bf16[88,1152]{1,0:T(8,128)(2,1)S(1)} collective-permute-done((bf16[88,1152]{1,0:T(8,128)(2,1)S(1)}, bf16[88,1152]{1,0:T(8,128)(2,1)S(1)}, u32[]{:S(2)}, u32[]{:S(2)}) %collective-permute-start.2) | collective-permute-done | bytes 202784 | tf_op jit(solution)/shard_map/ppermute | solution.py:31
  17.1 1.2 %collective-permute-start.7 = (bf16[88,1152]{1,0:T(8,128)(2,1)S(1)}, bf16[88,1152]{1,0:T(8,128)(2,1)S(1)}, u32[]{:S(2)}, u32[]{:S(2)}) collective-permute-start(bf16[88,1152]{1,0:T(8,128)(2,1)S(1)} %pad_maximum_fusion.4), channel_id=1, source_target_pairs={{0,4},{1,5},{2,6},{3,7},{4,0},{5,1},{6,2},{7,3},{8,12},{9,13},{10,... | collective-permute-start | bytes 608264 | tf_op jit(solution)/shard_map/ppermute | solution.py:31
  18.3 1.0 %collective-permute-done.3 = bf16[88,1152]{1,0:T(8,128)(2,1)S(1)} collective-permute-done((bf16[88,1152]{1,0:T(8,128)(2,1)S(1)}, bf16[88,1152]{1,0:T(8,128)(2,1)S(1)}, u32[]{:S(2)}, u32[]{:S(2)}) %collective-permute-start.3) | collective-permute-done | bytes 202784 | tf_op jit(solution)/shard_map/ppermute | solution.py:31
  19.5 2.8 %collective-permute-start.5 = (bf16[4,88,1152]{2,1,0:T(8,128)(2,1)S(1)}, bf16[4,88,1152]{2,1,0:T(8,128)(2,1)S(1)}, u32[]{:S(2)}, u32[]{:S(2)}) collective-permute-start(bf16[4,88,1152]{2,1,0:T(8,128)(2,1)S(1)} %pad_maximum_fusion.1.ta_ref), channel_id=1, source_target_pairs={{0,66},{1,49},{2,64},{3,51},{4,70},{5,53},{6,68},{7,55},{8,74},{9,... | collective-permute-start | bytes 2433032 | tf_op jit(solution)/shard_map/ppermute | solution.py:31
  22.3 1.1 %collective-permute-done.9 = bf16[88,1152]{1,0:T(8,128)(2,1)S(1)} collective-permute-done((bf16[88,1152]{1,0:T(8,128)(2,1)S(1)}, bf16[88,1152]{1,0:T(8,128)(2,1)S(1)}, u32[]{:S(2)}, u32[]{:S(2)}) %collective-permute-start.9) | collective-permute-done | bytes 202784 | tf_op jit(solution)/shard_map/ppermute | solution.py:31
  23.3 0.8 collective-permute-done.7
  24.2 1.9 %collective-permute-start.10 = (bf16[352,1152]{1,0:T(8,128)(2,1)S(1)}, bf16[352,1152]{1,0:T(8,128)(2,1)S(1)}, u32[]{:S(2)}, u32[]{:S(2)}) collective-permute-start(bf16[352,1152]{1,0:T(8,128)(2,1)S(1)} %pad_maximum_fusion.2.im0_ref), channel_id=1, source_target_pairs={{0,1},{1,0},{2,3},{3,2},{4,5},{5,4},{6,7},{7,6},{8,9},{9,8},{10,11... | collective-permute-start | bytes 2433032 | tf_op jit(solution)/shard_map/ppermute | solution.py:31
  27.4 3.0 %collective-permute-start.11 = (bf16[4,88,1152]{2,1,0:T(8,128)(2,1)S(1)}, bf16[4,88,1152]{2,1,0:T(8,128)(2,1)S(1)}, u32[]{:S(2)}, u32[]{:S(2)}) collective-permute-start(bf16[4,88,1152]{2,1,0:T(8,128)(2,1)S(1)} %pad_maximum_fusion.1.ta_ref), channel_id=1, source_target_pairs={{0,64},{1,33},{2,66},{3,35},{4,68},{5,37},{6,70},{7,39},{8,72},{9,... | collective-permute-start | bytes 2433032 | tf_op jit(solution)/shard_map/ppermute | solution.py:31
  30.4 1.8 %collective-permute-done.5.tb_ref = bf16[4,88,1152]{2,1,0:T(8,128)(2,1)S(1)} collective-permute-done((bf16[4,88,1152]{2,1,0:T(8,128)(2,1)S(1)}, bf16[4,88,1152]{2,1,0:T(8,128)(2,1)S(1)}, u32[]{:S(2)}, u32[]{:S(2)}) %collective-permute-start.5) | collective-permute-done | bytes 811040 | tf_op jit(solution)/shard_map/ppermute | solution.py:31
  32.2 1.5 %collective-permute-done.4.tb_ref = bf16[4,88,1152]{2,1,0:T(8,128)(2,1)S(1)} collective-permute-done((bf16[4,88,1152]{2,1,0:T(8,128)(2,1)S(1)}, bf16[4,88,1152]{2,1,0:T(8,128)(2,1)S(1)}, u32[]{:S(2)}, u32[]{:S(2)}) %collective-permute-start.4) | collective-permute-done | bytes 811040 | tf_op jit(solution)/shard_map/ppermute | solution.py:31
  33.7 5.7 %tile_near.1 = (f32[2,4,88,1152]{3,2,1,0:T(8,128)S(1)}, bf16[360,1152]{1,0:T(8,128)(2,1)S(1)}, bf16[704,1152]{1,0:T(8,128)(2,1)S(1)}, bf16[704,704]{1,0:T(8,128)(2,1)S(1)}, f32[8,128]{1,0:T(8,128)S(1)}) custom-call(s32[2]{0:T(128)S(1)} %pad_add_fusion.info_ref, f32[2]{0:T(128)S(1)} %pad_maximum_fusion.6.scale_ref, ...), custom_call_target="tpu_custom_call" | custom-call | flops 2283798528 | bytes 9934864 | tf_op jit(solution)/shard_map/tile_near/pallas_call | solution.py:258
  39.7 1.6 %image_near.1.before_ref = f32[704,1152]{1,0:T(8,128)S(1)} custom-call(bf16[704,1152]{1,0:T(8,128)(2,1)S(1)} %get-tuple-element.45.t_rel, bf16[704,704]{1,0:T(8,128)(2,1)S(1)} %get-tuple-element.46.coeff_low), custom_call_target="tpu_custom_call" | custom-call | flops 1141899264 | bytes 5857280 | tf_op jit(solution)/shard_map/image_near/pallas_call | solution.py:258
  41.3 0.9 collective-permute-done.11.ta_ref
  42.2 8.5 %tile_far.1 = (bf16[360,1152]{1,0:T(8,128)(2,1)S(1)}, bf16[360,1152]{1,0:T(8,128)(2,1)S(1)}, f32[360,1152]{1,0:T(8,128)S(1)}, f32[360,1152]{1,0:T(8,128)S(1)}) custom-call(s32[2]{0:T(128)S(1)} %pad_add_fusion.info_ref, f32[2]{0:T(128)S(1)} %pad_maximum_fusion.6.scale_ref, bf16[4,88,1152]{2,1,0:T(8,128)(2,1)S(1)} %collective-permute-done.11.ta_ref, ...), custom_call_target="tpu_custom_call" | custom-call | flops 3425697792 | bytes 11468816 | tf_op jit(solution)/shard_map/tile_far/pallas_call | solution.py:258
  50.6 0.6 collective-permute-done.12.r1_ref
  51.2 2.1 %collective-permute-start.13 = (f32[360,1152]{1,0:T(8,128)S(1)}, f32[360,1152]{1,0:T(8,128)S(1)}, u32[]{:S(2)}, u32[]{:S(2)}) collective-permute-start(f32[360,1152]{1,0:T(8,128)S(1)} %get-tuple-element.53), channel_id=1, source_target_pairs={{0,1},{1,0},{2,3},{3,2},{4,5},{5,4},{6,7},{7,6},{8,9},{9,8},{10,11... | collective-permute-start | bytes 4976648 | tf_op jit(solution)/shard_map/ppermute | solution.py:31
  53.3 1.6 %collective-permute-start.14 = (bf16[360,1152]{1,0:T(8,128)(2,1)S(1)}, bf16[360,1152]{1,0:T(8,128)(2,1)S(1)}, u32[]{:S(2)}, u32[]{:S(2)}) collective-permute-start(bf16[360,1152]{1,0:T(8,128)(2,1)S(1)} %get-tuple-element.59), channel_id=1, source_target_pairs={{0,64},{1,33},{2,66},{3,35},{4,68},{5,37},{6,70},{7,39},{8,72},{9,... | collective-permute-start | bytes 2488328 | tf_op jit(solution)/shard_map/ppermute | solution.py:31
  55.0 0.8 collective-permute-start.15
  55.7 0.7 collective-permute-done.13.other_ref
  56.5 1.0 image_first.1
  57.5 1.3 %collective-permute-start.16 = (bf16[96,1152]{1,0:T(8,128)(2,1)S(1)}, bf16[96,1152]{1,0:T(8,128)(2,1)S(1)}, u32[]{:S(2)}, u32[]{:S(2)}) collective-permute-start(bf16[96,1152]{1,0:T(8,128)(2,1)S(1)} %get-tuple-element.54), channel_id=1, source_target_pairs={{0,4},{1,5},{2,6},{3,7},{4,0},{5,1},{6,2},{7,3},{8,12},{9,13},{10,... | collective-permute-start | bytes 663560 | tf_op jit(solution)/shard_map/ppermute | solution.py:31
  58.8 2.5 %collective-permute-start.17 = (bf16[96,1152]{1,0:T(8,128)(2,1)S(1)}, bf16[96,1152]{1,0:T(8,128)(2,1)S(1)}, u32[]{:S(2)}, u32[]{:S(2)}) collective-permute-start(bf16[96,1152]{1,0:T(8,128)(2,1)S(1)} %get-tuple-element.55), channel_id=1, source_target_pairs={{0,8},{1,9},{2,10},{3,11},{4,12},{5,13},{6,14},{7,15},{8,0},{9,1},... | collective-permute-start | bytes 663560 | tf_op jit(solution)/shard_map/ppermute | solution.py:31
  61.4 0.8 text_near.1.own_ref
  62.2 1.8 %collective-permute-done.16.r1_ref = bf16[96,1152]{1,0:T(8,128)(2,1)S(1)} collective-permute-done((bf16[96,1152]{1,0:T(8,128)(2,1)S(1)}, bf16[96,1152]{1,0:T(8,128)(2,1)S(1)}, u32[]{:S(2)}, u32[]{:S(2)}) %collective-permute-start.16) | collective-permute-done | bytes 221216 | tf_op jit(solution)/shard_map/ppermute | solution.py:31
  64.0 7.0 %collective-permute-done.17.r2_ref = bf16[96,1152]{1,0:T(8,128)(2,1)S(1)} collective-permute-done((bf16[96,1152]{1,0:T(8,128)(2,1)S(1)}, bf16[96,1152]{1,0:T(8,128)(2,1)S(1)}, u32[]{:S(2)}, u32[]{:S(2)}) %collective-permute-start.17) | collective-permute-done | bytes 221216 | tf_op jit(solution)/shard_map/ppermute | solution.py:31
  71.0 2.3 %collective-permute-done.18.r3_ref = bf16[96,1152]{1,0:T(8,128)(2,1)S(1)} collective-permute-done((bf16[96,1152]{1,0:T(8,128)(2,1)S(1)}, bf16[96,1152]{1,0:T(8,128)(2,1)S(1)}, u32[]{:S(2)}, u32[]{:S(2)}) %collective-permute-start.18) | collective-permute-done | bytes 221216 | tf_op jit(solution)/shard_map/ppermute | solution.py:31
  73.2 0.6 image_last.1
  73.9 1.4 %collective-permute-done.15.r3_ref = bf16[360,1152]{1,0:T(8,128)(2,1)S(1)} collective-permute-done((bf16[360,1152]{1,0:T(8,128)(2,1)S(1)}, bf16[360,1152]{1,0:T(8,128)(2,1)S(1)}, u32[]{:S(2)}, u32[]{:S(2)}) %collective-permute-start.15) | collective-permute-done | bytes 829472 | tf_op jit(solution)/shard_map/ppermute | solution.py:31
  75.3 2.7 %text_first.1 = (f32[96,1152]{1,0:T(8,128)S(1)}, bf16[96,1152]{1,0:T(8,128)(2,1)S(1)}, bf16[96,1152]{1,0:T(8,128)(2,1)S(1)}, bf16[96,1152]{1,0:T(8,128)(2,1)S(1)}) custom-call(f32[352,1152]{1,0:T(8,128)S(1)} %text_near.1.own_ref, bf16[360,1152]{1,0:T(8,128)(2,1)S(1)} %collective-permute-done.14.r2_ref, bf16[360,1152]{1,0:T(8,128)(2,1)S(1)} %collective-permute-done.15.r3_ref, ...), custom_call_target="tpu_custom_call" | custom-call | bytes 4423680 | tf_op jit(solution)/shard_map/text_first/pallas_call | solution.py:258
  78.0 0.5 collective-permute-start.19
  78.5 1.9 %collective-permute-start.20 = (bf16[96,1152]{1,0:T(8,128)(2,1)S(1)}, bf16[96,1152]{1,0:T(8,128)(2,1)S(1)}, u32[]{:S(2)}, u32[]{:S(2)}) collective-permute-start(bf16[96,1152]{1,0:T(8,128)(2,1)S(1)} %get-tuple-element.65), channel_id=1, source_target_pairs={{0,32},{1,65},{2,34},{3,67},{4,36},{5,69},{6,38},{7,71},{8,40},{9,... | collective-permute-start | bytes 663560 | tf_op jit(solution)/shard_map/ppermute | solution.py:31
  80.5 1.5 %collective-permute-start.21 = (bf16[96,1152]{1,0:T(8,128)(2,1)S(1)}, bf16[96,1152]{1,0:T(8,128)(2,1)S(1)}, u32[]{:S(2)}, u32[]{:S(2)}) collective-permute-start(bf16[96,1152]{1,0:T(8,128)(2,1)S(1)} %get-tuple-element.66), channel_id=1, source_target_pairs={{0,48},{1,67},{2,50},{3,65},{4,52},{5,71},{6,54},{7,69},{8,56},{9,... | collective-permute-start | bytes 663560 | tf_op jit(solution)/shard_map/ppermute | solution.py:31
  82.2 1.0 %collective-permute-done.19.r1_ref = bf16[96,1152]{1,0:T(8,128)(2,1)S(1)} collective-permute-done((bf16[96,1152]{1,0:T(8,128)(2,1)S(1)}, bf16[96,1152]{1,0:T(8,128)(2,1)S(1)}, u32[]{:S(2)}, u32[]{:S(2)}) %collective-permute-start.19) | collective-permute-done | bytes 221216 | tf_op jit(solution)/shard_map/ppermute | solution.py:31
  83.2 3.3 %collective-permute-done.20.r2_ref = bf16[96,1152]{1,0:T(8,128)(2,1)S(1)} collective-permute-done((bf16[96,1152]{1,0:T(8,128)(2,1)S(1)}, bf16[96,1152]{1,0:T(8,128)(2,1)S(1)}, u32[]{:S(2)}, u32[]{:S(2)}) %collective-permute-start.20) | collective-permute-done | bytes 221216 | tf_op jit(solution)/shard_map/ppermute | solution.py:31
  86.5 2.3 %collective-permute-done.21.r3_ref = bf16[96,1152]{1,0:T(8,128)(2,1)S(1)} collective-permute-done((bf16[96,1152]{1,0:T(8,128)(2,1)S(1)}, bf16[96,1152]{1,0:T(8,128)(2,1)S(1)}, u32[]{:S(2)}, u32[]{:S(2)}) %collective-permute-start.21) | collective-permute-done | bytes 221216 | tf_op jit(solution)/shard_map/ppermute | solution.py:31
  88.8 0.6 text_last.1
  90.1 2.0 %collective-permute-start.23 = (f32[352,288]{0,1:T(8,128)S(1)}, f32[352,288]{0,1:T(8,128)S(1)}, u32[]{:S(2)}, u32[]{:S(2)}) collective-permute-start(f32[352,288]{0,1:T(8,128)S(1)} %copy.7), channel_id=1, source_target_pairs={{0,1},{1,0},{2,3},{3,2},{4,5},{5,4},{6,7},{7,6},{8,9},{9,8},{10,11... | collective-permute-start | bytes 1216520 | tf_op jit(solution)/shard_map/ppermute | solution.py:31
  92.1 1.2 %collective-permute-start.26 = (f32[8,128]{1,0:T(8,128)S(1)}, f32[8,128]{1,0:T(8,128)S(1)}, u32[]{:S(2)}, u32[]{:S(2)}) collective-permute-start(f32[8,128]{1,0:T(8,128)S(1)} %get-tuple-element.73), channel_id=1, source_target_pairs={{0,66},{1,49},{2,64},{3,51},{4,70},{5,53},{6,68},{7,55},{8,74},{9,... | collective-permute-start | bytes 12296 | tf_op jit(solution)/shard_map/ppermute | solution.py:31
  93.4 2.0 %collective-permute-start.24 = (f32[8,128]{1,0:T(8,128)S(1)}, f32[8,128]{1,0:T(8,128)S(1)}, u32[]{:S(2)}, u32[]{:S(2)}) collective-permute-start(f32[8,128]{1,0:T(8,128)S(1)} %get-tuple-element.73), channel_id=1, source_target_pairs={{0,2},{1,17},{2,0},{3,19},{4,6},{5,21},{6,4},{7,23},{8,10},{9,25},... | collective-permute-start | bytes 12296 | tf_op jit(solution)/shard_map/ppermute | solution.py:31
  95.6 1.7 %join.1 = (f32[288,352]{1,0:T(8,128)}, f32[288,352]{1,0:T(8,128)}) custom-call(s32[2]{0:T(128)S(1)} %pad_add_fusion.info_ref, f32[352,288]{1,0:T(8,128)S(1)} %get-tuple-element.80.own_ref, f32[352,288]{1,0:T(8,128)S(1)} %copy.8.got_ref), custom_call_target="tpu_custom_call" | custom-call | bytes 1622024 | tf_op jit(solution)/shard_map/join/pallas_call | solution.py:258
  (38 shorter events, 4.0 us)
Async XLA Ops:
  0.7 0.9 copy-start
  1.6 0.9 copy-start.1
  3.4 2.7 %collective-permute-start = (bf16[352,288]{1,0:T(8,128)(2,1)S(1)}, bf16[352,288]{1,0:T(8,128)(2,1)S(1)}, u32[]{:S(2)}, u32[]{:S(2)}) collective-permute-start(bf16[352,288]{1,0:T(8,128)(2,1)S(1)} %get-tuple-element.41), channel_id=1, source_target_pairs={{0,1},{1,0},{2,3},{3,2},{4,5},{5,4},{6,7},{7,6},{8,9},{9,8},{10,11... | collective-permute-start | bytes 608264 | tf_op jit(solution)/shard_map/ppermute | solution.py:31
  6.3 5.8 %collective-permute-start.6 = (bf16[88,576]{1,0:T(8,128)(2,1)S(1)}, bf16[88,576]{1,0:T(8,128)(2,1)S(1)}, u32[]{:S(2)}, u32[]{:S(2)}) collective-permute-start(bf16[88,576]{1,0:T(8,128)(2,1)S(1)} %get-tuple-element.83), channel_id=1, source_target_pairs={{0,2},{1,3},{2,0},{3,1},{4,6},{5,7},{6,4},{7,5},{8,10},{9,11},{10,... | collective-permute-start | bytes 304136 | tf_op jit(solution)/shard_map/ppermute | solution.py:31
  8.4 8.7 %collective-permute-start.2 = (bf16[88,1152]{1,0:T(8,128)(2,1)S(1)}, bf16[88,1152]{1,0:T(8,128)(2,1)S(1)}, u32[]{:S(2)}, u32[]{:S(2)}) collective-permute-start(bf16[88,1152]{1,0:T(8,128)(2,1)S(1)} %pad_maximum_fusion.3), channel_id=1, source_target_pairs={{0,32},{1,65},{2,34},{3,67},{4,36},{5,69},{6,38},{7,71},{8,40},{9,... | collective-permute-start | bytes 608264 | tf_op jit(solution)/shard_map/ppermute | solution.py:31
  11.7 6.6 %collective-permute-start.1 = (bf16[88,1152]{1,0:T(8,128)(2,1)S(1)}, bf16[88,1152]{1,0:T(8,128)(2,1)S(1)}, u32[]{:S(2)}, u32[]{:S(2)}) collective-permute-start(bf16[88,1152]{1,0:T(8,128)(2,1)S(1)} %pad_maximum_fusion.3), channel_id=1, source_target_pairs={{0,16},{1,3},{2,18},{3,1},{4,20},{5,7},{6,22},{7,5},{8,24},{9,11},... | collective-permute-start | bytes 608264 | tf_op jit(solution)/shard_map/ppermute | solution.py:31
  11.7 7.6 %collective-permute-start.3 = (bf16[88,1152]{1,0:T(8,128)(2,1)S(1)}, bf16[88,1152]{1,0:T(8,128)(2,1)S(1)}, u32[]{:S(2)}, u32[]{:S(2)}) collective-permute-start(bf16[88,1152]{1,0:T(8,128)(2,1)S(1)} %pad_maximum_fusion.3), channel_id=1, source_target_pairs={{0,48},{1,67},{2,50},{3,65},{4,52},{5,71},{6,54},{7,69},{8,56},{9,... | collective-permute-start | bytes 608264 | tf_op jit(solution)/shard_map/ppermute | solution.py:31
  12.2 11.1 %collective-permute-start.9 = (bf16[88,1152]{1,0:T(8,128)(2,1)S(1)}, bf16[88,1152]{1,0:T(8,128)(2,1)S(1)}, u32[]{:S(2)}, u32[]{:S(2)}) collective-permute-start(bf16[88,1152]{1,0:T(8,128)(2,1)S(1)} %pad_maximum_fusion.4), channel_id=1, source_target_pairs={{0,12},{1,13},{2,14},{3,15},{4,8},{5,9},{6,10},{7,11},{8,4},{9,5},... | collective-permute-start | bytes 608264 | tf_op jit(solution)/shard_map/ppermute | solution.py:31
  14.8 8.5 %collective-permute-start.8 = (bf16[88,1152]{1,0:T(8,128)(2,1)S(1)}, bf16[88,1152]{1,0:T(8,128)(2,1)S(1)}, u32[]{:S(2)}, u32[]{:S(2)}) collective-permute-start(bf16[88,1152]{1,0:T(8,128)(2,1)S(1)} %pad_maximum_fusion.4), channel_id=1, source_target_pairs={{0,8},{1,9},{2,10},{3,11},{4,12},{5,13},{6,14},{7,15},{8,0},{9,1},... | collective-permute-start | bytes 608264 | tf_op jit(solution)/shard_map/ppermute | solution.py:31
  17.1 7.0 %collective-permute-start.7 = (bf16[88,1152]{1,0:T(8,128)(2,1)S(1)}, bf16[88,1152]{1,0:T(8,128)(2,1)S(1)}, u32[]{:S(2)}, u32[]{:S(2)}) collective-permute-start(bf16[88,1152]{1,0:T(8,128)(2,1)S(1)} %pad_maximum_fusion.4), channel_id=1, source_target_pairs={{0,4},{1,5},{2,6},{3,7},{4,0},{5,1},{6,2},{7,3},{8,12},{9,13},{10,... | collective-permute-start | bytes 608264 | tf_op jit(solution)/shard_map/ppermute | solution.py:31
  19.5 12.8 %collective-permute-start.5 = (bf16[4,88,1152]{2,1,0:T(8,128)(2,1)S(1)}, bf16[4,88,1152]{2,1,0:T(8,128)(2,1)S(1)}, u32[]{:S(2)}, u32[]{:S(2)}) collective-permute-start(bf16[4,88,1152]{2,1,0:T(8,128)(2,1)S(1)} %pad_maximum_fusion.1.ta_ref), channel_id=1, source_target_pairs={{0,66},{1,49},{2,64},{3,51},{4,70},{5,53},{6,68},{7,55},{8,74},{9,... | collective-permute-start | bytes 2433032 | tf_op jit(solution)/shard_map/ppermute | solution.py:31
  22.3 11.4 %collective-permute-start.4 = (bf16[4,88,1152]{2,1,0:T(8,128)(2,1)S(1)}, bf16[4,88,1152]{2,1,0:T(8,128)(2,1)S(1)}, u32[]{:S(2)}, u32[]{:S(2)}) collective-permute-start(bf16[4,88,1152]{2,1,0:T(8,128)(2,1)S(1)} %pad_maximum_fusion.1.ta_ref), channel_id=1, source_target_pairs={{0,2},{1,17},{2,0},{3,19},{4,6},{5,21},{6,4},{7,23},{8,10},{9,25},... | collective-permute-start | bytes 2433032 | tf_op jit(solution)/shard_map/ppermute | solution.py:31
  24.2 9.5 %collective-permute-start.10 = (bf16[352,1152]{1,0:T(8,128)(2,1)S(1)}, bf16[352,1152]{1,0:T(8,128)(2,1)S(1)}, u32[]{:S(2)}, u32[]{:S(2)}) collective-permute-start(bf16[352,1152]{1,0:T(8,128)(2,1)S(1)} %pad_maximum_fusion.2.im0_ref), channel_id=1, source_target_pairs={{0,1},{1,0},{2,3},{3,2},{4,5},{5,4},{6,7},{7,6},{8,9},{9,8},{10,11... | collective-permute-start | bytes 2433032 | tf_op jit(solution)/shard_map/ppermute | solution.py:31
  27.4 14.8 %collective-permute-start.11 = (bf16[4,88,1152]{2,1,0:T(8,128)(2,1)S(1)}, bf16[4,88,1152]{2,1,0:T(8,128)(2,1)S(1)}, u32[]{:S(2)}, u32[]{:S(2)}) collective-permute-start(bf16[4,88,1152]{2,1,0:T(8,128)(2,1)S(1)} %pad_maximum_fusion.1.ta_ref), channel_id=1, source_target_pairs={{0,64},{1,33},{2,66},{3,35},{4,68},{5,37},{6,70},{7,39},{8,72},{9,... | collective-permute-start | bytes 2433032 | tf_op jit(solution)/shard_map/ppermute | solution.py:31
  39.4 11.9 %collective-permute-start.12 = (bf16[360,1152]{1,0:T(8,128)(2,1)S(1)}, bf16[360,1152]{1,0:T(8,128)(2,1)S(1)}, u32[]{:S(2)}, u32[]{:S(2)}) collective-permute-start(bf16[360,1152]{1,0:T(8,128)(2,1)S(1)} %get-tuple-element.52), channel_id=1, source_target_pairs={{0,2},{1,17},{2,0},{3,19},{4,6},{5,21},{6,4},{7,23},{8,10},{9,25},... | collective-permute-start | bytes 2488328 | tf_op jit(solution)/shard_map/ppermute | solution.py:31
  51.2 5.2 %collective-permute-start.13 = (f32[360,1152]{1,0:T(8,128)S(1)}, f32[360,1152]{1,0:T(8,128)S(1)}, u32[]{:S(2)}, u32[]{:S(2)}) collective-permute-start(f32[360,1152]{1,0:T(8,128)S(1)} %get-tuple-element.53), channel_id=1, source_target_pairs={{0,1},{1,0},{2,3},{3,2},{4,5},{5,4},{6,7},{7,6},{8,9},{9,8},{10,11... | collective-permute-start | bytes 4976648 | tf_op jit(solution)/shard_map/ppermute | solution.py:31
  53.3 20.6 %collective-permute-start.14 = (bf16[360,1152]{1,0:T(8,128)(2,1)S(1)}, bf16[360,1152]{1,0:T(8,128)(2,1)S(1)}, u32[]{:S(2)}, u32[]{:S(2)}) collective-permute-start(bf16[360,1152]{1,0:T(8,128)(2,1)S(1)} %get-tuple-element.59), channel_id=1, source_target_pairs={{0,64},{1,33},{2,66},{3,35},{4,68},{5,37},{6,70},{7,39},{8,72},{9,... | collective-permute-start | bytes 2488328 | tf_op jit(solution)/shard_map/ppermute | solution.py:31
  55.0 20.3 %collective-permute-start.15 = (bf16[360,1152]{1,0:T(8,128)(2,1)S(1)}, bf16[360,1152]{1,0:T(8,128)(2,1)S(1)}, u32[]{:S(2)}, u32[]{:S(2)}) collective-permute-start(bf16[360,1152]{1,0:T(8,128)(2,1)S(1)} %get-tuple-element.60), channel_id=1, source_target_pairs={{0,66},{1,49},{2,64},{3,51},{4,70},{5,53},{6,68},{7,55},{8,74},{9,... | collective-permute-start | bytes 2488328 | tf_op jit(solution)/shard_map/ppermute | solution.py:31
  57.5 6.5 %collective-permute-start.16 = (bf16[96,1152]{1,0:T(8,128)(2,1)S(1)}, bf16[96,1152]{1,0:T(8,128)(2,1)S(1)}, u32[]{:S(2)}, u32[]{:S(2)}) collective-permute-start(bf16[96,1152]{1,0:T(8,128)(2,1)S(1)} %get-tuple-element.54), channel_id=1, source_target_pairs={{0,4},{1,5},{2,6},{3,7},{4,0},{5,1},{6,2},{7,3},{8,12},{9,13},{10,... | collective-permute-start | bytes 663560 | tf_op jit(solution)/shard_map/ppermute | solution.py:31
  58.8 12.2 %collective-permute-start.17 = (bf16[96,1152]{1,0:T(8,128)(2,1)S(1)}, bf16[96,1152]{1,0:T(8,128)(2,1)S(1)}, u32[]{:S(2)}, u32[]{:S(2)}) collective-permute-start(bf16[96,1152]{1,0:T(8,128)(2,1)S(1)} %get-tuple-element.55), channel_id=1, source_target_pairs={{0,8},{1,9},{2,10},{3,11},{4,12},{5,13},{6,14},{7,15},{8,0},{9,1},... | collective-permute-start | bytes 663560 | tf_op jit(solution)/shard_map/ppermute | solution.py:31
  61.2 12.0 %collective-permute-start.18 = (bf16[96,1152]{1,0:T(8,128)(2,1)S(1)}, bf16[96,1152]{1,0:T(8,128)(2,1)S(1)}, u32[]{:S(2)}, u32[]{:S(2)}) collective-permute-start(bf16[96,1152]{1,0:T(8,128)(2,1)S(1)} %get-tuple-element.56), channel_id=1, source_target_pairs={{0,12},{1,13},{2,14},{3,15},{4,8},{5,9},{6,10},{7,11},{8,4},{9,5},... | collective-permute-start | bytes 663560 | tf_op jit(solution)/shard_map/ppermute | solution.py:31
  78.0 5.2 %collective-permute-start.19 = (bf16[96,1152]{1,0:T(8,128)(2,1)S(1)}, bf16[96,1152]{1,0:T(8,128)(2,1)S(1)}, u32[]{:S(2)}, u32[]{:S(2)}) collective-permute-start(bf16[96,1152]{1,0:T(8,128)(2,1)S(1)} %get-tuple-element.64), channel_id=1, source_target_pairs={{0,16},{1,3},{2,18},{3,1},{4,20},{5,7},{6,22},{7,5},{8,24},{9,11},... | collective-permute-start | bytes 663560 | tf_op jit(solution)/shard_map/ppermute | solution.py:31
  78.5 8.0 %collective-permute-start.20 = (bf16[96,1152]{1,0:T(8,128)(2,1)S(1)}, bf16[96,1152]{1,0:T(8,128)(2,1)S(1)}, u32[]{:S(2)}, u32[]{:S(2)}) collective-permute-start(bf16[96,1152]{1,0:T(8,128)(2,1)S(1)} %get-tuple-element.65), channel_id=1, source_target_pairs={{0,32},{1,65},{2,34},{3,67},{4,36},{5,69},{6,38},{7,71},{8,40},{9,... | collective-permute-start | bytes 663560 | tf_op jit(solution)/shard_map/ppermute | solution.py:31
  80.5 8.4 %collective-permute-start.21 = (bf16[96,1152]{1,0:T(8,128)(2,1)S(1)}, bf16[96,1152]{1,0:T(8,128)(2,1)S(1)}, u32[]{:S(2)}, u32[]{:S(2)}) collective-permute-start(bf16[96,1152]{1,0:T(8,128)(2,1)S(1)} %get-tuple-element.66), channel_id=1, source_target_pairs={{0,48},{1,67},{2,50},{3,65},{4,52},{5,71},{6,54},{7,69},{8,56},{9,... | collective-permute-start | bytes 663560 | tf_op jit(solution)/shard_map/ppermute | solution.py:31
  82.1 7.4 %collective-permute-start.22 = (f32[88,576]{1,0:T(8,128)S(1)}, f32[88,576]{1,0:T(8,128)S(1)}, u32[]{:S(2)}, u32[]{:S(2)}) collective-permute-start(f32[88,576]{1,0:T(8,128)S(1)} %slice.40), channel_id=1, source_target_pairs={{0,2},{1,3},{2,0},{3,1},{4,6},{5,7},{6,4},{7,5},{8,10},{9,11},{10,... | collective-permute-start | bytes 608264 | tf_op jit(solution)/shard_map/ppermute | solution.py:31
  90.1 5.3 %collective-permute-start.23 = (f32[352,288]{0,1:T(8,128)S(1)}, f32[352,288]{0,1:T(8,128)S(1)}, u32[]{:S(2)}, u32[]{:S(2)}) collective-permute-start(f32[352,288]{0,1:T(8,128)S(1)} %copy.7), channel_id=1, source_target_pairs={{0,1},{1,0},{2,3},{3,2},{4,5},{5,4},{6,7},{7,6},{8,9},{9,8},{10,11... | collective-permute-start | bytes 1216520 | tf_op jit(solution)/shard_map/ppermute | solution.py:31
  92.1 5.2 %collective-permute-start.26 = (f32[8,128]{1,0:T(8,128)S(1)}, f32[8,128]{1,0:T(8,128)S(1)}, u32[]{:S(2)}, u32[]{:S(2)}) collective-permute-start(f32[8,128]{1,0:T(8,128)S(1)} %get-tuple-element.73), channel_id=1, source_target_pairs={{0,66},{1,49},{2,64},{3,51},{4,70},{5,53},{6,68},{7,55},{8,74},{9,... | collective-permute-start | bytes 12296 | tf_op jit(solution)/shard_map/ppermute | solution.py:31
  93.3 4.0 %collective-permute-start.25 = (f32[8,128]{1,0:T(8,128)S(1)}, f32[8,128]{1,0:T(8,128)S(1)}, u32[]{:S(2)}, u32[]{:S(2)}) collective-permute-start(f32[8,128]{1,0:T(8,128)S(1)} %get-tuple-element.73), channel_id=1, source_target_pairs={{0,64},{1,33},{2,66},{3,35},{4,68},{5,37},{6,70},{7,39},{8,72},{9,... | collective-permute-start | bytes 12296 | tf_op jit(solution)/shard_map/ppermute | solution.py:31
  93.4 3.9 %collective-permute-start.24 = (f32[8,128]{1,0:T(8,128)S(1)}, f32[8,128]{1,0:T(8,128)S(1)}, u32[]{:S(2)}, u32[]{:S(2)}) collective-permute-start(f32[8,128]{1,0:T(8,128)S(1)} %get-tuple-element.73), channel_id=1, source_target_pairs={{0,2},{1,17},{2,0},{3,19},{4,6},{5,21},{6,4},{7,23},{8,10},{9,25},... | collective-permute-start | bytes 12296 | tf_op jit(solution)/shard_map/ppermute | solution.py:31

commit v18 on v16

--- a/solution.py
+++ b/solution.py
@@ -100,13 +100,13 @@
     return lax.dot_general(coeff_low[...], t_rel[...], (((0,), (0,)), ((), ())), preferred_element_type=F32)
 
 
-def split_kernel(rows, info_ref, texts_ref, images_ref, keep_ref, send_ref):
+def split_kernel(rows, width, info_ref, both_ref, keep_ref, send_ref):
     on0, step = info_ref[0] == 0, 2 * rows
-    for at, ref in ((0, texts_ref), (step, images_ref)):
-        whole = ref[...].astype(F32).T
+    for k in range(2):
+        whole = both_ref[k * width : (k + 1) * width, :].astype(F32).T
         first, second = whole[:step], whole[step:]
-        keep_ref[at : at + step, :] = jnp.where(on0, first, second).astype(BF)
-        send_ref[at : at + step, :] = jnp.where(on0, second, first).astype(BF)
+        keep_ref[k * step : (k + 1) * step, :] = jnp.where(on0, first, second).astype(BF)
+        send_ref[k * step : (k + 1) * step, :] = jnp.where(on0, second, first).astype(BF)
 
 
 def join_kernel(rows, info_ref, own_ref, got_ref, texts_ref, images_ref):
@@ -265,9 +265,8 @@
         )(*args)
 
     info = jnp.stack([core, z_lo]).astype(jnp.int32)
-    keep, send = call(
-        functools.partial(split_kernel, rows), "split", [bf16(height, width)] * 2, info, caption_embeds.T, picture_embeds.T, scalars=1
-    )
+    both = jnp.concatenate([caption_embeds.T, picture_embeds.T], axis=0)
+    keep, send = call(functools.partial(split_kernel, rows, width), "split", [bf16(height, width)] * 2, info, both, scalars=1)
     chip = jnp.concatenate(by(on0, keep, swap(send, CORE)), axis=1)
     packed = jnp.concatenate([chip[:rows], chip[rows:step]], axis=1)
     keep, send = by(lo0, chip[step : step + rows], chip[step + rows :])

time: 98.1 us -> 97.3 us (level)
  local copies, waits for them, and re-layouts: 2.92 us -> 1.05 us
  other arithmetic: 1.34 us -> 2.43 us
    unnamed x4 -> x0, local copies, waits for them, and re-layouts: 1.87 us -> none
    concatenate x0 -> x1, other arithmetic: none -> 1.09 us  [body(): both = jnp.concatenate([caption_embeds.T, picture_embeds.T], axis=0)]
where the time goes in v18:
time: 97.3 us; the launch traced here: 97 us
  starting transfers between devices  37 us (38%)
  waiting for transfers between devices  30.5 us (31%)
  Pallas kernels  23.9 us (25%)
  other arithmetic  2.43 us (2%)
  between operations  2.1 us (2%)
  local copies, waits for them, and re-layouts  1.05 us (1%)
    ppermute x27, starting transfers between devices, swap(): lax.ppermute(array, AXES, [(i, i ^ (mask1 if i & 1 else mask0)) for i in...  37 us
    ppermute x27, waiting for transfers between devices, swap(): lax.ppermute(array, AXES, [(i, i ^ (mask1 if i & 1 else mask0)) for i in...  30.5 us
    pallas_call x10, Pallas kernels, call(): pl.pallas_call(kernel, out_shape=out_shape, in_specs=[SMEM] * scalars + [...  23.9 us
  transfers between devices with their start and end apart: 27, of which 17 were waited for; matrix products, arithmetic and copies ran while one was open for 1% of the time, Pallas kernels for 21%

profile of v18, /device:TPU:1, one launch (start us, length us, event | category | flops | bytes accessed | tf_op | source)
XLA Modules:
  0.0 97.0 jit_solution(12989190559860999827)
XLA Ops:
  0.7 1.1 %pad_maximum_fusion.3.both_ref = bf16[576,352]{1,0:T(8,128)(2,1)S(1)} fusion(bf16[288,352]{1,0:T(8,128)(2,1)} %bitcast.13, bf16[288,352]{1,0:T(8,128)(2,1)} %bitcast.14), kind=kLoop, calls=%fused_computation.11 | loop fusion | flops 811008 | bytes 811008 | tf_op jit(solution)/shard_map/concatenate | solution.py:268
  1.8 0.8 split.1
  2.6 1.5 %collective-permute-start = (bf16[352,288]{1,0:T(8,128)(2,1)S(1)}, bf16[352,288]{1,0:T(8,128)(2,1)S(1)}, u32[]{:S(2)}, u32[]{:S(2)}) collective-permute-start(bf16[352,288]{1,0:T(8,128)(2,1)S(1)} %get-tuple-element.41), channel_id=1, source_target_pairs={{0,1},{1,0},{2,3},{3,2},{4,5},{5,4},{6,7},{7,6},{8,9},{9,8},{10,11... | collective-permute-start | bytes 608264 | tf_op jit(solution)/shard_map/ppermute | solution.py:31
  4.1 1.2 %collective-permute-done = bf16[352,288]{1,0:T(8,128)(2,1)S(1)} collective-permute-done((bf16[352,288]{1,0:T(8,128)(2,1)S(1)}, bf16[352,288]{1,0:T(8,128)(2,1)S(1)}, u32[]{:S(2)}, u32[]{:S(2)}) %collective-permute-start) | collective-permute-done | bytes 202784 | tf_op jit(solution)/shard_map/ppermute | solution.py:31
  5.6 1.8 %collective-permute-start.6 = (bf16[88,576]{1,0:T(8,128)(2,1)S(1)}, bf16[88,576]{1,0:T(8,128)(2,1)S(1)}, u32[]{:S(2)}, u32[]{:S(2)}) collective-permute-start(bf16[88,576]{1,0:T(8,128)(2,1)S(1)} %get-tuple-element.83), channel_id=1, source_target_pairs={{0,2},{1,3},{2,0},{3,1},{4,6},{5,7},{6,4},{7,5},{8,10},{9,11},{10,... | collective-permute-start | bytes 304136 | tf_op jit(solution)/shard_map/ppermute | solution.py:31
  7.6 3.4 %collective-permute-start.2 = (bf16[88,1152]{1,0:T(8,128)(2,1)S(1)}, bf16[88,1152]{1,0:T(8,128)(2,1)S(1)}, u32[]{:S(2)}, u32[]{:S(2)}) collective-permute-start(bf16[88,1152]{1,0:T(8,128)(2,1)S(1)} %pad_maximum_fusion.4), channel_id=1, source_target_pairs={{0,32},{1,65},{2,34},{3,67},{4,36},{5,69},{6,38},{7,71},{8,40},{9,... | collective-permute-start | bytes 608264 | tf_op jit(solution)/shard_map/ppermute | solution.py:31
  11.5 2.6 %collective-permute-start.9 = (bf16[88,1152]{1,0:T(8,128)(2,1)S(1)}, bf16[88,1152]{1,0:T(8,128)(2,1)S(1)}, u32[]{:S(2)}, u32[]{:S(2)}) collective-permute-start(bf16[88,1152]{1,0:T(8,128)(2,1)S(1)} %pad_maximum_fusion.5), channel_id=1, source_target_pairs={{0,12},{1,13},{2,14},{3,15},{4,8},{5,9},{6,10},{7,11},{8,4},{9,5},... | collective-permute-start | bytes 608264 | tf_op jit(solution)/shard_map/ppermute | solution.py:31
  14.0 0.5 collective-permute-start.8
  14.5 1.8 %collective-permute-done.2 = bf16[88,1152]{1,0:T(8,128)(2,1)S(1)} collective-permute-done((bf16[88,1152]{1,0:T(8,128)(2,1)S(1)}, bf16[88,1152]{1,0:T(8,128)(2,1)S(1)}, u32[]{:S(2)}, u32[]{:S(2)}) %collective-permute-start.2) | collective-permute-done | bytes 202784 | tf_op jit(solution)/shard_map/ppermute | solution.py:31
  16.3 1.2 %collective-permute-start.7 = (bf16[88,1152]{1,0:T(8,128)(2,1)S(1)}, bf16[88,1152]{1,0:T(8,128)(2,1)S(1)}, u32[]{:S(2)}, u32[]{:S(2)}) collective-permute-start(bf16[88,1152]{1,0:T(8,128)(2,1)S(1)} %pad_maximum_fusion.5), channel_id=1, source_target_pairs={{0,4},{1,5},{2,6},{3,7},{4,0},{5,1},{6,2},{7,3},{8,12},{9,13},{10,... | collective-permute-start | bytes 608264 | tf_op jit(solution)/shard_map/ppermute | solution.py:31
  17.5 1.0 %collective-permute-done.3 = bf16[88,1152]{1,0:T(8,128)(2,1)S(1)} collective-permute-done((bf16[88,1152]{1,0:T(8,128)(2,1)S(1)}, bf16[88,1152]{1,0:T(8,128)(2,1)S(1)}, u32[]{:S(2)}, u32[]{:S(2)}) %collective-permute-start.3) | collective-permute-done | bytes 202784 | tf_op jit(solution)/shard_map/ppermute | solution.py:31
  18.7 2.8 %collective-permute-start.5 = (bf16[4,88,1152]{2,1,0:T(8,128)(2,1)S(1)}, bf16[4,88,1152]{2,1,0:T(8,128)(2,1)S(1)}, u32[]{:S(2)}, u32[]{:S(2)}) collective-permute-start(bf16[4,88,1152]{2,1,0:T(8,128)(2,1)S(1)} %pad_maximum_fusion.1.ta_ref), channel_id=1, source_target_pairs={{0,66},{1,49},{2,64},{3,51},{4,70},{5,53},{6,68},{7,55},{8,74},{9,... | collective-permute-start | bytes 2433032 | tf_op jit(solution)/shard_map/ppermute | solution.py:31
  21.5 1.1 %collective-permute-done.9 = bf16[88,1152]{1,0:T(8,128)(2,1)S(1)} collective-permute-done((bf16[88,1152]{1,0:T(8,128)(2,1)S(1)}, bf16[88,1152]{1,0:T(8,128)(2,1)S(1)}, u32[]{:S(2)}, u32[]{:S(2)}) %collective-permute-start.9) | collective-permute-done | bytes 202784 | tf_op jit(solution)/shard_map/ppermute | solution.py:31
  22.6 0.8 collective-permute-done.7
  23.4 1.9 %collective-permute-start.10 = (bf16[352,1152]{1,0:T(8,128)(2,1)S(1)}, bf16[352,1152]{1,0:T(8,128)(2,1)S(1)}, u32[]{:S(2)}, u32[]{:S(2)}) collective-permute-start(bf16[352,1152]{1,0:T(8,128)(2,1)S(1)} %pad_maximum_fusion.2.im0_ref), channel_id=1, source_target_pairs={{0,1},{1,0},{2,3},{3,2},{4,5},{5,4},{6,7},{7,6},{8,9},{9,8},{10,11... | collective-permute-start | bytes 2433032 | tf_op jit(solution)/shard_map/ppermute | solution.py:31
  26.6 3.0 %collective-permute-start.11 = (bf16[4,88,1152]{2,1,0:T(8,128)(2,1)S(1)}, bf16[4,88,1152]{2,1,0:T(8,128)(2,1)S(1)}, u32[]{:S(2)}, u32[]{:S(2)}) collective-permute-start(bf16[4,88,1152]{2,1,0:T(8,128)(2,1)S(1)} %pad_maximum_fusion.1.ta_ref), channel_id=1, source_target_pairs={{0,64},{1,33},{2,66},{3,35},{4,68},{5,37},{6,70},{7,39},{8,72},{9,... | collective-permute-start | bytes 2433032 | tf_op jit(solution)/shard_map/ppermute | solution.py:31
  29.7 1.8 %collective-permute-done.5.tb_ref = bf16[4,88,1152]{2,1,0:T(8,128)(2,1)S(1)} collective-permute-done((bf16[4,88,1152]{2,1,0:T(8,128)(2,1)S(1)}, bf16[4,88,1152]{2,1,0:T(8,128)(2,1)S(1)}, u32[]{:S(2)}, u32[]{:S(2)}) %collective-permute-start.5) | collective-permute-done | bytes 811040 | tf_op jit(solution)/shard_map/ppermute | solution.py:31
  31.4 1.5 %collective-permute-done.4.tb_ref = bf16[4,88,1152]{2,1,0:T(8,128)(2,1)S(1)} collective-permute-done((bf16[4,88,1152]{2,1,0:T(8,128)(2,1)S(1)}, bf16[4,88,1152]{2,1,0:T(8,128)(2,1)S(1)}, u32[]{:S(2)}, u32[]{:S(2)}) %collective-permute-start.4) | collective-permute-done | bytes 811040 | tf_op jit(solution)/shard_map/ppermute | solution.py:31
  32.9 5.7 %tile_near.1 = (f32[2,4,88,1152]{3,2,1,0:T(8,128)S(1)}, bf16[360,1152]{1,0:T(8,128)(2,1)S(1)}, bf16[704,1152]{1,0:T(8,128)(2,1)S(1)}, bf16[704,704]{1,0:T(8,128)(2,1)S(1)}, f32[8,128]{1,0:T(8,128)S(1)}) custom-call(s32[2]{0:T(128)S(1)} %pad_add_fusion.info_ref, f32[2]{0:T(128)S(1)} %pad_maximum_fusion.7.scale_ref, ...), custom_call_target="tpu_custom_call" | custom-call | flops 2283798528 | bytes 9934864 | tf_op jit(solution)/shard_map/tile_near/pallas_call | solution.py:252
  38.9 1.6 %image_near.1.before_ref = f32[704,1152]{1,0:T(8,128)S(1)} custom-call(bf16[704,1152]{1,0:T(8,128)(2,1)S(1)} %get-tuple-element.45.t_rel, bf16[704,704]{1,0:T(8,128)(2,1)S(1)} %get-tuple-element.46.coeff_low), custom_call_target="tpu_custom_call" | custom-call | flops 1141899264 | bytes 5857280 | tf_op jit(solution)/shard_map/image_near/pallas_call | solution.py:252
  40.5 0.9 collective-permute-done.11.ta_ref
  41.4 8.5 %tile_far.1 = (bf16[360,1152]{1,0:T(8,128)(2,1)S(1)}, bf16[360,1152]{1,0:T(8,128)(2,1)S(1)}, f32[360,1152]{1,0:T(8,128)S(1)}, f32[360,1152]{1,0:T(8,128)S(1)}) custom-call(s32[2]{0:T(128)S(1)} %pad_add_fusion.info_ref, f32[2]{0:T(128)S(1)} %pad_maximum_fusion.7.scale_ref, bf16[4,88,1152]{2,1,0:T(8,128)(2,1)S(1)} %collective-permute-done.11.ta_ref, ...), custom_call_target="tpu_custom_call" | custom-call | flops 3425697792 | bytes 11468816 | tf_op jit(solution)/shard_map/tile_far/pallas_call | solution.py:252
  49.9 0.6 collective-permute-done.12.r1_ref
  50.5 2.1 %collective-permute-start.13 = (f32[360,1152]{1,0:T(8,128)S(1)}, f32[360,1152]{1,0:T(8,128)S(1)}, u32[]{:S(2)}, u32[]{:S(2)}) collective-permute-start(f32[360,1152]{1,0:T(8,128)S(1)} %get-tuple-element.53), channel_id=1, source_target_pairs={{0,1},{1,0},{2,3},{3,2},{4,5},{5,4},{6,7},{7,6},{8,9},{9,8},{10,11... | collective-permute-start | bytes 4976648 | tf_op jit(solution)/shard_map/ppermute | solution.py:31
  52.6 1.6 %collective-permute-start.14 = (bf16[360,1152]{1,0:T(8,128)(2,1)S(1)}, bf16[360,1152]{1,0:T(8,128)(2,1)S(1)}, u32[]{:S(2)}, u32[]{:S(2)}) collective-permute-start(bf16[360,1152]{1,0:T(8,128)(2,1)S(1)} %get-tuple-element.59), channel_id=1, source_target_pairs={{0,64},{1,33},{2,66},{3,35},{4,68},{5,37},{6,70},{7,39},{8,72},{9,... | collective-permute-start | bytes 2488328 | tf_op jit(solution)/shard_map/ppermute | solution.py:31
  54.2 0.8 collective-permute-start.15
  55.0 0.7 collective-permute-done.13.other_ref
  55.7 1.0 %image_first.1 = (f32[96,1152]{1,0:T(8,128)S(1)}, bf16[96,1152]{1,0:T(8,128)(2,1)S(1)}, bf16[96,1152]{1,0:T(8,128)(2,1)S(1)}, bf16[96,1152]{1,0:T(8,128)(2,1)S(1)}) custom-call(f32[360,1152]{1,0:T(8,128)S(1)} %get-tuple-element.50.own_ref, f32[360,1152]{1,0:T(8,128)S(1)} %collective-permute-done.13.other_ref), custom_call_target="tpu_custom_call" | custom-call | bytes 4423680 | tf_op jit(solution)/shard_map/image_first/pallas_call | solution.py:252
  56.7 1.3 %collective-permute-start.16 = (bf16[96,1152]{1,0:T(8,128)(2,1)S(1)}, bf16[96,1152]{1,0:T(8,128)(2,1)S(1)}, u32[]{:S(2)}, u32[]{:S(2)}) collective-permute-start(bf16[96,1152]{1,0:T(8,128)(2,1)S(1)} %get-tuple-element.54), channel_id=1, source_target_pairs={{0,4},{1,5},{2,6},{3,7},{4,0},{5,1},{6,2},{7,3},{8,12},{9,13},{10,... | collective-permute-start | bytes 663560 | tf_op jit(solution)/shard_map/ppermute | solution.py:31
  58.0 2.5 %collective-permute-start.17 = (bf16[96,1152]{1,0:T(8,128)(2,1)S(1)}, bf16[96,1152]{1,0:T(8,128)(2,1)S(1)}, u32[]{:S(2)}, u32[]{:S(2)}) collective-permute-start(bf16[96,1152]{1,0:T(8,128)(2,1)S(1)} %get-tuple-element.55), channel_id=1, source_target_pairs={{0,8},{1,9},{2,10},{3,11},{4,12},{5,13},{6,14},{7,15},{8,0},{9,1},... | collective-permute-start | bytes 663560 | tf_op jit(solution)/shard_map/ppermute | solution.py:31
  60.6 0.8 text_near.1.own_ref
  61.4 1.8 %collective-permute-done.16.r1_ref = bf16[96,1152]{1,0:T(8,128)(2,1)S(1)} collective-permute-done((bf16[96,1152]{1,0:T(8,128)(2,1)S(1)}, bf16[96,1152]{1,0:T(8,128)(2,1)S(1)}, u32[]{:S(2)}, u32[]{:S(2)}) %collective-permute-start.16) | collective-permute-done | bytes 221216 | tf_op jit(solution)/shard_map/ppermute | solution.py:31
  63.2 7.0 %collective-permute-done.17.r2_ref = bf16[96,1152]{1,0:T(8,128)(2,1)S(1)} collective-permute-done((bf16[96,1152]{1,0:T(8,128)(2,1)S(1)}, bf16[96,1152]{1,0:T(8,128)(2,1)S(1)}, u32[]{:S(2)}, u32[]{:S(2)}) %collective-permute-start.17) | collective-permute-done | bytes 221216 | tf_op jit(solution)/shard_map/ppermute | solution.py:31
  70.2 2.3 %collective-permute-done.18.r3_ref = bf16[96,1152]{1,0:T(8,128)(2,1)S(1)} collective-permute-done((bf16[96,1152]{1,0:T(8,128)(2,1)S(1)}, bf16[96,1152]{1,0:T(8,128)(2,1)S(1)}, u32[]{:S(2)}, u32[]{:S(2)}) %collective-permute-start.18) | collective-permute-done | bytes 221216 | tf_op jit(solution)/shard_map/ppermute | solution.py:31
  72.5 0.6 image_last.1
  73.1 1.4 %collective-permute-done.15.r3_ref = bf16[360,1152]{1,0:T(8,128)(2,1)S(1)} collective-permute-done((bf16[360,1152]{1,0:T(8,128)(2,1)S(1)}, bf16[360,1152]{1,0:T(8,128)(2,1)S(1)}, u32[]{:S(2)}, u32[]{:S(2)}) %collective-permute-start.15) | collective-permute-done | bytes 829472 | tf_op jit(solution)/shard_map/ppermute | solution.py:31
  74.5 2.6 %text_first.1 = (f32[96,1152]{1,0:T(8,128)S(1)}, bf16[96,1152]{1,0:T(8,128)(2,1)S(1)}, bf16[96,1152]{1,0:T(8,128)(2,1)S(1)}, bf16[96,1152]{1,0:T(8,128)(2,1)S(1)}) custom-call(f32[352,1152]{1,0:T(8,128)S(1)} %text_near.1.own_ref, bf16[360,1152]{1,0:T(8,128)(2,1)S(1)} %collective-permute-done.14.r2_ref, bf16[360,1152]{1,0:T(8,128)(2,1)S(1)} %collective-permute-done.15.r3_ref, ...), custom_call_target="tpu_custom_call" | custom-call | bytes 4423680 | tf_op jit(solution)/shard_map/text_first/pallas_call | solution.py:252
  77.2 0.5 collective-permute-start.19
  77.7 1.9 %collective-permute-start.20 = (bf16[96,1152]{1,0:T(8,128)(2,1)S(1)}, bf16[96,1152]{1,0:T(8,128)(2,1)S(1)}, u32[]{:S(2)}, u32[]{:S(2)}) collective-permute-start(bf16[96,1152]{1,0:T(8,128)(2,1)S(1)} %get-tuple-element.65), channel_id=1, source_target_pairs={{0,32},{1,65},{2,34},{3,67},{4,36},{5,69},{6,38},{7,71},{8,40},{9,... | collective-permute-start | bytes 663560 | tf_op jit(solution)/shard_map/ppermute | solution.py:31
  79.7 1.5 %collective-permute-start.21 = (bf16[96,1152]{1,0:T(8,128)(2,1)S(1)}, bf16[96,1152]{1,0:T(8,128)(2,1)S(1)}, u32[]{:S(2)}, u32[]{:S(2)}) collective-permute-start(bf16[96,1152]{1,0:T(8,128)(2,1)S(1)} %get-tuple-element.66), channel_id=1, source_target_pairs={{0,48},{1,67},{2,50},{3,65},{4,52},{5,71},{6,54},{7,69},{8,56},{9,... | collective-permute-start | bytes 663560 | tf_op jit(solution)/shard_map/ppermute | solution.py:31
  81.4 1.0 %collective-permute-done.19.r1_ref = bf16[96,1152]{1,0:T(8,128)(2,1)S(1)} collective-permute-done((bf16[96,1152]{1,0:T(8,128)(2,1)S(1)}, bf16[96,1152]{1,0:T(8,128)(2,1)S(1)}, u32[]{:S(2)}, u32[]{:S(2)}) %collective-permute-start.19) | collective-permute-done | bytes 221216 | tf_op jit(solution)/shard_map/ppermute | solution.py:31
  82.4 3.3 %collective-permute-done.20.r2_ref = bf16[96,1152]{1,0:T(8,128)(2,1)S(1)} collective-permute-done((bf16[96,1152]{1,0:T(8,128)(2,1)S(1)}, bf16[96,1152]{1,0:T(8,128)(2,1)S(1)}, u32[]{:S(2)}, u32[]{:S(2)}) %collective-permute-start.20) | collective-permute-done | bytes 221216 | tf_op jit(solution)/shard_map/ppermute | solution.py:31
  85.7 2.3 %collective-permute-done.21.r3_ref = bf16[96,1152]{1,0:T(8,128)(2,1)S(1)} collective-permute-done((bf16[96,1152]{1,0:T(8,128)(2,1)S(1)}, bf16[96,1152]{1,0:T(8,128)(2,1)S(1)}, u32[]{:S(2)}, u32[]{:S(2)}) %collective-permute-start.21) | collective-permute-done | bytes 221216 | tf_op jit(solution)/shard_map/ppermute | solution.py:31
  88.0 0.6 text_last.1
  89.3 2.0 %collective-permute-start.23 = (f32[352,288]{0,1:T(8,128)S(1)}, f32[352,288]{0,1:T(8,128)S(1)}, u32[]{:S(2)}, u32[]{:S(2)}) collective-permute-start(f32[352,288]{0,1:T(8,128)S(1)} %copy.7), channel_id=1, source_target_pairs={{0,1},{1,0},{2,3},{3,2},{4,5},{5,4},{6,7},{7,6},{8,9},{9,8},{10,11... | collective-permute-start | bytes 1216520 | tf_op jit(solution)/shard_map/ppermute | solution.py:31
  91.3 1.2 %collective-permute-start.26 = (f32[8,128]{1,0:T(8,128)S(1)}, f32[8,128]{1,0:T(8,128)S(1)}, u32[]{:S(2)}, u32[]{:S(2)}) collective-permute-start(f32[8,128]{1,0:T(8,128)S(1)} %get-tuple-element.73), channel_id=1, source_target_pairs={{0,66},{1,49},{2,64},{3,51},{4,70},{5,53},{6,68},{7,55},{8,74},{9,... | collective-permute-start | bytes 12296 | tf_op jit(solution)/shard_map/ppermute | solution.py:31
  92.6 2.0 %collective-permute-start.24 = (f32[8,128]{1,0:T(8,128)S(1)}, f32[8,128]{1,0:T(8,128)S(1)}, u32[]{:S(2)}, u32[]{:S(2)}) collective-permute-start(f32[8,128]{1,0:T(8,128)S(1)} %get-tuple-element.73), channel_id=1, source_target_pairs={{0,2},{1,17},{2,0},{3,19},{4,6},{5,21},{6,4},{7,23},{8,10},{9,25},... | collective-permute-start | bytes 12296 | tf_op jit(solution)/shard_map/ppermute | solution.py:31
  94.8 1.7 %join.1 = (f32[288,352]{1,0:T(8,128)}, f32[288,352]{1,0:T(8,128)}) custom-call(s32[2]{0:T(128)S(1)} %pad_add_fusion.info_ref, f32[352,288]{1,0:T(8,128)S(1)} %get-tuple-element.80.own_ref, f32[352,288]{1,0:T(8,128)S(1)} %copy.8.got_ref), custom_call_target="tpu_custom_call" | custom-call | bytes 1622024 | tf_op jit(solution)/shard_map/join/pallas_call | solution.py:252
  (35 shorter events, 3.4 us)
Async XLA Ops:
  2.6 2.7 %collective-permute-start = (bf16[352,288]{1,0:T(8,128)(2,1)S(1)}, bf16[352,288]{1,0:T(8,128)(2,1)S(1)}, u32[]{:S(2)}, u32[]{:S(2)}) collective-permute-start(bf16[352,288]{1,0:T(8,128)(2,1)S(1)} %get-tuple-element.41), channel_id=1, source_target_pairs={{0,1},{1,0},{2,3},{3,2},{4,5},{5,4},{6,7},{7,6},{8,9},{9,8},{10,11... | collective-permute-start | bytes 608264 | tf_op jit(solution)/shard_map/ppermute | solution.py:31
  5.6 5.8 %collective-permute-start.6 = (bf16[88,576]{1,0:T(8,128)(2,1)S(1)}, bf16[88,576]{1,0:T(8,128)(2,1)S(1)}, u32[]{:S(2)}, u32[]{:S(2)}) collective-permute-start(bf16[88,576]{1,0:T(8,128)(2,1)S(1)} %get-tuple-element.83), channel_id=1, source_target_pairs={{0,2},{1,3},{2,0},{3,1},{4,6},{5,7},{6,4},{7,5},{8,10},{9,11},{10,... | collective-permute-start | bytes 304136 | tf_op jit(solution)/shard_map/ppermute | solution.py:31
  7.6 8.7 %collective-permute-start.2 = (bf16[88,1152]{1,0:T(8,128)(2,1)S(1)}, bf16[88,1152]{1,0:T(8,128)(2,1)S(1)}, u32[]{:S(2)}, u32[]{:S(2)}) collective-permute-start(bf16[88,1152]{1,0:T(8,128)(2,1)S(1)} %pad_maximum_fusion.4), channel_id=1, source_target_pairs={{0,32},{1,65},{2,34},{3,67},{4,36},{5,69},{6,38},{7,71},{8,40},{9,... | collective-permute-start | bytes 608264 | tf_op jit(solution)/shard_map/ppermute | solution.py:31
  11.0 6.6 %collective-permute-start.1 = (bf16[88,1152]{1,0:T(8,128)(2,1)S(1)}, bf16[88,1152]{1,0:T(8,128)(2,1)S(1)}, u32[]{:S(2)}, u32[]{:S(2)}) collective-permute-start(bf16[88,1152]{1,0:T(8,128)(2,1)S(1)} %pad_maximum_fusion.4), channel_id=1, source_target_pairs={{0,16},{1,3},{2,18},{3,1},{4,20},{5,7},{6,22},{7,5},{8,24},{9,11},... | collective-permute-start | bytes 608264 | tf_op jit(solution)/shard_map/ppermute | solution.py:31
  11.0 7.6 %collective-permute-start.3 = (bf16[88,1152]{1,0:T(8,128)(2,1)S(1)}, bf16[88,1152]{1,0:T(8,128)(2,1)S(1)}, u32[]{:S(2)}, u32[]{:S(2)}) collective-permute-start(bf16[88,1152]{1,0:T(8,128)(2,1)S(1)} %pad_maximum_fusion.4), channel_id=1, source_target_pairs={{0,48},{1,67},{2,50},{3,65},{4,52},{5,71},{6,54},{7,69},{8,56},{9,... | collective-permute-start | bytes 608264 | tf_op jit(solution)/shard_map/ppermute | solution.py:31
  11.5 11.1 %collective-permute-start.9 = (bf16[88,1152]{1,0:T(8,128)(2,1)S(1)}, bf16[88,1152]{1,0:T(8,128)(2,1)S(1)}, u32[]{:S(2)}, u32[]{:S(2)}) collective-permute-start(bf16[88,1152]{1,0:T(8,128)(2,1)S(1)} %pad_maximum_fusion.5), channel_id=1, source_target_pairs={{0,12},{1,13},{2,14},{3,15},{4,8},{5,9},{6,10},{7,11},{8,4},{9,5},... | collective-permute-start | bytes 608264 | tf_op jit(solution)/shard_map/ppermute | solution.py:31
  14.0 8.5 %collective-permute-start.8 = (bf16[88,1152]{1,0:T(8,128)(2,1)S(1)}, bf16[88,1152]{1,0:T(8,128)(2,1)S(1)}, u32[]{:S(2)}, u32[]{:S(2)}) collective-permute-start(bf16[88,1152]{1,0:T(8,128)(2,1)S(1)} %pad_maximum_fusion.5), channel_id=1, source_target_pairs={{0,8},{1,9},{2,10},{3,11},{4,12},{5,13},{6,14},{7,15},{8,0},{9,1},... | collective-permute-start | bytes 608264 | tf_op jit(solution)/shard_map/ppermute | solution.py:31
  16.3 7.0 %collective-permute-start.7 = (bf16[88,1152]{1,0:T(8,128)(2,1)S(1)}, bf16[88,1152]{1,0:T(8,128)(2,1)S(1)}, u32[]{:S(2)}, u32[]{:S(2)}) collective-permute-start(bf16[88,1152]{1,0:T(8,128)(2,1)S(1)} %pad_maximum_fusion.5), channel_id=1, source_target_pairs={{0,4},{1,5},{2,6},{3,7},{4,0},{5,1},{6,2},{7,3},{8,12},{9,13},{10,... | collective-permute-start | bytes 608264 | tf_op jit(solution)/shard_map/ppermute | solution.py:31
  18.7 12.8 %collective-permute-start.5 = (bf16[4,88,1152]{2,1,0:T(8,128)(2,1)S(1)}, bf16[4,88,1152]{2,1,0:T(8,128)(2,1)S(1)}, u32[]{:S(2)}, u32[]{:S(2)}) collective-permute-start(bf16[4,88,1152]{2,1,0:T(8,128)(2,1)S(1)} %pad_maximum_fusion.1.ta_ref), channel_id=1, source_target_pairs={{0,66},{1,49},{2,64},{3,51},{4,70},{5,53},{6,68},{7,55},{8,74},{9,... | collective-permute-start | bytes 2433032 | tf_op jit(solution)/shard_map/ppermute | solution.py:31
  21.5 11.4 %collective-permute-start.4 = (bf16[4,88,1152]{2,1,0:T(8,128)(2,1)S(1)}, bf16[4,88,1152]{2,1,0:T(8,128)(2,1)S(1)}, u32[]{:S(2)}, u32[]{:S(2)}) collective-permute-start(bf16[4,88,1152]{2,1,0:T(8,128)(2,1)S(1)} %pad_maximum_fusion.1.ta_ref), channel_id=1, source_target_pairs={{0,2},{1,17},{2,0},{3,19},{4,6},{5,21},{6,4},{7,23},{8,10},{9,25},... | collective-permute-start | bytes 2433032 | tf_op jit(solution)/shard_map/ppermute | solution.py:31
  23.4 9.5 %collective-permute-start.10 = (bf16[352,1152]{1,0:T(8,128)(2,1)S(1)}, bf16[352,1152]{1,0:T(8,128)(2,1)S(1)}, u32[]{:S(2)}, u32[]{:S(2)}) collective-permute-start(bf16[352,1152]{1,0:T(8,128)(2,1)S(1)} %pad_maximum_fusion.2.im0_ref), channel_id=1, source_target_pairs={{0,1},{1,0},{2,3},{3,2},{4,5},{5,4},{6,7},{7,6},{8,9},{9,8},{10,11... | collective-permute-start | bytes 2433032 | tf_op jit(solution)/shard_map/ppermute | solution.py:31
  26.6 14.8 %collective-permute-start.11 = (bf16[4,88,1152]{2,1,0:T(8,128)(2,1)S(1)}, bf16[4,88,1152]{2,1,0:T(8,128)(2,1)S(1)}, u32[]{:S(2)}, u32[]{:S(2)}) collective-permute-start(bf16[4,88,1152]{2,1,0:T(8,128)(2,1)S(1)} %pad_maximum_fusion.1.ta_ref), channel_id=1, source_target_pairs={{0,64},{1,33},{2,66},{3,35},{4,68},{5,37},{6,70},{7,39},{8,72},{9,... | collective-permute-start | bytes 2433032 | tf_op jit(solution)/shard_map/ppermute | solution.py:31
  38.6 11.9 %collective-permute-start.12 = (bf16[360,1152]{1,0:T(8,128)(2,1)S(1)}, bf16[360,1152]{1,0:T(8,128)(2,1)S(1)}, u32[]{:S(2)}, u32[]{:S(2)}) collective-permute-start(bf16[360,1152]{1,0:T(8,128)(2,1)S(1)} %get-tuple-element.52), channel_id=1, source_target_pairs={{0,2},{1,17},{2,0},{3,19},{4,6},{5,21},{6,4},{7,23},{8,10},{9,25},... | collective-permute-start | bytes 2488328 | tf_op jit(solution)/shard_map/ppermute | solution.py:31
  50.5 5.2 %collective-permute-start.13 = (f32[360,1152]{1,0:T(8,128)S(1)}, f32[360,1152]{1,0:T(8,128)S(1)}, u32[]{:S(2)}, u32[]{:S(2)}) collective-permute-start(f32[360,1152]{1,0:T(8,128)S(1)} %get-tuple-element.53), channel_id=1, source_target_pairs={{0,1},{1,0},{2,3},{3,2},{4,5},{5,4},{6,7},{7,6},{8,9},{9,8},{10,11... | collective-permute-start | bytes 4976648 | tf_op jit(solution)/shard_map/ppermute | solution.py:31
  52.6 20.6 %collective-permute-start.14 = (bf16[360,1152]{1,0:T(8,128)(2,1)S(1)}, bf16[360,1152]{1,0:T(8,128)(2,1)S(1)}, u32[]{:S(2)}, u32[]{:S(2)}) collective-permute-start(bf16[360,1152]{1,0:T(8,128)(2,1)S(1)} %get-tuple-element.59), channel_id=1, source_target_pairs={{0,64},{1,33},{2,66},{3,35},{4,68},{5,37},{6,70},{7,39},{8,72},{9,... | collective-permute-start | bytes 2488328 | tf_op jit(solution)/shard_map/ppermute | solution.py:31
  54.2 20.4 %collective-permute-start.15 = (bf16[360,1152]{1,0:T(8,128)(2,1)S(1)}, bf16[360,1152]{1,0:T(8,128)(2,1)S(1)}, u32[]{:S(2)}, u32[]{:S(2)}) collective-permute-start(bf16[360,1152]{1,0:T(8,128)(2,1)S(1)} %get-tuple-element.60), channel_id=1, source_target_pairs={{0,66},{1,49},{2,64},{3,51},{4,70},{5,53},{6,68},{7,55},{8,74},{9,... | collective-permute-start | bytes 2488328 | tf_op jit(solution)/shard_map/ppermute | solution.py:31
  56.7 6.5 %collective-permute-start.16 = (bf16[96,1152]{1,0:T(8,128)(2,1)S(1)}, bf16[96,1152]{1,0:T(8,128)(2,1)S(1)}, u32[]{:S(2)}, u32[]{:S(2)}) collective-permute-start(bf16[96,1152]{1,0:T(8,128)(2,1)S(1)} %get-tuple-element.54), channel_id=1, source_target_pairs={{0,4},{1,5},{2,6},{3,7},{4,0},{5,1},{6,2},{7,3},{8,12},{9,13},{10,... | collective-permute-start | bytes 663560 | tf_op jit(solution)/shard_map/ppermute | solution.py:31
  58.0 12.2 %collective-permute-start.17 = (bf16[96,1152]{1,0:T(8,128)(2,1)S(1)}, bf16[96,1152]{1,0:T(8,128)(2,1)S(1)}, u32[]{:S(2)}, u32[]{:S(2)}) collective-permute-start(bf16[96,1152]{1,0:T(8,128)(2,1)S(1)} %get-tuple-element.55), channel_id=1, source_target_pairs={{0,8},{1,9},{2,10},{3,11},{4,12},{5,13},{6,14},{7,15},{8,0},{9,1},... | collective-permute-start | bytes 663560 | tf_op jit(solution)/shard_map/ppermute | solution.py:31
  60.4 12.0 %collective-permute-start.18 = (bf16[96,1152]{1,0:T(8,128)(2,1)S(1)}, bf16[96,1152]{1,0:T(8,128)(2,1)S(1)}, u32[]{:S(2)}, u32[]{:S(2)}) collective-permute-start(bf16[96,1152]{1,0:T(8,128)(2,1)S(1)} %get-tuple-element.56), channel_id=1, source_target_pairs={{0,12},{1,13},{2,14},{3,15},{4,8},{5,9},{6,10},{7,11},{8,4},{9,5},... | collective-permute-start | bytes 663560 | tf_op jit(solution)/shard_map/ppermute | solution.py:31
  77.2 5.2 %collective-permute-start.19 = (bf16[96,1152]{1,0:T(8,128)(2,1)S(1)}, bf16[96,1152]{1,0:T(8,128)(2,1)S(1)}, u32[]{:S(2)}, u32[]{:S(2)}) collective-permute-start(bf16[96,1152]{1,0:T(8,128)(2,1)S(1)} %get-tuple-element.64), channel_id=1, source_target_pairs={{0,16},{1,3},{2,18},{3,1},{4,20},{5,7},{6,22},{7,5},{8,24},{9,11},... | collective-permute-start | bytes 663560 | tf_op jit(solution)/shard_map/ppermute | solution.py:31
  77.7 8.0 %collective-permute-start.20 = (bf16[96,1152]{1,0:T(8,128)(2,1)S(1)}, bf16[96,1152]{1,0:T(8,128)(2,1)S(1)}, u32[]{:S(2)}, u32[]{:S(2)}) collective-permute-start(bf16[96,1152]{1,0:T(8,128)(2,1)S(1)} %get-tuple-element.65), channel_id=1, source_target_pairs={{0,32},{1,65},{2,34},{3,67},{4,36},{5,69},{6,38},{7,71},{8,40},{9,... | collective-permute-start | bytes 663560 | tf_op jit(solution)/shard_map/ppermute | solution.py:31
  79.7 8.4 %collective-permute-start.21 = (bf16[96,1152]{1,0:T(8,128)(2,1)S(1)}, bf16[96,1152]{1,0:T(8,128)(2,1)S(1)}, u32[]{:S(2)}, u32[]{:S(2)}) collective-permute-start(bf16[96,1152]{1,0:T(8,128)(2,1)S(1)} %get-tuple-element.66), channel_id=1, source_target_pairs={{0,48},{1,67},{2,50},{3,65},{4,52},{5,71},{6,54},{7,69},{8,56},{9,... | collective-permute-start | bytes 663560 | tf_op jit(solution)/shard_map/ppermute | solution.py:31
  81.3 7.4 %collective-permute-start.22 = (f32[88,576]{1,0:T(8,128)S(1)}, f32[88,576]{1,0:T(8,128)S(1)}, u32[]{:S(2)}, u32[]{:S(2)}) collective-permute-start(f32[88,576]{1,0:T(8,128)S(1)} %slice.40), channel_id=1, source_target_pairs={{0,2},{1,3},{2,0},{3,1},{4,6},{5,7},{6,4},{7,5},{8,10},{9,11},{10,... | collective-permute-start | bytes 608264 | tf_op jit(solution)/shard_map/ppermute | solution.py:31
  89.3 5.3 %collective-permute-start.23 = (f32[352,288]{0,1:T(8,128)S(1)}, f32[352,288]{0,1:T(8,128)S(1)}, u32[]{:S(2)}, u32[]{:S(2)}) collective-permute-start(f32[352,288]{0,1:T(8,128)S(1)} %copy.7), channel_id=1, source_target_pairs={{0,1},{1,0},{2,3},{3,2},{4,5},{5,4},{6,7},{7,6},{8,9},{9,8},{10,11... | collective-permute-start | bytes 1216520 | tf_op jit(solution)/shard_map/ppermute | solution.py:31
  91.3 5.2 %collective-permute-start.26 = (f32[8,128]{1,0:T(8,128)S(1)}, f32[8,128]{1,0:T(8,128)S(1)}, u32[]{:S(2)}, u32[]{:S(2)}) collective-permute-start(f32[8,128]{1,0:T(8,128)S(1)} %get-tuple-element.73), channel_id=1, source_target_pairs={{0,66},{1,49},{2,64},{3,51},{4,70},{5,53},{6,68},{7,55},{8,74},{9,... | collective-permute-start | bytes 12296 | tf_op jit(solution)/shard_map/ppermute | solution.py:31
  92.5 4.0 %collective-permute-start.25 = (f32[8,128]{1,0:T(8,128)S(1)}, f32[8,128]{1,0:T(8,128)S(1)}, u32[]{:S(2)}, u32[]{:S(2)}) collective-permute-start(f32[8,128]{1,0:T(8,128)S(1)} %get-tuple-element.73), channel_id=1, source_target_pairs={{0,64},{1,33},{2,66},{3,35},{4,68},{5,37},{6,70},{7,39},{8,72},{9,... | collective-permute-start | bytes 12296 | tf_op jit(solution)/shard_map/ppermute | solution.py:31
  92.6 3.9 %collective-permute-start.24 = (f32[8,128]{1,0:T(8,128)S(1)}, f32[8,128]{1,0:T(8,128)S(1)}, u32[]{:S(2)}, u32[]{:S(2)}) collective-permute-start(f32[8,128]{1,0:T(8,128)S(1)} %get-tuple-element.73), channel_id=1, source_target_pairs={{0,2},{1,17},{2,0},{3,19},{4,6},{5,21},{6,4},{7,23},{8,10},{9,25},... | collective-permute-start | bytes 12296 | tf_op jit(solution)/shard_map/ppermute | solution.py:31

commit v19 on v18

--- a/solution.py
+++ b/solution.py
@@ -188,7 +188,7 @@
     return total, (own_ref[n : n + 1, :] + tails[0]) + (tails[1] + tails[2])
 
 
-def image_last_kernel(feats, scale_ref, own_ref, r1_ref, r2_ref, r3_ref, out_ref, sums_ref):
+def image_last_kernel(feats, scale_ref, own_ref, r2_ref, r3_ref, r1_ref, out_ref, sums_ref):
     total, sums = with_scalars(own_ref, (r1_ref, r2_ref, r3_ref))
     out_ref[...] = total * scale_ref[0]
     sums_ref[...] = jnp.broadcast_to(sums, (8, feats))
@@ -212,7 +212,7 @@
         m_ref[...] = message([total[(i + 1) * rows : (i + 2) * rows, :]], feats, split3(sums_ref[0:1, :]))
 
 
-def text_last_kernel(scale_ref, own_ref, r1_ref, r2_ref, r3_ref, out_ref, sums_ref):
+def text_last_kernel(scale_ref, own_ref, r2_ref, r3_ref, r1_ref, out_ref, sums_ref):
     total, sums = with_scalars(own_ref, (r1_ref, r2_ref, r3_ref))
     out_ref[...] = total * scale_ref[0]
     sums_ref[...] = jnp.broadcast_to(sums[:, :128], (8, 128))
@@ -309,7 +309,7 @@
     (text,) = call(text_near_kernel, "text_near", [f32(quarter, feats)], after(text, *messages), got1)
     img, sums = call(
         functools.partial(image_last_kernel, feats), "image_last", [f32(rows, feats), f32(8, feats)],
-        logit_scaler, img, *img_got, scalars=1,
+        logit_scaler, img, img_got[1], img_got[2], img_got[0], scalars=1,
     )
     text, *messages = call(
         functools.partial(text_first_kernel, rows, feats), "text_first",
@@ -318,7 +318,7 @@
     )
     got = [swap(m, y_mask(i), z_mask(i)) for i, m in zip((1, 2, 3), messages)]
     text, sums = call(
-        text_last_kernel, "text_last", [f32(rows, feats), f32(8, 128)], logit_scaler, text, *got, scalars=1, products=2
+        text_last_kernel, "text_last", [f32(rows, feats), f32(8, 128)], logit_scaler, text, got[1], got[2], got[0], scalars=1, products=2
     )
     image = jnp.concatenate(by(lo0, img[:, :half], after(swap(img[:, half:], z_mask(1)), text)), axis=0)
     whole = jnp.concatenate([text[:, :half], text[:, half:], image], axis=0)

time: 97.3 us -> 97 us (level)
  starting transfers between devices: 37 us -> 35.9 us
  waiting for transfers between devices: 30.5 us -> 31.6 us
    ppermute x27, starting transfers between devices: 37 us -> 35.9 us  [swap(): lax.ppermute(array, AXES, [(i, i ^ (mask1 if i & 1 else mask0)) for i in...]
    ppermute x27, waiting for transfers between devices: 30.5 us -> 31.6 us  [swap(): lax.ppermute(array, AXES, [(i, i ^ (mask1 if i & 1 else mask0)) for i in...]
  transfers between devices with their start and end apart: 27 -> 27, of which waited for: 17 -> 18; matrix products, arithmetic and copies ran while one was open for 1% -> 1% of each run, Pallas kernels for 21% -> 21%
where the time goes in v19:
time: 97 us; the launch traced here: 96.9 us
  starting transfers between devices  35.9 us (37%)
  waiting for transfers between devices  31.6 us (33%)
  Pallas kernels  23.9 us (25%)
  other arithmetic  2.43 us (3%)
  between operations  2.09 us (2%)
  local copies, waits for them, and re-layouts  1.05 us (1%)
    ppermute x27, starting transfers between devices, swap(): lax.ppermute(array, AXES, [(i, i ^ (mask1 if i & 1 else mask0)) for i in...  35.9 us
    ppermute x27, waiting for transfers between devices, swap(): lax.ppermute(array, AXES, [(i, i ^ (mask1 if i & 1 else mask0)) for i in...  31.6 us
    pallas_call x10, Pallas kernels, call(): pl.pallas_call(kernel, out_shape=out_shape, in_specs=[SMEM] * scalars + [...  23.9 us
  transfers between devices with their start and end apart: 27, of which 18 were waited for; matrix products, arithmetic and copies ran while one was open for 1% of the time, Pallas kernels for 21%

profile of v19, /device:TPU:1, one launch (start us, length us, event | category | flops | bytes accessed | tf_op | source)
XLA Modules:
  0.0 96.9 jit_solution(6389468282175749861)
XLA Ops:
  0.7 1.1 %pad_maximum_fusion.3.both_ref = bf16[576,352]{1,0:T(8,128)(2,1)S(1)} fusion(bf16[288,352]{1,0:T(8,128)(2,1)} %bitcast.13, bf16[288,352]{1,0:T(8,128)(2,1)} %bitcast.14), kind=kLoop, calls=%fused_computation.11 | loop fusion | flops 811008 | bytes 811008 | tf_op jit(solution)/shard_map/concatenate | solution.py:268
  1.8 0.8 split.1
  2.6 1.5 %collective-permute-start = (bf16[352,288]{1,0:T(8,128)(2,1)S(1)}, bf16[352,288]{1,0:T(8,128)(2,1)S(1)}, u32[]{:S(2)}, u32[]{:S(2)}) collective-permute-start(bf16[352,288]{1,0:T(8,128)(2,1)S(1)} %get-tuple-element.41), channel_id=1, source_target_pairs={{0,1},{1,0},{2,3},{3,2},{4,5},{5,4},{6,7},{7,6},{8,9},{9,8},{10,11... | collective-permute-start | bytes 608264 | tf_op jit(solution)/shard_map/ppermute | solution.py:31
  4.1 1.2 %collective-permute-done = bf16[352,288]{1,0:T(8,128)(2,1)S(1)} collective-permute-done((bf16[352,288]{1,0:T(8,128)(2,1)S(1)}, bf16[352,288]{1,0:T(8,128)(2,1)S(1)}, u32[]{:S(2)}, u32[]{:S(2)}) %collective-permute-start) | collective-permute-done | bytes 202784 | tf_op jit(solution)/shard_map/ppermute | solution.py:31
  5.6 1.8 %collective-permute-start.6 = (bf16[88,576]{1,0:T(8,128)(2,1)S(1)}, bf16[88,576]{1,0:T(8,128)(2,1)S(1)}, u32[]{:S(2)}, u32[]{:S(2)}) collective-permute-start(bf16[88,576]{1,0:T(8,128)(2,1)S(1)} %get-tuple-element.83), channel_id=1, source_target_pairs={{0,2},{1,3},{2,0},{3,1},{4,6},{5,7},{6,4},{7,5},{8,10},{9,11},{10,... | collective-permute-start | bytes 304136 | tf_op jit(solution)/shard_map/ppermute | solution.py:31
  7.6 3.4 %collective-permute-start.2 = (bf16[88,1152]{1,0:T(8,128)(2,1)S(1)}, bf16[88,1152]{1,0:T(8,128)(2,1)S(1)}, u32[]{:S(2)}, u32[]{:S(2)}) collective-permute-start(bf16[88,1152]{1,0:T(8,128)(2,1)S(1)} %pad_maximum_fusion.4), channel_id=1, source_target_pairs={{0,32},{1,65},{2,34},{3,67},{4,36},{5,69},{6,38},{7,71},{8,40},{9,... | collective-permute-start | bytes 608264 | tf_op jit(solution)/shard_map/ppermute | solution.py:31
  11.5 2.6 %collective-permute-start.9 = (bf16[88,1152]{1,0:T(8,128)(2,1)S(1)}, bf16[88,1152]{1,0:T(8,128)(2,1)S(1)}, u32[]{:S(2)}, u32[]{:S(2)}) collective-permute-start(bf16[88,1152]{1,0:T(8,128)(2,1)S(1)} %pad_maximum_fusion.5), channel_id=1, source_target_pairs={{0,12},{1,13},{2,14},{3,15},{4,8},{5,9},{6,10},{7,11},{8,4},{9,5},... | collective-permute-start | bytes 608264 | tf_op jit(solution)/shard_map/ppermute | solution.py:31
  14.0 0.5 collective-permute-start.8
  14.5 1.8 %collective-permute-done.2 = bf16[88,1152]{1,0:T(8,128)(2,1)S(1)} collective-permute-done((bf16[88,1152]{1,0:T(8,128)(2,1)S(1)}, bf16[88,1152]{1,0:T(8,128)(2,1)S(1)}, u32[]{:S(2)}, u32[]{:S(2)}) %collective-permute-start.2) | collective-permute-done | bytes 202784 | tf_op jit(solution)/shard_map/ppermute | solution.py:31
  16.3 1.2 %collective-permute-start.7 = (bf16[88,1152]{1,0:T(8,128)(2,1)S(1)}, bf16[88,1152]{1,0:T(8,128)(2,1)S(1)}, u32[]{:S(2)}, u32[]{:S(2)}) collective-permute-start(bf16[88,1152]{1,0:T(8,128)(2,1)S(1)} %pad_maximum_fusion.5), channel_id=1, source_target_pairs={{0,4},{1,5},{2,6},{3,7},{4,0},{5,1},{6,2},{7,3},{8,12},{9,13},{10,... | collective-permute-start | bytes 608264 | tf_op jit(solution)/shard_map/ppermute | solution.py:31
  17.5 1.0 %collective-permute-done.3 = bf16[88,1152]{1,0:T(8,128)(2,1)S(1)} collective-permute-done((bf16[88,1152]{1,0:T(8,128)(2,1)S(1)}, bf16[88,1152]{1,0:T(8,128)(2,1)S(1)}, u32[]{:S(2)}, u32[]{:S(2)}) %collective-permute-start.3) | collective-permute-done | bytes 202784 | tf_op jit(solution)/shard_map/ppermute | solution.py:31
  18.7 2.8 %collective-permute-start.5 = (bf16[4,88,1152]{2,1,0:T(8,128)(2,1)S(1)}, bf16[4,88,1152]{2,1,0:T(8,128)(2,1)S(1)}, u32[]{:S(2)}, u32[]{:S(2)}) collective-permute-start(bf16[4,88,1152]{2,1,0:T(8,128)(2,1)S(1)} %pad_maximum_fusion.1.ta_ref), channel_id=1, source_target_pairs={{0,66},{1,49},{2,64},{3,51},{4,70},{5,53},{6,68},{7,55},{8,74},{9,... | collective-permute-start | bytes 2433032 | tf_op jit(solution)/shard_map/ppermute | solution.py:31
  21.5 1.1 %collective-permute-done.9 = bf16[88,1152]{1,0:T(8,128)(2,1)S(1)} collective-permute-done((bf16[88,1152]{1,0:T(8,128)(2,1)S(1)}, bf16[88,1152]{1,0:T(8,128)(2,1)S(1)}, u32[]{:S(2)}, u32[]{:S(2)}) %collective-permute-start.9) | collective-permute-done | bytes 202784 | tf_op jit(solution)/shard_map/ppermute | solution.py:31
  22.6 0.8 collective-permute-done.7
  23.4 1.9 %collective-permute-start.10 = (bf16[352,1152]{1,0:T(8,128)(2,1)S(1)}, bf16[352,1152]{1,0:T(8,128)(2,1)S(1)}, u32[]{:S(2)}, u32[]{:S(2)}) collective-permute-start(bf16[352,1152]{1,0:T(8,128)(2,1)S(1)} %pad_maximum_fusion.2.im0_ref), channel_id=1, source_target_pairs={{0,1},{1,0},{2,3},{3,2},{4,5},{5,4},{6,7},{7,6},{8,9},{9,8},{10,11... | collective-permute-start | bytes 2433032 | tf_op jit(solution)/shard_map/ppermute | solution.py:31
  26.6 3.0 %collective-permute-start.11 = (bf16[4,88,1152]{2,1,0:T(8,128)(2,1)S(1)}, bf16[4,88,1152]{2,1,0:T(8,128)(2,1)S(1)}, u32[]{:S(2)}, u32[]{:S(2)}) collective-permute-start(bf16[4,88,1152]{2,1,0:T(8,128)(2,1)S(1)} %pad_maximum_fusion.1.ta_ref), channel_id=1, source_target_pairs={{0,64},{1,33},{2,66},{3,35},{4,68},{5,37},{6,70},{7,39},{8,72},{9,... | collective-permute-start | bytes 2433032 | tf_op jit(solution)/shard_map/ppermute | solution.py:31
  29.7 1.8 %collective-permute-done.5.tb_ref = bf16[4,88,1152]{2,1,0:T(8,128)(2,1)S(1)} collective-permute-done((bf16[4,88,1152]{2,1,0:T(8,128)(2,1)S(1)}, bf16[4,88,1152]{2,1,0:T(8,128)(2,1)S(1)}, u32[]{:S(2)}, u32[]{:S(2)}) %collective-permute-start.5) | collective-permute-done | bytes 811040 | tf_op jit(solution)/shard_map/ppermute | solution.py:31
  31.4 1.5 %collective-permute-done.4.tb_ref = bf16[4,88,1152]{2,1,0:T(8,128)(2,1)S(1)} collective-permute-done((bf16[4,88,1152]{2,1,0:T(8,128)(2,1)S(1)}, bf16[4,88,1152]{2,1,0:T(8,128)(2,1)S(1)}, u32[]{:S(2)}, u32[]{:S(2)}) %collective-permute-start.4) | collective-permute-done | bytes 811040 | tf_op jit(solution)/shard_map/ppermute | solution.py:31
  32.9 5.7 %tile_near.1 = (f32[2,4,88,1152]{3,2,1,0:T(8,128)S(1)}, bf16[360,1152]{1,0:T(8,128)(2,1)S(1)}, bf16[704,1152]{1,0:T(8,128)(2,1)S(1)}, bf16[704,704]{1,0:T(8,128)(2,1)S(1)}, f32[8,128]{1,0:T(8,128)S(1)}) custom-call(s32[2]{0:T(128)S(1)} %pad_add_fusion.info_ref, f32[2]{0:T(128)S(1)} %pad_maximum_fusion.7.scale_ref, ...), custom_call_target="tpu_custom_call" | custom-call | flops 2283798528 | bytes 9934864 | tf_op jit(solution)/shard_map/tile_near/pallas_call | solution.py:252
  38.9 1.6 %image_near.1.before_ref = f32[704,1152]{1,0:T(8,128)S(1)} custom-call(bf16[704,1152]{1,0:T(8,128)(2,1)S(1)} %get-tuple-element.45.t_rel, bf16[704,704]{1,0:T(8,128)(2,1)S(1)} %get-tuple-element.46.coeff_low), custom_call_target="tpu_custom_call" | custom-call | flops 1141899264 | bytes 5857280 | tf_op jit(solution)/shard_map/image_near/pallas_call | solution.py:252
  40.5 0.9 collective-permute-done.11.ta_ref
  41.4 8.5 %tile_far.1 = (bf16[360,1152]{1,0:T(8,128)(2,1)S(1)}, bf16[360,1152]{1,0:T(8,128)(2,1)S(1)}, f32[360,1152]{1,0:T(8,128)S(1)}, f32[360,1152]{1,0:T(8,128)S(1)}) custom-call(s32[2]{0:T(128)S(1)} %pad_add_fusion.info_ref, f32[2]{0:T(128)S(1)} %pad_maximum_fusion.7.scale_ref, bf16[4,88,1152]{2,1,0:T(8,128)(2,1)S(1)} %collective-permute-done.11.ta_ref, ...), custom_call_target="tpu_custom_call" | custom-call | flops 3425697792 | bytes 11468816 | tf_op jit(solution)/shard_map/tile_far/pallas_call | solution.py:252
  49.9 0.6 collective-permute-done.12.r1_ref
  50.5 2.1 %collective-permute-start.13 = (f32[360,1152]{1,0:T(8,128)S(1)}, f32[360,1152]{1,0:T(8,128)S(1)}, u32[]{:S(2)}, u32[]{:S(2)}) collective-permute-start(f32[360,1152]{1,0:T(8,128)S(1)} %get-tuple-element.53), channel_id=1, source_target_pairs={{0,1},{1,0},{2,3},{3,2},{4,5},{5,4},{6,7},{7,6},{8,9},{9,8},{10,11... | collective-permute-start | bytes 4976648 | tf_op jit(solution)/shard_map/ppermute | solution.py:31
  52.6 1.6 %collective-permute-start.14 = (bf16[360,1152]{1,0:T(8,128)(2,1)S(1)}, bf16[360,1152]{1,0:T(8,128)(2,1)S(1)}, u32[]{:S(2)}, u32[]{:S(2)}) collective-permute-start(bf16[360,1152]{1,0:T(8,128)(2,1)S(1)} %get-tuple-element.59), channel_id=1, source_target_pairs={{0,64},{1,33},{2,66},{3,35},{4,68},{5,37},{6,70},{7,39},{8,72},{9,... | collective-permute-start | bytes 2488328 | tf_op jit(solution)/shard_map/ppermute | solution.py:31
  54.2 0.8 collective-permute-start.15
  55.0 0.7 collective-permute-done.13.other_ref
  55.7 1.0 %image_first.1 = (f32[96,1152]{1,0:T(8,128)S(1)}, bf16[96,1152]{1,0:T(8,128)(2,1)S(1)}, bf16[96,1152]{1,0:T(8,128)(2,1)S(1)}, bf16[96,1152]{1,0:T(8,128)(2,1)S(1)}) custom-call(f32[360,1152]{1,0:T(8,128)S(1)} %get-tuple-element.50.own_ref, f32[360,1152]{1,0:T(8,128)S(1)} %collective-permute-done.13.other_ref), custom_call_target="tpu_custom_call" | custom-call | bytes 4423680 | tf_op jit(solution)/shard_map/image_first/pallas_call | solution.py:252
  56.7 1.3 %collective-permute-start.18 = (bf16[96,1152]{1,0:T(8,128)(2,1)S(1)}, bf16[96,1152]{1,0:T(8,128)(2,1)S(1)}, u32[]{:S(2)}, u32[]{:S(2)}) collective-permute-start(bf16[96,1152]{1,0:T(8,128)(2,1)S(1)} %get-tuple-element.54), channel_id=1, source_target_pairs={{0,4},{1,5},{2,6},{3,7},{4,0},{5,1},{6,2},{7,3},{8,12},{9,13},{10,... | collective-permute-start | bytes 663560 | tf_op jit(solution)/shard_map/ppermute | solution.py:31
  58.0 2.5 %collective-permute-start.16 = (bf16[96,1152]{1,0:T(8,128)(2,1)S(1)}, bf16[96,1152]{1,0:T(8,128)(2,1)S(1)}, u32[]{:S(2)}, u32[]{:S(2)}) collective-permute-start(bf16[96,1152]{1,0:T(8,128)(2,1)S(1)} %get-tuple-element.55), channel_id=1, source_target_pairs={{0,8},{1,9},{2,10},{3,11},{4,12},{5,13},{6,14},{7,15},{8,0},{9,1},... | collective-permute-start | bytes 663560 | tf_op jit(solution)/shard_map/ppermute | solution.py:31
  60.6 0.8 text_near.1.own_ref
  61.4 1.8 %collective-permute-done.18.r1_ref = bf16[96,1152]{1,0:T(8,128)(2,1)S(1)} collective-permute-done((bf16[96,1152]{1,0:T(8,128)(2,1)S(1)}, bf16[96,1152]{1,0:T(8,128)(2,1)S(1)}, u32[]{:S(2)}, u32[]{:S(2)}) %collective-permute-start.18) | collective-permute-done | bytes 221216 | tf_op jit(solution)/shard_map/ppermute | solution.py:31
  63.2 7.0 %collective-permute-done.16.r2_ref = bf16[96,1152]{1,0:T(8,128)(2,1)S(1)} collective-permute-done((bf16[96,1152]{1,0:T(8,128)(2,1)S(1)}, bf16[96,1152]{1,0:T(8,128)(2,1)S(1)}, u32[]{:S(2)}, u32[]{:S(2)}) %collective-permute-start.16) | collective-permute-done | bytes 221216 | tf_op jit(solution)/shard_map/ppermute | solution.py:31
  70.2 2.3 %collective-permute-done.17.r3_ref = bf16[96,1152]{1,0:T(8,128)(2,1)S(1)} collective-permute-done((bf16[96,1152]{1,0:T(8,128)(2,1)S(1)}, bf16[96,1152]{1,0:T(8,128)(2,1)S(1)}, u32[]{:S(2)}, u32[]{:S(2)}) %collective-permute-start.17) | collective-permute-done | bytes 221216 | tf_op jit(solution)/shard_map/ppermute | solution.py:31
  72.5 0.6 image_last.1
  73.1 1.4 %collective-permute-done.15.r3_ref = bf16[360,1152]{1,0:T(8,128)(2,1)S(1)} collective-permute-done((bf16[360,1152]{1,0:T(8,128)(2,1)S(1)}, bf16[360,1152]{1,0:T(8,128)(2,1)S(1)}, u32[]{:S(2)}, u32[]{:S(2)}) %collective-permute-start.15) | collective-permute-done | bytes 829472 | tf_op jit(solution)/shard_map/ppermute | solution.py:31
  74.5 2.6 %text_first.1 = (f32[96,1152]{1,0:T(8,128)S(1)}, bf16[96,1152]{1,0:T(8,128)(2,1)S(1)}, bf16[96,1152]{1,0:T(8,128)(2,1)S(1)}, bf16[96,1152]{1,0:T(8,128)(2,1)S(1)}) custom-call(f32[352,1152]{1,0:T(8,128)S(1)} %text_near.1.own_ref, bf16[360,1152]{1,0:T(8,128)(2,1)S(1)} %collective-permute-done.14.r2_ref, bf16[360,1152]{1,0:T(8,128)(2,1)S(1)} %collective-permute-done.15.r3_ref, ...), custom_call_target="tpu_custom_call" | custom-call | bytes 4423680 | tf_op jit(solution)/shard_map/text_first/pallas_call | solution.py:252
  77.2 0.8 collective-permute-start.19
  78.0 2.1 %collective-permute-start.20 = (bf16[96,1152]{1,0:T(8,128)(2,1)S(1)}, bf16[96,1152]{1,0:T(8,128)(2,1)S(1)}, u32[]{:S(2)}, u32[]{:S(2)}) collective-permute-start(bf16[96,1152]{1,0:T(8,128)(2,1)S(1)} %get-tuple-element.65), channel_id=1, source_target_pairs={{0,48},{1,67},{2,50},{3,65},{4,52},{5,71},{6,54},{7,69},{8,56},{9,... | collective-permute-start | bytes 663560 | tf_op jit(solution)/shard_map/ppermute | solution.py:31
  80.2 1.5 %collective-permute-start.22 = (f32[88,576]{1,0:T(8,128)S(1)}, f32[88,576]{1,0:T(8,128)S(1)}, u32[]{:S(2)}, u32[]{:S(2)}) collective-permute-start(f32[88,576]{1,0:T(8,128)S(1)} %slice.40), channel_id=1, source_target_pairs={{0,2},{1,3},{2,0},{3,1},{4,6},{5,7},{6,4},{7,5},{8,10},{9,11},{10,... | collective-permute-start | bytes 608264 | tf_op jit(solution)/shard_map/ppermute | solution.py:31
  81.8 2.1 %collective-permute-done.19.r2_ref = bf16[96,1152]{1,0:T(8,128)(2,1)S(1)} collective-permute-done((bf16[96,1152]{1,0:T(8,128)(2,1)S(1)}, bf16[96,1152]{1,0:T(8,128)(2,1)S(1)}, u32[]{:S(2)}, u32[]{:S(2)}) %collective-permute-start.19) | collective-permute-done | bytes 221216 | tf_op jit(solution)/shard_map/ppermute | solution.py:31
  83.9 2.3 %collective-permute-done.20.r3_ref = bf16[96,1152]{1,0:T(8,128)(2,1)S(1)} collective-permute-done((bf16[96,1152]{1,0:T(8,128)(2,1)S(1)}, bf16[96,1152]{1,0:T(8,128)(2,1)S(1)}, u32[]{:S(2)}, u32[]{:S(2)}) %collective-permute-start.20) | collective-permute-done | bytes 221216 | tf_op jit(solution)/shard_map/ppermute | solution.py:31
  86.2 0.6 text_last.1
  86.9 3.0 %collective-permute-done.22 = f32[88,576]{1,0:T(8,128)S(1)} collective-permute-done((f32[88,576]{1,0:T(8,128)S(1)}, f32[88,576]{1,0:T(8,128)S(1)}, u32[]{:S(2)}, u32[]{:S(2)}) %collective-permute-start.22) | collective-permute-done | bytes 202784 | tf_op jit(solution)/shard_map/ppermute | solution.py:31
  91.0 1.5 %collective-permute-start.26 = (f32[8,128]{1,0:T(8,128)S(1)}, f32[8,128]{1,0:T(8,128)S(1)}, u32[]{:S(2)}, u32[]{:S(2)}) collective-permute-start(f32[8,128]{1,0:T(8,128)S(1)} %get-tuple-element.73), channel_id=1, source_target_pairs={{0,66},{1,49},{2,64},{3,51},{4,70},{5,53},{6,68},{7,55},{8,74},{9,... | collective-permute-start | bytes 12296 | tf_op jit(solution)/shard_map/ppermute | solution.py:31
  92.4 0.8 collective-permute-start.25
  93.2 1.0 %collective-permute-start.24 = (f32[8,128]{1,0:T(8,128)S(1)}, f32[8,128]{1,0:T(8,128)S(1)}, u32[]{:S(2)}, u32[]{:S(2)}) collective-permute-start(f32[8,128]{1,0:T(8,128)S(1)} %get-tuple-element.73), channel_id=1, source_target_pairs={{0,2},{1,17},{2,0},{3,19},{4,6},{5,21},{6,4},{7,23},{8,10},{9,25},... | collective-permute-start | bytes 12296 | tf_op jit(solution)/shard_map/ppermute | solution.py:31
  94.4 1.7 %join.1 = (f32[288,352]{1,0:T(8,128)}, f32[288,352]{1,0:T(8,128)}) custom-call(s32[2]{0:T(128)S(1)} %pad_add_fusion.info_ref, f32[352,288]{1,0:T(8,128)S(1)} %get-tuple-element.80.own_ref, f32[352,288]{1,0:T(8,128)S(1)} %copy.8.got_ref), custom_call_target="tpu_custom_call" | custom-call | bytes 1622024 | tf_op jit(solution)/shard_map/join/pallas_call | solution.py:252
  (35 shorter events, 4.0 us)
Async XLA Ops:
  2.6 2.7 %collective-permute-start = (bf16[352,288]{1,0:T(8,128)(2,1)S(1)}, bf16[352,288]{1,0:T(8,128)(2,1)S(1)}, u32[]{:S(2)}, u32[]{:S(2)}) collective-permute-start(bf16[352,288]{1,0:T(8,128)(2,1)S(1)} %get-tuple-element.41), channel_id=1, source_target_pairs={{0,1},{1,0},{2,3},{3,2},{4,5},{5,4},{6,7},{7,6},{8,9},{9,8},{10,11... | collective-permute-start | bytes 608264 | tf_op jit(solution)/shard_map/ppermute | solution.py:31
  5.6 5.8 %collective-permute-start.6 = (bf16[88,576]{1,0:T(8,128)(2,1)S(1)}, bf16[88,576]{1,0:T(8,128)(2,1)S(1)}, u32[]{:S(2)}, u32[]{:S(2)}) collective-permute-start(bf16[88,576]{1,0:T(8,128)(2,1)S(1)} %get-tuple-element.83), channel_id=1, source_target_pairs={{0,2},{1,3},{2,0},{3,1},{4,6},{5,7},{6,4},{7,5},{8,10},{9,11},{10,... | collective-permute-start | bytes 304136 | tf_op jit(solution)/shard_map/ppermute | solution.py:31
  7.6 8.7 %collective-permute-start.2 = (bf16[88,1152]{1,0:T(8,128)(2,1)S(1)}, bf16[88,1152]{1,0:T(8,128)(2,1)S(1)}, u32[]{:S(2)}, u32[]{:S(2)}) collective-permute-start(bf16[88,1152]{1,0:T(8,128)(2,1)S(1)} %pad_maximum_fusion.4), channel_id=1, source_target_pairs={{0,32},{1,65},{2,34},{3,67},{4,36},{5,69},{6,38},{7,71},{8,40},{9,... | collective-permute-start | bytes 608264 | tf_op jit(solution)/shard_map/ppermute | solution.py:31
  11.0 6.6 %collective-permute-start.1 = (bf16[88,1152]{1,0:T(8,128)(2,1)S(1)}, bf16[88,1152]{1,0:T(8,128)(2,1)S(1)}, u32[]{:S(2)}, u32[]{:S(2)}) collective-permute-start(bf16[88,1152]{1,0:T(8,128)(2,1)S(1)} %pad_maximum_fusion.4), channel_id=1, source_target_pairs={{0,16},{1,3},{2,18},{3,1},{4,20},{5,7},{6,22},{7,5},{8,24},{9,11},... | collective-permute-start | bytes 608264 | tf_op jit(solution)/shard_map/ppermute | solution.py:31
  11.0 7.6 %collective-permute-start.3 = (bf16[88,1152]{1,0:T(8,128)(2,1)S(1)}, bf16[88,1152]{1,0:T(8,128)(2,1)S(1)}, u32[]{:S(2)}, u32[]{:S(2)}) collective-permute-start(bf16[88,1152]{1,0:T(8,128)(2,1)S(1)} %pad_maximum_fusion.4), channel_id=1, source_target_pairs={{0,48},{1,67},{2,50},{3,65},{4,52},{5,71},{6,54},{7,69},{8,56},{9,... | collective-permute-start | bytes 608264 | tf_op jit(solution)/shard_map/ppermute | solution.py:31
  11.5 11.1 %collective-permute-start.9 = (bf16[88,1152]{1,0:T(8,128)(2,1)S(1)}, bf16[88,1152]{1,0:T(8,128)(2,1)S(1)}, u32[]{:S(2)}, u32[]{:S(2)}) collective-permute-start(bf16[88,1152]{1,0:T(8,128)(2,1)S(1)} %pad_maximum_fusion.5), channel_id=1, source_target_pairs={{0,12},{1,13},{2,14},{3,15},{4,8},{5,9},{6,10},{7,11},{8,4},{9,5},... | collective-permute-start | bytes 608264 | tf_op jit(solution)/shard_map/ppermute | solution.py:31
  14.0 8.5 %collective-permute-start.8 = (bf16[88,1152]{1,0:T(8,128)(2,1)S(1)}, bf16[88,1152]{1,0:T(8,128)(2,1)S(1)}, u32[]{:S(2)}, u32[]{:S(2)}) collective-permute-start(bf16[88,1152]{1,0:T(8,128)(2,1)S(1)} %pad_maximum_fusion.5), channel_id=1, source_target_pairs={{0,8},{1,9},{2,10},{3,11},{4,12},{5,13},{6,14},{7,15},{8,0},{9,1},... | collective-permute-start | bytes 608264 | tf_op jit(solution)/shard_map/ppermute | solution.py:31
  16.3 7.0 %collective-permute-start.7 = (bf16[88,1152]{1,0:T(8,128)(2,1)S(1)}, bf16[88,1152]{1,0:T(8,128)(2,1)S(1)}, u32[]{:S(2)}, u32[]{:S(2)}) collective-permute-start(bf16[88,1152]{1,0:T(8,128)(2,1)S(1)} %pad_maximum_fusion.5), channel_id=1, source_target_pairs={{0,4},{1,5},{2,6},{3,7},{4,0},{5,1},{6,2},{7,3},{8,12},{9,13},{10,... | collective-permute-start | bytes 608264 | tf_op jit(solution)/shard_map/ppermute | solution.py:31
  18.7 12.8 %collective-permute-start.5 = (bf16[4,88,1152]{2,1,0:T(8,128)(2,1)S(1)}, bf16[4,88,1152]{2,1,0:T(8,128)(2,1)S(1)}, u32[]{:S(2)}, u32[]{:S(2)}) collective-permute-start(bf16[4,88,1152]{2,1,0:T(8,128)(2,1)S(1)} %pad_maximum_fusion.1.ta_ref), channel_id=1, source_target_pairs={{0,66},{1,49},{2,64},{3,51},{4,70},{5,53},{6,68},{7,55},{8,74},{9,... | collective-permute-start | bytes 2433032 | tf_op jit(solution)/shard_map/ppermute | solution.py:31
  21.5 11.4 %collective-permute-start.4 = (bf16[4,88,1152]{2,1,0:T(8,128)(2,1)S(1)}, bf16[4,88,1152]{2,1,0:T(8,128)(2,1)S(1)}, u32[]{:S(2)}, u32[]{:S(2)}) collective-permute-start(bf16[4,88,1152]{2,1,0:T(8,128)(2,1)S(1)} %pad_maximum_fusion.1.ta_ref), channel_id=1, source_target_pairs={{0,2},{1,17},{2,0},{3,19},{4,6},{5,21},{6,4},{7,23},{8,10},{9,25},... | collective-permute-start | bytes 2433032 | tf_op jit(solution)/shard_map/ppermute | solution.py:31
  23.4 9.5 %collective-permute-start.10 = (bf16[352,1152]{1,0:T(8,128)(2,1)S(1)}, bf16[352,1152]{1,0:T(8,128)(2,1)S(1)}, u32[]{:S(2)}, u32[]{:S(2)}) collective-permute-start(bf16[352,1152]{1,0:T(8,128)(2,1)S(1)} %pad_maximum_fusion.2.im0_ref), channel_id=1, source_target_pairs={{0,1},{1,0},{2,3},{3,2},{4,5},{5,4},{6,7},{7,6},{8,9},{9,8},{10,11... | collective-permute-start | bytes 2433032 | tf_op jit(solution)/shard_map/ppermute | solution.py:31
  26.6 14.8 %collective-permute-start.11 = (bf16[4,88,1152]{2,1,0:T(8,128)(2,1)S(1)}, bf16[4,88,1152]{2,1,0:T(8,128)(2,1)S(1)}, u32[]{:S(2)}, u32[]{:S(2)}) collective-permute-start(bf16[4,88,1152]{2,1,0:T(8,128)(2,1)S(1)} %pad_maximum_fusion.1.ta_ref), channel_id=1, source_target_pairs={{0,64},{1,33},{2,66},{3,35},{4,68},{5,37},{6,70},{7,39},{8,72},{9,... | collective-permute-start | bytes 2433032 | tf_op jit(solution)/shard_map/ppermute | solution.py:31
  38.6 11.9 %collective-permute-start.12 = (bf16[360,1152]{1,0:T(8,128)(2,1)S(1)}, bf16[360,1152]{1,0:T(8,128)(2,1)S(1)}, u32[]{:S(2)}, u32[]{:S(2)}) collective-permute-start(bf16[360,1152]{1,0:T(8,128)(2,1)S(1)} %get-tuple-element.52), channel_id=1, source_target_pairs={{0,2},{1,17},{2,0},{3,19},{4,6},{5,21},{6,4},{7,23},{8,10},{9,25},... | collective-permute-start | bytes 2488328 | tf_op jit(solution)/shard_map/ppermute | solution.py:31
  50.5 5.2 %collective-permute-start.13 = (f32[360,1152]{1,0:T(8,128)S(1)}, f32[360,1152]{1,0:T(8,128)S(1)}, u32[]{:S(2)}, u32[]{:S(2)}) collective-permute-start(f32[360,1152]{1,0:T(8,128)S(1)} %get-tuple-element.53), channel_id=1, source_target_pairs={{0,1},{1,0},{2,3},{3,2},{4,5},{5,4},{6,7},{7,6},{8,9},{9,8},{10,11... | collective-permute-start | bytes 4976648 | tf_op jit(solution)/shard_map/ppermute | solution.py:31
  52.6 20.6 %collective-permute-start.14 = (bf16[360,1152]{1,0:T(8,128)(2,1)S(1)}, bf16[360,1152]{1,0:T(8,128)(2,1)S(1)}, u32[]{:S(2)}, u32[]{:S(2)}) collective-permute-start(bf16[360,1152]{1,0:T(8,128)(2,1)S(1)} %get-tuple-element.59), channel_id=1, source_target_pairs={{0,64},{1,33},{2,66},{3,35},{4,68},{5,37},{6,70},{7,39},{8,72},{9,... | collective-permute-start | bytes 2488328 | tf_op jit(solution)/shard_map/ppermute | solution.py:31
  54.2 20.4 %collective-permute-start.15 = (bf16[360,1152]{1,0:T(8,128)(2,1)S(1)}, bf16[360,1152]{1,0:T(8,128)(2,1)S(1)}, u32[]{:S(2)}, u32[]{:S(2)}) collective-permute-start(bf16[360,1152]{1,0:T(8,128)(2,1)S(1)} %get-tuple-element.60), channel_id=1, source_target_pairs={{0,66},{1,49},{2,64},{3,51},{4,70},{5,53},{6,68},{7,55},{8,74},{9,... | collective-permute-start | bytes 2488328 | tf_op jit(solution)/shard_map/ppermute | solution.py:31
  56.7 6.5 %collective-permute-start.18 = (bf16[96,1152]{1,0:T(8,128)(2,1)S(1)}, bf16[96,1152]{1,0:T(8,128)(2,1)S(1)}, u32[]{:S(2)}, u32[]{:S(2)}) collective-permute-start(bf16[96,1152]{1,0:T(8,128)(2,1)S(1)} %get-tuple-element.54), channel_id=1, source_target_pairs={{0,4},{1,5},{2,6},{3,7},{4,0},{5,1},{6,2},{7,3},{8,12},{9,13},{10,... | collective-permute-start | bytes 663560 | tf_op jit(solution)/shard_map/ppermute | solution.py:31
  58.0 12.2 %collective-permute-start.16 = (bf16[96,1152]{1,0:T(8,128)(2,1)S(1)}, bf16[96,1152]{1,0:T(8,128)(2,1)S(1)}, u32[]{:S(2)}, u32[]{:S(2)}) collective-permute-start(bf16[96,1152]{1,0:T(8,128)(2,1)S(1)} %get-tuple-element.55), channel_id=1, source_target_pairs={{0,8},{1,9},{2,10},{3,11},{4,12},{5,13},{6,14},{7,15},{8,0},{9,1},... | collective-permute-start | bytes 663560 | tf_op jit(solution)/shard_map/ppermute | solution.py:31
  60.4 12.0 %collective-permute-start.17 = (bf16[96,1152]{1,0:T(8,128)(2,1)S(1)}, bf16[96,1152]{1,0:T(8,128)(2,1)S(1)}, u32[]{:S(2)}, u32[]{:S(2)}) collective-permute-start(bf16[96,1152]{1,0:T(8,128)(2,1)S(1)} %get-tuple-element.56), channel_id=1, source_target_pairs={{0,12},{1,13},{2,14},{3,15},{4,8},{5,9},{6,10},{7,11},{8,4},{9,5},... | collective-permute-start | bytes 663560 | tf_op jit(solution)/shard_map/ppermute | solution.py:31
  77.2 6.7 %collective-permute-start.19 = (bf16[96,1152]{1,0:T(8,128)(2,1)S(1)}, bf16[96,1152]{1,0:T(8,128)(2,1)S(1)}, u32[]{:S(2)}, u32[]{:S(2)}) collective-permute-start(bf16[96,1152]{1,0:T(8,128)(2,1)S(1)} %get-tuple-element.64), channel_id=1, source_target_pairs={{0,32},{1,65},{2,34},{3,67},{4,36},{5,69},{6,38},{7,71},{8,40},{9,... | collective-permute-start | bytes 663560 | tf_op jit(solution)/shard_map/ppermute | solution.py:31
  78.0 8.2 %collective-permute-start.20 = (bf16[96,1152]{1,0:T(8,128)(2,1)S(1)}, bf16[96,1152]{1,0:T(8,128)(2,1)S(1)}, u32[]{:S(2)}, u32[]{:S(2)}) collective-permute-start(bf16[96,1152]{1,0:T(8,128)(2,1)S(1)} %get-tuple-element.65), channel_id=1, source_target_pairs={{0,48},{1,67},{2,50},{3,65},{4,52},{5,71},{6,54},{7,69},{8,56},{9,... | collective-permute-start | bytes 663560 | tf_op jit(solution)/shard_map/ppermute | solution.py:31
  80.1 6.1 %collective-permute-start.21 = (bf16[96,1152]{1,0:T(8,128)(2,1)S(1)}, bf16[96,1152]{1,0:T(8,128)(2,1)S(1)}, u32[]{:S(2)}, u32[]{:S(2)}) collective-permute-start(bf16[96,1152]{1,0:T(8,128)(2,1)S(1)} %get-tuple-element.66), channel_id=1, source_target_pairs={{0,16},{1,3},{2,18},{3,1},{4,20},{5,7},{6,22},{7,5},{8,24},{9,11},... | collective-permute-start | bytes 663560 | tf_op jit(solution)/shard_map/ppermute | solution.py:31
  80.2 9.6 %collective-permute-start.22 = (f32[88,576]{1,0:T(8,128)S(1)}, f32[88,576]{1,0:T(8,128)S(1)}, u32[]{:S(2)}, u32[]{:S(2)}) collective-permute-start(f32[88,576]{1,0:T(8,128)S(1)} %slice.40), channel_id=1, source_target_pairs={{0,2},{1,3},{2,0},{3,1},{4,6},{5,7},{6,4},{7,5},{8,10},{9,11},{10,... | collective-permute-start | bytes 608264 | tf_op jit(solution)/shard_map/ppermute | solution.py:31
  90.5 3.7 %collective-permute-start.23 = (f32[352,288]{0,1:T(8,128)S(1)}, f32[352,288]{0,1:T(8,128)S(1)}, u32[]{:S(2)}, u32[]{:S(2)}) collective-permute-start(f32[352,288]{0,1:T(8,128)S(1)} %copy.7), channel_id=1, source_target_pairs={{0,1},{1,0},{2,3},{3,2},{4,5},{5,4},{6,7},{7,6},{8,9},{9,8},{10,11... | collective-permute-start | bytes 1216520 | tf_op jit(solution)/shard_map/ppermute | solution.py:31
  91.0 5.2 %collective-permute-start.26 = (f32[8,128]{1,0:T(8,128)S(1)}, f32[8,128]{1,0:T(8,128)S(1)}, u32[]{:S(2)}, u32[]{:S(2)}) collective-permute-start(f32[8,128]{1,0:T(8,128)S(1)} %get-tuple-element.73), channel_id=1, source_target_pairs={{0,66},{1,49},{2,64},{3,51},{4,70},{5,53},{6,68},{7,55},{8,74},{9,... | collective-permute-start | bytes 12296 | tf_op jit(solution)/shard_map/ppermute | solution.py:31
  92.4 4.0 %collective-permute-start.25 = (f32[8,128]{1,0:T(8,128)S(1)}, f32[8,128]{1,0:T(8,128)S(1)}, u32[]{:S(2)}, u32[]{:S(2)}) collective-permute-start(f32[8,128]{1,0:T(8,128)S(1)} %get-tuple-element.73), channel_id=1, source_target_pairs={{0,64},{1,33},{2,66},{3,35},{4,68},{5,37},{6,70},{7,39},{8,72},{9,... | collective-permute-start | bytes 12296 | tf_op jit(solution)/shard_map/ppermute | solution.py:31
  93.2 3.2 %collective-permute-start.24 = (f32[8,128]{1,0:T(8,128)S(1)}, f32[8,128]{1,0:T(8,128)S(1)}, u32[]{:S(2)}, u32[]{:S(2)}) collective-permute-start(f32[8,128]{1,0:T(8,128)S(1)} %get-tuple-element.73), channel_id=1, source_target_pairs={{0,2},{1,17},{2,0},{3,19},{4,6},{5,21},{6,4},{7,23},{8,10},{9,25},... | collective-permute-start | bytes 12296 | tf_op jit(solution)/shard_map/ppermute | solution.py:31

commit v20 on v19

--- a/solution.py
+++ b/solution.py
@@ -317,10 +317,12 @@
         scratch=[pltpu.VMEM((quarter, feats), F32)],
     )
     got = [swap(m, y_mask(i), z_mask(i)) for i, m in zip((1, 2, 3), messages)]
+    back = swap(img[:, half:], z_mask(1))
+    got[1] = after(got[1], back)
     text, sums = call(
         text_last_kernel, "text_last", [f32(rows, feats), f32(8, 128)], logit_scaler, text, got[1], got[2], got[0], scalars=1, products=2
     )
-    image = jnp.concatenate(by(lo0, img[:, :half], after(swap(img[:, half:], z_mask(1)), text)), axis=0)
+    image = jnp.concatenate(by(lo0, img[:, :half], back), axis=0)
     whole = jnp.concatenate([text[:, :half], text[:, half:], image], axis=0)
     mine, other = by(on0, whole[:, :width], whole[:, width:])
     sums = after(sums, other)

time: 97 us -> 97 us (level)
  waiting for transfers between devices: 31.6 us -> 29.1 us
  starting transfers between devices: 35.9 us -> 38.2 us
    ppermute x27, waiting for transfers between devices: 31.6 us -> 29.1 us  [swap(): lax.ppermute(array, AXES, [(i, i ^ (mask1 if i & 1 else mask0)) for i in...]
    ppermute x27, starting transfers between devices: 35.9 us -> 38.2 us  [swap(): lax.ppermute(array, AXES, [(i, i ^ (mask1 if i & 1 else mask0)) for i in...]
  transfers between devices with their start and end apart: 27 -> 27, of which waited for: 18 -> 16; matrix products, arithmetic and copies ran while one was open for 1% -> 1% of each run, Pallas kernels for 21% -> 23%
where the time goes in v20:
time: 97 us; the launch traced here: 96.8 us
  starting transfers between devices  38.2 us (39%)
  waiting for transfers between devices  29.1 us (30%)
  Pallas kernels  23.9 us (25%)
  other arithmetic  2.33 us (2%)
  between operations  2.11 us (2%)
  local copies, waits for them, and re-layouts  1.17 us (1%)
    ppermute x27, starting transfers between devices, swap(): lax.ppermute(array, AXES, [(i, i ^ (mask1 if i & 1 else mask0)) for i in...  38.2 us
    ppermute x27, waiting for transfers between devices, swap(): lax.ppermute(array, AXES, [(i, i ^ (mask1 if i & 1 else mask0)) for i in...  29.1 us
    pallas_call x10, Pallas kernels, call(): pl.pallas_call(kernel, out_shape=out_shape, in_specs=[SMEM] * scalars + [...  23.9 us
  transfers between devices with their start and end apart: 27, of which 16 were waited for; matrix products, arithmetic and copies ran while one was open for 1% of the time, Pallas kernels for 23%

profile of v20, /device:TPU:1, one launch (start us, length us, event | category | flops | bytes accessed | tf_op | source)
XLA Modules:
  0.0 96.8 jit_solution(17898675664495454518)
XLA Ops:
  0.7 1.1 %pad_maximum_fusion.3.both_ref = bf16[576,352]{1,0:T(8,128)(2,1)S(1)} fusion(bf16[288,352]{1,0:T(8,128)(2,1)} %bitcast.13, bf16[288,352]{1,0:T(8,128)(2,1)} %bitcast.14), kind=kLoop, calls=%fused_computation.11 | loop fusion | flops 811008 | bytes 811008 | tf_op jit(solution)/shard_map/concatenate | solution.py:268
  1.8 0.8 split.1
  2.6 1.5 %collective-permute-start = (bf16[352,288]{1,0:T(8,128)(2,1)S(1)}, bf16[352,288]{1,0:T(8,128)(2,1)S(1)}, u32[]{:S(2)}, u32[]{:S(2)}) collective-permute-start(bf16[352,288]{1,0:T(8,128)(2,1)S(1)} %get-tuple-element.41), channel_id=1, source_target_pairs={{0,1},{1,0},{2,3},{3,2},{4,5},{5,4},{6,7},{7,6},{8,9},{9,8},{10,11... | collective-permute-start | bytes 608264 | tf_op jit(solution)/shard_map/ppermute | solution.py:31
  4.1 1.2 %collective-permute-done = bf16[352,288]{1,0:T(8,128)(2,1)S(1)} collective-permute-done((bf16[352,288]{1,0:T(8,128)(2,1)S(1)}, bf16[352,288]{1,0:T(8,128)(2,1)S(1)}, u32[]{:S(2)}, u32[]{:S(2)}) %collective-permute-start) | collective-permute-done | bytes 202784 | tf_op jit(solution)/shard_map/ppermute | solution.py:31
  5.6 1.8 %collective-permute-start.6 = (bf16[88,576]{1,0:T(8,128)(2,1)S(1)}, bf16[88,576]{1,0:T(8,128)(2,1)S(1)}, u32[]{:S(2)}, u32[]{:S(2)}) collective-permute-start(bf16[88,576]{1,0:T(8,128)(2,1)S(1)} %get-tuple-element.83), channel_id=1, source_target_pairs={{0,2},{1,3},{2,0},{3,1},{4,6},{5,7},{6,4},{7,5},{8,10},{9,11},{10,... | collective-permute-start | bytes 304136 | tf_op jit(solution)/shard_map/ppermute | solution.py:31
  7.6 3.4 %collective-permute-start.2 = (bf16[88,1152]{1,0:T(8,128)(2,1)S(1)}, bf16[88,1152]{1,0:T(8,128)(2,1)S(1)}, u32[]{:S(2)}, u32[]{:S(2)}) collective-permute-start(bf16[88,1152]{1,0:T(8,128)(2,1)S(1)} %pad_maximum_fusion.4), channel_id=1, source_target_pairs={{0,32},{1,65},{2,34},{3,67},{4,36},{5,69},{6,38},{7,71},{8,40},{9,... | collective-permute-start | bytes 608264 | tf_op jit(solution)/shard_map/ppermute | solution.py:31
  11.5 2.6 %collective-permute-start.9 = (bf16[88,1152]{1,0:T(8,128)(2,1)S(1)}, bf16[88,1152]{1,0:T(8,128)(2,1)S(1)}, u32[]{:S(2)}, u32[]{:S(2)}) collective-permute-start(bf16[88,1152]{1,0:T(8,128)(2,1)S(1)} %pad_maximum_fusion.5), channel_id=1, source_target_pairs={{0,12},{1,13},{2,14},{3,15},{4,8},{5,9},{6,10},{7,11},{8,4},{9,5},... | collective-permute-start | bytes 608264 | tf_op jit(solution)/shard_map/ppermute | solution.py:31
  14.0 0.5 collective-permute-start.8
  14.5 1.8 %collective-permute-done.2 = bf16[88,1152]{1,0:T(8,128)(2,1)S(1)} collective-permute-done((bf16[88,1152]{1,0:T(8,128)(2,1)S(1)}, bf16[88,1152]{1,0:T(8,128)(2,1)S(1)}, u32[]{:S(2)}, u32[]{:S(2)}) %collective-permute-start.2) | collective-permute-done | bytes 202784 | tf_op jit(solution)/shard_map/ppermute | solution.py:31
  16.3 1.2 %collective-permute-start.7 = (bf16[88,1152]{1,0:T(8,128)(2,1)S(1)}, bf16[88,1152]{1,0:T(8,128)(2,1)S(1)}, u32[]{:S(2)}, u32[]{:S(2)}) collective-permute-start(bf16[88,1152]{1,0:T(8,128)(2,1)S(1)} %pad_maximum_fusion.5), channel_id=1, source_target_pairs={{0,4},{1,5},{2,6},{3,7},{4,0},{5,1},{6,2},{7,3},{8,12},{9,13},{10,... | collective-permute-start | bytes 608264 | tf_op jit(solution)/shard_map/ppermute | solution.py:31
  17.5 1.0 %collective-permute-done.3 = bf16[88,1152]{1,0:T(8,128)(2,1)S(1)} collective-permute-done((bf16[88,1152]{1,0:T(8,128)(2,1)S(1)}, bf16[88,1152]{1,0:T(8,128)(2,1)S(1)}, u32[]{:S(2)}, u32[]{:S(2)}) %collective-permute-start.3) | collective-permute-done | bytes 202784 | tf_op jit(solution)/shard_map/ppermute | solution.py:31
  18.7 2.8 %collective-permute-start.5 = (bf16[4,88,1152]{2,1,0:T(8,128)(2,1)S(1)}, bf16[4,88,1152]{2,1,0:T(8,128)(2,1)S(1)}, u32[]{:S(2)}, u32[]{:S(2)}) collective-permute-start(bf16[4,88,1152]{2,1,0:T(8,128)(2,1)S(1)} %pad_maximum_fusion.1.ta_ref), channel_id=1, source_target_pairs={{0,66},{1,49},{2,64},{3,51},{4,70},{5,53},{6,68},{7,55},{8,74},{9,... | collective-permute-start | bytes 2433032 | tf_op jit(solution)/shard_map/ppermute | solution.py:31
  21.5 1.1 %collective-permute-done.9 = bf16[88,1152]{1,0:T(8,128)(2,1)S(1)} collective-permute-done((bf16[88,1152]{1,0:T(8,128)(2,1)S(1)}, bf16[88,1152]{1,0:T(8,128)(2,1)S(1)}, u32[]{:S(2)}, u32[]{:S(2)}) %collective-permute-start.9) | collective-permute-done | bytes 202784 | tf_op jit(solution)/shard_map/ppermute | solution.py:31
  22.6 0.8 collective-permute-done.7
  23.4 1.9 %collective-permute-start.10 = (bf16[352,1152]{1,0:T(8,128)(2,1)S(1)}, bf16[352,1152]{1,0:T(8,128)(2,1)S(1)}, u32[]{:S(2)}, u32[]{:S(2)}) collective-permute-start(bf16[352,1152]{1,0:T(8,128)(2,1)S(1)} %pad_maximum_fusion.2.im0_ref), channel_id=1, source_target_pairs={{0,1},{1,0},{2,3},{3,2},{4,5},{5,4},{6,7},{7,6},{8,9},{9,8},{10,11... | collective-permute-start | bytes 2433032 | tf_op jit(solution)/shard_map/ppermute | solution.py:31
  26.6 3.0 %collective-permute-start.11 = (bf16[4,88,1152]{2,1,0:T(8,128)(2,1)S(1)}, bf16[4,88,1152]{2,1,0:T(8,128)(2,1)S(1)}, u32[]{:S(2)}, u32[]{:S(2)}) collective-permute-start(bf16[4,88,1152]{2,1,0:T(8,128)(2,1)S(1)} %pad_maximum_fusion.1.ta_ref), channel_id=1, source_target_pairs={{0,64},{1,33},{2,66},{3,35},{4,68},{5,37},{6,70},{7,39},{8,72},{9,... | collective-permute-start | bytes 2433032 | tf_op jit(solution)/shard_map/ppermute | solution.py:31
  29.7 1.8 %collective-permute-done.5.tb_ref = bf16[4,88,1152]{2,1,0:T(8,128)(2,1)S(1)} collective-permute-done((bf16[4,88,1152]{2,1,0:T(8,128)(2,1)S(1)}, bf16[4,88,1152]{2,1,0:T(8,128)(2,1)S(1)}, u32[]{:S(2)}, u32[]{:S(2)}) %collective-permute-start.5) | collective-permute-done | bytes 811040 | tf_op jit(solution)/shard_map/ppermute | solution.py:31
  31.4 1.5 %collective-permute-done.4.tb_ref = bf16[4,88,1152]{2,1,0:T(8,128)(2,1)S(1)} collective-permute-done((bf16[4,88,1152]{2,1,0:T(8,128)(2,1)S(1)}, bf16[4,88,1152]{2,1,0:T(8,128)(2,1)S(1)}, u32[]{:S(2)}, u32[]{:S(2)}) %collective-permute-start.4) | collective-permute-done | bytes 811040 | tf_op jit(solution)/shard_map/ppermute | solution.py:31
  32.9 5.7 %tile_near.1 = (f32[2,4,88,1152]{3,2,1,0:T(8,128)S(1)}, bf16[360,1152]{1,0:T(8,128)(2,1)S(1)}, bf16[704,1152]{1,0:T(8,128)(2,1)S(1)}, bf16[704,704]{1,0:T(8,128)(2,1)S(1)}, f32[8,128]{1,0:T(8,128)S(1)}) custom-call(s32[2]{0:T(128)S(1)} %pad_add_fusion.info_ref, f32[2]{0:T(128)S(1)} %pad_maximum_fusion.7.scale_ref, ...), custom_call_target="tpu_custom_call" | custom-call | flops 2283798528 | bytes 9934864 | tf_op jit(solution)/shard_map/tile_near/pallas_call | solution.py:252
  38.9 1.6 %image_near.1.before_ref = f32[704,1152]{1,0:T(8,128)S(1)} custom-call(bf16[704,1152]{1,0:T(8,128)(2,1)S(1)} %get-tuple-element.45.t_rel, bf16[704,704]{1,0:T(8,128)(2,1)S(1)} %get-tuple-element.46.coeff_low), custom_call_target="tpu_custom_call" | custom-call | flops 1141899264 | bytes 5857280 | tf_op jit(solution)/shard_map/image_near/pallas_call | solution.py:252
  40.5 0.9 collective-permute-done.11.ta_ref
  41.4 8.5 %tile_far.1 = (bf16[360,1152]{1,0:T(8,128)(2,1)S(1)}, bf16[360,1152]{1,0:T(8,128)(2,1)S(1)}, f32[360,1152]{1,0:T(8,128)S(1)}, f32[360,1152]{1,0:T(8,128)S(1)}) custom-call(s32[2]{0:T(128)S(1)} %pad_add_fusion.info_ref, f32[2]{0:T(128)S(1)} %pad_maximum_fusion.7.scale_ref, bf16[4,88,1152]{2,1,0:T(8,128)(2,1)S(1)} %collective-permute-done.11.ta_ref, ...), custom_call_target="tpu_custom_call" | custom-call | flops 3425697792 | bytes 11468816 | tf_op jit(solution)/shard_map/tile_far/pallas_call | solution.py:252
  49.9 0.6 collective-permute-done.12.r1_ref
  50.5 2.1 %collective-permute-start.13 = (f32[360,1152]{1,0:T(8,128)S(1)}, f32[360,1152]{1,0:T(8,128)S(1)}, u32[]{:S(2)}, u32[]{:S(2)}) collective-permute-start(f32[360,1152]{1,0:T(8,128)S(1)} %get-tuple-element.53), channel_id=1, source_target_pairs={{0,1},{1,0},{2,3},{3,2},{4,5},{5,4},{6,7},{7,6},{8,9},{9,8},{10,11... | collective-permute-start | bytes 4976648 | tf_op jit(solution)/shard_map/ppermute | solution.py:31
  52.6 1.6 %collective-permute-start.14 = (bf16[360,1152]{1,0:T(8,128)(2,1)S(1)}, bf16[360,1152]{1,0:T(8,128)(2,1)S(1)}, u32[]{:S(2)}, u32[]{:S(2)}) collective-permute-start(bf16[360,1152]{1,0:T(8,128)(2,1)S(1)} %get-tuple-element.59), channel_id=1, source_target_pairs={{0,64},{1,33},{2,66},{3,35},{4,68},{5,37},{6,70},{7,39},{8,72},{9,... | collective-permute-start | bytes 2488328 | tf_op jit(solution)/shard_map/ppermute | solution.py:31
  54.2 0.8 collective-permute-start.15
  55.0 0.7 collective-permute-done.13.other_ref
  55.7 1.0 %image_first.1 = (f32[96,1152]{1,0:T(8,128)S(1)}, bf16[96,1152]{1,0:T(8,128)(2,1)S(1)}, bf16[96,1152]{1,0:T(8,128)(2,1)S(1)}, bf16[96,1152]{1,0:T(8,128)(2,1)S(1)}) custom-call(f32[360,1152]{1,0:T(8,128)S(1)} %get-tuple-element.50.own_ref, f32[360,1152]{1,0:T(8,128)S(1)} %collective-permute-done.13.other_ref), custom_call_target="tpu_custom_call" | custom-call | bytes 4423680 | tf_op jit(solution)/shard_map/image_first/pallas_call | solution.py:252
  56.7 1.3 %collective-permute-start.18 = (bf16[96,1152]{1,0:T(8,128)(2,1)S(1)}, bf16[96,1152]{1,0:T(8,128)(2,1)S(1)}, u32[]{:S(2)}, u32[]{:S(2)}) collective-permute-start(bf16[96,1152]{1,0:T(8,128)(2,1)S(1)} %get-tuple-element.54), channel_id=1, source_target_pairs={{0,4},{1,5},{2,6},{3,7},{4,0},{5,1},{6,2},{7,3},{8,12},{9,13},{10,... | collective-permute-start | bytes 663560 | tf_op jit(solution)/shard_map/ppermute | solution.py:31
  58.0 2.5 %collective-permute-start.16 = (bf16[96,1152]{1,0:T(8,128)(2,1)S(1)}, bf16[96,1152]{1,0:T(8,128)(2,1)S(1)}, u32[]{:S(2)}, u32[]{:S(2)}) collective-permute-start(bf16[96,1152]{1,0:T(8,128)(2,1)S(1)} %get-tuple-element.55), channel_id=1, source_target_pairs={{0,8},{1,9},{2,10},{3,11},{4,12},{5,13},{6,14},{7,15},{8,0},{9,1},... | collective-permute-start | bytes 663560 | tf_op jit(solution)/shard_map/ppermute | solution.py:31
  60.6 2.6 %collective-permute-done.18.r1_ref = bf16[96,1152]{1,0:T(8,128)(2,1)S(1)} collective-permute-done((bf16[96,1152]{1,0:T(8,128)(2,1)S(1)}, bf16[96,1152]{1,0:T(8,128)(2,1)S(1)}, u32[]{:S(2)}, u32[]{:S(2)}) %collective-permute-start.18) | collective-permute-done | bytes 221216 | tf_op jit(solution)/shard_map/ppermute | solution.py:31
  63.2 7.0 %collective-permute-done.16.r2_ref = bf16[96,1152]{1,0:T(8,128)(2,1)S(1)} collective-permute-done((bf16[96,1152]{1,0:T(8,128)(2,1)S(1)}, bf16[96,1152]{1,0:T(8,128)(2,1)S(1)}, u32[]{:S(2)}, u32[]{:S(2)}) %collective-permute-start.16) | collective-permute-done | bytes 221216 | tf_op jit(solution)/shard_map/ppermute | solution.py:31
  70.2 2.3 %collective-permute-done.17.r3_ref = bf16[96,1152]{1,0:T(8,128)(2,1)S(1)} collective-permute-done((bf16[96,1152]{1,0:T(8,128)(2,1)S(1)}, bf16[96,1152]{1,0:T(8,128)(2,1)S(1)}, u32[]{:S(2)}, u32[]{:S(2)}) %collective-permute-start.17) | collective-permute-done | bytes 221216 | tf_op jit(solution)/shard_map/ppermute | solution.py:31
  72.5 0.6 image_last.1
  73.2 1.0 %collective-permute-start.20 = (f32[88,576]{1,0:T(8,128)S(1)}, f32[88,576]{1,0:T(8,128)S(1)}, u32[]{:S(2)}, u32[]{:S(2)}) collective-permute-start(f32[88,576]{1,0:T(8,128)S(1)} %slice.37), channel_id=1, source_target_pairs={{0,2},{1,3},{2,0},{3,1},{4,6},{5,7},{6,4},{7,5},{8,10},{9,11},{10,... | collective-permute-start | bytes 608264 | tf_op jit(solution)/shard_map/ppermute | solution.py:31
  74.3 0.8 text_near.1.own_ref
  75.0 2.7 %text_first.1 = (f32[96,1152]{1,0:T(8,128)S(1)}, bf16[96,1152]{1,0:T(8,128)(2,1)S(1)}, bf16[96,1152]{1,0:T(8,128)(2,1)S(1)}, bf16[96,1152]{1,0:T(8,128)(2,1)S(1)}) custom-call(f32[352,1152]{1,0:T(8,128)S(1)} %text_near.1.own_ref, bf16[360,1152]{1,0:T(8,128)(2,1)S(1)} %collective-permute-done.14.r2_ref, bf16[360,1152]{1,0:T(8,128)(2,1)S(1)} %collective-permute-done.15.r3_ref, ...), custom_call_target="tpu_custom_call" | custom-call | bytes 4423680 | tf_op jit(solution)/shard_map/text_first/pallas_call | solution.py:252
  77.7 1.7 %collective-permute-start.19 = (bf16[96,1152]{1,0:T(8,128)(2,1)S(1)}, bf16[96,1152]{1,0:T(8,128)(2,1)S(1)}, u32[]{:S(2)}, u32[]{:S(2)}) collective-permute-start(bf16[96,1152]{1,0:T(8,128)(2,1)S(1)} %get-tuple-element.64), channel_id=1, source_target_pairs={{0,32},{1,65},{2,34},{3,67},{4,36},{5,69},{6,38},{7,71},{8,40},{9,... | collective-permute-start | bytes 663560 | tf_op jit(solution)/shard_map/ppermute | solution.py:31
  79.4 1.5 %collective-permute-start.21 = (bf16[96,1152]{1,0:T(8,128)(2,1)S(1)}, bf16[96,1152]{1,0:T(8,128)(2,1)S(1)}, u32[]{:S(2)}, u32[]{:S(2)}) collective-permute-start(bf16[96,1152]{1,0:T(8,128)(2,1)S(1)} %get-tuple-element.67), channel_id=1, source_target_pairs={{0,48},{1,67},{2,50},{3,65},{4,52},{5,71},{6,54},{7,69},{8,56},{9,... | collective-permute-start | bytes 663560 | tf_op jit(solution)/shard_map/ppermute | solution.py:31
  80.9 3.2 %collective-permute-done.19.r2_ref = bf16[96,1152]{1,0:T(8,128)(2,1)S(1)} collective-permute-done((bf16[96,1152]{1,0:T(8,128)(2,1)S(1)}, bf16[96,1152]{1,0:T(8,128)(2,1)S(1)}, u32[]{:S(2)}, u32[]{:S(2)}) %collective-permute-start.19) | collective-permute-done | bytes 221216 | tf_op jit(solution)/shard_map/ppermute | solution.py:31
  84.2 2.6 %collective-permute-done.21.r3_ref = bf16[96,1152]{1,0:T(8,128)(2,1)S(1)} collective-permute-done((bf16[96,1152]{1,0:T(8,128)(2,1)S(1)}, bf16[96,1152]{1,0:T(8,128)(2,1)S(1)}, u32[]{:S(2)}, u32[]{:S(2)}) %collective-permute-start.21) | collective-permute-done | bytes 221216 | tf_op jit(solution)/shard_map/ppermute | solution.py:31
  86.7 0.6 text_last.1
  88.0 3.0 %collective-permute-start.23 = (f32[352,288]{0,1:T(8,128)S(1)}, f32[352,288]{0,1:T(8,128)S(1)}, u32[]{:S(2)}, u32[]{:S(2)}) collective-permute-start(f32[352,288]{0,1:T(8,128)S(1)} %copy.7), channel_id=1, source_target_pairs={{0,1},{1,0},{2,3},{3,2},{4,5},{5,4},{6,7},{7,6},{8,9},{9,8},{10,11... | collective-permute-start | bytes 1216520 | tf_op jit(solution)/shard_map/ppermute | solution.py:31
  90.9 1.3 %collective-permute-start.26 = (f32[8,128]{1,0:T(8,128)S(1)}, f32[8,128]{1,0:T(8,128)S(1)}, u32[]{:S(2)}, u32[]{:S(2)}) collective-permute-start(f32[8,128]{1,0:T(8,128)S(1)} %get-tuple-element.73), channel_id=1, source_target_pairs={{0,66},{1,49},{2,64},{3,51},{4,70},{5,53},{6,68},{7,55},{8,74},{9,... | collective-permute-start | bytes 12296 | tf_op jit(solution)/shard_map/ppermute | solution.py:31
  92.3 0.5 collective-permute-start.25
  92.8 1.4 %collective-permute-start.24 = (f32[8,128]{1,0:T(8,128)S(1)}, f32[8,128]{1,0:T(8,128)S(1)}, u32[]{:S(2)}, u32[]{:S(2)}) collective-permute-start(f32[8,128]{1,0:T(8,128)S(1)} %get-tuple-element.73), channel_id=1, source_target_pairs={{0,2},{1,17},{2,0},{3,19},{4,6},{5,21},{6,4},{7,23},{8,10},{9,25},... | collective-permute-start | bytes 12296 | tf_op jit(solution)/shard_map/ppermute | solution.py:31
  94.4 1.7 %join.1 = (f32[288,352]{1,0:T(8,128)}, f32[288,352]{1,0:T(8,128)}) custom-call(s32[2]{0:T(128)S(1)} %pad_add_fusion.info_ref, f32[352,288]{1,0:T(8,128)S(1)} %get-tuple-element.80.own_ref, f32[352,288]{1,0:T(8,128)S(1)} %copy.8.got_ref), custom_call_target="tpu_custom_call" | custom-call | bytes 1622024 | tf_op jit(solution)/shard_map/join/pallas_call | solution.py:252
  96.2 0.5 slice_bitcast_fusion
  (36 shorter events, 2.9 us)
Async XLA Ops:
  2.6 2.7 %collective-permute-start = (bf16[352,288]{1,0:T(8,128)(2,1)S(1)}, bf16[352,288]{1,0:T(8,128)(2,1)S(1)}, u32[]{:S(2)}, u32[]{:S(2)}) collective-permute-start(bf16[352,288]{1,0:T(8,128)(2,1)S(1)} %get-tuple-element.41), channel_id=1, source_target_pairs={{0,1},{1,0},{2,3},{3,2},{4,5},{5,4},{6,7},{7,6},{8,9},{9,8},{10,11... | collective-permute-start | bytes 608264 | tf_op jit(solution)/shard_map/ppermute | solution.py:31
  5.6 5.8 %collective-permute-start.6 = (bf16[88,576]{1,0:T(8,128)(2,1)S(1)}, bf16[88,576]{1,0:T(8,128)(2,1)S(1)}, u32[]{:S(2)}, u32[]{:S(2)}) collective-permute-start(bf16[88,576]{1,0:T(8,128)(2,1)S(1)} %get-tuple-element.83), channel_id=1, source_target_pairs={{0,2},{1,3},{2,0},{3,1},{4,6},{5,7},{6,4},{7,5},{8,10},{9,11},{10,... | collective-permute-start | bytes 304136 | tf_op jit(solution)/shard_map/ppermute | solution.py:31
  7.6 8.7 %collective-permute-start.2 = (bf16[88,1152]{1,0:T(8,128)(2,1)S(1)}, bf16[88,1152]{1,0:T(8,128)(2,1)S(1)}, u32[]{:S(2)}, u32[]{:S(2)}) collective-permute-start(bf16[88,1152]{1,0:T(8,128)(2,1)S(1)} %pad_maximum_fusion.4), channel_id=1, source_target_pairs={{0,32},{1,65},{2,34},{3,67},{4,36},{5,69},{6,38},{7,71},{8,40},{9,... | collective-permute-start | bytes 608264 | tf_op jit(solution)/shard_map/ppermute | solution.py:31
  11.0 6.6 %collective-permute-start.1 = (bf16[88,1152]{1,0:T(8,128)(2,1)S(1)}, bf16[88,1152]{1,0:T(8,128)(2,1)S(1)}, u32[]{:S(2)}, u32[]{:S(2)}) collective-permute-start(bf16[88,1152]{1,0:T(8,128)(2,1)S(1)} %pad_maximum_fusion.4), channel_id=1, source_target_pairs={{0,16},{1,3},{2,18},{3,1},{4,20},{5,7},{6,22},{7,5},{8,24},{9,11},... | collective-permute-start | bytes 608264 | tf_op jit(solution)/shard_map/ppermute | solution.py:31
  11.0 7.6 %collective-permute-start.3 = (bf16[88,1152]{1,0:T(8,128)(2,1)S(1)}, bf16[88,1152]{1,0:T(8,128)(2,1)S(1)}, u32[]{:S(2)}, u32[]{:S(2)}) collective-permute-start(bf16[88,1152]{1,0:T(8,128)(2,1)S(1)} %pad_maximum_fusion.4), channel_id=1, source_target_pairs={{0,48},{1,67},{2,50},{3,65},{4,52},{5,71},{6,54},{7,69},{8,56},{9,... | collective-permute-start | bytes 608264 | tf_op jit(solution)/shard_map/ppermute | solution.py:31
  11.5 11.1 %collective-permute-start.9 = (bf16[88,1152]{1,0:T(8,128)(2,1)S(1)}, bf16[88,1152]{1,0:T(8,128)(2,1)S(1)}, u32[]{:S(2)}, u32[]{:S(2)}) collective-permute-start(bf16[88,1152]{1,0:T(8,128)(2,1)S(1)} %pad_maximum_fusion.5), channel_id=1, source_target_pairs={{0,12},{1,13},{2,14},{3,15},{4,8},{5,9},{6,10},{7,11},{8,4},{9,5},... | collective-permute-start | bytes 608264 | tf_op jit(solution)/shard_map/ppermute | solution.py:31
  14.0 8.5 %collective-permute-start.8 = (bf16[88,1152]{1,0:T(8,128)(2,1)S(1)}, bf16[88,1152]{1,0:T(8,128)(2,1)S(1)}, u32[]{:S(2)}, u32[]{:S(2)}) collective-permute-start(bf16[88,1152]{1,0:T(8,128)(2,1)S(1)} %pad_maximum_fusion.5), channel_id=1, source_target_pairs={{0,8},{1,9},{2,10},{3,11},{4,12},{5,13},{6,14},{7,15},{8,0},{9,1},... | collective-permute-start | bytes 608264 | tf_op jit(solution)/shard_map/ppermute | solution.py:31
  16.3 7.0 %collective-permute-start.7 = (bf16[88,1152]{1,0:T(8,128)(2,1)S(1)}, bf16[88,1152]{1,0:T(8,128)(2,1)S(1)}, u32[]{:S(2)}, u32[]{:S(2)}) collective-permute-start(bf16[88,1152]{1,0:T(8,128)(2,1)S(1)} %pad_maximum_fusion.5), channel_id=1, source_target_pairs={{0,4},{1,5},{2,6},{3,7},{4,0},{5,1},{6,2},{7,3},{8,12},{9,13},{10,... | collective-permute-start | bytes 608264 | tf_op jit(solution)/shard_map/ppermute | solution.py:31
  18.7 12.8 %collective-permute-start.5 = (bf16[4,88,1152]{2,1,0:T(8,128)(2,1)S(1)}, bf16[4,88,1152]{2,1,0:T(8,128)(2,1)S(1)}, u32[]{:S(2)}, u32[]{:S(2)}) collective-permute-start(bf16[4,88,1152]{2,1,0:T(8,128)(2,1)S(1)} %pad_maximum_fusion.1.ta_ref), channel_id=1, source_target_pairs={{0,66},{1,49},{2,64},{3,51},{4,70},{5,53},{6,68},{7,55},{8,74},{9,... | collective-permute-start | bytes 2433032 | tf_op jit(solution)/shard_map/ppermute | solution.py:31
  21.5 11.4 %collective-permute-start.4 = (bf16[4,88,1152]{2,1,0:T(8,128)(2,1)S(1)}, bf16[4,88,1152]{2,1,0:T(8,128)(2,1)S(1)}, u32[]{:S(2)}, u32[]{:S(2)}) collective-permute-start(bf16[4,88,1152]{2,1,0:T(8,128)(2,1)S(1)} %pad_maximum_fusion.1.ta_ref), channel_id=1, source_target_pairs={{0,2},{1,17},{2,0},{3,19},{4,6},{5,21},{6,4},{7,23},{8,10},{9,25},... | collective-permute-start | bytes 2433032 | tf_op jit(solution)/shard_map/ppermute | solution.py:31
  23.4 9.5 %collective-permute-start.10 = (bf16[352,1152]{1,0:T(8,128)(2,1)S(1)}, bf16[352,1152]{1,0:T(8,128)(2,1)S(1)}, u32[]{:S(2)}, u32[]{:S(2)}) collective-permute-start(bf16[352,1152]{1,0:T(8,128)(2,1)S(1)} %pad_maximum_fusion.2.im0_ref), channel_id=1, source_target_pairs={{0,1},{1,0},{2,3},{3,2},{4,5},{5,4},{6,7},{7,6},{8,9},{9,8},{10,11... | collective-permute-start | bytes 2433032 | tf_op jit(solution)/shard_map/ppermute | solution.py:31
  26.6 14.8 %collective-permute-start.11 = (bf16[4,88,1152]{2,1,0:T(8,128)(2,1)S(1)}, bf16[4,88,1152]{2,1,0:T(8,128)(2,1)S(1)}, u32[]{:S(2)}, u32[]{:S(2)}) collective-permute-start(bf16[4,88,1152]{2,1,0:T(8,128)(2,1)S(1)} %pad_maximum_fusion.1.ta_ref), channel_id=1, source_target_pairs={{0,64},{1,33},{2,66},{3,35},{4,68},{5,37},{6,70},{7,39},{8,72},{9,... | collective-permute-start | bytes 2433032 | tf_op jit(solution)/shard_map/ppermute | solution.py:31
  38.6 11.9 %collective-permute-start.12 = (bf16[360,1152]{1,0:T(8,128)(2,1)S(1)}, bf16[360,1152]{1,0:T(8,128)(2,1)S(1)}, u32[]{:S(2)}, u32[]{:S(2)}) collective-permute-start(bf16[360,1152]{1,0:T(8,128)(2,1)S(1)} %get-tuple-element.52), channel_id=1, source_target_pairs={{0,2},{1,17},{2,0},{3,19},{4,6},{5,21},{6,4},{7,23},{8,10},{9,25},... | collective-permute-start | bytes 2488328 | tf_op jit(solution)/shard_map/ppermute | solution.py:31
  50.5 5.2 %collective-permute-start.13 = (f32[360,1152]{1,0:T(8,128)S(1)}, f32[360,1152]{1,0:T(8,128)S(1)}, u32[]{:S(2)}, u32[]{:S(2)}) collective-permute-start(f32[360,1152]{1,0:T(8,128)S(1)} %get-tuple-element.53), channel_id=1, source_target_pairs={{0,1},{1,0},{2,3},{3,2},{4,5},{5,4},{6,7},{7,6},{8,9},{9,8},{10,11... | collective-permute-start | bytes 4976648 | tf_op jit(solution)/shard_map/ppermute | solution.py:31
  52.6 22.5 %collective-permute-start.14 = (bf16[360,1152]{1,0:T(8,128)(2,1)S(1)}, bf16[360,1152]{1,0:T(8,128)(2,1)S(1)}, u32[]{:S(2)}, u32[]{:S(2)}) collective-permute-start(bf16[360,1152]{1,0:T(8,128)(2,1)S(1)} %get-tuple-element.59), channel_id=1, source_target_pairs={{0,64},{1,33},{2,66},{3,35},{4,68},{5,37},{6,70},{7,39},{8,72},{9,... | collective-permute-start | bytes 2488328 | tf_op jit(solution)/shard_map/ppermute | solution.py:31
  54.2 20.8 %collective-permute-start.15 = (bf16[360,1152]{1,0:T(8,128)(2,1)S(1)}, bf16[360,1152]{1,0:T(8,128)(2,1)S(1)}, u32[]{:S(2)}, u32[]{:S(2)}) collective-permute-start(bf16[360,1152]{1,0:T(8,128)(2,1)S(1)} %get-tuple-element.60), channel_id=1, source_target_pairs={{0,66},{1,49},{2,64},{3,51},{4,70},{5,53},{6,68},{7,55},{8,74},{9,... | collective-permute-start | bytes 2488328 | tf_op jit(solution)/shard_map/ppermute | solution.py:31
  56.7 6.5 %collective-permute-start.18 = (bf16[96,1152]{1,0:T(8,128)(2,1)S(1)}, bf16[96,1152]{1,0:T(8,128)(2,1)S(1)}, u32[]{:S(2)}, u32[]{:S(2)}) collective-permute-start(bf16[96,1152]{1,0:T(8,128)(2,1)S(1)} %get-tuple-element.54), channel_id=1, source_target_pairs={{0,4},{1,5},{2,6},{3,7},{4,0},{5,1},{6,2},{7,3},{8,12},{9,13},{10,... | collective-permute-start | bytes 663560 | tf_op jit(solution)/shard_map/ppermute | solution.py:31
  58.0 12.2 %collective-permute-start.16 = (bf16[96,1152]{1,0:T(8,128)(2,1)S(1)}, bf16[96,1152]{1,0:T(8,128)(2,1)S(1)}, u32[]{:S(2)}, u32[]{:S(2)}) collective-permute-start(bf16[96,1152]{1,0:T(8,128)(2,1)S(1)} %get-tuple-element.55), channel_id=1, source_target_pairs={{0,8},{1,9},{2,10},{3,11},{4,12},{5,13},{6,14},{7,15},{8,0},{9,1},... | collective-permute-start | bytes 663560 | tf_op jit(solution)/shard_map/ppermute | solution.py:31
  60.4 12.0 %collective-permute-start.17 = (bf16[96,1152]{1,0:T(8,128)(2,1)S(1)}, bf16[96,1152]{1,0:T(8,128)(2,1)S(1)}, u32[]{:S(2)}, u32[]{:S(2)}) collective-permute-start(bf16[96,1152]{1,0:T(8,128)(2,1)S(1)} %get-tuple-element.56), channel_id=1, source_target_pairs={{0,12},{1,13},{2,14},{3,15},{4,8},{5,9},{6,10},{7,11},{8,4},{9,5},... | collective-permute-start | bytes 663560 | tf_op jit(solution)/shard_map/ppermute | solution.py:31
  73.2 7.7 %collective-permute-start.20 = (f32[88,576]{1,0:T(8,128)S(1)}, f32[88,576]{1,0:T(8,128)S(1)}, u32[]{:S(2)}, u32[]{:S(2)}) collective-permute-start(f32[88,576]{1,0:T(8,128)S(1)} %slice.37), channel_id=1, source_target_pairs={{0,2},{1,3},{2,0},{3,1},{4,6},{5,7},{6,4},{7,5},{8,10},{9,11},{10,... | collective-permute-start | bytes 608264 | tf_op jit(solution)/shard_map/ppermute | solution.py:31
  77.7 6.5 %collective-permute-start.19 = (bf16[96,1152]{1,0:T(8,128)(2,1)S(1)}, bf16[96,1152]{1,0:T(8,128)(2,1)S(1)}, u32[]{:S(2)}, u32[]{:S(2)}) collective-permute-start(bf16[96,1152]{1,0:T(8,128)(2,1)S(1)} %get-tuple-element.64), channel_id=1, source_target_pairs={{0,32},{1,65},{2,34},{3,67},{4,36},{5,69},{6,38},{7,71},{8,40},{9,... | collective-permute-start | bytes 663560 | tf_op jit(solution)/shard_map/ppermute | solution.py:31
  79.4 7.3 %collective-permute-start.21 = (bf16[96,1152]{1,0:T(8,128)(2,1)S(1)}, bf16[96,1152]{1,0:T(8,128)(2,1)S(1)}, u32[]{:S(2)}, u32[]{:S(2)}) collective-permute-start(bf16[96,1152]{1,0:T(8,128)(2,1)S(1)} %get-tuple-element.67), channel_id=1, source_target_pairs={{0,48},{1,67},{2,50},{3,65},{4,52},{5,71},{6,54},{7,69},{8,56},{9,... | collective-permute-start | bytes 663560 | tf_op jit(solution)/shard_map/ppermute | solution.py:31
  80.9 5.8 %collective-permute-start.22 = (bf16[96,1152]{1,0:T(8,128)(2,1)S(1)}, bf16[96,1152]{1,0:T(8,128)(2,1)S(1)}, u32[]{:S(2)}, u32[]{:S(2)}) collective-permute-start(bf16[96,1152]{1,0:T(8,128)(2,1)S(1)} %get-tuple-element.68), channel_id=1, source_target_pairs={{0,16},{1,3},{2,18},{3,1},{4,20},{5,7},{6,22},{7,5},{8,24},{9,11},... | collective-permute-start | bytes 663560 | tf_op jit(solution)/shard_map/ppermute | solution.py:31
  88.0 6.2 %collective-permute-start.23 = (f32[352,288]{0,1:T(8,128)S(1)}, f32[352,288]{0,1:T(8,128)S(1)}, u32[]{:S(2)}, u32[]{:S(2)}) collective-permute-start(f32[352,288]{0,1:T(8,128)S(1)} %copy.7), channel_id=1, source_target_pairs={{0,1},{1,0},{2,3},{3,2},{4,5},{5,4},{6,7},{7,6},{8,9},{9,8},{10,11... | collective-permute-start | bytes 1216520 | tf_op jit(solution)/shard_map/ppermute | solution.py:31
  90.9 5.2 %collective-permute-start.26 = (f32[8,128]{1,0:T(8,128)S(1)}, f32[8,128]{1,0:T(8,128)S(1)}, u32[]{:S(2)}, u32[]{:S(2)}) collective-permute-start(f32[8,128]{1,0:T(8,128)S(1)} %get-tuple-element.73), channel_id=1, source_target_pairs={{0,66},{1,49},{2,64},{3,51},{4,70},{5,53},{6,68},{7,55},{8,74},{9,... | collective-permute-start | bytes 12296 | tf_op jit(solution)/shard_map/ppermute | solution.py:31
  92.3 4.0 %collective-permute-start.25 = (f32[8,128]{1,0:T(8,128)S(1)}, f32[8,128]{1,0:T(8,128)S(1)}, u32[]{:S(2)}, u32[]{:S(2)}) collective-permute-start(f32[8,128]{1,0:T(8,128)S(1)} %get-tuple-element.73), channel_id=1, source_target_pairs={{0,64},{1,33},{2,66},{3,35},{4,68},{5,37},{6,70},{7,39},{8,72},{9,... | collective-permute-start | bytes 12296 | tf_op jit(solution)/shard_map/ppermute | solution.py:31
  92.8 3.5 %collective-permute-start.24 = (f32[8,128]{1,0:T(8,128)S(1)}, f32[8,128]{1,0:T(8,128)S(1)}, u32[]{:S(2)}, u32[]{:S(2)}) collective-permute-start(f32[8,128]{1,0:T(8,128)S(1)} %get-tuple-element.73), channel_id=1, source_target_pairs={{0,2},{1,17},{2,0},{3,19},{4,6},{5,21},{6,4},{7,23},{8,10},{9,25},... | collective-permute-start | bytes 12296 | tf_op jit(solution)/shard_map/ppermute | solution.py:31
